TPU v7x, 32 devices: a whole 2x2x4 slice. The times are simulated.
32 devices in a mesh: groups: 2 (over x), expert: 16 (over z, y, core).
Axes of the slice: x: 2, y: 2, z: 4, core: 2. Of those that a mesh axis runs over, the one named last changes fastest.
Arguments:
- hidden_in: bfloat16 [4096, 7168], P(('groups', 'expert')), parts along dimension 0, may hold values from -6 to 6
- out_grads: bfloat16 [4096, 8, 2048], P(('groups', 'expert')), parts along dimension 0, may hold values from -6 to 6
- routes: int32 [4096, 8], P(('groups', 'expert')), parts along dimension 0, may hold values from 0 to 63, all different within a row; in each aligned block of 128 rows (0 to 127, 128 to 255, ...) at most 24 rows name the same one
- segments: int32 [4096], P(('groups', 'expert')), parts along dimension 0, may hold values from 0 to 31, as said below
- in_proj: bfloat16 [64, 7168], replicated, may hold values from -0.0625 to 0.0625
- out_proj: bfloat16 [64, 64, 2048], P('expert'), may hold values from -0.125 to 0.125
Outputs:
- example_grads: bfloat16 [64, 64, 4096], P(('groups', 'expert')), parts along dimension 0
There are 2 independent parts, one for each index of `groups`. A program takes and returns all parts, laid end to end along the dimension named above; an argument that names none is the same for every part. Nothing has to cross between parts.
Inputs may be any that keep to these rules, and one draw needn't show every extreme that they name: `routes`: each row names 8 different experts. Within the rows of one index of expert (aligned blocks of 128 rows) no expert is named more than 24 times, a bound that some block reaches. `segments`: tokens k * 128 to (k + 1) * 128 - 1 belong to examples k * 2 to k * 2 + 1, each of which has at least one token; ids never fall.
All inputs are finite; a program needn't handle non-finite values.
Results may differ from a plain program's by a relative error of at most 0.0058.
Values may be sent and summed in bfloat16 or wider, within the bound.
No kernel may reach another device: no remote copies, remote signals or barrier semaphores. Data moves between devices by JAX's collectives and lax.ppermute only.
A program may use at most 128 MiB of HBM per device.

v0:
```python
import jax
import jax.numpy as jnp
from jax import lax
from jax.sharding import PartitionSpec as P

SEG_DEV = 2


def local(hidden_in, out_grads, routes, segments, in_proj, out_proj):
    tokens_here, top_count = routes.shape
    exp_here, rank_dim, hidden_dim = out_proj.shape
    owners = lax.axis_size("expert")
    experts = exp_here * owners
    capacity = max(2, 3 * tokens_here * top_count // (2 * experts))
    pair_count = tokens_here * top_count
    projected = lax.dot_general(
        hidden_in, in_proj, (((1,), (1,)), ((), ())), preferred_element_type=jnp.float32
    ).astype(jnp.bfloat16)
    local_seg = segments - lax.axis_index("expert") * SEG_DEV
    seg_mask = (local_seg[:, None] == jnp.arange(SEG_DEV, dtype=jnp.int32)[None, :]).astype(
        jnp.bfloat16
    )
    spread = (seg_mask[:, :, None] * projected[:, None, :]).reshape(tokens_here, SEG_DEV * rank_dim)
    flat_routes = routes.reshape(pair_count)
    ordering = jnp.argsort(flat_routes, stable=True)
    sorted_routes = flat_routes[ordering]
    counts = jnp.sum(
        (flat_routes[:, None] == jnp.arange(experts, dtype=jnp.int32)[None, :]).astype(jnp.int32),
        axis=0,
    )
    starts = jnp.cumsum(counts) - counts
    within = jnp.arange(pair_count, dtype=jnp.int32) - starts[sorted_routes]
    slot_table = (
        jnp.full((experts * capacity,), pair_count, jnp.int32)
        .at[sorted_routes * capacity + within]
        .set(ordering)
    )
    send_grads = jnp.take(
        out_grads.reshape(pair_count, hidden_dim), slot_table, axis=0, mode="fill", fill_value=0
    )
    send_grads = send_grads.reshape(owners, exp_here, capacity, hidden_dim)
    slot_rows = jnp.take(spread, slot_table // top_count, axis=0, mode="fill", fill_value=0)
    reduced = jnp.einsum(
        "dech,erh->decr",
        lax.all_to_all(send_grads, "expert", split_axis=0, concat_axis=0, tiled=True),
        out_proj,
        preferred_element_type=jnp.float32,
    ).astype(jnp.bfloat16)
    reduced = reduced.reshape(owners, exp_here, capacity * rank_dim)
    back = lax.all_to_all(reduced, "expert", split_axis=0, concat_axis=0, tiled=True)
    back = back.reshape(experts, capacity, rank_dim)
    factors = slot_rows.reshape(experts, capacity, SEG_DEV, rank_dim)
    blocks = jnp.einsum("ecr,ecsj->serj", back, factors, preferred_element_type=jnp.float32)
    return blocks.astype(jnp.bfloat16).reshape(SEG_DEV, experts, rank_dim * rank_dim)


def solution(mesh):
    placed = (
        P(("groups", "expert"), None),
        P(("groups", "expert"), None, None),
        P(("groups", "expert"), None),
        P(("groups", "expert")),
        P(),
        P("expert", None, None),
    )
    return jax.shard_map(
        local,
        mesh=mesh,
        in_specs=placed,
        out_specs=P(("groups", "expert"), None, None),
        check_vma=False,
    )
```

profile of v0, /device:TPU:1, one launch (start us, length us, event | category | flops | bytes accessed | tf_op | source)
XLA Modules:
  0.0 254.6 jit_solution(6140362143712430233)
XLA Ops:
  0.0 0.0 copy-start
  0.0 0.9 copy.26
  0.9 0.1 reshape.136
  1.0 0.1 convert_reduce_fusion
  1.1 0.1 copy.27
  1.2 0.1 reduce-window.9
  1.3 0.1 reduce.1
  1.5 0.7 fusion.20
  2.2 0.7 fusion.21
  2.9 0.7 fusion.18
  3.6 0.7 fusion.19
  4.3 4.4 %sort.17 = (s32[1024]{0:T(1024)}, s32[1024]{0:T(1024)S(1)}) sort(s32[1024]{0:T(1024)S(1)} %reshape.136, s32[1024]{0:T(1024)S(1)} %iota.19), dimensions={0}, to_apply=%region_0.0 | sort | flops 10240 | bytes 16384 | tf_op jit(solution)/shard_map/jit(argsort)/sort | solution.py:25
  8.7 4.5 %gather_fusion = s32[1024]{0:T(1024)S(1)} fusion(s32[1024]{0:T(1024)S(1)} %reshape.136, s32[1024]{0:T(1024)S(1)} %fusion.14), kind=kCustom, calls=%fused_computation | custom fusion | bytes 12288 | tf_op jit(solution)/shard_map/gather | solution.py:26
  13.2 4.3 %compare_select_fusion.3 = (s32[1024,1]{0,1:T(1,128)S(1)}, s32[1024,1]{0,1:T(1,128)S(1)}) fusion(s32[]{:T(128)} %bitcast.59, s32[]{:T(128)} %bitcast.60, s32[]{:T(128)} %bitcast.61, s32[]{:T(128)} %bitcast.62, s32[]{:T(128)} %bitcast.63, s32[]{:T(128)} %bitcast.65, s32[]{:T(128)} %bitcast.64, s32[1024,1]{0,1:T(1,128)S(1)} %bitcast.95), kind=kLoop, calls=%fused_computation.79 | loop fusion | flops 15360 | bytes 12316 | tf_op jit(solution)/shard_map/gather | solution.py:32
  17.5 0.7 compare_reduce_fusion.56
  18.3 35.6 %select_select_fusion = s32[1024]{0:T(1024)S(1)} fusion(pred[1024]{0:T(1024)(128)(4,1)S(1)} %get-tuple-element.63, pred[1024]{0:T(1024)(128)(4,1)S(1)} %get-tuple-element.62, pred[1024]{0:T(1024)(128)(4,1)S(1)} %get-tuple-element.61, pred[1024]{0:T(1024)(128)(4,1)S(1)} %get-tuple-element.60, pred[1024]{0:T(1024)(128)(4,1)S(1)} %get-tuple-element.59, ...), kind=kLoop, calls=%fused_computation.99 | loop fusion | flops 58368 | bytes 66788 | tf_op jit(solution)/shard_map/gather | solution.py:32
  53.9 4.3 %scatter_custom_fusion = s32[1536]{0:T(1024)S(1)} fusion(s32[1024]{0:T(1024)S(1)} %bitcast.99, s32[1024]{0:T(1024)S(1)} %get-tuple-element.6, s32[]{:T(128)} %constant.32.clone.1), kind=kCustom, calls=%fused_computation.100 | custom fusion | bytes 6148 | tf_op jit(solution)/shard_map/scatter | solution.py:36
  58.3 0.1 broadcast_in_dim.47
  58.4 15.4 %gather_fusion.2 = bf16[1536,2048]{1,0:T(8,128)(2,1)} fusion(bf16[1024,2048]{1,0:T(8,128)(2,1)} %bitcast.92, s32[2048]{0:T(1024)S(1)} %pad_clamp_fusion), kind=kCustom, calls=%fused_computation.2 | custom fusion | bytes 12589056 | tf_op jit(solution)/shard_map/jit(_take)/gather | solution.py:38
  73.8 6.0 %broadcast_select_fusion = bf16[16,4,24,2048]{3,2,1,0:T(8,128)(2,1)} fusion(bf16[16,4,24,2048]{3,2,1,0:T(8,128)(2,1)} %bitcast.93, pred[16,4,24]{2,1,0:T(4,128)(4,1)S(1)} %broadcast_in_dim.47), kind=kLoop, calls=%fused_computation.6 | loop fusion | flops 3145728 | bytes 12584448 | tf_op jit(solution)/shard_map/jit(_take)/select_n | solution.py:38
  79.8 0.0 copy-start.2
  79.8 0.0 copy-start.1
  79.8 7.5 %all-to-all-start = ((bf16[16,4,24,2048]{3,2,1,0:T(8,128)(2,1)}), bf16[16,4,24,2048]{3,2,1,0:T(8,128)(2,1)}, u32[]{:S(2)}, u32[]{:S(2)}) async-start(bf16[16,4,24,2048]{3,2,1,0:T(8,128)(2,1)} %broadcast_select_fusion), calls=%async_computation | async-start | bytes 12582912 | tf_op jit(solution)/shard_map/all_to_all | solution.py:45
  87.3 0.0 copy-done.2
  87.3 0.0 copy-done
  87.3 0.0 copy-done.1
  87.3 0.8 convolution_convert_fusion
  88.0 113.8 %all-to-all-done = bf16[16,4,24,2048]{3,2,1,0:T(8,128)(2,1)} async-done(((bf16[16,4,24,2048]{3,2,1,0:T(8,128)(2,1)}), bf16[16,4,24,2048]{3,2,1,0:T(8,128)(2,1)}, u32[]{:S(2)}, u32[]{:S(2)}) %all-to-all-start) | async-done | bytes 6291488 | tf_op jit(solution)/shard_map/all_to_all | solution.py:45
  201.9 4.8 %fusion.5 = bf16[16,4,24,64]{3,2,0,1:T(8,128)(2,1)S(1)} fusion(bf16[16,4,24,2048]{3,2,1,0:T(8,128)(2,1)} %all-to-all-done, bf16[4,64,2048]{2,1,0:T(8,128)(2,1)} %param.11), kind=kOutput, calls=%fused_computation.9 | convolution fusion | flops 402751488 | bytes 7536640 | tf_op jit(solution)/shard_map/dech,erh->decr/dot_general | solution.py:43
  206.7 0.3 reshape.140
  206.9 0.8 copy.31
  207.8 27.7 %all-to-all-start.1 = ((bf16[16,4,1536]{2,1,0:T(4,128)(2,1)}), bf16[16,4,1536]{2,1,0:T(4,128)(2,1)S(1)}, u32[]{:S(2)}, u32[]{:S(2)}) async-start(bf16[16,4,1536]{2,1,0:T(4,128)(2,1)} %copy.31), calls=%async_computation.1 | async-start | bytes 393216 | tf_op jit(solution)/shard_map/all_to_all | solution.py:50
  235.5 0.1 copy.28
  235.6 3.2 %gather_fusion.1 = bf16[1536,128]{1,0:T(8,128)(2,1)S(1)} fusion(bf16[128,128]{1,0:T(8,128)(2,1)S(1)} %copy.28, s32[2048]{0:T(1024)S(1)} %pad_clamp_fusion.1), kind=kCustom, calls=%fused_computation.1 | custom fusion | bytes 792576 | tf_op jit(solution)/shard_map/jit(_take)/gather | solution.py:42
  238.9 0.3 gather.27
  239.2 0.1 broadcast_in_dim.43
  239.3 4.5 %all-to-all-done.1 = bf16[16,4,1536]{2,1,0:T(4,128)(2,1)S(1)} async-done(((bf16[16,4,1536]{2,1,0:T(4,128)(2,1)}), bf16[16,4,1536]{2,1,0:T(4,128)(2,1)S(1)}, u32[]{:S(2)}, u32[]{:S(2)}) %all-to-all-start.1) | async-done | bytes 196640 | tf_op jit(solution)/shard_map/all_to_all | solution.py:50
  243.8 0.2 reshape.391
  244.0 2.3 convert_bitcast_fusion
  246.4 4.1 %copy.32 = bf16[2,64,64,64]{3,2,1,0:T(8,128)(2,1)} copy(bf16[2,64,64,64]{2,3,0,1:T(8,128)(2,1)} %convert_bitcast_fusion) | data formatting | bytes 2097152 | tf_op jit(solution)/shard_map/convert_element_type | solution.py:54
  250.5 4.1 %reshape.142 = bf16[2,64,4096]{2,1,0:T(8,128)(2,1)} reshape(bf16[2,64,64,64]{3,2,1,0:T(8,128)(2,1)} %copy.32) | data formatting | bytes 2097152 | tf_op jit(solution)/shard_map/reshape | solution.py:54
  (11 shorter events, 0.1 us)
Async XLA Ops:
  0.0 87.3 %copy-start = (bf16[128,7168]{1,0:T(8,128)(2,1)S(1)}, bf16[128,7168]{1,0:T(8,128)(2,1)}, u32[]{:S(2)}) copy-start(bf16[128,7168]{1,0:T(8,128)(2,1)} %param.6) | copy-start | bytes 5505028
  79.8 7.5 %copy-start.2 = (s32[128]{0:T(128)S(1)}, s32[128]{0:T(128)}, u32[]{:S(2)}) copy-start(s32[128]{0:T(128)} %param.9) | copy-start | bytes 1540
  79.8 7.5 %copy-start.1 = (bf16[64,7168]{1,0:T(8,128)(2,1)S(1)}, bf16[64,7168]{1,0:T(8,128)(2,1)}, u32[]{:S(2)}) copy-start(bf16[64,7168]{1,0:T(8,128)(2,1)} %param.10) | copy-start | bytes 2752516
  79.8 122.1 %all-to-all-start = ((bf16[16,4,24,2048]{3,2,1,0:T(8,128)(2,1)}), bf16[16,4,24,2048]{3,2,1,0:T(8,128)(2,1)}, u32[]{:S(2)}, u32[]{:S(2)}) async-start(bf16[16,4,24,2048]{3,2,1,0:T(8,128)(2,1)} %broadcast_select_fusion), calls=%async_computation | async-start | bytes 12582912 | tf_op jit(solution)/shard_map/all_to_all | solution.py:45
  207.8 36.0 %all-to-all-start.1 = ((bf16[16,4,1536]{2,1,0:T(4,128)(2,1)}), bf16[16,4,1536]{2,1,0:T(4,128)(2,1)S(1)}, u32[]{:S(2)}, u32[]{:S(2)}) async-start(bf16[16,4,1536]{2,1,0:T(4,128)(2,1)} %copy.31), calls=%async_computation.1 | async-start | bytes 393216 | tf_op jit(solution)/shard_map/all_to_all | solution.py:50
where the time goes:
time: 256 us; the launch traced here: 255 us
  waiting for transfers between devices  118 us (46%)
  other arithmetic  51.4 us (20%)
  local copies, waits for them, and re-layouts  41.6 us (16%)
  starting transfers between devices  35.2 us (14%)
  matrix products  7.92 us (3%)
    all_to_all x1, waiting for transfers between devices, local(): lax.all_to_all(send_grads, 'expert', split_axis=0, concat_axis=0, tiled=T...  114 us
    gather x3, other arithmetic, local(): within = jnp.arange(pair_count, dtype=jnp.int32) - starts[sorted_routes]  40.7 us
    all_to_all x1, starting transfers between devices, local(): lax.all_to_all(reduced, 'expert', split_axis=0, concat_axis=0, tiled=True)  27.7 us
    gather x1, local copies, waits for them, and re-layouts, local(): jnp.take(out_grads.reshape(pair_count, hidden_dim), slot_table, axis=0, m...  15.4 us
    all_to_all x1, starting transfers between devices, local(): lax.all_to_all(send_grads, 'expert', split_axis=0, concat_axis=0, tiled=T...  7.48 us
    select_n x2, other arithmetic, local(): jnp.take(out_grads.reshape(pair_count, hidden_dim), slot_table, axis=0, m...  5.96 us
  transfers between devices with their start and end apart: 2, of which 2 were waited for; matrix products, arithmetic and copies ran while one was open for 2% of the time, Pallas kernels for 0%

commit v1 on v0

v1 whole, which is shorter than its diff:
```python
import functools

import jax
import jax.numpy as jnp
from jax import lax
from jax.experimental import pallas as pl
from jax.experimental.pallas import tpu as pltpu
from jax.sharding import PartitionSpec as P

SEG_DEV = 2
ROWS = 256


def reduce_kernel(tops, tokens, rank, grads_ref, routes_ref, weight_ref, basis_ref, out_ref, held):
    step = pl.program_id(0)
    dense = lax.dot_general(
        grads_ref[...], weight_ref[...], (((1,), (1,)), ((), ())), preferred_element_type=jnp.float32
    )
    first = step * (ROWS // rank)
    lanes = first + lax.broadcasted_iota(jnp.int32, (tokens, ROWS), 1) // rank
    total = jnp.zeros((tokens, ROWS), jnp.float32)
    for k in range(tops):
        rows = pl.ds(k * tokens, tokens)
        chosen = routes_ref[rows, :]
        chosen = jnp.concatenate([chosen] * (ROWS // 128), axis=1)
        total = total + jnp.where(chosen == lanes, dense[k * tokens : (k + 1) * tokens], 0.0)
    held[pl.ds(pl.multiple_of(step * ROWS, ROWS), ROWS), :] = total.T

    @pl.when(step == pl.num_programs(0) - 1)
    def _():
        experts = out_ref.shape[1]
        for pair in range(rank // 2):
            left = held[pl.ds(2 * pair, experts, stride=rank), :]
            right = held[pl.ds(2 * pair + 1, experts, stride=rank), :]
            both = jnp.concatenate([left, right], axis=1).astype(jnp.bfloat16)
            block = jnp.dot(both, basis_ref[...], preferred_element_type=jnp.float32)
            block = block.astype(jnp.bfloat16)
            for s in range(SEG_DEV):
                out_ref[s, :, pl.ds(pair * 2 * rank, 2 * rank)] = block[
                    :, s * 2 * rank : (s + 1) * 2 * rank
                ]


def local(hidden_in, out_grads, routes, segments, in_proj, out_proj):
    tokens, tops = routes.shape
    exp_here, rank, width = out_proj.shape
    experts = exp_here * lax.axis_size("expert")
    pairs = tokens * tops
    gathered = lax.all_gather(out_proj.reshape(exp_here * rank, width), "expert", axis=0, tiled=True)
    projected = lax.dot_general(
        hidden_in, in_proj, (((1,), (1,)), ((), ())), preferred_element_type=jnp.float32
    ).astype(jnp.bfloat16)
    local_seg = segments - lax.axis_index("expert") * SEG_DEV
    seg_mask = (local_seg[:, None] == jnp.arange(SEG_DEV, dtype=jnp.int32)[None, :]).astype(
        jnp.bfloat16
    )
    spread = seg_mask[:, :, None] * projected[:, None, :]
    parity = jnp.eye(2, dtype=jnp.bfloat16)
    basis = (parity[:, None, None, :, None] * spread[None, :, :, None, :]).reshape(
        2 * tokens, SEG_DEV * 2 * rank
    )
    grads = jnp.swapaxes(out_grads, 0, 1).reshape(pairs, width)
    chosen = jnp.broadcast_to(routes.T.reshape(pairs, 1), (pairs, 128))
    steps = experts * rank // ROWS
    return pl.pallas_call(
        functools.partial(reduce_kernel, tops, tokens, rank),
        grid=(steps,),
        out_shape=jax.ShapeDtypeStruct((SEG_DEV, experts, rank * rank), jnp.bfloat16),
        in_specs=[
            pl.BlockSpec((pairs, width), lambda i: (0, 0)),
            pl.BlockSpec((pairs, 128), lambda i: (0, 0)),
            pl.BlockSpec((ROWS, width), lambda i: (i, 0)),
            pl.BlockSpec((2 * tokens, SEG_DEV * 2 * rank), lambda i: (0, 0)),
        ],
        out_specs=pl.BlockSpec((SEG_DEV, experts, rank * rank), lambda i: (0, 0, 0)),
        scratch_shapes=[pltpu.VMEM((experts * rank, tokens), jnp.float32)],
        compiler_params=pltpu.CompilerParams(vmem_limit_bytes=56 * 1024 * 1024),
        cost_estimate=pl.CostEstimate(
            flops=2 * pairs * width * experts * rank,
            bytes_accessed=experts * rank * width * 2,
            transcendentals=0,
        ),
    )(grads, chosen, gathered, basis)


def solution(mesh):
    placed = (
        P(("groups", "expert"), None),
        P(("groups", "expert"), None, None),
        P(("groups", "expert"), None),
        P(("groups", "expert")),
        P(),
        P("expert", None, None),
    )
    return jax.shard_map(
        local,
        mesh=mesh,
        in_specs=placed,
        out_specs=P(("groups", "expert"), None, None),
        check_vma=False,
    )
```

time: 256 us -> 174 us (0.68)
  other arithmetic: 51.4 us -> 0.85 us
  starting transfers between devices: 35.2 us -> 0.01 us
  local copies, waits for them, and re-layouts: 41.6 us -> 8.3 us
  Pallas kernels: 0 us -> 27 us
  between operations: 0.2 us -> 13.4 us
  matrix products: 7.92 us -> 1.93 us
  waiting for transfers between devices: 118 us -> 122 us
    all_gather x0 -> x1, waiting for transfers between devices: none -> 122 us  [local(): lax.all_gather(out_proj.reshape(exp_here * rank, width), 'expert', axis=0...]
    all_to_all x2 -> x0, waiting for transfers between devices: 118 us -> none  [the longest x1 114 us: local(): lax.all_to_all(send_grads, 'expert', split_axis=0, concat_axis=0, tiled=T...]
    gather x6 -> x0, other arithmetic: 40.7 us -> none  [the longest x3 40.7 us: local(): within = jnp.arange(pair_count, dtype=jnp.int32) - starts[sorted_routes]]
    all_to_all x2 -> x0, starting transfers between devices: 35.2 us -> none  [the longest x1 27.7 us: local(): lax.all_to_all(reduced, 'expert', split_axis=0, concat_axis=0, tiled=True)]
    pallas_call x0 -> x1, Pallas kernels: none -> 27 us  [local(): pl.pallas_call(functools.partial(reduce_kernel, tops, tokens, rank), grid...]
    gather x8 -> x0, local copies, waits for them, and re-layouts: 26.3 us -> none  [the longest x1 15.4 us: local(): jnp.take(out_grads.reshape(pair_count, hidden_dim), slot_table, axis=0, m...]
    dot_general x2 -> x0, matrix products: 7.17 us -> none  [the longest x1 4.82 us: local(): jnp.einsum('dech,erh->decr', lax.all_to_all(send_grads, 'expert', split_a...]
    transpose x0 -> x1, local copies, waits for them, and re-layouts: none -> 6.43 us  [local(): grads = jnp.swapaxes(out_grads, 0, 1).reshape(pairs, width)]
  transfers between devices with their start and end apart: 2 -> 1, of which waited for: 2 -> 1; matrix products, arithmetic and copies ran while one was open for 2% -> 6% of each run, Pallas kernels for 0% -> 0%
where the time goes in v1:
time: 174 us
  waiting for transfers between devices  122 us (70%)
  Pallas kernels  27 us (16%)
  between operations  13.4 us (8%)
  local copies, waits for them, and re-layouts  8.3 us (5%)
  matrix products  1.93 us (1%)
    all_gather x1, waiting for transfers between devices, local(): lax.all_gather(out_proj.reshape(exp_here * rank, width), 'expert', axis=0...  122 us
    pallas_call x1, Pallas kernels, local(): pl.pallas_call(functools.partial(reduce_kernel, tops, tokens, rank), grid...  27 us
    transpose x1, local copies, waits for them, and re-layouts, local(): grads = jnp.swapaxes(out_grads, 0, 1).reshape(pairs, width)  6.43 us
  transfers between devices with their start and end apart: 1, of which 1 were waited for; matrix products, arithmetic and copies ran while one was open for 6% of the time, Pallas kernels for 0%

profile of v1, /device:TPU:1, one launch (start us, length us, event | category | flops | bytes accessed | tf_op | source)
XLA Modules:
  0.0 173.8 jit_solution(18302253825640957158)
XLA Ops:
  6.5 0.0 copy-start
  6.5 0.0 all-gather.2.cloned.1.call-start
  6.5 0.7 all-gather.2.cloned.1.call-update
  7.3 0.7 broadcast_subtract_fusion
  7.9 0.1 copy-done
  8.0 1.9 %convolution_convert_fusion = bf16[128,64]{0,1:T(8,128)(2,1)S(1)} fusion(bf16[128,7168]{1,0:T(8,128)(2,1)S(1)} %copy-done, bf16[64,7168]{1,0:T(8,128)(2,1)} %param.10), kind=kOutput, calls=%fused_computation | convolution fusion | flops 117448704 | bytes 2768896 | tf_op jit(solution)/shard_map/dot_general | solution.py:50
  10.0 0.2 broadcast_multiply_fusion
  10.2 0.7 copy.10.basis_ref
  10.9 0.0 copy-start.1
  10.9 6.4 %copy.9 = bf16[8,128,2048]{2,1,0:T(8,128)(2,1)} copy(bf16[8,128,2048]{2,0,1:T(8,128)(2,1)} %bitcast.15) | data formatting | bytes 8388608 | tf_op jit(solution)/shard_map/transpose | solution.py:62
  17.4 121.6 %all-gather.2.cloned.1.call-done.weight_ref = bf16[4096,2048]{1,0:T(8,128)(2,1)} async-done(((bf16[256,2048]{1,0:T(8,128)(2,1)}), bf16[4096,2048]{1,0:T(8,128)(2,1)}) %all-gather.2.cloned.1.call-update) | async-done | bytes 16777232 | tf_op jit(solution)/shard_map/all_gather | solution.py:49
  139.0 0.0 copy-done.1
  139.0 1.0 broadcast_in_dim.5.routes_ref
  140.0 27.0 %shard_map.64 = bf16[2,64,4096]{2,1,0:T(8,128)(2,1)} custom-call(bf16[1024,2048]{1,0:T(8,128)(2,1)} %bitcast.16, s32[1024,128]{1,0:T(8,128)} %broadcast_in_dim.5.routes_ref, bf16[4096,2048]{1,0:T(8,128)(2,1)} %all-gather.2.cloned.1.call-done.weight_ref, bf16[256,256]{1,0:T(8,128)(2,1)} %copy.10.basis_ref), custom_call_target="tpu_custom_call" | custom-call | flops 17179869184 | bytes 16777216 | tf_op jit(solution)/shard_map/pallas_call | solution.py:65
  (4 shorter events, 0.0 us)
Async XLA Ops:
  6.5 1.5 copy-start
  6.5 132.4 %all-gather.2.cloned.1.call-start = ((), (), s32[]{:S(2)}) async-start(), calls=%async_computation | async-start | bytes 17825792 | tf_op jit(solution)/shard_map/all_gather | solution.py:49
  10.9 128.0 %copy-start.1 = (s32[128,8]{0,1:T(8,128)S(1)}, s32[128,8]{0,1:T(8,128)}, u32[]{:S(2)}) copy-start(s32[128,8]{0,1:T(8,128)} %param.8) | copy-start | bytes 12292
Sparse Core Ops, SparseCore 0:
  9.5 129.3 all-gather.1

commit v2 on v1

v2 whole, which is shorter than its diff:
```python
import functools

import jax
import jax.numpy as jnp
from jax import lax
from jax.experimental import pallas as pl
from jax.experimental.pallas import tpu as pltpu
from jax.sharding import PartitionSpec as P

SEG_DEV = 2
LANES = 128
CORES = 2
SIDES = 2
QUAD = 4
BOTH = ("groups", "expert")


def partial_kernel(plan, rank, fresh, bases_ref, tidx_ref, widx_ref, *refs):
    blocks, units, new_blocks = plan["blocks"], plan["units"], plan["new_blocks"]
    token_refs = refs[:blocks]
    weight_refs = refs[blocks : blocks + units]
    routes_ref = refs[blocks + units]
    acc_in = None if fresh else refs[blocks + units + 1]
    acc_out = refs[blocks + units + (1 if fresh else 2)]
    token_vmem, weight_vmem, sems = refs[-3:]
    copies = [
        pltpu.make_async_copy(ref, token_vmem.at[i], sems.at[i]) for i, ref in enumerate(token_refs)
    ] + [
        pltpu.make_async_copy(ref, weight_vmem.at[i], sems.at[blocks + i])
        for i, ref in enumerate(weight_refs)
    ]
    for copy in copies:
        copy.start()
    if fresh:
        acc_out[...] = jnp.zeros_like(acc_out)
    else:
        acc_out[...] = acc_in[...]
    for copy in copies:
        copy.wait()
    rows, width = token_vmem.shape[1:]
    cols = weight_vmem.shape[1]
    lane = lax.broadcasted_iota(jnp.int32, (1, LANES), 1) // rank
    per_tile = LANES // rank
    half = cols // CORES

    def step(i, carry):
        t, w = tidx_ref[i], widx_ref[i]
        dense = lax.dot_general(
            token_vmem[t],
            weight_vmem[w],
            (((1,), (1,)), ((), ())),
            preferred_element_type=jnp.float32,
        )
        here = pl.ds(pl.multiple_of(t * rows, rows), rows)
        chosen = routes_ref[here, :]
        total = acc_out[here, :]
        for j in range(cols // LANES):
            core, tile = divmod(j, half // LANES)
            expert = bases_ref[w * CORES + core] + tile * per_tile + lane
            total = total + jnp.where(
                chosen == expert, dense[:, j * LANES : (j + 1) * LANES], 0.0
            )
        acc_out[here, :] = total
        return carry

    lax.fori_loop(0, len(plan["steps"]), step, 0)


def accumulate(tokens, units, bases, routes, acc, steps, rank):
    rows, width = tokens[0].shape
    cols = units[0].shape[0]
    plan = {"blocks": len(tokens), "units": len(units), "steps": steps, "new_blocks": 0}
    fresh = acc is None
    total_rows = routes.shape[0]
    smem = pl.BlockSpec(memory_space=pltpu.SMEM)
    vmem = pl.BlockSpec(memory_space=pltpu.VMEM)
    hbm = pl.BlockSpec(memory_space=pl.ANY)
    tidx = jnp.array([t for t, _ in steps], jnp.int32)
    widx = jnp.array([w for _, w in steps], jnp.int32)
    operands = [jnp.stack(bases).reshape(-1), tidx, widx, *tokens, *units, routes]
    specs = [smem] * 3 + [hbm] * (len(tokens) + len(units)) + [vmem]
    aliases = {}
    if not fresh:
        aliases = {len(operands): 0}
        operands.append(acc)
        specs.append(vmem)
    return pl.pallas_call(
        functools.partial(partial_kernel, plan, rank, fresh),
        out_shape=jax.ShapeDtypeStruct((total_rows, LANES), jnp.float32),
        in_specs=specs,
        out_specs=vmem,
        scratch_shapes=[
            pltpu.VMEM((len(tokens), rows, width), jnp.bfloat16),
            pltpu.VMEM((len(units), cols, width), jnp.bfloat16),
            pltpu.SemaphoreType.DMA((len(tokens) + len(units),)),
        ],
        input_output_aliases=aliases,
        compiler_params=pltpu.CompilerParams(vmem_limit_bytes=40 * 1024 * 1024),
        cost_estimate=pl.CostEstimate(
            flops=2 * rows * cols * width * len(steps),
            bytes_accessed=(len(tokens) * rows + len(units) * cols) * width * 2,
            transcendentals=0,
        ),
    )(*operands)


def fold_kernel(rank, acc_ref, own_ref, *send_refs):
    half = own_ref.shape[0]
    low = lax.broadcasted_iota(jnp.int32, (half, LANES), 1) < rank
    for i, out in enumerate([own_ref, *send_refs]):
        one = acc_ref[2 * half * i : 2 * half * i + half, :]
        two = acc_ref[2 * half * i + half : 2 * half * (i + 1), :]
        one = one + pltpu.roll(one, rank, 1)
        two = two + pltpu.roll(two, rank, 1)
        out[...] = jnp.where(low, one, two).astype(out.dtype)


def fold(acc, rank):
    half = acc.shape[0] // QUAD // 2
    vmem = pl.BlockSpec(memory_space=pltpu.VMEM)
    return pl.pallas_call(
        functools.partial(fold_kernel, rank),
        out_shape=[jax.ShapeDtypeStruct((half, LANES), jnp.float32)]
        + [jax.ShapeDtypeStruct((half, LANES), jnp.bfloat16)] * (QUAD - 1),
        in_specs=[vmem],
        out_specs=[vmem] * QUAD,
        compiler_params=pltpu.CompilerParams(vmem_limit_bytes=16 * 1024 * 1024),
    )(acc)


def blocks_kernel(tops, rank, routes_ref, basis_ref, own_ref, b_ref, c_ref, d_ref, out_ref, pairs, turned, spread):
    half = own_ref.shape[0]
    tokens = 2 * half // tops
    total = own_ref[...]
    for ref in (b_ref, c_ref, d_ref):
        total = total + ref[...].astype(jnp.float32)
    total = total.astype(jnp.bfloat16).astype(jnp.float32)
    pairs[0:half, :] = total
    pairs[half : 2 * half, :] = pltpu.roll(total, rank, 1)
    for k in range(tops):
        turned[k] = pairs[pl.ds(k, tokens, stride=tops), :].T[0:rank, :]
    experts = out_ref.shape[1]

    def expand(tile, carry):
        first = pl.multiple_of(tile * 8, 8)
        ids = first + lax.broadcasted_iota(jnp.int32, (8, tokens), 0)
        masks = [routes_ref[k : k + 1, :] == ids for k in range(tops)]
        for r in range(rank):
            value = jnp.zeros((8, tokens), jnp.float32)
            for k in range(tops):
                value = jnp.where(masks[k], turned[k, r : r + 1, :], value)
            spread[r, pl.ds(first, 8), :] = value
        return carry

    lax.fori_loop(0, experts // 8, expand, 0)
    for pair in range(rank // 2):
        both = jnp.concatenate([spread[2 * pair], spread[2 * pair + 1]], axis=1)
        block = jnp.dot(
            both.astype(jnp.bfloat16), basis_ref[...], preferred_element_type=jnp.float32
        ).astype(jnp.bfloat16)
        for s in range(SEG_DEV):
            out_ref[s, :, pl.ds(pair * 2 * rank, 2 * rank)] = block[
                :, s * 2 * rank : (s + 1) * 2 * rank
            ]


def local(hidden_in, out_grads, routes, segments, in_proj, out_proj):
    tokens, tops = routes.shape
    exp_here, rank, width = out_proj.shape
    owners, groups = lax.axis_size("expert"), lax.axis_size("groups")
    experts = exp_here * owners
    pairs = tokens * tops
    quarter = width // QUAD
    group, index = lax.axis_index("groups"), lax.axis_index("expert")
    mine = (group % SIDES) * CORES + index % CORES

    def swap(array, side, bit):
        table = [
            (g * owners + e, (g ^ side) * owners + (e ^ bit))
            for g in range(groups)
            for e in range(owners)
        ]
        return lax.ppermute(array, BOTH, table)

    def onward(array):
        return lax.ppermute(
            array, "expert", [(e, (e + 2 * CORES) % owners) for e in range(owners)]
        )

    def columns(array, who):
        return lax.dynamic_slice_in_dim(array, who * quarter, quarter, axis=array.ndim - 1)

    weights = out_proj.reshape(exp_here * rank, width)
    other = swap(columns(weights, mine ^ 1), 0, 1)
    unit = jnp.concatenate([columns(weights, mine), other], axis=0)

    part = tokens // 2

    def token_block(who, turn):
        piece = lax.dynamic_slice(
            out_grads, (turn * part, 0, who * quarter), (part, tops, quarter)
        )
        return piece.reshape(part * tops, quarter)

    own_blocks = [token_block(mine, h) for h in range(2)]
    core_blocks = [swap(token_block(mine ^ 1, h), 0, 1) for h in range(2)]
    side_plan = [(2, 0, 0), (2, 0, 1), (3, 1, 0), (3, 1, 1)]

    all_routes = jnp.concatenate(
        [routes.reshape(pairs)]
        + [swap(routes, side, bit).reshape(pairs) for side, bit in ((0, 1), (1, 0), (1, 1))]
    )
    wide_routes = jnp.broadcast_to(all_routes[:, None], (QUAD * pairs, LANES))

    def base_of(chip):
        return [
            (chip * CORES + index % CORES) * exp_here,
            (chip * CORES + 1 - index % CORES) * exp_here,
        ]

    chip = index // CORES
    chips = owners // CORES
    slots = chips // 2
    block_list = own_blocks + core_blocks
    unit_list, base_list = [unit], [base_of(chip)]
    acc = None
    done_units = 0
    line = unit
    sent = None
    for slot in range(max(slots, len(side_plan))):
        known = len(block_list)
        before = done_units
        if slot < len(side_plan):
            flip, bit, turn = side_plan[slot]
            piece = token_block(mine ^ flip, turn)
            if sent is not None:
                piece, sent = lax.optimization_barrier((piece, sent))
            sent = swap(piece, 1, bit)
            block_list.append(sent)
        if slot < slots:
            at = (chip - 2 * slot) % chips
            unit_list.append(swap(line, 0, CORES))
            base_list.append(base_of(at ^ 1))
            if slot + 1 < slots:
                line = onward(line)
                unit_list.append(line)
                base_list.append(base_of((chip - 2 * (slot + 1)) % chips))
        done_units = len(unit_list)
        steps = [(t, w) for t in range(known) for w in range(before, done_units)]
        steps += [(t, w) for t in range(known, len(block_list)) for w in range(done_units)]
        acc = accumulate(
            block_list,
            unit_list,
            [b for pair in base_list for b in pair],
            wide_routes,
            acc,
            steps,
            rank,
        )

    own, for_core, for_side, for_diagonal = fold(acc, rank)
    from_core = swap(for_core, 0, 1)
    from_side = swap(for_side, 1, 0)
    from_diagonal = swap(for_diagonal, 1, 1)

    projected = lax.dot_general(
        hidden_in, in_proj, (((1,), (1,)), ((), ())), preferred_element_type=jnp.float32
    ).astype(jnp.bfloat16)
    local_seg = segments - index * SEG_DEV
    seg_mask = (local_seg[:, None] == jnp.arange(SEG_DEV, dtype=jnp.int32)[None, :]).astype(
        jnp.bfloat16
    )
    picked = seg_mask[:, :, None] * projected[:, None, :]
    parity = jnp.eye(2, dtype=jnp.bfloat16)
    basis = (parity[:, None, None, :, None] * picked[None, :, :, None, :]).reshape(
        2 * tokens, SEG_DEV * 2 * rank
    )
    vmem = pl.BlockSpec(memory_space=pltpu.VMEM)
    return pl.pallas_call(
        functools.partial(blocks_kernel, tops, rank),
        out_shape=jax.ShapeDtypeStruct((SEG_DEV, experts, rank * rank), jnp.bfloat16),
        in_specs=[vmem] * 6,
        out_specs=vmem,
        scratch_shapes=[
            pltpu.VMEM((pairs, LANES), jnp.float32),
            pltpu.VMEM((tops, rank, tokens), jnp.float32),
            pltpu.VMEM((rank, experts, tokens), jnp.float32),
        ],
        compiler_params=pltpu.CompilerParams(vmem_limit_bytes=40 * 1024 * 1024),
        cost_estimate=pl.CostEstimate(
            flops=2 * rank * experts * tokens * SEG_DEV * 2 * rank,
            bytes_accessed=2 * SEG_DEV * experts * rank * rank,
            transcendentals=0,
        ),
    )(routes.T, basis, own, from_core, from_side, from_diagonal)


def solution(mesh):
    placed = (
        P(("groups", "expert"), None),
        P(("groups", "expert"), None, None),
        P(("groups", "expert"), None),
        P(("groups", "expert")),
        P(),
        P("expert", None, None),
    )
    return jax.shard_map(
        local,
        mesh=mesh,
        in_specs=placed,
        out_specs=P(("groups", "expert"), None, None),
        check_vma=False,
    )
```

time: 174 us -> 103 us (0.59)
  waiting for transfers between devices: 122 us -> 26.9 us
  starting transfers between devices: 0.01 us -> 19.5 us
  Pallas kernels: 27 us -> 45 us
  between operations: 13.4 us -> 0.39 us
    all_gather x1 -> x0, waiting for transfers between devices: 122 us -> none  [local(): lax.all_gather(out_proj.reshape(exp_here * rank, width), 'expert', axis=0...]
    ppermute x0 -> x20, waiting for transfers between devices: none -> 26.9 us  [the longest x17 23.1 us: swap(): return lax.ppermute(array, BOTH, table)]
    ppermute x0 -> x20, starting transfers between devices: none -> 19.5 us  [the longest x17 16.9 us: swap(): return lax.ppermute(array, BOTH, table)]
    pallas_call x1 -> x6, Pallas kernels: 27 us -> 45 us  [the longest x4 41.4 us: accumulate(): pl.pallas_call(functools.partial(partial_kernel, plan, rank, fresh), out_...]
    transpose x1 -> x0, local copies, waits for them, and re-layouts: 6.43 us -> none  [local(): grads = jnp.swapaxes(out_grads, 0, 1).reshape(pairs, width)]
    reshape x0 -> x5, local copies, waits for them, and re-layouts: none -> 4.22 us  [the longest x1 3.86 us: token_block(): return piece.reshape(part * tops, quarter)]
    dynamic_slice x0 -> x1, local copies, waits for them, and re-layouts: none -> 1.89 us  [columns(): lax.dynamic_slice_in_dim(array, who * quarter, quarter, axis=array.ndim - 1)]
  transfers between devices with their start and end apart: 1 -> 20, of which waited for: 1 -> 8; matrix products, arithmetic and copies ran while one was open for 6% -> 7% of each run, Pallas kernels for 0% -> 30%
where the time goes in v2:
time: 103 us
  Pallas kernels  45 us (44%)
  waiting for transfers between devices  26.9 us (26%)
  starting transfers between devices  19.5 us (19%)
  local copies, waits for them, and re-layouts  9.26 us (9%)
  other arithmetic  1.17 us (1%)
    pallas_call x4, Pallas kernels, accumulate(): pl.pallas_call(functools.partial(partial_kernel, plan, rank, fresh), out_...  41.4 us
    ppermute x17, waiting for transfers between devices, swap(): return lax.ppermute(array, BOTH, table)  23.1 us
    ppermute x17, starting transfers between devices, swap(): return lax.ppermute(array, BOTH, table)  16.9 us
    reshape x1, local copies, waits for them, and re-layouts, token_block(): return piece.reshape(part * tops, quarter)  3.86 us
    ppermute x3, waiting for transfers between devices, onward(): lax.ppermute(array, 'expert', [(e, (e + 2 * CORES) % owners) for e in ran...  3.79 us
    pallas_call x1, Pallas kernels, local(): pl.pallas_call(functools.partial(blocks_kernel, tops, rank), out_shape=ja...  2.99 us
    ppermute x3, starting transfers between devices, onward(): lax.ppermute(array, 'expert', [(e, (e + 2 * CORES) % owners) for e in ran...  2.65 us
  transfers between devices with their start and end apart: 20, of which 8 were waited for; matrix products, arithmetic and copies ran while one was open for 7% of the time, Pallas kernels for 30%

profile of v2, /device:TPU:1, one launch (start us, length us, event | category | flops | bytes accessed | tf_op | source)
XLA Modules:
  0.0 103.0 jit_solution(10243957637357385435)
XLA Ops:
  0.0 1.9 %constant_dynamic-slice_fusion.1 = (bf16[256,512]{1,0:T(8,128)(2,1)}, bf16[256,512]{1,0:T(8,128)(2,1)S(1)}) fusion(bf16[256,2048]{1,0:T(8,128)(2,1)} %bitcast.46, s32[]{:T(128)S(6)} %select_n.94, s32[]{:T(128)S(6)} %select_n.95), kind=kLoop, calls=%fused_computation.15 | loop fusion | bytes 1048584 | tf_op jit(solution)/shard_map/dynamic_slice | solution.py:191
  2.0 3.9 %dynamic-slice_bitcast_fusion = (bf16[512,512]{1,0:T(8,128)(2,1)}, bf16[512,512]{1,0:T(8,128)(2,1)}, bf16[512,512]{1,0:T(8,128)(2,1)S(1)}, bf16[512,512]{1,0:T(8...) fusion(bf16[128,8,2048]{2,1,0:T(8,128)(2,1)} %param.15, ...), kind=kLoop, calls=%fused_computation.2 | loop fusion | bytes 8388624 | tf_op jit(solution)/shard_map/reshape | solution.py:203
  5.8 2.7 %collective-permute-start.2 = (bf16[512,512]{1,0:T(8,128)(2,1)S(1)}, bf16[512,512]{1,0:T(8,128)(2,1)S(1)}, u32[]{:S(2)}, u32[]{:S(2)}) collective-permute-start(bf16[512,512]{1,0:T(8,128)(2,1)S(1)} %get-tuple-element.21), channel_id=1, source_target_pairs={{0,16},{1,17},{2,18},{3,19},{4,20},{5,21},{6,22},{7,23},{8,24},{9,... | collective-permute-start | bytes 1572872 | tf_op jit(solution)/shard_map/ppermute | solution.py:183
  8.5 0.7 copy-done.15
  9.2 1.0 pad_maximum_fusion.refs_5_.refs_6_.refs_7_.refs_8_
  10.2 1.3 %collective-permute-start.8 = (bf16[512,512]{1,0:T(8,128)(2,1)S(1)}, bf16[512,512]{1,0:T(8,128)(2,1)}, u32[]{:S(2)}, u32[]{:S(2)}) collective-permute-start(bf16[512,512]{1,0:T(8,128)(2,1)S(1)} %pad_maximum_fusion.refs_5_.refs_6_.refs_7_.refs_8_), channel_id=1, source_target_pairs={{0,4},{1,5},{2,6},{3,7},{4,8},{5,9},{6,10},{7,11},{8,12},{9,13},{1... | collective-permute-start | bytes 1572872 | tf_op jit(solution)/shard_map/ppermute | solution.py:186
  11.5 0.6 collective-permute-start.14
  12.1 0.3 collective-permute-start.15
  12.4 0.3 collective-permute-start
  12.6 8.2 %collective-permute-done.2.refs_4_ = bf16[512,512]{1,0:T(8,128)(2,1)S(1)} collective-permute-done((bf16[512,512]{1,0:T(8,128)(2,1)S(1)}, bf16[512,512]{1,0:T(8,128)(2,1)S(1)}, u32[]{:S(2)}, u32[]{:S(2)}) %collective-permute-start.2) | collective-permute-done | bytes 524320 | tf_op jit(solution)/shard_map/ppermute | solution.py:183
  20.9 0.8 copy-done.2
  21.7 1.3 %collective-permute-start.3 = (bf16[512,512]{1,0:T(8,128)(2,1)}, bf16[512,512]{1,0:T(8,128)(2,1)}, u32[]{:S(2)}, u32[]{:S(2)}) collective-permute-start(bf16[512,512]{1,0:T(8,128)(2,1)} %get-tuple-element.12), channel_id=1, source_target_pairs={{0,16},{1,17},{2,18},{3,19},{4,20},{5,21},{6,22},{7,23},{8,24},{9,... | collective-permute-start | bytes 1572872 | tf_op jit(solution)/shard_map/ppermute | solution.py:183
  22.9 0.8 convolution_convert_fusion
  23.7 1.7 %collective-permute-done.8.refs_7_.refs_8_.refs_9_.refs_10_ = bf16[512,512]{1,0:T(8,128)(2,1)} collective-permute-done((bf16[512,512]{1,0:T(8,128)(2,1)S(1)}, bf16[512,512]{1,0:T(8,128)(2,1)}, u32[]{:S(2)}, u32[]{:S(2)}) %collective-permute-start.8) | collective-permute-done | bytes 524320 | tf_op jit(solution)/shard_map/ppermute | solution.py:186
  25.5 1.1 %collective-permute-start.1 = (bf16[512,512]{1,0:T(8,128)(2,1)}, bf16[512,512]{1,0:T(8,128)(2,1)}, u32[]{:S(2)}, u32[]{:S(2)}) collective-permute-start(bf16[512,512]{1,0:T(8,128)(2,1)} %get-tuple-element.22), channel_id=1, source_target_pairs={{0,1},{1,0},{2,3},{3,2},{4,5},{5,4},{6,7},{7,6},{8,9},{9,8},{10,11... | collective-permute-start | bytes 1572872 | tf_op jit(solution)/shard_map/ppermute | solution.py:183
  26.6 1.3 %collective-permute-start.7 = (bf16[512,512]{1,0:T(8,128)(2,1)S(1)}, bf16[512,512]{1,0:T(8,128)(2,1)}, u32[]{:S(2)}, u32[]{:S(2)}) collective-permute-start(bf16[512,512]{1,0:T(8,128)(2,1)S(1)} %pad_maximum_fusion.refs_5_.refs_6_.refs_7_.refs_8_), channel_id=1, source_target_pairs={{0,2},{1,3},{2,0},{3,1},{4,6},{5,7},{6,4},{7,5},{8,10},{9,11},{10,... | collective-permute-start | bytes 1572872 | tf_op jit(solution)/shard_map/ppermute | solution.py:183
  27.9 7.0 %collective-permute-done.3.refs_5_ = bf16[512,512]{1,0:T(8,128)(2,1)} collective-permute-done((bf16[512,512]{1,0:T(8,128)(2,1)}, bf16[512,512]{1,0:T(8,128)(2,1)}, u32[]{:S(2)}, u32[]{:S(2)}) %collective-permute-start.3) | collective-permute-done | bytes 524320 | tf_op jit(solution)/shard_map/ppermute | solution.py:183
  34.9 2.5 %collective-permute-start.16 = (s32[128,8]{0,1:T(8,128)S(1)}, s32[128,8]{0,1:T(8,128)S(1)}, u32[]{:S(2)}, u32[]{:S(2)}) collective-permute-start(s32[128,8]{0,1:T(8,128)S(1)} %copy-done.1), channel_id=1, source_target_pairs={{0,17},{1,16},{2,19},{3,18},{4,21},{5,20},{6,23},{7,22},{8,25},{9,... | collective-permute-start | bytes 12296 | tf_op jit(solution)/shard_map/ppermute | solution.py:183
  37.5 1.7 %collective-permute-done.16 = s32[128,8]{0,1:T(8,128)S(1)} collective-permute-done((s32[128,8]{0,1:T(8,128)S(1)}, s32[128,8]{0,1:T(8,128)S(1)}, u32[]{:S(2)}, u32[]{:S(2)}) %collective-permute-start.16) | collective-permute-done | bytes 4128 | tf_op jit(solution)/shard_map/ppermute | solution.py:183
  39.2 1.2 %collective-permute-start.9 = (bf16[512,512]{1,0:T(8,128)(2,1)}, bf16[512,512]{1,0:T(8,128)(2,1)}, u32[]{:S(2)}, u32[]{:S(2)}) collective-permute-start(bf16[512,512]{1,0:T(8,128)(2,1)} %collective-permute-done.8.refs_7_.refs_8_.refs_9_.refs_10_), channel_id=1, source_target_pairs={{0,2},{1,3},{2,0},{3,1},{4,6},{5,7},{6,4},{7,5},{8,10},{9,11},{10,... | collective-permute-start | bytes 1572872 | tf_op jit(solution)/shard_map/ppermute | solution.py:183
  40.4 1.6 %collective-permute-start.4 = (bf16[512,512]{1,0:T(8,128)(2,1)}, bf16[512,512]{1,0:T(8,128)(2,1)}, u32[]{:S(2)}, u32[]{:S(2)}) collective-permute-start(bf16[512,512]{1,0:T(8,128)(2,1)} %get-tuple-element.13), channel_id=1, source_target_pairs={{0,17},{1,16},{2,19},{3,18},{4,21},{5,20},{6,23},{7,22},{8,25},{9,... | collective-permute-start | bytes 1572872 | tf_op jit(solution)/shard_map/ppermute | solution.py:183
  42.0 1.3 %collective-permute-start.12 = (bf16[512,512]{1,0:T(8,128)(2,1)}, bf16[512,512]{1,0:T(8,128)(2,1)}, u32[]{:S(2)}, u32[]{:S(2)}) collective-permute-start(bf16[512,512]{1,0:T(8,128)(2,1)} %collective-permute-done.10.refs_10_.refs_11_.refs_12_), channel_id=1, source_target_pairs={{0,4},{1,5},{2,6},{3,7},{4,8},{5,9},{6,10},{7,11},{8,12},{9,13},{1... | collective-permute-start | bytes 1572872 | tf_op jit(solution)/shard_map/ppermute | solution.py:186
  43.3 0.1 copy.19
  43.8 0.1 stack.107.bases_ref
  43.9 0.1 stack.106.bases_ref
  44.0 0.1 copy.20
  44.1 0.1 reshape.86
  44.2 0.1 copy.21
  44.4 0.1 copy.22
  44.6 0.3 collective-permute-start.11
  44.9 0.6 broadcast_in_dim.2.refs_8_.refs_11_.refs_14_.refs_16_
  45.5 0.1 copy-done.3
  45.6 9.3 %shard_map.136.refs_12_ = f32[4096,128]{1,0:T(8,128)S(1)} custom-call(s32[6]{0:T(128)S(1)} %stack.109.bases_ref, s32[15]{0:T(128)S(1)} %copy-done.10, s32[15]{0:T(128)S(1)} %copy-done.11, bf16[512,512]{1,0:T(8,128)(2,1)S(1)} %get-tuple-element.25.refs_0_, bf16[512,512]{1,0:T(8,128)(2,1)S(1)} %get-tuple-element.24.refs_1_, ...), custom_call_target="tpu_custom_call" | custom-call | flops 4026531840 | bytes 4194304 | tf_op jit(solution)/shard_map/pallas_call | solution.py:87
  54.9 0.1 collective-permute-done.4.refs_6_
  55.1 0.7 collective-permute-start.5
  55.8 2.0 %collective-permute-done.12.refs_13_.refs_14_ = bf16[512,512]{1,0:T(8,128)(2,1)} collective-permute-done((bf16[512,512]{1,0:T(8,128)(2,1)}, bf16[512,512]{1,0:T(8,128)(2,1)}, u32[]{:S(2)}, u32[]{:S(2)}) %collective-permute-start.12) | collective-permute-done | bytes 524320 | tf_op jit(solution)/shard_map/ppermute | solution.py:186
  57.9 9.8 %shard_map.137.refs_15_ = f32[4096,128]{1,0:T(8,128)S(1)} custom-call(s32[10]{0:T(128)S(1)} %stack.108.bases_ref, s32[15]{0:T(128)S(1)} %copy-done.8, s32[15]{0:T(128)S(1)} %copy-done.9, bf16[512,512]{1,0:T(8,128)(2,1)S(1)} %get-tuple-element.25.refs_0_, bf16[512,512]{1,0:T(8,128)(2,1)S(1)} %get-tuple-element.24.refs_1_, ...), custom_call_target="tpu_custom_call", output_to_operand_aliasing={{}: (15, {})} | custom-call | flops 4026531840 | bytes 5767168 | tf_op jit(solution)/shard_map/pallas_call | solution.py:87
  67.7 12.1 %shard_map.138.refs_17_ = f32[4096,128]{1,0:T(8,128)S(1)} custom-call(s32[14]{0:T(128)S(1)} %stack.107.bases_ref, s32[19]{0:T(128)S(1)} %copy-done.6, s32[19]{0:T(128)S(1)} %copy-done.7, bf16[512,512]{1,0:T(8,128)(2,1)S(1)} %get-tuple-element.25.refs_0_, bf16[512,512]{1,0:T(8,128)(2,1)S(1)} %get-tuple-element.24.refs_1_, ...), custom_call_target="tpu_custom_call", output_to_operand_aliasing={{}: (18, {})} | custom-call | flops 5100273664 | bytes 7340032 | tf_op jit(solution)/shard_map/pallas_call | solution.py:87
  79.8 10.2 %shard_map.139.acc_ref = f32[4096,128]{1,0:T(8,128)S(1)} custom-call(s32[16]{0:T(128)S(1)} %stack.106.bases_ref, s32[15]{0:T(128)S(1)} %copy-done.4, s32[15]{0:T(128)S(1)} %copy-done.5, bf16[512,512]{1,0:T(8,128)(2,1)S(1)} %get-tuple-element.25.refs_0_, bf16[512,512]{1,0:T(8,128)(2,1)S(1)} %get-tuple-element.24.refs_1_, ...), custom_call_target="tpu_custom_call", output_to_operand_aliasing={{}: (20, {})} | custom-call | flops 4026531840 | bytes 8388608 | tf_op jit(solution)/shard_map/pallas_call | solution.py:87
  90.1 0.6 shard_map.140
  90.7 1.3 %collective-permute-start.17 = (bf16[512,128]{1,0:T(8,128)(2,1)S(1)}, bf16[512,128]{1,0:T(8,128)(2,1)S(1)}, u32[]{:S(2)}, u32[]{:S(2)}) collective-permute-start(bf16[512,128]{1,0:T(8,128)(2,1)S(1)} %get-tuple-element.16), channel_id=1, source_target_pairs={{0,1},{1,0},{2,3},{3,2},{4,5},{5,4},{6,7},{7,6},{8,9},{9,8},{10,11... | collective-permute-start | bytes 393224 | tf_op jit(solution)/shard_map/ppermute | solution.py:183
  91.9 0.3 collective-permute-start.18
  92.2 1.4 %collective-permute-start.19 = (bf16[512,128]{1,0:T(8,128)(2,1)S(1)}, bf16[512,128]{1,0:T(8,128)(2,1)S(1)}, u32[]{:S(2)}, u32[]{:S(2)}) collective-permute-start(bf16[512,128]{1,0:T(8,128)(2,1)S(1)} %get-tuple-element.18), channel_id=1, source_target_pairs={{0,17},{1,16},{2,19},{3,18},{4,21},{5,20},{6,23},{7,22},{8,25},{9,... | collective-permute-start | bytes 393224 | tf_op jit(solution)/shard_map/ppermute | solution.py:183
  93.7 0.2 broadcast_multiply_fusion
  93.9 0.1 copy.23.basis_ref
  94.0 3.1 %collective-permute-done.18.c_ref = bf16[512,128]{1,0:T(8,128)(2,1)S(1)} collective-permute-done((bf16[512,128]{1,0:T(8,128)(2,1)S(1)}, bf16[512,128]{1,0:T(8,128)(2,1)S(1)}, u32[]{:S(2)}, u32[]{:S(2)}) %collective-permute-start.18) | collective-permute-done | bytes 131104 | tf_op jit(solution)/shard_map/ppermute | solution.py:183
  97.0 3.0 %collective-permute-done.19.d_ref = bf16[512,128]{1,0:T(8,128)(2,1)S(1)} collective-permute-done((bf16[512,128]{1,0:T(8,128)(2,1)S(1)}, bf16[512,128]{1,0:T(8,128)(2,1)S(1)}, u32[]{:S(2)}, u32[]{:S(2)}) %collective-permute-start.19) | collective-permute-done | bytes 131104 | tf_op jit(solution)/shard_map/ppermute | solution.py:183
  100.0 3.0 %shard_map.141 = bf16[2,64,4096]{2,1,0:T(8,128)(2,1)} custom-call(s32[8,128]{1,0:T(8,128)S(1)} %bitcast.43, bf16[256,256]{1,0:T(8,128)(2,1)S(1)} %copy.23.basis_ref, f32[512,128]{1,0:T(8,128)S(1)} %get-tuple-element.15.own_ref, bf16[512,128]{1,0:T(8,128)(2,1)S(1)} %collective-permute-done.17.b_ref, bf16[512,128]{1,0:T(8,128)(2,1)S(1)} %collective-permute-done.18.c_ref, ...), custom_call_target="tpu_custom_call" | custom-call | flops 268435456 | bytes 1048576 | tf_op jit(solution)/shard_map/pallas_call | solution.py:279
  (57 shorter events, 0.7 us)
Async XLA Ops:
  0.0 22.9 %copy-start = (bf16[128,7168]{1,0:T(8,128)(2,1)S(1)}, bf16[128,7168]{1,0:T(8,128)(2,1)}, u32[]{:S(2)}) copy-start(bf16[128,7168]{1,0:T(8,128)(2,1)} %param.14) | copy-start | bytes 5505028
  1.9 6.6 %collective-permute-start.6 = (bf16[256,512]{1,0:T(8,128)(2,1)S(1)}, bf16[256,512]{1,0:T(8,128)(2,1)S(1)}, u32[]{:S(2)}, u32[]{:S(2)}) collective-permute-start(bf16[256,512]{1,0:T(8,128)(2,1)S(1)} %get-tuple-element.28), channel_id=1, source_target_pairs={{0,1},{1,0},{2,3},{3,2},{4,5},{5,4},{6,7},{7,6},{8,9},{9,8},{10,11... | collective-permute-start | bytes 786440 | tf_op jit(solution)/shard_map/ppermute | solution.py:183
  1.9 7.2 %copy-start.12 = (bf16[256,512]{1,0:T(8,128)(2,1)S(1)}, bf16[256,512]{1,0:T(8,128)(2,1)}, u32[]{:S(2)}) copy-start(bf16[256,512]{1,0:T(8,128)(2,1)} %get-tuple-element.27) | copy-start | bytes 786436
  1.9 9.6 %copy-start.1 = (s32[128,8]{0,1:T(8,128)S(1)}, s32[128,8]{0,1:T(8,128)}, u32[]{:S(2)}) copy-start(s32[128,8]{0,1:T(8,128)} %param.16) | copy-start | bytes 12292
  2.0 21.0 %copy-start.13 = (bf16[64,7168]{1,0:T(8,128)(2,1)S(1)}, bf16[64,7168]{1,0:T(8,128)(2,1)}, u32[]{:S(2)}) copy-start(bf16[64,7168]{1,0:T(8,128)(2,1)} %param.18) | copy-start | bytes 2752516
  5.8 19.7 %copy-start.16 = (s32[128]{0:T(128)S(1)}, s32[128]{0:T(128)}, u32[]{:S(2)}) copy-start(s32[128]{0:T(128)} %param.17) | copy-start | bytes 1540
  5.8 15.0 %collective-permute-start.2 = (bf16[512,512]{1,0:T(8,128)(2,1)S(1)}, bf16[512,512]{1,0:T(8,128)(2,1)S(1)}, u32[]{:S(2)}, u32[]{:S(2)}) collective-permute-start(bf16[512,512]{1,0:T(8,128)(2,1)S(1)} %get-tuple-element.21), channel_id=1, source_target_pairs={{0,16},{1,17},{2,18},{3,19},{4,20},{5,21},{6,22},{7,23},{8,24},{9,... | collective-permute-start | bytes 1572872 | tf_op jit(solution)/shard_map/ppermute | solution.py:183
  8.5 0.7 copy-start.15
  10.2 15.3 %collective-permute-start.8 = (bf16[512,512]{1,0:T(8,128)(2,1)S(1)}, bf16[512,512]{1,0:T(8,128)(2,1)}, u32[]{:S(2)}, u32[]{:S(2)}) collective-permute-start(bf16[512,512]{1,0:T(8,128)(2,1)S(1)} %pad_maximum_fusion.refs_5_.refs_6_.refs_7_.refs_8_), channel_id=1, source_target_pairs={{0,4},{1,5},{2,6},{3,7},{4,8},{5,9},{6,10},{7,11},{8,12},{9,13},{1... | collective-permute-start | bytes 1572872 | tf_op jit(solution)/shard_map/ppermute | solution.py:186
  11.5 14.0 %collective-permute-start.14 = (s32[128,8]{0,1:T(8,128)S(1)}, s32[128,8]{0,1:T(8,128)S(1)}, u32[]{:S(2)}, u32[]{:S(2)}) collective-permute-start(s32[128,8]{0,1:T(8,128)S(1)} %copy-done.1), channel_id=1, source_target_pairs={{0,1},{1,0},{2,3},{3,2},{4,5},{5,4},{6,7},{7,6},{8,9},{9,8},{10,11... | collective-permute-start | bytes 12296 | tf_op jit(solution)/shard_map/ppermute | solution.py:183
  12.1 14.5 %collective-permute-start.15 = (s32[128,8]{0,1:T(8,128)S(1)}, s32[128,8]{0,1:T(8,128)S(1)}, u32[]{:S(2)}, u32[]{:S(2)}) collective-permute-start(s32[128,8]{0,1:T(8,128)S(1)} %copy-done.1), channel_id=1, source_target_pairs={{0,16},{1,17},{2,18},{3,19},{4,20},{5,21},{6,22},{7,23},{8,24},{9,... | collective-permute-start | bytes 12296 | tf_op jit(solution)/shard_map/ppermute | solution.py:183
  12.4 28.0 %collective-permute-start = (bf16[512,512]{1,0:T(8,128)(2,1)}, bf16[512,512]{1,0:T(8,128)(2,1)}, u32[]{:S(2)}, u32[]{:S(2)}) collective-permute-start(bf16[512,512]{1,0:T(8,128)(2,1)} %get-tuple-element.23), channel_id=1, source_target_pairs={{0,1},{1,0},{2,3},{3,2},{4,5},{5,4},{6,7},{7,6},{8,9},{9,8},{10,11... | collective-permute-start | bytes 1572872 | tf_op jit(solution)/shard_map/ppermute | solution.py:183
  20.9 0.8 copy-start.2
  21.7 13.3 %collective-permute-start.3 = (bf16[512,512]{1,0:T(8,128)(2,1)}, bf16[512,512]{1,0:T(8,128)(2,1)}, u32[]{:S(2)}, u32[]{:S(2)}) collective-permute-start(bf16[512,512]{1,0:T(8,128)(2,1)} %get-tuple-element.12), channel_id=1, source_target_pairs={{0,16},{1,17},{2,18},{3,19},{4,20},{5,21},{6,22},{7,23},{8,24},{9,... | collective-permute-start | bytes 1572872 | tf_op jit(solution)/shard_map/ppermute | solution.py:183
  23.7 21.8 %copy-start.10 = (s32[15]{0:T(128)S(1)}, s32[15]{0:T(128)}, u32[]{:S(2)}) copy-start(s32[15]{0:T(128)} %constant.132.clone.tidx_ref) | copy-start | bytes 184
  23.7 21.8 %copy-start.11 = (s32[15]{0:T(128)S(1)}, s32[15]{0:T(128)}, u32[]{:S(2)}) copy-start(s32[15]{0:T(128)} %constant.133.clone.widx_ref) | copy-start | bytes 184
  25.5 16.6 %collective-permute-start.10 = (bf16[512,512]{1,0:T(8,128)(2,1)}, bf16[512,512]{1,0:T(8,128)(2,1)}, u32[]{:S(2)}, u32[]{:S(2)}) collective-permute-start(bf16[512,512]{1,0:T(8,128)(2,1)} %collective-permute-done.8.refs_7_.refs_8_.refs_9_.refs_10_), channel_id=1, source_target_pairs={{0,4},{1,5},{2,6},{3,7},{4,8},{5,9},{6,10},{7,11},{8,12},{9,13},{1... | collective-permute-start | bytes 1572872 | tf_op jit(solution)/shard_map/ppermute | solution.py:186
  25.5 19.1 %collective-permute-start.1 = (bf16[512,512]{1,0:T(8,128)(2,1)}, bf16[512,512]{1,0:T(8,128)(2,1)}, u32[]{:S(2)}, u32[]{:S(2)}) collective-permute-start(bf16[512,512]{1,0:T(8,128)(2,1)} %get-tuple-element.22), channel_id=1, source_target_pairs={{0,1},{1,0},{2,3},{3,2},{4,5},{5,4},{6,7},{7,6},{8,9},{9,8},{10,11... | collective-permute-start | bytes 1572872 | tf_op jit(solution)/shard_map/ppermute | solution.py:183
  26.6 18.3 %collective-permute-start.7 = (bf16[512,512]{1,0:T(8,128)(2,1)S(1)}, bf16[512,512]{1,0:T(8,128)(2,1)}, u32[]{:S(2)}, u32[]{:S(2)}) collective-permute-start(bf16[512,512]{1,0:T(8,128)(2,1)S(1)} %pad_maximum_fusion.refs_5_.refs_6_.refs_7_.refs_8_), channel_id=1, source_target_pairs={{0,2},{1,3},{2,0},{3,1},{4,6},{5,7},{6,4},{7,5},{8,10},{9,11},{10,... | collective-permute-start | bytes 1572872 | tf_op jit(solution)/shard_map/ppermute | solution.py:183
  34.9 4.2 %collective-permute-start.16 = (s32[128,8]{0,1:T(8,128)S(1)}, s32[128,8]{0,1:T(8,128)S(1)}, u32[]{:S(2)}, u32[]{:S(2)}) collective-permute-start(s32[128,8]{0,1:T(8,128)S(1)} %copy-done.1), channel_id=1, source_target_pairs={{0,17},{1,16},{2,19},{3,18},{4,21},{5,20},{6,23},{7,22},{8,25},{9,... | collective-permute-start | bytes 12296 | tf_op jit(solution)/shard_map/ppermute | solution.py:183
  39.2 18.7 %collective-permute-start.9 = (bf16[512,512]{1,0:T(8,128)(2,1)}, bf16[512,512]{1,0:T(8,128)(2,1)}, u32[]{:S(2)}, u32[]{:S(2)}) collective-permute-start(bf16[512,512]{1,0:T(8,128)(2,1)} %collective-permute-done.8.refs_7_.refs_8_.refs_9_.refs_10_), channel_id=1, source_target_pairs={{0,2},{1,3},{2,0},{3,1},{4,6},{5,7},{6,4},{7,5},{8,10},{9,11},{10,... | collective-permute-start | bytes 1572872 | tf_op jit(solution)/shard_map/ppermute | solution.py:183
  40.4 14.7 %collective-permute-start.4 = (bf16[512,512]{1,0:T(8,128)(2,1)}, bf16[512,512]{1,0:T(8,128)(2,1)}, u32[]{:S(2)}, u32[]{:S(2)}) collective-permute-start(bf16[512,512]{1,0:T(8,128)(2,1)} %get-tuple-element.13), channel_id=1, source_target_pairs={{0,17},{1,16},{2,19},{3,18},{4,21},{5,20},{6,23},{7,22},{8,25},{9,... | collective-permute-start | bytes 1572872 | tf_op jit(solution)/shard_map/ppermute | solution.py:183
  42.0 15.8 %collective-permute-start.12 = (bf16[512,512]{1,0:T(8,128)(2,1)}, bf16[512,512]{1,0:T(8,128)(2,1)}, u32[]{:S(2)}, u32[]{:S(2)}) collective-permute-start(bf16[512,512]{1,0:T(8,128)(2,1)} %collective-permute-done.10.refs_10_.refs_11_.refs_12_), channel_id=1, source_target_pairs={{0,4},{1,5},{2,6},{3,7},{4,8},{5,9},{6,10},{7,11},{8,12},{9,13},{1... | collective-permute-start | bytes 1572872 | tf_op jit(solution)/shard_map/ppermute | solution.py:186
  44.6 1.0 %copy-start.3 = (bf16[512,512]{1,0:T(8,128)(2,1)S(1)}, bf16[512,512]{1,0:T(8,128)(2,1)}, u32[]{:S(2)}) copy-start(bf16[512,512]{1,0:T(8,128)(2,1)} %copy-done.2) | copy-start | bytes 1572868
  44.6 23.1 %collective-permute-start.11 = (bf16[512,512]{1,0:T(8,128)(2,1)}, bf16[512,512]{1,0:T(8,128)(2,1)S(1)}, u32[]{:S(2)}, u32[]{:S(2)}) collective-permute-start(bf16[512,512]{1,0:T(8,128)(2,1)} %collective-permute-done.10.refs_10_.refs_11_.refs_12_), channel_id=1, source_target_pairs={{0,2},{1,3},{2,0},{3,1},{4,6},{5,7},{6,4},{7,5},{8,10},{9,11},{10,... | collective-permute-start | bytes 1572872 | tf_op jit(solution)/shard_map/ppermute | solution.py:183
  45.6 9.4 %copy-start.14 = (bf16[512,512]{1,0:T(8,128)(2,1)S(1)}, bf16[512,512]{1,0:T(8,128)(2,1)}, u32[]{:S(2)}) copy-start(bf16[512,512]{1,0:T(8,128)(2,1)} %get-tuple-element.14) | copy-start | bytes 1572868
  45.6 12.2 %copy-start.8 = (s32[15]{0:T(128)S(1)}, s32[15]{0:T(128)}, u32[]{:S(2)}) copy-start(s32[15]{0:T(128)} %constant.134.clone.tidx_ref) | copy-start | bytes 184
  45.6 12.2 %copy-start.9 = (s32[15]{0:T(128)S(1)}, s32[15]{0:T(128)}, u32[]{:S(2)}) copy-start(s32[15]{0:T(128)} %constant.135.clone.widx_ref) | copy-start | bytes 184
  55.1 12.6 %copy-start.6 = (s32[19]{0:T(128)S(1)}, s32[19]{0:T(128)}, u32[]{:S(2)}) copy-start(s32[19]{0:T(128)} %constant.136.clone.tidx_ref) | copy-start | bytes 232
  55.1 12.7 %copy-start.7 = (s32[19]{0:T(128)S(1)}, s32[19]{0:T(128)}, u32[]{:S(2)}) copy-start(s32[19]{0:T(128)} %constant.137.clone.widx_ref) | copy-start | bytes 232
  55.1 24.7 %collective-permute-start.5 = (bf16[512,512]{1,0:T(8,128)(2,1)S(1)}, bf16[512,512]{1,0:T(8,128)(2,1)S(1)}, u32[]{:S(2)}, u32[]{:S(2)}) collective-permute-start(bf16[512,512]{1,0:T(8,128)(2,1)S(1)} %copy-done.14), channel_id=1, source_target_pairs={{0,17},{1,16},{2,19},{3,18},{4,21},{5,20},{6,23},{7,22},{8,25},{9,... | collective-permute-start | bytes 1572872 | tf_op jit(solution)/shard_map/ppermute | solution.py:183
  57.8 22.0 %collective-permute-start.13 = (bf16[512,512]{1,0:T(8,128)(2,1)}, bf16[512,512]{1,0:T(8,128)(2,1)S(1)}, u32[]{:S(2)}, u32[]{:S(2)}) collective-permute-start(bf16[512,512]{1,0:T(8,128)(2,1)} %collective-permute-done.12.refs_13_.refs_14_), channel_id=1, source_target_pairs={{0,2},{1,3},{2,0},{3,1},{4,6},{5,7},{6,4},{7,5},{8,10},{9,11},{10,... | collective-permute-start | bytes 1572872 | tf_op jit(solution)/shard_map/ppermute | solution.py:183
  67.7 12.1 %copy-start.4 = (s32[15]{0:T(128)S(1)}, s32[15]{0:T(128)}, u32[]{:S(2)}) copy-start(s32[15]{0:T(128)} %constant.138.clone.tidx_ref) | copy-start | bytes 184
  67.7 12.1 %copy-start.5 = (s32[15]{0:T(128)S(1)}, s32[15]{0:T(128)}, u32[]{:S(2)}) copy-start(s32[15]{0:T(128)} %constant.139.clone.widx_ref) | copy-start | bytes 184
  90.7 3.3 %collective-permute-start.17 = (bf16[512,128]{1,0:T(8,128)(2,1)S(1)}, bf16[512,128]{1,0:T(8,128)(2,1)S(1)}, u32[]{:S(2)}, u32[]{:S(2)}) collective-permute-start(bf16[512,128]{1,0:T(8,128)(2,1)S(1)} %get-tuple-element.16), channel_id=1, source_target_pairs={{0,1},{1,0},{2,3},{3,2},{4,5},{5,4},{6,7},{7,6},{8,9},{9,8},{10,11... | collective-permute-start | bytes 393224 | tf_op jit(solution)/shard_map/ppermute | solution.py:183
  91.9 5.1 %collective-permute-start.18 = (bf16[512,128]{1,0:T(8,128)(2,1)S(1)}, bf16[512,128]{1,0:T(8,128)(2,1)S(1)}, u32[]{:S(2)}, u32[]{:S(2)}) collective-permute-start(bf16[512,128]{1,0:T(8,128)(2,1)S(1)} %get-tuple-element.17), channel_id=1, source_target_pairs={{0,16},{1,17},{2,18},{3,19},{4,20},{5,21},{6,22},{7,23},{8,24},{9,... | collective-permute-start | bytes 393224 | tf_op jit(solution)/shard_map/ppermute | solution.py:183
  92.2 7.8 %collective-permute-start.19 = (bf16[512,128]{1,0:T(8,128)(2,1)S(1)}, bf16[512,128]{1,0:T(8,128)(2,1)S(1)}, u32[]{:S(2)}, u32[]{:S(2)}) collective-permute-start(bf16[512,128]{1,0:T(8,128)(2,1)S(1)} %get-tuple-element.18), channel_id=1, source_target_pairs={{0,17},{1,16},{2,19},{3,18},{4,21},{5,20},{6,23},{7,22},{8,25},{9,... | collective-permute-start | bytes 393224 | tf_op jit(solution)/shard_map/ppermute | solution.py:183

commit v3 on v0

v3 whole, which is shorter than its diff:
```python
import functools

import jax
import jax.numpy as jnp
from jax import lax
from jax.experimental import pallas as pl
from jax.experimental.pallas import tpu as pltpu
from jax.sharding import PartitionSpec as P

SEG_DEV = 2
LANES = 128
CORES = 2
SIDES = 2
QUAD = 4
CHUNKS = 4
BOTH = ("groups", "expert")
MIB = 1024 * 1024
VMEM = pl.BlockSpec(memory_space=pltpu.VMEM)
SMEM = pl.BlockSpec(memory_space=pltpu.SMEM)
HBM = pl.BlockSpec(memory_space=pl.ANY)
QUICK = pl.CostEstimate(flops=1, bytes_accessed=1, transcendentals=0)


def columns_of(ref, who, width):
    return ref.at[..., pl.ds(pl.multiple_of(who * width, width), width)]


def weights_kernel(who_ref, weight_ref, grads_ref, mine_ref, core_ref, chunk_ref, stage, sems):
    width = mine_ref.shape[0]
    part = chunk_ref.shape[0]
    one = pltpu.make_async_copy(columns_of(weight_ref, who_ref[1], width), stage.at[0], sems.at[0])
    two = pltpu.make_async_copy(columns_of(weight_ref, who_ref[0], width), stage.at[1], sems.at[1])
    cut = pltpu.make_async_copy(
        columns_of(grads_ref.at[pl.ds(0, part)], who_ref[2], width), chunk_ref, sems.at[2]
    )
    one.start()
    two.start()
    cut.start()
    one.wait()
    core_ref[...] = stage[0].T
    two.wait()
    mine_ref[...] = stage[1].T
    cut.wait()


def tokens_kernel(plan, who_ref, grads_ref, *refs):
    outs, sems = refs[:-1], refs[-1]
    copies = []
    for i, (out, (who, first)) in enumerate(zip(outs, plan)):
        part, _, width = out.shape
        source = columns_of(grads_ref.at[pl.ds(first, part)], who_ref[who], width)
        copies.append(pltpu.make_async_copy(source, out, sems.at[i]))
    for copy in copies:
        copy.start()
    for copy in copies:
        copy.wait()


def partial_kernel(rank, loops, new_tokens, new_units, fresh, who_ref, bases_ref, routes_ref, *refs):
    token_refs, refs = refs[: len(new_tokens)], refs[len(new_tokens) :]
    unit_refs, refs = refs[: len(new_units)], refs[len(new_units) :]
    if fresh:
        grads_ref, tokens, units, total, stage, sem = refs
        width = units.shape[1]
        copy = pltpu.make_async_copy(columns_of(grads_ref, who_ref[0], width), stage, sem)
        copy.start()
        total[...] = jnp.zeros_like(total)
        copy.wait()
        pairs = stage.shape[0] * stage.shape[1]
        tokens[0:pairs, :] = stage[...].reshape(pairs, width)
    else:
        tokens, units, total = refs[3:6]
    for ref, first in zip(token_refs, new_tokens):
        tokens[first : first + ref.shape[0], :] = ref[...]
    for ref, place in zip(unit_refs, new_units):
        units[place] = ref[...]
    cols = units.shape[2]
    lane = lax.broadcasted_iota(jnp.int32, (1, LANES), 1) // rank
    per_tile = LANES // rank
    for rows, first_t, count_t, first_w, count_w, both in loops:

        def step(i, carry, rows=rows, first_t=first_t, count_t=count_t, first_w=first_w, both=both):
            here = pl.ds(pl.multiple_of((first_t + i % count_t) * rows, rows), rows)
            place = first_w + (i // count_t) * both
            chosen = routes_ref[here, :]
            grads = tokens[here, :]
            added = total[here, :]
            for more in range(both):
                dense = jnp.dot(grads, units[place + more], preferred_element_type=jnp.float32)
                base = bases_ref[place + more]
                for j in range(cols // LANES):
                    added = added + jnp.where(
                        chosen == base + j * per_tile + lane,
                        dense[:, j * LANES : (j + 1) * LANES],
                        0.0,
                    )
            total[here, :] = added
            return carry

        lax.fori_loop(0, count_t * count_w // both, step, 0)


def accumulate(state, who, bases, routes, tokens, units, loops, rank, grads=None, places=0):
    fresh = state is None
    operands = [who, bases, routes, *[a for a, _ in tokens], *[a for a, _ in units]]
    specs = [SMEM, SMEM] + [VMEM] * (len(operands) - 2)
    scratch = []
    if fresh:
        operands.append(grads)
        specs.append(HBM)
        count, tops, whole = grads.shape
        width = whole // QUAD
        scratch = [pltpu.VMEM((count, tops, width), jnp.bfloat16), pltpu.SemaphoreType.DMA]
        shapes = [
            jax.ShapeDtypeStruct((routes.shape[0], width), jnp.bfloat16),
            jax.ShapeDtypeStruct((places, *units[0][0].shape), jnp.bfloat16),
            jax.ShapeDtypeStruct((routes.shape[0], LANES), jnp.float32),
        ]
        aliases = {}
    else:
        aliases = {len(operands) + i: i for i in range(3)}
        operands += state
        specs += [VMEM] * 3
        shapes = [jax.ShapeDtypeStruct(a.shape, a.dtype) for a in state]
    return pl.pallas_call(
        functools.partial(
            partial_kernel, rank, loops, [f for _, f in tokens], [p for _, p in units], fresh
        ),
        out_shape=shapes,
        in_specs=specs,
        out_specs=[VMEM] * 3,
        scratch_shapes=scratch,
        input_output_aliases=aliases,
        compiler_params=pltpu.CompilerParams(vmem_limit_bytes=36 * MIB),
        cost_estimate=QUICK,
    )(*operands)


def fold_kernel(rank, total_ref, own_ref, *send_refs):
    half = own_ref.shape[0]
    low = lax.broadcasted_iota(jnp.int32, (half, LANES), 1) < rank
    for i, out in enumerate([own_ref, *send_refs]):
        one = total_ref[2 * half * i : 2 * half * i + half, :]
        two = total_ref[2 * half * i + half : 2 * half * (i + 1), :]
        one = one + pltpu.roll(one, rank, 1)
        two = two + pltpu.roll(two, rank, 1)
        out[...] = jnp.where(low, one, two).astype(out.dtype)


def fold(total, rank):
    half = total.shape[0] // QUAD // 2
    return pl.pallas_call(
        functools.partial(fold_kernel, rank),
        out_shape=[jax.ShapeDtypeStruct((half, LANES), jnp.float32)]
        + [jax.ShapeDtypeStruct((half, LANES), jnp.bfloat16)] * (QUAD - 1),
        in_specs=[VMEM],
        out_specs=[VMEM] * QUAD,
        compiler_params=pltpu.CompilerParams(vmem_limit_bytes=16 * MIB),
        cost_estimate=QUICK,
    )(total)


def blocks_kernel(
    tops, rank, routes_ref, basis_ref, own_ref, b_ref, c_ref, d_ref, out_ref, pairs, turned, spread
):
    half = own_ref.shape[0]
    tokens = 2 * half // tops
    total = own_ref[...]
    for ref in (b_ref, c_ref, d_ref):
        total = total + ref[...].astype(jnp.float32)
    total = total.astype(jnp.bfloat16).astype(jnp.float32)
    pairs[0:half, :] = total
    pairs[half : 2 * half, :] = pltpu.roll(total, rank, 1)
    for k in range(tops):
        turned[k] = pairs[pl.ds(k, tokens, stride=tops), :].T[0:rank, :]
    experts = out_ref.shape[1]

    def expand(tile, carry):
        first = pl.multiple_of(tile * 8, 8)
        ids = first + lax.broadcasted_iota(jnp.int32, (8, tokens), 0)
        masks = [routes_ref[k : k + 1, :] == ids for k in range(tops)]
        for r in range(rank):
            value = jnp.zeros((8, tokens), jnp.float32)
            for k in range(tops):
                value = jnp.where(masks[k], turned[k, r : r + 1, :], value)
            spread[r, pl.ds(first, 8), :] = value
        return carry

    lax.fori_loop(0, experts // 8, expand, 0)
    for pair in range(rank // 2):
        both = jnp.concatenate([spread[2 * pair], spread[2 * pair + 1]], axis=1)
        block = jnp.dot(
            both.astype(jnp.bfloat16), basis_ref[...], preferred_element_type=jnp.float32
        ).astype(jnp.bfloat16)
        for s in range(SEG_DEV):
            out_ref[s, :, pl.ds(pair * 2 * rank, 2 * rank)] = block[
                :, s * 2 * rank : (s + 1) * 2 * rank
            ]


def local(hidden_in, out_grads, routes, segments, in_proj, out_proj):
    tokens, tops = routes.shape
    exp_here, rank, width = out_proj.shape
    owners, groups = lax.axis_size("expert"), lax.axis_size("groups")
    experts = exp_here * owners
    pairs = tokens * tops
    quarter = width // QUAD
    cols = exp_here * rank
    group, index = lax.axis_index("groups"), lax.axis_index("expert")
    core, chip = index % CORES, index // CORES
    chips = owners // CORES
    slots = chips // 2
    mine = (group % SIDES) * CORES + core
    who = jnp.stack([mine, mine ^ 1, mine ^ 2, mine ^ 3]).astype(jnp.int32)

    def swap(array, side, bit):
        table = [
            (g * owners + e, (g ^ side) * owners + (e ^ bit))
            for g in range(groups)
            for e in range(owners)
        ]
        return lax.ppermute(array, BOTH, table)

    def onward(array):
        return lax.ppermute(
            array, "expert", [(e, (e + 2 * CORES) % owners) for e in range(owners)]
        )

    def tie(*arrays):
        return lax.optimization_barrier(arrays)

    part = tokens // 2
    rows = part * tops
    chunk_shape = jax.ShapeDtypeStruct((part, tops, quarter), jnp.bfloat16)
    unit_shape = jax.ShapeDtypeStruct((quarter, cols), jnp.bfloat16)
    mine_unit, core_unit, first_chunk = pl.pallas_call(
        weights_kernel,
        out_shape=[unit_shape, unit_shape, chunk_shape],
        in_specs=[SMEM, HBM, HBM],
        out_specs=[VMEM, VMEM, HBM],
        scratch_shapes=[
            pltpu.VMEM((2, cols, quarter), jnp.bfloat16),
            pltpu.SemaphoreType.DMA((3,)),
        ],
        compiler_params=pltpu.CompilerParams(vmem_limit_bytes=16 * MIB),
        cost_estimate=QUICK,
    )(who, out_proj.reshape(cols, width), out_grads)
    other_unit = swap(core_unit, 0, 1)
    chunks = {0: swap(first_chunk.reshape(rows, quarter), 1, 0)}
    later_who, later_first, _ = tie(who, out_grads, mine_unit)
    for_core, *cut = pl.pallas_call(
        functools.partial(tokens_kernel, [(1, 0), (2, part), (3, 0), (3, part)]),
        out_shape=[jax.ShapeDtypeStruct((tokens, tops, quarter), jnp.bfloat16)] + [chunk_shape] * 3,
        in_specs=[SMEM, HBM],
        out_specs=[HBM] * 4,
        scratch_shapes=[pltpu.SemaphoreType.DMA((4,))],
        compiler_params=pltpu.CompilerParams(vmem_limit_bytes=16 * MIB),
        cost_estimate=QUICK,
    )(later_who, later_first)
    cut = [None] + [piece.reshape(rows, quarter) for piece in cut]
    chunks[1] = swap(cut[1], 1, 0)
    from_core = swap(for_core.reshape(pairs, quarter), 0, 1)

    all_routes = jnp.concatenate(
        [routes.reshape(pairs)]
        + [swap(routes, side, bit).reshape(pairs) for side, bit in ((0, 1), (1, 0), (1, 1))]
    )
    wide_routes = jnp.broadcast_to(all_routes[:, None], (QUAD * pairs, LANES))

    base_list = [(chip * CORES + core) * exp_here, (chip * CORES + 1 - core) * exp_here]
    for slot in range(slots):
        here = (chip - 2 * slot) % chips
        after = (chip - 2 * (slot + 1)) % chips
        for flip in (0, 1):
            at_core = core ^ flip
            base_list.append(((here ^ 1) * CORES + at_core) * exp_here)
            if slot + 1 < slots:
                base_list.append((after * CORES + at_core) * exp_here)
    bases = jnp.stack(base_list).astype(jnp.int32)
    places = len(base_list)

    line = [mine_unit, other_unit]
    across = [swap(line[0], 0, CORES), swap(line[1], 0, CORES)]
    ahead = [onward(line[0]), onward(line[1])]
    call = functools.partial(accumulate, who=who, bases=bases, routes=wide_routes, rank=rank)
    own_blocks = pairs // rows
    state = call(
        None,
        tokens=[],
        units=[(line[0], 0), (line[1], 1)],
        loops=[(pairs, 0, 1, 0, 2, 1)],
        grads=out_grads,
        places=places,
    )
    known_units = 2
    known_blocks = own_blocks

    def block_loops(first_w, count_w):
        double = known_blocks // 2
        loops = [(2 * rows, 0, double, first_w, count_w, 1)]
        if known_blocks % 2:
            loops.append((rows, known_blocks - 1, 1, first_w, count_w, 1))
        return loops

    state = call(
        state,
        tokens=[(from_core, pairs)],
        units=[],
        loops=[(pairs, 1, 1, 0, 2, 1)],
    )
    known_blocks = 2 * own_blocks
    for slot in range(slots):
        for chain in range(2):
            arrived = [(across[chain], known_units)]
            count = 1
            if slot + 1 < slots:
                line[chain], *state = tie(ahead[chain], *state)
                if slot + 2 < slots:
                    ahead[chain] = onward(line[chain])
                across[chain] = swap(line[chain], 0, CORES)
                arrived.append((line[chain], known_units + 1))
                count = 2
            state = call(state, tokens=[], units=arrived, loops=block_loops(known_units, count))
            known_units += count
            take = slot if (chain == 0 and slot < CHUNKS - 1) else None
            if slot == slots - 1 and chain == 1:
                take = CHUNKS - 1
            if take is not None:
                if take + 2 < CHUNKS:
                    nxt, chunk, *state = tie(cut[take + 2], chunks[take], *state)
                    chunks[take + 2] = swap(nxt, 1, 1)
                    chunks[take] = chunk
                state = call(
                    state,
                    tokens=[(chunks[take], known_blocks * rows)],
                    units=[],
                    loops=[(rows, known_blocks, 1, 0, known_units // 2 * 2, 2)]
                    + ([(rows, known_blocks, 1, known_units - 1, 1, 1)] if known_units % 2 else []),
                )
                known_blocks += 1

    own, for_core, for_side, for_diagonal = fold(state[2], rank)
    from_core = swap(for_core, 0, 1)
    from_side = swap(for_side, 1, 0)
    from_diagonal = swap(for_diagonal, 1, 1)

    projected = lax.dot_general(
        hidden_in, in_proj, (((1,), (1,)), ((), ())), preferred_element_type=jnp.float32
    ).astype(jnp.bfloat16)
    local_seg = segments - index * SEG_DEV
    seg_mask = (local_seg[:, None] == jnp.arange(SEG_DEV, dtype=jnp.int32)[None, :]).astype(
        jnp.bfloat16
    )
    picked = seg_mask[:, :, None] * projected[:, None, :]
    parity = jnp.eye(2, dtype=jnp.bfloat16)
    basis = (parity[:, None, None, :, None] * picked[None, :, :, None, :]).reshape(
        2 * tokens, SEG_DEV * 2 * rank
    )
    return pl.pallas_call(
        functools.partial(blocks_kernel, tops, rank),
        out_shape=jax.ShapeDtypeStruct((SEG_DEV, experts, rank * rank), jnp.bfloat16),
        in_specs=[VMEM] * 6,
        out_specs=VMEM,
        scratch_shapes=[
            pltpu.VMEM((pairs, LANES), jnp.float32),
            pltpu.VMEM((tops, rank, tokens), jnp.float32),
            pltpu.VMEM((rank, experts, tokens), jnp.float32),
        ],
        compiler_params=pltpu.CompilerParams(vmem_limit_bytes=40 * MIB),
        cost_estimate=QUICK,
    )(routes.T, basis, own, from_core, from_side, from_diagonal)


def solution(mesh):
    placed = (
        P(("groups", "expert"), None),
        P(("groups", "expert"), None, None),
        P(("groups", "expert"), None),
        P(("groups", "expert")),
        P(),
        P("expert", None, None),
    )
    return jax.shard_map(
        local,
        mesh=mesh,
        in_specs=placed,
        out_specs=P(("groups", "expert"), None, None),
        check_vma=False,
    )
```

time: 256 us -> 121 us (0.47)
  waiting for transfers between devices: 118 us -> 21.6 us
  other arithmetic: 51.4 us -> 0.27 us
  Pallas kernels: 0 us -> 47.2 us
  local copies, waits for them, and re-layouts: 41.6 us -> 22.7 us
  starting transfers between devices: 35.2 us -> 27.2 us
  matrix products: 7.92 us -> 0.75 us
    all_to_all x2 -> x0, waiting for transfers between devices: 118 us -> none  [the longest x1 114 us: local(): lax.all_to_all(send_grads, 'expert', split_axis=0, concat_axis=0, tiled=T...]
    pallas_call x0 -> x18, Pallas kernels: none -> 47.2 us  [the longest x14 39.5 us: accumulate(): pl.pallas_call(functools.partial(partial_kernel, rank, loops, [f for _, f...]
    gather x6 -> x0, other arithmetic: 40.7 us -> none  [the longest x3 40.7 us: local(): within = jnp.arange(pair_count, dtype=jnp.int32) - starts[sorted_routes]]
    all_to_all x2 -> x0, starting transfers between devices: 35.2 us -> none  [the longest x1 27.7 us: local(): lax.all_to_all(reduced, 'expert', split_axis=0, concat_axis=0, tiled=True)]
    ppermute x0 -> x26, starting transfers between devices: none -> 27.2 us  [the longest x20 20.4 us: swap(): return lax.ppermute(array, BOTH, table)]
    gather x8 -> x0, local copies, waits for them, and re-layouts: 26.3 us -> none  [the longest x1 15.4 us: local(): jnp.take(out_grads.reshape(pair_count, hidden_dim), slot_table, axis=0, m...]
    ppermute x0 -> x26, waiting for transfers between devices: none -> 21.6 us  [the longest x20 21.6 us: swap(): return lax.ppermute(array, BOTH, table)]
    unnamed x7 -> x40, local copies, waits for them, and re-layouts: 0.93 us -> 21.3 us
  transfers between devices with their start and end apart: 2 -> 26, of which waited for: 2 -> 7; matrix products, arithmetic and copies ran while one was open for 2% -> 2% of each run, Pallas kernels for 0% -> 29%
where the time goes in v3:
time: 121 us; the launch traced here: 120 us
  Pallas kernels  47.2 us (39%)
  starting transfers between devices  27.2 us (22%)
  local copies, waits for them, and re-layouts  22.7 us (19%)
  waiting for transfers between devices  21.6 us (18%)
    pallas_call x14, Pallas kernels, accumulate(): pl.pallas_call(functools.partial(partial_kernel, rank, loops, [f for _, f...  39.5 us
    ppermute x20, waiting for transfers between devices, swap(): return lax.ppermute(array, BOTH, table)  21.6 us
    unnamed x40, local copies, waits for them, and re-layouts  21.3 us
    ppermute x20, starting transfers between devices, swap(): return lax.ppermute(array, BOTH, table)  20.4 us
    ppermute x6, starting transfers between devices, onward(): lax.ppermute(array, 'expert', [(e, (e + 2 * CORES) % owners) for e in ran...  6.8 us
    pallas_call x1, Pallas kernels, local(): pl.pallas_call(functools.partial(blocks_kernel, tops, rank), out_shape=ja...  2.98 us
  transfers between devices with their start and end apart: 26, of which 7 were waited for; matrix products, arithmetic and copies ran while one was open for 2% of the time, Pallas kernels for 29%

profile of v3, /device:TPU:1, one launch (start us, length us, event | category | flops | bytes accessed | tf_op | source)
XLA Modules:
  0.0 120.2 jit_solution(10846292571777433268)
XLA Ops:
  0.1 2.3 %copy-done.9 = bf16[128,8,2048]{2,1,0:T(8,128)(2,1)S(1)} copy-done((bf16[128,8,2048]{2,1,0:T(8,128)(2,1)S(1)}, bf16[128,8,2048]{2,1,0:T(8,128)(2,1)}, u32[]{:S(2)}) %copy-start.9) | copy-done | bytes 4194328
  2.4 1.2 %copy-done.11 = bf16[4,64,2048]{2,1,0:T(8,128)(2,1)S(1)} copy-done((bf16[4,64,2048]{2,1,0:T(8,128)(2,1)S(1)}, bf16[4,64,2048]{2,1,0:T(8,128)(2,1)}, u32[]{:S(2)}) %copy-start.11) | copy-done | bytes 1048600
  3.6 2.2 %shard_map.64 = (bf16[512,256]{1,0:T(8,128)(2,1)}, bf16[512,256]{1,0:T(8,128)(2,1)}, bf16[64,8,512]{2,1,0:T(8,128)(2,1)}) custom-call(s32[4]{0:T(128)S(1)} %pad_add_fusion.1.who_ref, bf16[256,2048]{1,0:T(8,128)(2,1)S(1)} %bitcast.36, bf16[128,8,2048]{2,1,0:T(8,128)(2,1)S(1)} %copy-done.9), custom_call_target="tpu_custom_call" | custom-call | flops 1 | bytes 1 | tf_op jit(solution)/shard_map/pallas_call | solution.py:236
  5.8 1.9 %shard_map.65 = (bf16[128,8,512]{2,1,0:T(8,128)(2,1)}, bf16[64,8,512]{2,1,0:T(8,128)(2,1)}, bf16[64,8,512]{2,1,0:T(8,128)(2,1)}, bf16[64,8,512]{2,1,0:T(8,128)(2,1)S(1)}) custom-call(s32[4]{0:T(128)S(1)} %pad_add_fusion.1.who_ref, bf16[128,8,2048]{2,1,0:T(8,128)(2,1)S(1)} %copy-done.9), custom_call_target="tpu_custom_call" | custom-call | flops 1 | bytes 1 | tf_op jit(solution)/shard_map/pallas_call | solution.py:251
  8.6 2.7 %collective-permute-start.11 = (bf16[512,512]{1,0:T(8,128)(2,1)}, bf16[512,512]{1,0:T(8,128)(2,1)S(1)}, u32[]{:S(2)}, u32[]{:S(2)}) collective-permute-start(bf16[512,512]{1,0:T(8,128)(2,1)} %bitcast.26), channel_id=1, source_target_pairs={{0,16},{1,17},{2,18},{3,19},{4,20},{5,21},{6,22},{7,23},{8,24},{9,... | collective-permute-start | bytes 1572872 | tf_op jit(solution)/shard_map/ppermute | solution.py:222
  11.5 1.3 %collective-permute-start.4 = (bf16[512,256]{1,0:T(8,128)(2,1)}, bf16[512,256]{1,0:T(8,128)(2,1)}, u32[]{:S(2)}, u32[]{:S(2)}) collective-permute-start(bf16[512,256]{1,0:T(8,128)(2,1)} %get-tuple-element.92.refs_0_), channel_id=1, source_target_pairs={{0,4},{1,5},{2,6},{3,7},{4,8},{5,9},{6,10},{7,11},{8,12},{9,13},{1... | collective-permute-start | bytes 786440 | tf_op jit(solution)/shard_map/ppermute | solution.py:225
  14.4 9.4 %collective-permute-done.1 = s32[128,8]{0,1:T(8,128)S(1)} collective-permute-done((s32[128,8]{0,1:T(8,128)S(1)}, s32[128,8]{0,1:T(8,128)S(1)}, u32[]{:S(2)}, u32[]{:S(2)}) %collective-permute-start.1) | collective-permute-done | bytes 4128 | tf_op jit(solution)/shard_map/ppermute | solution.py:222
  23.8 1.9 %collective-permute-start.2 = (s32[128,8]{0,1:T(8,128)S(1)}, s32[128,8]{0,1:T(8,128)S(1)}, u32[]{:S(2)}, u32[]{:S(2)}) collective-permute-start(s32[128,8]{0,1:T(8,128)S(1)} %copy-done.14), channel_id=1, source_target_pairs={{0,17},{1,16},{2,19},{3,18},{4,21},{5,20},{6,23},{7,22},{8,25},{9,... | collective-permute-start | bytes 12296 | tf_op jit(solution)/shard_map/ppermute | solution.py:222
  25.8 1.3 %collective-permute-done.2 = s32[128,8]{0,1:T(8,128)S(1)} collective-permute-done((s32[128,8]{0,1:T(8,128)S(1)}, s32[128,8]{0,1:T(8,128)S(1)}, u32[]{:S(2)}, u32[]{:S(2)}) %collective-permute-start.2) | collective-permute-done | bytes 4128 | tf_op jit(solution)/shard_map/ppermute | solution.py:222
  27.1 1.5 %collective-permute-start.12 = (bf16[512,256]{1,0:T(8,128)(2,1)}, bf16[512,256]{1,0:T(8,128)(2,1)}, u32[]{:S(2)}, u32[]{:S(2)}) collective-permute-start(bf16[512,256]{1,0:T(8,128)(2,1)} %get-tuple-element.92.refs_0_), channel_id=1, source_target_pairs={{0,2},{1,3},{2,0},{3,1},{4,6},{5,7},{6,4},{7,5},{8,10},{9,11},{10,... | collective-permute-start | bytes 786440 | tf_op jit(solution)/shard_map/ppermute | solution.py:222
  29.5 1.3 %collective-permute-start.10 = (bf16[512,256]{1,0:T(8,128)(2,1)}, bf16[512,256]{1,0:T(8,128)(2,1)}, u32[]{:S(2)}, u32[]{:S(2)}) collective-permute-start(bf16[512,256]{1,0:T(8,128)(2,1)} %collective-permute-done.6.refs_1_), channel_id=1, source_target_pairs={{0,4},{1,5},{2,6},{3,7},{4,8},{5,9},{6,10},{7,11},{8,12},{9,13},{1... | collective-permute-start | bytes 786440 | tf_op jit(solution)/shard_map/ppermute | solution.py:225
  31.4 2.2 %copy-done.10 = bf16[128,8,2048]{2,1,0:T(8,128)(2,1)S(1)} copy-done((bf16[128,8,2048]{2,1,0:T(8,128)(2,1)S(1)}, bf16[128,8,2048]{2,1,0:T(8,128)(2,1)}, u32[]{:S(2)}) %copy-start.10) | copy-done | bytes 4194328
  33.6 2.7 %shard_map.66 = (bf16[4096,512]{1,0:T(8,128)(2,1)S(1)}, bf16[16,512,256]{2,1,0:T(8,128)(2,1)S(1)}, f32[4096,128]{1,0:T(8,128)S(1)}) custom-call(s32[4]{0:T(128)S(1)} %pad_add_fusion.1.who_ref, s32[16]{0:T(128)S(1)} %stack.87.bases_ref, s32[4096,128]{1,0:T(8,128)S(1)} %broadcast_in_dim.2.routes_ref, bf16[512,256]{1,0:T(8,128)(2,1)} %get-tuple-element.92.refs_0_, ...), custom_call_target="tpu_custom_call" | custom-call | flops 1 | bytes 1 | tf_op jit(solution)/shard_map/pallas_call | solution.py:125
  36.6 1.5 %shard_map.67 = (bf16[4096,512]{1,0:T(8,128)(2,1)S(1)}, bf16[16,512,256]{2,1,0:T(8,128)(2,1)S(1)}, f32[4096,128]{1,0:T(8,128)S(1)}) custom-call(s32[4]{0:T(128)S(1)} %pad_add_fusion.1.who_ref, s32[16]{0:T(128)S(1)} %stack.87.bases_ref, s32[4096,128]{1,0:T(8,128)S(1)} %broadcast_in_dim.2.routes_ref, ...), custom_call_target="tpu_custom_call", output_to_operand_aliasing={{0}: (4, {}), {1}: (5, {}), {2}: (6, {})} | custom-call | flops 1 | bytes 1 | tf_op jit(solution)/shard_map/pallas_call | solution.py:125
  38.1 1.4 %collective-permute-start.8 = (bf16[512,256]{1,0:T(8,128)(2,1)}, bf16[512,256]{1,0:T(8,128)(2,1)}, u32[]{:S(2)}, u32[]{:S(2)}) collective-permute-start(bf16[512,256]{1,0:T(8,128)(2,1)} %collective-permute-done.4.refs_1_), channel_id=1, source_target_pairs={{0,4},{1,5},{2,6},{3,7},{4,8},{5,9},{6,10},{7,11},{8,12},{9,13},{1... | collective-permute-start | bytes 786440 | tf_op jit(solution)/shard_map/ppermute | solution.py:225
  40.3 2.8 %shard_map.68 = (bf16[4096,512]{1,0:T(8,128)(2,1)S(1)}, bf16[16,512,256]{2,1,0:T(8,128)(2,1)S(1)}, f32[4096,128]{1,0:T(8,128)S(1)}) custom-call(s32[4]{0:T(128)S(1)} %pad_add_fusion.1.who_ref, s32[16]{0:T(128)S(1)} %stack.87.bases_ref, s32[4096,128]{1,0:T(8,128)S(1)} %broadcast_in_dim.2.routes_ref, ...), custom_call_target="tpu_custom_call", output_to_operand_aliasing={{0}: (5, {}), {1}: (6, {}), {2}: (7, {})} | custom-call | flops 1 | bytes 1 | tf_op jit(solution)/shard_map/pallas_call | solution.py:125
  43.1 1.3 %collective-permute-start.7 = (bf16[512,256]{1,0:T(8,128)(2,1)}, bf16[512,256]{1,0:T(8,128)(2,1)}, u32[]{:S(2)}, u32[]{:S(2)}) collective-permute-start(bf16[512,256]{1,0:T(8,128)(2,1)} %collective-permute-done.4.refs_1_), channel_id=1, source_target_pairs={{0,2},{1,3},{2,0},{3,1},{4,6},{5,7},{6,4},{7,5},{8,10},{9,11},{10,... | collective-permute-start | bytes 786440 | tf_op jit(solution)/shard_map/ppermute | solution.py:222
  44.4 1.5 %shard_map.69 = (bf16[4096,512]{1,0:T(8,128)(2,1)S(1)}, bf16[16,512,256]{2,1,0:T(8,128)(2,1)S(1)}, f32[4096,128]{1,0:T(8,128)S(1)}) custom-call(s32[4]{0:T(128)S(1)} %pad_add_fusion.1.who_ref, s32[16]{0:T(128)S(1)} %stack.87.bases_ref, s32[4096,128]{1,0:T(8,128)S(1)} %broadcast_in_dim.2.routes_ref, ...), custom_call_target="tpu_custom_call", output_to_operand_aliasing={{0}: (4, {}), {1}: (5, {}), {2}: (6, {})} | custom-call | flops 1 | bytes 1 | tf_op jit(solution)/shard_map/pallas_call | solution.py:125
  45.9 2.0 %copy-done.1 = bf16[4096,512]{1,0:T(8,128)(2,1)} copy-done((bf16[4096,512]{1,0:T(8,128)(2,1)}, bf16[4096,512]{1,0:T(8,128)(2,1)S(1)}, u32[]{:S(2)}) %copy-start.1) | copy-done | bytes 4194328
  47.9 2.0 %copy-done.3 = bf16[16,512,256]{2,1,0:T(8,128)(2,1)} copy-done((bf16[16,512,256]{2,1,0:T(8,128)(2,1)}, bf16[16,512,256]{2,1,0:T(8,128)(2,1)S(1)}, u32[]{:S(2)}) %copy-start.3) | copy-done | bytes 4194328
  49.9 1.4 %copy-done.7 = f32[4096,128]{1,0:T(8,128)} copy-done((f32[4096,128]{1,0:T(8,128)}, f32[4096,128]{1,0:T(8,128)S(1)}, u32[]{:S(2)}) %copy-start.7) | copy-done | bytes 2097176
  51.3 1.3 %collective-permute-start.14 = (bf16[512,256]{1,0:T(8,128)(2,1)}, bf16[512,256]{1,0:T(8,128)(2,1)S(1)}, u32[]{:S(2)}, u32[]{:S(2)}) collective-permute-start(bf16[512,256]{1,0:T(8,128)(2,1)} %collective-permute-done.10.refs_1_), channel_id=1, source_target_pairs={{0,4},{1,5},{2,6},{3,7},{4,8},{5,9},{6,10},{7,11},{8,12},{9,13},{1... | collective-permute-start | bytes 786440 | tf_op jit(solution)/shard_map/ppermute | solution.py:225
  53.5 3.2 %collective-permute-start.16 = (bf16[512,512]{1,0:T(8,128)(2,1)}, bf16[512,512]{1,0:T(8,128)(2,1)S(1)}, u32[]{:S(2)}, u32[]{:S(2)}) collective-permute-start(bf16[512,512]{1,0:T(8,128)(2,1)} %bitcast.25), channel_id=1, source_target_pairs={{0,17},{1,16},{2,19},{3,18},{4,21},{5,20},{6,23},{7,22},{8,25},{9,... | collective-permute-start | bytes 1572872 | tf_op jit(solution)/shard_map/ppermute | solution.py:222
  57.5 2.2 %copy-done.2 = bf16[4096,512]{1,0:T(8,128)(2,1)S(1)} copy-done((bf16[4096,512]{1,0:T(8,128)(2,1)S(1)}, bf16[4096,512]{1,0:T(8,128)(2,1)}, u32[]{:S(2)}) %copy-start.2) | copy-done | bytes 4194328
  59.7 2.2 %copy-done.4 = bf16[16,512,256]{2,1,0:T(8,128)(2,1)S(1)} copy-done((bf16[16,512,256]{2,1,0:T(8,128)(2,1)S(1)}, bf16[16,512,256]{2,1,0:T(8,128)(2,1)}, u32[]{:S(2)}) %copy-start.4) | copy-done | bytes 4194328
  61.9 1.6 %copy-done.6 = s32[4096,128]{1,0:T(8,128)S(1)} copy-done((s32[4096,128]{1,0:T(8,128)S(1)}, s32[4096,128]{1,0:T(8,128)}, u32[]{:S(2)}) %copy-start.6) | copy-done | bytes 2097176
  63.4 1.6 %copy-done.8 = f32[4096,128]{1,0:T(8,128)S(1)} copy-done((f32[4096,128]{1,0:T(8,128)S(1)}, f32[4096,128]{1,0:T(8,128)}, u32[]{:S(2)}) %copy-start.8) | copy-done | bytes 2097176
  65.0 0.9 copy-done.13
  66.0 3.3 %shard_map.70 = (bf16[4096,512]{1,0:T(8,128)(2,1)S(1)}, bf16[16,512,256]{2,1,0:T(8,128)(2,1)S(1)}, f32[4096,128]{1,0:T(8,128)S(1)}) custom-call(s32[4]{0:T(128)S(1)} %pad_add_fusion.1.who_ref, s32[16]{0:T(128)S(1)} %stack.87.bases_ref, s32[4096,128]{1,0:T(8,128)S(1)} %copy-done.6, ...), custom_call_target="tpu_custom_call", output_to_operand_aliasing={{0}: (5, {}), {1}: (6, {}), {2}: (7, {})} | custom-call | flops 1 | bytes 1 | tf_op jit(solution)/shard_map/pallas_call | solution.py:125
  69.4 3.4 %shard_map.71 = (bf16[4096,512]{1,0:T(8,128)(2,1)S(1)}, bf16[16,512,256]{2,1,0:T(8,128)(2,1)S(1)}, f32[4096,128]{1,0:T(8,128)S(1)}) custom-call(s32[4]{0:T(128)S(1)} %pad_add_fusion.1.who_ref, s32[16]{0:T(128)S(1)} %stack.87.bases_ref, s32[4096,128]{1,0:T(8,128)S(1)} %copy-done.6, ...), custom_call_target="tpu_custom_call", output_to_operand_aliasing={{0}: (5, {}), {1}: (6, {}), {2}: (7, {})} | custom-call | flops 1 | bytes 1 | tf_op jit(solution)/shard_map/pallas_call | solution.py:125
  72.9 1.3 %collective-permute-start.17 = (bf16[512,256]{1,0:T(8,128)(2,1)}, bf16[512,256]{1,0:T(8,128)(2,1)S(1)}, u32[]{:S(2)}, u32[]{:S(2)}) collective-permute-start(bf16[512,256]{1,0:T(8,128)(2,1)} %collective-permute-done.8.refs_1_), channel_id=1, source_target_pairs={{0,2},{1,3},{2,0},{3,1},{4,6},{5,7},{6,4},{7,5},{8,10},{9,11},{10,... | collective-permute-start | bytes 786440 | tf_op jit(solution)/shard_map/ppermute | solution.py:222
  74.2 2.3 %shard_map.72 = (bf16[4096,512]{1,0:T(8,128)(2,1)S(1)}, bf16[16,512,256]{2,1,0:T(8,128)(2,1)S(1)}, f32[4096,128]{1,0:T(8,128)S(1)}) custom-call(s32[4]{0:T(128)S(1)} %pad_add_fusion.1.who_ref, s32[16]{0:T(128)S(1)} %stack.87.bases_ref, s32[4096,128]{1,0:T(8,128)S(1)} %copy-done.6, ...), custom_call_target="tpu_custom_call", output_to_operand_aliasing={{0}: (4, {}), {1}: (5, {}), {2}: (6, {})} | custom-call | flops 1 | bytes 1 | tf_op jit(solution)/shard_map/pallas_call | solution.py:125
  76.6 1.4 %collective-permute-start.15 = (bf16[512,256]{1,0:T(8,128)(2,1)S(1)}, bf16[512,256]{1,0:T(8,128)(2,1)S(1)}, u32[]{:S(2)}, u32[]{:S(2)}) collective-permute-start(bf16[512,256]{1,0:T(8,128)(2,1)S(1)} %collective-permute-done.14.refs_1_), channel_id=1, source_target_pairs={{0,4},{1,5},{2,6},{3,7},{4,8},{5,9},{6,10},{7,11},{8,12},{9,13},{1... | collective-permute-start | bytes 786440 | tf_op jit(solution)/shard_map/ppermute | solution.py:225
  78.0 0.9 collective-permute-start.13
  78.9 3.2 %shard_map.73 = (bf16[4096,512]{1,0:T(8,128)(2,1)S(1)}, bf16[16,512,256]{2,1,0:T(8,128)(2,1)S(1)}, f32[4096,128]{1,0:T(8,128)S(1)}) custom-call(s32[4]{0:T(128)S(1)} %pad_add_fusion.1.who_ref, s32[16]{0:T(128)S(1)} %stack.87.bases_ref, s32[4096,128]{1,0:T(8,128)S(1)} %copy-done.6, ...), custom_call_target="tpu_custom_call", output_to_operand_aliasing={{0}: (5, {}), {1}: (6, {}), {2}: (7, {})} | custom-call | flops 1 | bytes 1 | tf_op jit(solution)/shard_map/pallas_call | solution.py:125
  82.5 1.2 %collective-permute-start.21 = (bf16[512,256]{1,0:T(8,128)(2,1)S(1)}, bf16[512,256]{1,0:T(8,128)(2,1)S(1)}, u32[]{:S(2)}, u32[]{:S(2)}) collective-permute-start(bf16[512,256]{1,0:T(8,128)(2,1)S(1)} %collective-permute-done.18.refs_1_), channel_id=1, source_target_pairs={{0,2},{1,3},{2,0},{3,1},{4,6},{5,7},{6,4},{7,5},{8,10},{9,11},{10,... | collective-permute-start | bytes 786440 | tf_op jit(solution)/shard_map/ppermute | solution.py:222
  83.7 3.2 %shard_map.74 = (bf16[4096,512]{1,0:T(8,128)(2,1)S(1)}, bf16[16,512,256]{2,1,0:T(8,128)(2,1)S(1)}, f32[4096,128]{1,0:T(8,128)S(1)}) custom-call(s32[4]{0:T(128)S(1)} %pad_add_fusion.1.who_ref, s32[16]{0:T(128)S(1)} %stack.87.bases_ref, s32[4096,128]{1,0:T(8,128)S(1)} %copy-done.6, ...), custom_call_target="tpu_custom_call", output_to_operand_aliasing={{0}: (5, {}), {1}: (6, {}), {2}: (7, {})} | custom-call | flops 1 | bytes 1 | tf_op jit(solution)/shard_map/pallas_call | solution.py:125
  86.9 3.2 %shard_map.75 = (bf16[4096,512]{1,0:T(8,128)(2,1)S(1)}, bf16[16,512,256]{2,1,0:T(8,128)(2,1)S(1)}, f32[4096,128]{1,0:T(8,128)S(1)}) custom-call(s32[4]{0:T(128)S(1)} %pad_add_fusion.1.who_ref, s32[16]{0:T(128)S(1)} %stack.87.bases_ref, s32[4096,128]{1,0:T(8,128)S(1)} %copy-done.6, ...), custom_call_target="tpu_custom_call", output_to_operand_aliasing={{0}: (4, {}), {1}: (5, {}), {2}: (6, {})} | custom-call | flops 1 | bytes 1 | tf_op jit(solution)/shard_map/pallas_call | solution.py:125
  90.5 3.8 %shard_map.76 = (bf16[4096,512]{1,0:T(8,128)(2,1)S(1)}, bf16[16,512,256]{2,1,0:T(8,128)(2,1)S(1)}, f32[4096,128]{1,0:T(8,128)S(1)}) custom-call(s32[4]{0:T(128)S(1)} %pad_add_fusion.1.who_ref, s32[16]{0:T(128)S(1)} %stack.87.bases_ref, s32[4096,128]{1,0:T(8,128)S(1)} %copy-done.6, ...), custom_call_target="tpu_custom_call", output_to_operand_aliasing={{0}: (5, {}), {1}: (6, {}), {2}: (7, {})} | custom-call | flops 1 | bytes 1 | tf_op jit(solution)/shard_map/pallas_call | solution.py:125
  94.9 2.2 %shard_map.77 = (bf16[4096,512]{1,0:T(8,128)(2,1)S(1)}, bf16[16,512,256]{2,1,0:T(8,128)(2,1)S(1)}, f32[4096,128]{1,0:T(8,128)S(1)}) custom-call(s32[4]{0:T(128)S(1)} %pad_add_fusion.1.who_ref, s32[16]{0:T(128)S(1)} %stack.87.bases_ref, s32[4096,128]{1,0:T(8,128)S(1)} %copy-done.6, ...), custom_call_target="tpu_custom_call", output_to_operand_aliasing={{0}: (4, {}), {1}: (5, {}), {2}: (6, {})} | custom-call | flops 1 | bytes 1 | tf_op jit(solution)/shard_map/pallas_call | solution.py:125
  97.1 3.4 %collective-permute-done.20.refs_0_ = bf16[512,256]{1,0:T(8,128)(2,1)S(1)} collective-permute-done((bf16[512,256]{1,0:T(8,128)(2,1)S(1)}, bf16[512,256]{1,0:T(8,128)(2,1)S(1)}, u32[]{:S(2)}, u32[]{:S(2)}) %collective-permute-start.20) | collective-permute-done | bytes 262176 | tf_op jit(solution)/shard_map/ppermute | solution.py:222
  100.5 2.2 %shard_map.78 = (bf16[4096,512]{1,0:T(8,128)(2,1)S(1)}, bf16[16,512,256]{2,1,0:T(8,128)(2,1)S(1)}, f32[4096,128]{1,0:T(8,128)S(1)}) custom-call(s32[4]{0:T(128)S(1)} %pad_add_fusion.1.who_ref, s32[16]{0:T(128)S(1)} %stack.87.bases_ref, s32[4096,128]{1,0:T(8,128)S(1)} %copy-done.6, ...), custom_call_target="tpu_custom_call", output_to_operand_aliasing={{0}: (4, {}), {1}: (5, {}), {2}: (6, {})} | custom-call | flops 1 | bytes 1 | tf_op jit(solution)/shard_map/pallas_call | solution.py:125
  102.7 4.1 %shard_map.79 = (bf16[4096,512]{1,0:T(8,128)(2,1)S(1)}, bf16[16,512,256]{2,1,0:T(8,128)(2,1)S(1)}, f32[4096,128]{1,0:T(8,128)S(1)}) custom-call(s32[4]{0:T(128)S(1)} %pad_add_fusion.1.who_ref, s32[16]{0:T(128)S(1)} %stack.87.bases_ref, s32[4096,128]{1,0:T(8,128)S(1)} %copy-done.6, ...), custom_call_target="tpu_custom_call", output_to_operand_aliasing={{0}: (4, {}), {1}: (5, {}), {2}: (6, {})} | custom-call | flops 1 | bytes 1 | tf_op jit(solution)/shard_map/pallas_call | solution.py:125
  107.5 1.7 %collective-permute-start.23 = (bf16[512,128]{1,0:T(8,128)(2,1)S(1)}, bf16[512,128]{1,0:T(8,128)(2,1)S(1)}, u32[]{:S(2)}, u32[]{:S(2)}) collective-permute-start(bf16[512,128]{1,0:T(8,128)(2,1)S(1)} %get-tuple-element.176), channel_id=1, source_target_pairs={{0,1},{1,0},{2,3},{3,2},{4,5},{5,4},{6,7},{7,6},{8,9},{9,8},{10,11... | collective-permute-start | bytes 393224 | tf_op jit(solution)/shard_map/ppermute | solution.py:222
  109.2 1.2 %collective-permute-start.24 = (bf16[512,128]{1,0:T(8,128)(2,1)S(1)}, bf16[512,128]{1,0:T(8,128)(2,1)S(1)}, u32[]{:S(2)}, u32[]{:S(2)}) collective-permute-start(bf16[512,128]{1,0:T(8,128)(2,1)S(1)} %get-tuple-element.177), channel_id=1, source_target_pairs={{0,16},{1,17},{2,18},{3,19},{4,20},{5,21},{6,22},{7,23},{8,24},{9,... | collective-permute-start | bytes 393224 | tf_op jit(solution)/shard_map/ppermute | solution.py:222
  111.2 3.1 %collective-permute-done.24.c_ref = bf16[512,128]{1,0:T(8,128)(2,1)S(1)} collective-permute-done((bf16[512,128]{1,0:T(8,128)(2,1)S(1)}, bf16[512,128]{1,0:T(8,128)(2,1)S(1)}, u32[]{:S(2)}, u32[]{:S(2)}) %collective-permute-start.24) | collective-permute-done | bytes 131104 | tf_op jit(solution)/shard_map/ppermute | solution.py:222
  114.3 3.0 %collective-permute-done.25.d_ref = bf16[512,128]{1,0:T(8,128)(2,1)S(1)} collective-permute-done((bf16[512,128]{1,0:T(8,128)(2,1)S(1)}, bf16[512,128]{1,0:T(8,128)(2,1)S(1)}, u32[]{:S(2)}, u32[]{:S(2)}) %collective-permute-start.25) | collective-permute-done | bytes 131104 | tf_op jit(solution)/shard_map/ppermute | solution.py:222
  117.3 3.0 %shard_map.81 = bf16[2,64,4096]{2,1,0:T(8,128)(2,1)} custom-call(s32[8,128]{1,0:T(8,128)S(1)} %bitcast.37, bf16[256,256]{1,0:T(8,128)(2,1)S(1)} %copy.51.basis_ref, f32[512,128]{1,0:T(8,128)S(1)} %get-tuple-element.175.own_ref, bf16[512,128]{1,0:T(8,128)(2,1)S(1)} %collective-permute-done.23.b_ref, bf16[512,128]{1,0:T(8,128)(2,1)S(1)} %collective-permute-done.24.c_ref, ...), custom_call_target="tpu_custom_call" | custom-call | flops 1 | bytes 1 | tf_op jit(solution)/shard_map/pallas_call | solution.py:359
  (80 shorter events, 9.8 us)
Async XLA Ops:
  0.0 56.7 %copy-start = (bf16[128,7168]{1,0:T(8,128)(2,1)S(1)}, bf16[128,7168]{1,0:T(8,128)(2,1)}, u32[]{:S(2)}) copy-start(bf16[128,7168]{1,0:T(8,128)(2,1)} %param.6) | copy-start | bytes 5505028
  0.1 2.3 %copy-start.9 = (bf16[128,8,2048]{2,1,0:T(8,128)(2,1)S(1)}, bf16[128,8,2048]{2,1,0:T(8,128)(2,1)}, u32[]{:S(2)}) copy-start(bf16[128,8,2048]{2,1,0:T(8,128)(2,1)} %refs_2_.1) | copy-start | bytes 12582916
  2.4 1.2 %copy-start.11 = (bf16[4,64,2048]{2,1,0:T(8,128)(2,1)S(1)}, bf16[4,64,2048]{2,1,0:T(8,128)(2,1)}, u32[]{:S(2)}) copy-start(bf16[4,64,2048]{2,1,0:T(8,128)(2,1)} %param.11) | copy-start | bytes 3145732
  3.6 9.2 %copy-start.14 = (s32[128,8]{0,1:T(8,128)S(1)}, s32[128,8]{0,1:T(8,128)}, u32[]{:S(2)}) copy-start(s32[128,8]{0,1:T(8,128)} %param.8) | copy-start | bytes 12292
  7.7 0.8 copy-start.15
  8.5 27.8 %collective-permute-start.5 = (bf16[1024,512]{1,0:T(8,128)(2,1)}, bf16[1024,512]{1,0:T(8,128)(2,1)S(1)}, u32[]{:S(2)}, u32[]{:S(2)}) collective-permute-start(bf16[1024,512]{1,0:T(8,128)(2,1)} %bitcast.24), channel_id=1, source_target_pairs={{0,1},{1,0},{2,3},{3,2},{4,5},{5,4},{6,7},{7,6},{8,9},{9,8},{10,11... | collective-permute-start | bytes 3145736 | tf_op jit(solution)/shard_map/ppermute | solution.py:222
  8.6 34.5 %collective-permute-start.11 = (bf16[512,512]{1,0:T(8,128)(2,1)}, bf16[512,512]{1,0:T(8,128)(2,1)S(1)}, u32[]{:S(2)}, u32[]{:S(2)}) collective-permute-start(bf16[512,512]{1,0:T(8,128)(2,1)} %bitcast.26), channel_id=1, source_target_pairs={{0,16},{1,17},{2,18},{3,19},{4,20},{5,21},{6,22},{7,23},{8,24},{9,... | collective-permute-start | bytes 1572872 | tf_op jit(solution)/shard_map/ppermute | solution.py:222
  11.3 18.2 %collective-permute-start.6 = (bf16[512,256]{1,0:T(8,128)(2,1)}, bf16[512,256]{1,0:T(8,128)(2,1)}, u32[]{:S(2)}, u32[]{:S(2)}) collective-permute-start(bf16[512,256]{1,0:T(8,128)(2,1)} %get-tuple-element.98), channel_id=1, source_target_pairs={{0,1},{1,0},{2,3},{3,2},{4,5},{5,4},{6,7},{7,6},{8,9},{9,8},{10,11... | collective-permute-start | bytes 786440 | tf_op jit(solution)/shard_map/ppermute | solution.py:222
  11.5 26.6 %collective-permute-start.4 = (bf16[512,256]{1,0:T(8,128)(2,1)}, bf16[512,256]{1,0:T(8,128)(2,1)}, u32[]{:S(2)}, u32[]{:S(2)}) collective-permute-start(bf16[512,256]{1,0:T(8,128)(2,1)} %get-tuple-element.92.refs_0_), channel_id=1, source_target_pairs={{0,4},{1,5},{2,6},{3,7},{4,8},{5,9},{6,10},{7,11},{8,12},{9,13},{1... | collective-permute-start | bytes 786440 | tf_op jit(solution)/shard_map/ppermute | solution.py:225
  12.8 1.3 %collective-permute-start = (s32[128,8]{0,1:T(8,128)S(1)}, s32[128,8]{0,1:T(8,128)S(1)}, u32[]{:S(2)}, u32[]{:S(2)}) collective-permute-start(s32[128,8]{0,1:T(8,128)S(1)} %copy-done.14), channel_id=1, source_target_pairs={{0,1},{1,0},{2,3},{3,2},{4,5},{5,4},{6,7},{7,6},{8,9},{9,8},{10,11... | collective-permute-start | bytes 12296 | tf_op jit(solution)/shard_map/ppermute | solution.py:222
  14.2 9.7 %collective-permute-start.1 = (s32[128,8]{0,1:T(8,128)S(1)}, s32[128,8]{0,1:T(8,128)S(1)}, u32[]{:S(2)}, u32[]{:S(2)}) collective-permute-start(s32[128,8]{0,1:T(8,128)S(1)} %copy-done.14), channel_id=1, source_target_pairs={{0,16},{1,17},{2,18},{3,19},{4,20},{5,21},{6,22},{7,23},{8,24},{9,... | collective-permute-start | bytes 12296 | tf_op jit(solution)/shard_map/ppermute | solution.py:222
  23.8 3.2 %collective-permute-start.2 = (s32[128,8]{0,1:T(8,128)S(1)}, s32[128,8]{0,1:T(8,128)S(1)}, u32[]{:S(2)}, u32[]{:S(2)}) collective-permute-start(s32[128,8]{0,1:T(8,128)S(1)} %copy-done.14), channel_id=1, source_target_pairs={{0,17},{1,16},{2,19},{3,18},{4,21},{5,20},{6,23},{7,22},{8,25},{9,... | collective-permute-start | bytes 12296 | tf_op jit(solution)/shard_map/ppermute | solution.py:222
  27.1 12.4 %collective-permute-start.12 = (bf16[512,256]{1,0:T(8,128)(2,1)}, bf16[512,256]{1,0:T(8,128)(2,1)}, u32[]{:S(2)}, u32[]{:S(2)}) collective-permute-start(bf16[512,256]{1,0:T(8,128)(2,1)} %get-tuple-element.92.refs_0_), channel_id=1, source_target_pairs={{0,2},{1,3},{2,0},{3,1},{4,6},{5,7},{6,4},{7,5},{8,10},{9,11},{10,... | collective-permute-start | bytes 786440 | tf_op jit(solution)/shard_map/ppermute | solution.py:222
  29.5 21.8 %collective-permute-start.10 = (bf16[512,256]{1,0:T(8,128)(2,1)}, bf16[512,256]{1,0:T(8,128)(2,1)}, u32[]{:S(2)}, u32[]{:S(2)}) collective-permute-start(bf16[512,256]{1,0:T(8,128)(2,1)} %collective-permute-done.6.refs_1_), channel_id=1, source_target_pairs={{0,4},{1,5},{2,6},{3,7},{4,8},{5,9},{6,10},{7,11},{8,12},{9,13},{1... | collective-permute-start | bytes 786440 | tf_op jit(solution)/shard_map/ppermute | solution.py:225
  31.4 2.2 %copy-start.10 = (bf16[128,8,2048]{2,1,0:T(8,128)(2,1)S(1)}, bf16[128,8,2048]{2,1,0:T(8,128)(2,1)}, u32[]{:S(2)}) copy-start(bf16[128,8,2048]{2,1,0:T(8,128)(2,1)} %refs_2_.1) | copy-start | bytes 12582916
  33.6 10.8 %copy-start.5 = (s32[4096,128]{1,0:T(8,128)}, s32[4096,128]{1,0:T(8,128)S(1)}, u32[]{:S(2)}) copy-start(s32[4096,128]{1,0:T(8,128)S(1)} %broadcast_in_dim.2.routes_ref) | copy-start | bytes 6291460
  36.3 16.3 %collective-permute-start.9 = (bf16[512,256]{1,0:T(8,128)(2,1)}, bf16[512,256]{1,0:T(8,128)(2,1)S(1)}, u32[]{:S(2)}, u32[]{:S(2)}) collective-permute-start(bf16[512,256]{1,0:T(8,128)(2,1)} %collective-permute-done.6.refs_1_), channel_id=1, source_target_pairs={{0,2},{1,3},{2,0},{3,1},{4,6},{5,7},{6,4},{7,5},{8,10},{9,11},{10,... | collective-permute-start | bytes 786440 | tf_op jit(solution)/shard_map/ppermute | solution.py:222
  38.1 15.4 %collective-permute-start.8 = (bf16[512,256]{1,0:T(8,128)(2,1)}, bf16[512,256]{1,0:T(8,128)(2,1)}, u32[]{:S(2)}, u32[]{:S(2)}) collective-permute-start(bf16[512,256]{1,0:T(8,128)(2,1)} %collective-permute-done.4.refs_1_), channel_id=1, source_target_pairs={{0,4},{1,5},{2,6},{3,7},{4,8},{5,9},{6,10},{7,11},{8,12},{9,13},{1... | collective-permute-start | bytes 786440 | tf_op jit(solution)/shard_map/ppermute | solution.py:225
  39.5 33.4 %collective-permute-start.3 = (bf16[512,512]{1,0:T(8,128)(2,1)}, bf16[512,512]{1,0:T(8,128)(2,1)S(1)}, u32[]{:S(2)}, u32[]{:S(2)}) collective-permute-start(bf16[512,512]{1,0:T(8,128)(2,1)} %bitcast.23), channel_id=1, source_target_pairs={{0,16},{1,17},{2,18},{3,19},{4,20},{5,21},{6,22},{7,23},{8,24},{9,... | collective-permute-start | bytes 1572872 | tf_op jit(solution)/shard_map/ppermute | solution.py:222
  43.1 26.2 %collective-permute-start.7 = (bf16[512,256]{1,0:T(8,128)(2,1)}, bf16[512,256]{1,0:T(8,128)(2,1)}, u32[]{:S(2)}, u32[]{:S(2)}) collective-permute-start(bf16[512,256]{1,0:T(8,128)(2,1)} %collective-permute-done.4.refs_1_), channel_id=1, source_target_pairs={{0,2},{1,3},{2,0},{3,1},{4,6},{5,7},{6,4},{7,5},{8,10},{9,11},{10,... | collective-permute-start | bytes 786440 | tf_op jit(solution)/shard_map/ppermute | solution.py:222
  44.4 12.3 %copy-start.17 = (bf16[64,7168]{1,0:T(8,128)(2,1)S(1)}, bf16[64,7168]{1,0:T(8,128)(2,1)}, u32[]{:S(2)}) copy-start(bf16[64,7168]{1,0:T(8,128)(2,1)} %param.10) | copy-start | bytes 2752516
  45.9 2.0 %copy-start.1 = (bf16[4096,512]{1,0:T(8,128)(2,1)}, bf16[4096,512]{1,0:T(8,128)(2,1)S(1)}, u32[]{:S(2)}) copy-start(bf16[4096,512]{1,0:T(8,128)(2,1)S(1)} %get-tuple-element.122.refs_2_) | copy-start | bytes 12582916
  47.9 2.0 %copy-start.3 = (bf16[16,512,256]{2,1,0:T(8,128)(2,1)}, bf16[16,512,256]{2,1,0:T(8,128)(2,1)S(1)}, u32[]{:S(2)}) copy-start(bf16[16,512,256]{2,1,0:T(8,128)(2,1)S(1)} %get-tuple-element.123.refs_3_) | copy-start | bytes 12582916
  49.9 1.4 %copy-start.7 = (f32[4096,128]{1,0:T(8,128)}, f32[4096,128]{1,0:T(8,128)S(1)}, u32[]{:S(2)}) copy-start(f32[4096,128]{1,0:T(8,128)S(1)} %get-tuple-element.124.refs_4_) | copy-start | bytes 6291460
  51.3 25.2 %collective-permute-start.14 = (bf16[512,256]{1,0:T(8,128)(2,1)}, bf16[512,256]{1,0:T(8,128)(2,1)S(1)}, u32[]{:S(2)}, u32[]{:S(2)}) collective-permute-start(bf16[512,256]{1,0:T(8,128)(2,1)} %collective-permute-done.10.refs_1_), channel_id=1, source_target_pairs={{0,4},{1,5},{2,6},{3,7},{4,8},{5,9},{6,10},{7,11},{8,12},{9,13},{1... | collective-permute-start | bytes 786440 | tf_op jit(solution)/shard_map/ppermute | solution.py:225
  52.6 0.7 copy-start.12
  53.3 24.7 %collective-permute-start.19 = (bf16[512,256]{1,0:T(8,128)(2,1)}, bf16[512,256]{1,0:T(8,128)(2,1)S(1)}, u32[]{:S(2)}, u32[]{:S(2)}) collective-permute-start(bf16[512,256]{1,0:T(8,128)(2,1)} %collective-permute-done.10.refs_1_), channel_id=1, source_target_pairs={{0,2},{1,3},{2,0},{3,1},{4,6},{5,7},{6,4},{7,5},{8,10},{9,11},{10,... | collective-permute-start | bytes 786440 | tf_op jit(solution)/shard_map/ppermute | solution.py:222
  53.5 33.4 %collective-permute-start.16 = (bf16[512,512]{1,0:T(8,128)(2,1)}, bf16[512,512]{1,0:T(8,128)(2,1)S(1)}, u32[]{:S(2)}, u32[]{:S(2)}) collective-permute-start(bf16[512,512]{1,0:T(8,128)(2,1)} %bitcast.25), channel_id=1, source_target_pairs={{0,17},{1,16},{2,19},{3,18},{4,21},{5,20},{6,23},{7,22},{8,25},{9,... | collective-permute-start | bytes 1572872 | tf_op jit(solution)/shard_map/ppermute | solution.py:222
  57.5 2.2 %copy-start.2 = (bf16[4096,512]{1,0:T(8,128)(2,1)S(1)}, bf16[4096,512]{1,0:T(8,128)(2,1)}, u32[]{:S(2)}) copy-start(bf16[4096,512]{1,0:T(8,128)(2,1)} %copy-done.1) | copy-start | bytes 12582916
  59.7 2.2 %copy-start.4 = (bf16[16,512,256]{2,1,0:T(8,128)(2,1)S(1)}, bf16[16,512,256]{2,1,0:T(8,128)(2,1)}, u32[]{:S(2)}) copy-start(bf16[16,512,256]{2,1,0:T(8,128)(2,1)} %copy-done.3) | copy-start | bytes 12582916
  61.9 1.6 %copy-start.6 = (s32[4096,128]{1,0:T(8,128)S(1)}, s32[4096,128]{1,0:T(8,128)}, u32[]{:S(2)}) copy-start(s32[4096,128]{1,0:T(8,128)} %copy-done.5) | copy-start | bytes 6291460
  63.4 1.6 %copy-start.8 = (f32[4096,128]{1,0:T(8,128)S(1)}, f32[4096,128]{1,0:T(8,128)}, u32[]{:S(2)}) copy-start(f32[4096,128]{1,0:T(8,128)} %copy-done.7) | copy-start | bytes 6291460
  65.0 0.9 copy-start.13
  69.4 12.8 %collective-permute-start.18 = (bf16[512,256]{1,0:T(8,128)(2,1)}, bf16[512,256]{1,0:T(8,128)(2,1)S(1)}, u32[]{:S(2)}, u32[]{:S(2)}) collective-permute-start(bf16[512,256]{1,0:T(8,128)(2,1)} %collective-permute-done.8.refs_1_), channel_id=1, source_target_pairs={{0,4},{1,5},{2,6},{3,7},{4,8},{5,9},{6,10},{7,11},{8,12},{9,13},{1... | collective-permute-start | bytes 786440 | tf_op jit(solution)/shard_map/ppermute | solution.py:225
  72.9 9.6 %collective-permute-start.17 = (bf16[512,256]{1,0:T(8,128)(2,1)}, bf16[512,256]{1,0:T(8,128)(2,1)S(1)}, u32[]{:S(2)}, u32[]{:S(2)}) collective-permute-start(bf16[512,256]{1,0:T(8,128)(2,1)} %collective-permute-done.8.refs_1_), channel_id=1, source_target_pairs={{0,2},{1,3},{2,0},{3,1},{4,6},{5,7},{6,4},{7,5},{8,10},{9,11},{10,... | collective-permute-start | bytes 786440 | tf_op jit(solution)/shard_map/ppermute | solution.py:222
  74.2 3.8 %copy-start.18 = (s32[128]{0:T(128)S(1)}, s32[128]{0:T(128)}, u32[]{:S(2)}) copy-start(s32[128]{0:T(128)} %param.9) | copy-start | bytes 1540
  74.2 3.8 %copy-start.16 = (bf16[64,8,512]{2,1,0:T(8,128)(2,1)S(1)}, bf16[64,8,512]{2,1,0:T(8,128)(2,1)}, u32[]{:S(2)}) copy-start(bf16[64,8,512]{2,1,0:T(8,128)(2,1)} %copy-done.15) | copy-start | bytes 1572868
  76.6 13.6 %collective-permute-start.15 = (bf16[512,256]{1,0:T(8,128)(2,1)S(1)}, bf16[512,256]{1,0:T(8,128)(2,1)S(1)}, u32[]{:S(2)}, u32[]{:S(2)}) collective-permute-start(bf16[512,256]{1,0:T(8,128)(2,1)S(1)} %collective-permute-done.14.refs_1_), channel_id=1, source_target_pairs={{0,4},{1,5},{2,6},{3,7},{4,8},{5,9},{6,10},{7,11},{8,12},{9,13},{1... | collective-permute-start | bytes 786440 | tf_op jit(solution)/shard_map/ppermute | solution.py:225
  78.0 24.7 %collective-permute-start.13 = (bf16[512,512]{1,0:T(8,128)(2,1)S(1)}, bf16[512,512]{1,0:T(8,128)(2,1)S(1)}, u32[]{:S(2)}, u32[]{:S(2)}) collective-permute-start(bf16[512,512]{1,0:T(8,128)(2,1)S(1)} %bitcast.38), channel_id=1, source_target_pairs={{0,17},{1,16},{2,19},{3,18},{4,21},{5,20},{6,23},{7,22},{8,25},{9,... | collective-permute-start | bytes 1572872 | tf_op jit(solution)/shard_map/ppermute | solution.py:222
  82.2 8.3 %collective-permute-start.22 = (bf16[512,256]{1,0:T(8,128)(2,1)S(1)}, bf16[512,256]{1,0:T(8,128)(2,1)S(1)}, u32[]{:S(2)}, u32[]{:S(2)}) collective-permute-start(bf16[512,256]{1,0:T(8,128)(2,1)S(1)} %collective-permute-done.14.refs_1_), channel_id=1, source_target_pairs={{0,2},{1,3},{2,0},{3,1},{4,6},{5,7},{6,4},{7,5},{8,10},{9,11},{10,... | collective-permute-start | bytes 786440 | tf_op jit(solution)/shard_map/ppermute | solution.py:222
  82.5 12.5 %collective-permute-start.21 = (bf16[512,256]{1,0:T(8,128)(2,1)S(1)}, bf16[512,256]{1,0:T(8,128)(2,1)S(1)}, u32[]{:S(2)}, u32[]{:S(2)}) collective-permute-start(bf16[512,256]{1,0:T(8,128)(2,1)S(1)} %collective-permute-done.18.refs_1_), channel_id=1, source_target_pairs={{0,2},{1,3},{2,0},{3,1},{4,6},{5,7},{6,4},{7,5},{8,10},{9,11},{10,... | collective-permute-start | bytes 786440 | tf_op jit(solution)/shard_map/ppermute | solution.py:222
  90.2 10.4 %collective-permute-start.20 = (bf16[512,256]{1,0:T(8,128)(2,1)S(1)}, bf16[512,256]{1,0:T(8,128)(2,1)S(1)}, u32[]{:S(2)}, u32[]{:S(2)}) collective-permute-start(bf16[512,256]{1,0:T(8,128)(2,1)S(1)} %collective-permute-done.15.refs_1_), channel_id=1, source_target_pairs={{0,2},{1,3},{2,0},{3,1},{4,6},{5,7},{6,4},{7,5},{8,10},{9,11},{10,... | collective-permute-start | bytes 786440 | tf_op jit(solution)/shard_map/ppermute | solution.py:222
  107.5 3.7 %collective-permute-start.23 = (bf16[512,128]{1,0:T(8,128)(2,1)S(1)}, bf16[512,128]{1,0:T(8,128)(2,1)S(1)}, u32[]{:S(2)}, u32[]{:S(2)}) collective-permute-start(bf16[512,128]{1,0:T(8,128)(2,1)S(1)} %get-tuple-element.176), channel_id=1, source_target_pairs={{0,1},{1,0},{2,3},{3,2},{4,5},{5,4},{6,7},{7,6},{8,9},{9,8},{10,11... | collective-permute-start | bytes 393224 | tf_op jit(solution)/shard_map/ppermute | solution.py:222
  109.2 5.1 %collective-permute-start.24 = (bf16[512,128]{1,0:T(8,128)(2,1)S(1)}, bf16[512,128]{1,0:T(8,128)(2,1)S(1)}, u32[]{:S(2)}, u32[]{:S(2)}) collective-permute-start(bf16[512,128]{1,0:T(8,128)(2,1)S(1)} %get-tuple-element.177), channel_id=1, source_target_pairs={{0,16},{1,17},{2,18},{3,19},{4,20},{5,21},{6,22},{7,23},{8,24},{9,... | collective-permute-start | bytes 393224 | tf_op jit(solution)/shard_map/ppermute | solution.py:222
  110.5 6.8 %collective-permute-start.25 = (bf16[512,128]{1,0:T(8,128)(2,1)S(1)}, bf16[512,128]{1,0:T(8,128)(2,1)S(1)}, u32[]{:S(2)}, u32[]{:S(2)}) collective-permute-start(bf16[512,128]{1,0:T(8,128)(2,1)S(1)} %get-tuple-element.178), channel_id=1, source_target_pairs={{0,17},{1,16},{2,19},{3,18},{4,21},{5,20},{6,23},{7,22},{8,25},{9,... | collective-permute-start | bytes 393224 | tf_op jit(solution)/shard_map/ppermute | solution.py:222

commit v4 on v3

v4 whole, which is shorter than its diff:
```python
import functools

import jax
import jax.numpy as jnp
import numpy as np
from jax import lax
from jax.experimental import pallas as pl
from jax.experimental.pallas import tpu as pltpu
from jax.sharding import PartitionSpec as P

SEG_DEV = 2
CORES = 2
SIDES = 2
QUAD = 4
CHUNKS = 4
BOTH = ("groups", "expert")
MIB = 1024 * 1024
VMEM = pl.BlockSpec(memory_space=pltpu.VMEM)
SMEM = pl.BlockSpec(memory_space=pltpu.SMEM)
HBM = pl.BlockSpec(memory_space=pltpu.HBM)
QUICK = pl.CostEstimate(flops=1, bytes_accessed=1, transcendentals=0)


def columns_of(ref, who, width):
    return ref.at[..., pl.ds(pl.multiple_of(who * width, width), width)]


def cut_kernel(plan, who_ref, *refs):
    sources, outs, sems = refs[:2], refs[2:-1], refs[-1]
    copies = []
    for i, (out, (source, who, first)) in enumerate(zip(outs, plan)):
        part = out.shape[0]
        block = columns_of(sources[source].at[pl.ds(first, part)], who_ref[who], out.shape[-1])
        copies.append(pltpu.make_async_copy(block, out, sems.at[i]))
    for copy in copies:
        copy.start()
    for copy in copies:
        copy.wait()


def cut(plan, shapes, who, weights, grads):
    return pl.pallas_call(
        functools.partial(cut_kernel, plan),
        out_shape=[jax.ShapeDtypeStruct(shape, jnp.bfloat16) for shape in shapes],
        in_specs=[SMEM, HBM, HBM],
        out_specs=[HBM] * len(plan),
        scratch_shapes=[pltpu.SemaphoreType.DMA((len(plan),))],
        compiler_params=pltpu.CompilerParams(vmem_limit_bytes=4 * MIB),
        cost_estimate=QUICK,
    )(who, weights, grads)


def basis_kernel(hidden_ref, proj_ref, segment_ref, out_ref):
    projected = lax.dot_general(
        hidden_ref[...], proj_ref[...], (((1,), (1,)), ((), ())), preferred_element_type=jnp.float32
    )
    zero = jnp.zeros_like(projected)
    picked = [jnp.where(segment_ref[...] == s, projected, zero) for s in range(SEG_DEV)]
    even = jnp.concatenate([b for p in picked for b in (p, zero)], axis=1)
    odd = jnp.concatenate([b for p in picked for b in (zero, p)], axis=1)
    out_ref[...] = jnp.concatenate([even, odd], axis=0).astype(out_ref.dtype)


def partial_kernel(
    rank, loops, new_tokens, new_units, fresh, sends, who_ref, bases_ref, routes_ref, *refs
):
    token_refs, refs = refs[: len(new_tokens)], refs[len(new_tokens) :]
    unit_refs, refs = refs[: len(new_units)], refs[len(new_units) :]
    if fresh:
        grads_ref, tokens, units, total, stage, sem = refs
        width = units.shape[2]
        copy = pltpu.make_async_copy(columns_of(grads_ref, who_ref[0], width), stage, sem)
        copy.start()
        total[...] = jnp.zeros_like(total)
        copy.wait()
        pairs = stage.shape[0] * stage.shape[1]
        tokens[0:pairs, :] = stage[...].reshape(pairs, width)
        send_refs = ()
    else:
        tokens, units, total = refs[3:6]
        send_refs = refs[6:]
    for ref, first in zip(token_refs, new_tokens):
        tokens[first : first + ref.shape[0], :] = ref[...]
    for ref, place in zip(unit_refs, new_units):
        units[place] = ref[...]
    cols, width = units.shape[1:]
    rows = total.shape[2]
    for first_t, count_t, first_w, count_w, together in loops:

        def step(i, carry, first_t=first_t, count_t=count_t, first_w=first_w, together=together):
            t = first_t + i % count_t
            w = first_w + (i // count_t) * together
            here = pl.ds(pl.multiple_of(t * rows, rows), rows)
            dense = lax.dot_general(
                units[pl.ds(w, together)].reshape(together * cols, width),
                tokens[here, :],
                (((1,), (1,)), ((), ())),
                preferred_element_type=jnp.float32,
            )
            chosen = routes_ref[pl.ds(t, 1), :]
            value = total[t]
            for more in range(together):
                base = bases_ref[w + more]
                for expert in range(cols // rank):
                    first = more * cols + expert * rank
                    value = jnp.where(chosen == base + expert, dense[first : first + rank], value)
            total[t] = value
            return carry

        lax.fori_loop(0, count_t * (count_w // together), step, 0)
    for ref, first in zip(send_refs, sends):
        ref[...] = total[first : first + ref.shape[0]].astype(ref.dtype)


def accumulate(
    state, who, bases, routes, tokens, units, loops, rank, grads=None, places=0, sends=()
):
    fresh = state is None
    operands = [who, bases, routes, *[a for a, _ in tokens], *[a for a, _ in units]]
    specs = [SMEM, SMEM] + [VMEM] * (len(operands) - 2)
    scratch = []
    blocks, rows = routes.shape
    if fresh:
        operands.append(grads)
        specs.append(HBM)
        count, tops, whole = grads.shape
        width = whole // QUAD
        scratch = [pltpu.VMEM((count, tops, width), jnp.bfloat16), pltpu.SemaphoreType.DMA]
        shapes = [
            jax.ShapeDtypeStruct((blocks * rows, width), jnp.bfloat16),
            jax.ShapeDtypeStruct((places, *units[0][0].shape), jnp.bfloat16),
            jax.ShapeDtypeStruct((blocks, rank, rows), jnp.float32),
        ]
        aliases = {}
    else:
        aliases = {len(operands) + i: i for i in range(3)}
        operands += state
        specs += [VMEM] * 3
        shapes = [jax.ShapeDtypeStruct(a.shape, a.dtype) for a in state]
    shapes += [jax.ShapeDtypeStruct((blocks // QUAD, rank, rows), jnp.bfloat16)] * len(sends)
    return pl.pallas_call(
        functools.partial(
            partial_kernel,
            rank,
            loops,
            [f for _, f in tokens],
            [p for _, p in units],
            fresh,
            sends,
        ),
        out_shape=shapes,
        in_specs=specs,
        out_specs=[VMEM] * len(shapes),
        scratch_shapes=scratch,
        input_output_aliases=aliases,
        compiler_params=pltpu.CompilerParams(vmem_limit_bytes=24 * MIB),
        cost_estimate=QUICK,
    )(*operands)


def blocks_kernel(
    tops, rank, routes_ref, basis_ref, own_ref, b_ref, c_ref, d_ref, out_ref, pairs, turned, spread
):
    halves, _, rows = b_ref.shape
    tokens = halves * rows // tops
    for h in range(halves):
        value = own_ref[h]
        for ref in (b_ref, c_ref, d_ref):
            value = value + ref[h].astype(jnp.float32)
        value = value.astype(jnp.bfloat16).astype(jnp.float32)
        pairs[h * rows : (h + 1) * rows, 0:rank] = value.T
    for k in range(tops):
        turned[k] = pairs[pl.ds(k, tokens, stride=tops), :].T[0:rank, :]
    experts = out_ref.shape[1]

    def expand(tile, carry):
        first = pl.multiple_of(tile * 8, 8)
        ids = first + lax.broadcasted_iota(jnp.int32, (8, tokens), 0)
        masks = [routes_ref[k : k + 1, :] == ids for k in range(tops)]
        for r in range(rank):
            value = jnp.zeros((8, tokens), jnp.float32)
            for k in range(tops):
                value = jnp.where(masks[k], turned[k, r : r + 1, :], value)
            spread[r, pl.ds(first, 8), :] = value
        return carry

    lax.fori_loop(0, experts // 8, expand, 0)
    for pair in range(rank // 2):
        both = jnp.concatenate([spread[2 * pair], spread[2 * pair + 1]], axis=1)
        block = jnp.dot(
            both.astype(jnp.bfloat16), basis_ref[...], preferred_element_type=jnp.float32
        ).astype(jnp.bfloat16)
        for s in range(SEG_DEV):
            out_ref[s, :, pl.ds(pair * 2 * rank, 2 * rank)] = block[
                :, s * 2 * rank : (s + 1) * 2 * rank
            ]


def local(hidden_in, out_grads, routes, segments, in_proj, out_proj):
    tokens, tops = routes.shape
    exp_here, rank, width = out_proj.shape
    owners, groups = lax.axis_size("expert"), lax.axis_size("groups")
    experts = exp_here * owners
    pairs = tokens * tops
    quarter = width // QUAD
    cols = exp_here * rank
    group, index = lax.axis_index("groups"), lax.axis_index("expert")
    core = index % CORES
    slots = owners // CORES // 2
    mine = (group % SIDES) * CORES + core
    who = jnp.stack([mine, mine ^ 1, mine ^ 2, mine ^ 3]).astype(jnp.int32)
    ring = [0, *range(1, slots, 2), *range((slots - 1) // 2 * 2, 0, -2)]
    following = {a: b for a, b in zip(ring, ring[1:] + ring[:1])}
    before = {b: a for a, b in following.items()}

    def swap(array, side, bit):
        table = [
            (g * owners + e, (g ^ side) * owners + (e ^ bit))
            for g in range(groups)
            for e in range(owners)
        ]
        return lax.ppermute(array, BOTH, table)

    def onward(array):
        wide = 2 * CORES
        table = [(e, following[e // wide] * wide + e % wide) for e in range(owners)]
        return lax.ppermute(array, "expert", table)

    def tie(*arrays):
        return lax.optimization_barrier(arrays)

    rows_of = []
    for e in range(owners):
        z, y, c = e // (2 * CORES), e // CORES % 2, e % CORES
        named = [(z, y, c), (z, y, 1 - c)]
        here = z
        for slot in range(slots):
            after = before[here]
            for flip in (0, 1):
                named.append((here, 1 - y, c ^ flip))
                if slot + 1 < slots:
                    named.append((after, y, c ^ flip))
            here = after
        rows_of.append([((a * 2 + b) * CORES + d) * exp_here for a, b, d in named])
    places = len(rows_of[0])
    bases = lax.dynamic_index_in_dim(
        jnp.asarray(np.array(rows_of, np.int32)), index, axis=0, keepdims=False
    )

    part = tokens // 2
    rows = part * tops
    flat_routes = routes.reshape(1, pairs)
    around = [swap(flat_routes, side, bit) for side, bit in ((0, 1), (1, 0), (1, 1))]
    all_routes = jnp.concatenate([flat_routes, *around], axis=0).reshape(QUAD * pairs // rows, rows)

    weights = out_proj.reshape(cols, width)
    unit_shape, chunk_shape = (cols, quarter), (part, tops, quarter)
    mine_unit, core_unit, first_chunk = cut(
        [(0, 0, 0), (0, 1, 0), (1, 2, 0)],
        [unit_shape, unit_shape, chunk_shape],
        who,
        weights,
        out_grads,
    )
    other_unit = swap(core_unit, 0, 1)
    later_who, _ = tie(who, mine_unit)
    for_core, *pieces = cut(
        [(1, 1, 0), (1, 2, part), (1, 3, 0), (1, 3, part)],
        [(tokens, tops, quarter)] + [chunk_shape] * 3,
        later_who,
        weights,
        out_grads,
    )
    pieces = [first_chunk, *pieces]
    chunks = [
        swap(piece.reshape(rows, quarter), 1, bit) for piece, bit in zip(pieces, (0, 0, 1, 1))
    ]
    from_core = swap(for_core.reshape(pairs, quarter), 0, 1)

    basis = pl.pallas_call(
        basis_kernel,
        out_shape=jax.ShapeDtypeStruct((2 * tokens, SEG_DEV * 2 * rank), jnp.bfloat16),
        in_specs=[VMEM] * 3,
        out_specs=VMEM,
        compiler_params=pltpu.CompilerParams(vmem_limit_bytes=16 * MIB),
        cost_estimate=QUICK,
    )(hidden_in, in_proj, (segments - index * SEG_DEV).reshape(tokens, 1))

    line = [mine_unit, other_unit]
    across = [swap(line[0], 0, CORES), swap(line[1], 0, CORES)]
    ahead = [onward(line[0]), onward(line[1])]
    call = functools.partial(accumulate, who=who, bases=bases, routes=all_routes, rank=rank)
    own_blocks = pairs // rows
    state = call(
        None,
        tokens=[],
        units=[(line[0], 0), (line[1], 1)],
        loops=[(0, own_blocks, 0, 2, 2)],
        grads=out_grads,
        places=places,
    )
    basis, *state = tie(basis, *state)
    state = call(
        state,
        tokens=[(from_core, pairs)],
        units=[],
        loops=[(own_blocks, own_blocks, 0, 2, 2)],
    )
    known_units, known_blocks = 2, 2 * own_blocks
    sent = []
    for slot in range(slots):
        for chain in range(2):
            arrived = [(across[chain], known_units)]
            if slot + 1 < slots:
                line[chain], *state = tie(ahead[chain], *state)
                if slot + 2 < slots:
                    ahead[chain] = onward(line[chain])
                across[chain] = swap(line[chain], 0, CORES)
                arrived.append((line[chain], known_units + 1))
            count = len(arrived)
            last = slot + 1 == slots and chain == 1
            state = call(
                state,
                tokens=[],
                units=arrived,
                loops=[(0, known_blocks, known_units, count, count)],
                sends=[own_blocks, 2 * own_blocks] if last else [],
            )
            state, sent = state[:3], sent + list(state[3:])
            known_units += count
            take = slot if chain == 0 and slot < CHUNKS - 1 else CHUNKS - 1 if last else None
            if take is not None:
                loops = [(known_blocks, 1, 0, known_units // 2 * 2, 2)]
                if known_units % 2:
                    loops.append((known_blocks, 1, known_units - 1, 1, 1))
                state = call(
                    state,
                    tokens=[(chunks[take], known_blocks * rows)],
                    units=[],
                    loops=loops,
                    sends=[3 * own_blocks] if last else [],
                )
                state, sent = state[:3], sent + list(state[3:])
                known_blocks += 1

    from_core = swap(sent[0], 0, 1)
    from_side = swap(sent[1], 1, 0)
    from_diagonal = swap(sent[2], 1, 1)
    return pl.pallas_call(
        functools.partial(blocks_kernel, tops, rank),
        out_shape=jax.ShapeDtypeStruct((SEG_DEV, experts, rank * rank), jnp.bfloat16),
        in_specs=[VMEM] * 6,
        out_specs=VMEM,
        scratch_shapes=[
            pltpu.VMEM((pairs, 2 * rank), jnp.float32),
            pltpu.VMEM((tops, rank, tokens), jnp.float32),
            pltpu.VMEM((rank, experts, tokens), jnp.float32),
        ],
        compiler_params=pltpu.CompilerParams(vmem_limit_bytes=32 * MIB),
        cost_estimate=QUICK,
    )(routes.T, basis, state[2], from_core, from_side, from_diagonal)


def solution(mesh):
    placed = (
        P(("groups", "expert"), None),
        P(("groups", "expert"), None, None),
        P(("groups", "expert"), None),
        P(("groups", "expert")),
        P(),
        P("expert", None, None),
    )
    return jax.shard_map(
        local,
        mesh=mesh,
        in_specs=placed,
        out_specs=P(("groups", "expert"), None, None),
        check_vma=False,
    )
```

time: 121 us -> 102 us (0.84)
  local copies, waits for them, and re-layouts: 22.7 us -> 11 us
  waiting for transfers between devices: 21.6 us -> 12.7 us
  starting transfers between devices: 27.2 us -> 29.2 us
    unnamed x40 -> x27, local copies, waits for them, and re-layouts: 21.3 us -> 10.1 us
    ppermute x20, waiting for transfers between devices: 21.6 us -> 10.8 us  [swap(): return lax.ppermute(array, BOTH, table)]
    ppermute x6, waiting for transfers between devices: 0.02 us -> 1.87 us  [onward(): return lax.ppermute(array, 'expert', table)]
    pallas_call x14, Pallas kernels: 39.5 us -> 41.1 us  [accumulate(): pl.pallas_call(functools.partial(partial_kernel, rank, loops, [f for _, f...]
    ppermute x6, starting transfers between devices: 6.8 us -> 8.11 us  [onward(): return lax.ppermute(array, 'expert', table)]
  transfers between devices with their start and end apart: 26 -> 26, of which waited for: 7 -> 5; matrix products, arithmetic and copies ran while one was open for 2% -> 1% of each run, Pallas kernels for 29% -> 37%
where the time goes in v4:
time: 102 us; the launch traced here: 101 us
  Pallas kernels  47.7 us (47%)
  starting transfers between devices  29.2 us (29%)
  waiting for transfers between devices  12.7 us (12%)
  local copies, waits for them, and re-layouts  11 us (11%)
    pallas_call x14, Pallas kernels, accumulate(): pl.pallas_call(functools.partial(partial_kernel, rank, loops, [f for _, f...  41.1 us
    ppermute x20, starting transfers between devices, swap(): return lax.ppermute(array, BOTH, table)  21.1 us
    ppermute x20, waiting for transfers between devices, swap(): return lax.ppermute(array, BOTH, table)  10.8 us
    unnamed x27, local copies, waits for them, and re-layouts  10.1 us
    ppermute x6, starting transfers between devices, onward(): return lax.ppermute(array, 'expert', table)  8.11 us
    pallas_call x1, Pallas kernels, local(): pl.pallas_call(functools.partial(blocks_kernel, tops, rank), out_shape=ja...  2.99 us
    pallas_call x2, Pallas kernels, cut(): pl.pallas_call(functools.partial(cut_kernel, plan), out_shape=[jax.ShapeD...  2.93 us
  transfers between devices with their start and end apart: 26, of which 5 were waited for; matrix products, arithmetic and copies ran while one was open for 1% of the time, Pallas kernels for 37%

profile of v4, /device:TPU:1, one launch (start us, length us, event | category | flops | bytes accessed | tf_op | source)
XLA Modules:
  0.0 101.0 jit_solution(1017989641051620243)
XLA Ops:
  0.1 2.2 %copy-done = bf16[128,8,2048]{2,1,0:T(8,128)(2,1)S(1)} copy-done((bf16[128,8,2048]{2,1,0:T(8,128)(2,1)S(1)}, bf16[128,8,2048]{2,1,0:T(8,128)(2,1)}, u32[]{:S(2)}) %copy-start) | copy-done | bytes 4194328
  2.3 1.2 %copy-done.2 = bf16[4,64,2048]{2,1,0:T(8,128)(2,1)S(1)} copy-done((bf16[4,64,2048]{2,1,0:T(8,128)(2,1)S(1)}, bf16[4,64,2048]{2,1,0:T(8,128)(2,1)}, u32[]{:S(2)}) %copy-start.2) | copy-done | bytes 1048600
  3.5 1.4 %shard_map.74 = (bf16[256,512]{1,0:T(8,128)(2,1)}, bf16[256,512]{1,0:T(8,128)(2,1)}, bf16[64,8,512]{2,1,0:T(8,128)(2,1)S(1)}) custom-call(s32[4]{0:T(128)S(1)} %pad_add_fusion.1.who_ref, bf16[256,2048]{1,0:T(8,128)(2,1)S(1)} %bitcast.15, bf16[128,8,2048]{2,1,0:T(8,128)(2,1)S(1)} %copy-done), custom_call_target="tpu_custom_call" | custom-call | flops 1 | bytes 1 | tf_op jit(solution)/shard_map/pallas_call | solution.py:42
  4.9 0.8 copy-done.11
  5.7 1.6 %shard_map.76 = (bf16[128,8,512]{2,1,0:T(8,128)(2,1)}, bf16[64,8,512]{2,1,0:T(8,128)(2,1)S(1)}, bf16[64,8,512]{2,1,0:T(8,128)(2,1)S(1)}, bf16[64,8,512]{2,1,0:T(8,128)(2,1)S(1)}) custom-call(s32[4]{0:T(128)S(1)} %pad_add_fusion.1.who_ref, bf16[256,2048]{1,0:T(8,128)(2,1)S(1)} %bitcast.16, bf16[128,8,2048]{2,1,0:T(8,128)(2,1)S(1)} %copy-done), custom_call_target="tpu_custom_call" | custom-call | flops 1 | bytes 1 | tf_op jit(solution)/shard_map/pallas_call | solution.py:42
  7.2 0.8 copy-done.6
  8.0 0.8 copy-done.8
  8.8 0.8 copy-done.10
  9.9 0.5 collective-permute-start
  10.4 2.3 %collective-permute-start.1 = (s32[1,1024]{1,0:T(1,128)S(1)}, s32[1,1024]{1,0:T(1,128)S(1)}, u32[]{:S(2)}, u32[]{:S(2)}) collective-permute-start(s32[1,1024]{1,0:T(1,128)S(1)} %reshape.28), channel_id=1, source_target_pairs={{0,16},{1,17},{2,18},{3,19},{4,20},{5,21},{6,22},{7,23},{8,24},{9,... | collective-permute-start | bytes 12296 | tf_op jit(solution)/shard_map/ppermute | solution.py:222
  13.0 1.8 %collective-permute-start.8 = (bf16[256,512]{1,0:T(8,128)(2,1)}, bf16[256,512]{1,0:T(8,128)(2,1)}, u32[]{:S(2)}, u32[]{:S(2)}) collective-permute-start(bf16[256,512]{1,0:T(8,128)(2,1)} %get-tuple-element.84.refs_0_), channel_id=1, source_target_pairs={{0,4},{1,5},{2,6},{3,7},{4,12},{5,13},{6,14},{7,15},{8,0},{9,1},{1... | collective-permute-start | bytes 786440 | tf_op jit(solution)/shard_map/ppermute | solution.py:227
  14.8 1.2 %collective-permute-start.7 = (bf16[256,512]{1,0:T(8,128)(2,1)}, bf16[256,512]{1,0:T(8,128)(2,1)}, u32[]{:S(2)}, u32[]{:S(2)}) collective-permute-start(bf16[256,512]{1,0:T(8,128)(2,1)} %get-tuple-element.84.refs_0_), channel_id=1, source_target_pairs={{0,2},{1,3},{2,0},{3,1},{4,6},{5,7},{6,4},{7,5},{8,10},{9,11},{10,... | collective-permute-start | bytes 786440 | tf_op jit(solution)/shard_map/ppermute | solution.py:222
  16.5 1.1 %collective-permute-start.6 = (bf16[512,512]{1,0:T(8,128)(2,1)}, bf16[512,512]{1,0:T(8,128)(2,1)S(1)}, u32[]{:S(2)}, u32[]{:S(2)}) collective-permute-start(bf16[512,512]{1,0:T(8,128)(2,1)} %bitcast.21), channel_id=1, source_target_pairs={{0,16},{1,17},{2,18},{3,19},{4,20},{5,21},{6,22},{7,23},{8,24},{9,... | collective-permute-start | bytes 1572872 | tf_op jit(solution)/shard_map/ppermute | solution.py:222
  17.8 0.7 dynamic-slice_bitcast_fusion.bases_ref
  18.5 2.4 %collective-permute-start.5 = (bf16[256,512]{1,0:T(8,128)(2,1)}, bf16[256,512]{1,0:T(8,128)(2,1)S(1)}, u32[]{:S(2)}, u32[]{:S(2)}) collective-permute-start(bf16[256,512]{1,0:T(8,128)(2,1)} %collective-permute-done.3.refs_1_), channel_id=1, source_target_pairs={{0,4},{1,5},{2,6},{3,7},{4,12},{5,13},{6,14},{7,15},{8,0},{9,1},{1... | collective-permute-start | bytes 786440 | tf_op jit(solution)/shard_map/ppermute | solution.py:227
  20.9 1.9 %collective-permute-done.8.refs_1_ = bf16[256,512]{1,0:T(8,128)(2,1)} collective-permute-done((bf16[256,512]{1,0:T(8,128)(2,1)}, bf16[256,512]{1,0:T(8,128)(2,1)}, u32[]{:S(2)}, u32[]{:S(2)}) %collective-permute-start.8) | collective-permute-done | bytes 262176 | tf_op jit(solution)/shard_map/ppermute | solution.py:227
  22.7 1.3 %collective-permute-start.11 = (bf16[512,512]{1,0:T(8,128)(2,1)}, bf16[512,512]{1,0:T(8,128)(2,1)S(1)}, u32[]{:S(2)}, u32[]{:S(2)}) collective-permute-start(bf16[512,512]{1,0:T(8,128)(2,1)} %bitcast.20), channel_id=1, source_target_pairs={{0,16},{1,17},{2,18},{3,19},{4,20},{5,21},{6,22},{7,23},{8,24},{9,... | collective-permute-start | bytes 1572872 | tf_op jit(solution)/shard_map/ppermute | solution.py:222
  24.0 1.2 %copy-done.4 = bf16[64,7168]{1,0:T(8,128)(2,1)S(1)} copy-done((bf16[64,7168]{1,0:T(8,128)(2,1)S(1)}, bf16[64,7168]{1,0:T(8,128)(2,1)}, u32[]{:S(2)}) %copy-start.4) | copy-done | bytes 917528
  25.2 0.7 shard_map.73.basis_ref
  25.9 2.2 %copy-done.1 = bf16[128,8,2048]{2,1,0:T(8,128)(2,1)S(1)} copy-done((bf16[128,8,2048]{2,1,0:T(8,128)(2,1)S(1)}, bf16[128,8,2048]{2,1,0:T(8,128)(2,1)}, u32[]{:S(2)}) %copy-start.1) | copy-done | bytes 4194328
  28.1 2.3 %shard_map.75 = (bf16[4096,512]{1,0:T(8,128)(2,1)S(1)}, bf16[16,256,512]{2,1,0:T(8,128)(2,1)S(1)}, f32[8,64,512]{2,1,0:T(8,128)S(1)}) custom-call(s32[4]{0:T(128)S(1)} %pad_add_fusion.1.who_ref, s32[16]{0:T(128)S(1)} %dynamic-slice_bitcast_fusion.bases_ref, s32[8,512]{1,0:T(8,128)S(1)} %reshape.29.routes_ref, bf16[256,512]{1,0:T(8,128)(2,1)} %get-tuple-element.84.refs_0_, ...), custom_call_target="tpu_custom_call" | custom-call | flops 1 | bytes 1 | tf_op jit(solution)/shard_map/pallas_call | solution.py:141
  30.5 1.3 %collective-permute-start.14 = (bf16[256,512]{1,0:T(8,128)(2,1)}, bf16[256,512]{1,0:T(8,128)(2,1)S(1)}, u32[]{:S(2)}, u32[]{:S(2)}) collective-permute-start(bf16[256,512]{1,0:T(8,128)(2,1)} %collective-permute-done.3.refs_1_), channel_id=1, source_target_pairs={{0,2},{1,3},{2,0},{3,1},{4,6},{5,7},{6,4},{7,5},{8,10},{9,11},{10,... | collective-permute-start | bytes 786440 | tf_op jit(solution)/shard_map/ppermute | solution.py:222
  31.8 1.6 %shard_map.77 = (bf16[4096,512]{1,0:T(8,128)(2,1)S(1)}, bf16[16,256,512]{2,1,0:T(8,128)(2,1)S(1)}, f32[8,64,512]{2,1,0:T(8,128)S(1)}) custom-call(s32[4]{0:T(128)S(1)} %pad_add_fusion.1.who_ref, s32[16]{0:T(128)S(1)} %dynamic-slice_bitcast_fusion.bases_ref, ...), custom_call_target="tpu_custom_call", output_to_operand_aliasing={{0}: (4, {}), {1}: (5, {}), {2}: (6, {})} | custom-call | flops 1 | bytes 1 | tf_op jit(solution)/shard_map/pallas_call | solution.py:141
  33.3 0.6 collective-permute-start.13
  33.9 3.0 %shard_map.78 = (bf16[4096,512]{1,0:T(8,128)(2,1)S(1)}, bf16[16,256,512]{2,1,0:T(8,128)(2,1)S(1)}, f32[8,64,512]{2,1,0:T(8,128)S(1)}) custom-call(s32[4]{0:T(128)S(1)} %pad_add_fusion.1.who_ref, s32[16]{0:T(128)S(1)} %dynamic-slice_bitcast_fusion.bases_ref, ...), custom_call_target="tpu_custom_call", output_to_operand_aliasing={{0}: (5, {}), {1}: (6, {}), {2}: (7, {})} | custom-call | flops 1 | bytes 1 | tf_op jit(solution)/shard_map/pallas_call | solution.py:141
  37.2 1.5 %shard_map.79 = (bf16[4096,512]{1,0:T(8,128)(2,1)S(1)}, bf16[16,256,512]{2,1,0:T(8,128)(2,1)S(1)}, f32[8,64,512]{2,1,0:T(8,128)S(1)}) custom-call(s32[4]{0:T(128)S(1)} %pad_add_fusion.1.who_ref, s32[16]{0:T(128)S(1)} %dynamic-slice_bitcast_fusion.bases_ref, ...), custom_call_target="tpu_custom_call", output_to_operand_aliasing={{0}: (4, {}), {1}: (5, {}), {2}: (6, {})} | custom-call | flops 1 | bytes 1 | tf_op jit(solution)/shard_map/pallas_call | solution.py:141
  38.7 3.2 %collective-permute-start.10 = (bf16[256,512]{1,0:T(8,128)(2,1)S(1)}, bf16[256,512]{1,0:T(8,128)(2,1)S(1)}, u32[]{:S(2)}, u32[]{:S(2)}) collective-permute-start(bf16[256,512]{1,0:T(8,128)(2,1)S(1)} %collective-permute-done.5.refs_1_), channel_id=1, source_target_pairs={{0,4},{1,5},{2,6},{3,7},{4,12},{5,13},{6,14},{7,15},{8,0},{9,1},{1... | collective-permute-start | bytes 786440 | tf_op jit(solution)/shard_map/ppermute | solution.py:227
  41.9 2.5 %collective-permute-start.16 = (bf16[512,512]{1,0:T(8,128)(2,1)S(1)}, bf16[512,512]{1,0:T(8,128)(2,1)S(1)}, u32[]{:S(2)}, u32[]{:S(2)}) collective-permute-start(bf16[512,512]{1,0:T(8,128)(2,1)S(1)} %bitcast.19), channel_id=1, source_target_pairs={{0,17},{1,16},{2,19},{3,18},{4,21},{5,20},{6,23},{7,22},{8,25},{9,... | collective-permute-start | bytes 1572872 | tf_op jit(solution)/shard_map/ppermute | solution.py:222
  44.4 1.2 %collective-permute-start.19 = (bf16[256,512]{1,0:T(8,128)(2,1)S(1)}, bf16[256,512]{1,0:T(8,128)(2,1)S(1)}, u32[]{:S(2)}, u32[]{:S(2)}) collective-permute-start(bf16[256,512]{1,0:T(8,128)(2,1)S(1)} %collective-permute-done.5.refs_1_), channel_id=1, source_target_pairs={{0,2},{1,3},{2,0},{3,1},{4,6},{5,7},{6,4},{7,5},{8,10},{9,11},{10,... | collective-permute-start | bytes 786440 | tf_op jit(solution)/shard_map/ppermute | solution.py:222
  45.6 2.9 %shard_map.80 = (bf16[4096,512]{1,0:T(8,128)(2,1)S(1)}, bf16[16,256,512]{2,1,0:T(8,128)(2,1)S(1)}, f32[8,64,512]{2,1,0:T(8,128)S(1)}) custom-call(s32[4]{0:T(128)S(1)} %pad_add_fusion.1.who_ref, s32[16]{0:T(128)S(1)} %dynamic-slice_bitcast_fusion.bases_ref, ...), custom_call_target="tpu_custom_call", output_to_operand_aliasing={{0}: (5, {}), {1}: (6, {}), {2}: (7, {})} | custom-call | flops 1 | bytes 1 | tf_op jit(solution)/shard_map/pallas_call | solution.py:141
  48.7 2.9 %shard_map.81 = (bf16[4096,512]{1,0:T(8,128)(2,1)S(1)}, bf16[16,256,512]{2,1,0:T(8,128)(2,1)S(1)}, f32[8,64,512]{2,1,0:T(8,128)S(1)}) custom-call(s32[4]{0:T(128)S(1)} %pad_add_fusion.1.who_ref, s32[16]{0:T(128)S(1)} %dynamic-slice_bitcast_fusion.bases_ref, ...), custom_call_target="tpu_custom_call", output_to_operand_aliasing={{0}: (5, {}), {1}: (6, {}), {2}: (7, {})} | custom-call | flops 1 | bytes 1 | tf_op jit(solution)/shard_map/pallas_call | solution.py:141
  51.9 2.5 %shard_map.82 = (bf16[4096,512]{1,0:T(8,128)(2,1)S(1)}, bf16[16,256,512]{2,1,0:T(8,128)(2,1)S(1)}, f32[8,64,512]{2,1,0:T(8,128)S(1)}) custom-call(s32[4]{0:T(128)S(1)} %pad_add_fusion.1.who_ref, s32[16]{0:T(128)S(1)} %dynamic-slice_bitcast_fusion.bases_ref, ...), custom_call_target="tpu_custom_call", output_to_operand_aliasing={{0}: (4, {}), {1}: (5, {}), {2}: (6, {})} | custom-call | flops 1 | bytes 1 | tf_op jit(solution)/shard_map/pallas_call | solution.py:141
  54.6 4.4 %collective-permute-start.4 = (bf16[512,512]{1,0:T(8,128)(2,1)S(1)}, bf16[512,512]{1,0:T(8,128)(2,1)S(1)}, u32[]{:S(2)}, u32[]{:S(2)}) collective-permute-start(bf16[512,512]{1,0:T(8,128)(2,1)S(1)} %bitcast.18), channel_id=1, source_target_pairs={{0,17},{1,16},{2,19},{3,18},{4,21},{5,20},{6,23},{7,22},{8,25},{9,... | collective-permute-start | bytes 1572872 | tf_op jit(solution)/shard_map/ppermute | solution.py:222
  58.9 3.4 %shard_map.83 = (bf16[4096,512]{1,0:T(8,128)(2,1)S(1)}, bf16[16,256,512]{2,1,0:T(8,128)(2,1)S(1)}, f32[8,64,512]{2,1,0:T(8,128)S(1)}) custom-call(s32[4]{0:T(128)S(1)} %pad_add_fusion.1.who_ref, s32[16]{0:T(128)S(1)} %dynamic-slice_bitcast_fusion.bases_ref, ...), custom_call_target="tpu_custom_call", output_to_operand_aliasing={{0}: (5, {}), {1}: (6, {}), {2}: (7, {})} | custom-call | flops 1 | bytes 1 | tf_op jit(solution)/shard_map/pallas_call | solution.py:141
  62.5 1.4 %collective-permute-start.21 = (bf16[256,512]{1,0:T(8,128)(2,1)S(1)}, bf16[256,512]{1,0:T(8,128)(2,1)S(1)}, u32[]{:S(2)}, u32[]{:S(2)}) collective-permute-start(bf16[256,512]{1,0:T(8,128)(2,1)S(1)} %collective-permute-done.18.refs_1_), channel_id=1, source_target_pairs={{0,2},{1,3},{2,0},{3,1},{4,6},{5,7},{6,4},{7,5},{8,10},{9,11},{10,... | collective-permute-start | bytes 786440 | tf_op jit(solution)/shard_map/ppermute | solution.py:222
  63.9 3.4 %shard_map.84 = (bf16[4096,512]{1,0:T(8,128)(2,1)S(1)}, bf16[16,256,512]{2,1,0:T(8,128)(2,1)S(1)}, f32[8,64,512]{2,1,0:T(8,128)S(1)}) custom-call(s32[4]{0:T(128)S(1)} %pad_add_fusion.1.who_ref, s32[16]{0:T(128)S(1)} %dynamic-slice_bitcast_fusion.bases_ref, ...), custom_call_target="tpu_custom_call", output_to_operand_aliasing={{0}: (5, {}), {1}: (6, {}), {2}: (7, {})} | custom-call | flops 1 | bytes 1 | tf_op jit(solution)/shard_map/pallas_call | solution.py:141
  67.3 3.4 %shard_map.85 = (bf16[4096,512]{1,0:T(8,128)(2,1)S(1)}, bf16[16,256,512]{2,1,0:T(8,128)(2,1)S(1)}, f32[8,64,512]{2,1,0:T(8,128)S(1)}) custom-call(s32[4]{0:T(128)S(1)} %pad_add_fusion.1.who_ref, s32[16]{0:T(128)S(1)} %dynamic-slice_bitcast_fusion.bases_ref, ...), custom_call_target="tpu_custom_call", output_to_operand_aliasing={{0}: (4, {}), {1}: (5, {}), {2}: (6, {})} | custom-call | flops 1 | bytes 1 | tf_op jit(solution)/shard_map/pallas_call | solution.py:141
  70.9 3.9 %shard_map.86 = (bf16[4096,512]{1,0:T(8,128)(2,1)S(1)}, bf16[16,256,512]{2,1,0:T(8,128)(2,1)S(1)}, f32[8,64,512]{2,1,0:T(8,128)S(1)}) custom-call(s32[4]{0:T(128)S(1)} %pad_add_fusion.1.who_ref, s32[16]{0:T(128)S(1)} %dynamic-slice_bitcast_fusion.bases_ref, ...), custom_call_target="tpu_custom_call", output_to_operand_aliasing={{0}: (5, {}), {1}: (6, {}), {2}: (7, {})} | custom-call | flops 1 | bytes 1 | tf_op jit(solution)/shard_map/pallas_call | solution.py:141
  74.8 1.3 %collective-permute-done.21.refs_0_ = bf16[256,512]{1,0:T(8,128)(2,1)S(1)} collective-permute-done((bf16[256,512]{1,0:T(8,128)(2,1)S(1)}, bf16[256,512]{1,0:T(8,128)(2,1)S(1)}, u32[]{:S(2)}, u32[]{:S(2)}) %collective-permute-start.21) | collective-permute-done | bytes 262176 | tf_op jit(solution)/shard_map/ppermute | solution.py:222
  76.1 3.0 %shard_map.87 = (bf16[4096,512]{1,0:T(8,128)(2,1)S(1)}, bf16[16,256,512]{2,1,0:T(8,128)(2,1)S(1)}, f32[8,64,512]{2,1,0:T(8,128)S(1)}) custom-call(s32[4]{0:T(128)S(1)} %pad_add_fusion.1.who_ref, s32[16]{0:T(128)S(1)} %dynamic-slice_bitcast_fusion.bases_ref, ...), custom_call_target="tpu_custom_call", output_to_operand_aliasing={{0}: (4, {}), {1}: (5, {}), {2}: (6, {})} | custom-call | flops 1 | bytes 1 | tf_op jit(solution)/shard_map/pallas_call | solution.py:141
  79.1 2.7 %collective-permute-done.20.refs_0_ = bf16[256,512]{1,0:T(8,128)(2,1)S(1)} collective-permute-done((bf16[256,512]{1,0:T(8,128)(2,1)S(1)}, bf16[256,512]{1,0:T(8,128)(2,1)S(1)}, u32[]{:S(2)}, u32[]{:S(2)}) %collective-permute-start.20) | collective-permute-done | bytes 262176 | tf_op jit(solution)/shard_map/ppermute | solution.py:222
  81.7 3.0 %shard_map.88 = (bf16[4096,512]{1,0:T(8,128)(2,1)S(1)}, bf16[16,256,512]{2,1,0:T(8,128)(2,1)S(1)}, f32[8,64,512]{2,1,0:T(8,128)S(1)}, bf16[2,64,512]{2,1,0:T(8,128)(2,1)S(1)}, bf16[2,64,512]{2,1,0:T(8,128)(2,1)S(1)}) custom-call(s32[4]{0:T(128)S(1)} %pad_add_fusion.1.who_ref, ...), custom_call_target="tpu_custom_call", output_to_operand_aliasing={{0}: (4, {}), {1}: (5, {}), {2}: (6, {})} | custom-call | flops 1 | bytes 1 | tf_op jit(solution)/shard_map/pallas_call | solution.py:141
  84.7 4.3 %shard_map.89 = (bf16[4096,512]{1,0:T(8,128)(2,1)S(1)}, bf16[16,256,512]{2,1,0:T(8,128)(2,1)S(1)}, f32[8,64,512]{2,1,0:T(8,128)S(1)}, bf16[2,64,512]{2,1,0:T(8,128)(2,1)S(1)}) custom-call(s32[4]{0:T(128)S(1)} %pad_add_fusion.1.who_ref, s32[16]{0:T(128)S(1)} %dynamic-slice_bitcast_fusion.bases_ref, ...), custom_call_target="tpu_custom_call", output_to_operand_aliasing={{0}: (4, {}), {1}: (5, {}), {2}: (6, {})} | custom-call | flops 1 | bytes 1 | tf_op jit(solution)/shard_map/pallas_call | solution.py:141
  89.1 0.6 collective-permute-start.25
  90.1 1.1 %collective-permute-start.24 = (bf16[2,64,512]{2,1,0:T(8,128)(2,1)S(1)}, bf16[2,64,512]{2,1,0:T(8,128)(2,1)S(1)}, u32[]{:S(2)}, u32[]{:S(2)}) collective-permute-start(bf16[2,64,512]{2,1,0:T(8,128)(2,1)S(1)} %get-tuple-element.161), channel_id=1, source_target_pairs={{0,16},{1,17},{2,18},{3,19},{4,20},{5,21},{6,22},{7,23},{8,24},{9,... | collective-permute-start | bytes 393224 | tf_op jit(solution)/shard_map/ppermute | solution.py:222
  91.2 4.0 %collective-permute-done.25.d_ref = bf16[2,64,512]{2,1,0:T(8,128)(2,1)S(1)} collective-permute-done((bf16[2,64,512]{2,1,0:T(8,128)(2,1)S(1)}, bf16[2,64,512]{2,1,0:T(8,128)(2,1)S(1)}, u32[]{:S(2)}, u32[]{:S(2)}) %collective-permute-start.25) | collective-permute-done | bytes 131104 | tf_op jit(solution)/shard_map/ppermute | solution.py:222
  95.2 2.8 %collective-permute-done.24.c_ref = bf16[2,64,512]{2,1,0:T(8,128)(2,1)S(1)} collective-permute-done((bf16[2,64,512]{2,1,0:T(8,128)(2,1)S(1)}, bf16[2,64,512]{2,1,0:T(8,128)(2,1)S(1)}, u32[]{:S(2)}, u32[]{:S(2)}) %collective-permute-start.24) | collective-permute-done | bytes 131104 | tf_op jit(solution)/shard_map/ppermute | solution.py:222
  98.0 3.0 %shard_map.90 = bf16[2,64,4096]{2,1,0:T(8,128)(2,1)} custom-call(s32[8,128]{1,0:T(8,128)S(1)} %bitcast.17, bf16[256,256]{1,0:T(8,128)(2,1)S(1)} %shard_map.73.basis_ref, f32[8,64,512]{2,1,0:T(8,128)S(1)} %get-tuple-element.159.own_ref, bf16[2,64,512]{2,1,0:T(8,128)(2,1)S(1)} %collective-permute-done.23.b_ref, ...), custom_call_target="tpu_custom_call" | custom-call | flops 1 | bytes 1 | tf_op jit(solution)/shard_map/pallas_call | solution.py:349
  (56 shorter events, 2.8 us)
Async XLA Ops:
  0.1 2.2 %copy-start = (bf16[128,8,2048]{2,1,0:T(8,128)(2,1)S(1)}, bf16[128,8,2048]{2,1,0:T(8,128)(2,1)}, u32[]{:S(2)}) copy-start(bf16[128,8,2048]{2,1,0:T(8,128)(2,1)} %refs_1_.3) | copy-start | bytes 12582916
  2.3 1.2 %copy-start.2 = (bf16[4,64,2048]{2,1,0:T(8,128)(2,1)S(1)}, bf16[4,64,2048]{2,1,0:T(8,128)(2,1)}, u32[]{:S(2)}) copy-start(bf16[4,64,2048]{2,1,0:T(8,128)(2,1)} %param.12) | copy-start | bytes 3145732
  3.5 6.2 %copy-start.5 = (s32[128,8]{0,1:T(8,128)S(1)}, s32[128,8]{0,1:T(8,128)}, u32[]{:S(2)}) copy-start(s32[128,8]{0,1:T(8,128)} %param.9) | copy-start | bytes 12292
  3.5 14.2 %copy-start.12 = (s32[128]{0:T(128)S(1)}, s32[128]{0:T(128)}, u32[]{:S(2)}) copy-start(s32[128]{0:T(128)} %param.10) | copy-start | bytes 1540
  3.5 20.5 %copy-start.3 = (bf16[128,7168]{1,0:T(8,128)(2,1)S(1)}, bf16[128,7168]{1,0:T(8,128)(2,1)}, u32[]{:S(2)}) copy-start(bf16[128,7168]{1,0:T(8,128)(2,1)} %hidden_ref.1) | copy-start | bytes 5505028
  4.9 0.8 copy-start.11
  7.2 0.8 copy-start.6
  8.0 0.8 copy-start.8
  8.8 0.8 copy-start.10
  9.6 20.8 %collective-permute-start.9 = (bf16[1024,512]{1,0:T(8,128)(2,1)}, bf16[1024,512]{1,0:T(8,128)(2,1)S(1)}, u32[]{:S(2)}, u32[]{:S(2)}) collective-permute-start(bf16[1024,512]{1,0:T(8,128)(2,1)} %bitcast.10), channel_id=1, source_target_pairs={{0,1},{1,0},{2,3},{3,2},{4,5},{5,4},{6,7},{7,6},{8,9},{9,8},{10,11... | collective-permute-start | bytes 3145736 | tf_op jit(solution)/shard_map/ppermute | solution.py:222
  9.9 5.0 %collective-permute-start = (s32[1,1024]{1,0:T(1,128)S(1)}, s32[1,1024]{1,0:T(1,128)S(1)}, u32[]{:S(2)}, u32[]{:S(2)}) collective-permute-start(s32[1,1024]{1,0:T(1,128)S(1)} %reshape.28), channel_id=1, source_target_pairs={{0,1},{1,0},{2,3},{3,2},{4,5},{5,4},{6,7},{7,6},{8,9},{9,8},{10,11... | collective-permute-start | bytes 12296 | tf_op jit(solution)/shard_map/ppermute | solution.py:222
  10.4 5.7 %collective-permute-start.1 = (s32[1,1024]{1,0:T(1,128)S(1)}, s32[1,1024]{1,0:T(1,128)S(1)}, u32[]{:S(2)}, u32[]{:S(2)}) collective-permute-start(s32[1,1024]{1,0:T(1,128)S(1)} %reshape.28), channel_id=1, source_target_pairs={{0,16},{1,17},{2,18},{3,19},{4,20},{5,21},{6,22},{7,23},{8,24},{9,... | collective-permute-start | bytes 12296 | tf_op jit(solution)/shard_map/ppermute | solution.py:222
  12.7 3.8 %collective-permute-start.2 = (s32[1,1024]{1,0:T(1,128)S(1)}, s32[1,1024]{1,0:T(1,128)S(1)}, u32[]{:S(2)}, u32[]{:S(2)}) collective-permute-start(s32[1,1024]{1,0:T(1,128)S(1)} %reshape.28), channel_id=1, source_target_pairs={{0,17},{1,16},{2,19},{3,18},{4,21},{5,20},{6,23},{7,22},{8,25},{9,... | collective-permute-start | bytes 12296 | tf_op jit(solution)/shard_map/ppermute | solution.py:222
  13.0 9.7 %collective-permute-start.8 = (bf16[256,512]{1,0:T(8,128)(2,1)}, bf16[256,512]{1,0:T(8,128)(2,1)}, u32[]{:S(2)}, u32[]{:S(2)}) collective-permute-start(bf16[256,512]{1,0:T(8,128)(2,1)} %get-tuple-element.84.refs_0_), channel_id=1, source_target_pairs={{0,4},{1,5},{2,6},{3,7},{4,12},{5,13},{6,14},{7,15},{8,0},{9,1},{1... | collective-permute-start | bytes 786440 | tf_op jit(solution)/shard_map/ppermute | solution.py:227
  14.8 18.5 %collective-permute-start.7 = (bf16[256,512]{1,0:T(8,128)(2,1)}, bf16[256,512]{1,0:T(8,128)(2,1)}, u32[]{:S(2)}, u32[]{:S(2)}) collective-permute-start(bf16[256,512]{1,0:T(8,128)(2,1)} %get-tuple-element.84.refs_0_), channel_id=1, source_target_pairs={{0,2},{1,3},{2,0},{3,1},{4,6},{5,7},{6,4},{7,5},{8,10},{9,11},{10,... | collective-permute-start | bytes 786440 | tf_op jit(solution)/shard_map/ppermute | solution.py:222
  16.1 2.4 %collective-permute-start.3 = (bf16[256,512]{1,0:T(8,128)(2,1)}, bf16[256,512]{1,0:T(8,128)(2,1)}, u32[]{:S(2)}, u32[]{:S(2)}) collective-permute-start(bf16[256,512]{1,0:T(8,128)(2,1)} %get-tuple-element.85), channel_id=1, source_target_pairs={{0,1},{1,0},{2,3},{3,2},{4,5},{5,4},{6,7},{7,6},{8,9},{9,8},{10,11... | collective-permute-start | bytes 786440 | tf_op jit(solution)/shard_map/ppermute | solution.py:222
  16.5 20.3 %collective-permute-start.6 = (bf16[512,512]{1,0:T(8,128)(2,1)}, bf16[512,512]{1,0:T(8,128)(2,1)S(1)}, u32[]{:S(2)}, u32[]{:S(2)}) collective-permute-start(bf16[512,512]{1,0:T(8,128)(2,1)} %bitcast.21), channel_id=1, source_target_pairs={{0,16},{1,17},{2,18},{3,19},{4,20},{5,21},{6,22},{7,23},{8,24},{9,... | collective-permute-start | bytes 1572872 | tf_op jit(solution)/shard_map/ppermute | solution.py:222
  18.5 20.2 %collective-permute-start.5 = (bf16[256,512]{1,0:T(8,128)(2,1)}, bf16[256,512]{1,0:T(8,128)(2,1)S(1)}, u32[]{:S(2)}, u32[]{:S(2)}) collective-permute-start(bf16[256,512]{1,0:T(8,128)(2,1)} %collective-permute-done.3.refs_1_), channel_id=1, source_target_pairs={{0,4},{1,5},{2,6},{3,7},{4,12},{5,13},{6,14},{7,15},{8,0},{9,1},{1... | collective-permute-start | bytes 786440 | tf_op jit(solution)/shard_map/ppermute | solution.py:227
  22.7 28.9 %collective-permute-start.11 = (bf16[512,512]{1,0:T(8,128)(2,1)}, bf16[512,512]{1,0:T(8,128)(2,1)S(1)}, u32[]{:S(2)}, u32[]{:S(2)}) collective-permute-start(bf16[512,512]{1,0:T(8,128)(2,1)} %bitcast.20), channel_id=1, source_target_pairs={{0,16},{1,17},{2,18},{3,19},{4,20},{5,21},{6,22},{7,23},{8,24},{9,... | collective-permute-start | bytes 1572872 | tf_op jit(solution)/shard_map/ppermute | solution.py:222
  24.0 1.2 %copy-start.4 = (bf16[64,7168]{1,0:T(8,128)(2,1)S(1)}, bf16[64,7168]{1,0:T(8,128)(2,1)}, u32[]{:S(2)}) copy-start(bf16[64,7168]{1,0:T(8,128)(2,1)} %proj_ref.1) | copy-start | bytes 2752516
  25.9 2.2 %copy-start.1 = (bf16[128,8,2048]{2,1,0:T(8,128)(2,1)S(1)}, bf16[128,8,2048]{2,1,0:T(8,128)(2,1)}, u32[]{:S(2)}) copy-start(bf16[128,8,2048]{2,1,0:T(8,128)(2,1)} %refs_1_.3) | copy-start | bytes 12582916
  30.5 11.4 %collective-permute-start.14 = (bf16[256,512]{1,0:T(8,128)(2,1)}, bf16[256,512]{1,0:T(8,128)(2,1)S(1)}, u32[]{:S(2)}, u32[]{:S(2)}) collective-permute-start(bf16[256,512]{1,0:T(8,128)(2,1)} %collective-permute-done.3.refs_1_), channel_id=1, source_target_pairs={{0,2},{1,3},{2,0},{3,1},{4,6},{5,7},{6,4},{7,5},{8,10},{9,11},{10,... | collective-permute-start | bytes 786440 | tf_op jit(solution)/shard_map/ppermute | solution.py:222
  33.3 11.0 %collective-permute-start.13 = (bf16[256,512]{1,0:T(8,128)(2,1)}, bf16[256,512]{1,0:T(8,128)(2,1)S(1)}, u32[]{:S(2)}, u32[]{:S(2)}) collective-permute-start(bf16[256,512]{1,0:T(8,128)(2,1)} %collective-permute-done.8.refs_1_), channel_id=1, source_target_pairs={{0,4},{1,5},{2,6},{3,7},{4,12},{5,13},{6,14},{7,15},{8,0},{9,1},{1... | collective-permute-start | bytes 786440 | tf_op jit(solution)/shard_map/ppermute | solution.py:227
  36.9 11.7 %collective-permute-start.12 = (bf16[256,512]{1,0:T(8,128)(2,1)}, bf16[256,512]{1,0:T(8,128)(2,1)S(1)}, u32[]{:S(2)}, u32[]{:S(2)}) collective-permute-start(bf16[256,512]{1,0:T(8,128)(2,1)} %collective-permute-done.8.refs_1_), channel_id=1, source_target_pairs={{0,2},{1,3},{2,0},{3,1},{4,6},{5,7},{6,4},{7,5},{8,10},{9,11},{10,... | collective-permute-start | bytes 786440 | tf_op jit(solution)/shard_map/ppermute | solution.py:222
  37.2 4.7 %copy-start.9 = (bf16[64,8,512]{2,1,0:T(8,128)(2,1)S(1)}, bf16[64,8,512]{2,1,0:T(8,128)(2,1)}, u32[]{:S(2)}) copy-start(bf16[64,8,512]{2,1,0:T(8,128)(2,1)} %copy-done.8) | copy-start | bytes 1572868
  38.7 15.7 %collective-permute-start.10 = (bf16[256,512]{1,0:T(8,128)(2,1)S(1)}, bf16[256,512]{1,0:T(8,128)(2,1)S(1)}, u32[]{:S(2)}, u32[]{:S(2)}) collective-permute-start(bf16[256,512]{1,0:T(8,128)(2,1)S(1)} %collective-permute-done.5.refs_1_), channel_id=1, source_target_pairs={{0,4},{1,5},{2,6},{3,7},{4,12},{5,13},{6,14},{7,15},{8,0},{9,1},{1... | collective-permute-start | bytes 786440 | tf_op jit(solution)/shard_map/ppermute | solution.py:227
  41.9 25.5 %collective-permute-start.16 = (bf16[512,512]{1,0:T(8,128)(2,1)S(1)}, bf16[512,512]{1,0:T(8,128)(2,1)S(1)}, u32[]{:S(2)}, u32[]{:S(2)}) collective-permute-start(bf16[512,512]{1,0:T(8,128)(2,1)S(1)} %bitcast.19), channel_id=1, source_target_pairs={{0,17},{1,16},{2,19},{3,18},{4,21},{5,20},{6,23},{7,22},{8,25},{9,... | collective-permute-start | bytes 1572872 | tf_op jit(solution)/shard_map/ppermute | solution.py:222
  44.4 10.2 %collective-permute-start.19 = (bf16[256,512]{1,0:T(8,128)(2,1)S(1)}, bf16[256,512]{1,0:T(8,128)(2,1)S(1)}, u32[]{:S(2)}, u32[]{:S(2)}) collective-permute-start(bf16[256,512]{1,0:T(8,128)(2,1)S(1)} %collective-permute-done.5.refs_1_), channel_id=1, source_target_pairs={{0,2},{1,3},{2,0},{3,1},{4,6},{5,7},{6,4},{7,5},{8,10},{9,11},{10,... | collective-permute-start | bytes 786440 | tf_op jit(solution)/shard_map/ppermute | solution.py:222
  48.6 13.8 %collective-permute-start.18 = (bf16[256,512]{1,0:T(8,128)(2,1)S(1)}, bf16[256,512]{1,0:T(8,128)(2,1)S(1)}, u32[]{:S(2)}, u32[]{:S(2)}) collective-permute-start(bf16[256,512]{1,0:T(8,128)(2,1)S(1)} %collective-permute-done.13.refs_1_), channel_id=1, source_target_pairs={{0,4},{1,5},{2,6},{3,7},{4,12},{5,13},{6,14},{7,15},{8,0},{9,1},{1... | collective-permute-start | bytes 786440 | tf_op jit(solution)/shard_map/ppermute | solution.py:227
  51.6 10.9 %collective-permute-start.17 = (bf16[256,512]{1,0:T(8,128)(2,1)S(1)}, bf16[256,512]{1,0:T(8,128)(2,1)S(1)}, u32[]{:S(2)}, u32[]{:S(2)}) collective-permute-start(bf16[256,512]{1,0:T(8,128)(2,1)S(1)} %collective-permute-done.13.refs_1_), channel_id=1, source_target_pairs={{0,2},{1,3},{2,0},{3,1},{4,6},{5,7},{6,4},{7,5},{8,10},{9,11},{10,... | collective-permute-start | bytes 786440 | tf_op jit(solution)/shard_map/ppermute | solution.py:222
  51.9 2.7 %copy-start.7 = (bf16[64,8,512]{2,1,0:T(8,128)(2,1)S(1)}, bf16[64,8,512]{2,1,0:T(8,128)(2,1)}, u32[]{:S(2)}) copy-start(bf16[64,8,512]{2,1,0:T(8,128)(2,1)} %copy-done.6) | copy-start | bytes 1572868
  54.4 16.4 %collective-permute-start.15 = (bf16[256,512]{1,0:T(8,128)(2,1)S(1)}, bf16[256,512]{1,0:T(8,128)(2,1)S(1)}, u32[]{:S(2)}, u32[]{:S(2)}) collective-permute-start(bf16[256,512]{1,0:T(8,128)(2,1)S(1)} %collective-permute-done.10.refs_1_), channel_id=1, source_target_pairs={{0,4},{1,5},{2,6},{3,7},{4,12},{5,13},{6,14},{7,15},{8,0},{9,1},{1... | collective-permute-start | bytes 786440 | tf_op jit(solution)/shard_map/ppermute | solution.py:227
  54.6 30.2 %collective-permute-start.4 = (bf16[512,512]{1,0:T(8,128)(2,1)S(1)}, bf16[512,512]{1,0:T(8,128)(2,1)S(1)}, u32[]{:S(2)}, u32[]{:S(2)}) collective-permute-start(bf16[512,512]{1,0:T(8,128)(2,1)S(1)} %bitcast.18), channel_id=1, source_target_pairs={{0,17},{1,16},{2,19},{3,18},{4,21},{5,20},{6,23},{7,22},{8,25},{9,... | collective-permute-start | bytes 1572872 | tf_op jit(solution)/shard_map/ppermute | solution.py:222
  62.4 8.5 %collective-permute-start.22 = (bf16[256,512]{1,0:T(8,128)(2,1)S(1)}, bf16[256,512]{1,0:T(8,128)(2,1)S(1)}, u32[]{:S(2)}, u32[]{:S(2)}) collective-permute-start(bf16[256,512]{1,0:T(8,128)(2,1)S(1)} %collective-permute-done.10.refs_1_), channel_id=1, source_target_pairs={{0,2},{1,3},{2,0},{3,1},{4,6},{5,7},{6,4},{7,5},{8,10},{9,11},{10,... | collective-permute-start | bytes 786440 | tf_op jit(solution)/shard_map/ppermute | solution.py:222
  62.5 13.6 %collective-permute-start.21 = (bf16[256,512]{1,0:T(8,128)(2,1)S(1)}, bf16[256,512]{1,0:T(8,128)(2,1)S(1)}, u32[]{:S(2)}, u32[]{:S(2)}) collective-permute-start(bf16[256,512]{1,0:T(8,128)(2,1)S(1)} %collective-permute-done.18.refs_1_), channel_id=1, source_target_pairs={{0,2},{1,3},{2,0},{3,1},{4,6},{5,7},{6,4},{7,5},{8,10},{9,11},{10,... | collective-permute-start | bytes 786440 | tf_op jit(solution)/shard_map/ppermute | solution.py:222
  70.8 11.0 %collective-permute-start.20 = (bf16[256,512]{1,0:T(8,128)(2,1)S(1)}, bf16[256,512]{1,0:T(8,128)(2,1)S(1)}, u32[]{:S(2)}, u32[]{:S(2)}) collective-permute-start(bf16[256,512]{1,0:T(8,128)(2,1)S(1)} %collective-permute-done.15.refs_1_), channel_id=1, source_target_pairs={{0,2},{1,3},{2,0},{3,1},{4,6},{5,7},{6,4},{7,5},{8,10},{9,11},{10,... | collective-permute-start | bytes 786440 | tf_op jit(solution)/shard_map/ppermute | solution.py:222
  89.1 6.1 %collective-permute-start.25 = (bf16[2,64,512]{2,1,0:T(8,128)(2,1)S(1)}, bf16[2,64,512]{2,1,0:T(8,128)(2,1)S(1)}, u32[]{:S(2)}, u32[]{:S(2)}) collective-permute-start(bf16[2,64,512]{2,1,0:T(8,128)(2,1)S(1)} %get-tuple-element.162), channel_id=1, source_target_pairs={{0,17},{1,16},{2,19},{3,18},{4,21},{5,20},{6,23},{7,22},{8,25},{9,... | collective-permute-start | bytes 393224 | tf_op jit(solution)/shard_map/ppermute | solution.py:222
  89.7 5.5 %collective-permute-start.23 = (bf16[2,64,512]{2,1,0:T(8,128)(2,1)S(1)}, bf16[2,64,512]{2,1,0:T(8,128)(2,1)S(1)}, u32[]{:S(2)}, u32[]{:S(2)}) collective-permute-start(bf16[2,64,512]{2,1,0:T(8,128)(2,1)S(1)} %get-tuple-element.160), channel_id=1, source_target_pairs={{0,1},{1,0},{2,3},{3,2},{4,5},{5,4},{6,7},{7,6},{8,9},{9,8},{10,11... | collective-permute-start | bytes 393224 | tf_op jit(solution)/shard_map/ppermute | solution.py:222
  90.1 7.9 %collective-permute-start.24 = (bf16[2,64,512]{2,1,0:T(8,128)(2,1)S(1)}, bf16[2,64,512]{2,1,0:T(8,128)(2,1)S(1)}, u32[]{:S(2)}, u32[]{:S(2)}) collective-permute-start(bf16[2,64,512]{2,1,0:T(8,128)(2,1)S(1)} %get-tuple-element.161), channel_id=1, source_target_pairs={{0,16},{1,17},{2,18},{3,19},{4,20},{5,21},{6,22},{7,23},{8,24},{9,... | collective-permute-start | bytes 393224 | tf_op jit(solution)/shard_map/ppermute | solution.py:222

commit v5 on v4

v5 whole, which is shorter than its diff:
```python
import functools

import jax
import jax.numpy as jnp
import numpy as np
from jax import lax
from jax.experimental import pallas as pl
from jax.experimental.pallas import tpu as pltpu
from jax.sharding import PartitionSpec as P

SEG_DEV = 2
CORES = 2
SIDES = 2
QUAD = 4
PIECES = 4
LANES = 128
ALIGN = 16
DIGIT = 32
BOTH = ("groups", "expert")
MIB = 1024 * 1024
VMEM = pl.BlockSpec(memory_space=pltpu.VMEM)
SMEM = pl.BlockSpec(memory_space=pltpu.SMEM)
HBM = pl.BlockSpec(memory_space=pl.ANY)
QUICK = pl.CostEstimate(flops=1, bytes_accessed=1, transcendentals=0)
NT = (((1,), (1,)), ((), ()))


def columns_of(ref, who, width):
    return ref.at[..., pl.ds(pl.multiple_of(who * width, width), width)]


def key_column(routes_row):
    count = routes_row.shape[1]
    keys = routes_row * count + lax.broadcasted_iota(jnp.int32, (1, count), 1)
    return jnp.broadcast_to(keys.astype(jnp.float32), (8, count)).T[:, 0:1]


def ranks(column, keys):
    total = jnp.zeros(keys.shape, jnp.float32)
    for first in range(0, column.shape[0], 128):
        smaller = jnp.where(column[first : first + 128] < keys, 1.0, 0.0)
        total = total + jnp.sum(smaller, axis=0, keepdims=True)
    return total


def sort_kernel(
    who_ref,
    routes_ref,
    weight_ref,
    grads_ref,
    mine_ref,
    core_ref,
    starts_ref,
    head_ref,
    order_ref,
    piece_ref,
    next_ref,
    stage,
    sems,
):
    width = mine_ref.shape[1]
    copies = [
        pltpu.make_async_copy(columns_of(grads_ref, who_ref[2], width), stage, sems.at[0]),
        pltpu.make_async_copy(columns_of(weight_ref, who_ref[0], width), mine_ref, sems.at[1]),
        pltpu.make_async_copy(columns_of(weight_ref, who_ref[1], width), core_ref, sems.at[2]),
    ]
    for copy in copies:
        copy.start()
    routes = routes_ref[...]
    pairs = routes.shape[1]
    column = key_column(routes)
    keys = routes * pairs + lax.broadcasted_iota(jnp.int32, (1, pairs), 1)
    place = ranks(column, keys.astype(jnp.float32)).astype(jnp.int32)
    firsts = lax.broadcasted_iota(jnp.int32, starts_ref.shape, 1) * pairs
    starts = ranks(column, firsts.astype(jnp.float32)).astype(jnp.int32)
    starts_ref[...] = starts
    wide = head_ref.shape[1] - starts.shape[1]
    digits = [starts // DIGIT, starts % DIGIT]
    digits = [jnp.pad(d.astype(jnp.float32), ((0, 0), (0, wide))) for d in digits]
    row = lax.broadcasted_iota(jnp.int32, head_ref.shape, 0)
    head = jnp.where(row == 0, digits[0], jnp.where(row == 1, digits[1], 0.0))
    head_ref[...] = head.astype(jnp.bfloat16)
    rows = next_ref.shape[0]
    for first in range(0, pairs, rows):
        ids = first + lax.broadcasted_iota(jnp.int32, (rows, pairs), 0)
        order_ref[first : first + rows, :] = jnp.where(place == ids, 1.0, 0.0).astype(jnp.bfloat16)
    for copy in copies:
        copy.wait()
    sorted_rows = jnp.dot(
        order_ref[0 : 2 * rows, :],
        stage[...].reshape(pairs, width),
        preferred_element_type=jnp.float32,
    ).astype(jnp.bfloat16)
    piece_ref[0:rows, :] = sorted_rows[0:rows]
    piece_ref[rows:, :] = head_ref[...]
    next_ref[...] = sorted_rows[rows:]


def permute_kernel(plan, who_ref, order_ref, head_ref, grads_ref, *refs):
    outs, stage, sems = refs[:-2], refs[-2], refs[-1]
    pairs, width = order_ref.shape[0], outs[0].shape[1]
    devices = sorted({device for device, _, _ in plan})
    copies = {
        device: pltpu.make_async_copy(
            columns_of(grads_ref, who_ref[device], width), stage.at[i], sems.at[i]
        )
        for i, device in enumerate(devices)
    }
    for copy in copies.values():
        copy.start()
    for i, device in enumerate(devices):
        copies[device].wait()
        grads = stage[i].reshape(pairs, width)
        for out, (target, first, rows) in zip(outs, plan):
            if target == device:
                out[0:rows, :] = jnp.dot(
                    order_ref[first : first + rows, :], grads, preferred_element_type=jnp.float32
                ).astype(jnp.bfloat16)
                if out.shape[0] > rows:
                    out[rows:, :] = head_ref[...]


def basis_kernel(
    hidden_ref, proj_ref, segment_ref, routes_ref, turned_ref, out_ref, order_ref
):
    projected = lax.dot_general(
        hidden_ref[...], proj_ref[...], NT, preferred_element_type=jnp.float32
    )
    zero = jnp.zeros_like(projected)
    picked = [jnp.where(segment_ref[...] == s, projected, zero) for s in range(SEG_DEV)]
    even = jnp.concatenate([b for p in picked for b in (p, zero)], axis=1)
    odd = jnp.concatenate([b for p in picked for b in (zero, p)], axis=1)
    out_ref[...] = jnp.concatenate([even, odd], axis=0).astype(out_ref.dtype)
    pairs = routes_ref.shape[1]
    tops, tokens = turned_ref.shape
    column = key_column(routes_ref[...])
    at = [
        turned_ref[k : k + 1, :] * pairs + lax.broadcasted_iota(jnp.int32, (1, tokens), 1) * tops + k
        for k in range(tops)
    ]
    place = ranks(column, jnp.concatenate(at, axis=1).astype(jnp.float32)).astype(jnp.int32)
    for first in range(0, pairs, 256):
        ids = first + lax.broadcasted_iota(jnp.int32, (256, pairs), 0)
        order_ref[first : first + 256, :] = jnp.where(place == ids, 1.0, 0.0).astype(jnp.bfloat16)


def packed(total, first, pairs, rank):
    half = pairs // 2
    low = lax.broadcasted_iota(jnp.int32, (half, LANES), 1) < rank
    one = total[first : first + half, :]
    two = total[first + half : first + pairs, :]
    return jnp.where(low, one + pltpu.roll(one, rank, 1), two + pltpu.roll(two, rank, 1))


def partial_kernel(
    rank, pairs, window, new_tokens, new_units, tasks, fresh, sends, groups, bases_ref, *refs
):
    start_refs = dict(zip(groups, refs))
    refs = refs[len(groups) :]
    token_refs, refs = refs[: len(new_tokens)], refs[len(new_tokens) :]
    unit_refs, refs = refs[: len(new_units)], refs[len(new_units) :]
    if fresh:
        tokens, units, total = refs
        send_refs = ()
        total[...] = jnp.zeros_like(total)
    else:
        tokens, units, total = refs[3:6]
        send_refs = refs[6:]
    for ref, (first, count) in zip(token_refs, new_tokens):
        tokens[first : first + count, :] = ref[0:count, :]
    for ref, place in zip(unit_refs, new_units):
        units[place] = ref[...]
    cols = units.shape[1]
    held = cols // rank
    per_tile = LANES // rank
    low = lax.broadcasted_iota(jnp.int32, (1, LANES), 1) < rank

    def process(w, members):
        base = bases_ref[w]
        heres, offsets = [], []
        for g in members:
            at = jnp.minimum(start_refs[g][0, base] & -ALIGN, pairs - window)
            offsets.append(at)
            heres.append(pl.ds(pl.multiple_of(g * pairs + at, ALIGN), window))
        rows = [tokens[here, :] for here in heres]
        rows = jnp.concatenate(rows, axis=0) if len(rows) > 1 else rows[0]
        dense = lax.dot_general(rows, units[w], NT, preferred_element_type=jnp.float32)
        for n, g in enumerate(members):
            value = total[heres[n], :]
            number = offsets[n] + lax.broadcasted_iota(jnp.int32, (window, LANES), 0)
            for j in range(cols // LANES):
                edge = [start_refs[g][0, base + j * per_tile + i] for i in range(per_tile + 1)]
                inside = (number >= jnp.where(low, edge[0], edge[1])) & (
                    number < jnp.where(low, edge[1], edge[2])
                )
                part = dense[n * window : (n + 1) * window, j * LANES : (j + 1) * LANES]
                value = jnp.where(inside, part, value)
            total[heres[n], :] = value

    for task in tasks:
        if task[0] == "units":
            _, members, first_w, count = task

            def each(i, carry, members=members, first_w=first_w):
                process(first_w + i, members)
                return carry

        else:
            _, member, first_row, end_row, first_w, count = task

            def each(
                i, carry, member=member, first_row=first_row, end_row=end_row, first_w=first_w
            ):
                w = first_w + i
                base = bases_ref[w]
                touches = (start_refs[member][0, base] < end_row) & (
                    start_refs[member][0, base + held] > first_row
                )

                @pl.when(touches)
                def _():
                    process(w, [member])

                return carry

        lax.fori_loop(0, count, each, 0)
    for ref, g in zip(send_refs, sends):
        ref[...] = packed(total, g * pairs, pairs, rank).astype(ref.dtype)


def accumulate(
    state, bases, starts, tokens, units, tasks, rank, pairs, window, places=0, sends=()
):
    fresh = state is None
    operands = [bases, *starts.values(), *[a for a, _, _ in tokens], *[a for a, _ in units]]
    specs = [SMEM] * (1 + len(starts)) + [VMEM] * (len(tokens) + len(units))
    if fresh:
        width = units[0][0].shape[1]
        shapes = [
            jax.ShapeDtypeStruct((QUAD * pairs, width), jnp.bfloat16),
            jax.ShapeDtypeStruct((places, *units[0][0].shape), jnp.bfloat16),
            jax.ShapeDtypeStruct((QUAD * pairs, LANES), jnp.float32),
        ]
        aliases = {}
    else:
        aliases = {len(operands) + i: i for i in range(3)}
        operands += state
        specs += [VMEM] * 3
        shapes = [jax.ShapeDtypeStruct(a.shape, a.dtype) for a in state]
    shapes += [jax.ShapeDtypeStruct((pairs // 2, LANES), jnp.bfloat16)] * len(sends)
    out = pl.pallas_call(
        functools.partial(
            partial_kernel,
            rank,
            pairs,
            window,
            [(first, count) for _, first, count in tokens],
            [p for _, p in units],
            tasks,
            fresh,
            sends,
            list(starts),
        ),
        out_shape=shapes,
        in_specs=specs,
        out_specs=[VMEM] * len(shapes),
        input_output_aliases=aliases,
        compiler_params=pltpu.CompilerParams(vmem_limit_bytes=20 * MIB),
        cost_estimate=QUICK,
    )(*operands)
    return list(out[:3]), list(out[3:])


def blocks_kernel(
    tops, rank, routes_ref, basis_ref, order_ref, total_ref, b_ref, c_ref, d_ref, out_ref, turned, spread
):
    half = b_ref.shape[0]
    tokens = 2 * half // tops
    value = packed(total_ref, 0, 2 * half, rank)
    for ref in (b_ref, c_ref, d_ref):
        value = value + ref[...].astype(jnp.float32)
    value = value.T
    value = jnp.concatenate([value[0:rank], value[rank : 2 * rank]], axis=1).astype(jnp.bfloat16)
    turned[...] = jnp.dot(value, order_ref[...], preferred_element_type=jnp.float32)
    experts = out_ref.shape[1]

    def expand(tile, carry):
        first = pl.multiple_of(tile * 8, 8)
        ids = first + lax.broadcasted_iota(jnp.int32, (8, tokens), 0)
        masks = [routes_ref[k : k + 1, :] == ids for k in range(tops)]
        for r in range(rank):
            value = jnp.zeros((8, tokens), jnp.float32)
            for k in range(tops):
                row = turned[r : r + 1, k * tokens : (k + 1) * tokens]
                value = jnp.where(masks[k], row, value)
            spread[r, pl.ds(first, 8), :] = value
        return carry

    lax.fori_loop(0, experts // 8, expand, 0)
    for pair in range(rank // 2):
        both = jnp.concatenate([spread[2 * pair], spread[2 * pair + 1]], axis=1)
        block = jnp.dot(
            both.astype(jnp.bfloat16), basis_ref[...], preferred_element_type=jnp.float32
        ).astype(jnp.bfloat16)
        for s in range(SEG_DEV):
            out_ref[s, :, pl.ds(pair * 2 * rank, 2 * rank)] = block[
                :, s * 2 * rank : (s + 1) * 2 * rank
            ]


def local(hidden_in, out_grads, routes, segments, in_proj, out_proj):
    tokens, tops = routes.shape
    exp_here, rank, width = out_proj.shape
    owners, groups = lax.axis_size("expert"), lax.axis_size("groups")
    experts = exp_here * owners
    pairs = tokens * tops
    capacity = max(2, 3 * pairs // (2 * experts))
    window = min(pairs, -(-(exp_here * capacity + ALIGN - 1) // ALIGN) * ALIGN)
    quarter = width // QUAD
    cols = exp_here * rank
    rows = pairs // PIECES
    group, index = lax.axis_index("groups"), lax.axis_index("expert")
    core = index % CORES
    slots = owners // CORES // 2
    mine = (group % SIDES) * CORES + core
    who = jnp.stack([mine, mine ^ 1, mine ^ 2, mine ^ 3]).astype(jnp.int32)
    ring = [0, *range(1, slots, 2), *range((slots - 1) // 2 * 2, 0, -2)]
    following = {a: b for a, b in zip(ring, ring[1:] + ring[:1])}
    before = {b: a for a, b in following.items()}

    def swap(array, side, bit):
        table = [
            (g * owners + e, (g ^ side) * owners + (e ^ bit))
            for g in range(groups)
            for e in range(owners)
        ]
        return lax.ppermute(array, BOTH, table)

    def onward(array, bit=0):
        wide = 2 * CORES
        table = [(e, following[e // wide] * wide + (e % wide ^ bit)) for e in range(owners)]
        return lax.ppermute(array, "expert", table)

    def tie(*arrays):
        return lax.optimization_barrier(arrays)

    rows_of = []
    for e in range(owners):
        z, y, c = e // (2 * CORES), e // CORES % 2, e % CORES
        named = [(z, y, c), (z, y, 1 - c)]
        here = z
        for slot in range(slots):
            after = before[here]
            for flip in (0, 1):
                named.append((here, 1 - y, c ^ flip))
                if slot + 1 < slots:
                    named.append((after, y, c ^ flip))
            here = after
        rows_of.append([((a * 2 + b) * CORES + d) * exp_here for a, b, d in named])
    places = len(rows_of[0])
    bases = lax.dynamic_index_in_dim(
        jnp.asarray(np.array(rows_of, np.int32)), index, axis=0, keepdims=False
    )

    flat_routes = routes.reshape(1, pairs)
    unit_shape = jax.ShapeDtypeStruct((cols, quarter), jnp.bfloat16)
    order_shape = jax.ShapeDtypeStruct((pairs, pairs), jnp.bfloat16)

    def rows_shape(count):
        return jax.ShapeDtypeStruct((count, quarter), jnp.bfloat16)

    stage = pltpu.VMEM((tokens, tops, quarter), jnp.bfloat16)
    edges = -(-(experts + 1) // LANES) * LANES
    mine_unit, core_unit, own_starts, head, order, *first_pieces = pl.pallas_call(
        sort_kernel,
        out_shape=[
            unit_shape,
            unit_shape,
            jax.ShapeDtypeStruct((1, edges), jnp.int32),
            rows_shape(ALIGN),
            order_shape,
            rows_shape(rows + ALIGN),
            rows_shape(rows),
        ],
        in_specs=[SMEM, VMEM, HBM, HBM],
        out_specs=[HBM, HBM, VMEM, VMEM, VMEM, VMEM, VMEM],
        scratch_shapes=[stage, pltpu.SemaphoreType.DMA((3,))],
        compiler_params=pltpu.CompilerParams(vmem_limit_bytes=60 * MIB),
        cost_estimate=QUICK,
    )(who, flat_routes, out_proj.reshape(cols, width), out_grads)

    def permuted(plan, headed, *after):
        count = len({device for device, _, _ in plan})
        held, *_ = tie(who, *after)
        return pl.pallas_call(
            functools.partial(permute_kernel, plan),
            out_shape=[
                rows_shape(many + (ALIGN if n in headed else 0))
                for n, (_, _, many) in enumerate(plan)
            ],
            in_specs=[SMEM, VMEM, VMEM, HBM],
            out_specs=[VMEM] * len(plan),
            scratch_shapes=[
                pltpu.VMEM((count, tokens, tops, quarter), jnp.bfloat16),
                pltpu.SemaphoreType.DMA((count,)),
            ],
            compiler_params=pltpu.CompilerParams(vmem_limit_bytes=56 * MIB),
            cost_estimate=QUICK,
        )(held, order, head, out_grads)

    def starts_in(block, count):
        digits = block[count : count + 2, :edges].astype(jnp.int32)
        return (digits[0] * DIGIT + digits[1]).reshape(1, edges)

    other_unit = swap(core_unit, 0, 1)
    pieces = [
        *first_pieces,
        *permuted([(2, n * rows, rows) for n in range(2, PIECES)], [], other_unit),
    ]

    def send_piece(number):
        return swap(pieces[number], 1, number // PIECES)

    flying = [
        [send_piece(0), swap(mine_unit, 0, CORES), onward(mine_unit)],
        [send_piece(1), swap(core_unit, 0, CORES + 1), onward(core_unit, 1)],
    ]
    own_tokens, for_core = permuted([(0, 0, pairs), (1, 0, pairs)], [1], *pieces[2:])
    pieces += permuted([(3, n * rows, rows) for n in range(PIECES)], [0], own_tokens)
    from_core = swap(for_core, 0, 1)
    local_segments, *_ = tie(segments, *pieces[PIECES:])
    basis, order_back = pl.pallas_call(
        basis_kernel,
        out_shape=[
            jax.ShapeDtypeStruct((2 * tokens, SEG_DEV * 2 * rank), jnp.bfloat16),
            order_shape,
        ],
        in_specs=[VMEM] * 5,
        out_specs=[VMEM] * 2,
        compiler_params=pltpu.CompilerParams(vmem_limit_bytes=16 * MIB),
        cost_estimate=QUICK,
    )(
        hidden_in,
        in_proj,
        (local_segments - index * SEG_DEV).reshape(tokens, 1),
        flat_routes,
        routes.T,
    )

    call = functools.partial(
        accumulate, bases=bases, rank=rank, pairs=pairs, window=window, places=places
    )
    steps = 2 * slots
    core_step = min(4, steps - 1)
    units = [(mine_unit, 0), (other_unit, 1)]
    known_units = 0
    members = [0]
    starts = {0: own_starts}
    state, sent = None, []
    held = [own_tokens, basis, order_back]
    for event in [[0, 1], *[[n] for n in range(2, steps)]]:
        arrived, waiting = [], []
        for step in event:
            chain = step % 2
            piece, across, ahead = flying[chain]
            upcoming = [None, None, None]
            if ahead is not None:
                number = step + 2
                if number < 2 * PIECES:
                    pieces[number], piece, across, ahead, *held = tie(
                        pieces[number], piece, across, ahead, *held
                    )
                    upcoming[0] = send_piece(number)
                else:
                    across, ahead, *held = tie(across, ahead, *held)
                upcoming[1] = swap(ahead, 0, CORES)
                if step + 4 < steps:
                    upcoming[2] = onward(ahead)
            flying[chain] = upcoming
            units.append((across, known_units + len(units)))
            if ahead is not None:
                units.append((ahead, known_units + len(units)))
            if piece is not None:
                waiting.append((piece, step))
        if state is None:
            own_tokens, basis, order_back = held
            arrived.append((own_tokens, 0, pairs))
        else:
            state = held
        tasks = [("units", list(members), known_units, len(units))]
        known_units += len(units)
        if event[0] == core_step:
            starts[1] = starts_in(from_core, pairs)
            arrived.append((from_core, pairs, pairs))
            tasks.append(("units", [1], 0, known_units))
            members.append(1)
        for piece, number in waiting:
            g, part = 2 + number // PIECES, number % PIECES
            arrived.append((piece, g * pairs + part * rows, rows))
            if part == 0:
                starts[g] = starts_in(piece, rows)
                members.append(g)
            tasks.append(("piece", g, part * rows, (part + 1) * rows, 0, known_units))
        last = event[-1] + 1 == steps
        state, out = call(
            state,
            starts=starts,
            tokens=arrived,
            units=units,
            tasks=tasks,
            sends=[1, 2, 3] if last else [],
        )
        sent += out
        held = state
        units = []

    from_core = swap(sent[0], 0, 1)
    from_side = swap(sent[1], 1, 0)
    from_diagonal = swap(sent[2], 1, 1)
    return pl.pallas_call(
        functools.partial(blocks_kernel, tops, rank),
        out_shape=jax.ShapeDtypeStruct((SEG_DEV, experts, rank * rank), jnp.bfloat16),
        in_specs=[VMEM] * 7,
        out_specs=VMEM,
        scratch_shapes=[
            pltpu.VMEM((rank, pairs), jnp.float32),
            pltpu.VMEM((rank, experts, tokens), jnp.float32),
        ],
        compiler_params=pltpu.CompilerParams(vmem_limit_bytes=32 * MIB),
        cost_estimate=QUICK,
    )(routes.T, basis, order_back, state[2], from_core, from_side, from_diagonal)


def solution(mesh):
    placed = (
        P(("groups", "expert"), None),
        P(("groups", "expert"), None, None),
        P(("groups", "expert"), None),
        P(("groups", "expert")),
        P(),
        P("expert", None, None),
    )
    return jax.shard_map(
        local,
        mesh=mesh,
        in_specs=placed,
        out_specs=P(("groups", "expert"), None, None),
        check_vma=False,
    )
```

time: 102 us -> 121 us (1.19)
  waiting for transfers between devices: 12.7 us -> 26 us
  Pallas kernels: 47.7 us -> 60.4 us
  starting transfers between devices: 29.2 us -> 23.1 us
  local copies, waits for them, and re-layouts: 11 us -> 9.18 us
    pallas_call x17 -> x12, Pallas kernels: 44.7 us -> 57 us  [the longest x7 20 us: accumulate(): pl.pallas_call(functools.partial(partial_kernel, rank, pairs, window, [(f...]
    ppermute x6, waiting for transfers between devices: 1.87 us -> 13.7 us  [onward(): return lax.ppermute(array, 'expert', table)]
    ppermute x6, starting transfers between devices: 8.11 us -> 4.16 us  [onward(): return lax.ppermute(array, 'expert', table)]
    unnamed x27 -> x35, local copies, waits for them, and re-layouts: 10.1 us -> 7.69 us
    ppermute x20 -> x21, starting transfers between devices: 21.1 us -> 18.9 us  [swap(): return lax.ppermute(array, BOTH, table)]
    ppermute x20 -> x21, waiting for transfers between devices: 10.8 us -> 12.3 us  [swap(): return lax.ppermute(array, BOTH, table)]
  transfers between devices with their start and end apart: 26 -> 27, of which waited for: 5 -> 8; matrix products, arithmetic and copies ran while one was open for 1% -> 1% of each run, Pallas kernels for 37% -> 29%
where the time goes in v5:
time: 121 us; the launch traced here: 120 us
  Pallas kernels  60.4 us (50%)
  waiting for transfers between devices  26 us (21%)
  starting transfers between devices  23.1 us (19%)
  local copies, waits for them, and re-layouts  9.18 us (8%)
    pallas_call x7, Pallas kernels, accumulate(): pl.pallas_call(functools.partial(partial_kernel, rank, pairs, window, [(f...  20 us
    pallas_call x1, Pallas kernels, local(): pl.pallas_call(sort_kernel, out_shape=[unit_shape, unit_shape, jax.ShapeD...  19.8 us
    ppermute x21, starting transfers between devices, swap(): return lax.ppermute(array, BOTH, table)  18.9 us
    pallas_call x3, Pallas kernels, permuted(): pl.pallas_call(functools.partial(permute_kernel, plan), out_shape=[rows_s...  15.5 us
    ppermute x6, waiting for transfers between devices, onward(): return lax.ppermute(array, 'expert', table)  13.7 us
    ppermute x21, waiting for transfers between devices, swap(): return lax.ppermute(array, BOTH, table)  12.3 us
    unnamed x35, local copies, waits for them, and re-layouts  7.69 us
    ppermute x6, starting transfers between devices, onward(): return lax.ppermute(array, 'expert', table)  4.16 us
  transfers between devices with their start and end apart: 27, of which 8 were waited for; matrix products, arithmetic and copies ran while one was open for 1% of the time, Pallas kernels for 29%

profile of v5, /device:TPU:1, one launch (start us, length us, event | category | flops | bytes accessed | tf_op | source)
XLA Modules:
  0.0 119.6 jit_solution(10595465537031155470)
XLA Ops:
  0.0 0.8 copy.28
  0.8 0.7 reshape.12.routes_ref
  1.5 0.6 pad_add_fusion.who_ref
  2.1 19.8 %shard_map.73 = (bf16[256,512]{1,0:T(8,128)(2,1)}, bf16[256,512]{1,0:T(8,128)(2,1)}, s32[1,128]{1,0:T(1,128)}, bf16[16,512]{1,0:T(8,128)(2,1)}, bf16[1024,1024]{...) custom-call(s32[4]{0:T(128)} %pad_add_fusion.who_ref, s32[1,1024]{1,0:T(1,128)} %reshape.12.routes_ref, ...), custom_call_target="tpu_custom_call" | custom-call | flops 1 | bytes 1 | tf_op jit(solution)/shard_map/pallas_call | solution.py:374
  22.1 2.7 %collective-permute-start.4 = (bf16[272,512]{1,0:T(8,128)(2,1)}, bf16[272,512]{1,0:T(8,128)(2,1)S(1)}, u32[]{:S(2)}, u32[]{:S(2)}) collective-permute-start(bf16[272,512]{1,0:T(8,128)(2,1)} %get-tuple-element.97), channel_id=1, source_target_pairs={{0,16},{1,17},{2,18},{3,19},{4,20},{5,21},{6,22},{7,23},{8,24},{9,... | collective-permute-start | bytes 835592 | tf_op jit(solution)/shard_map/ppermute | solution.py:337
  24.7 1.2 %collective-permute-start.5 = (bf16[256,512]{1,0:T(8,128)(2,1)}, bf16[256,512]{1,0:T(8,128)(2,1)S(1)}, u32[]{:S(2)}, u32[]{:S(2)}) collective-permute-start(bf16[256,512]{1,0:T(8,128)(2,1)} %get-tuple-element.98.refs_5_), channel_id=1, source_target_pairs={{0,2},{1,3},{2,0},{3,1},{4,6},{5,7},{6,4},{7,5},{8,10},{9,11},{10,... | collective-permute-start | bytes 786440 | tf_op jit(solution)/shard_map/ppermute | solution.py:337
  26.0 1.3 %collective-permute-start.6 = (bf16[256,512]{1,0:T(8,128)(2,1)}, bf16[256,512]{1,0:T(8,128)(2,1)}, u32[]{:S(2)}, u32[]{:S(2)}) collective-permute-start(bf16[256,512]{1,0:T(8,128)(2,1)} %get-tuple-element.98.refs_5_), channel_id=1, source_target_pairs={{0,4},{1,5},{2,6},{3,7},{4,12},{5,13},{6,14},{7,15},{8,0},{9,1},{1... | collective-permute-start | bytes 786440 | tf_op jit(solution)/shard_map/ppermute | solution.py:342
  27.3 1.0 collective-permute-start.2
  28.5 4.3 %shard_map.74 = (bf16[256,512]{1,0:T(8,128)(2,1)}, bf16[256,512]{1,0:T(8,128)(2,1)}) custom-call(s32[4]{0:T(128)} %pad_add_fusion.who_ref, bf16[1024,1024]{1,0:T(8,128)(2,1)} %get-tuple-element.92.order_ref, bf16[16,512]{1,0:T(8,128)(2,1)} %get-tuple-element.93.head_ref, bf16[128,8,2048]{2,1,0:T(8,128)(2,1)} %grads_ref.7), custom_call_target="tpu_custom_call" | custom-call | flops 1 | bytes 1 | tf_op jit(solution)/shard_map/pallas_call | solution.py:395
  32.8 6.3 %shard_map.75 = (bf16[1024,512]{1,0:T(8,128)(2,1)}, bf16[1040,512]{1,0:T(8,128)(2,1)}) custom-call(s32[4]{0:T(128)} %pad_add_fusion.who_ref, bf16[1024,1024]{1,0:T(8,128)(2,1)} %get-tuple-element.92.order_ref, bf16[16,512]{1,0:T(8,128)(2,1)} %get-tuple-element.93.head_ref, bf16[128,8,2048]{2,1,0:T(8,128)(2,1)} %grads_ref.7), custom_call_target="tpu_custom_call" | custom-call | flops 1 | bytes 1 | tf_op jit(solution)/shard_map/pallas_call | solution.py:395
  39.2 4.9 %shard_map.76 = (bf16[272,512]{1,0:T(8,128)(2,1)}, bf16[256,512]{1,0:T(8,128)(2,1)}, bf16[256,512]{1,0:T(8,128)(2,1)}, bf16[256,512]{1,0:T(8,128)(2,1)}) custom-call(s32[4]{0:T(128)} %pad_add_fusion.who_ref, bf16[1024,1024]{1,0:T(8,128)(2,1)} %get-tuple-element.92.order_ref, bf16[16,512]{1,0:T(8,128)(2,1)} %get-tuple-element.93.head_ref, ...), custom_call_target="tpu_custom_call" | custom-call | flops 1 | bytes 1 | tf_op jit(solution)/shard_map/pallas_call | solution.py:395
  44.3 0.7 copy-done.6
  45.0 2.4 %collective-permute-start.3 = (bf16[256,512]{1,0:T(8,128)(2,1)}, bf16[256,512]{1,0:T(8,128)(2,1)}, u32[]{:S(2)}, u32[]{:S(2)}) collective-permute-start(bf16[256,512]{1,0:T(8,128)(2,1)} %get-tuple-element.90), channel_id=1, source_target_pairs={{0,5},{1,4},{2,7},{3,6},{4,13},{5,12},{6,15},{7,14},{8,1},{9,0},{1... | collective-permute-start | bytes 786440 | tf_op jit(solution)/shard_map/ppermute | solution.py:342
  47.4 1.5 %copy-done = bf16[128,7168]{1,0:T(8,128)(2,1)S(1)} copy-done((bf16[128,7168]{1,0:T(8,128)(2,1)S(1)}, bf16[128,7168]{1,0:T(8,128)(2,1)}, u32[]{:S(2)}) %copy-start) | copy-done | bytes 1835032
  48.9 1.2 copy-done.2
  50.1 1.7 %shard_map.77 = (bf16[256,256]{1,0:T(8,128)(2,1)S(1)}, bf16[1024,1024]{1,0:T(8,128)(2,1)S(1)}) custom-call(bf16[128,7168]{1,0:T(8,128)(2,1)S(1)} %copy-done, bf16[64,7168]{1,0:T(8,128)(2,1)S(1)} %copy-done.2, s32[128,1]{1,0:T(8,128)S(1)} %copy.29.segment_ref, s32[1,1024]{1,0:T(1,128)S(1)} %copy-done.11, s32[8,128]{1,0:T(8,128)S(1)} %bitcast.10), custom_call_target="tpu_custom_call" | custom-call | flops 1 | bytes 1 | tf_op jit(solution)/shard_map/pallas_call | solution.py:432
  51.8 0.6 copy-done.8
  52.6 0.7 dynamic-slice_bitcast_fusion.bases_ref
  53.3 0.5 collective-permute-start.7
  53.8 1.2 %collective-permute-start.9 = (bf16[256,512]{1,0:T(8,128)(2,1)}, bf16[256,512]{1,0:T(8,128)(2,1)S(1)}, u32[]{:S(2)}, u32[]{:S(2)}) collective-permute-start(bf16[256,512]{1,0:T(8,128)(2,1)} %collective-permute-done.6.refs_8_), channel_id=1, source_target_pairs={{0,2},{1,3},{2,0},{3,1},{4,6},{5,7},{6,4},{7,5},{8,10},{9,11},{10,... | collective-permute-start | bytes 786440 | tf_op jit(solution)/shard_map/ppermute | solution.py:337
  55.1 1.2 %collective-permute-start.8 = (bf16[256,512]{1,0:T(8,128)(2,1)}, bf16[256,512]{1,0:T(8,128)(2,1)S(1)}, u32[]{:S(2)}, u32[]{:S(2)}) collective-permute-start(bf16[256,512]{1,0:T(8,128)(2,1)} %get-tuple-element.117), channel_id=1, source_target_pairs={{0,16},{1,17},{2,18},{3,19},{4,20},{5,21},{6,22},{7,23},{8,24},{9,... | collective-permute-start | bytes 786440 | tf_op jit(solution)/shard_map/ppermute | solution.py:337
  56.6 4.7 %collective-permute-done.10.refs_4_ = bf16[256,512]{1,0:T(8,128)(2,1)} collective-permute-done((bf16[256,512]{1,0:T(8,128)(2,1)}, bf16[256,512]{1,0:T(8,128)(2,1)}, u32[]{:S(2)}, u32[]{:S(2)}) %collective-permute-start.10) | collective-permute-done | bytes 262176 | tf_op jit(solution)/shard_map/ppermute | solution.py:342
  61.2 0.5 collective-permute-start.15
  61.8 0.9 copy-done.3
  62.7 0.9 copy-done.5
  63.7 0.9 copy-done.7
  64.6 4.1 %shard_map.78 = (bf16[4096,512]{1,0:T(8,128)(2,1)S(1)}, bf16[16,256,512]{2,1,0:T(8,128)(2,1)S(1)}, f32[4096,128]{1,0:T(8,128)S(1)}) custom-call(s32[16]{0:T(128)S(1)} %dynamic-slice_bitcast_fusion.bases_ref, s32[1,128]{1,0:T(1,128)S(1)} %copy-done.12, s32[1,128]{1,0:T(1,128)S(1)} %slice_add_fusion.2.refs_1_, bf16[1024,512]{1,0:T(8,128)(2,1)S(1)} %copy-done.1, ...), custom_call_target="tpu_custom_call" | custom-call | flops 1 | bytes 1 | tf_op jit(solution)/shard_map/pallas_call | solution.py:251
  68.8 3.2 %collective-permute-start.11 = (bf16[272,512]{1,0:T(8,128)(2,1)}, bf16[272,512]{1,0:T(8,128)(2,1)S(1)}, u32[]{:S(2)}, u32[]{:S(2)}) collective-permute-start(bf16[272,512]{1,0:T(8,128)(2,1)} %get-tuple-element.127), channel_id=1, source_target_pairs={{0,17},{1,16},{2,19},{3,18},{4,21},{5,20},{6,23},{7,22},{8,25},{9,... | collective-permute-start | bytes 835592 | tf_op jit(solution)/shard_map/ppermute | solution.py:337
  72.0 0.5 collective-permute-start.12
  72.5 2.4 %shard_map.79 = (bf16[4096,512]{1,0:T(8,128)(2,1)S(1)}, bf16[16,256,512]{2,1,0:T(8,128)(2,1)S(1)}, f32[4096,128]{1,0:T(8,128)S(1)}) custom-call(s32[16]{0:T(128)S(1)} %dynamic-slice_bitcast_fusion.bases_ref, s32[1,128]{1,0:T(1,128)S(1)} %copy-done.12, ...), custom_call_target="tpu_custom_call", output_to_operand_aliasing={{0}: (6, {}), {1}: (7, {}), {2}: (8, {})} | custom-call | flops 1 | bytes 1 | tf_op jit(solution)/shard_map/pallas_call | solution.py:251
  74.8 6.5 %collective-permute-done.16.refs_4_ = bf16[256,512]{1,0:T(8,128)(2,1)S(1)} collective-permute-done((bf16[256,512]{1,0:T(8,128)(2,1)}, bf16[256,512]{1,0:T(8,128)(2,1)S(1)}, u32[]{:S(2)}, u32[]{:S(2)}) %collective-permute-start.16) | collective-permute-done | bytes 262176 | tf_op jit(solution)/shard_map/ppermute | solution.py:342
  81.5 1.7 %shard_map.80 = (bf16[4096,512]{1,0:T(8,128)(2,1)S(1)}, bf16[16,256,512]{2,1,0:T(8,128)(2,1)S(1)}, f32[4096,128]{1,0:T(8,128)S(1)}) custom-call(s32[16]{0:T(128)S(1)} %dynamic-slice_bitcast_fusion.bases_ref, s32[1,128]{1,0:T(1,128)S(1)} %copy-done.12, ...), custom_call_target="tpu_custom_call", output_to_operand_aliasing={{0}: (6, {}), {1}: (7, {}), {2}: (8, {})} | custom-call | flops 1 | bytes 1 | tf_op jit(solution)/shard_map/pallas_call | solution.py:251
  83.4 2.5 %collective-permute-done.13.refs_7_ = bf16[256,512]{1,0:T(8,128)(2,1)S(1)} collective-permute-done((bf16[256,512]{1,0:T(8,128)(2,1)}, bf16[256,512]{1,0:T(8,128)(2,1)S(1)}, u32[]{:S(2)}, u32[]{:S(2)}) %collective-permute-start.13) | collective-permute-done | bytes 262176 | tf_op jit(solution)/shard_map/ppermute | solution.py:342
  85.9 1.4 %collective-permute-start.17 = (bf16[256,512]{1,0:T(8,128)(2,1)S(1)}, bf16[256,512]{1,0:T(8,128)(2,1)S(1)}, u32[]{:S(2)}, u32[]{:S(2)}) collective-permute-start(bf16[256,512]{1,0:T(8,128)(2,1)S(1)} %copy-done.15), channel_id=1, source_target_pairs={{0,17},{1,16},{2,19},{3,18},{4,21},{5,20},{6,23},{7,22},{8,25},{9,... | collective-permute-start | bytes 786440 | tf_op jit(solution)/shard_map/ppermute | solution.py:337
  87.7 0.6 collective-permute-start.23
  88.3 4.9 %shard_map.81 = (bf16[4096,512]{1,0:T(8,128)(2,1)S(1)}, bf16[16,256,512]{2,1,0:T(8,128)(2,1)S(1)}, f32[4096,128]{1,0:T(8,128)S(1)}) custom-call(s32[16]{0:T(128)S(1)} %dynamic-slice_bitcast_fusion.bases_ref, s32[1,128]{1,0:T(1,128)S(1)} %copy-done.12, ...), custom_call_target="tpu_custom_call", output_to_operand_aliasing={{0}: (9, {}), {1}: (10, {}), {2}: (11, {})} | custom-call | flops 1 | bytes 1 | tf_op jit(solution)/shard_map/pallas_call | solution.py:251
  93.2 1.6 %collective-permute-done.17.refs_4_ = bf16[256,512]{1,0:T(8,128)(2,1)S(1)} collective-permute-done((bf16[256,512]{1,0:T(8,128)(2,1)S(1)}, bf16[256,512]{1,0:T(8,128)(2,1)S(1)}, u32[]{:S(2)}, u32[]{:S(2)}) %collective-permute-start.17) | collective-permute-done | bytes 262176 | tf_op jit(solution)/shard_map/ppermute | solution.py:337
  94.8 1.2 %collective-permute-start.20 = (bf16[256,512]{1,0:T(8,128)(2,1)S(1)}, bf16[256,512]{1,0:T(8,128)(2,1)S(1)}, u32[]{:S(2)}, u32[]{:S(2)}) collective-permute-start(bf16[256,512]{1,0:T(8,128)(2,1)S(1)} %copy-done.13), channel_id=1, source_target_pairs={{0,17},{1,16},{2,19},{3,18},{4,21},{5,20},{6,23},{7,22},{8,25},{9,... | collective-permute-start | bytes 786440 | tf_op jit(solution)/shard_map/ppermute | solution.py:337
  96.0 0.4 collective-permute-start.21
  96.4 2.1 %shard_map.82 = (bf16[4096,512]{1,0:T(8,128)(2,1)S(1)}, bf16[16,256,512]{2,1,0:T(8,128)(2,1)S(1)}, f32[4096,128]{1,0:T(8,128)S(1)}) custom-call(s32[16]{0:T(128)S(1)} %dynamic-slice_bitcast_fusion.bases_ref, s32[1,128]{1,0:T(1,128)S(1)} %copy-done.12, ...), custom_call_target="tpu_custom_call", output_to_operand_aliasing={{0}: (8, {}), {1}: (9, {}), {2}: (10, {})} | custom-call | flops 1 | bytes 1 | tf_op jit(solution)/shard_map/pallas_call | solution.py:251
  98.5 1.9 %collective-permute-done.22.refs_4_ = bf16[256,512]{1,0:T(8,128)(2,1)S(1)} collective-permute-done((bf16[256,512]{1,0:T(8,128)(2,1)S(1)}, bf16[256,512]{1,0:T(8,128)(2,1)S(1)}, u32[]{:S(2)}, u32[]{:S(2)}) %collective-permute-start.22) | collective-permute-done | bytes 262176 | tf_op jit(solution)/shard_map/ppermute | solution.py:337
  100.4 2.2 %shard_map.83 = (bf16[4096,512]{1,0:T(8,128)(2,1)S(1)}, bf16[16,256,512]{2,1,0:T(8,128)(2,1)S(1)}, f32[4096,128]{1,0:T(8,128)S(1)}) custom-call(s32[16]{0:T(128)S(1)} %dynamic-slice_bitcast_fusion.bases_ref, s32[1,128]{1,0:T(1,128)S(1)} %copy-done.12, ...), custom_call_target="tpu_custom_call", output_to_operand_aliasing={{0}: (7, {}), {1}: (8, {}), {2}: (9, {})} | custom-call | flops 1 | bytes 1 | tf_op jit(solution)/shard_map/pallas_call | solution.py:251
  102.6 2.4 %collective-permute-done.20.refs_4_ = bf16[256,512]{1,0:T(8,128)(2,1)S(1)} collective-permute-done((bf16[256,512]{1,0:T(8,128)(2,1)S(1)}, bf16[256,512]{1,0:T(8,128)(2,1)S(1)}, u32[]{:S(2)}, u32[]{:S(2)}) %collective-permute-start.20) | collective-permute-done | bytes 262176 | tf_op jit(solution)/shard_map/ppermute | solution.py:337
  105.0 2.5 %shard_map.84 = (bf16[4096,512]{1,0:T(8,128)(2,1)S(1)}, bf16[16,256,512]{2,1,0:T(8,128)(2,1)S(1)}, f32[4096,128]{1,0:T(8,128)S(1)}, bf16[512,128]{1,0:T(8,128)(2...) custom-call(s32[16]{0:T(128)S(1)} %dynamic-slice_bitcast_fusion.base, ...), custom_call_target="tpu_custom_call", output_to_operand_aliasing={{0}: (7, {}), {1}: (8, {}), {2}: (9, {})} | custom-call | flops 1 | bytes 1 | tf_op jit(solution)/shard_map/pallas_call | solution.py:251
  107.6 2.0 %collective-permute-start.25 = (bf16[512,128]{1,0:T(8,128)(2,1)S(1)}, bf16[512,128]{1,0:T(8,128)(2,1)S(1)}, u32[]{:S(2)}, u32[]{:S(2)}) collective-permute-start(bf16[512,128]{1,0:T(8,128)(2,1)S(1)} %get-tuple-element.173), channel_id=1, source_target_pairs={{0,16},{1,17},{2,18},{3,19},{4,20},{5,21},{6,22},{7,23},{8,24},{9,... | collective-permute-start | bytes 393224 | tf_op jit(solution)/shard_map/ppermute | solution.py:337
  109.8 3.6 %collective-permute-done.25.c_ref = bf16[512,128]{1,0:T(8,128)(2,1)S(1)} collective-permute-done((bf16[512,128]{1,0:T(8,128)(2,1)S(1)}, bf16[512,128]{1,0:T(8,128)(2,1)S(1)}, u32[]{:S(2)}, u32[]{:S(2)}) %collective-permute-start.25) | collective-permute-done | bytes 131104 | tf_op jit(solution)/shard_map/ppermute | solution.py:337
  113.3 2.9 %collective-permute-done.26.d_ref = bf16[512,128]{1,0:T(8,128)(2,1)S(1)} collective-permute-done((bf16[512,128]{1,0:T(8,128)(2,1)S(1)}, bf16[512,128]{1,0:T(8,128)(2,1)S(1)}, u32[]{:S(2)}, u32[]{:S(2)}) %collective-permute-start.26) | collective-permute-done | bytes 131104 | tf_op jit(solution)/shard_map/ppermute | solution.py:337
  116.2 3.4 %shard_map.85 = bf16[2,64,4096]{2,1,0:T(8,128)(2,1)} custom-call(s32[8,128]{1,0:T(8,128)S(1)} %bitcast.11, bf16[256,256]{1,0:T(8,128)(2,1)S(1)} %copy-done.9, bf16[1024,1024]{1,0:T(8,128)(2,1)S(1)} %get-tuple-element.113.order_ref, f32[4096,128]{1,0:T(8,128)S(1)} %get-tuple-element.171.total_ref, bf16[512,128]{1,0:T(8,128)(2,1)S(1)} %collective-permute-done.24.b_ref, ...), custom_call_target="tpu_custom_call" | custom-call | flops 1 | bytes 1 | tf_op jit(solution)/shard_map/pallas_call | solution.py:520
  (65 shorter events, 2.0 us)
Async XLA Ops:
  21.9 6.4 %collective-permute-start = (bf16[256,512]{1,0:T(8,128)(2,1)}, bf16[256,512]{1,0:T(8,128)(2,1)S(1)}, u32[]{:S(2)}, u32[]{:S(2)}) collective-permute-start(bf16[256,512]{1,0:T(8,128)(2,1)} %get-tuple-element.90), channel_id=1, source_target_pairs={{0,1},{1,0},{2,3},{3,2},{4,5},{5,4},{6,7},{7,6},{8,9},{9,8},{10,11... | collective-permute-start | bytes 786440 | tf_op jit(solution)/shard_map/ppermute | solution.py:337
  22.1 30.3 %collective-permute-start.4 = (bf16[272,512]{1,0:T(8,128)(2,1)}, bf16[272,512]{1,0:T(8,128)(2,1)S(1)}, u32[]{:S(2)}, u32[]{:S(2)}) collective-permute-start(bf16[272,512]{1,0:T(8,128)(2,1)} %get-tuple-element.97), channel_id=1, source_target_pairs={{0,16},{1,17},{2,18},{3,19},{4,20},{5,21},{6,22},{7,23},{8,24},{9,... | collective-permute-start | bytes 835592 | tf_op jit(solution)/shard_map/ppermute | solution.py:337
  24.7 19.5 %collective-permute-start.5 = (bf16[256,512]{1,0:T(8,128)(2,1)}, bf16[256,512]{1,0:T(8,128)(2,1)S(1)}, u32[]{:S(2)}, u32[]{:S(2)}) collective-permute-start(bf16[256,512]{1,0:T(8,128)(2,1)} %get-tuple-element.98.refs_5_), channel_id=1, source_target_pairs={{0,2},{1,3},{2,0},{3,1},{4,6},{5,7},{6,4},{7,5},{8,10},{9,11},{10,... | collective-permute-start | bytes 786440 | tf_op jit(solution)/shard_map/ppermute | solution.py:337
  26.0 26.4 %collective-permute-start.6 = (bf16[256,512]{1,0:T(8,128)(2,1)}, bf16[256,512]{1,0:T(8,128)(2,1)}, u32[]{:S(2)}, u32[]{:S(2)}) collective-permute-start(bf16[256,512]{1,0:T(8,128)(2,1)} %get-tuple-element.98.refs_5_), channel_id=1, source_target_pairs={{0,4},{1,5},{2,6},{3,7},{4,12},{5,13},{6,14},{7,15},{8,0},{9,1},{1... | collective-permute-start | bytes 786440 | tf_op jit(solution)/shard_map/ppermute | solution.py:342
  27.3 27.8 %collective-permute-start.2 = (bf16[256,512]{1,0:T(8,128)(2,1)}, bf16[256,512]{1,0:T(8,128)(2,1)}, u32[]{:S(2)}, u32[]{:S(2)}) collective-permute-start(bf16[256,512]{1,0:T(8,128)(2,1)} %get-tuple-element.90), channel_id=1, source_target_pairs={{0,3},{1,2},{2,1},{3,0},{4,7},{5,6},{6,5},{7,4},{8,11},{9,10},{10,... | collective-permute-start | bytes 786440 | tf_op jit(solution)/shard_map/ppermute | solution.py:337
  28.3 10.9 %copy-start.4 = (bf16[256,512]{1,0:T(8,128)(2,1)}, bf16[256,512]{1,0:T(8,128)(2,1)S(1)}, u32[]{:S(2)}) copy-start(bf16[256,512]{1,0:T(8,128)(2,1)S(1)} %collective-permute-done.refs_6_) | copy-start | bytes 786436
  28.3 25.5 %collective-permute-start.1 = (bf16[256,512]{1,0:T(8,128)(2,1)}, bf16[256,512]{1,0:T(8,128)(2,1)}, u32[]{:S(2)}, u32[]{:S(2)}) collective-permute-start(bf16[256,512]{1,0:T(8,128)(2,1)} %get-tuple-element.95), channel_id=1, source_target_pairs={{0,16},{1,17},{2,18},{3,19},{4,20},{5,21},{6,22},{7,23},{8,24},{9,... | collective-permute-start | bytes 786440 | tf_op jit(solution)/shard_map/ppermute | solution.py:337
  39.2 5.0 %copy-start.16 = (s32[128]{0:T(128)S(1)}, s32[128]{0:T(128)}, u32[]{:S(2)}) copy-start(s32[128]{0:T(128)} %param.10) | copy-start | bytes 1540
  39.2 8.2 %copy-start.10 = (s32[128,8]{0,1:T(8,128)S(1)}, s32[128,8]{0,1:T(8,128)}, u32[]{:S(2)}) copy-start(s32[128,8]{0,1:T(8,128)} %param.9) | copy-start | bytes 12292
  39.2 8.2 %copy-start.11 = (s32[1,1024]{1,0:T(1,128)S(1)}, s32[1,1024]{1,0:T(1,128)}, u32[]{:S(2)}) copy-start(s32[1,1024]{1,0:T(1,128)} %reshape.12.routes_ref) | copy-start | bytes 12292
  39.2 22.6 %copy-start.1 = (bf16[1024,512]{1,0:T(8,128)(2,1)S(1)}, bf16[1024,512]{1,0:T(8,128)(2,1)}, u32[]{:S(2)}) copy-start(bf16[1024,512]{1,0:T(8,128)(2,1)} %get-tuple-element.119.refs_2_) | copy-start | bytes 3145732
  39.2 22.5 %copy-start.12 = (s32[1,128]{1,0:T(1,128)S(1)}, s32[1,128]{1,0:T(1,128)}, u32[]{:S(2)}) copy-start(s32[1,128]{1,0:T(1,128)} %get-tuple-element.114.refs_0_) | copy-start | bytes 1540
  44.3 0.7 copy-start.6
  45.0 10.1 %collective-permute-start.3 = (bf16[256,512]{1,0:T(8,128)(2,1)}, bf16[256,512]{1,0:T(8,128)(2,1)}, u32[]{:S(2)}, u32[]{:S(2)}) collective-permute-start(bf16[256,512]{1,0:T(8,128)(2,1)} %get-tuple-element.90), channel_id=1, source_target_pairs={{0,5},{1,4},{2,7},{3,6},{4,13},{5,12},{6,15},{7,14},{8,1},{9,0},{1... | collective-permute-start | bytes 786440 | tf_op jit(solution)/shard_map/ppermute | solution.py:342
  47.4 1.5 %copy-start = (bf16[128,7168]{1,0:T(8,128)(2,1)S(1)}, bf16[128,7168]{1,0:T(8,128)(2,1)}, u32[]{:S(2)}) copy-start(bf16[128,7168]{1,0:T(8,128)(2,1)} %hidden_ref.1) | copy-start | bytes 5505028
  48.9 1.2 copy-start.2
  51.7 0.7 copy-start.8
  52.4 8.8 %collective-permute-start.10 = (bf16[256,512]{1,0:T(8,128)(2,1)}, bf16[256,512]{1,0:T(8,128)(2,1)}, u32[]{:S(2)}, u32[]{:S(2)}) collective-permute-start(bf16[256,512]{1,0:T(8,128)(2,1)} %collective-permute-done.6.refs_8_), channel_id=1, source_target_pairs={{0,4},{1,5},{2,6},{3,7},{4,12},{5,13},{6,14},{7,15},{8,0},{9,1},{1... | collective-permute-start | bytes 786440 | tf_op jit(solution)/shard_map/ppermute | solution.py:342
  53.3 34.4 %collective-permute-start.7 = (bf16[1040,512]{1,0:T(8,128)(2,1)}, bf16[1040,512]{1,0:T(8,128)(2,1)S(1)}, u32[]{:S(2)}, u32[]{:S(2)}) collective-permute-start(bf16[1040,512]{1,0:T(8,128)(2,1)} %get-tuple-element.116), channel_id=1, source_target_pairs={{0,1},{1,0},{2,3},{3,2},{4,5},{5,4},{6,7},{7,6},{8,9},{9,8},{10,11... | collective-permute-start | bytes 3194888 | tf_op jit(solution)/shard_map/ppermute | solution.py:337
  53.8 15.0 %collective-permute-start.9 = (bf16[256,512]{1,0:T(8,128)(2,1)}, bf16[256,512]{1,0:T(8,128)(2,1)S(1)}, u32[]{:S(2)}, u32[]{:S(2)}) collective-permute-start(bf16[256,512]{1,0:T(8,128)(2,1)} %collective-permute-done.6.refs_8_), channel_id=1, source_target_pairs={{0,2},{1,3},{2,0},{3,1},{4,6},{5,7},{6,4},{7,5},{8,10},{9,11},{10,... | collective-permute-start | bytes 786440 | tf_op jit(solution)/shard_map/ppermute | solution.py:337
  55.1 13.7 %collective-permute-start.8 = (bf16[256,512]{1,0:T(8,128)(2,1)}, bf16[256,512]{1,0:T(8,128)(2,1)S(1)}, u32[]{:S(2)}, u32[]{:S(2)}) collective-permute-start(bf16[256,512]{1,0:T(8,128)(2,1)} %get-tuple-element.117), channel_id=1, source_target_pairs={{0,16},{1,17},{2,18},{3,19},{4,20},{5,21},{6,22},{7,23},{8,24},{9,... | collective-permute-start | bytes 786440 | tf_op jit(solution)/shard_map/ppermute | solution.py:337
  56.3 15.7 %collective-permute-start.14 = (bf16[256,512]{1,0:T(8,128)(2,1)}, bf16[256,512]{1,0:T(8,128)(2,1)S(1)}, u32[]{:S(2)}, u32[]{:S(2)}) collective-permute-start(bf16[256,512]{1,0:T(8,128)(2,1)} %get-tuple-element.129), channel_id=1, source_target_pairs={{0,16},{1,17},{2,18},{3,19},{4,20},{5,21},{6,22},{7,23},{8,24},{9,... | collective-permute-start | bytes 786440 | tf_op jit(solution)/shard_map/ppermute | solution.py:337
  61.2 11.2 %collective-permute-start.15 = (bf16[256,512]{1,0:T(8,128)(2,1)}, bf16[256,512]{1,0:T(8,128)(2,1)S(1)}, u32[]{:S(2)}, u32[]{:S(2)}) collective-permute-start(bf16[256,512]{1,0:T(8,128)(2,1)} %collective-permute-done.3.refs_10_), channel_id=1, source_target_pairs={{0,2},{1,3},{2,0},{3,1},{4,6},{5,7},{6,4},{7,5},{8,10},{9,11},{10,... | collective-permute-start | bytes 786440 | tf_op jit(solution)/shard_map/ppermute | solution.py:337
  61.8 1.0 copy-start.3
  62.7 0.9 copy-start.5
  63.7 0.9 copy-start.7
  68.8 18.5 %collective-permute-start.11 = (bf16[272,512]{1,0:T(8,128)(2,1)}, bf16[272,512]{1,0:T(8,128)(2,1)S(1)}, u32[]{:S(2)}, u32[]{:S(2)}) collective-permute-start(bf16[272,512]{1,0:T(8,128)(2,1)} %get-tuple-element.127), channel_id=1, source_target_pairs={{0,17},{1,16},{2,19},{3,18},{4,21},{5,20},{6,23},{7,22},{8,25},{9,... | collective-permute-start | bytes 835592 | tf_op jit(solution)/shard_map/ppermute | solution.py:337
  71.9 9.4 %collective-permute-start.16 = (bf16[256,512]{1,0:T(8,128)(2,1)}, bf16[256,512]{1,0:T(8,128)(2,1)S(1)}, u32[]{:S(2)}, u32[]{:S(2)}) collective-permute-start(bf16[256,512]{1,0:T(8,128)(2,1)} %collective-permute-done.3.refs_10_), channel_id=1, source_target_pairs={{0,4},{1,5},{2,6},{3,7},{4,12},{5,13},{6,14},{7,15},{8,0},{9,1},{1... | collective-permute-start | bytes 786440 | tf_op jit(solution)/shard_map/ppermute | solution.py:342
  72.0 11.2 %collective-permute-start.12 = (bf16[256,512]{1,0:T(8,128)(2,1)}, bf16[256,512]{1,0:T(8,128)(2,1)S(1)}, u32[]{:S(2)}, u32[]{:S(2)}) collective-permute-start(bf16[256,512]{1,0:T(8,128)(2,1)} %collective-permute-done.10.refs_4_), channel_id=1, source_target_pairs={{0,2},{1,3},{2,0},{3,1},{4,6},{5,7},{6,4},{7,5},{8,10},{9,11},{10,... | collective-permute-start | bytes 786440 | tf_op jit(solution)/shard_map/ppermute | solution.py:337
  72.5 13.5 %collective-permute-start.13 = (bf16[256,512]{1,0:T(8,128)(2,1)}, bf16[256,512]{1,0:T(8,128)(2,1)S(1)}, u32[]{:S(2)}, u32[]{:S(2)}) collective-permute-start(bf16[256,512]{1,0:T(8,128)(2,1)} %collective-permute-done.10.refs_4_), channel_id=1, source_target_pairs={{0,4},{1,5},{2,6},{3,7},{4,12},{5,13},{6,14},{7,15},{8,0},{9,1},{1... | collective-permute-start | bytes 786440 | tf_op jit(solution)/shard_map/ppermute | solution.py:342
  81.3 4.6 %copy-start.15 = (bf16[256,512]{1,0:T(8,128)(2,1)S(1)}, bf16[256,512]{1,0:T(8,128)(2,1)}, u32[]{:S(2)}) copy-start(bf16[256,512]{1,0:T(8,128)(2,1)} %get-tuple-element.148) | copy-start | bytes 786436
  81.3 6.0 %copy-start.14 = (bf16[256,512]{1,0:T(8,128)(2,1)S(1)}, bf16[256,512]{1,0:T(8,128)(2,1)}, u32[]{:S(2)}) copy-start(bf16[256,512]{1,0:T(8,128)(2,1)} %get-tuple-element.159) | copy-start | bytes 786436
  81.3 13.4 %collective-permute-start.18 = (bf16[256,512]{1,0:T(8,128)(2,1)S(1)}, bf16[256,512]{1,0:T(8,128)(2,1)S(1)}, u32[]{:S(2)}, u32[]{:S(2)}) collective-permute-start(bf16[256,512]{1,0:T(8,128)(2,1)S(1)} %collective-permute-done.16.refs_4_), channel_id=1, source_target_pairs={{0,2},{1,3},{2,0},{3,1},{4,6},{5,7},{6,4},{7,5},{8,10},{9,11},{10,... | collective-permute-start | bytes 786440 | tf_op jit(solution)/shard_map/ppermute | solution.py:337
  83.2 11.6 %collective-permute-start.19 = (bf16[256,512]{1,0:T(8,128)(2,1)S(1)}, bf16[256,512]{1,0:T(8,128)(2,1)S(1)}, u32[]{:S(2)}, u32[]{:S(2)}) collective-permute-start(bf16[256,512]{1,0:T(8,128)(2,1)S(1)} %collective-permute-done.16.refs_4_), channel_id=1, source_target_pairs={{0,4},{1,5},{2,6},{3,7},{4,12},{5,13},{6,14},{7,15},{8,0},{9,1},{1... | collective-permute-start | bytes 786440 | tf_op jit(solution)/shard_map/ppermute | solution.py:342
  85.9 8.9 %collective-permute-start.17 = (bf16[256,512]{1,0:T(8,128)(2,1)S(1)}, bf16[256,512]{1,0:T(8,128)(2,1)S(1)}, u32[]{:S(2)}, u32[]{:S(2)}) collective-permute-start(bf16[256,512]{1,0:T(8,128)(2,1)S(1)} %copy-done.15), channel_id=1, source_target_pairs={{0,17},{1,16},{2,19},{3,18},{4,21},{5,20},{6,23},{7,22},{8,25},{9,... | collective-permute-start | bytes 786440 | tf_op jit(solution)/shard_map/ppermute | solution.py:337
  87.3 13.1 %collective-permute-start.22 = (bf16[256,512]{1,0:T(8,128)(2,1)S(1)}, bf16[256,512]{1,0:T(8,128)(2,1)S(1)}, u32[]{:S(2)}, u32[]{:S(2)}) collective-permute-start(bf16[256,512]{1,0:T(8,128)(2,1)S(1)} %copy-done.14), channel_id=1, source_target_pairs={{0,17},{1,16},{2,19},{3,18},{4,21},{5,20},{6,23},{7,22},{8,25},{9,... | collective-permute-start | bytes 786440 | tf_op jit(solution)/shard_map/ppermute | solution.py:337
  87.7 12.7 %collective-permute-start.23 = (bf16[256,512]{1,0:T(8,128)(2,1)S(1)}, bf16[256,512]{1,0:T(8,128)(2,1)S(1)}, u32[]{:S(2)}, u32[]{:S(2)}) collective-permute-start(bf16[256,512]{1,0:T(8,128)(2,1)S(1)} %collective-permute-done.13.refs_7_), channel_id=1, source_target_pairs={{0,2},{1,3},{2,0},{3,1},{4,6},{5,7},{6,4},{7,5},{8,10},{9,11},{10,... | collective-permute-start | bytes 786440 | tf_op jit(solution)/shard_map/ppermute | solution.py:337
  88.3 6.5 %copy-start.13 = (bf16[256,512]{1,0:T(8,128)(2,1)S(1)}, bf16[256,512]{1,0:T(8,128)(2,1)}, u32[]{:S(2)}) copy-start(bf16[256,512]{1,0:T(8,128)(2,1)} %get-tuple-element.157) | copy-start | bytes 786436
  94.8 10.2 %collective-permute-start.20 = (bf16[256,512]{1,0:T(8,128)(2,1)S(1)}, bf16[256,512]{1,0:T(8,128)(2,1)S(1)}, u32[]{:S(2)}, u32[]{:S(2)}) collective-permute-start(bf16[256,512]{1,0:T(8,128)(2,1)S(1)} %copy-done.13), channel_id=1, source_target_pairs={{0,17},{1,16},{2,19},{3,18},{4,21},{5,20},{6,23},{7,22},{8,25},{9,... | collective-permute-start | bytes 786440 | tf_op jit(solution)/shard_map/ppermute | solution.py:337
  96.0 9.0 %collective-permute-start.21 = (bf16[256,512]{1,0:T(8,128)(2,1)S(1)}, bf16[256,512]{1,0:T(8,128)(2,1)S(1)}, u32[]{:S(2)}, u32[]{:S(2)}) collective-permute-start(bf16[256,512]{1,0:T(8,128)(2,1)S(1)} %collective-permute-done.19.refs_6_), channel_id=1, source_target_pairs={{0,2},{1,3},{2,0},{3,1},{4,6},{5,7},{6,4},{7,5},{8,10},{9,11},{10,... | collective-permute-start | bytes 786440 | tf_op jit(solution)/shard_map/ppermute | solution.py:337
  105.0 11.2 %copy-start.9 = (bf16[256,256]{1,0:T(8,128)(2,1)S(1)}, bf16[256,256]{1,0:T(8,128)(2,1)}, u32[]{:S(2)}) copy-start(bf16[256,256]{1,0:T(8,128)(2,1)} %copy-done.8) | copy-start | bytes 393220
  107.6 2.2 %collective-permute-start.24 = (bf16[512,128]{1,0:T(8,128)(2,1)S(1)}, bf16[512,128]{1,0:T(8,128)(2,1)S(1)}, u32[]{:S(2)}, u32[]{:S(2)}) collective-permute-start(bf16[512,128]{1,0:T(8,128)(2,1)S(1)} %get-tuple-element.172), channel_id=1, source_target_pairs={{0,1},{1,0},{2,3},{3,2},{4,5},{5,4},{6,7},{7,6},{8,9},{9,8},{10,11... | collective-permute-start | bytes 393224 | tf_op jit(solution)/shard_map/ppermute | solution.py:337
  107.6 5.7 %collective-permute-start.25 = (bf16[512,128]{1,0:T(8,128)(2,1)S(1)}, bf16[512,128]{1,0:T(8,128)(2,1)S(1)}, u32[]{:S(2)}, u32[]{:S(2)}) collective-permute-start(bf16[512,128]{1,0:T(8,128)(2,1)S(1)} %get-tuple-element.173), channel_id=1, source_target_pairs={{0,16},{1,17},{2,18},{3,19},{4,20},{5,21},{6,22},{7,23},{8,24},{9,... | collective-permute-start | bytes 393224 | tf_op jit(solution)/shard_map/ppermute | solution.py:337
  109.6 6.6 %collective-permute-start.26 = (bf16[512,128]{1,0:T(8,128)(2,1)S(1)}, bf16[512,128]{1,0:T(8,128)(2,1)S(1)}, u32[]{:S(2)}, u32[]{:S(2)}) collective-permute-start(bf16[512,128]{1,0:T(8,128)(2,1)S(1)} %get-tuple-element.174), channel_id=1, source_target_pairs={{0,17},{1,16},{2,19},{3,18},{4,21},{5,20},{6,23},{7,22},{8,25},{9,... | collective-permute-start | bytes 393224 | tf_op jit(solution)/shard_map/ppermute | solution.py:337

commit v6 on v5

--- a/solution.py
+++ b/solution.py
@@ -22,11 +22,38 @@
 SMEM = pl.BlockSpec(memory_space=pltpu.SMEM)
 HBM = pl.BlockSpec(memory_space=pl.ANY)
 QUICK = pl.CostEstimate(flops=1, bytes_accessed=1, transcendentals=0)
+SHORT = pl.CostEstimate(flops=6 * 10**8, bytes_accessed=1, transcendentals=0)
 NT = (((1,), (1,)), ((), ()))
 
 
-def columns_of(ref, who, width):
-    return ref.at[..., pl.ds(pl.multiple_of(who * width, width), width)]
+def in_vmem(array):
+    return pltpu.with_memory_space_constraint(array, pltpu.VMEM)
+
+
+def in_hbm(array):
+    return pltpu.with_memory_space_constraint(array, pltpu.HBM)
+
+
+def place_in_quad(flip):
+    side, core = lax.axis_index("groups") % SIDES, lax.axis_index("expert") % CORES
+    return (side ^ (flip // CORES)) * CORES + (core ^ (flip % CORES))
+
+
+def columns_of(flip, width):
+    return pl.ds(pl.multiple_of(place_in_quad(flip) * width, width), width)
+
+
+def row_of(routes):
+    tops, tokens = routes.shape
+    pairs = tops * tokens
+    lane = lax.broadcasted_iota(jnp.int32, (tokens, pairs), 1)
+    token = lax.broadcasted_iota(jnp.int32, (tokens, pairs), 0)
+    spread = jnp.where(lane // tops == token, 1.0, 0.0).astype(jnp.bfloat16)
+    values = routes.astype(jnp.float32).astype(jnp.bfloat16)
+    every = jnp.dot(values, spread, preferred_element_type=jnp.float32)
+    lane = lax.broadcasted_iota(jnp.int32, (tops, pairs), 1)
+    k = lax.broadcasted_iota(jnp.int32, (tops, pairs), 0)
+    return jnp.sum(jnp.where(lane % tops == k, every, 0.0), axis=0, keepdims=True).astype(jnp.int32)
 
 
 def key_column(routes_row):
@@ -44,10 +71,10 @@
 
 
 def sort_kernel(
-    who_ref,
     routes_ref,
     weight_ref,
     grads_ref,
+    held_ref,
     mine_ref,
     core_ref,
     starts_ref,
@@ -59,14 +86,15 @@
     sems,
 ):
     width = mine_ref.shape[1]
-    copies = [
-        pltpu.make_async_copy(columns_of(grads_ref, who_ref[2], width), stage, sems.at[0]),
-        pltpu.make_async_copy(columns_of(weight_ref, who_ref[0], width), mine_ref, sems.at[1]),
-        pltpu.make_async_copy(columns_of(weight_ref, who_ref[1], width), core_ref, sems.at[2]),
-    ]
+    count = sems.shape[0] - 1
+    part = grads_ref.shape[0] // count
+    copies = [pltpu.make_async_copy(weight_ref, stage, sems.at[count])]
+    for n in range(count):
+        here = pl.ds(n * part, part)
+        copies.append(pltpu.make_async_copy(grads_ref.at[here], held_ref.at[here], sems.at[n]))
     for copy in copies:
         copy.start()
-    routes = routes_ref[...]
+    routes = row_of(routes_ref[...])
     pairs = routes.shape[1]
     column = key_column(routes)
     keys = routes * pairs + lax.broadcasted_iota(jnp.int32, (1, pairs), 1)
@@ -84,11 +112,14 @@
     for first in range(0, pairs, rows):
         ids = first + lax.broadcasted_iota(jnp.int32, (rows, pairs), 0)
         order_ref[first : first + rows, :] = jnp.where(place == ids, 1.0, 0.0).astype(jnp.bfloat16)
-    for copy in copies:
+    copies[0].wait()
+    mine_ref[...] = stage[:, columns_of(0, width)]
+    core_ref[...] = stage[:, columns_of(1, width)]
+    for copy in copies[1:]:
         copy.wait()
     sorted_rows = jnp.dot(
         order_ref[0 : 2 * rows, :],
-        stage[...].reshape(pairs, width),
+        held_ref[:, :, columns_of(2, width)].reshape(pairs, width),
         preferred_element_type=jnp.float32,
     ).astype(jnp.bfloat16)
     piece_ref[0:rows, :] = sorted_rows[0:rows]
@@ -96,21 +127,10 @@
     next_ref[...] = sorted_rows[rows:]
 
 
-def permute_kernel(plan, who_ref, order_ref, head_ref, grads_ref, *refs):
-    outs, stage, sems = refs[:-2], refs[-2], refs[-1]
+def permute_kernel(plan, order_ref, head_ref, grads_ref, *outs):
     pairs, width = order_ref.shape[0], outs[0].shape[1]
-    devices = sorted({device for device, _, _ in plan})
-    copies = {
-        device: pltpu.make_async_copy(
-            columns_of(grads_ref, who_ref[device], width), stage.at[i], sems.at[i]
-        )
-        for i, device in enumerate(devices)
-    }
-    for copy in copies.values():
-        copy.start()
-    for i, device in enumerate(devices):
-        copies[device].wait()
-        grads = stage[i].reshape(pairs, width)
+    for device in sorted({device for device, _, _ in plan}):
+        grads = grads_ref[:, :, columns_of(device, width)].reshape(pairs, width)
         for out, (target, first, rows) in zip(outs, plan):
             if target == device:
                 out[0:rows, :] = jnp.dot(
@@ -121,7 +141,7 @@
 
 
 def basis_kernel(
-    hidden_ref, proj_ref, segment_ref, routes_ref, turned_ref, out_ref, order_ref
+    hidden_ref, proj_ref, segment_ref, routes_ref, out_ref, order_ref
 ):
     projected = lax.dot_general(
         hidden_ref[...], proj_ref[...], NT, preferred_element_type=jnp.float32
@@ -131,11 +151,11 @@
     even = jnp.concatenate([b for p in picked for b in (p, zero)], axis=1)
     odd = jnp.concatenate([b for p in picked for b in (zero, p)], axis=1)
     out_ref[...] = jnp.concatenate([even, odd], axis=0).astype(out_ref.dtype)
-    pairs = routes_ref.shape[1]
-    tops, tokens = turned_ref.shape
-    column = key_column(routes_ref[...])
+    tops, tokens = routes_ref.shape
+    pairs = tops * tokens
+    column = key_column(row_of(routes_ref[...]))
     at = [
-        turned_ref[k : k + 1, :] * pairs + lax.broadcasted_iota(jnp.int32, (1, tokens), 1) * tops + k
+        routes_ref[k : k + 1, :] * pairs + lax.broadcasted_iota(jnp.int32, (1, tokens), 1) * tops + k
         for k in range(tops)
     ]
     place = ranks(column, jnp.concatenate(at, axis=1).astype(jnp.float32)).astype(jnp.int32)
@@ -175,8 +195,10 @@
     per_tile = LANES // rank
     low = lax.broadcasted_iota(jnp.int32, (1, LANES), 1) < rank
 
+    device = lax.axis_index("expert")
+
     def process(w, members):
-        base = bases_ref[w]
+        base = bases_ref[device, w]
         heres, offsets = [], []
         for g in members:
             at = jnp.minimum(start_refs[g][0, base] & -ALIGN, pairs - window)
@@ -212,7 +234,7 @@
                 i, carry, member=member, first_row=first_row, end_row=end_row, first_w=first_w
             ):
                 w = first_w + i
-                base = bases_ref[w]
+                base = bases_ref[device, w]
                 touches = (start_refs[member][0, base] < end_row) & (
                     start_refs[member][0, base + held] > first_row
                 )
@@ -237,17 +259,17 @@
     if fresh:
         width = units[0][0].shape[1]
         shapes = [
-            jax.ShapeDtypeStruct((QUAD * pairs, width), jnp.bfloat16),
-            jax.ShapeDtypeStruct((places, *units[0][0].shape), jnp.bfloat16),
-            jax.ShapeDtypeStruct((QUAD * pairs, LANES), jnp.float32),
+            pltpu.VMEM((QUAD * pairs, width), jnp.bfloat16),
+            pltpu.VMEM((places, *units[0][0].shape), jnp.bfloat16),
+            pltpu.VMEM((QUAD * pairs, LANES), jnp.float32),
         ]
         aliases = {}
     else:
         aliases = {len(operands) + i: i for i in range(3)}
-        operands += state
+        operands += [in_vmem(a) for a in state]
         specs += [VMEM] * 3
-        shapes = [jax.ShapeDtypeStruct(a.shape, a.dtype) for a in state]
-    shapes += [jax.ShapeDtypeStruct((pairs // 2, LANES), jnp.bfloat16)] * len(sends)
+        shapes = [pltpu.VMEM(a.shape, a.dtype) for a in state]
+    shapes += [pltpu.VMEM((pairs // 2, LANES), jnp.bfloat16)] * len(sends)
     out = pl.pallas_call(
         functools.partial(
             partial_kernel,
@@ -265,8 +287,8 @@
         in_specs=specs,
         out_specs=[VMEM] * len(shapes),
         input_output_aliases=aliases,
-        compiler_params=pltpu.CompilerParams(vmem_limit_bytes=20 * MIB),
-        cost_estimate=QUICK,
+        compiler_params=pltpu.CompilerParams(vmem_limit_bytes=16 * MIB),
+        cost_estimate=SHORT,
     )(*operands)
     return list(out[:3]), list(out[3:])
 
@@ -319,11 +341,8 @@
     quarter = width // QUAD
     cols = exp_here * rank
     rows = pairs // PIECES
-    group, index = lax.axis_index("groups"), lax.axis_index("expert")
-    core = index % CORES
+    index = lax.axis_index("expert")
     slots = owners // CORES // 2
-    mine = (group % SIDES) * CORES + core
-    who = jnp.stack([mine, mine ^ 1, mine ^ 2, mine ^ 3]).astype(jnp.int32)
     ring = [0, *range(1, slots, 2), *range((slots - 1) // 2 * 2, 0, -2)]
     following = {a: b for a, b in zip(ring, ring[1:] + ring[:1])}
     before = {b: a for a, b in following.items()}
@@ -358,22 +377,20 @@
             here = after
         rows_of.append([((a * 2 + b) * CORES + d) * exp_here for a, b, d in named])
     places = len(rows_of[0])
-    bases = lax.dynamic_index_in_dim(
-        jnp.asarray(np.array(rows_of, np.int32)), index, axis=0, keepdims=False
-    )
-
-    flat_routes = routes.reshape(1, pairs)
-    unit_shape = jax.ShapeDtypeStruct((cols, quarter), jnp.bfloat16)
-    order_shape = jax.ShapeDtypeStruct((pairs, pairs), jnp.bfloat16)
+    bases = jnp.asarray(np.array(rows_of, np.int32))
+
+    unit_shape = pltpu.VMEM((cols, quarter), jnp.bfloat16)
+    order_shape = pltpu.VMEM((pairs, pairs), jnp.bfloat16)
 
     def rows_shape(count):
-        return jax.ShapeDtypeStruct((count, quarter), jnp.bfloat16)
-
-    stage = pltpu.VMEM((tokens, tops, quarter), jnp.bfloat16)
+        return pltpu.VMEM((count, quarter), jnp.bfloat16)
+
+    by_rank = routes.T
     edges = -(-(experts + 1) // LANES) * LANES
-    mine_unit, core_unit, own_starts, head, order, *first_pieces = pl.pallas_call(
+    held_grads, mine_unit, core_unit, own_starts, head, order, *first_pieces = pl.pallas_call(
         sort_kernel,
         out_shape=[
+            pltpu.VMEM(out_grads.shape, jnp.bfloat16),
             unit_shape,
             unit_shape,
             jax.ShapeDtypeStruct((1, edges), jnp.int32),
@@ -382,31 +399,29 @@
             rows_shape(rows + ALIGN),
             rows_shape(rows),
         ],
-        in_specs=[SMEM, VMEM, HBM, HBM],
-        out_specs=[HBM, HBM, VMEM, VMEM, VMEM, VMEM, VMEM],
-        scratch_shapes=[stage, pltpu.SemaphoreType.DMA((3,))],
-        compiler_params=pltpu.CompilerParams(vmem_limit_bytes=60 * MIB),
+        in_specs=[VMEM, HBM, HBM],
+        out_specs=[VMEM] * 8,
+        scratch_shapes=[
+            pltpu.VMEM((cols, width), jnp.bfloat16),
+            pltpu.SemaphoreType.DMA((9,)),
+        ],
+        compiler_params=pltpu.CompilerParams(vmem_limit_bytes=24 * MIB),
         cost_estimate=QUICK,
-    )(who, flat_routes, out_proj.reshape(cols, width), out_grads)
+    )(by_rank, in_hbm(out_proj.reshape(cols, width)), in_hbm(out_grads))
 
     def permuted(plan, headed, *after):
-        count = len({device for device, _, _ in plan})
-        held, *_ = tie(who, *after)
+        held, *_ = tie(order, *after)
         return pl.pallas_call(
             functools.partial(permute_kernel, plan),
             out_shape=[
                 rows_shape(many + (ALIGN if n in headed else 0))
                 for n, (_, _, many) in enumerate(plan)
             ],
-            in_specs=[SMEM, VMEM, VMEM, HBM],
+            in_specs=[VMEM] * 3,
             out_specs=[VMEM] * len(plan),
-            scratch_shapes=[
-                pltpu.VMEM((count, tokens, tops, quarter), jnp.bfloat16),
-                pltpu.SemaphoreType.DMA((count,)),
-            ],
-            compiler_params=pltpu.CompilerParams(vmem_limit_bytes=56 * MIB),
+            compiler_params=pltpu.CompilerParams(vmem_limit_bytes=24 * MIB),
             cost_estimate=QUICK,
-        )(held, order, head, out_grads)
+        )(in_vmem(held), head, in_vmem(held_grads))
 
     def starts_in(block, count):
         digits = block[count : count + 2, :edges].astype(jnp.int32)
@@ -432,10 +447,10 @@
     basis, order_back = pl.pallas_call(
         basis_kernel,
         out_shape=[
-            jax.ShapeDtypeStruct((2 * tokens, SEG_DEV * 2 * rank), jnp.bfloat16),
+            pltpu.VMEM((2 * tokens, SEG_DEV * 2 * rank), jnp.bfloat16),
             order_shape,
         ],
-        in_specs=[VMEM] * 5,
+        in_specs=[VMEM] * 4,
         out_specs=[VMEM] * 2,
         compiler_params=pltpu.CompilerParams(vmem_limit_bytes=16 * MIB),
         cost_estimate=QUICK,
@@ -443,8 +458,7 @@
         hidden_in,
         in_proj,
         (local_segments - index * SEG_DEV).reshape(tokens, 1),
-        flat_routes,
-        routes.T,
+        by_rank,
     )
 
     call = functools.partial(
@@ -528,7 +542,7 @@
         ],
         compiler_params=pltpu.CompilerParams(vmem_limit_bytes=32 * MIB),
         cost_estimate=QUICK,
-    )(routes.T, basis, order_back, state[2], from_core, from_side, from_diagonal)
+    )(by_rank, basis, in_vmem(order_back), in_vmem(state[2]), from_core, from_side, from_diagonal)
 
 
 def solution(mesh):

time: 121 us -> 97.6 us (0.81)
  Pallas kernels: 60.4 us -> 35 us
  local copies, waits for them, and re-layouts: 9.18 us -> 13 us
  waiting for transfers between devices: 26 us -> 22.7 us
  starting transfers between devices: 23.1 us -> 25.8 us
    pallas_call x2, Pallas kernels: 21.5 us -> 6.11 us  [the longest x1 4.12 us: local(): pl.pallas_call(sort_kernel, out_shape=[pltpu.VMEM(out_grads.shape, jnp.bf...]
    ppermute x6, waiting for transfers between devices: 13.7 us -> 1.75 us  [onward(): return lax.ppermute(array, 'expert', table)]
    pallas_call x3, Pallas kernels: 15.5 us -> 4.3 us  [permuted(): pl.pallas_call(functools.partial(permute_kernel, plan), out_shape=[rows_s...]
    ppermute x21, waiting for transfers between devices: 12.3 us -> 21 us  [swap(): return lax.ppermute(array, BOTH, table)]
    unnamed x35 -> x44, local copies, waits for them, and re-layouts: 7.69 us -> 12.8 us
    ppermute x21, starting transfers between devices: 18.9 us -> 20.8 us  [swap(): return lax.ppermute(array, BOTH, table)]
  transfers between devices with their start and end apart: 27 -> 27, of which waited for: 8 -> 10; matrix products, arithmetic and copies ran while one was open for 1% -> 0% of each run, Pallas kernels for 29% -> 25%
where the time goes in v6:
time: 97.6 us; the launch traced here: 96.8 us
  Pallas kernels  35 us (36%)
  starting transfers between devices  25.8 us (26%)
  waiting for transfers between devices  22.7 us (23%)
  local copies, waits for them, and re-layouts  13 us (13%)
    pallas_call x7, Pallas kernels, accumulate(): pl.pallas_call(functools.partial(partial_kernel, rank, pairs, window, [(f...  21.2 us
    ppermute x21, waiting for transfers between devices, swap(): return lax.ppermute(array, BOTH, table)  21 us
    ppermute x21, starting transfers between devices, swap(): return lax.ppermute(array, BOTH, table)  20.8 us
    unnamed x44, local copies, waits for them, and re-layouts  12.8 us
    ppermute x6, starting transfers between devices, onward(): return lax.ppermute(array, 'expert', table)  4.97 us
    pallas_call x3, Pallas kernels, permuted(): pl.pallas_call(functools.partial(permute_kernel, plan), out_shape=[rows_s...  4.3 us
    pallas_call x1, Pallas kernels, local(): pl.pallas_call(sort_kernel, out_shape=[pltpu.VMEM(out_grads.shape, jnp.bf...  4.12 us
    pallas_call x1, Pallas kernels, local(): pl.pallas_call(functools.partial(blocks_kernel, tops, rank), out_shape=ja...  3.43 us
  transfers between devices with their start and end apart: 27, of which 10 were waited for; matrix products, arithmetic and copies ran while one was open for 0% of the time, Pallas kernels for 25%

profile of v6, /device:TPU:1, one launch (start us, length us, event | category | flops | bytes accessed | tf_op | source)
XLA Modules:
  0.0 96.8 jit_solution(13208715146893081142)
XLA Ops:
  0.0 0.7 copy-done.7
  0.7 4.1 %shard_map.73 = (bf16[128,8,2048]{2,1,0:T(8,128)(2,1)S(1)}, bf16[256,512]{1,0:T(8,128)(2,1)}, bf16[256,512]{1,0:T(8,128)(2,1)}, s32[1,128]{1,0:T(1,128)S(1)}, bf...) custom-call(s32[8,128]{1,0:T(8,128)S(1)} %bitcast.4, ...), custom_call_target="tpu_custom_call" | custom-call | flops 1 | bytes 1 | tf_op jit(solution)/shard_map/pallas_call | solution.py:390
  4.8 2.0 %copy-done = bf16[128,8,2048]{2,1,0:T(8,128)(2,1)} copy-done((bf16[128,8,2048]{2,1,0:T(8,128)(2,1)}, bf16[128,8,2048]{2,1,0:T(8,128)(2,1)S(1)}, u32[]{:S(2)}) %copy-start) | copy-done | bytes 4194328
  6.8 0.7 copy-done.19
  7.6 2.7 %collective-permute-start.4 = (bf16[272,512]{1,0:T(8,128)(2,1)}, bf16[272,512]{1,0:T(8,128)(2,1)S(1)}, u32[]{:S(2)}, u32[]{:S(2)}) collective-permute-start(bf16[272,512]{1,0:T(8,128)(2,1)} %get-tuple-element.99), channel_id=1, source_target_pairs={{0,16},{1,17},{2,18},{3,19},{4,20},{5,21},{6,22},{7,23},{8,24},{9,... | collective-permute-start | bytes 835592 | tf_op jit(solution)/shard_map/ppermute | solution.py:356
  10.2 1.2 %collective-permute-start.5 = (bf16[256,512]{1,0:T(8,128)(2,1)}, bf16[256,512]{1,0:T(8,128)(2,1)}, u32[]{:S(2)}, u32[]{:S(2)}) collective-permute-start(bf16[256,512]{1,0:T(8,128)(2,1)} %get-tuple-element.100.refs_5_), channel_id=1, source_target_pairs={{0,2},{1,3},{2,0},{3,1},{4,6},{5,7},{6,4},{7,5},{8,10},{9,11},{10,... | collective-permute-start | bytes 786440 | tf_op jit(solution)/shard_map/ppermute | solution.py:356
  11.5 1.3 %collective-permute-start.6 = (bf16[256,512]{1,0:T(8,128)(2,1)}, bf16[256,512]{1,0:T(8,128)(2,1)}, u32[]{:S(2)}, u32[]{:S(2)}) collective-permute-start(bf16[256,512]{1,0:T(8,128)(2,1)} %get-tuple-element.100.refs_5_), channel_id=1, source_target_pairs={{0,4},{1,5},{2,6},{3,7},{4,12},{5,13},{6,14},{7,15},{8,0},{9,1},{1... | collective-permute-start | bytes 786440 | tf_op jit(solution)/shard_map/ppermute | solution.py:361
  12.8 1.0 collective-permute-start.2
  13.7 2.1 %collective-permute-start.3 = (bf16[256,512]{1,0:T(8,128)(2,1)}, bf16[256,512]{1,0:T(8,128)(2,1)}, u32[]{:S(2)}, u32[]{:S(2)}) collective-permute-start(bf16[256,512]{1,0:T(8,128)(2,1)} %get-tuple-element.92), channel_id=1, source_target_pairs={{0,5},{1,4},{2,7},{3,6},{4,13},{5,12},{6,15},{7,14},{8,1},{9,0},{1... | collective-permute-start | bytes 786440 | tf_op jit(solution)/shard_map/ppermute | solution.py:361
  15.9 2.2 %copy-done.1 = bf16[128,8,2048]{2,1,0:T(8,128)(2,1)S(1)} copy-done((bf16[128,8,2048]{2,1,0:T(8,128)(2,1)S(1)}, bf16[128,8,2048]{2,1,0:T(8,128)(2,1)}, u32[]{:S(2)}) %copy-start.1) | copy-done | bytes 4194328
  18.1 0.7 shard_map.74
  19.6 2.3 %shard_map.75 = (bf16[1024,512]{1,0:T(8,128)(2,1)S(1)}, bf16[1040,512]{1,0:T(8,128)(2,1)S(1)}) custom-call(bf16[1024,1024]{1,0:T(8,128)(2,1)S(1)} %get-tuple-element.103.order_ref, bf16[16,512]{1,0:T(8,128)(2,1)S(1)} %get-tuple-element.94.head_ref, bf16[128,8,2048]{2,1,0:T(8,128)(2,1)S(1)} %copy-done.1), custom_call_target="tpu_custom_call" | custom-call | flops 1 | bytes 1 | tf_op jit(solution)/shard_map/pallas_call | solution.py:414
  22.0 1.3 %shard_map.76 = (bf16[272,512]{1,0:T(8,128)(2,1)S(1)}, bf16[256,512]{1,0:T(8,128)(2,1)S(1)}, bf16[256,512]{1,0:T(8,128)(2,1)S(1)}, bf16[256,512]{1,0:T(8,128)(2,1)S(1)}) custom-call(bf16[1024,1024]{1,0:T(8,128)(2,1)S(1)} %get-tuple-element.103.order_ref, bf16[16,512]{1,0:T(8,128)(2,1)S(1)} %get-tuple-element.94.head_ref, bf16[128,8,2048]{2,1,0:T(8,128)(2,1)S(1)} %copy-done.1), custom_call_target="tpu_custom_call" | custom-call | flops 1 | bytes 1 | tf_op jit(solution)/shard_map/pallas_call | solution.py:414
  23.2 0.7 copy-done.10
  24.0 0.7 copy-done.12
  24.7 0.7 copy-done.14
  25.4 0.7 copy-done.16
  26.2 1.5 %copy-done.2 = bf16[128,7168]{1,0:T(8,128)(2,1)S(1)} copy-done((bf16[128,7168]{1,0:T(8,128)(2,1)S(1)}, bf16[128,7168]{1,0:T(8,128)(2,1)}, u32[]{:S(2)}) %copy-start.2) | copy-done | bytes 1835032
  27.7 1.2 %copy-done.3 = bf16[64,7168]{1,0:T(8,128)(2,1)S(1)} copy-done((bf16[64,7168]{1,0:T(8,128)(2,1)S(1)}, bf16[64,7168]{1,0:T(8,128)(2,1)}, u32[]{:S(2)}) %copy-start.3) | copy-done | bytes 917528
  28.9 2.0 %shard_map.77 = (bf16[256,256]{1,0:T(8,128)(2,1)S(1)}, bf16[1024,1024]{1,0:T(8,128)(2,1)S(1)}) custom-call(bf16[128,7168]{1,0:T(8,128)(2,1)S(1)} %copy-done.2, bf16[64,7168]{1,0:T(8,128)(2,1)S(1)} %copy-done.3, s32[128,1]{1,0:T(8,128)S(1)} %copy.26.segment_ref, s32[8,128]{1,0:T(8,128)S(1)} %bitcast.5), custom_call_target="tpu_custom_call" | custom-call | flops 1 | bytes 1 | tf_op jit(solution)/shard_map/pallas_call | solution.py:447
  31.5 1.0 %collective-permute-start.7 = (bf16[1040,512]{1,0:T(8,128)(2,1)}, bf16[1040,512]{1,0:T(8,128)(2,1)S(1)}, u32[]{:S(2)}, u32[]{:S(2)}) collective-permute-start(bf16[1040,512]{1,0:T(8,128)(2,1)} %copy-done.9), channel_id=1, source_target_pairs={{0,1},{1,0},{2,3},{3,2},{4,5},{5,4},{6,7},{7,6},{8,9},{9,8},{10,11... | collective-permute-start | bytes 3194888 | tf_op jit(solution)/shard_map/ppermute | solution.py:356
  32.5 1.2 %collective-permute-start.8 = (bf16[256,512]{1,0:T(8,128)(2,1)}, bf16[256,512]{1,0:T(8,128)(2,1)S(1)}, u32[]{:S(2)}, u32[]{:S(2)}) collective-permute-start(bf16[256,512]{1,0:T(8,128)(2,1)} %copy-done.20), channel_id=1, source_target_pairs={{0,16},{1,17},{2,18},{3,19},{4,20},{5,21},{6,22},{7,23},{8,24},{9,... | collective-permute-start | bytes 786440 | tf_op jit(solution)/shard_map/ppermute | solution.py:356
  33.8 1.2 %collective-permute-start.9 = (bf16[256,512]{1,0:T(8,128)(2,1)}, bf16[256,512]{1,0:T(8,128)(2,1)S(1)}, u32[]{:S(2)}, u32[]{:S(2)}) collective-permute-start(bf16[256,512]{1,0:T(8,128)(2,1)} %collective-permute-done.6.refs_8_), channel_id=1, source_target_pairs={{0,2},{1,3},{2,0},{3,1},{4,6},{5,7},{6,4},{7,5},{8,10},{9,11},{10,... | collective-permute-start | bytes 786440 | tf_op jit(solution)/shard_map/ppermute | solution.py:356
  35.0 3.5 %collective-permute-done.1.refs_4_ = bf16[256,512]{1,0:T(8,128)(2,1)S(1)} collective-permute-done((bf16[256,512]{1,0:T(8,128)(2,1)}, bf16[256,512]{1,0:T(8,128)(2,1)S(1)}, u32[]{:S(2)}, u32[]{:S(2)}) %collective-permute-start.1) | collective-permute-done | bytes 262176 | tf_op jit(solution)/shard_map/ppermute | solution.py:356
  40.0 4.1 %collective-permute-done.8.refs_2_ = bf16[256,512]{1,0:T(8,128)(2,1)S(1)} collective-permute-done((bf16[256,512]{1,0:T(8,128)(2,1)}, bf16[256,512]{1,0:T(8,128)(2,1)S(1)}, u32[]{:S(2)}, u32[]{:S(2)}) %collective-permute-start.8) | collective-permute-done | bytes 262176 | tf_op jit(solution)/shard_map/ppermute | solution.py:356
  44.5 0.9 copy-done.6
  45.4 4.5 %shard_map.78 = (bf16[4096,512]{1,0:T(8,128)(2,1)S(1)}, bf16[16,256,512]{2,1,0:T(8,128)(2,1)S(1)}, f32[4096,128]{1,0:T(8,128)S(1)}) custom-call(s32[16,16]{1,0:T(8,128)S(1)} %copy-done.4, s32[1,128]{1,0:T(1,128)S(1)} %get-tuple-element.116.refs_0_, s32[1,128]{1,0:T(1,128)S(1)} %slice_add_fusion.2.refs_1_, bf16[1024,512]{1,0:T(8,128)(2,1)S(1)} %get-tuple-element.121.refs_2_, ...), custom_call_target="tpu_custom_call" | custom-call | flops 600000000 | bytes 1 | tf_op jit(solution)/shard_map/pallas_call | solution.py:273
  49.9 2.5 %collective-permute-start.11 = (bf16[272,512]{1,0:T(8,128)(2,1)S(1)}, bf16[272,512]{1,0:T(8,128)(2,1)S(1)}, u32[]{:S(2)}, u32[]{:S(2)}) collective-permute-start(bf16[272,512]{1,0:T(8,128)(2,1)S(1)} %copy-done.11), channel_id=1, source_target_pairs={{0,17},{1,16},{2,19},{3,18},{4,21},{5,20},{6,23},{7,22},{8,25},{9,... | collective-permute-start | bytes 835592 | tf_op jit(solution)/shard_map/ppermute | solution.py:356
  52.4 1.0 %collective-permute-start.12 = (bf16[256,512]{1,0:T(8,128)(2,1)S(1)}, bf16[256,512]{1,0:T(8,128)(2,1)S(1)}, u32[]{:S(2)}, u32[]{:S(2)}) collective-permute-start(bf16[256,512]{1,0:T(8,128)(2,1)S(1)} %collective-permute-done.10.refs_4_), channel_id=1, source_target_pairs={{0,2},{1,3},{2,0},{3,1},{4,6},{5,7},{6,4},{7,5},{8,10},{9,11},{10,... | collective-permute-start | bytes 786440 | tf_op jit(solution)/shard_map/ppermute | solution.py:356
  54.1 2.0 %shard_map.79 = (bf16[4096,512]{1,0:T(8,128)(2,1)S(1)}, bf16[16,256,512]{2,1,0:T(8,128)(2,1)S(1)}, f32[4096,128]{1,0:T(8,128)S(1)}) custom-call(s32[16,16]{1,0:T(8,128)S(1)} %copy-done.4, s32[1,128]{1,0:T(1,128)S(1)} %get-tuple-element.116.refs_0_, s32[1,128]{1,0:T(1,128)S(1)} %slice_add_fusion.2.refs_1_, ...), custom_call_target="tpu_custom_call", output_to_operand_aliasing={{0}: (6, {}), {1}: (7, {}), {2}: (8, {})} | custom-call | flops 600000000 | bytes 1 | tf_op jit(solution)/shard_map/pallas_call | solution.py:273
  56.3 2.1 %shard_map.80 = (bf16[4096,512]{1,0:T(8,128)(2,1)S(1)}, bf16[16,256,512]{2,1,0:T(8,128)(2,1)S(1)}, f32[4096,128]{1,0:T(8,128)S(1)}) custom-call(s32[16,16]{1,0:T(8,128)S(1)} %copy-done.4, s32[1,128]{1,0:T(1,128)S(1)} %get-tuple-element.116.refs_0_, s32[1,128]{1,0:T(1,128)S(1)} %slice_add_fusion.2.refs_1_, ...), custom_call_target="tpu_custom_call", output_to_operand_aliasing={{0}: (6, {}), {1}: (7, {}), {2}: (8, {})} | custom-call | flops 600000000 | bytes 1 | tf_op jit(solution)/shard_map/pallas_call | solution.py:273
  58.4 2.0 %collective-permute-done.12.refs_6_ = bf16[256,512]{1,0:T(8,128)(2,1)S(1)} collective-permute-done((bf16[256,512]{1,0:T(8,128)(2,1)S(1)}, bf16[256,512]{1,0:T(8,128)(2,1)S(1)}, u32[]{:S(2)}, u32[]{:S(2)}) %collective-permute-start.12) | collective-permute-done | bytes 262176 | tf_op jit(solution)/shard_map/ppermute | solution.py:356
  60.6 1.1 %collective-permute-done.13.refs_7_ = bf16[256,512]{1,0:T(8,128)(2,1)S(1)} collective-permute-done((bf16[256,512]{1,0:T(8,128)(2,1)S(1)}, bf16[256,512]{1,0:T(8,128)(2,1)S(1)}, u32[]{:S(2)}, u32[]{:S(2)}) %collective-permute-start.13) | collective-permute-done | bytes 262176 | tf_op jit(solution)/shard_map/ppermute | solution.py:361
  61.8 1.7 %collective-permute-start.17 = (bf16[256,512]{1,0:T(8,128)(2,1)S(1)}, bf16[256,512]{1,0:T(8,128)(2,1)S(1)}, u32[]{:S(2)}, u32[]{:S(2)}) collective-permute-start(bf16[256,512]{1,0:T(8,128)(2,1)S(1)} %copy-done.17), channel_id=1, source_target_pairs={{0,17},{1,16},{2,19},{3,18},{4,21},{5,20},{6,23},{7,22},{8,25},{9,... | collective-permute-start | bytes 786440 | tf_op jit(solution)/shard_map/ppermute | solution.py:356
  63.6 0.7 collective-permute-start.23
  64.3 5.1 %shard_map.81 = (bf16[4096,512]{1,0:T(8,128)(2,1)S(1)}, bf16[16,256,512]{2,1,0:T(8,128)(2,1)S(1)}, f32[4096,128]{1,0:T(8,128)S(1)}) custom-call(s32[16,16]{1,0:T(8,128)S(1)} %copy-done.4, s32[1,128]{1,0:T(1,128)S(1)} %get-tuple-element.116.refs_0_, ...), custom_call_target="tpu_custom_call", output_to_operand_aliasing={{0}: (9, {}), {1}: (10, {}), {2}: (11, {})} | custom-call | flops 600000000 | bytes 1 | tf_op jit(solution)/shard_map/pallas_call | solution.py:273
  69.4 0.8 collective-permute-done.17.refs_4_
  70.2 1.7 %collective-permute-start.20 = (bf16[256,512]{1,0:T(8,128)(2,1)S(1)}, bf16[256,512]{1,0:T(8,128)(2,1)S(1)}, u32[]{:S(2)}, u32[]{:S(2)}) collective-permute-start(bf16[256,512]{1,0:T(8,128)(2,1)S(1)} %copy-done.13), channel_id=1, source_target_pairs={{0,17},{1,16},{2,19},{3,18},{4,21},{5,20},{6,23},{7,22},{8,25},{9,... | collective-permute-start | bytes 786440 | tf_op jit(solution)/shard_map/ppermute | solution.py:356
  72.5 2.3 %shard_map.82 = (bf16[4096,512]{1,0:T(8,128)(2,1)S(1)}, bf16[16,256,512]{2,1,0:T(8,128)(2,1)S(1)}, f32[4096,128]{1,0:T(8,128)S(1)}) custom-call(s32[16,16]{1,0:T(8,128)S(1)} %copy-done.4, s32[1,128]{1,0:T(1,128)S(1)} %get-tuple-element.116.refs_0_, ...), custom_call_target="tpu_custom_call", output_to_operand_aliasing={{0}: (8, {}), {1}: (9, {}), {2}: (10, {})} | custom-call | flops 600000000 | bytes 1 | tf_op jit(solution)/shard_map/pallas_call | solution.py:273
  74.8 1.0 %collective-permute-done.22.refs_4_ = bf16[256,512]{1,0:T(8,128)(2,1)S(1)} collective-permute-done((bf16[256,512]{1,0:T(8,128)(2,1)S(1)}, bf16[256,512]{1,0:T(8,128)(2,1)S(1)}, u32[]{:S(2)}, u32[]{:S(2)}) %collective-permute-start.22) | collective-permute-done | bytes 262176 | tf_op jit(solution)/shard_map/ppermute | solution.py:356
  75.8 2.4 %shard_map.83 = (bf16[4096,512]{1,0:T(8,128)(2,1)S(1)}, bf16[16,256,512]{2,1,0:T(8,128)(2,1)S(1)}, f32[4096,128]{1,0:T(8,128)S(1)}) custom-call(s32[16,16]{1,0:T(8,128)S(1)} %copy-done.4, s32[1,128]{1,0:T(1,128)S(1)} %get-tuple-element.116.refs_0_, s32[1,128]{1,0:T(1,128)S(1)} %slice_add_fusion.2.refs_1_, ...), custom_call_target="tpu_custom_call", output_to_operand_aliasing={{0}: (7, {}), {1}: (8, {}), {2}: (9, {})} | custom-call | flops 600000000 | bytes 1 | tf_op jit(solution)/shard_map/pallas_call | solution.py:273
  78.2 3.2 %collective-permute-done.20.refs_4_ = bf16[256,512]{1,0:T(8,128)(2,1)S(1)} collective-permute-done((bf16[256,512]{1,0:T(8,128)(2,1)S(1)}, bf16[256,512]{1,0:T(8,128)(2,1)S(1)}, u32[]{:S(2)}, u32[]{:S(2)}) %collective-permute-start.20) | collective-permute-done | bytes 262176 | tf_op jit(solution)/shard_map/ppermute | solution.py:356
  81.4 2.9 %shard_map.84 = (bf16[4096,512]{1,0:T(8,128)(2,1)S(1)}, bf16[16,256,512]{2,1,0:T(8,128)(2,1)S(1)}, f32[4096,128]{1,0:T(8,128)S(1)}, bf16[512,128]{1,0:T(8,128)(2...) custom-call(s32[16,16]{1,0:T(8,128)S(1)} %copy-done.4, ...), custom_call_target="tpu_custom_call", output_to_operand_aliasing={{0}: (7, {}), {1}: (8, {}), {2}: (9, {})} | custom-call | flops 600000000 | bytes 1 | tf_op jit(solution)/shard_map/pallas_call | solution.py:273
  84.3 1.0 %collective-permute-start.24 = (bf16[512,128]{1,0:T(8,128)(2,1)S(1)}, bf16[512,128]{1,0:T(8,128)(2,1)S(1)}, u32[]{:S(2)}, u32[]{:S(2)}) collective-permute-start(bf16[512,128]{1,0:T(8,128)(2,1)S(1)} %get-tuple-element.174), channel_id=1, source_target_pairs={{0,1},{1,0},{2,3},{3,2},{4,5},{5,4},{6,7},{7,6},{8,9},{9,8},{10,11... | collective-permute-start | bytes 393224 | tf_op jit(solution)/shard_map/ppermute | solution.py:356
  85.9 1.1 %collective-permute-start.26 = (bf16[512,128]{1,0:T(8,128)(2,1)S(1)}, bf16[512,128]{1,0:T(8,128)(2,1)S(1)}, u32[]{:S(2)}, u32[]{:S(2)}) collective-permute-start(bf16[512,128]{1,0:T(8,128)(2,1)S(1)} %get-tuple-element.176), channel_id=1, source_target_pairs={{0,17},{1,16},{2,19},{3,18},{4,21},{5,20},{6,23},{7,22},{8,25},{9,... | collective-permute-start | bytes 393224 | tf_op jit(solution)/shard_map/ppermute | solution.py:356
  87.0 3.4 %collective-permute-done.25.c_ref = bf16[512,128]{1,0:T(8,128)(2,1)S(1)} collective-permute-done((bf16[512,128]{1,0:T(8,128)(2,1)S(1)}, bf16[512,128]{1,0:T(8,128)(2,1)S(1)}, u32[]{:S(2)}, u32[]{:S(2)}) %collective-permute-start.25) | collective-permute-done | bytes 131104 | tf_op jit(solution)/shard_map/ppermute | solution.py:356
  90.4 3.0 %collective-permute-done.26.d_ref = bf16[512,128]{1,0:T(8,128)(2,1)S(1)} collective-permute-done((bf16[512,128]{1,0:T(8,128)(2,1)S(1)}, bf16[512,128]{1,0:T(8,128)(2,1)S(1)}, u32[]{:S(2)}, u32[]{:S(2)}) %collective-permute-start.26) | collective-permute-done | bytes 131104 | tf_op jit(solution)/shard_map/ppermute | solution.py:356
  93.3 3.4 %shard_map.85 = bf16[2,64,4096]{2,1,0:T(8,128)(2,1)} custom-call(s32[8,128]{1,0:T(8,128)S(1)} %bitcast.6, bf16[256,256]{1,0:T(8,128)(2,1)S(1)} %get-tuple-element.114.basis_ref, bf16[1024,1024]{1,0:T(8,128)(2,1)S(1)} %get-tuple-element.115.order_ref, f32[4096,128]{1,0:T(8,128)S(1)} %get-tuple-element.173.total_ref, ...), custom_call_target="tpu_custom_call" | custom-call | flops 1 | bytes 1 | tf_op jit(solution)/shard_map/pallas_call | solution.py:534
  (71 shorter events, 5.8 us)
Async XLA Ops:
  4.8 2.0 %copy-start = (bf16[128,8,2048]{2,1,0:T(8,128)(2,1)}, bf16[128,8,2048]{2,1,0:T(8,128)(2,1)S(1)}, u32[]{:S(2)}) copy-start(bf16[128,8,2048]{2,1,0:T(8,128)(2,1)S(1)} %get-tuple-element.95.grads_ref) | copy-start | bytes 12582916
  6.8 0.7 copy-start.19
  7.5 6.2 %collective-permute-start = (bf16[256,512]{1,0:T(8,128)(2,1)}, bf16[256,512]{1,0:T(8,128)(2,1)S(1)}, u32[]{:S(2)}, u32[]{:S(2)}) collective-permute-start(bf16[256,512]{1,0:T(8,128)(2,1)} %get-tuple-element.92), channel_id=1, source_target_pairs={{0,1},{1,0},{2,3},{3,2},{4,5},{5,4},{6,7},{7,6},{8,9},{9,8},{10,11... | collective-permute-start | bytes 786440 | tf_op jit(solution)/shard_map/ppermute | solution.py:356
  7.6 23.7 %collective-permute-start.4 = (bf16[272,512]{1,0:T(8,128)(2,1)}, bf16[272,512]{1,0:T(8,128)(2,1)S(1)}, u32[]{:S(2)}, u32[]{:S(2)}) collective-permute-start(bf16[272,512]{1,0:T(8,128)(2,1)} %get-tuple-element.99), channel_id=1, source_target_pairs={{0,16},{1,17},{2,18},{3,19},{4,20},{5,21},{6,22},{7,23},{8,24},{9,... | collective-permute-start | bytes 835592 | tf_op jit(solution)/shard_map/ppermute | solution.py:356
  10.2 20.7 %collective-permute-start.5 = (bf16[256,512]{1,0:T(8,128)(2,1)}, bf16[256,512]{1,0:T(8,128)(2,1)}, u32[]{:S(2)}, u32[]{:S(2)}) collective-permute-start(bf16[256,512]{1,0:T(8,128)(2,1)} %get-tuple-element.100.refs_5_), channel_id=1, source_target_pairs={{0,2},{1,3},{2,0},{3,1},{4,6},{5,7},{6,4},{7,5},{8,10},{9,11},{10,... | collective-permute-start | bytes 786440 | tf_op jit(solution)/shard_map/ppermute | solution.py:356
  11.5 19.8 %collective-permute-start.6 = (bf16[256,512]{1,0:T(8,128)(2,1)}, bf16[256,512]{1,0:T(8,128)(2,1)}, u32[]{:S(2)}, u32[]{:S(2)}) collective-permute-start(bf16[256,512]{1,0:T(8,128)(2,1)} %get-tuple-element.100.refs_5_), channel_id=1, source_target_pairs={{0,4},{1,5},{2,6},{3,7},{4,12},{5,13},{6,14},{7,15},{8,0},{9,1},{1... | collective-permute-start | bytes 786440 | tf_op jit(solution)/shard_map/ppermute | solution.py:361
  12.8 19.8 %collective-permute-start.2 = (bf16[256,512]{1,0:T(8,128)(2,1)}, bf16[256,512]{1,0:T(8,128)(2,1)}, u32[]{:S(2)}, u32[]{:S(2)}) collective-permute-start(bf16[256,512]{1,0:T(8,128)(2,1)} %get-tuple-element.92), channel_id=1, source_target_pairs={{0,3},{1,2},{2,1},{3,0},{4,7},{5,6},{6,5},{7,4},{8,11},{9,10},{10,... | collective-permute-start | bytes 786440 | tf_op jit(solution)/shard_map/ppermute | solution.py:356
  13.7 5.1 %copy-start.5 = (bf16[256,512]{1,0:T(8,128)(2,1)}, bf16[256,512]{1,0:T(8,128)(2,1)S(1)}, u32[]{:S(2)}) copy-start(bf16[256,512]{1,0:T(8,128)(2,1)S(1)} %collective-permute-done.refs_6_) | copy-start | bytes 786436
  13.7 20.0 %collective-permute-start.3 = (bf16[256,512]{1,0:T(8,128)(2,1)}, bf16[256,512]{1,0:T(8,128)(2,1)}, u32[]{:S(2)}, u32[]{:S(2)}) collective-permute-start(bf16[256,512]{1,0:T(8,128)(2,1)} %get-tuple-element.92), channel_id=1, source_target_pairs={{0,5},{1,4},{2,7},{3,6},{4,13},{5,12},{6,15},{7,14},{8,1},{9,0},{1... | collective-permute-start | bytes 786440 | tf_op jit(solution)/shard_map/ppermute | solution.py:361
  15.9 2.2 %copy-start.1 = (bf16[128,8,2048]{2,1,0:T(8,128)(2,1)S(1)}, bf16[128,8,2048]{2,1,0:T(8,128)(2,1)}, u32[]{:S(2)}) copy-start(bf16[128,8,2048]{2,1,0:T(8,128)(2,1)} %copy-done) | copy-start | bytes 12582916
  18.8 0.7 copy-start.18
  18.8 0.8 copy-start.20
  21.9 4.2 %copy-start.9 = (bf16[1040,512]{1,0:T(8,128)(2,1)}, bf16[1040,512]{1,0:T(8,128)(2,1)S(1)}, u32[]{:S(2)}) copy-start(bf16[1040,512]{1,0:T(8,128)(2,1)S(1)} %get-tuple-element.118) | copy-start | bytes 3194884
  21.9 4.2 %copy-start.21 = (s32[128]{0:T(128)S(1)}, s32[128]{0:T(128)}, u32[]{:S(2)}) copy-start(s32[128]{0:T(128)} %param.10) | copy-start | bytes 1540
  21.9 4.3 %copy-start.8 = (s32[128,8]{0,1:T(8,128)S(1)}, s32[128,8]{0,1:T(8,128)}, u32[]{:S(2)}) copy-start(s32[128,8]{0,1:T(8,128)} %param.9) | copy-start | bytes 12292
  21.9 22.5 %copy-start.4 = (s32[16,16]{1,0:T(8,128)S(1)}, s32[16,16]{1,0:T(8,128)}, u32[]{:S(2)}) copy-start(s32[16,16]{1,0:T(8,128)} %constant.10.clone.bases_ref) | copy-start | bytes 3076
  23.2 0.7 copy-start.10
  24.0 0.7 copy-start.12
  24.7 0.7 copy-start.14
  25.4 0.7 copy-start.16
  26.2 1.5 %copy-start.2 = (bf16[128,7168]{1,0:T(8,128)(2,1)S(1)}, bf16[128,7168]{1,0:T(8,128)(2,1)}, u32[]{:S(2)}) copy-start(bf16[128,7168]{1,0:T(8,128)(2,1)} %hidden_ref.1) | copy-start | bytes 5505028
  27.7 1.2 %copy-start.3 = (bf16[64,7168]{1,0:T(8,128)(2,1)S(1)}, bf16[64,7168]{1,0:T(8,128)(2,1)}, u32[]{:S(2)}) copy-start(bf16[64,7168]{1,0:T(8,128)(2,1)} %proj_ref.1) | copy-start | bytes 2752516
  28.9 21.0 %copy-start.11 = (bf16[272,512]{1,0:T(8,128)(2,1)S(1)}, bf16[272,512]{1,0:T(8,128)(2,1)}, u32[]{:S(2)}) copy-start(bf16[272,512]{1,0:T(8,128)(2,1)} %copy-done.10) | copy-start | bytes 835588
  30.9 7.6 %collective-permute-start.1 = (bf16[256,512]{1,0:T(8,128)(2,1)}, bf16[256,512]{1,0:T(8,128)(2,1)S(1)}, u32[]{:S(2)}, u32[]{:S(2)}) collective-permute-start(bf16[256,512]{1,0:T(8,128)(2,1)} %copy-done.19), channel_id=1, source_target_pairs={{0,16},{1,17},{2,18},{3,19},{4,20},{5,21},{6,22},{7,23},{8,24},{9,... | collective-permute-start | bytes 786440 | tf_op jit(solution)/shard_map/ppermute | solution.py:356
  31.2 8.1 %collective-permute-start.10 = (bf16[256,512]{1,0:T(8,128)(2,1)}, bf16[256,512]{1,0:T(8,128)(2,1)S(1)}, u32[]{:S(2)}, u32[]{:S(2)}) collective-permute-start(bf16[256,512]{1,0:T(8,128)(2,1)} %collective-permute-done.6.refs_8_), channel_id=1, source_target_pairs={{0,4},{1,5},{2,6},{3,7},{4,12},{5,13},{6,14},{7,15},{8,0},{9,1},{1... | collective-permute-start | bytes 786440 | tf_op jit(solution)/shard_map/ppermute | solution.py:361
  31.5 32.1 %collective-permute-start.7 = (bf16[1040,512]{1,0:T(8,128)(2,1)}, bf16[1040,512]{1,0:T(8,128)(2,1)S(1)}, u32[]{:S(2)}, u32[]{:S(2)}) collective-permute-start(bf16[1040,512]{1,0:T(8,128)(2,1)} %copy-done.9), channel_id=1, source_target_pairs={{0,1},{1,0},{2,3},{3,2},{4,5},{5,4},{6,7},{7,6},{8,9},{9,8},{10,11... | collective-permute-start | bytes 3194888 | tf_op jit(solution)/shard_map/ppermute | solution.py:356
  32.5 11.6 %collective-permute-start.8 = (bf16[256,512]{1,0:T(8,128)(2,1)}, bf16[256,512]{1,0:T(8,128)(2,1)S(1)}, u32[]{:S(2)}, u32[]{:S(2)}) collective-permute-start(bf16[256,512]{1,0:T(8,128)(2,1)} %copy-done.20), channel_id=1, source_target_pairs={{0,16},{1,17},{2,18},{3,19},{4,20},{5,21},{6,22},{7,23},{8,24},{9,... | collective-permute-start | bytes 786440 | tf_op jit(solution)/shard_map/ppermute | solution.py:356
  33.8 16.1 %collective-permute-start.9 = (bf16[256,512]{1,0:T(8,128)(2,1)}, bf16[256,512]{1,0:T(8,128)(2,1)S(1)}, u32[]{:S(2)}, u32[]{:S(2)}) collective-permute-start(bf16[256,512]{1,0:T(8,128)(2,1)} %collective-permute-done.6.refs_8_), channel_id=1, source_target_pairs={{0,2},{1,3},{2,0},{3,1},{4,6},{5,7},{6,4},{7,5},{8,10},{9,11},{10,... | collective-permute-start | bytes 786440 | tf_op jit(solution)/shard_map/ppermute | solution.py:356
  38.5 13.9 %collective-permute-start.14 = (bf16[256,512]{1,0:T(8,128)(2,1)}, bf16[256,512]{1,0:T(8,128)(2,1)S(1)}, u32[]{:S(2)}, u32[]{:S(2)}) collective-permute-start(bf16[256,512]{1,0:T(8,128)(2,1)} %copy-done.18), channel_id=1, source_target_pairs={{0,16},{1,17},{2,18},{3,19},{4,20},{5,21},{6,22},{7,23},{8,24},{9,... | collective-permute-start | bytes 786440 | tf_op jit(solution)/shard_map/ppermute | solution.py:356
  39.3 14.1 %collective-permute-start.15 = (bf16[256,512]{1,0:T(8,128)(2,1)}, bf16[256,512]{1,0:T(8,128)(2,1)S(1)}, u32[]{:S(2)}, u32[]{:S(2)}) collective-permute-start(bf16[256,512]{1,0:T(8,128)(2,1)} %collective-permute-done.3.refs_10_), channel_id=1, source_target_pairs={{0,2},{1,3},{2,0},{3,1},{4,6},{5,7},{6,4},{7,5},{8,10},{9,11},{10,... | collective-permute-start | bytes 786440 | tf_op jit(solution)/shard_map/ppermute | solution.py:356
  44.1 12.1 %collective-permute-start.16 = (bf16[256,512]{1,0:T(8,128)(2,1)}, bf16[256,512]{1,0:T(8,128)(2,1)S(1)}, u32[]{:S(2)}, u32[]{:S(2)}) collective-permute-start(bf16[256,512]{1,0:T(8,128)(2,1)} %collective-permute-done.3.refs_10_), channel_id=1, source_target_pairs={{0,4},{1,5},{2,6},{3,7},{4,12},{5,13},{6,14},{7,15},{8,0},{9,1},{1... | collective-permute-start | bytes 786440 | tf_op jit(solution)/shard_map/ppermute | solution.py:361
  44.5 1.0 copy-start.6
  49.9 13.6 %collective-permute-start.11 = (bf16[272,512]{1,0:T(8,128)(2,1)S(1)}, bf16[272,512]{1,0:T(8,128)(2,1)S(1)}, u32[]{:S(2)}, u32[]{:S(2)}) collective-permute-start(bf16[272,512]{1,0:T(8,128)(2,1)S(1)} %copy-done.11), channel_id=1, source_target_pairs={{0,17},{1,16},{2,19},{3,18},{4,21},{5,20},{6,23},{7,22},{8,25},{9,... | collective-permute-start | bytes 835592 | tf_op jit(solution)/shard_map/ppermute | solution.py:356
  52.4 8.0 %collective-permute-start.12 = (bf16[256,512]{1,0:T(8,128)(2,1)S(1)}, bf16[256,512]{1,0:T(8,128)(2,1)S(1)}, u32[]{:S(2)}, u32[]{:S(2)}) collective-permute-start(bf16[256,512]{1,0:T(8,128)(2,1)S(1)} %collective-permute-done.10.refs_4_), channel_id=1, source_target_pairs={{0,2},{1,3},{2,0},{3,1},{4,6},{5,7},{6,4},{7,5},{8,10},{9,11},{10,... | collective-permute-start | bytes 786440 | tf_op jit(solution)/shard_map/ppermute | solution.py:356
  53.5 8.3 %collective-permute-start.13 = (bf16[256,512]{1,0:T(8,128)(2,1)S(1)}, bf16[256,512]{1,0:T(8,128)(2,1)S(1)}, u32[]{:S(2)}, u32[]{:S(2)}) collective-permute-start(bf16[256,512]{1,0:T(8,128)(2,1)S(1)} %collective-permute-done.10.refs_4_), channel_id=1, source_target_pairs={{0,4},{1,5},{2,6},{3,7},{4,12},{5,13},{6,14},{7,15},{8,0},{9,1},{1... | collective-permute-start | bytes 786440 | tf_op jit(solution)/shard_map/ppermute | solution.py:361
  56.2 5.6 %copy-start.17 = (bf16[256,512]{1,0:T(8,128)(2,1)S(1)}, bf16[256,512]{1,0:T(8,128)(2,1)}, u32[]{:S(2)}) copy-start(bf16[256,512]{1,0:T(8,128)(2,1)} %copy-done.16) | copy-start | bytes 786436
  56.2 7.3 %copy-start.15 = (bf16[256,512]{1,0:T(8,128)(2,1)S(1)}, bf16[256,512]{1,0:T(8,128)(2,1)}, u32[]{:S(2)}) copy-start(bf16[256,512]{1,0:T(8,128)(2,1)} %copy-done.14) | copy-start | bytes 786436
  56.2 13.9 %collective-permute-start.18 = (bf16[256,512]{1,0:T(8,128)(2,1)S(1)}, bf16[256,512]{1,0:T(8,128)(2,1)S(1)}, u32[]{:S(2)}, u32[]{:S(2)}) collective-permute-start(bf16[256,512]{1,0:T(8,128)(2,1)S(1)} %collective-permute-done.16.refs_4_), channel_id=1, source_target_pairs={{0,2},{1,3},{2,0},{3,1},{4,6},{5,7},{6,4},{7,5},{8,10},{9,11},{10,... | collective-permute-start | bytes 786440 | tf_op jit(solution)/shard_map/ppermute | solution.py:356
  60.4 9.7 %collective-permute-start.19 = (bf16[256,512]{1,0:T(8,128)(2,1)S(1)}, bf16[256,512]{1,0:T(8,128)(2,1)S(1)}, u32[]{:S(2)}, u32[]{:S(2)}) collective-permute-start(bf16[256,512]{1,0:T(8,128)(2,1)S(1)} %collective-permute-done.16.refs_4_), channel_id=1, source_target_pairs={{0,4},{1,5},{2,6},{3,7},{4,12},{5,13},{6,14},{7,15},{8,0},{9,1},{1... | collective-permute-start | bytes 786440 | tf_op jit(solution)/shard_map/ppermute | solution.py:361
  61.8 8.4 %collective-permute-start.17 = (bf16[256,512]{1,0:T(8,128)(2,1)S(1)}, bf16[256,512]{1,0:T(8,128)(2,1)S(1)}, u32[]{:S(2)}, u32[]{:S(2)}) collective-permute-start(bf16[256,512]{1,0:T(8,128)(2,1)S(1)} %copy-done.17), channel_id=1, source_target_pairs={{0,17},{1,16},{2,19},{3,18},{4,21},{5,20},{6,23},{7,22},{8,25},{9,... | collective-permute-start | bytes 786440 | tf_op jit(solution)/shard_map/ppermute | solution.py:356
  63.5 12.3 %collective-permute-start.22 = (bf16[256,512]{1,0:T(8,128)(2,1)S(1)}, bf16[256,512]{1,0:T(8,128)(2,1)S(1)}, u32[]{:S(2)}, u32[]{:S(2)}) collective-permute-start(bf16[256,512]{1,0:T(8,128)(2,1)S(1)} %copy-done.15), channel_id=1, source_target_pairs={{0,17},{1,16},{2,19},{3,18},{4,21},{5,20},{6,23},{7,22},{8,25},{9,... | collective-permute-start | bytes 786440 | tf_op jit(solution)/shard_map/ppermute | solution.py:356
  63.6 12.2 %collective-permute-start.23 = (bf16[256,512]{1,0:T(8,128)(2,1)S(1)}, bf16[256,512]{1,0:T(8,128)(2,1)S(1)}, u32[]{:S(2)}, u32[]{:S(2)}) collective-permute-start(bf16[256,512]{1,0:T(8,128)(2,1)S(1)} %collective-permute-done.13.refs_7_), channel_id=1, source_target_pairs={{0,2},{1,3},{2,0},{3,1},{4,6},{5,7},{6,4},{7,5},{8,10},{9,11},{10,... | collective-permute-start | bytes 786440 | tf_op jit(solution)/shard_map/ppermute | solution.py:356
  64.3 5.8 %copy-start.13 = (bf16[256,512]{1,0:T(8,128)(2,1)S(1)}, bf16[256,512]{1,0:T(8,128)(2,1)}, u32[]{:S(2)}) copy-start(bf16[256,512]{1,0:T(8,128)(2,1)} %copy-done.12) | copy-start | bytes 786436
  70.2 11.2 %collective-permute-start.20 = (bf16[256,512]{1,0:T(8,128)(2,1)S(1)}, bf16[256,512]{1,0:T(8,128)(2,1)S(1)}, u32[]{:S(2)}, u32[]{:S(2)}) collective-permute-start(bf16[256,512]{1,0:T(8,128)(2,1)S(1)} %copy-done.13), channel_id=1, source_target_pairs={{0,17},{1,16},{2,19},{3,18},{4,21},{5,20},{6,23},{7,22},{8,25},{9,... | collective-permute-start | bytes 786440 | tf_op jit(solution)/shard_map/ppermute | solution.py:356
  71.9 9.5 %collective-permute-start.21 = (bf16[256,512]{1,0:T(8,128)(2,1)S(1)}, bf16[256,512]{1,0:T(8,128)(2,1)S(1)}, u32[]{:S(2)}, u32[]{:S(2)}) collective-permute-start(bf16[256,512]{1,0:T(8,128)(2,1)S(1)} %collective-permute-done.19.refs_6_), channel_id=1, source_target_pairs={{0,2},{1,3},{2,0},{3,1},{4,6},{5,7},{6,4},{7,5},{8,10},{9,11},{10,... | collective-permute-start | bytes 786440 | tf_op jit(solution)/shard_map/ppermute | solution.py:356
  84.3 2.7 %collective-permute-start.24 = (bf16[512,128]{1,0:T(8,128)(2,1)S(1)}, bf16[512,128]{1,0:T(8,128)(2,1)S(1)}, u32[]{:S(2)}, u32[]{:S(2)}) collective-permute-start(bf16[512,128]{1,0:T(8,128)(2,1)S(1)} %get-tuple-element.174), channel_id=1, source_target_pairs={{0,1},{1,0},{2,3},{3,2},{4,5},{5,4},{6,7},{7,6},{8,9},{9,8},{10,11... | collective-permute-start | bytes 393224 | tf_op jit(solution)/shard_map/ppermute | solution.py:356
  85.3 5.1 %collective-permute-start.25 = (bf16[512,128]{1,0:T(8,128)(2,1)S(1)}, bf16[512,128]{1,0:T(8,128)(2,1)S(1)}, u32[]{:S(2)}, u32[]{:S(2)}) collective-permute-start(bf16[512,128]{1,0:T(8,128)(2,1)S(1)} %get-tuple-element.175), channel_id=1, source_target_pairs={{0,16},{1,17},{2,18},{3,19},{4,20},{5,21},{6,22},{7,23},{8,24},{9,... | collective-permute-start | bytes 393224 | tf_op jit(solution)/shard_map/ppermute | solution.py:356
  85.9 7.4 %collective-permute-start.26 = (bf16[512,128]{1,0:T(8,128)(2,1)S(1)}, bf16[512,128]{1,0:T(8,128)(2,1)S(1)}, u32[]{:S(2)}, u32[]{:S(2)}) collective-permute-start(bf16[512,128]{1,0:T(8,128)(2,1)S(1)} %get-tuple-element.176), channel_id=1, source_target_pairs={{0,17},{1,16},{2,19},{3,18},{4,21},{5,20},{6,23},{7,22},{8,25},{9,... | collective-permute-start | bytes 393224 | tf_op jit(solution)/shard_map/ppermute | solution.py:356
  (1 other events, 0.7 us)

commit v7 on v6

--- a/solution.py
+++ b/solution.py
@@ -22,7 +22,7 @@
 SMEM = pl.BlockSpec(memory_space=pltpu.SMEM)
 HBM = pl.BlockSpec(memory_space=pl.ANY)
 QUICK = pl.CostEstimate(flops=1, bytes_accessed=1, transcendentals=0)
-SHORT = pl.CostEstimate(flops=6 * 10**8, bytes_accessed=1, transcendentals=0)
+SHORT = pl.CostEstimate(flops=10**9, bytes_accessed=1, transcendentals=0)
 NT = (((1,), (1,)), ((), ()))
 
 
@@ -81,7 +81,6 @@
     head_ref,
     order_ref,
     piece_ref,
-    next_ref,
     stage,
     sems,
 ):
@@ -108,7 +107,7 @@
     row = lax.broadcasted_iota(jnp.int32, head_ref.shape, 0)
     head = jnp.where(row == 0, digits[0], jnp.where(row == 1, digits[1], 0.0))
     head_ref[...] = head.astype(jnp.bfloat16)
-    rows = next_ref.shape[0]
+    rows = piece_ref.shape[0] - ALIGN
     for first in range(0, pairs, rows):
         ids = first + lax.broadcasted_iota(jnp.int32, (rows, pairs), 0)
         order_ref[first : first + rows, :] = jnp.where(place == ids, 1.0, 0.0).astype(jnp.bfloat16)
@@ -117,14 +116,18 @@
     core_ref[...] = stage[:, columns_of(1, width)]
     for copy in copies[1:]:
         copy.wait()
-    sorted_rows = jnp.dot(
-        order_ref[0 : 2 * rows, :],
+    piece_ref[0:rows, :] = jnp.dot(
+        order_ref[0:rows, :],
         held_ref[:, :, columns_of(2, width)].reshape(pairs, width),
         preferred_element_type=jnp.float32,
     ).astype(jnp.bfloat16)
-    piece_ref[0:rows, :] = sorted_rows[0:rows]
     piece_ref[rows:, :] = head_ref[...]
-    next_ref[...] = sorted_rows[rows:]
+
+
+def join_kernel(one_ref, two_ref, out_ref):
+    half = one_ref.shape[0]
+    out_ref[0:half, :] = one_ref[...]
+    out_ref[half:, :] = two_ref[...]
 
 
 def permute_kernel(plan, order_ref, head_ref, grads_ref, *outs):
@@ -141,16 +144,16 @@
 
 
 def basis_kernel(
-    hidden_ref, proj_ref, segment_ref, routes_ref, out_ref, order_ref
+    hidden_ref, proj_ref, segment_ref, routes_ref, out_ref, order_ref, hidden, proj, sems
 ):
-    projected = lax.dot_general(
-        hidden_ref[...], proj_ref[...], NT, preferred_element_type=jnp.float32
-    )
-    zero = jnp.zeros_like(projected)
-    picked = [jnp.where(segment_ref[...] == s, projected, zero) for s in range(SEG_DEV)]
-    even = jnp.concatenate([b for p in picked for b in (p, zero)], axis=1)
-    odd = jnp.concatenate([b for p in picked for b in (zero, p)], axis=1)
-    out_ref[...] = jnp.concatenate([even, odd], axis=0).astype(out_ref.dtype)
+    count = sems.shape[0] - 1
+    part = hidden.shape[0] // count
+    copies = [pltpu.make_async_copy(proj_ref, proj, sems.at[count])]
+    for n in range(count):
+        here = pl.ds(n * part, part)
+        copies.append(pltpu.make_async_copy(hidden_ref.at[here], hidden.at[here], sems.at[n]))
+    for copy in copies:
+        copy.start()
     tops, tokens = routes_ref.shape
     pairs = tops * tokens
     column = key_column(row_of(routes_ref[...]))
@@ -162,6 +165,16 @@
     for first in range(0, pairs, 256):
         ids = first + lax.broadcasted_iota(jnp.int32, (256, pairs), 0)
         order_ref[first : first + 256, :] = jnp.where(place == ids, 1.0, 0.0).astype(jnp.bfloat16)
+    segment = (segment_ref[...] - lax.axis_index("expert") * SEG_DEV).astype(jnp.float32)
+    segment = jnp.broadcast_to(segment, (8, tokens)).T[:, 0:1]
+    for copy in copies:
+        copy.wait()
+    projected = lax.dot_general(hidden[...], proj[...], NT, preferred_element_type=jnp.float32)
+    zero = jnp.zeros_like(projected)
+    picked = [jnp.where(segment == float(s), projected, zero) for s in range(SEG_DEV)]
+    even = jnp.concatenate([b for p in picked for b in (p, zero)], axis=1)
+    odd = jnp.concatenate([b for p in picked for b in (zero, p)], axis=1)
+    out_ref[...] = jnp.concatenate([even, odd], axis=0).astype(out_ref.dtype)
 
 
 def packed(total, first, pairs, rank):
@@ -188,9 +201,10 @@
         send_refs = refs[6:]
     for ref, (first, count) in zip(token_refs, new_tokens):
         tokens[first : first + count, :] = ref[0:count, :]
+    cols = units.shape[1]
     for ref, place in zip(unit_refs, new_units):
-        units[place] = ref[...]
-    cols = units.shape[1]
+        for half in range(CORES):
+            units[place + half] = ref[half * cols : (half + 1) * cols, :]
     held = cols // rank
     per_tile = LANES // rank
     low = lax.broadcasted_iota(jnp.int32, (1, LANES), 1) < rank
@@ -251,7 +265,7 @@
 
 
 def accumulate(
-    state, bases, starts, tokens, units, tasks, rank, pairs, window, places=0, sends=()
+    state, bases, starts, tokens, units, tasks, rank, pairs, window, places=0, sends=(), cost=QUICK
 ):
     fresh = state is None
     operands = [bases, *starts.values(), *[a for a, _, _ in tokens], *[a for a, _ in units]]
@@ -260,7 +274,7 @@
         width = units[0][0].shape[1]
         shapes = [
             pltpu.VMEM((QUAD * pairs, width), jnp.bfloat16),
-            pltpu.VMEM((places, *units[0][0].shape), jnp.bfloat16),
+            pltpu.VMEM((places, units[0][0].shape[0] // CORES, width), jnp.bfloat16),
             pltpu.VMEM((QUAD * pairs, LANES), jnp.float32),
         ]
         aliases = {}
@@ -287,8 +301,8 @@
         in_specs=specs,
         out_specs=[VMEM] * len(shapes),
         input_output_aliases=aliases,
-        compiler_params=pltpu.CompilerParams(vmem_limit_bytes=16 * MIB),
-        cost_estimate=SHORT,
+        compiler_params=pltpu.CompilerParams(vmem_limit_bytes=8 * MIB),
+        cost_estimate=cost,
     )(*operands)
     return list(out[:3]), list(out[3:])
 
@@ -355,27 +369,36 @@
         ]
         return lax.ppermute(array, BOTH, table)
 
-    def onward(array, bit=0):
+    def along(array, table):
         wide = 2 * CORES
-        table = [(e, following[e // wide] * wide + (e % wide ^ bit)) for e in range(owners)]
-        return lax.ppermute(array, "expert", table)
+        pairs_of = [(e, table[e // wide] * wide + e % wide) for e in range(owners)]
+        return lax.ppermute(array, "expert", pairs_of)
 
     def tie(*arrays):
         return lax.optimization_barrier(arrays)
 
-    rows_of = []
-    for e in range(owners):
-        z, y, c = e // (2 * CORES), e // CORES % 2, e % CORES
-        named = [(z, y, c), (z, y, 1 - c)]
-        here = z
-        for slot in range(slots):
-            after = before[here]
-            for flip in (0, 1):
-                named.append((here, 1 - y, c ^ flip))
-                if slot + 1 < slots:
-                    named.append((after, y, c ^ flip))
-            here = after
-        rows_of.append([((a * 2 + b) * CORES + d) * exp_here for a, b, d in named])
+    ahead, back = slots // 2, (slots - 1) // 2
+    landing = [0]
+    for n in range(1, ahead + 1):
+        landing += [n] + ([-n] if n <= back else [])
+    known_first = [(n, 0) for n in landing[:-1]] + [(n, 1) for n in landing[:-2]]
+    known_next = [(landing[-1], 0), (landing[-2], 1)]
+    arrival = known_first + known_next + [(landing[-1], 1)]
+
+    def source(z, n):
+        for _ in range(abs(n)):
+            z = before[z] if n > 0 else following[z]
+        return z
+
+    rows_of = [
+        [
+            ((source(e // (2 * CORES), n) * 2 + (e // CORES % 2 ^ crossed)) * CORES + (e % CORES ^ flip))
+            * exp_here
+            for n, crossed in arrival
+            for flip in (0, 1)
+        ]
+        for e in range(owners)
+    ]
     places = len(rows_of[0])
     bases = jnp.asarray(np.array(rows_of, np.int32))
 
@@ -387,7 +410,7 @@
 
     by_rank = routes.T
     edges = -(-(experts + 1) // LANES) * LANES
-    held_grads, mine_unit, core_unit, own_starts, head, order, *first_pieces = pl.pallas_call(
+    held_grads, mine_unit, core_unit, own_starts, head, order, first_piece = pl.pallas_call(
         sort_kernel,
         out_shape=[
             pltpu.VMEM(out_grads.shape, jnp.bfloat16),
@@ -396,16 +419,15 @@
             jax.ShapeDtypeStruct((1, edges), jnp.int32),
             rows_shape(ALIGN),
             order_shape,
-            rows_shape(rows + ALIGN),
-            rows_shape(rows),
+            rows_shape(2 * rows + ALIGN),
         ],
         in_specs=[VMEM, HBM, HBM],
-        out_specs=[VMEM] * 8,
+        out_specs=[VMEM] * 7,
         scratch_shapes=[
             pltpu.VMEM((cols, width), jnp.bfloat16),
             pltpu.SemaphoreType.DMA((9,)),
         ],
-        compiler_params=pltpu.CompilerParams(vmem_limit_bytes=24 * MIB),
+        compiler_params=pltpu.CompilerParams(vmem_limit_bytes=12 * MIB),
         cost_estimate=QUICK,
     )(by_rank, in_hbm(out_proj.reshape(cols, width)), in_hbm(out_grads))
 
@@ -419,7 +441,7 @@
             ],
             in_specs=[VMEM] * 3,
             out_specs=[VMEM] * len(plan),
-            compiler_params=pltpu.CompilerParams(vmem_limit_bytes=24 * MIB),
+            compiler_params=pltpu.CompilerParams(vmem_limit_bytes=12 * MIB),
             cost_estimate=QUICK,
         )(in_vmem(held), head, in_vmem(held_grads))
 
@@ -427,106 +449,132 @@
         digits = block[count : count + 2, :edges].astype(jnp.int32)
         return (digits[0] * DIGIT + digits[1]).reshape(1, edges)
 
+    side_pieces = [swap(first_piece, 1, 0)]
     other_unit = swap(core_unit, 0, 1)
-    pieces = [
-        *first_pieces,
-        *permuted([(2, n * rows, rows) for n in range(2, PIECES)], [], other_unit),
-    ]
-
-    def send_piece(number):
-        return swap(pieces[number], 1, number // PIECES)
-
-    flying = [
-        [send_piece(0), swap(mine_unit, 0, CORES), onward(mine_unit)],
-        [send_piece(1), swap(core_unit, 0, CORES + 1), onward(core_unit, 1)],
-    ]
-    own_tokens, for_core = permuted([(0, 0, pairs), (1, 0, pairs)], [1], *pieces[2:])
-    pieces += permuted([(3, n * rows, rows) for n in range(PIECES)], [0], own_tokens)
-    from_core = swap(for_core, 0, 1)
-    local_segments, *_ = tie(segments, *pieces[PIECES:])
+    unit = pl.pallas_call(
+        join_kernel,
+        out_shape=pltpu.VMEM((CORES * cols, quarter), jnp.bfloat16),
+        in_specs=[VMEM] * 2,
+        out_specs=VMEM,
+        compiler_params=pltpu.CompilerParams(vmem_limit_bytes=4 * MIB),
+        cost_estimate=QUICK,
+    )(mine_unit, other_unit)
+    (second_piece,) = permuted([(2, 2 * rows, 2 * rows)], [], unit)
+    own_tokens, *for_core = permuted(
+        [(0, 0, pairs), (1, 0, 2 * rows), (1, 2 * rows, 2 * rows)], [1], second_piece
+    )
+    third_piece, last_piece = permuted(
+        [(3, 0, 3 * rows), (3, 3 * rows, rows)], [0], own_tokens
+    )
+    from_core = [swap(piece, 0, 1) for piece in for_core]
+    side_pieces.append(swap(second_piece, 1, 0))
+    diagonal_pieces = [swap(third_piece, 1, 1), swap(last_piece, 1, 1)]
+    local_segments, *_ = tie(segments, last_piece)
     basis, order_back = pl.pallas_call(
         basis_kernel,
         out_shape=[
             pltpu.VMEM((2 * tokens, SEG_DEV * 2 * rank), jnp.bfloat16),
             order_shape,
         ],
-        in_specs=[VMEM] * 4,
+        in_specs=[HBM, HBM, VMEM, VMEM],
         out_specs=[VMEM] * 2,
-        compiler_params=pltpu.CompilerParams(vmem_limit_bytes=16 * MIB),
+        scratch_shapes=[
+            pltpu.VMEM(hidden_in.shape, jnp.bfloat16),
+            pltpu.VMEM(in_proj.shape, jnp.bfloat16),
+            pltpu.SemaphoreType.DMA((5,)),
+        ],
+        compiler_params=pltpu.CompilerParams(vmem_limit_bytes=12 * MIB),
         cost_estimate=QUICK,
-    )(
-        hidden_in,
-        in_proj,
-        (local_segments - index * SEG_DEV).reshape(tokens, 1),
-        by_rank,
-    )
+    )(in_hbm(hidden_in), in_hbm(in_proj), local_segments.reshape(1, tokens), by_rank)
 
     call = functools.partial(
         accumulate, bases=bases, rank=rank, pairs=pairs, window=window, places=places
     )
-    steps = 2 * slots
-    core_step = min(4, steps - 1)
-    units = [(mine_unit, 0), (other_unit, 1)]
-    known_units = 0
-    members = [0]
-    starts = {0: own_starts}
-    state, sent = None, []
-    held = [own_tokens, basis, order_back]
-    for event in [[0, 1], *[[n] for n in range(2, steps)]]:
-        arrived, waiting = [], []
-        for step in event:
-            chain = step % 2
-            piece, across, ahead = flying[chain]
-            upcoming = [None, None, None]
-            if ahead is not None:
-                number = step + 2
-                if number < 2 * PIECES:
-                    pieces[number], piece, across, ahead, *held = tie(
-                        pieces[number], piece, across, ahead, *held
-                    )
-                    upcoming[0] = send_piece(number)
-                else:
-                    across, ahead, *held = tie(across, ahead, *held)
-                upcoming[1] = swap(ahead, 0, CORES)
-                if step + 4 < steps:
-                    upcoming[2] = onward(ahead)
-            flying[chain] = upcoming
-            units.append((across, known_units + len(units)))
-            if ahead is not None:
-                units.append((ahead, known_units + len(units)))
-            if piece is not None:
-                waiting.append((piece, step))
-        if state is None:
-            own_tokens, basis, order_back = held
-            arrived.append((own_tokens, 0, pairs))
+    place_of = {name: CORES * n for n, name in enumerate(arrival)}
+    held = {(0, 0): unit}
+    crossings = []
+    state = None
+
+    def cross(name):
+        held[name, 1] = swap(held[name, 0], 0, CORES)
+        crossings.append((name, 1))
+
+    held[1, 0] = along(unit, following)
+    cross(0)
+    if back:
+        held[-1, 0] = along(unit, before)
+    for name in landing[1:]:
+        final = name == landing[-1]
+        if final:
+            state, _ = call(
+                None,
+                starts={0: own_starts, 2: starts_in(side_pieces[0], 2 * rows)},
+                tokens=[
+                    (own_tokens, 0, pairs),
+                    (side_pieces[0], 2 * pairs, 2 * rows),
+                    (side_pieces[1], 2 * pairs + 2 * rows, 2 * rows),
+                ],
+                units=[(held[n], place_of[n]) for n in known_first],
+                tasks=[("units", [0, 2], 0, CORES * len(known_first))],
+                cost=SHORT,
+            )
+            old = crossings[-1:]
         else:
-            state = held
-        tasks = [("units", list(members), known_units, len(units))]
-        known_units += len(units)
-        if event[0] == core_step:
-            starts[1] = starts_in(from_core, pairs)
-            arrived.append((from_core, pairs, pairs))
-            tasks.append(("units", [1], 0, known_units))
-            members.append(1)
-        for piece, number in waiting:
-            g, part = 2 + number // PIECES, number % PIECES
-            arrived.append((piece, g * pairs + part * rows, rows))
-            if part == 0:
-                starts[g] = starts_in(piece, rows)
-                members.append(g)
-            tasks.append(("piece", g, part * rows, (part + 1) * rows, 0, known_units))
-        last = event[-1] + 1 == steps
-        state, out = call(
-            state,
-            starts=starts,
-            tokens=arrived,
-            units=units,
-            tasks=tasks,
-            sends=[1, 2, 3] if last else [],
-        )
-        sent += out
-        held = state
-        units = []
+            old = crossings[-2:-1]
+        if old and state is None:
+            side_pieces[0], *old_units = tie(side_pieces[0], *[held[n] for n in old])
+            held.update(zip(old, old_units))
+        tied = tie(held[name, 0], *[held[n] for n in old], *(state or []), basis, order_back)
+        held[name, 0], *tied = tied
+        for n in old:
+            held[n], *tied = tied
+        if state is not None:
+            state, tied = tied[:3], tied[3:]
+        basis, order_back = tied
+        cross(name)
+        if name > 0 and name < ahead:
+            held[name + 1, 0] = along(held[name, 0], following)
+        if name < 0 and -name < back:
+            held[name - 1, 0] = along(held[name, 0], before)
+
+    starts = {
+        0: own_starts,
+        1: starts_in(from_core[0], 2 * rows),
+        2: starts_in(side_pieces[0], 2 * rows),
+    }
+    first = CORES * len(known_first)
+    state, _ = call(
+        state,
+        starts=starts,
+        tokens=[
+            (from_core[0], pairs, 2 * rows),
+            (from_core[1], pairs + 2 * rows, 2 * rows),
+        ],
+        units=[(held[n], place_of[n]) for n in known_next],
+        tasks=[
+            ("units", [0, 2], first, CORES * len(known_next)),
+            ("units", [1], 0, first + CORES * len(known_next)),
+        ],
+    )
+    starts[3] = starts_in(diagonal_pieces[0], 3 * rows)
+    state, _ = call(
+        state,
+        starts=starts,
+        tokens=[(diagonal_pieces[0], 3 * pairs, 3 * rows)],
+        units=[],
+        tasks=[("piece", 3, 0, 3 * rows, 0, places - CORES)],
+    )
+    state, sent = call(
+        state,
+        starts=starts,
+        tokens=[(diagonal_pieces[1], 3 * pairs + 3 * rows, rows)],
+        units=[(held[arrival[-1]], places - CORES)],
+        tasks=[
+            ("units", [0, 1, 2, 3], places - CORES, CORES),
+            ("piece", 3, 3 * rows, 4 * rows, 0, places - CORES),
+        ],
+        sends=[1, 2, 3],
+    )
 
     from_core = swap(sent[0], 0, 1)
     from_side = swap(sent[1], 1, 0)

time: 97.6 us -> 88.4 us (0.906)
  the two profiles are of different devices: /device:TPU:1 before, /device:TPU:29 now
where the time goes in v7:
time: 88.4 us; the launch traced here: 88.2 us
  waiting for transfers between devices  40.3 us (46%)
  Pallas kernels  28.9 us (33%)
  starting transfers between devices  18.2 us (21%)
    ppermute x14, waiting for transfers between devices, swap(): return lax.ppermute(array, BOTH, table)  25.7 us
    ppermute x14, starting transfers between devices, swap(): return lax.ppermute(array, BOTH, table)  15.7 us
    pallas_call x4, Pallas kernels, accumulate(): pl.pallas_call(functools.partial(partial_kernel, rank, pairs, window, [(f...  15 us
    ppermute x3, waiting for transfers between devices, along(): return lax.ppermute(array, 'expert', pairs_of)  14.6 us
    pallas_call x3, Pallas kernels, permuted(): pl.pallas_call(functools.partial(permute_kernel, plan), out_shape=[rows_s...  4.34 us
    pallas_call x1, Pallas kernels, local(): pl.pallas_call(functools.partial(blocks_kernel, tops, rank), out_shape=ja...  3.45 us
    pallas_call x1, Pallas kernels, local(): pl.pallas_call(sort_kernel, out_shape=[pltpu.VMEM(out_grads.shape, jnp.bf...  3.26 us
    pallas_call x1, Pallas kernels, local(): pl.pallas_call(basis_kernel, out_shape=[pltpu.VMEM((2 * tokens, SEG_DEV *...  2.79 us
  transfers between devices with their start and end apart: 17, of which 6 were waited for; matrix products, arithmetic and copies ran while one was open for 0% of the time, Pallas kernels for 21%

profile of v7, /device:TPU:29, one launch (start us, length us, event | category | flops | bytes accessed | tf_op | source)
XLA Modules:
  0.0 88.2 jit_solution(3130151417869503189)
XLA Ops:
  0.0 0.7 copy-done.1
  0.7 3.3 %shard_map.73 = (bf16[128,8,2048]{2,1,0:T(8,128)(2,1)S(1)}, bf16[256,512]{1,0:T(8,128)(2,1)S(1)}, bf16[256,512]{1,0:T(8,128)(2,1)S(1)}, s32[1,128]{1,0:T(1,128)S...) custom-call(s32[8,128]{1,0:T(8,128)S(1)} %bitcast.3, ...), custom_call_target="tpu_custom_call" | custom-call | flops 1 | bytes 1 | tf_op jit(solution)/shard_map/pallas_call | solution.py:413
  4.0 0.7 collective-permute-start
  4.7 1.2 %collective-permute-start.4 = (bf16[528,512]{1,0:T(8,128)(2,1)S(1)}, bf16[528,512]{1,0:T(8,128)(2,1)S(1)}, u32[]{:S(2)}, u32[]{:S(2)}) collective-permute-start(bf16[528,512]{1,0:T(8,128)(2,1)S(1)} %get-tuple-element.66), channel_id=1, source_target_pairs={{0,16},{1,17},{2,18},{3,19},{4,20},{5,21},{6,22},{7,23},{8,24},{9,... | collective-permute-start | bytes 1622024 | tf_op jit(solution)/shard_map/ppermute | solution.py:370
  5.9 0.0 collective-permute-done.two_ref
  6.0 0.2 collective-permute-start.1
  6.2 0.2 collective-permute-start.5
  6.4 0.7 shard_map.75
  7.1 2.4 %shard_map.76 = (bf16[1024,512]{1,0:T(8,128)(2,1)S(1)}, bf16[528,512]{1,0:T(8,128)(2,1)S(1)}, bf16[512,512]{1,0:T(8,128)(2,1)S(1)}) custom-call(bf16[1024,1024]{1,0:T(8,128)(2,1)S(1)} %get-tuple-element.60.order_ref, bf16[16,512]{1,0:T(8,128)(2,1)S(1)} %get-tuple-element.56.head_ref, bf16[128,8,2048]{2,1,0:T(8,128)(2,1)S(1)} %get-tuple-element.57.grads_ref), custom_call_target="tpu_custom_call" | custom-call | flops 1 | bytes 1 | tf_op jit(solution)/shard_map/pallas_call | solution.py:436
  9.5 0.0 copy-start.2
  9.5 0.0 copy-start.3
  9.5 1.0 %collective-permute-start.9 = (bf16[528,512]{1,0:T(8,128)(2,1)S(1)}, bf16[528,512]{1,0:T(8,128)(2,1)S(1)}, u32[]{:S(2)}, u32[]{:S(2)}) collective-permute-start(bf16[528,512]{1,0:T(8,128)(2,1)S(1)} %get-tuple-element.81), channel_id=1, source_target_pairs={{0,1},{1,0},{2,3},{3,2},{4,5},{5,4},{6,7},{7,6},{8,9},{9,8},{10,11... | collective-permute-start | bytes 1622024 | tf_op jit(solution)/shard_map/ppermute | solution.py:370
  10.5 2.2 %collective-permute-start.3 = (bf16[512,512]{1,0:T(8,128)(2,1)S(1)}, bf16[512,512]{1,0:T(8,128)(2,1)S(1)}, u32[]{:S(2)}, u32[]{:S(2)}) collective-permute-start(bf16[512,512]{1,0:T(8,128)(2,1)S(1)} %shard_map.74.refs_5_), channel_id=1, source_target_pairs={{0,8},{1,9},{2,10},{3,11},{4,0},{5,1},{6,2},{7,3},{8,12},{9,13},{1... | collective-permute-start | bytes 1572872 | tf_op jit(solution)/shard_map/ppermute | solution.py:375
  12.7 1.3 %shard_map.77 = (bf16[784,512]{1,0:T(8,128)(2,1)S(1)}, bf16[256,512]{1,0:T(8,128)(2,1)S(1)}) custom-call(bf16[1024,1024]{1,0:T(8,128)(2,1)S(1)} %get-tuple-element.60.order_ref, bf16[16,512]{1,0:T(8,128)(2,1)S(1)} %get-tuple-element.56.head_ref, bf16[128,8,2048]{2,1,0:T(8,128)(2,1)S(1)} %get-tuple-element.57.grads_ref), custom_call_target="tpu_custom_call" | custom-call | flops 1 | bytes 1 | tf_op jit(solution)/shard_map/pallas_call | solution.py:436
  14.0 0.0 copy-done.2
  14.0 2.8 %shard_map.78 = (bf16[256,256]{1,0:T(8,128)(2,1)S(1)}, bf16[1024,1024]{1,0:T(8,128)(2,1)S(1)}) custom-call(bf16[128,7168]{1,0:T(8,128)(2,1)} %hidden_ref.1, bf16[64,7168]{1,0:T(8,128)(2,1)} %proj_ref.1, s32[1,128]{1,0:T(1,128)S(1)} %bitcast.6, s32[8,128]{1,0:T(8,128)S(1)} %bitcast.4), custom_call_target="tpu_custom_call" | custom-call | flops 1 | bytes 1 | tf_op jit(solution)/shard_map/pallas_call | solution.py:473
  16.8 14.6 %collective-permute-done.1.refs_6_ = bf16[512,512]{1,0:T(8,128)(2,1)S(1)} collective-permute-done((bf16[512,512]{1,0:T(8,128)(2,1)S(1)}, bf16[512,512]{1,0:T(8,128)(2,1)S(1)}, u32[]{:S(2)}, u32[]{:S(2)}) %collective-permute-start.1) | collective-permute-done | bytes 524320 | tf_op jit(solution)/shard_map/ppermute | solution.py:375
  31.4 1.1 %collective-permute-start.7 = (bf16[512,512]{1,0:T(8,128)(2,1)S(1)}, bf16[512,512]{1,0:T(8,128)(2,1)S(1)}, u32[]{:S(2)}, u32[]{:S(2)}) collective-permute-start(bf16[512,512]{1,0:T(8,128)(2,1)S(1)} %shard_map.75), channel_id=1, source_target_pairs={{0,16},{1,17},{2,18},{3,19},{4,20},{5,21},{6,22},{7,23},{8,24},{9,... | collective-permute-start | bytes 1572872 | tf_op jit(solution)/shard_map/ppermute | solution.py:370
  32.5 0.0 collective-permute-done.4.refs_3_
  32.5 1.7 %collective-permute-start.10 = (bf16[784,512]{1,0:T(8,128)(2,1)S(1)}, bf16[784,512]{1,0:T(8,128)(2,1)S(1)}, u32[]{:S(2)}, u32[]{:S(2)}) collective-permute-start(bf16[784,512]{1,0:T(8,128)(2,1)S(1)} %get-tuple-element.82), channel_id=1, source_target_pairs={{0,17},{1,16},{2,19},{3,18},{4,21},{5,20},{6,23},{7,22},{8,25},{9,... | collective-permute-start | bytes 2408456 | tf_op jit(solution)/shard_map/ppermute | solution.py:370
  34.2 0.0 collective-permute-done.5.refs_8_
  34.2 0.2 collective-permute-start.8
  34.4 0.0 collective-permute-done.3.refs_7_
  34.4 0.0 collective-permute-start.2
  34.4 0.0 collective-permute-done.9.refs_3_
  34.4 1.3 %collective-permute-start.6 = (bf16[512,512]{1,0:T(8,128)(2,1)S(1)}, bf16[512,512]{1,0:T(8,128)(2,1)S(1)}, u32[]{:S(2)}, u32[]{:S(2)}) collective-permute-start(bf16[512,512]{1,0:T(8,128)(2,1)S(1)} %collective-permute-done.3.refs_7_), channel_id=1, source_target_pairs={{0,2},{1,3},{2,0},{3,1},{4,6},{5,7},{6,4},{7,5},{8,10},{9,11},{10,... | collective-permute-start | bytes 1572872 | tf_op jit(solution)/shard_map/ppermute | solution.py:370
  35.7 7.9 %collective-permute-done.7.refs_4_ = bf16[512,512]{1,0:T(8,128)(2,1)S(1)} collective-permute-done((bf16[512,512]{1,0:T(8,128)(2,1)S(1)}, bf16[512,512]{1,0:T(8,128)(2,1)S(1)}, u32[]{:S(2)}, u32[]{:S(2)}) %collective-permute-start.7) | collective-permute-done | bytes 524320 | tf_op jit(solution)/shard_map/ppermute | solution.py:370
  43.6 4.8 %collective-permute-start.11 = (bf16[256,512]{1,0:T(8,128)(2,1)S(1)}, bf16[256,512]{1,0:T(8,128)(2,1)S(1)}, u32[]{:S(2)}, u32[]{:S(2)}) collective-permute-start(bf16[256,512]{1,0:T(8,128)(2,1)S(1)} %get-tuple-element.61), channel_id=1, source_target_pairs={{0,17},{1,16},{2,19},{3,18},{4,21},{5,20},{6,23},{7,22},{8,25},{9,... | collective-permute-start | bytes 786440 | tf_op jit(solution)/shard_map/ppermute | solution.py:370
  48.4 0.0 collective-permute-done.8.refs_9_
  48.4 0.4 collective-permute-start.13
  48.8 3.7 %shard_map.79 = (bf16[4096,512]{1,0:T(8,128)(2,1)S(1)}, bf16[16,256,512]{2,1,0:T(8,128)(2,1)S(1)}, f32[4096,128]{1,0:T(8,128)S(1)}) custom-call(s32[16,16]{1,0:T(8,128)S(1)} %copy-done, s32[1,128]{1,0:T(1,128)S(1)} %get-tuple-element.71.refs_0_, s32[1,128]{1,0:T(1,128)S(1)} %slice_add_fusion.2.refs_1_.refs_2_, ...), custom_call_target="tpu_custom_call" | custom-call | flops 1000000000 | bytes 1 | tf_op jit(solution)/shard_map/pallas_call | solution.py:287
  52.5 6.5 %collective-permute-done.6.refs_6_ = bf16[512,512]{1,0:T(8,128)(2,1)S(1)} collective-permute-done((bf16[512,512]{1,0:T(8,128)(2,1)S(1)}, bf16[512,512]{1,0:T(8,128)(2,1)S(1)}, u32[]{:S(2)}, u32[]{:S(2)}) %collective-permute-start.6) | collective-permute-done | bytes 524320 | tf_op jit(solution)/shard_map/ppermute | solution.py:370
  59.0 0.0 collective-permute-done.2.refs_5_
  59.0 0.2 collective-permute-start.12
  59.3 4.9 %collective-permute-done.10.refs_4_ = bf16[784,512]{1,0:T(8,128)(2,1)S(1)} collective-permute-done((bf16[784,512]{1,0:T(8,128)(2,1)S(1)}, bf16[784,512]{1,0:T(8,128)(2,1)S(1)}, u32[]{:S(2)}, u32[]{:S(2)}) %collective-permute-start.10) | collective-permute-done | bytes 802848 | tf_op jit(solution)/shard_map/ppermute | solution.py:370
  64.2 0.0 collective-permute-done.13.refs_4_
  64.2 4.9 %shard_map.80 = (bf16[4096,512]{1,0:T(8,128)(2,1)S(1)}, bf16[16,256,512]{2,1,0:T(8,128)(2,1)S(1)}, f32[4096,128]{1,0:T(8,128)S(1)}) custom-call(s32[16,16]{1,0:T(8,128)S(1)} %copy-done, s32[1,128]{1,0:T(1,128)S(1)} %get-tuple-element.71.refs_0_, s32[1,128]{1,0:T(1,128)S(1)} %slice_add_fusion.1.refs_1_, ...), custom_call_target="tpu_custom_call", output_to_operand_aliasing={{0}: (8, {}), {1}: (9, {}), {2}: (10, {})} | custom-call | flops 1 | bytes 1 | tf_op jit(solution)/shard_map/pallas_call | solution.py:287
  69.1 3.2 %shard_map.81 = (bf16[4096,512]{1,0:T(8,128)(2,1)S(1)}, bf16[16,256,512]{2,1,0:T(8,128)(2,1)S(1)}, f32[4096,128]{1,0:T(8,128)S(1)}) custom-call(s32[16,16]{1,0:T(8,128)S(1)} %copy-done, s32[1,128]{1,0:T(1,128)S(1)} %get-tuple-element.71.refs_0_, s32[1,128]{1,0:T(1,128)S(1)} %slice_add_fusion.1.refs_1_, ...), custom_call_target="tpu_custom_call", output_to_operand_aliasing={{0}: (6, {}), {1}: (7, {}), {2}: (8, {})} | custom-call | flops 1 | bytes 1 | tf_op jit(solution)/shard_map/pallas_call | solution.py:287
  72.3 0.0 collective-permute-done.11.refs_4_
  72.3 0.0 collective-permute-done.12.refs_5_
  72.4 3.2 %shard_map.82 = (bf16[4096,512]{1,0:T(8,128)(2,1)S(1)}, bf16[16,256,512]{2,1,0:T(8,128)(2,1)S(1)}, f32[4096,128]{1,0:T(8,128)S(1)}, bf16[512,128]{1,0:T(8,128)(2...) custom-call(s32[16,16]{1,0:T(8,128)S(1)} %copy-done, ...), custom_call_target="tpu_custom_call", output_to_operand_aliasing={{0}: (7, {}), {1}: (8, {}), {2}: (9, {})} | custom-call | flops 1 | bytes 1 | tf_op jit(solution)/shard_map/pallas_call | solution.py:287
  75.6 1.1 %collective-permute-start.14 = (bf16[512,128]{1,0:T(8,128)(2,1)S(1)}, bf16[512,128]{1,0:T(8,128)(2,1)S(1)}, u32[]{:S(2)}, u32[]{:S(2)}) collective-permute-start(bf16[512,128]{1,0:T(8,128)(2,1)S(1)} %get-tuple-element.96), channel_id=1, source_target_pairs={{0,1},{1,0},{2,3},{3,2},{4,5},{5,4},{6,7},{7,6},{8,9},{9,8},{10,11... | collective-permute-start | bytes 393224 | tf_op jit(solution)/shard_map/ppermute | solution.py:370
  76.7 0.8 collective-permute-start.15
  77.4 0.9 %collective-permute-start.16 = (bf16[512,128]{1,0:T(8,128)(2,1)S(1)}, bf16[512,128]{1,0:T(8,128)(2,1)S(1)}, u32[]{:S(2)}, u32[]{:S(2)}) collective-permute-start(bf16[512,128]{1,0:T(8,128)(2,1)S(1)} %get-tuple-element.98), channel_id=1, source_target_pairs={{0,17},{1,16},{2,19},{3,18},{4,21},{5,20},{6,23},{7,22},{8,25},{9,... | collective-permute-start | bytes 393224 | tf_op jit(solution)/shard_map/ppermute | solution.py:370
  78.4 0.0 collective-permute-done.14.b_ref
  78.4 3.4 %collective-permute-done.15.c_ref = bf16[512,128]{1,0:T(8,128)(2,1)S(1)} collective-permute-done((bf16[512,128]{1,0:T(8,128)(2,1)S(1)}, bf16[512,128]{1,0:T(8,128)(2,1)S(1)}, u32[]{:S(2)}, u32[]{:S(2)}) %collective-permute-start.15) | collective-permute-done | bytes 131104 | tf_op jit(solution)/shard_map/ppermute | solution.py:370
  81.8 3.0 %collective-permute-done.16.d_ref = bf16[512,128]{1,0:T(8,128)(2,1)S(1)} collective-permute-done((bf16[512,128]{1,0:T(8,128)(2,1)S(1)}, bf16[512,128]{1,0:T(8,128)(2,1)S(1)}, u32[]{:S(2)}, u32[]{:S(2)}) %collective-permute-start.16) | collective-permute-done | bytes 131104 | tf_op jit(solution)/shard_map/ppermute | solution.py:370
  84.7 3.5 %shard_map.83 = bf16[2,64,4096]{2,1,0:T(8,128)(2,1)} custom-call(s32[8,128]{1,0:T(8,128)S(1)} %bitcast.5, bf16[256,256]{1,0:T(8,128)(2,1)S(1)} %get-tuple-element.79.basis_ref, bf16[1024,1024]{1,0:T(8,128)(2,1)S(1)} %get-tuple-element.80.order_ref, f32[4096,128]{1,0:T(8,128)S(1)} %get-tuple-element.95.total_ref, ...), custom_call_target="tpu_custom_call" | custom-call | flops 1 | bytes 1 | tf_op jit(solution)/shard_map/pallas_call | solution.py:582
  (11 shorter events, 0.1 us)
Async XLA Ops:
  0.0 0.7 copy-start.1
  4.0 2.0 %collective-permute-start = (bf16[256,512]{1,0:T(8,128)(2,1)S(1)}, bf16[256,512]{1,0:T(8,128)(2,1)S(1)}, u32[]{:S(2)}, u32[]{:S(2)}) collective-permute-start(bf16[256,512]{1,0:T(8,128)(2,1)S(1)} %get-tuple-element.53), channel_id=1, source_target_pairs={{0,1},{1,0},{2,3},{3,2},{4,5},{5,4},{6,7},{7,6},{8,9},{9,8},{10,11... | collective-permute-start | bytes 786440 | tf_op jit(solution)/shard_map/ppermute | solution.py:370
  4.7 27.8 %collective-permute-start.4 = (bf16[528,512]{1,0:T(8,128)(2,1)S(1)}, bf16[528,512]{1,0:T(8,128)(2,1)S(1)}, u32[]{:S(2)}, u32[]{:S(2)}) collective-permute-start(bf16[528,512]{1,0:T(8,128)(2,1)S(1)} %get-tuple-element.66), channel_id=1, source_target_pairs={{0,16},{1,17},{2,18},{3,19},{4,20},{5,21},{6,22},{7,23},{8,24},{9,... | collective-permute-start | bytes 1622024 | tf_op jit(solution)/shard_map/ppermute | solution.py:370
  6.0 25.4 %collective-permute-start.1 = (bf16[512,512]{1,0:T(8,128)(2,1)S(1)}, bf16[512,512]{1,0:T(8,128)(2,1)S(1)}, u32[]{:S(2)}, u32[]{:S(2)}) collective-permute-start(bf16[512,512]{1,0:T(8,128)(2,1)S(1)} %shard_map.74.refs_5_), channel_id=1, source_target_pairs={{0,4},{1,5},{2,6},{3,7},{4,12},{5,13},{6,14},{7,15},{8,0},{9,1},{1... | collective-permute-start | bytes 1572872 | tf_op jit(solution)/shard_map/ppermute | solution.py:375
  6.2 28.0 %collective-permute-start.5 = (bf16[512,512]{1,0:T(8,128)(2,1)S(1)}, bf16[512,512]{1,0:T(8,128)(2,1)S(1)}, u32[]{:S(2)}, u32[]{:S(2)}) collective-permute-start(bf16[512,512]{1,0:T(8,128)(2,1)S(1)} %shard_map.74.refs_5_), channel_id=1, source_target_pairs={{0,2},{1,3},{2,0},{3,1},{4,6},{5,7},{6,4},{7,5},{8,10},{9,11},{10,... | collective-permute-start | bytes 1572872 | tf_op jit(solution)/shard_map/ppermute | solution.py:370
  9.5 4.5 %copy-start.2 = (s32[128,8]{0,1:T(8,128)S(1)}, s32[128,8]{0,1:T(8,128)}, u32[]{:S(2)}) copy-start(s32[128,8]{0,1:T(8,128)} %param.9) | copy-start | bytes 12292
  9.5 4.5 %copy-start.3 = (s32[128]{0:T(128)S(1)}, s32[128]{0:T(128)}, u32[]{:S(2)}) copy-start(s32[128]{0:T(128)} %param.10) | copy-start | bytes 1540
  9.5 24.9 %collective-permute-start.9 = (bf16[528,512]{1,0:T(8,128)(2,1)S(1)}, bf16[528,512]{1,0:T(8,128)(2,1)S(1)}, u32[]{:S(2)}, u32[]{:S(2)}) collective-permute-start(bf16[528,512]{1,0:T(8,128)(2,1)S(1)} %get-tuple-element.81), channel_id=1, source_target_pairs={{0,1},{1,0},{2,3},{3,2},{4,5},{5,4},{6,7},{7,6},{8,9},{9,8},{10,11... | collective-permute-start | bytes 1622024 | tf_op jit(solution)/shard_map/ppermute | solution.py:370
  10.5 23.9 %collective-permute-start.3 = (bf16[512,512]{1,0:T(8,128)(2,1)S(1)}, bf16[512,512]{1,0:T(8,128)(2,1)S(1)}, u32[]{:S(2)}, u32[]{:S(2)}) collective-permute-start(bf16[512,512]{1,0:T(8,128)(2,1)S(1)} %shard_map.74.refs_5_), channel_id=1, source_target_pairs={{0,8},{1,9},{2,10},{3,11},{4,0},{5,1},{6,2},{7,3},{8,12},{9,13},{1... | collective-permute-start | bytes 1572872 | tf_op jit(solution)/shard_map/ppermute | solution.py:375
  12.7 36.1 %copy-start = (s32[16,16]{1,0:T(8,128)S(1)}, s32[16,16]{1,0:T(8,128)}, u32[]{:S(2)}) copy-start(s32[16,16]{1,0:T(8,128)} %constant.4.clone.bases_ref) | copy-start | bytes 3076
  31.4 12.2 %collective-permute-start.7 = (bf16[512,512]{1,0:T(8,128)(2,1)S(1)}, bf16[512,512]{1,0:T(8,128)(2,1)S(1)}, u32[]{:S(2)}, u32[]{:S(2)}) collective-permute-start(bf16[512,512]{1,0:T(8,128)(2,1)S(1)} %shard_map.75), channel_id=1, source_target_pairs={{0,16},{1,17},{2,18},{3,19},{4,20},{5,21},{6,22},{7,23},{8,24},{9,... | collective-permute-start | bytes 1572872 | tf_op jit(solution)/shard_map/ppermute | solution.py:370
  32.5 31.7 %collective-permute-start.10 = (bf16[784,512]{1,0:T(8,128)(2,1)S(1)}, bf16[784,512]{1,0:T(8,128)(2,1)S(1)}, u32[]{:S(2)}, u32[]{:S(2)}) collective-permute-start(bf16[784,512]{1,0:T(8,128)(2,1)S(1)} %get-tuple-element.82), channel_id=1, source_target_pairs={{0,17},{1,16},{2,19},{3,18},{4,21},{5,20},{6,23},{7,22},{8,25},{9,... | collective-permute-start | bytes 2408456 | tf_op jit(solution)/shard_map/ppermute | solution.py:370
  34.2 14.3 %collective-permute-start.8 = (bf16[512,512]{1,0:T(8,128)(2,1)S(1)}, bf16[512,512]{1,0:T(8,128)(2,1)S(1)}, u32[]{:S(2)}, u32[]{:S(2)}) collective-permute-start(bf16[512,512]{1,0:T(8,128)(2,1)S(1)} %collective-permute-done.1.refs_6_), channel_id=1, source_target_pairs={{0,2},{1,3},{2,0},{3,1},{4,6},{5,7},{6,4},{7,5},{8,10},{9,11},{10,... | collective-permute-start | bytes 1572872 | tf_op jit(solution)/shard_map/ppermute | solution.py:370
  34.4 24.6 %collective-permute-start.2 = (bf16[512,512]{1,0:T(8,128)(2,1)S(1)}, bf16[512,512]{1,0:T(8,128)(2,1)S(1)}, u32[]{:S(2)}, u32[]{:S(2)}) collective-permute-start(bf16[512,512]{1,0:T(8,128)(2,1)S(1)} %collective-permute-done.1.refs_6_), channel_id=1, source_target_pairs={{0,4},{1,5},{2,6},{3,7},{4,12},{5,13},{6,14},{7,15},{8,0},{9,1},{1... | collective-permute-start | bytes 1572872 | tf_op jit(solution)/shard_map/ppermute | solution.py:375
  34.4 24.6 %collective-permute-start.6 = (bf16[512,512]{1,0:T(8,128)(2,1)S(1)}, bf16[512,512]{1,0:T(8,128)(2,1)S(1)}, u32[]{:S(2)}, u32[]{:S(2)}) collective-permute-start(bf16[512,512]{1,0:T(8,128)(2,1)S(1)} %collective-permute-done.3.refs_7_), channel_id=1, source_target_pairs={{0,2},{1,3},{2,0},{3,1},{4,6},{5,7},{6,4},{7,5},{8,10},{9,11},{10,... | collective-permute-start | bytes 1572872 | tf_op jit(solution)/shard_map/ppermute | solution.py:370
  43.6 28.7 %collective-permute-start.11 = (bf16[256,512]{1,0:T(8,128)(2,1)S(1)}, bf16[256,512]{1,0:T(8,128)(2,1)S(1)}, u32[]{:S(2)}, u32[]{:S(2)}) collective-permute-start(bf16[256,512]{1,0:T(8,128)(2,1)S(1)} %get-tuple-element.61), channel_id=1, source_target_pairs={{0,17},{1,16},{2,19},{3,18},{4,21},{5,20},{6,23},{7,22},{8,25},{9,... | collective-permute-start | bytes 786440 | tf_op jit(solution)/shard_map/ppermute | solution.py:370
  48.4 15.8 %collective-permute-start.13 = (bf16[512,512]{1,0:T(8,128)(2,1)S(1)}, bf16[512,512]{1,0:T(8,128)(2,1)S(1)}, u32[]{:S(2)}, u32[]{:S(2)}) collective-permute-start(bf16[512,512]{1,0:T(8,128)(2,1)S(1)} %get-tuple-element.84), channel_id=1, source_target_pairs={{0,1},{1,0},{2,3},{3,2},{4,5},{5,4},{6,7},{7,6},{8,9},{9,8},{10,11... | collective-permute-start | bytes 1572872 | tf_op jit(solution)/shard_map/ppermute | solution.py:370
  59.0 13.3 %collective-permute-start.12 = (bf16[512,512]{1,0:T(8,128)(2,1)S(1)}, bf16[512,512]{1,0:T(8,128)(2,1)S(1)}, u32[]{:S(2)}, u32[]{:S(2)}) collective-permute-start(bf16[512,512]{1,0:T(8,128)(2,1)S(1)} %collective-permute-done.2.refs_5_), channel_id=1, source_target_pairs={{0,2},{1,3},{2,0},{3,1},{4,6},{5,7},{6,4},{7,5},{8,10},{9,11},{10,... | collective-permute-start | bytes 1572872 | tf_op jit(solution)/shard_map/ppermute | solution.py:370
  75.6 2.8 %collective-permute-start.14 = (bf16[512,128]{1,0:T(8,128)(2,1)S(1)}, bf16[512,128]{1,0:T(8,128)(2,1)S(1)}, u32[]{:S(2)}, u32[]{:S(2)}) collective-permute-start(bf16[512,128]{1,0:T(8,128)(2,1)S(1)} %get-tuple-element.96), channel_id=1, source_target_pairs={{0,1},{1,0},{2,3},{3,2},{4,5},{5,4},{6,7},{7,6},{8,9},{9,8},{10,11... | collective-permute-start | bytes 393224 | tf_op jit(solution)/shard_map/ppermute | solution.py:370
  76.7 5.1 %collective-permute-start.15 = (bf16[512,128]{1,0:T(8,128)(2,1)S(1)}, bf16[512,128]{1,0:T(8,128)(2,1)S(1)}, u32[]{:S(2)}, u32[]{:S(2)}) collective-permute-start(bf16[512,128]{1,0:T(8,128)(2,1)S(1)} %get-tuple-element.97), channel_id=1, source_target_pairs={{0,16},{1,17},{2,18},{3,19},{4,20},{5,21},{6,22},{7,23},{8,24},{9,... | collective-permute-start | bytes 393224 | tf_op jit(solution)/shard_map/ppermute | solution.py:370
  77.4 7.3 %collective-permute-start.16 = (bf16[512,128]{1,0:T(8,128)(2,1)S(1)}, bf16[512,128]{1,0:T(8,128)(2,1)S(1)}, u32[]{:S(2)}, u32[]{:S(2)}) collective-permute-start(bf16[512,128]{1,0:T(8,128)(2,1)S(1)} %get-tuple-element.98), channel_id=1, source_target_pairs={{0,17},{1,16},{2,19},{3,18},{4,21},{5,20},{6,23},{7,22},{8,25},{9,... | collective-permute-start | bytes 393224 | tf_op jit(solution)/shard_map/ppermute | solution.py:370

commit v8 on v7

--- a/solution.py
+++ b/solution.py
@@ -72,22 +72,18 @@
 
 def sort_kernel(
     routes_ref,
-    weight_ref,
     grads_ref,
     held_ref,
-    mine_ref,
-    core_ref,
     starts_ref,
     head_ref,
     order_ref,
     piece_ref,
-    stage,
     sems,
 ):
-    width = mine_ref.shape[1]
-    count = sems.shape[0] - 1
+    width = piece_ref.shape[1]
+    count = sems.shape[0]
     part = grads_ref.shape[0] // count
-    copies = [pltpu.make_async_copy(weight_ref, stage, sems.at[count])]
+    copies = []
     for n in range(count):
         here = pl.ds(n * part, part)
         copies.append(pltpu.make_async_copy(grads_ref.at[here], held_ref.at[here], sems.at[n]))
@@ -111,10 +107,7 @@
     for first in range(0, pairs, rows):
         ids = first + lax.broadcasted_iota(jnp.int32, (rows, pairs), 0)
         order_ref[first : first + rows, :] = jnp.where(place == ids, 1.0, 0.0).astype(jnp.bfloat16)
-    copies[0].wait()
-    mine_ref[...] = stage[:, columns_of(0, width)]
-    core_ref[...] = stage[:, columns_of(1, width)]
-    for copy in copies[1:]:
+    for copy in copies:
         copy.wait()
     piece_ref[0:rows, :] = jnp.dot(
         order_ref[0:rows, :],
@@ -122,6 +115,24 @@
         preferred_element_type=jnp.float32,
     ).astype(jnp.bfloat16)
     piece_ref[rows:, :] = head_ref[...]
+
+
+def weights_kernel(weight_ref, mine_ref, core_ref, stage, sems):
+    rows, width = mine_ref.shape
+    count = sems.shape[0]
+    part = rows // count
+    copies = [
+        pltpu.make_async_copy(
+            weight_ref.at[pl.ds(n * part, part)], stage.at[pl.ds(n * part, part)], sems.at[n]
+        )
+        for n in range(count)
+    ]
+    for copy in copies:
+        copy.start()
+    for copy in copies:
+        copy.wait()
+    core_ref[...] = stage[:, columns_of(1, width)]
+    mine_ref[...] = stage[:, columns_of(0, width)]
 
 
 def join_kernel(one_ref, two_ref, out_ref):
@@ -377,29 +388,25 @@
     def tie(*arrays):
         return lax.optimization_barrier(arrays)
 
-    ahead, back = slots // 2, (slots - 1) // 2
-    landing = [0]
-    for n in range(1, ahead + 1):
-        landing += [n] + ([-n] if n <= back else [])
-    known_first = [(n, 0) for n in landing[:-1]] + [(n, 1) for n in landing[:-2]]
-    known_next = [(landing[-1], 0), (landing[-2], 1)]
-    arrival = known_first + known_next + [(landing[-1], 1)]
-
-    def source(z, n):
-        for _ in range(abs(n)):
-            z = before[z] if n > 0 else following[z]
+    final = slots - 1
+    first_names = [(n, 0) for n in range(final)] + [(n, 1) for n in range(final - 1)]
+    next_names = [(final, 0), (final - 1, 1)]
+    arrival = first_names + next_names + [(final, 1)]
+
+    def source(z, hops):
+        for _ in range(hops):
+            z = before[z]
         return z
 
     rows_of = [
         [
-            ((source(e // (2 * CORES), n) * 2 + (e // CORES % 2 ^ crossed)) * CORES + (e % CORES ^ flip))
-            * exp_here
-            for n, crossed in arrival
-            for flip in (0, 1)
+            ((source(e // (2 * CORES), n) * 2 + (e // CORES % 2 ^ y)) * CORES + (e % CORES ^ c)) * exp_here
+            for n, y in arrival
+            for c in range(CORES)
         ]
         for e in range(owners)
     ]
-    places = len(rows_of[0])
+    places = CORES * len(arrival)
     bases = jnp.asarray(np.array(rows_of, np.int32))
 
     unit_shape = pltpu.VMEM((cols, quarter), jnp.bfloat16)
@@ -408,28 +415,43 @@
     def rows_shape(count):
         return pltpu.VMEM((count, quarter), jnp.bfloat16)
 
-    by_rank = routes.T
+    mine_unit, core_unit = pl.pallas_call(
+        weights_kernel,
+        out_shape=[unit_shape, unit_shape],
+        in_specs=[HBM],
+        out_specs=[VMEM] * 2,
+        scratch_shapes=[pltpu.VMEM((cols, width), jnp.bfloat16), pltpu.SemaphoreType.DMA((4,))],
+        compiler_params=pltpu.CompilerParams(vmem_limit_bytes=8 * MIB),
+        cost_estimate=QUICK,
+    )(in_hbm(out_proj.reshape(cols, width)))
+    other_unit = swap(core_unit, 0, 1)
+    unit = pl.pallas_call(
+        join_kernel,
+        out_shape=pltpu.VMEM((CORES * cols, quarter), jnp.bfloat16),
+        in_specs=[VMEM] * 2,
+        out_specs=VMEM,
+        compiler_params=pltpu.CompilerParams(vmem_limit_bytes=4 * MIB),
+        cost_estimate=QUICK,
+    )(mine_unit, other_unit)
+    held = {(0, 0): unit, (1, 0): along(unit, following), (0, 1): swap(unit, 0, CORES)}
+
+    by_rank, _ = tie(routes.T, unit)
     edges = -(-(experts + 1) // LANES) * LANES
-    held_grads, mine_unit, core_unit, own_starts, head, order, first_piece = pl.pallas_call(
+    held_grads, own_starts, head, order, first_piece = pl.pallas_call(
         sort_kernel,
         out_shape=[
             pltpu.VMEM(out_grads.shape, jnp.bfloat16),
-            unit_shape,
-            unit_shape,
             jax.ShapeDtypeStruct((1, edges), jnp.int32),
             rows_shape(ALIGN),
             order_shape,
             rows_shape(2 * rows + ALIGN),
         ],
-        in_specs=[VMEM, HBM, HBM],
-        out_specs=[VMEM] * 7,
-        scratch_shapes=[
-            pltpu.VMEM((cols, width), jnp.bfloat16),
-            pltpu.SemaphoreType.DMA((9,)),
-        ],
+        in_specs=[VMEM, HBM],
+        out_specs=[VMEM] * 5,
+        scratch_shapes=[pltpu.SemaphoreType.DMA((8,))],
         compiler_params=pltpu.CompilerParams(vmem_limit_bytes=12 * MIB),
         cost_estimate=QUICK,
-    )(by_rank, in_hbm(out_proj.reshape(cols, width)), in_hbm(out_grads))
+    )(by_rank, in_hbm(out_grads))
 
     def permuted(plan, headed, *after):
         held, *_ = tie(order, *after)
@@ -450,16 +472,7 @@
         return (digits[0] * DIGIT + digits[1]).reshape(1, edges)
 
     side_pieces = [swap(first_piece, 1, 0)]
-    other_unit = swap(core_unit, 0, 1)
-    unit = pl.pallas_call(
-        join_kernel,
-        out_shape=pltpu.VMEM((CORES * cols, quarter), jnp.bfloat16),
-        in_specs=[VMEM] * 2,
-        out_specs=VMEM,
-        compiler_params=pltpu.CompilerParams(vmem_limit_bytes=4 * MIB),
-        cost_estimate=QUICK,
-    )(mine_unit, other_unit)
-    (second_piece,) = permuted([(2, 2 * rows, 2 * rows)], [], unit)
+    (second_piece,) = permuted([(2, 2 * rows, 2 * rows)], [])
     own_tokens, *for_core = permuted(
         [(0, 0, pairs), (1, 0, 2 * rows), (1, 2 * rows, 2 * rows)], [1], second_piece
     )
@@ -491,90 +504,64 @@
         accumulate, bases=bases, rank=rank, pairs=pairs, window=window, places=places
     )
     place_of = {name: CORES * n for n, name in enumerate(arrival)}
-    held = {(0, 0): unit}
-    crossings = []
+    starts = {0: own_starts}
+    members = []
+    known_units = 0
     state = None
 
-    def cross(name):
-        held[name, 1] = swap(held[name, 0], 0, CORES)
-        crossings.append((name, 1))
-
-    held[1, 0] = along(unit, following)
-    cross(0)
-    if back:
-        held[-1, 0] = along(unit, before)
-    for name in landing[1:]:
-        final = name == landing[-1]
-        if final:
-            state, _ = call(
-                None,
-                starts={0: own_starts, 2: starts_in(side_pieces[0], 2 * rows)},
-                tokens=[
-                    (own_tokens, 0, pairs),
-                    (side_pieces[0], 2 * pairs, 2 * rows),
-                    (side_pieces[1], 2 * pairs + 2 * rows, 2 * rows),
-                ],
-                units=[(held[n], place_of[n]) for n in known_first],
-                tasks=[("units", [0, 2], 0, CORES * len(known_first))],
-                cost=SHORT,
+    def work(names, tokens, sends=(), cost=QUICK):
+        nonlocal state, known_units
+        tasks, arrived = [], []
+        if names and members:
+            tasks.append(("units", list(members), known_units, CORES * len(names)))
+        known_units += CORES * len(names)
+        for group, piece, first, count in tokens:
+            arrived.append((piece, group * pairs + first, count))
+            if first == 0:
+                members.append(group)
+                if group:
+                    starts[group] = starts_in(piece, count)
+            if count == pairs:
+                tasks.append(("units", [group], 0, known_units))
+            else:
+                tasks.append(("piece", group, first, first + count, 0, known_units))
+        state, out = call(
+            state,
+            starts=starts,
+            tokens=arrived,
+            units=[(held[n], place_of[n]) for n in names],
+            tasks=tasks,
+            sends=sends,
+            cost=cost,
+        )
+        return out
+
+    for n in range(1, slots):
+        tied = [held[n, 0], held[n - 1, 1]]
+        if n == final - 1:
+            tied += [side_pieces[0], basis, order_back]
+        if n == final:
+            work(
+                first_names,
+                [(0, own_tokens, 0, pairs)]
+                + [(2, piece, part * 2 * rows, 2 * rows) for part, piece in enumerate(side_pieces)],
             )
-            old = crossings[-1:]
+            tied += state
+        held[n, 0], held[n - 1, 1], *tied = tie(*tied)
+        if n == final - 1:
+            side_pieces[0], basis, order_back = tied
+        if n == final:
+            state = tied
         else:
-            old = crossings[-2:-1]
-        if old and state is None:
-            side_pieces[0], *old_units = tie(side_pieces[0], *[held[n] for n in old])
-            held.update(zip(old, old_units))
-        tied = tie(held[name, 0], *[held[n] for n in old], *(state or []), basis, order_back)
-        held[name, 0], *tied = tied
-        for n in old:
-            held[n], *tied = tied
-        if state is not None:
-            state, tied = tied[:3], tied[3:]
-        basis, order_back = tied
-        cross(name)
-        if name > 0 and name < ahead:
-            held[name + 1, 0] = along(held[name, 0], following)
-        if name < 0 and -name < back:
-            held[name - 1, 0] = along(held[name, 0], before)
-
-    starts = {
-        0: own_starts,
-        1: starts_in(from_core[0], 2 * rows),
-        2: starts_in(side_pieces[0], 2 * rows),
-    }
-    first = CORES * len(known_first)
-    state, _ = call(
-        state,
-        starts=starts,
-        tokens=[
-            (from_core[0], pairs, 2 * rows),
-            (from_core[1], pairs + 2 * rows, 2 * rows),
-        ],
-        units=[(held[n], place_of[n]) for n in known_next],
-        tasks=[
-            ("units", [0, 2], first, CORES * len(known_next)),
-            ("units", [1], 0, first + CORES * len(known_next)),
-        ],
+            held[n + 1, 0] = along(held[n, 0], following)
+        held[n, 1] = swap(held[n, 0], 0, CORES)
+
+    work(
+        next_names,
+        [(1, piece, part * 2 * rows, 2 * rows) for part, piece in enumerate(from_core)],
     )
-    starts[3] = starts_in(diagonal_pieces[0], 3 * rows)
-    state, _ = call(
-        state,
-        starts=starts,
-        tokens=[(diagonal_pieces[0], 3 * pairs, 3 * rows)],
-        units=[],
-        tasks=[("piece", 3, 0, 3 * rows, 0, places - CORES)],
-    )
-    state, sent = call(
-        state,
-        starts=starts,
-        tokens=[(diagonal_pieces[1], 3 * pairs + 3 * rows, rows)],
-        units=[(held[arrival[-1]], places - CORES)],
-        tasks=[
-            ("units", [0, 1, 2, 3], places - CORES, CORES),
-            ("piece", 3, 3 * rows, 4 * rows, 0, places - CORES),
-        ],
-        sends=[1, 2, 3],
-    )
+    work([], [(3, diagonal_pieces[0], 0, 3 * rows)])
+    sent = work([arrival[-1]], [(3, diagonal_pieces[1], 3 * rows, rows)], sends=[1, 2, 3])
 
     from_core = swap(sent[0], 0, 1)
     from_side = swap(sent[1], 1, 0)

time: 88.4 us -> 83.7 us (0.947)
  the two profiles are of different devices: /device:TPU:29 before, /device:TPU:1 now
where the time goes in v8:
time: 83.7 us; the launch traced here: 82.7 us
  Pallas kernels  33 us (39%)
  waiting for transfers between devices  25.6 us (31%)
  starting transfers between devices  23.2 us (28%)
    ppermute x14, waiting for transfers between devices, swap(): return lax.ppermute(array, BOTH, table)  20 us
    pallas_call x4, Pallas kernels, accumulate(): pl.pallas_call(functools.partial(partial_kernel, rank, pairs, window, [(f...  17.7 us
    ppermute x14, starting transfers between devices, swap(): return lax.ppermute(array, BOTH, table)  17.2 us
    ppermute x3, starting transfers between devices, along(): return lax.ppermute(array, 'expert', pairs_of)  6 us
    ppermute x3, waiting for transfers between devices, along(): return lax.ppermute(array, 'expert', pairs_of)  5.62 us
    pallas_call x3, Pallas kernels, permuted(): pl.pallas_call(functools.partial(permute_kernel, plan), out_shape=[rows_s...  4.33 us
    pallas_call x1, Pallas kernels, local(): pl.pallas_call(functools.partial(blocks_kernel, tops, rank), out_shape=ja...  3.45 us
    pallas_call x1, Pallas kernels, local(): pl.pallas_call(sort_kernel, out_shape=[pltpu.VMEM(out_grads.shape, jnp.bf...  3.37 us
  transfers between devices with their start and end apart: 17, of which 8 were waited for; matrix products, arithmetic and copies ran while one was open for 0% of the time, Pallas kernels for 30%

profile of v8, /device:TPU:1, one launch (start us, length us, event | category | flops | bytes accessed | tf_op | source)
XLA Modules:
  0.0 82.7 jit_solution(8416649831142771646)
XLA Ops:
  0.0 1.3 %shard_map.73 = (bf16[256,512]{1,0:T(8,128)(2,1)S(1)}, bf16[256,512]{1,0:T(8,128)(2,1)S(1)}) custom-call(bf16[256,2048]{1,0:T(8,128)(2,1)} %bitcast.7), custom_call_target="tpu_custom_call" | custom-call | flops 1 | bytes 1 | tf_op jit(solution)/shard_map/pallas_call | solution.py:418
  1.3 0.1 collective-permute-start
  1.4 1.5 %collective-permute-done.two_ref = bf16[256,512]{1,0:T(8,128)(2,1)S(1)} collective-permute-done((bf16[256,512]{1,0:T(8,128)(2,1)S(1)}, bf16[256,512]{1,0:T(8,128)(2,1)S(1)}, u32[]{:S(2)}, u32[]{:S(2)}) %collective-permute-start) | collective-permute-done | bytes 262176 | tf_op jit(solution)/shard_map/ppermute | solution.py:381
  2.9 2.5 %collective-permute-start.1 = (bf16[512,512]{1,0:T(8,128)(2,1)S(1)}, bf16[512,512]{1,0:T(8,128)(2,1)S(1)}, u32[]{:S(2)}, u32[]{:S(2)}) collective-permute-start(bf16[512,512]{1,0:T(8,128)(2,1)S(1)} %shard_map.74.refs_5_), channel_id=1, source_target_pairs={{0,4},{1,5},{2,6},{3,7},{4,12},{5,13},{6,14},{7,15},{8,0},{9,1},{1... | collective-permute-start | bytes 1572872 | tf_op jit(solution)/shard_map/ppermute | solution.py:386
  5.4 1.2 %collective-permute-start.2 = (bf16[512,512]{1,0:T(8,128)(2,1)S(1)}, bf16[512,512]{1,0:T(8,128)(2,1)S(1)}, u32[]{:S(2)}, u32[]{:S(2)}) collective-permute-start(bf16[512,512]{1,0:T(8,128)(2,1)S(1)} %shard_map.74.refs_5_), channel_id=1, source_target_pairs={{0,2},{1,3},{2,0},{3,1},{4,6},{5,7},{6,4},{7,5},{8,10},{9,11},{10,... | collective-permute-start | bytes 1572872 | tf_op jit(solution)/shard_map/ppermute | solution.py:381
  6.6 0.7 copy-done.1
  7.3 3.4 %shard_map.75 = (bf16[128,8,2048]{2,1,0:T(8,128)(2,1)S(1)}, s32[1,128]{1,0:T(1,128)S(1)}, bf16[16,512]{1,0:T(8,128)(2,1)S(1)}, bf16[1024,1024]{1,0:T(8,128)(2,1)S(1)}, bf16[528,512]{1,0:T(8,128)(2,1)S(1)}) custom-call(s32[8,128]{1,0:T(8,128)S(1)} %bitcast.3, bf16[128,8,2048]{2,1,0:T(8,128)(2,1)} %grads_ref.1), custom_call_target="tpu_custom_call" | custom-call | flops 1 | bytes 1 | tf_op jit(solution)/shard_map/pallas_call | solution.py:440
  10.7 1.3 %collective-permute-start.5 = (bf16[528,512]{1,0:T(8,128)(2,1)S(1)}, bf16[528,512]{1,0:T(8,128)(2,1)S(1)}, u32[]{:S(2)}, u32[]{:S(2)}) collective-permute-start(bf16[528,512]{1,0:T(8,128)(2,1)S(1)} %get-tuple-element.52), channel_id=1, source_target_pairs={{0,16},{1,17},{2,18},{3,19},{4,20},{5,21},{6,22},{7,23},{8,24},{9,... | collective-permute-start | bytes 1622024 | tf_op jit(solution)/shard_map/ppermute | solution.py:381
  12.0 0.7 shard_map.76
  12.7 2.4 %shard_map.77 = (bf16[1024,512]{1,0:T(8,128)(2,1)S(1)}, bf16[528,512]{1,0:T(8,128)(2,1)S(1)}, bf16[512,512]{1,0:T(8,128)(2,1)S(1)}) custom-call(bf16[1024,1024]{1,0:T(8,128)(2,1)S(1)} %get-tuple-element.58.order_ref, bf16[16,512]{1,0:T(8,128)(2,1)S(1)} %get-tuple-element.54.head_ref, bf16[128,8,2048]{2,1,0:T(8,128)(2,1)S(1)} %get-tuple-element.55.grads_ref), custom_call_target="tpu_custom_call" | custom-call | flops 1 | bytes 1 | tf_op jit(solution)/shard_map/pallas_call | solution.py:458
  15.1 0.0 copy-start.2
  15.1 0.0 copy-start.3
  15.1 1.3 %collective-permute-start.6 = (bf16[528,512]{1,0:T(8,128)(2,1)S(1)}, bf16[528,512]{1,0:T(8,128)(2,1)S(1)}, u32[]{:S(2)}, u32[]{:S(2)}) collective-permute-start(bf16[528,512]{1,0:T(8,128)(2,1)S(1)} %get-tuple-element.67), channel_id=1, source_target_pairs={{0,1},{1,0},{2,3},{3,2},{4,5},{5,4},{6,7},{7,6},{8,9},{9,8},{10,11... | collective-permute-start | bytes 1622024 | tf_op jit(solution)/shard_map/ppermute | solution.py:381
  16.4 2.0 %collective-permute-done.1.refs_6_ = bf16[512,512]{1,0:T(8,128)(2,1)S(1)} collective-permute-done((bf16[512,512]{1,0:T(8,128)(2,1)S(1)}, bf16[512,512]{1,0:T(8,128)(2,1)S(1)}, u32[]{:S(2)}, u32[]{:S(2)}) %collective-permute-start.1) | collective-permute-done | bytes 524320 | tf_op jit(solution)/shard_map/ppermute | solution.py:386
  18.4 0.0 collective-permute-done.2.refs_8_
  18.4 2.1 %collective-permute-start.3 = (bf16[512,512]{1,0:T(8,128)(2,1)S(1)}, bf16[512,512]{1,0:T(8,128)(2,1)S(1)}, u32[]{:S(2)}, u32[]{:S(2)}) collective-permute-start(bf16[512,512]{1,0:T(8,128)(2,1)S(1)} %collective-permute-done.1.refs_6_), channel_id=1, source_target_pairs={{0,4},{1,5},{2,6},{3,7},{4,12},{5,13},{6,14},{7,15},{8,0},{9,1},{1... | collective-permute-start | bytes 1572872 | tf_op jit(solution)/shard_map/ppermute | solution.py:386
  20.5 1.2 %collective-permute-start.4 = (bf16[512,512]{1,0:T(8,128)(2,1)S(1)}, bf16[512,512]{1,0:T(8,128)(2,1)S(1)}, u32[]{:S(2)}, u32[]{:S(2)}) collective-permute-start(bf16[512,512]{1,0:T(8,128)(2,1)S(1)} %collective-permute-done.1.refs_6_), channel_id=1, source_target_pairs={{0,2},{1,3},{2,0},{3,1},{4,6},{5,7},{6,4},{7,5},{8,10},{9,11},{10,... | collective-permute-start | bytes 1572872 | tf_op jit(solution)/shard_map/ppermute | solution.py:381
  21.8 1.2 %collective-permute-start.11 = (bf16[512,512]{1,0:T(8,128)(2,1)S(1)}, bf16[512,512]{1,0:T(8,128)(2,1)S(1)}, u32[]{:S(2)}, u32[]{:S(2)}) collective-permute-start(bf16[512,512]{1,0:T(8,128)(2,1)S(1)} %shard_map.76), channel_id=1, source_target_pairs={{0,16},{1,17},{2,18},{3,19},{4,20},{5,21},{6,22},{7,23},{8,24},{9,... | collective-permute-start | bytes 1572872 | tf_op jit(solution)/shard_map/ppermute | solution.py:381
  23.0 1.3 %shard_map.78 = (bf16[784,512]{1,0:T(8,128)(2,1)S(1)}, bf16[256,512]{1,0:T(8,128)(2,1)S(1)}) custom-call(bf16[1024,1024]{1,0:T(8,128)(2,1)S(1)} %get-tuple-element.58.order_ref, bf16[16,512]{1,0:T(8,128)(2,1)S(1)} %get-tuple-element.54.head_ref, bf16[128,8,2048]{2,1,0:T(8,128)(2,1)S(1)} %get-tuple-element.55.grads_ref), custom_call_target="tpu_custom_call" | custom-call | flops 1 | bytes 1 | tf_op jit(solution)/shard_map/pallas_call | solution.py:458
  24.3 2.8 %shard_map.79 = (bf16[256,256]{1,0:T(8,128)(2,1)S(1)}, bf16[1024,1024]{1,0:T(8,128)(2,1)S(1)}) custom-call(bf16[128,7168]{1,0:T(8,128)(2,1)} %hidden_ref.1, bf16[64,7168]{1,0:T(8,128)(2,1)} %proj_ref.1, s32[1,128]{1,0:T(1,128)S(1)} %bitcast.6, s32[8,128]{1,0:T(8,128)S(1)} %bitcast.4), custom_call_target="tpu_custom_call" | custom-call | flops 1 | bytes 1 | tf_op jit(solution)/shard_map/pallas_call | solution.py:486
  27.1 0.0 collective-permute-done.5.refs_3_
  27.1 2.6 %collective-permute-start.8 = (bf16[256,512]{1,0:T(8,128)(2,1)S(1)}, bf16[256,512]{1,0:T(8,128)(2,1)S(1)}, u32[]{:S(2)}, u32[]{:S(2)}) collective-permute-start(bf16[256,512]{1,0:T(8,128)(2,1)S(1)} %get-tuple-element.59), channel_id=1, source_target_pairs={{0,17},{1,16},{2,19},{3,18},{4,21},{5,20},{6,23},{7,22},{8,25},{9,... | collective-permute-start | bytes 786440 | tf_op jit(solution)/shard_map/ppermute | solution.py:381
  29.6 1.8 %collective-permute-done.3.refs_7_ = bf16[512,512]{1,0:T(8,128)(2,1)S(1)} collective-permute-done((bf16[512,512]{1,0:T(8,128)(2,1)S(1)}, bf16[512,512]{1,0:T(8,128)(2,1)S(1)}, u32[]{:S(2)}, u32[]{:S(2)}) %collective-permute-start.3) | collective-permute-done | bytes 524320 | tf_op jit(solution)/shard_map/ppermute | solution.py:386
  31.4 3.1 %collective-permute-start.7 = (bf16[784,512]{1,0:T(8,128)(2,1)S(1)}, bf16[784,512]{1,0:T(8,128)(2,1)S(1)}, u32[]{:S(2)}, u32[]{:S(2)}) collective-permute-start(bf16[784,512]{1,0:T(8,128)(2,1)S(1)} %get-tuple-element.68), channel_id=1, source_target_pairs={{0,17},{1,16},{2,19},{3,18},{4,21},{5,20},{6,23},{7,22},{8,25},{9,... | collective-permute-start | bytes 2408456 | tf_op jit(solution)/shard_map/ppermute | solution.py:381
  34.5 0.0 collective-permute-done.4.refs_9_
  34.5 1.2 %collective-permute-start.10 = (bf16[512,512]{1,0:T(8,128)(2,1)S(1)}, bf16[512,512]{1,0:T(8,128)(2,1)S(1)}, u32[]{:S(2)}, u32[]{:S(2)}) collective-permute-start(bf16[512,512]{1,0:T(8,128)(2,1)S(1)} %collective-permute-done.3.refs_7_), channel_id=1, source_target_pairs={{0,2},{1,3},{2,0},{3,1},{4,6},{5,7},{6,4},{7,5},{8,10},{9,11},{10,... | collective-permute-start | bytes 1572872 | tf_op jit(solution)/shard_map/ppermute | solution.py:381
  35.8 0.0 collective-permute-done.6.refs_3_
  35.8 1.4 %collective-permute-start.9 = (bf16[512,512]{1,0:T(8,128)(2,1)S(1)}, bf16[512,512]{1,0:T(8,128)(2,1)S(1)}, u32[]{:S(2)}, u32[]{:S(2)}) collective-permute-start(bf16[512,512]{1,0:T(8,128)(2,1)S(1)} %collective-permute-done.3.refs_7_), channel_id=1, source_target_pairs={{0,4},{1,5},{2,6},{3,7},{4,12},{5,13},{6,14},{7,15},{8,0},{9,1},{1... | collective-permute-start | bytes 1572872 | tf_op jit(solution)/shard_map/ppermute | solution.py:386
  37.2 0.0 collective-permute-done.11.refs_4_
  37.2 1.5 %collective-permute-start.13 = (bf16[512,512]{1,0:T(8,128)(2,1)S(1)}, bf16[512,512]{1,0:T(8,128)(2,1)S(1)}, u32[]{:S(2)}, u32[]{:S(2)}) collective-permute-start(bf16[512,512]{1,0:T(8,128)(2,1)S(1)} %get-tuple-element.76), channel_id=1, source_target_pairs={{0,1},{1,0},{2,3},{3,2},{4,5},{5,4},{6,7},{7,6},{8,9},{9,8},{10,11... | collective-permute-start | bytes 1572872 | tf_op jit(solution)/shard_map/ppermute | solution.py:381
  38.7 5.9 %shard_map.80 = (bf16[4096,512]{1,0:T(8,128)(2,1)S(1)}, bf16[16,256,512]{2,1,0:T(8,128)(2,1)S(1)}, f32[4096,128]{1,0:T(8,128)S(1)}) custom-call(s32[16,16]{1,0:T(8,128)S(1)} %copy-done, s32[1,128]{1,0:T(1,128)S(1)} %get-tuple-element.65.refs_0_, s32[1,128]{1,0:T(1,128)S(1)} %slice_add_fusion.2.refs_1_, bf16[1024,512]{1,0:T(8,128)(2,1)S(1)} %get-tuple-element.57.refs_2_, ...), custom_call_target="tpu_custom_call" | custom-call | flops 1 | bytes 1 | tf_op jit(solution)/shard_map/pallas_call | solution.py:298
  44.6 3.2 %collective-permute-done.10.refs_6_ = bf16[512,512]{1,0:T(8,128)(2,1)S(1)} collective-permute-done((bf16[512,512]{1,0:T(8,128)(2,1)S(1)}, bf16[512,512]{1,0:T(8,128)(2,1)S(1)}, u32[]{:S(2)}, u32[]{:S(2)}) %collective-permute-start.10) | collective-permute-done | bytes 524320 | tf_op jit(solution)/shard_map/ppermute | solution.py:381
  47.7 1.8 %collective-permute-done.9.refs_5_ = bf16[512,512]{1,0:T(8,128)(2,1)S(1)} collective-permute-done((bf16[512,512]{1,0:T(8,128)(2,1)S(1)}, bf16[512,512]{1,0:T(8,128)(2,1)S(1)}, u32[]{:S(2)}, u32[]{:S(2)}) %collective-permute-start.9) | collective-permute-done | bytes 524320 | tf_op jit(solution)/shard_map/ppermute | solution.py:386
  49.6 0.2 collective-permute-start.12
  49.8 9.3 %collective-permute-done.7.refs_4_ = bf16[784,512]{1,0:T(8,128)(2,1)S(1)} collective-permute-done((bf16[784,512]{1,0:T(8,128)(2,1)S(1)}, bf16[784,512]{1,0:T(8,128)(2,1)S(1)}, u32[]{:S(2)}, u32[]{:S(2)}) %collective-permute-start.7) | collective-permute-done | bytes 802848 | tf_op jit(solution)/shard_map/ppermute | solution.py:381
  59.1 0.0 collective-permute-done.13.refs_4_
  59.1 5.4 %shard_map.81 = (bf16[4096,512]{1,0:T(8,128)(2,1)S(1)}, bf16[16,256,512]{2,1,0:T(8,128)(2,1)S(1)}, f32[4096,128]{1,0:T(8,128)S(1)}) custom-call(s32[16,16]{1,0:T(8,128)S(1)} %copy-done, s32[1,128]{1,0:T(1,128)S(1)} %get-tuple-element.65.refs_0_, s32[1,128]{1,0:T(1,128)S(1)} %slice_add_fusion.2.refs_1_, ...), custom_call_target="tpu_custom_call", output_to_operand_aliasing={{0}: (8, {}), {1}: (9, {}), {2}: (10, {})} | custom-call | flops 1 | bytes 1 | tf_op jit(solution)/shard_map/pallas_call | solution.py:298
  64.5 3.4 %shard_map.82 = (bf16[4096,512]{1,0:T(8,128)(2,1)S(1)}, bf16[16,256,512]{2,1,0:T(8,128)(2,1)S(1)}, f32[4096,128]{1,0:T(8,128)S(1)}) custom-call(s32[16,16]{1,0:T(8,128)S(1)} %copy-done, s32[1,128]{1,0:T(1,128)S(1)} %get-tuple-element.65.refs_0_, s32[1,128]{1,0:T(1,128)S(1)} %slice_add_fusion.2.refs_1_, ...), custom_call_target="tpu_custom_call", output_to_operand_aliasing={{0}: (6, {}), {1}: (7, {}), {2}: (8, {})} | custom-call | flops 1 | bytes 1 | tf_op jit(solution)/shard_map/pallas_call | solution.py:298
  67.9 0.0 collective-permute-done.8.refs_4_
  67.9 0.0 collective-permute-done.12.refs_5_
  68.0 3.1 %shard_map.83 = (bf16[4096,512]{1,0:T(8,128)(2,1)S(1)}, bf16[16,256,512]{2,1,0:T(8,128)(2,1)S(1)}, f32[4096,128]{1,0:T(8,128)S(1)}, bf16[512,128]{1,0:T(8,128)(2...) custom-call(s32[16,16]{1,0:T(8,128)S(1)} %copy-done, ...), custom_call_target="tpu_custom_call", output_to_operand_aliasing={{0}: (7, {}), {1}: (8, {}), {2}: (9, {})} | custom-call | flops 1 | bytes 1 | tf_op jit(solution)/shard_map/pallas_call | solution.py:298
  71.0 0.1 collective-permute-start.14
  71.1 1.3 %collective-permute-start.15 = (bf16[512,128]{1,0:T(8,128)(2,1)S(1)}, bf16[512,128]{1,0:T(8,128)(2,1)S(1)}, u32[]{:S(2)}, u32[]{:S(2)}) collective-permute-start(bf16[512,128]{1,0:T(8,128)(2,1)S(1)} %get-tuple-element.89), channel_id=1, source_target_pairs={{0,16},{1,17},{2,18},{3,19},{4,20},{5,21},{6,22},{7,23},{8,24},{9,... | collective-permute-start | bytes 393224 | tf_op jit(solution)/shard_map/ppermute | solution.py:381
  72.4 0.9 %collective-permute-start.16 = (bf16[512,128]{1,0:T(8,128)(2,1)S(1)}, bf16[512,128]{1,0:T(8,128)(2,1)S(1)}, u32[]{:S(2)}, u32[]{:S(2)}) collective-permute-start(bf16[512,128]{1,0:T(8,128)(2,1)S(1)} %get-tuple-element.90), channel_id=1, source_target_pairs={{0,17},{1,16},{2,19},{3,18},{4,21},{5,20},{6,23},{7,22},{8,25},{9,... | collective-permute-start | bytes 393224 | tf_op jit(solution)/shard_map/ppermute | solution.py:381
  73.2 0.0 collective-permute-done.14.b_ref
  73.2 2.6 %collective-permute-done.15.c_ref = bf16[512,128]{1,0:T(8,128)(2,1)S(1)} collective-permute-done((bf16[512,128]{1,0:T(8,128)(2,1)S(1)}, bf16[512,128]{1,0:T(8,128)(2,1)S(1)}, u32[]{:S(2)}, u32[]{:S(2)}) %collective-permute-start.15) | collective-permute-done | bytes 131104 | tf_op jit(solution)/shard_map/ppermute | solution.py:381
  75.8 3.4 %collective-permute-done.16.d_ref = bf16[512,128]{1,0:T(8,128)(2,1)S(1)} collective-permute-done((bf16[512,128]{1,0:T(8,128)(2,1)S(1)}, bf16[512,128]{1,0:T(8,128)(2,1)S(1)}, u32[]{:S(2)}, u32[]{:S(2)}) %collective-permute-start.16) | collective-permute-done | bytes 131104 | tf_op jit(solution)/shard_map/ppermute | solution.py:381
  79.2 3.5 %shard_map.84 = bf16[2,64,4096]{2,1,0:T(8,128)(2,1)} custom-call(s32[8,128]{1,0:T(8,128)S(1)} %bitcast.5, bf16[256,256]{1,0:T(8,128)(2,1)S(1)} %get-tuple-element.63.basis_ref, bf16[1024,1024]{1,0:T(8,128)(2,1)S(1)} %get-tuple-element.64.order_ref, f32[4096,128]{1,0:T(8,128)S(1)} %get-tuple-element.87.total_ref, ...), custom_call_target="tpu_custom_call" | custom-call | flops 1 | bytes 1 | tf_op jit(solution)/shard_map/pallas_call | solution.py:569
  (12 shorter events, 0.1 us)
Async XLA Ops:
  1.3 1.6 %collective-permute-start = (bf16[256,512]{1,0:T(8,128)(2,1)S(1)}, bf16[256,512]{1,0:T(8,128)(2,1)S(1)}, u32[]{:S(2)}, u32[]{:S(2)}) collective-permute-start(bf16[256,512]{1,0:T(8,128)(2,1)S(1)} %get-tuple-element.49), channel_id=1, source_target_pairs={{0,1},{1,0},{2,3},{3,2},{4,5},{5,4},{6,7},{7,6},{8,9},{9,8},{10,11... | collective-permute-start | bytes 786440 | tf_op jit(solution)/shard_map/ppermute | solution.py:381
  2.9 15.5 %collective-permute-start.1 = (bf16[512,512]{1,0:T(8,128)(2,1)S(1)}, bf16[512,512]{1,0:T(8,128)(2,1)S(1)}, u32[]{:S(2)}, u32[]{:S(2)}) collective-permute-start(bf16[512,512]{1,0:T(8,128)(2,1)S(1)} %shard_map.74.refs_5_), channel_id=1, source_target_pairs={{0,4},{1,5},{2,6},{3,7},{4,12},{5,13},{6,14},{7,15},{8,0},{9,1},{1... | collective-permute-start | bytes 1572872 | tf_op jit(solution)/shard_map/ppermute | solution.py:386
  5.4 13.0 %collective-permute-start.2 = (bf16[512,512]{1,0:T(8,128)(2,1)S(1)}, bf16[512,512]{1,0:T(8,128)(2,1)S(1)}, u32[]{:S(2)}, u32[]{:S(2)}) collective-permute-start(bf16[512,512]{1,0:T(8,128)(2,1)S(1)} %shard_map.74.refs_5_), channel_id=1, source_target_pairs={{0,2},{1,3},{2,0},{3,1},{4,6},{5,7},{6,4},{7,5},{8,10},{9,11},{10,... | collective-permute-start | bytes 1572872 | tf_op jit(solution)/shard_map/ppermute | solution.py:381
  6.6 0.7 copy-start.1
  10.7 16.4 %collective-permute-start.5 = (bf16[528,512]{1,0:T(8,128)(2,1)S(1)}, bf16[528,512]{1,0:T(8,128)(2,1)S(1)}, u32[]{:S(2)}, u32[]{:S(2)}) collective-permute-start(bf16[528,512]{1,0:T(8,128)(2,1)S(1)} %get-tuple-element.52), channel_id=1, source_target_pairs={{0,16},{1,17},{2,18},{3,19},{4,20},{5,21},{6,22},{7,23},{8,24},{9,... | collective-permute-start | bytes 1622024 | tf_op jit(solution)/shard_map/ppermute | solution.py:381
  15.1 9.2 %copy-start.2 = (s32[128,8]{0,1:T(8,128)S(1)}, s32[128,8]{0,1:T(8,128)}, u32[]{:S(2)}) copy-start(s32[128,8]{0,1:T(8,128)} %param.9) | copy-start | bytes 12292
  15.1 9.2 %copy-start.3 = (s32[128]{0:T(128)S(1)}, s32[128]{0:T(128)}, u32[]{:S(2)}) copy-start(s32[128]{0:T(128)} %param.10) | copy-start | bytes 1540
  15.1 20.7 %collective-permute-start.6 = (bf16[528,512]{1,0:T(8,128)(2,1)S(1)}, bf16[528,512]{1,0:T(8,128)(2,1)S(1)}, u32[]{:S(2)}, u32[]{:S(2)}) collective-permute-start(bf16[528,512]{1,0:T(8,128)(2,1)S(1)} %get-tuple-element.67), channel_id=1, source_target_pairs={{0,1},{1,0},{2,3},{3,2},{4,5},{5,4},{6,7},{7,6},{8,9},{9,8},{10,11... | collective-permute-start | bytes 1622024 | tf_op jit(solution)/shard_map/ppermute | solution.py:381
  18.4 13.0 %collective-permute-start.3 = (bf16[512,512]{1,0:T(8,128)(2,1)S(1)}, bf16[512,512]{1,0:T(8,128)(2,1)S(1)}, u32[]{:S(2)}, u32[]{:S(2)}) collective-permute-start(bf16[512,512]{1,0:T(8,128)(2,1)S(1)} %collective-permute-done.1.refs_6_), channel_id=1, source_target_pairs={{0,4},{1,5},{2,6},{3,7},{4,12},{5,13},{6,14},{7,15},{8,0},{9,1},{1... | collective-permute-start | bytes 1572872 | tf_op jit(solution)/shard_map/ppermute | solution.py:386
  20.5 14.0 %collective-permute-start.4 = (bf16[512,512]{1,0:T(8,128)(2,1)S(1)}, bf16[512,512]{1,0:T(8,128)(2,1)S(1)}, u32[]{:S(2)}, u32[]{:S(2)}) collective-permute-start(bf16[512,512]{1,0:T(8,128)(2,1)S(1)} %collective-permute-done.1.refs_6_), channel_id=1, source_target_pairs={{0,2},{1,3},{2,0},{3,1},{4,6},{5,7},{6,4},{7,5},{8,10},{9,11},{10,... | collective-permute-start | bytes 1572872 | tf_op jit(solution)/shard_map/ppermute | solution.py:381
  21.8 15.5 %collective-permute-start.11 = (bf16[512,512]{1,0:T(8,128)(2,1)S(1)}, bf16[512,512]{1,0:T(8,128)(2,1)S(1)}, u32[]{:S(2)}, u32[]{:S(2)}) collective-permute-start(bf16[512,512]{1,0:T(8,128)(2,1)S(1)} %shard_map.76), channel_id=1, source_target_pairs={{0,16},{1,17},{2,18},{3,19},{4,20},{5,21},{6,22},{7,23},{8,24},{9,... | collective-permute-start | bytes 1572872 | tf_op jit(solution)/shard_map/ppermute | solution.py:381
  23.0 15.7 %copy-start = (s32[16,16]{1,0:T(8,128)S(1)}, s32[16,16]{1,0:T(8,128)}, u32[]{:S(2)}) copy-start(s32[16,16]{1,0:T(8,128)} %constant.4.clone.bases_ref) | copy-start | bytes 3076
  27.1 40.9 %collective-permute-start.8 = (bf16[256,512]{1,0:T(8,128)(2,1)S(1)}, bf16[256,512]{1,0:T(8,128)(2,1)S(1)}, u32[]{:S(2)}, u32[]{:S(2)}) collective-permute-start(bf16[256,512]{1,0:T(8,128)(2,1)S(1)} %get-tuple-element.59), channel_id=1, source_target_pairs={{0,17},{1,16},{2,19},{3,18},{4,21},{5,20},{6,23},{7,22},{8,25},{9,... | collective-permute-start | bytes 786440 | tf_op jit(solution)/shard_map/ppermute | solution.py:381
  31.4 27.7 %collective-permute-start.7 = (bf16[784,512]{1,0:T(8,128)(2,1)S(1)}, bf16[784,512]{1,0:T(8,128)(2,1)S(1)}, u32[]{:S(2)}, u32[]{:S(2)}) collective-permute-start(bf16[784,512]{1,0:T(8,128)(2,1)S(1)} %get-tuple-element.68), channel_id=1, source_target_pairs={{0,17},{1,16},{2,19},{3,18},{4,21},{5,20},{6,23},{7,22},{8,25},{9,... | collective-permute-start | bytes 2408456 | tf_op jit(solution)/shard_map/ppermute | solution.py:381
  34.5 13.2 %collective-permute-start.10 = (bf16[512,512]{1,0:T(8,128)(2,1)S(1)}, bf16[512,512]{1,0:T(8,128)(2,1)S(1)}, u32[]{:S(2)}, u32[]{:S(2)}) collective-permute-start(bf16[512,512]{1,0:T(8,128)(2,1)S(1)} %collective-permute-done.3.refs_7_), channel_id=1, source_target_pairs={{0,2},{1,3},{2,0},{3,1},{4,6},{5,7},{6,4},{7,5},{8,10},{9,11},{10,... | collective-permute-start | bytes 1572872 | tf_op jit(solution)/shard_map/ppermute | solution.py:381
  35.8 13.8 %collective-permute-start.9 = (bf16[512,512]{1,0:T(8,128)(2,1)S(1)}, bf16[512,512]{1,0:T(8,128)(2,1)S(1)}, u32[]{:S(2)}, u32[]{:S(2)}) collective-permute-start(bf16[512,512]{1,0:T(8,128)(2,1)S(1)} %collective-permute-done.3.refs_7_), channel_id=1, source_target_pairs={{0,4},{1,5},{2,6},{3,7},{4,12},{5,13},{6,14},{7,15},{8,0},{9,1},{1... | collective-permute-start | bytes 1572872 | tf_op jit(solution)/shard_map/ppermute | solution.py:386
  37.2 21.9 %collective-permute-start.13 = (bf16[512,512]{1,0:T(8,128)(2,1)S(1)}, bf16[512,512]{1,0:T(8,128)(2,1)S(1)}, u32[]{:S(2)}, u32[]{:S(2)}) collective-permute-start(bf16[512,512]{1,0:T(8,128)(2,1)S(1)} %get-tuple-element.76), channel_id=1, source_target_pairs={{0,1},{1,0},{2,3},{3,2},{4,5},{5,4},{6,7},{7,6},{8,9},{9,8},{10,11... | collective-permute-start | bytes 1572872 | tf_op jit(solution)/shard_map/ppermute | solution.py:381
  49.6 18.4 %collective-permute-start.12 = (bf16[512,512]{1,0:T(8,128)(2,1)S(1)}, bf16[512,512]{1,0:T(8,128)(2,1)S(1)}, u32[]{:S(2)}, u32[]{:S(2)}) collective-permute-start(bf16[512,512]{1,0:T(8,128)(2,1)S(1)} %collective-permute-done.9.refs_5_), channel_id=1, source_target_pairs={{0,2},{1,3},{2,0},{3,1},{4,6},{5,7},{6,4},{7,5},{8,10},{9,11},{10,... | collective-permute-start | bytes 1572872 | tf_op jit(solution)/shard_map/ppermute | solution.py:381
  71.0 2.2 %collective-permute-start.14 = (bf16[512,128]{1,0:T(8,128)(2,1)S(1)}, bf16[512,128]{1,0:T(8,128)(2,1)S(1)}, u32[]{:S(2)}, u32[]{:S(2)}) collective-permute-start(bf16[512,128]{1,0:T(8,128)(2,1)S(1)} %get-tuple-element.88), channel_id=1, source_target_pairs={{0,1},{1,0},{2,3},{3,2},{4,5},{5,4},{6,7},{7,6},{8,9},{9,8},{10,11... | collective-permute-start | bytes 393224 | tf_op jit(solution)/shard_map/ppermute | solution.py:381
  71.1 4.7 %collective-permute-start.15 = (bf16[512,128]{1,0:T(8,128)(2,1)S(1)}, bf16[512,128]{1,0:T(8,128)(2,1)S(1)}, u32[]{:S(2)}, u32[]{:S(2)}) collective-permute-start(bf16[512,128]{1,0:T(8,128)(2,1)S(1)} %get-tuple-element.89), channel_id=1, source_target_pairs={{0,16},{1,17},{2,18},{3,19},{4,20},{5,21},{6,22},{7,23},{8,24},{9,... | collective-permute-start | bytes 393224 | tf_op jit(solution)/shard_map/ppermute | solution.py:381
  72.4 6.8 %collective-permute-start.16 = (bf16[512,128]{1,0:T(8,128)(2,1)S(1)}, bf16[512,128]{1,0:T(8,128)(2,1)S(1)}, u32[]{:S(2)}, u32[]{:S(2)}) collective-permute-start(bf16[512,128]{1,0:T(8,128)(2,1)S(1)} %get-tuple-element.90), channel_id=1, source_target_pairs={{0,17},{1,16},{2,19},{3,18},{4,21},{5,20},{6,23},{7,22},{8,25},{9,... | collective-permute-start | bytes 393224 | tf_op jit(solution)/shard_map/ppermute | solution.py:381

commit v9 on v8

--- a/solution.py
+++ b/solution.py
@@ -390,8 +390,7 @@
 
     final = slots - 1
     first_names = [(n, 0) for n in range(final)] + [(n, 1) for n in range(final - 1)]
-    next_names = [(final, 0), (final - 1, 1)]
-    arrival = first_names + next_names + [(final, 1)]
+    arrival = first_names + [(final - 1, 1), (final, 1), (final, 0)]
 
     def source(z, hops):
         for _ in range(hops):
@@ -425,17 +424,7 @@
         cost_estimate=QUICK,
     )(in_hbm(out_proj.reshape(cols, width)))
     other_unit = swap(core_unit, 0, 1)
-    unit = pl.pallas_call(
-        join_kernel,
-        out_shape=pltpu.VMEM((CORES * cols, quarter), jnp.bfloat16),
-        in_specs=[VMEM] * 2,
-        out_specs=VMEM,
-        compiler_params=pltpu.CompilerParams(vmem_limit_bytes=4 * MIB),
-        cost_estimate=QUICK,
-    )(mine_unit, other_unit)
-    held = {(0, 0): unit, (1, 0): along(unit, following), (0, 1): swap(unit, 0, CORES)}
-
-    by_rank, _ = tie(routes.T, unit)
+    by_rank, _ = tie(routes.T, core_unit)
     edges = -(-(experts + 1) // LANES) * LANES
     held_grads, own_starts, head, order, first_piece = pl.pallas_call(
         sort_kernel,
@@ -453,6 +442,17 @@
         cost_estimate=QUICK,
     )(by_rank, in_hbm(out_grads))
 
+    *joined, order = tie(mine_unit, other_unit, order)
+    unit = pl.pallas_call(
+        join_kernel,
+        out_shape=pltpu.VMEM((CORES * cols, quarter), jnp.bfloat16),
+        in_specs=[VMEM] * 2,
+        out_specs=VMEM,
+        compiler_params=pltpu.CompilerParams(vmem_limit_bytes=4 * MIB),
+        cost_estimate=QUICK,
+    )(*joined)
+    held = {(0, 0): unit, (1, 0): along(unit, following), (0, 1): swap(unit, 0, CORES)}
+
     def permuted(plan, headed, *after):
         held, *_ = tie(order, *after)
         return pl.pallas_call(
@@ -472,7 +472,7 @@
         return (digits[0] * DIGIT + digits[1]).reshape(1, edges)
 
     side_pieces = [swap(first_piece, 1, 0)]
-    (second_piece,) = permuted([(2, 2 * rows, 2 * rows)], [])
+    (second_piece,) = permuted([(2, 2 * rows, 2 * rows)], [], unit)
     own_tokens, *for_core = permuted(
         [(0, 0, pairs), (1, 0, 2 * rows), (1, 2 * rows, 2 * rows)], [1], second_piece
     )
@@ -481,6 +481,7 @@
     )
     from_core = [swap(piece, 0, 1) for piece in for_core]
     side_pieces.append(swap(second_piece, 1, 0))
+    third_piece, last_piece, side_pieces[0] = tie(third_piece, last_piece, side_pieces[0])
     diagonal_pieces = [swap(third_piece, 1, 1), swap(last_piece, 1, 1)]
     local_segments, *_ = tie(segments, last_piece)
     basis, order_back = pl.pallas_call(
@@ -509,22 +510,26 @@
     known_units = 0
     state = None
 
-    def work(names, tokens, sends=(), cost=QUICK):
+    def work(names, complete=(), partial=(), sends=(), cost=QUICK):
         nonlocal state, known_units
         tasks, arrived = [], []
-        if names and members:
+        for group, blocks in complete:
+            first = 0
+            for piece, count in blocks:
+                arrived.append((piece, group * pairs + first, count))
+                first += count
+            if group:
+                starts[group] = starts_in(*blocks[0])
+            members.append(group)
+        if names:
             tasks.append(("units", list(members), known_units, CORES * len(names)))
         known_units += CORES * len(names)
-        for group, piece, first, count in tokens:
+        for group, piece, first, count in partial:
             arrived.append((piece, group * pairs + first, count))
             if first == 0:
+                starts[group] = starts_in(piece, count)
                 members.append(group)
-                if group:
-                    starts[group] = starts_in(piece, count)
-            if count == pairs:
-                tasks.append(("units", [group], 0, known_units))
-            else:
-                tasks.append(("piece", group, first, first + count, 0, known_units))
+            tasks.append(("piece", group, first, first + count, 0, known_units))
         state, out = call(
             state,
             starts=starts,
@@ -537,31 +542,36 @@
         return out
 
     for n in range(1, slots):
+        if n == final:
+            break
         tied = [held[n, 0], held[n - 1, 1]]
+        if n == 1:
+            tied.append(side_pieces[0])
         if n == final - 1:
-            tied += [side_pieces[0], basis, order_back]
-        if n == final:
+            tied += [basis, order_back]
+        held[n, 0], held[n - 1, 1], *tied = tie(*tied)
+        if n == 1:
+            side_pieces[0], *tied = tied
+        if n == final - 1:
+            basis, order_back = tied
+            half = 2 * rows
             work(
                 first_names,
-                [(0, own_tokens, 0, pairs)]
-                + [(2, piece, part * 2 * rows, 2 * rows) for part, piece in enumerate(side_pieces)],
+                complete=[
+                    (0, [(own_tokens, pairs)]),
+                    (1, [(piece, half) for piece in from_core]),
+                    (2, [(piece, half) for piece in side_pieces]),
+                ],
             )
-            tied += state
-        held[n, 0], held[n - 1, 1], *tied = tie(*tied)
-        if n == final - 1:
-            side_pieces[0], basis, order_back = tied
-        if n == final:
-            state = tied
-        else:
-            held[n + 1, 0] = along(held[n, 0], following)
+        held[n + 1, 0] = along(held[n, 0], following)
         held[n, 1] = swap(held[n, 0], 0, CORES)
-
-    work(
-        next_names,
-        [(1, piece, part * 2 * rows, 2 * rows) for part, piece in enumerate(from_core)],
+    held[final, 1] = along(held[0, 1], before)
+
+    work([(final - 1, 1)], partial=[(3, diagonal_pieces[0], 0, 3 * rows)])
+    work([(final, 1)], cost=SHORT)
+    sent = work(
+        [(final, 0)], partial=[(3, diagonal_pieces[1], 3 * rows, rows)], sends=[1, 2, 3], cost=SHORT
     )
-    work([], [(3, diagonal_pieces[0], 0, 3 * rows)])
-    sent = work([arrival[-1]], [(3, diagonal_pieces[1], 3 * rows, rows)], sends=[1, 2, 3])
 
     from_core = swap(sent[0], 0, 1)
     from_side = swap(sent[1], 1, 0)

time: 83.7 us -> 82.3 us (0.983)
  waiting for transfers between devices: 25.6 us -> 35.3 us
  Pallas kernels: 33 us -> 27.2 us
  starting transfers between devices: 23.2 us -> 18.7 us
    ppermute x14 -> x13, waiting for transfers between devices: 20 us -> 28.2 us  [swap(): return lax.ppermute(array, BOTH, table)]
    pallas_call x4, Pallas kernels: 17.7 us -> 11.9 us  [accumulate(): pl.pallas_call(functools.partial(partial_kernel, rank, pairs, window, [(f...]
    ppermute x14 -> x13, starting transfers between devices: 17.2 us -> 13.8 us  [swap(): return lax.ppermute(array, BOTH, table)]
    ppermute x3 -> x4, waiting for transfers between devices: 5.62 us -> 7.05 us  [along(): return lax.ppermute(array, 'expert', pairs_of)]
    ppermute x3 -> x4, starting transfers between devices: 6 us -> 4.91 us  [along(): return lax.ppermute(array, 'expert', pairs_of)]
  transfers between devices with their start and end apart: 17 -> 17, of which waited for: 8 -> 7; matrix products, arithmetic and copies ran while one was open for 0% -> 0% of each run, Pallas kernels for 30% -> 23%
where the time goes in v9:
time: 82.3 us; the launch traced here: 82.1 us
  waiting for transfers between devices  35.3 us (43%)
  Pallas kernels  27.2 us (33%)
  starting transfers between devices  18.7 us (23%)
    ppermute x13, waiting for transfers between devices, swap(): return lax.ppermute(array, BOTH, table)  28.2 us
    ppermute x13, starting transfers between devices, swap(): return lax.ppermute(array, BOTH, table)  13.8 us
    pallas_call x4, Pallas kernels, accumulate(): pl.pallas_call(functools.partial(partial_kernel, rank, pairs, window, [(f...  11.9 us
    ppermute x4, waiting for transfers between devices, along(): return lax.ppermute(array, 'expert', pairs_of)  7.05 us
    ppermute x4, starting transfers between devices, along(): return lax.ppermute(array, 'expert', pairs_of)  4.91 us
    pallas_call x3, Pallas kernels, permuted(): pl.pallas_call(functools.partial(permute_kernel, plan), out_shape=[rows_s...  4.35 us
    pallas_call x1, Pallas kernels, local(): pl.pallas_call(functools.partial(blocks_kernel, tops, rank), out_shape=ja...  3.45 us
    pallas_call x1, Pallas kernels, local(): pl.pallas_call(sort_kernel, out_shape=[pltpu.VMEM(out_grads.shape, jnp.bf...  3.37 us
  transfers between devices with their start and end apart: 17, of which 7 were waited for; matrix products, arithmetic and copies ran while one was open for 0% of the time, Pallas kernels for 23%

profile of v9, /device:TPU:1, one launch (start us, length us, event | category | flops | bytes accessed | tf_op | source)
XLA Modules:
  0.0 82.1 jit_solution(7537031045973530363)
XLA Ops:
  0.0 1.3 %shard_map.73 = (bf16[256,512]{1,0:T(8,128)(2,1)S(1)}, bf16[256,512]{1,0:T(8,128)(2,1)S(1)}) custom-call(bf16[256,2048]{1,0:T(8,128)(2,1)} %bitcast.7), custom_call_target="tpu_custom_call" | custom-call | flops 1 | bytes 1 | tf_op jit(solution)/shard_map/pallas_call | solution.py:417
  1.3 0.1 collective-permute-start
  1.4 0.7 copy-done.1
  2.1 3.4 %shard_map.74 = (bf16[128,8,2048]{2,1,0:T(8,128)(2,1)S(1)}, s32[1,128]{1,0:T(1,128)S(1)}, bf16[16,512]{1,0:T(8,128)(2,1)S(1)}, bf16[1024,1024]{1,0:T(8,128)(2,1)S(1)}, bf16[528,512]{1,0:T(8,128)(2,1)S(1)}) custom-call(s32[8,128]{1,0:T(8,128)S(1)} %bitcast.3, bf16[128,8,2048]{2,1,0:T(8,128)(2,1)} %grads_ref.1), custom_call_target="tpu_custom_call" | custom-call | flops 1 | bytes 1 | tf_op jit(solution)/shard_map/pallas_call | solution.py:429
  5.5 2.7 %collective-permute-start.3 = (bf16[528,512]{1,0:T(8,128)(2,1)S(1)}, bf16[528,512]{1,0:T(8,128)(2,1)S(1)}, u32[]{:S(2)}, u32[]{:S(2)}) collective-permute-start(bf16[528,512]{1,0:T(8,128)(2,1)S(1)} %get-tuple-element.65), channel_id=1, source_target_pairs={{0,16},{1,17},{2,18},{3,19},{4,20},{5,21},{6,22},{7,23},{8,24},{9,... | collective-permute-start | bytes 1622024 | tf_op jit(solution)/shard_map/ppermute | solution.py:381
  8.2 0.0 collective-permute-done.two_ref
  8.2 1.3 %collective-permute-start.2 = (bf16[512,512]{1,0:T(8,128)(2,1)S(1)}, bf16[512,512]{1,0:T(8,128)(2,1)S(1)}, u32[]{:S(2)}, u32[]{:S(2)}) collective-permute-start(bf16[512,512]{1,0:T(8,128)(2,1)S(1)} %shard_map.75.refs_8_), channel_id=1, source_target_pairs={{0,2},{1,3},{2,0},{3,1},{4,6},{5,7},{6,4},{7,5},{8,10},{9,11},{10,... | collective-permute-start | bytes 1572872 | tf_op jit(solution)/shard_map/ppermute | solution.py:381
  9.5 1.3 %collective-permute-start.1 = (bf16[512,512]{1,0:T(8,128)(2,1)S(1)}, bf16[512,512]{1,0:T(8,128)(2,1)S(1)}, u32[]{:S(2)}, u32[]{:S(2)}) collective-permute-start(bf16[512,512]{1,0:T(8,128)(2,1)S(1)} %shard_map.75.refs_8_), channel_id=1, source_target_pairs={{0,4},{1,5},{2,6},{3,7},{4,12},{5,13},{6,14},{7,15},{8,0},{9,1},{1... | collective-permute-start | bytes 1572872 | tf_op jit(solution)/shard_map/ppermute | solution.py:386
  10.8 0.7 shard_map.76
  11.5 2.4 %shard_map.77 = (bf16[1024,512]{1,0:T(8,128)(2,1)S(1)}, bf16[528,512]{1,0:T(8,128)(2,1)S(1)}, bf16[512,512]{1,0:T(8,128)(2,1)S(1)}) custom-call(bf16[1024,1024]{1,0:T(8,128)(2,1)S(1)} %get-tuple-element.62.order_ref, bf16[16,512]{1,0:T(8,128)(2,1)S(1)} %get-tuple-element.58.head_ref, bf16[128,8,2048]{2,1,0:T(8,128)(2,1)S(1)} %get-tuple-element.59.grads_ref), custom_call_target="tpu_custom_call" | custom-call | flops 1 | bytes 1 | tf_op jit(solution)/shard_map/pallas_call | solution.py:458
  13.9 0.0 copy-start.2
  13.9 0.0 copy-start.3
  13.9 0.9 %collective-permute-start.6 = (bf16[528,512]{1,0:T(8,128)(2,1)S(1)}, bf16[528,512]{1,0:T(8,128)(2,1)S(1)}, u32[]{:S(2)}, u32[]{:S(2)}) collective-permute-start(bf16[528,512]{1,0:T(8,128)(2,1)S(1)} %get-tuple-element.75), channel_id=1, source_target_pairs={{0,1},{1,0},{2,3},{3,2},{4,5},{5,4},{6,7},{7,6},{8,9},{9,8},{10,11... | collective-permute-start | bytes 1622024 | tf_op jit(solution)/shard_map/ppermute | solution.py:381
  14.9 0.3 collective-permute-start.13
  15.1 1.3 %shard_map.78 = (bf16[784,512]{1,0:T(8,128)(2,1)S(1)}, bf16[256,512]{1,0:T(8,128)(2,1)S(1)}) custom-call(bf16[1024,1024]{1,0:T(8,128)(2,1)S(1)} %get-tuple-element.62.order_ref, bf16[16,512]{1,0:T(8,128)(2,1)S(1)} %get-tuple-element.58.head_ref, bf16[128,8,2048]{2,1,0:T(8,128)(2,1)S(1)} %get-tuple-element.59.grads_ref), custom_call_target="tpu_custom_call" | custom-call | flops 1 | bytes 1 | tf_op jit(solution)/shard_map/pallas_call | solution.py:458
  16.4 4.4 %collective-permute-done.3.refs_6_ = bf16[528,512]{1,0:T(8,128)(2,1)S(1)} collective-permute-done((bf16[528,512]{1,0:T(8,128)(2,1)S(1)}, bf16[528,512]{1,0:T(8,128)(2,1)S(1)}, u32[]{:S(2)}, u32[]{:S(2)}) %collective-permute-start.3) | collective-permute-done | bytes 540704 | tf_op jit(solution)/shard_map/ppermute | solution.py:381
  20.8 2.3 %collective-permute-start.7 = (bf16[784,512]{1,0:T(8,128)(2,1)S(1)}, bf16[784,512]{1,0:T(8,128)(2,1)S(1)}, u32[]{:S(2)}, u32[]{:S(2)}) collective-permute-start(bf16[784,512]{1,0:T(8,128)(2,1)S(1)} %get-tuple-element.77), channel_id=1, source_target_pairs={{0,17},{1,16},{2,19},{3,18},{4,21},{5,20},{6,23},{7,22},{8,25},{9,... | collective-permute-start | bytes 2408456 | tf_op jit(solution)/shard_map/ppermute | solution.py:381
  23.2 2.8 %shard_map.79 = (bf16[256,256]{1,0:T(8,128)(2,1)S(1)}, bf16[1024,1024]{1,0:T(8,128)(2,1)S(1)}) custom-call(bf16[128,7168]{1,0:T(8,128)(2,1)} %hidden_ref.1, bf16[64,7168]{1,0:T(8,128)(2,1)} %proj_ref.1, s32[1,128]{1,0:T(1,128)S(1)} %bitcast.6, s32[8,128]{1,0:T(8,128)S(1)} %bitcast.4), custom_call_target="tpu_custom_call" | custom-call | flops 1 | bytes 1 | tf_op jit(solution)/shard_map/pallas_call | solution.py:487
  25.9 0.0 collective-permute-done.2.refs_11_
  26.0 0.0 collective-permute-done.1.refs_9_
  26.0 1.3 %collective-permute-start.5 = (bf16[512,512]{1,0:T(8,128)(2,1)S(1)}, bf16[512,512]{1,0:T(8,128)(2,1)S(1)}, u32[]{:S(2)}, u32[]{:S(2)}) collective-permute-start(bf16[512,512]{1,0:T(8,128)(2,1)S(1)} %collective-permute-done.1.refs_9_), channel_id=1, source_target_pairs={{0,2},{1,3},{2,0},{3,1},{4,6},{5,7},{6,4},{7,5},{8,10},{9,11},{10,... | collective-permute-start | bytes 1572872 | tf_op jit(solution)/shard_map/ppermute | solution.py:381
  27.3 1.3 %collective-permute-start.4 = (bf16[512,512]{1,0:T(8,128)(2,1)S(1)}, bf16[512,512]{1,0:T(8,128)(2,1)S(1)}, u32[]{:S(2)}, u32[]{:S(2)}) collective-permute-start(bf16[512,512]{1,0:T(8,128)(2,1)S(1)} %collective-permute-done.1.refs_9_), channel_id=1, source_target_pairs={{0,4},{1,5},{2,6},{3,7},{4,12},{5,13},{6,14},{7,15},{8,0},{9,1},{1... | collective-permute-start | bytes 1572872 | tf_op jit(solution)/shard_map/ppermute | solution.py:386
  28.6 0.0 collective-permute-done.6.refs_4_
  28.6 0.0 collective-permute-start.12
  28.6 11.2 %collective-permute-done.5.refs_12_ = bf16[512,512]{1,0:T(8,128)(2,1)S(1)} collective-permute-done((bf16[512,512]{1,0:T(8,128)(2,1)S(1)}, bf16[512,512]{1,0:T(8,128)(2,1)S(1)}, u32[]{:S(2)}, u32[]{:S(2)}) %collective-permute-start.5) | collective-permute-done | bytes 524320 | tf_op jit(solution)/shard_map/ppermute | solution.py:381
  39.8 2.3 %collective-permute-start.10 = (bf16[512,512]{1,0:T(8,128)(2,1)S(1)}, bf16[512,512]{1,0:T(8,128)(2,1)S(1)}, u32[]{:S(2)}, u32[]{:S(2)}) collective-permute-start(bf16[512,512]{1,0:T(8,128)(2,1)S(1)} %collective-permute-done.2.refs_11_), channel_id=1, source_target_pairs={{0,8},{1,9},{2,10},{3,11},{4,0},{5,1},{6,2},{7,3},{8,12},{9,13},{1... | collective-permute-start | bytes 1572872 | tf_op jit(solution)/shard_map/ppermute | solution.py:386
  42.1 0.0 collective-permute-done.4.refs_10_
  42.1 1.2 %collective-permute-start.11 = (bf16[512,512]{1,0:T(8,128)(2,1)S(1)}, bf16[512,512]{1,0:T(8,128)(2,1)S(1)}, u32[]{:S(2)}, u32[]{:S(2)}) collective-permute-start(bf16[512,512]{1,0:T(8,128)(2,1)S(1)} %collective-permute-done.4.refs_10_), channel_id=1, source_target_pairs={{0,2},{1,3},{2,0},{3,1},{4,6},{5,7},{6,4},{7,5},{8,10},{9,11},{10,... | collective-permute-start | bytes 1572872 | tf_op jit(solution)/shard_map/ppermute | solution.py:381
  43.3 0.0 collective-permute-done.13.refs_7_
  43.3 1.3 %collective-permute-start.8 = (bf16[256,512]{1,0:T(8,128)(2,1)S(1)}, bf16[256,512]{1,0:T(8,128)(2,1)S(1)}, u32[]{:S(2)}, u32[]{:S(2)}) collective-permute-start(bf16[256,512]{1,0:T(8,128)(2,1)S(1)} %get-tuple-element.68), channel_id=1, source_target_pairs={{0,17},{1,16},{2,19},{3,18},{4,21},{5,20},{6,23},{7,22},{8,25},{9,... | collective-permute-start | bytes 786440 | tf_op jit(solution)/shard_map/ppermute | solution.py:381
  44.6 0.0 collective-permute-done.12.refs_5_
  44.6 0.0 collective-permute-start.9
  44.6 4.0 %shard_map.80 = (bf16[4096,512]{1,0:T(8,128)(2,1)S(1)}, bf16[16,256,512]{2,1,0:T(8,128)(2,1)S(1)}, f32[4096,128]{1,0:T(8,128)S(1)}) custom-call(s32[16,16]{1,0:T(8,128)S(1)} %copy-done, s32[1,128]{1,0:T(1,128)S(1)} %get-tuple-element.74.refs_0_, s32[1,128]{1,0:T(1,128)S(1)} %slice_add_fusion.2.refs_1_, s32[1,128]{1,0:T(1,128)S(1)} %slice_add_fusion.1.refs_2_, ...), custom_call_target="tpu_custom_call" | custom-call | flops 1 | bytes 1 | tf_op jit(solution)/shard_map/pallas_call | solution.py:298
  48.7 1.0 %collective-permute-done.7.refs_4_ = bf16[784,512]{1,0:T(8,128)(2,1)S(1)} collective-permute-done((bf16[784,512]{1,0:T(8,128)(2,1)S(1)}, bf16[784,512]{1,0:T(8,128)(2,1)S(1)}, u32[]{:S(2)}, u32[]{:S(2)}) %collective-permute-start.7) | collective-permute-done | bytes 802848 | tf_op jit(solution)/shard_map/ppermute | solution.py:381
  49.7 5.5 %collective-permute-done.11.refs_5_ = bf16[512,512]{1,0:T(8,128)(2,1)S(1)} collective-permute-done((bf16[512,512]{1,0:T(8,128)(2,1)S(1)}, bf16[512,512]{1,0:T(8,128)(2,1)S(1)}, u32[]{:S(2)}, u32[]{:S(2)}) %collective-permute-start.11) | collective-permute-done | bytes 524320 | tf_op jit(solution)/shard_map/ppermute | solution.py:381
  55.1 3.3 %shard_map.81 = (bf16[4096,512]{1,0:T(8,128)(2,1)S(1)}, bf16[16,256,512]{2,1,0:T(8,128)(2,1)S(1)}, f32[4096,128]{1,0:T(8,128)S(1)}) custom-call(s32[16,16]{1,0:T(8,128)S(1)} %copy-done, s32[1,128]{1,0:T(1,128)S(1)} %get-tuple-element.74.refs_0_, s32[1,128]{1,0:T(1,128)S(1)} %slice_add_fusion.2.refs_1_, ...), custom_call_target="tpu_custom_call", output_to_operand_aliasing={{0}: (7, {}), {1}: (8, {}), {2}: (9, {})} | custom-call | flops 1 | bytes 1 | tf_op jit(solution)/shard_map/pallas_call | solution.py:298
  58.4 0.0 collective-permute-done.10.refs_4_
  58.4 1.4 %shard_map.82 = (bf16[4096,512]{1,0:T(8,128)(2,1)S(1)}, bf16[16,256,512]{2,1,0:T(8,128)(2,1)S(1)}, f32[4096,128]{1,0:T(8,128)S(1)}) custom-call(s32[16,16]{1,0:T(8,128)S(1)} %copy-done, s32[1,128]{1,0:T(1,128)S(1)} %get-tuple-element.74.refs_0_, s32[1,128]{1,0:T(1,128)S(1)} %slice_add_fusion.2.refs_1_, ...), custom_call_target="tpu_custom_call", output_to_operand_aliasing={{0}: (6, {}), {1}: (7, {}), {2}: (8, {})} | custom-call | flops 1000000000 | bytes 1 | tf_op jit(solution)/shard_map/pallas_call | solution.py:298
  59.8 0.0 collective-permute-done.8.refs_4_
  59.8 7.0 %collective-permute-done.9.refs_5_ = bf16[512,512]{1,0:T(8,128)(2,1)S(1)} collective-permute-done((bf16[512,512]{1,0:T(8,128)(2,1)S(1)}, bf16[512,512]{1,0:T(8,128)(2,1)S(1)}, u32[]{:S(2)}, u32[]{:S(2)}) %collective-permute-start.9) | collective-permute-done | bytes 524320 | tf_op jit(solution)/shard_map/ppermute | solution.py:386
  66.8 3.3 %shard_map.83 = (bf16[4096,512]{1,0:T(8,128)(2,1)S(1)}, bf16[16,256,512]{2,1,0:T(8,128)(2,1)S(1)}, f32[4096,128]{1,0:T(8,128)S(1)}, bf16[512,128]{1,0:T(8,128)(2...) custom-call(s32[16,16]{1,0:T(8,128)S(1)} %copy-done, ...), custom_call_target="tpu_custom_call", output_to_operand_aliasing={{0}: (7, {}), {1}: (8, {}), {2}: (9, {})} | custom-call | flops 1000000000 | bytes 1 | tf_op jit(solution)/shard_map/pallas_call | solution.py:298
  70.1 0.5 collective-permute-start.14
  70.6 0.0 collective-permute-start.15
  70.6 1.8 %collective-permute-start.16 = (bf16[512,128]{1,0:T(8,128)(2,1)S(1)}, bf16[512,128]{1,0:T(8,128)(2,1)S(1)}, u32[]{:S(2)}, u32[]{:S(2)}) collective-permute-start(bf16[512,128]{1,0:T(8,128)(2,1)S(1)} %get-tuple-element.94), channel_id=1, source_target_pairs={{0,17},{1,16},{2,19},{3,18},{4,21},{5,20},{6,23},{7,22},{8,25},{9,... | collective-permute-start | bytes 393224 | tf_op jit(solution)/shard_map/ppermute | solution.py:381
  72.4 0.0 collective-permute-done.14.b_ref
  72.4 3.1 %collective-permute-done.15.c_ref = bf16[512,128]{1,0:T(8,128)(2,1)S(1)} collective-permute-done((bf16[512,128]{1,0:T(8,128)(2,1)S(1)}, bf16[512,128]{1,0:T(8,128)(2,1)S(1)}, u32[]{:S(2)}, u32[]{:S(2)}) %collective-permute-start.15) | collective-permute-done | bytes 131104 | tf_op jit(solution)/shard_map/ppermute | solution.py:381
  75.5 3.1 %collective-permute-done.16.d_ref = bf16[512,128]{1,0:T(8,128)(2,1)S(1)} collective-permute-done((bf16[512,128]{1,0:T(8,128)(2,1)S(1)}, bf16[512,128]{1,0:T(8,128)(2,1)S(1)}, u32[]{:S(2)}, u32[]{:S(2)}) %collective-permute-start.16) | collective-permute-done | bytes 131104 | tf_op jit(solution)/shard_map/ppermute | solution.py:381
  78.6 3.4 %shard_map.84 = bf16[2,64,4096]{2,1,0:T(8,128)(2,1)} custom-call(s32[8,128]{1,0:T(8,128)S(1)} %bitcast.5, bf16[256,256]{1,0:T(8,128)(2,1)S(1)} %get-tuple-element.72.basis_ref, bf16[1024,1024]{1,0:T(8,128)(2,1)S(1)} %get-tuple-element.73.order_ref, f32[4096,128]{1,0:T(8,128)S(1)} %get-tuple-element.91.total_ref, ...), custom_call_target="tpu_custom_call" | custom-call | flops 1 | bytes 1 | tf_op jit(solution)/shard_map/pallas_call | solution.py:579
  (12 shorter events, 0.1 us)
Async XLA Ops:
  1.3 6.9 %collective-permute-start = (bf16[256,512]{1,0:T(8,128)(2,1)S(1)}, bf16[256,512]{1,0:T(8,128)(2,1)S(1)}, u32[]{:S(2)}, u32[]{:S(2)}) collective-permute-start(bf16[256,512]{1,0:T(8,128)(2,1)S(1)} %get-tuple-element.50), channel_id=1, source_target_pairs={{0,1},{1,0},{2,3},{3,2},{4,5},{5,4},{6,7},{7,6},{8,9},{9,8},{10,11... | collective-permute-start | bytes 786440 | tf_op jit(solution)/shard_map/ppermute | solution.py:381
  1.4 0.7 copy-start.1
  5.5 15.4 %collective-permute-start.3 = (bf16[528,512]{1,0:T(8,128)(2,1)S(1)}, bf16[528,512]{1,0:T(8,128)(2,1)S(1)}, u32[]{:S(2)}, u32[]{:S(2)}) collective-permute-start(bf16[528,512]{1,0:T(8,128)(2,1)S(1)} %get-tuple-element.65), channel_id=1, source_target_pairs={{0,16},{1,17},{2,18},{3,19},{4,20},{5,21},{6,22},{7,23},{8,24},{9,... | collective-permute-start | bytes 1622024 | tf_op jit(solution)/shard_map/ppermute | solution.py:381
  8.2 17.7 %collective-permute-start.2 = (bf16[512,512]{1,0:T(8,128)(2,1)S(1)}, bf16[512,512]{1,0:T(8,128)(2,1)S(1)}, u32[]{:S(2)}, u32[]{:S(2)}) collective-permute-start(bf16[512,512]{1,0:T(8,128)(2,1)S(1)} %shard_map.75.refs_8_), channel_id=1, source_target_pairs={{0,2},{1,3},{2,0},{3,1},{4,6},{5,7},{6,4},{7,5},{8,10},{9,11},{10,... | collective-permute-start | bytes 1572872 | tf_op jit(solution)/shard_map/ppermute | solution.py:381
  9.5 16.4 %collective-permute-start.1 = (bf16[512,512]{1,0:T(8,128)(2,1)S(1)}, bf16[512,512]{1,0:T(8,128)(2,1)S(1)}, u32[]{:S(2)}, u32[]{:S(2)}) collective-permute-start(bf16[512,512]{1,0:T(8,128)(2,1)S(1)} %shard_map.75.refs_8_), channel_id=1, source_target_pairs={{0,4},{1,5},{2,6},{3,7},{4,12},{5,13},{6,14},{7,15},{8,0},{9,1},{1... | collective-permute-start | bytes 1572872 | tf_op jit(solution)/shard_map/ppermute | solution.py:386
  13.9 9.2 %copy-start.2 = (s32[128,8]{0,1:T(8,128)S(1)}, s32[128,8]{0,1:T(8,128)}, u32[]{:S(2)}) copy-start(s32[128,8]{0,1:T(8,128)} %param.9) | copy-start | bytes 12292
  13.9 9.2 %copy-start.3 = (s32[128]{0:T(128)S(1)}, s32[128]{0:T(128)}, u32[]{:S(2)}) copy-start(s32[128]{0:T(128)} %param.10) | copy-start | bytes 1540
  13.9 14.6 %collective-permute-start.6 = (bf16[528,512]{1,0:T(8,128)(2,1)S(1)}, bf16[528,512]{1,0:T(8,128)(2,1)S(1)}, u32[]{:S(2)}, u32[]{:S(2)}) collective-permute-start(bf16[528,512]{1,0:T(8,128)(2,1)S(1)} %get-tuple-element.75), channel_id=1, source_target_pairs={{0,1},{1,0},{2,3},{3,2},{4,5},{5,4},{6,7},{7,6},{8,9},{9,8},{10,11... | collective-permute-start | bytes 1622024 | tf_op jit(solution)/shard_map/ppermute | solution.py:381
  14.9 28.5 %collective-permute-start.13 = (bf16[512,512]{1,0:T(8,128)(2,1)S(1)}, bf16[512,512]{1,0:T(8,128)(2,1)S(1)}, u32[]{:S(2)}, u32[]{:S(2)}) collective-permute-start(bf16[512,512]{1,0:T(8,128)(2,1)S(1)} %shard_map.76), channel_id=1, source_target_pairs={{0,16},{1,17},{2,18},{3,19},{4,20},{5,21},{6,22},{7,23},{8,24},{9,... | collective-permute-start | bytes 1572872 | tf_op jit(solution)/shard_map/ppermute | solution.py:381
  15.1 29.5 %copy-start = (s32[16,16]{1,0:T(8,128)S(1)}, s32[16,16]{1,0:T(8,128)}, u32[]{:S(2)}) copy-start(s32[16,16]{1,0:T(8,128)} %constant.4.clone.bases_ref) | copy-start | bytes 3076
  20.8 28.8 %collective-permute-start.7 = (bf16[784,512]{1,0:T(8,128)(2,1)S(1)}, bf16[784,512]{1,0:T(8,128)(2,1)S(1)}, u32[]{:S(2)}, u32[]{:S(2)}) collective-permute-start(bf16[784,512]{1,0:T(8,128)(2,1)S(1)} %get-tuple-element.77), channel_id=1, source_target_pairs={{0,17},{1,16},{2,19},{3,18},{4,21},{5,20},{6,23},{7,22},{8,25},{9,... | collective-permute-start | bytes 2408456 | tf_op jit(solution)/shard_map/ppermute | solution.py:381
  26.0 13.8 %collective-permute-start.5 = (bf16[512,512]{1,0:T(8,128)(2,1)S(1)}, bf16[512,512]{1,0:T(8,128)(2,1)S(1)}, u32[]{:S(2)}, u32[]{:S(2)}) collective-permute-start(bf16[512,512]{1,0:T(8,128)(2,1)S(1)} %collective-permute-done.1.refs_9_), channel_id=1, source_target_pairs={{0,2},{1,3},{2,0},{3,1},{4,6},{5,7},{6,4},{7,5},{8,10},{9,11},{10,... | collective-permute-start | bytes 1572872 | tf_op jit(solution)/shard_map/ppermute | solution.py:381
  27.3 14.8 %collective-permute-start.4 = (bf16[512,512]{1,0:T(8,128)(2,1)S(1)}, bf16[512,512]{1,0:T(8,128)(2,1)S(1)}, u32[]{:S(2)}, u32[]{:S(2)}) collective-permute-start(bf16[512,512]{1,0:T(8,128)(2,1)S(1)} %collective-permute-done.1.refs_9_), channel_id=1, source_target_pairs={{0,4},{1,5},{2,6},{3,7},{4,12},{5,13},{6,14},{7,15},{8,0},{9,1},{1... | collective-permute-start | bytes 1572872 | tf_op jit(solution)/shard_map/ppermute | solution.py:386
  28.6 16.1 %collective-permute-start.12 = (bf16[512,512]{1,0:T(8,128)(2,1)S(1)}, bf16[512,512]{1,0:T(8,128)(2,1)S(1)}, u32[]{:S(2)}, u32[]{:S(2)}) collective-permute-start(bf16[512,512]{1,0:T(8,128)(2,1)S(1)} %get-tuple-element.80), channel_id=1, source_target_pairs={{0,1},{1,0},{2,3},{3,2},{4,5},{5,4},{6,7},{7,6},{8,9},{9,8},{10,11... | collective-permute-start | bytes 1572872 | tf_op jit(solution)/shard_map/ppermute | solution.py:381
  39.8 18.7 %collective-permute-start.10 = (bf16[512,512]{1,0:T(8,128)(2,1)S(1)}, bf16[512,512]{1,0:T(8,128)(2,1)S(1)}, u32[]{:S(2)}, u32[]{:S(2)}) collective-permute-start(bf16[512,512]{1,0:T(8,128)(2,1)S(1)} %collective-permute-done.2.refs_11_), channel_id=1, source_target_pairs={{0,8},{1,9},{2,10},{3,11},{4,0},{5,1},{6,2},{7,3},{8,12},{9,13},{1... | collective-permute-start | bytes 1572872 | tf_op jit(solution)/shard_map/ppermute | solution.py:386
  42.1 13.0 %collective-permute-start.11 = (bf16[512,512]{1,0:T(8,128)(2,1)S(1)}, bf16[512,512]{1,0:T(8,128)(2,1)S(1)}, u32[]{:S(2)}, u32[]{:S(2)}) collective-permute-start(bf16[512,512]{1,0:T(8,128)(2,1)S(1)} %collective-permute-done.4.refs_10_), channel_id=1, source_target_pairs={{0,2},{1,3},{2,0},{3,1},{4,6},{5,7},{6,4},{7,5},{8,10},{9,11},{10,... | collective-permute-start | bytes 1572872 | tf_op jit(solution)/shard_map/ppermute | solution.py:381
  43.3 16.5 %collective-permute-start.8 = (bf16[256,512]{1,0:T(8,128)(2,1)S(1)}, bf16[256,512]{1,0:T(8,128)(2,1)S(1)}, u32[]{:S(2)}, u32[]{:S(2)}) collective-permute-start(bf16[256,512]{1,0:T(8,128)(2,1)S(1)} %get-tuple-element.68), channel_id=1, source_target_pairs={{0,17},{1,16},{2,19},{3,18},{4,21},{5,20},{6,23},{7,22},{8,25},{9,... | collective-permute-start | bytes 786440 | tf_op jit(solution)/shard_map/ppermute | solution.py:381
  44.6 22.2 %collective-permute-start.9 = (bf16[512,512]{1,0:T(8,128)(2,1)S(1)}, bf16[512,512]{1,0:T(8,128)(2,1)S(1)}, u32[]{:S(2)}, u32[]{:S(2)}) collective-permute-start(bf16[512,512]{1,0:T(8,128)(2,1)S(1)} %collective-permute-done.4.refs_10_), channel_id=1, source_target_pairs={{0,4},{1,5},{2,6},{3,7},{4,12},{5,13},{6,14},{7,15},{8,0},{9,1},{1... | collective-permute-start | bytes 1572872 | tf_op jit(solution)/shard_map/ppermute | solution.py:386
  70.1 2.3 %collective-permute-start.14 = (bf16[512,128]{1,0:T(8,128)(2,1)S(1)}, bf16[512,128]{1,0:T(8,128)(2,1)S(1)}, u32[]{:S(2)}, u32[]{:S(2)}) collective-permute-start(bf16[512,128]{1,0:T(8,128)(2,1)S(1)} %get-tuple-element.92), channel_id=1, source_target_pairs={{0,1},{1,0},{2,3},{3,2},{4,5},{5,4},{6,7},{7,6},{8,9},{9,8},{10,11... | collective-permute-start | bytes 393224 | tf_op jit(solution)/shard_map/ppermute | solution.py:381
  70.6 4.9 %collective-permute-start.15 = (bf16[512,128]{1,0:T(8,128)(2,1)S(1)}, bf16[512,128]{1,0:T(8,128)(2,1)S(1)}, u32[]{:S(2)}, u32[]{:S(2)}) collective-permute-start(bf16[512,128]{1,0:T(8,128)(2,1)S(1)} %get-tuple-element.93), channel_id=1, source_target_pairs={{0,16},{1,17},{2,18},{3,19},{4,20},{5,21},{6,22},{7,23},{8,24},{9,... | collective-permute-start | bytes 393224 | tf_op jit(solution)/shard_map/ppermute | solution.py:381
  70.6 8.0 %collective-permute-start.16 = (bf16[512,128]{1,0:T(8,128)(2,1)S(1)}, bf16[512,128]{1,0:T(8,128)(2,1)S(1)}, u32[]{:S(2)}, u32[]{:S(2)}) collective-permute-start(bf16[512,128]{1,0:T(8,128)(2,1)S(1)} %get-tuple-element.94), channel_id=1, source_target_pairs={{0,17},{1,16},{2,19},{3,18},{4,21},{5,20},{6,23},{7,22},{8,25},{9,... | collective-permute-start | bytes 393224 | tf_op jit(solution)/shard_map/ppermute | solution.py:381

commit v10 on v9

--- a/solution.py
+++ b/solution.py
@@ -318,11 +318,72 @@
     return list(out[:3]), list(out[3:])
 
 
+def late_kernel(
+    rank, pairs, window, place, groups, bases_ref, *refs
+):
+    start_refs, (tokens, unit_ref), outs = refs[:groups], refs[groups : groups + 2], refs[groups + 2 :]
+    cols = unit_ref.shape[0] // CORES
+    per_tile = LANES // rank
+    low = lax.broadcasted_iota(jnp.int32, (1, LANES), 1) < rank
+    device = lax.axis_index("expert")
+    first_core = device % CORES == 0
+    folded = []
+    for half in range(CORES):
+        base = bases_ref[device, place + half]
+        offsets, rows = [], []
+        for g in range(groups):
+            at = jnp.minimum(start_refs[g][0, base] & -ALIGN, pairs - window)
+            offsets.append(at)
+            rows.append(tokens[pl.ds(pl.multiple_of(g * pairs + at, ALIGN), window), :])
+        dense = lax.dot_general(
+            jnp.concatenate(rows, axis=0),
+            unit_ref[half * cols : (half + 1) * cols, :],
+            NT,
+            preferred_element_type=jnp.float32,
+        )
+        found = []
+        for g in range(groups):
+            value = jnp.zeros((window, LANES), jnp.float32)
+            number = offsets[g] + lax.broadcasted_iota(jnp.int32, (window, LANES), 0)
+            for j in range(cols // LANES):
+                edge = [start_refs[g][0, base + j * per_tile + i] for i in range(per_tile + 1)]
+                inside = (number >= jnp.where(low, edge[0], edge[1])) & (
+                    number < jnp.where(low, edge[1], edge[2])
+                )
+                part = dense[g * window : (g + 1) * window, j * LANES : (j + 1) * LANES]
+                value = jnp.where(inside, part, value)
+            found.append(value + pltpu.roll(value, rank, 1))
+        folded.append(found)
+    for g, out in enumerate(outs):
+        one, two = folded[0][g], folded[1][g]
+        zero = jnp.where(first_core, one, two)
+        other = jnp.where(first_core, two, one)
+        out[...] = jnp.where(low, zero, other).astype(out.dtype)
+
+
+def expand(routes_ref, turned, spread, first, tiles):
+    tops, tokens = routes_ref.shape
+    rank = turned.shape[0]
+
+    def one(tile, carry):
+        here = pl.multiple_of(tile * 8, 8)
+        ids = first + here + lax.broadcasted_iota(jnp.int32, (8, tokens), 0)
+        masks = [routes_ref[k : k + 1, :] == ids for k in range(tops)]
+        for r in range(rank):
+            value = jnp.zeros((8, tokens), jnp.float32)
+            for k in range(tops):
+                row = turned[r : r + 1, k * tokens : (k + 1) * tokens]
+                value = jnp.where(masks[k], row, value)
+            spread[r, pl.ds(here, 8), :] = value
+        return carry
+
+    lax.fori_loop(0, tiles, one, 0)
+
+
 def blocks_kernel(
-    tops, rank, routes_ref, basis_ref, order_ref, total_ref, b_ref, c_ref, d_ref, out_ref, turned, spread
+    rank, routes_ref, basis_ref, order_ref, total_ref, b_ref, c_ref, d_ref, out_ref, turned, spread
 ):
     half = b_ref.shape[0]
-    tokens = 2 * half // tops
     value = packed(total_ref, 0, 2 * half, rank)
     for ref in (b_ref, c_ref, d_ref):
         value = value + ref[...].astype(jnp.float32)
@@ -330,20 +391,7 @@
     value = jnp.concatenate([value[0:rank], value[rank : 2 * rank]], axis=1).astype(jnp.bfloat16)
     turned[...] = jnp.dot(value, order_ref[...], preferred_element_type=jnp.float32)
     experts = out_ref.shape[1]
-
-    def expand(tile, carry):
-        first = pl.multiple_of(tile * 8, 8)
-        ids = first + lax.broadcasted_iota(jnp.int32, (8, tokens), 0)
-        masks = [routes_ref[k : k + 1, :] == ids for k in range(tops)]
-        for r in range(rank):
-            value = jnp.zeros((8, tokens), jnp.float32)
-            for k in range(tops):
-                row = turned[r : r + 1, k * tokens : (k + 1) * tokens]
-                value = jnp.where(masks[k], row, value)
-            spread[r, pl.ds(first, 8), :] = value
-        return carry
-
-    lax.fori_loop(0, experts // 8, expand, 0)
+    expand(routes_ref, turned, spread, 0, experts // 8)
     for pair in range(rank // 2):
         both = jnp.concatenate([spread[2 * pair], spread[2 * pair + 1]], axis=1)
         block = jnp.dot(
@@ -353,6 +401,65 @@
             out_ref[s, :, pl.ds(pair * 2 * rank, 2 * rank)] = block[
                 :, s * 2 * rank : (s + 1) * 2 * rank
             ]
+
+
+def last_kernel(
+    rank,
+    place,
+    count,
+    held,
+    bases_ref,
+    starts_ref,
+    routes_ref,
+    basis_ref,
+    order_ref,
+    turned_ref,
+    own_ref,
+    b_ref,
+    c_ref,
+    d_ref,
+    _,
+    out_ref,
+    turned,
+    spread,
+    block,
+    sem,
+):
+    window = own_ref.shape[0]
+    pairs = order_ref.shape[0]
+    value = own_ref[...]
+    for ref in (b_ref, c_ref, d_ref):
+        value = value + ref[...].astype(jnp.float32)
+    value = value.T.astype(jnp.bfloat16)
+    first = bases_ref[lax.axis_index("expert"), place] // count * count
+    unit = bases_ref[lax.axis_index("expert"), place] // (CORES * held) * (CORES * held)
+    total = turned_ref[...]
+    for core in range(CORES):
+        at = jnp.minimum(starts_ref[0, unit + core * held] & -ALIGN, pairs - window)
+        rows = order_ref[pl.ds(pl.multiple_of(at, ALIGN), window), :]
+        total = total + jnp.dot(
+            value[core * rank : (core + 1) * rank], rows, preferred_element_type=jnp.float32
+        )
+    turned[...] = total
+    expand(routes_ref, turned, spread, first, count // 8)
+    lines = [
+        jnp.concatenate([spread[2 * pair], spread[2 * pair + 1]], axis=1) for pair in range(rank // 2)
+    ]
+    made = jnp.dot(
+        jnp.concatenate(lines, axis=0).astype(jnp.bfloat16),
+        basis_ref[...],
+        preferred_element_type=jnp.float32,
+    ).astype(jnp.bfloat16)
+    for pair in range(rank // 2):
+        for s in range(SEG_DEV):
+            block[s, :, pl.ds(pair * 2 * rank, 2 * rank)] = made[
+                pair * count : (pair + 1) * count, s * 2 * rank : (s + 1) * 2 * rank
+            ]
+    copy = pltpu.make_async_copy(
+        block, out_ref.at[:, pl.ds(pl.multiple_of(first, count), count), :], sem
+    )
+    copy.start()
+    copy.wait()
 
 
 def local(hidden_in, out_grads, routes, segments, in_proj, out_proj):
@@ -568,26 +675,56 @@
     held[final, 1] = along(held[0, 1], before)
 
     work([(final - 1, 1)], partial=[(3, diagonal_pieces[0], 0, 3 * rows)])
-    work([(final, 1)], cost=SHORT)
     sent = work(
-        [(final, 0)], partial=[(3, diagonal_pieces[1], 3 * rows, rows)], sends=[1, 2, 3], cost=SHORT
+        [(final, 1)], partial=[(3, diagonal_pieces[1], 3 * rows, rows)], sends=[1, 2, 3], cost=SHORT
     )
 
-    from_core = swap(sent[0], 0, 1)
-    from_side = swap(sent[1], 1, 0)
-    from_diagonal = swap(sent[2], 1, 1)
+    def returned(arrays):
+        return [
+            swap(array, side, bit) for array, (side, bit) in zip(arrays, ((0, 1), (1, 0), (1, 1)))
+        ]
+
+    early = returned(sent)
+    place = places - CORES
+    own_late, *sent = pl.pallas_call(
+        functools.partial(late_kernel, rank, pairs, window, place, QUAD),
+        out_shape=[pltpu.VMEM((window, LANES), jnp.float32)]
+        + [pltpu.VMEM((window, LANES), jnp.bfloat16)] * (QUAD - 1),
+        in_specs=[SMEM] * (1 + QUAD) + [VMEM] * 2,
+        out_specs=[VMEM] * QUAD,
+        compiler_params=pltpu.CompilerParams(vmem_limit_bytes=8 * MIB),
+        cost_estimate=QUICK,
+    )(bases, *[starts[g] for g in range(QUAD)], in_vmem(state[0]), held[final, 0])
+    late = returned(sent)
+    *early, own_late = tie(*early, own_late)
+    out, turned = pl.pallas_call(
+        functools.partial(blocks_kernel, rank),
+        out_shape=[
+            jax.ShapeDtypeStruct((SEG_DEV, experts, rank * rank), jnp.bfloat16),
+            pltpu.VMEM((rank, pairs), jnp.float32),
+        ],
+        in_specs=[VMEM] * 7,
+        out_specs=[VMEM] * 2,
+        scratch_shapes=[pltpu.VMEM((rank, experts, tokens), jnp.float32)],
+        compiler_params=pltpu.CompilerParams(vmem_limit_bytes=32 * MIB),
+        cost_estimate=QUICK,
+    )(by_rank, basis, in_vmem(order_back), in_vmem(state[2]), *early)
+    count = 2 * CORES * exp_here
     return pl.pallas_call(
-        functools.partial(blocks_kernel, tops, rank),
-        out_shape=jax.ShapeDtypeStruct((SEG_DEV, experts, rank * rank), jnp.bfloat16),
-        in_specs=[VMEM] * 7,
-        out_specs=VMEM,
+        functools.partial(last_kernel, rank, place, count, exp_here),
+        out_shape=jax.ShapeDtypeStruct(out.shape, out.dtype),
+        in_specs=[SMEM] * 2 + [VMEM] * 8 + [HBM],
+        out_specs=HBM,
         scratch_shapes=[
             pltpu.VMEM((rank, pairs), jnp.float32),
-            pltpu.VMEM((rank, experts, tokens), jnp.float32),
+            pltpu.VMEM((rank, count, tokens), jnp.float32),
+            pltpu.VMEM((SEG_DEV, count, rank * rank), jnp.bfloat16),
+            pltpu.SemaphoreType.DMA,
         ],
-        compiler_params=pltpu.CompilerParams(vmem_limit_bytes=32 * MIB),
+        input_output_aliases={10: 0},
+        compiler_params=pltpu.CompilerParams(vmem_limit_bytes=16 * MIB),
         cost_estimate=QUICK,
-    )(by_rank, basis, in_vmem(order_back), in_vmem(state[2]), from_core, from_side, from_diagonal)
+    )(bases, own_starts, by_rank, basis, in_vmem(order_back), in_vmem(turned), own_late, *late, out)
 
 
 def solution(mesh):

time: 82.3 us -> 77.1 us (0.937)
  waiting for transfers between devices: 35.3 us -> 24.9 us
  starting transfers between devices: 18.7 us -> 21.7 us
  Pallas kernels: 27.2 us -> 29.1 us
    ppermute x13 -> x16, waiting for transfers between devices: 28.2 us -> 22.8 us  [swap(): return lax.ppermute(array, BOTH, table)]
    ppermute x4, waiting for transfers between devices: 7.05 us -> 2.1 us  [along(): return lax.ppermute(array, 'expert', pairs_of)]
    pallas_call x1 -> x3, Pallas kernels: 3.45 us -> 6.83 us  [the longest x1 3.46 us: local(): pl.pallas_call(functools.partial(blocks_kernel, rank), out_shape=[jax.Sha...]
    ppermute x13 -> x16, starting transfers between devices: 13.8 us -> 16.8 us  [swap(): return lax.ppermute(array, BOTH, table)]
    pallas_call x4 -> x3, Pallas kernels: 11.9 us -> 10.5 us  [accumulate(): pl.pallas_call(functools.partial(partial_kernel, rank, pairs, window, [(f...]
  transfers between devices with their start and end apart: 17 -> 20, of which waited for: 7 -> 6; matrix products, arithmetic and copies ran while one was open for 0% -> 0% of each run, Pallas kernels for 23% -> 34%
where the time goes in v10:
time: 77.1 us; the launch traced here: 76.7 us
  Pallas kernels  29.1 us (38%)
  waiting for transfers between devices  24.9 us (32%)
  starting transfers between devices  21.7 us (28%)
    ppermute x16, waiting for transfers between devices, swap(): return lax.ppermute(array, BOTH, table)  22.8 us
    ppermute x16, starting transfers between devices, swap(): return lax.ppermute(array, BOTH, table)  16.8 us
    pallas_call x3, Pallas kernels, accumulate(): pl.pallas_call(functools.partial(partial_kernel, rank, pairs, window, [(f...  10.5 us
    ppermute x4, starting transfers between devices, along(): return lax.ppermute(array, 'expert', pairs_of)  4.9 us
    pallas_call x3, Pallas kernels, permuted(): pl.pallas_call(functools.partial(permute_kernel, plan), out_shape=[rows_s...  4.33 us
    pallas_call x1, Pallas kernels, local(): pl.pallas_call(functools.partial(blocks_kernel, rank), out_shape=[jax.Sha...  3.46 us
    pallas_call x1, Pallas kernels, local(): pl.pallas_call(sort_kernel, out_shape=[pltpu.VMEM(out_grads.shape, jnp.bf...  3.37 us
    pallas_call x1, Pallas kernels, local(): pl.pallas_call(basis_kernel, out_shape=[pltpu.VMEM((2 * tokens, SEG_DEV *...  2.79 us
  transfers between devices with their start and end apart: 20, of which 6 were waited for; matrix products, arithmetic and copies ran while one was open for 0% of the time, Pallas kernels for 34%

profile of v10, /device:TPU:1, one launch (start us, length us, event | category | flops | bytes accessed | tf_op | source)
XLA Modules:
  0.0 76.7 jit_solution(17899397583869416623)
XLA Ops:
  0.0 1.3 %shard_map.73 = (bf16[256,512]{1,0:T(8,128)(2,1)S(1)}, bf16[256,512]{1,0:T(8,128)(2,1)S(1)}) custom-call(bf16[256,2048]{1,0:T(8,128)(2,1)} %bitcast.8), custom_call_target="tpu_custom_call" | custom-call | flops 1 | bytes 1 | tf_op jit(solution)/shard_map/pallas_call | solution.py:524
  1.3 0.1 collective-permute-start
  1.4 0.7 copy-done.1
  2.1 3.4 %shard_map.74 = (bf16[128,8,2048]{2,1,0:T(8,128)(2,1)S(1)}, s32[1,128]{1,0:T(1,128)S(1)}, bf16[16,512]{1,0:T(8,128)(2,1)S(1)}, bf16[1024,1024]{1,0:T(8,128)(2,1)S(1)}, bf16[528,512]{1,0:T(8,128)(2,1)S(1)}) custom-call(s32[8,128]{1,0:T(8,128)S(1)} %bitcast.3, bf16[128,8,2048]{2,1,0:T(8,128)(2,1)} %grads_ref.1), custom_call_target="tpu_custom_call" | custom-call | flops 1 | bytes 1 | tf_op jit(solution)/shard_map/pallas_call | solution.py:536
  5.5 2.7 %collective-permute-start.3 = (bf16[528,512]{1,0:T(8,128)(2,1)S(1)}, bf16[528,512]{1,0:T(8,128)(2,1)S(1)}, u32[]{:S(2)}, u32[]{:S(2)}) collective-permute-start(bf16[528,512]{1,0:T(8,128)(2,1)S(1)} %get-tuple-element.74), channel_id=1, source_target_pairs={{0,16},{1,17},{2,18},{3,19},{4,20},{5,21},{6,22},{7,23},{8,24},{9,... | collective-permute-start | bytes 1622024 | tf_op jit(solution)/shard_map/ppermute | solution.py:488
  8.2 0.0 collective-permute-done.two_ref
  8.2 1.3 %collective-permute-start.2 = (bf16[512,512]{1,0:T(8,128)(2,1)S(1)}, bf16[512,512]{1,0:T(8,128)(2,1)S(1)}, u32[]{:S(2)}, u32[]{:S(2)}) collective-permute-start(bf16[512,512]{1,0:T(8,128)(2,1)S(1)} %shard_map.75.refs_8_), channel_id=1, source_target_pairs={{0,2},{1,3},{2,0},{3,1},{4,6},{5,7},{6,4},{7,5},{8,10},{9,11},{10,... | collective-permute-start | bytes 1572872 | tf_op jit(solution)/shard_map/ppermute | solution.py:488
  9.5 1.3 %collective-permute-start.1 = (bf16[512,512]{1,0:T(8,128)(2,1)S(1)}, bf16[512,512]{1,0:T(8,128)(2,1)S(1)}, u32[]{:S(2)}, u32[]{:S(2)}) collective-permute-start(bf16[512,512]{1,0:T(8,128)(2,1)S(1)} %shard_map.75.refs_8_), channel_id=1, source_target_pairs={{0,4},{1,5},{2,6},{3,7},{4,12},{5,13},{6,14},{7,15},{8,0},{9,1},{1... | collective-permute-start | bytes 1572872 | tf_op jit(solution)/shard_map/ppermute | solution.py:493
  10.8 0.7 shard_map.76
  11.6 2.4 %shard_map.77 = (bf16[1024,512]{1,0:T(8,128)(2,1)S(1)}, bf16[528,512]{1,0:T(8,128)(2,1)S(1)}, bf16[512,512]{1,0:T(8,128)(2,1)S(1)}) custom-call(bf16[1024,1024]{1,0:T(8,128)(2,1)S(1)} %get-tuple-element.71.order_ref, bf16[16,512]{1,0:T(8,128)(2,1)S(1)} %get-tuple-element.67.head_ref, bf16[128,8,2048]{2,1,0:T(8,128)(2,1)S(1)} %get-tuple-element.68.grads_ref), custom_call_target="tpu_custom_call" | custom-call | flops 1 | bytes 1 | tf_op jit(solution)/shard_map/pallas_call | solution.py:565
  13.9 0.0 copy-start.3
  13.9 0.9 %collective-permute-start.6 = (bf16[528,512]{1,0:T(8,128)(2,1)S(1)}, bf16[528,512]{1,0:T(8,128)(2,1)S(1)}, u32[]{:S(2)}, u32[]{:S(2)}) collective-permute-start(bf16[528,512]{1,0:T(8,128)(2,1)S(1)} %get-tuple-element.83), channel_id=1, source_target_pairs={{0,1},{1,0},{2,3},{3,2},{4,5},{5,4},{6,7},{7,6},{8,9},{9,8},{10,11... | collective-permute-start | bytes 1622024 | tf_op jit(solution)/shard_map/ppermute | solution.py:488
  14.8 0.3 collective-permute-start.12
  15.1 1.3 %shard_map.78 = (bf16[784,512]{1,0:T(8,128)(2,1)S(1)}, bf16[256,512]{1,0:T(8,128)(2,1)S(1)}) custom-call(bf16[1024,1024]{1,0:T(8,128)(2,1)S(1)} %get-tuple-element.71.order_ref, bf16[16,512]{1,0:T(8,128)(2,1)S(1)} %get-tuple-element.67.head_ref, bf16[128,8,2048]{2,1,0:T(8,128)(2,1)S(1)} %get-tuple-element.68.grads_ref), custom_call_target="tpu_custom_call" | custom-call | flops 1 | bytes 1 | tf_op jit(solution)/shard_map/pallas_call | solution.py:565
  16.4 4.4 %collective-permute-done.3.refs_6_ = bf16[528,512]{1,0:T(8,128)(2,1)S(1)} collective-permute-done((bf16[528,512]{1,0:T(8,128)(2,1)S(1)}, bf16[528,512]{1,0:T(8,128)(2,1)S(1)}, u32[]{:S(2)}, u32[]{:S(2)}) %collective-permute-start.3) | collective-permute-done | bytes 540704 | tf_op jit(solution)/shard_map/ppermute | solution.py:488
  20.8 2.3 %collective-permute-start.7 = (bf16[784,512]{1,0:T(8,128)(2,1)S(1)}, bf16[784,512]{1,0:T(8,128)(2,1)S(1)}, u32[]{:S(2)}, u32[]{:S(2)}) collective-permute-start(bf16[784,512]{1,0:T(8,128)(2,1)S(1)} %get-tuple-element.85), channel_id=1, source_target_pairs={{0,17},{1,16},{2,19},{3,18},{4,21},{5,20},{6,23},{7,22},{8,25},{9,... | collective-permute-start | bytes 2408456 | tf_op jit(solution)/shard_map/ppermute | solution.py:488
  23.1 2.8 %shard_map.79 = (bf16[256,256]{1,0:T(8,128)(2,1)S(1)}, bf16[1024,1024]{1,0:T(8,128)(2,1)S(1)}) custom-call(bf16[128,7168]{1,0:T(8,128)(2,1)} %hidden_ref.1, bf16[64,7168]{1,0:T(8,128)(2,1)} %proj_ref.1, s32[1,128]{1,0:T(1,128)S(1)} %bitcast.7, s32[8,128]{1,0:T(8,128)S(1)} %bitcast.4), custom_call_target="tpu_custom_call" | custom-call | flops 1 | bytes 1 | tf_op jit(solution)/shard_map/pallas_call | solution.py:594
  25.9 0.0 collective-permute-done.2.refs_11_
  26.0 0.0 collective-permute-done.1.refs_9_
  26.0 1.3 %collective-permute-start.5 = (bf16[512,512]{1,0:T(8,128)(2,1)S(1)}, bf16[512,512]{1,0:T(8,128)(2,1)S(1)}, u32[]{:S(2)}, u32[]{:S(2)}) collective-permute-start(bf16[512,512]{1,0:T(8,128)(2,1)S(1)} %collective-permute-done.1.refs_9_), channel_id=1, source_target_pairs={{0,2},{1,3},{2,0},{3,1},{4,6},{5,7},{6,4},{7,5},{8,10},{9,11},{10,... | collective-permute-start | bytes 1572872 | tf_op jit(solution)/shard_map/ppermute | solution.py:488
  27.3 1.3 %collective-permute-start.4 = (bf16[512,512]{1,0:T(8,128)(2,1)S(1)}, bf16[512,512]{1,0:T(8,128)(2,1)S(1)}, u32[]{:S(2)}, u32[]{:S(2)}) collective-permute-start(bf16[512,512]{1,0:T(8,128)(2,1)S(1)} %collective-permute-done.1.refs_9_), channel_id=1, source_target_pairs={{0,4},{1,5},{2,6},{3,7},{4,12},{5,13},{6,14},{7,15},{8,0},{9,1},{1... | collective-permute-start | bytes 1572872 | tf_op jit(solution)/shard_map/ppermute | solution.py:493
  28.6 0.0 collective-permute-done.6.refs_4_
  28.6 11.2 %collective-permute-done.5.refs_12_ = bf16[512,512]{1,0:T(8,128)(2,1)S(1)} collective-permute-done((bf16[512,512]{1,0:T(8,128)(2,1)S(1)}, bf16[512,512]{1,0:T(8,128)(2,1)S(1)}, u32[]{:S(2)}, u32[]{:S(2)}) %collective-permute-start.5) | collective-permute-done | bytes 524320 | tf_op jit(solution)/shard_map/ppermute | solution.py:488
  39.8 2.3 %collective-permute-start.9 = (bf16[512,512]{1,0:T(8,128)(2,1)S(1)}, bf16[512,512]{1,0:T(8,128)(2,1)S(1)}, u32[]{:S(2)}, u32[]{:S(2)}) collective-permute-start(bf16[512,512]{1,0:T(8,128)(2,1)S(1)} %collective-permute-done.2.refs_11_), channel_id=1, source_target_pairs={{0,8},{1,9},{2,10},{3,11},{4,0},{5,1},{6,2},{7,3},{8,12},{9,13},{1... | collective-permute-start | bytes 1572872 | tf_op jit(solution)/shard_map/ppermute | solution.py:493
  42.1 0.0 collective-permute-done.4.refs_10_
  42.1 1.2 %collective-permute-start.10 = (bf16[512,512]{1,0:T(8,128)(2,1)S(1)}, bf16[512,512]{1,0:T(8,128)(2,1)S(1)}, u32[]{:S(2)}, u32[]{:S(2)}) collective-permute-start(bf16[512,512]{1,0:T(8,128)(2,1)S(1)} %collective-permute-done.4.refs_10_), channel_id=1, source_target_pairs={{0,2},{1,3},{2,0},{3,1},{4,6},{5,7},{6,4},{7,5},{8,10},{9,11},{10,... | collective-permute-start | bytes 1572872 | tf_op jit(solution)/shard_map/ppermute | solution.py:488
  43.3 0.0 collective-permute-done.12.refs_7_
  43.3 1.3 %collective-permute-start.8 = (bf16[256,512]{1,0:T(8,128)(2,1)S(1)}, bf16[256,512]{1,0:T(8,128)(2,1)S(1)}, u32[]{:S(2)}, u32[]{:S(2)}) collective-permute-start(bf16[256,512]{1,0:T(8,128)(2,1)S(1)} %get-tuple-element.77), channel_id=1, source_target_pairs={{0,17},{1,16},{2,19},{3,18},{4,21},{5,20},{6,23},{7,22},{8,25},{9,... | collective-permute-start | bytes 786440 | tf_op jit(solution)/shard_map/ppermute | solution.py:488
  44.6 0.0 collective-permute-done.11.refs_5_
  44.6 0.0 collective-permute-start.16
  44.6 4.0 %shard_map.80 = (bf16[4096,512]{1,0:T(8,128)(2,1)S(1)}, bf16[16,256,512]{2,1,0:T(8,128)(2,1)S(1)}, f32[4096,128]{1,0:T(8,128)S(1)}) custom-call(s32[16,16]{1,0:T(8,128)S(1)} %copy-done, s32[1,128]{1,0:T(1,128)S(1)} %get-tuple-element.60.refs_0_.starts_ref, s32[1,128]{1,0:T(1,128)S(1)} %slice_add_fusion.2.refs_1_, s32[1,128]{1,0:T(1,128)S(1)} %slice_add_fusion.1.refs_2_, ...), custom_call_target="tpu_custom_call" | custom-call | flops 1 | bytes 1 | tf_op jit(solution)/shard_map/pallas_call | solution.py:298
  48.7 1.0 %collective-permute-done.7.refs_4_ = bf16[784,512]{1,0:T(8,128)(2,1)S(1)} collective-permute-done((bf16[784,512]{1,0:T(8,128)(2,1)S(1)}, bf16[784,512]{1,0:T(8,128)(2,1)S(1)}, u32[]{:S(2)}, u32[]{:S(2)}) %collective-permute-start.7) | collective-permute-done | bytes 802848 | tf_op jit(solution)/shard_map/ppermute | solution.py:488
  49.7 5.4 %collective-permute-done.10.refs_5_ = bf16[512,512]{1,0:T(8,128)(2,1)S(1)} collective-permute-done((bf16[512,512]{1,0:T(8,128)(2,1)S(1)}, bf16[512,512]{1,0:T(8,128)(2,1)S(1)}, u32[]{:S(2)}, u32[]{:S(2)}) %collective-permute-start.10) | collective-permute-done | bytes 524320 | tf_op jit(solution)/shard_map/ppermute | solution.py:488
  55.1 3.5 %shard_map.81 = (bf16[4096,512]{1,0:T(8,128)(2,1)S(1)}, bf16[16,256,512]{2,1,0:T(8,128)(2,1)S(1)}, f32[4096,128]{1,0:T(8,128)S(1)}) custom-call(s32[16,16]{1,0:T(8,128)S(1)} %copy-done, s32[1,128]{1,0:T(1,128)S(1)} %get-tuple-element.60.refs_0_.starts_ref, ...), custom_call_target="tpu_custom_call", output_to_operand_aliasing={{0}: (7, {}), {1}: (8, {}), {2}: (9, {})} | custom-call | flops 1 | bytes 1 | tf_op jit(solution)/shard_map/pallas_call | solution.py:298
  58.6 0.0 collective-permute-done.9.refs_5_
  58.6 3.0 %shard_map.82 = (bf16[4096,512]{1,0:T(8,128)(2,1)S(1)}, bf16[16,256,512]{2,1,0:T(8,128)(2,1)S(1)}, f32[4096,128]{1,0:T(8,128)S(1)}, bf16[512,128]{1,0:T(8,128)(2...) custom-call(s32[16,16]{1,0:T(8,128)S(1)} %copy-done, ...), custom_call_target="tpu_custom_call", output_to_operand_aliasing={{0}: (7, {}), {1}: (8, {}), {2}: (9, {})} | custom-call | flops 1000000000 | bytes 1 | tf_op jit(solution)/shard_map/pallas_call | solution.py:298
  61.7 0.0 copy-start.2
  61.7 1.4 %collective-permute-start.13 = (bf16[512,128]{1,0:T(8,128)(2,1)S(1)}, bf16[512,128]{1,0:T(8,128)(2,1)S(1)}, u32[]{:S(2)}, u32[]{:S(2)}) collective-permute-start(bf16[512,128]{1,0:T(8,128)(2,1)S(1)} %get-tuple-element.97), channel_id=1, source_target_pairs={{0,1},{1,0},{2,3},{3,2},{4,5},{5,4},{6,7},{7,6},{8,9},{9,8},{10,11... | collective-permute-start | bytes 393224 | tf_op jit(solution)/shard_map/ppermute | solution.py:488
  63.0 0.2 collective-permute-start.14
  63.2 1.6 %collective-permute-start.15 = (bf16[512,128]{1,0:T(8,128)(2,1)S(1)}, bf16[512,128]{1,0:T(8,128)(2,1)S(1)}, u32[]{:S(2)}, u32[]{:S(2)}) collective-permute-start(bf16[512,128]{1,0:T(8,128)(2,1)S(1)} %get-tuple-element.99), channel_id=1, source_target_pairs={{0,17},{1,16},{2,19},{3,18},{4,21},{5,20},{6,23},{7,22},{8,25},{9,... | collective-permute-start | bytes 393224 | tf_op jit(solution)/shard_map/ppermute | solution.py:488
  64.8 2.1 %collective-permute-done.16.refs_5_ = bf16[512,512]{1,0:T(8,128)(2,1)S(1)} collective-permute-done((bf16[512,512]{1,0:T(8,128)(2,1)S(1)}, bf16[512,512]{1,0:T(8,128)(2,1)S(1)}, u32[]{:S(2)}, u32[]{:S(2)}) %collective-permute-start.16) | collective-permute-done | bytes 524320 | tf_op jit(solution)/shard_map/ppermute | solution.py:493
  66.9 1.2 %shard_map.83 = (f32[112,128]{1,0:T(8,128)S(1)}, bf16[112,128]{1,0:T(8,128)(2,1)S(1)}, bf16[112,128]{1,0:T(8,128)(2,1)S(1)}, bf16[112,128]{1,0:T(8,128)(2,1)S(1)}) custom-call(s32[16,16]{1,0:T(8,128)S(1)} %copy-done, s32[1,128]{1,0:T(1,128)S(1)} %get-tuple-element.60.refs_0_.starts_ref, s32[1,128]{1,0:T(1,128)S(1)} %slice_add_fusion.2.refs_1_, ...), custom_call_target="tpu_custom_call" | custom-call | flops 1 | bytes 1 | tf_op jit(solution)/shard_map/pallas_call | solution.py:689
  68.1 0.5 collective-permute-start.17
  68.6 0.2 collective-permute-start.18
  68.7 1.6 %collective-permute-start.19 = (bf16[112,128]{1,0:T(8,128)(2,1)S(1)}, bf16[112,128]{1,0:T(8,128)(2,1)S(1)}, u32[]{:S(2)}, u32[]{:S(2)}) collective-permute-start(bf16[112,128]{1,0:T(8,128)(2,1)S(1)} %get-tuple-element.109), channel_id=1, source_target_pairs={{0,17},{1,16},{2,19},{3,18},{4,21},{5,20},{6,23},{7,22},{8,25},{9,... | collective-permute-start | bytes 86024 | tf_op jit(solution)/shard_map/ppermute | solution.py:488
  70.3 0.8 %collective-permute-done.15.d_ref = bf16[512,128]{1,0:T(8,128)(2,1)S(1)} collective-permute-done((bf16[512,128]{1,0:T(8,128)(2,1)S(1)}, bf16[512,128]{1,0:T(8,128)(2,1)S(1)}, u32[]{:S(2)}, u32[]{:S(2)}) %collective-permute-start.15) | collective-permute-done | bytes 131104 | tf_op jit(solution)/shard_map/ppermute | solution.py:488
  71.1 3.5 %shard_map.84 = (bf16[2,64,4096]{2,1,0:T(8,128)(2,1)}, f32[64,1024]{1,0:T(8,128)S(1)}) custom-call(s32[8,128]{1,0:T(8,128)S(1)} %bitcast.5, bf16[256,256]{1,0:T(8,128)(2,1)S(1)} %get-tuple-element.81.basis_ref, bf16[1024,1024]{1,0:T(8,128)(2,1)S(1)} %get-tuple-element.82.order_ref, f32[4096,128]{1,0:T(8,128)S(1)} %get-tuple-element.96.total_ref, ...), custom_call_target="tpu_custom_call" | custom-call | flops 1 | bytes 1 | tf_op jit(solution)/shard_map/pallas_call | solution.py:700
  74.6 2.1 %shard_map.85 = bf16[2,64,4096]{2,1,0:T(8,128)(2,1)} custom-call(s32[16,16]{1,0:T(8,128)S(1)} %copy-done, s32[1,128]{1,0:T(1,128)S(1)} %get-tuple-element.60.refs_0_.starts_ref, s32[8,128]{1,0:T(8,128)S(1)} %bitcast.6, bf16[256,256]{1,0:T(8,128)(2,1)S(1)} %get-tuple-element.81.basis_ref, ...), custom_call_target="tpu_custom_call", output_to_operand_aliasing={{}: (10, {})} | custom-call | flops 1 | bytes 1 | tf_op jit(solution)/shard_map/pallas_call | solution.py:713
  (19 shorter events, 0.1 us)
Async XLA Ops:
  1.3 6.9 %collective-permute-start = (bf16[256,512]{1,0:T(8,128)(2,1)S(1)}, bf16[256,512]{1,0:T(8,128)(2,1)S(1)}, u32[]{:S(2)}, u32[]{:S(2)}) collective-permute-start(bf16[256,512]{1,0:T(8,128)(2,1)S(1)} %get-tuple-element.58), channel_id=1, source_target_pairs={{0,1},{1,0},{2,3},{3,2},{4,5},{5,4},{6,7},{7,6},{8,9},{9,8},{10,11... | collective-permute-start | bytes 786440 | tf_op jit(solution)/shard_map/ppermute | solution.py:488
  1.4 0.7 copy-start.1
  5.5 15.4 %collective-permute-start.3 = (bf16[528,512]{1,0:T(8,128)(2,1)S(1)}, bf16[528,512]{1,0:T(8,128)(2,1)S(1)}, u32[]{:S(2)}, u32[]{:S(2)}) collective-permute-start(bf16[528,512]{1,0:T(8,128)(2,1)S(1)} %get-tuple-element.74), channel_id=1, source_target_pairs={{0,16},{1,17},{2,18},{3,19},{4,20},{5,21},{6,22},{7,23},{8,24},{9,... | collective-permute-start | bytes 1622024 | tf_op jit(solution)/shard_map/ppermute | solution.py:488
  8.2 17.7 %collective-permute-start.2 = (bf16[512,512]{1,0:T(8,128)(2,1)S(1)}, bf16[512,512]{1,0:T(8,128)(2,1)S(1)}, u32[]{:S(2)}, u32[]{:S(2)}) collective-permute-start(bf16[512,512]{1,0:T(8,128)(2,1)S(1)} %shard_map.75.refs_8_), channel_id=1, source_target_pairs={{0,2},{1,3},{2,0},{3,1},{4,6},{5,7},{6,4},{7,5},{8,10},{9,11},{10,... | collective-permute-start | bytes 1572872 | tf_op jit(solution)/shard_map/ppermute | solution.py:488
  9.5 16.4 %collective-permute-start.1 = (bf16[512,512]{1,0:T(8,128)(2,1)S(1)}, bf16[512,512]{1,0:T(8,128)(2,1)S(1)}, u32[]{:S(2)}, u32[]{:S(2)}) collective-permute-start(bf16[512,512]{1,0:T(8,128)(2,1)S(1)} %shard_map.75.refs_8_), channel_id=1, source_target_pairs={{0,4},{1,5},{2,6},{3,7},{4,12},{5,13},{6,14},{7,15},{8,0},{9,1},{1... | collective-permute-start | bytes 1572872 | tf_op jit(solution)/shard_map/ppermute | solution.py:493
  13.9 9.2 %copy-start.3 = (s32[128]{0:T(128)S(1)}, s32[128]{0:T(128)}, u32[]{:S(2)}) copy-start(s32[128]{0:T(128)} %param.10) | copy-start | bytes 1540
  13.9 14.6 %collective-permute-start.6 = (bf16[528,512]{1,0:T(8,128)(2,1)S(1)}, bf16[528,512]{1,0:T(8,128)(2,1)S(1)}, u32[]{:S(2)}, u32[]{:S(2)}) collective-permute-start(bf16[528,512]{1,0:T(8,128)(2,1)S(1)} %get-tuple-element.83), channel_id=1, source_target_pairs={{0,1},{1,0},{2,3},{3,2},{4,5},{5,4},{6,7},{7,6},{8,9},{9,8},{10,11... | collective-permute-start | bytes 1622024 | tf_op jit(solution)/shard_map/ppermute | solution.py:488
  14.8 28.5 %collective-permute-start.12 = (bf16[512,512]{1,0:T(8,128)(2,1)S(1)}, bf16[512,512]{1,0:T(8,128)(2,1)S(1)}, u32[]{:S(2)}, u32[]{:S(2)}) collective-permute-start(bf16[512,512]{1,0:T(8,128)(2,1)S(1)} %shard_map.76), channel_id=1, source_target_pairs={{0,16},{1,17},{2,18},{3,19},{4,20},{5,21},{6,22},{7,23},{8,24},{9,... | collective-permute-start | bytes 1572872 | tf_op jit(solution)/shard_map/ppermute | solution.py:488
  15.1 29.5 %copy-start = (s32[16,16]{1,0:T(8,128)S(1)}, s32[16,16]{1,0:T(8,128)}, u32[]{:S(2)}) copy-start(s32[16,16]{1,0:T(8,128)} %constant.4.clone.bases_ref) | copy-start | bytes 3076
  20.8 28.8 %collective-permute-start.7 = (bf16[784,512]{1,0:T(8,128)(2,1)S(1)}, bf16[784,512]{1,0:T(8,128)(2,1)S(1)}, u32[]{:S(2)}, u32[]{:S(2)}) collective-permute-start(bf16[784,512]{1,0:T(8,128)(2,1)S(1)} %get-tuple-element.85), channel_id=1, source_target_pairs={{0,17},{1,16},{2,19},{3,18},{4,21},{5,20},{6,23},{7,22},{8,25},{9,... | collective-permute-start | bytes 2408456 | tf_op jit(solution)/shard_map/ppermute | solution.py:488
  26.0 13.8 %collective-permute-start.5 = (bf16[512,512]{1,0:T(8,128)(2,1)S(1)}, bf16[512,512]{1,0:T(8,128)(2,1)S(1)}, u32[]{:S(2)}, u32[]{:S(2)}) collective-permute-start(bf16[512,512]{1,0:T(8,128)(2,1)S(1)} %collective-permute-done.1.refs_9_), channel_id=1, source_target_pairs={{0,2},{1,3},{2,0},{3,1},{4,6},{5,7},{6,4},{7,5},{8,10},{9,11},{10,... | collective-permute-start | bytes 1572872 | tf_op jit(solution)/shard_map/ppermute | solution.py:488
  27.3 14.8 %collective-permute-start.4 = (bf16[512,512]{1,0:T(8,128)(2,1)S(1)}, bf16[512,512]{1,0:T(8,128)(2,1)S(1)}, u32[]{:S(2)}, u32[]{:S(2)}) collective-permute-start(bf16[512,512]{1,0:T(8,128)(2,1)S(1)} %collective-permute-done.1.refs_9_), channel_id=1, source_target_pairs={{0,4},{1,5},{2,6},{3,7},{4,12},{5,13},{6,14},{7,15},{8,0},{9,1},{1... | collective-permute-start | bytes 1572872 | tf_op jit(solution)/shard_map/ppermute | solution.py:493
  28.6 16.1 %collective-permute-start.11 = (bf16[512,512]{1,0:T(8,128)(2,1)S(1)}, bf16[512,512]{1,0:T(8,128)(2,1)S(1)}, u32[]{:S(2)}, u32[]{:S(2)}) collective-permute-start(bf16[512,512]{1,0:T(8,128)(2,1)S(1)} %get-tuple-element.88), channel_id=1, source_target_pairs={{0,1},{1,0},{2,3},{3,2},{4,5},{5,4},{6,7},{7,6},{8,9},{9,8},{10,11... | collective-permute-start | bytes 1572872 | tf_op jit(solution)/shard_map/ppermute | solution.py:488
  39.8 18.9 %collective-permute-start.9 = (bf16[512,512]{1,0:T(8,128)(2,1)S(1)}, bf16[512,512]{1,0:T(8,128)(2,1)S(1)}, u32[]{:S(2)}, u32[]{:S(2)}) collective-permute-start(bf16[512,512]{1,0:T(8,128)(2,1)S(1)} %collective-permute-done.2.refs_11_), channel_id=1, source_target_pairs={{0,8},{1,9},{2,10},{3,11},{4,0},{5,1},{6,2},{7,3},{8,12},{9,13},{1... | collective-permute-start | bytes 1572872 | tf_op jit(solution)/shard_map/ppermute | solution.py:493
  42.1 13.0 %collective-permute-start.10 = (bf16[512,512]{1,0:T(8,128)(2,1)S(1)}, bf16[512,512]{1,0:T(8,128)(2,1)S(1)}, u32[]{:S(2)}, u32[]{:S(2)}) collective-permute-start(bf16[512,512]{1,0:T(8,128)(2,1)S(1)} %collective-permute-done.4.refs_10_), channel_id=1, source_target_pairs={{0,2},{1,3},{2,0},{3,1},{4,6},{5,7},{6,4},{7,5},{8,10},{9,11},{10,... | collective-permute-start | bytes 1572872 | tf_op jit(solution)/shard_map/ppermute | solution.py:488
  43.3 15.3 %collective-permute-start.8 = (bf16[256,512]{1,0:T(8,128)(2,1)S(1)}, bf16[256,512]{1,0:T(8,128)(2,1)S(1)}, u32[]{:S(2)}, u32[]{:S(2)}) collective-permute-start(bf16[256,512]{1,0:T(8,128)(2,1)S(1)} %get-tuple-element.77), channel_id=1, source_target_pairs={{0,17},{1,16},{2,19},{3,18},{4,21},{5,20},{6,23},{7,22},{8,25},{9,... | collective-permute-start | bytes 786440 | tf_op jit(solution)/shard_map/ppermute | solution.py:488
  44.6 22.2 %collective-permute-start.16 = (bf16[512,512]{1,0:T(8,128)(2,1)S(1)}, bf16[512,512]{1,0:T(8,128)(2,1)S(1)}, u32[]{:S(2)}, u32[]{:S(2)}) collective-permute-start(bf16[512,512]{1,0:T(8,128)(2,1)S(1)} %collective-permute-done.4.refs_10_), channel_id=1, source_target_pairs={{0,4},{1,5},{2,6},{3,7},{4,12},{5,13},{6,14},{7,15},{8,0},{9,1},{1... | collective-permute-start | bytes 1572872 | tf_op jit(solution)/shard_map/ppermute | solution.py:493
  61.7 9.5 %copy-start.2 = (s32[128,8]{0,1:T(8,128)S(1)}, s32[128,8]{0,1:T(8,128)}, u32[]{:S(2)}) copy-start(s32[128,8]{0,1:T(8,128)} %param.9) | copy-start | bytes 12292
  61.7 7.1 %collective-permute-start.13 = (bf16[512,128]{1,0:T(8,128)(2,1)S(1)}, bf16[512,128]{1,0:T(8,128)(2,1)S(1)}, u32[]{:S(2)}, u32[]{:S(2)}) collective-permute-start(bf16[512,128]{1,0:T(8,128)(2,1)S(1)} %get-tuple-element.97), channel_id=1, source_target_pairs={{0,1},{1,0},{2,3},{3,2},{4,5},{5,4},{6,7},{7,6},{8,9},{9,8},{10,11... | collective-permute-start | bytes 393224 | tf_op jit(solution)/shard_map/ppermute | solution.py:488
  63.0 7.3 %collective-permute-start.14 = (bf16[512,128]{1,0:T(8,128)(2,1)S(1)}, bf16[512,128]{1,0:T(8,128)(2,1)S(1)}, u32[]{:S(2)}, u32[]{:S(2)}) collective-permute-start(bf16[512,128]{1,0:T(8,128)(2,1)S(1)} %get-tuple-element.98), channel_id=1, source_target_pairs={{0,16},{1,17},{2,18},{3,19},{4,20},{5,21},{6,22},{7,23},{8,24},{9,... | collective-permute-start | bytes 393224 | tf_op jit(solution)/shard_map/ppermute | solution.py:488
  63.2 7.9 %collective-permute-start.15 = (bf16[512,128]{1,0:T(8,128)(2,1)S(1)}, bf16[512,128]{1,0:T(8,128)(2,1)S(1)}, u32[]{:S(2)}, u32[]{:S(2)}) collective-permute-start(bf16[512,128]{1,0:T(8,128)(2,1)S(1)} %get-tuple-element.99), channel_id=1, source_target_pairs={{0,17},{1,16},{2,19},{3,18},{4,21},{5,20},{6,23},{7,22},{8,25},{9,... | collective-permute-start | bytes 393224 | tf_op jit(solution)/shard_map/ppermute | solution.py:488
  68.1 6.5 %collective-permute-start.17 = (bf16[112,128]{1,0:T(8,128)(2,1)S(1)}, bf16[112,128]{1,0:T(8,128)(2,1)S(1)}, u32[]{:S(2)}, u32[]{:S(2)}) collective-permute-start(bf16[112,128]{1,0:T(8,128)(2,1)S(1)} %get-tuple-element.107), channel_id=1, source_target_pairs={{0,1},{1,0},{2,3},{3,2},{4,5},{5,4},{6,7},{7,6},{8,9},{9,8},{10,11... | collective-permute-start | bytes 86024 | tf_op jit(solution)/shard_map/ppermute | solution.py:488
  68.6 6.0 %collective-permute-start.18 = (bf16[112,128]{1,0:T(8,128)(2,1)S(1)}, bf16[112,128]{1,0:T(8,128)(2,1)S(1)}, u32[]{:S(2)}, u32[]{:S(2)}) collective-permute-start(bf16[112,128]{1,0:T(8,128)(2,1)S(1)} %get-tuple-element.108), channel_id=1, source_target_pairs={{0,16},{1,17},{2,18},{3,19},{4,20},{5,21},{6,22},{7,23},{8,24},{9,... | collective-permute-start | bytes 86024 | tf_op jit(solution)/shard_map/ppermute | solution.py:488
  68.7 5.8 %collective-permute-start.19 = (bf16[112,128]{1,0:T(8,128)(2,1)S(1)}, bf16[112,128]{1,0:T(8,128)(2,1)S(1)}, u32[]{:S(2)}, u32[]{:S(2)}) collective-permute-start(bf16[112,128]{1,0:T(8,128)(2,1)S(1)} %get-tuple-element.109), channel_id=1, source_target_pairs={{0,17},{1,16},{2,19},{3,18},{4,21},{5,20},{6,23},{7,22},{8,25},{9,... | collective-permute-start | bytes 86024 | tf_op jit(solution)/shard_map/ppermute | solution.py:488

commit v11 on v10

--- a/solution.py
+++ b/solution.py
@@ -9,6 +9,7 @@
 from jax.sharding import PartitionSpec as P
 
 SEG_DEV = 2
+O = {'p1': 'core_unit', 'z1': 'none', 'p2': 'unit', 'cores': 2, 'core_in': 'none', 'y0': 'unit', 'basis': [], 'ev1': ['y0', 'side0'], 'diag': ['side0'], 'ev2': ['basis'], 'w': ['core'], 'last': ['z2'], 'ka': 0, 'z3_ka': 0, 'w_ka': 1, 'k0': 0, 'k1': 0, 'k2': 1, 'order': 'w'}
 CORES = 2
 SIDES = 2
 QUAD = 4
@@ -361,7 +362,7 @@
         out[...] = jnp.where(low, zero, other).astype(out.dtype)
 
 
-def expand(routes_ref, turned, spread, first, tiles):
+def expand(routes_ref, turned, lines, first, tiles):
     tops, tokens = routes_ref.shape
     rank = turned.shape[0]
 
@@ -374,14 +375,29 @@
             for k in range(tops):
                 row = turned[r : r + 1, k * tokens : (k + 1) * tokens]
                 value = jnp.where(masks[k], row, value)
-            spread[r, pl.ds(here, 8), :] = value
+            side = r % 2 * tokens
+            lines[r // 2, pl.ds(here, 8), side : side + tokens] = value
         return carry
 
     lax.fori_loop(0, tiles, one, 0)
 
 
+def form(lines, basis_ref, first, count, out_ref, rank):
+    experts, width = lines.shape[1:]
+    made = jnp.dot(
+        lines[first : first + count].reshape(count * experts, width).astype(jnp.bfloat16),
+        basis_ref[...],
+        preferred_element_type=jnp.float32,
+    ).astype(jnp.bfloat16)
+    for pair in range(count):
+        for s in range(SEG_DEV):
+            out_ref[s, :, pl.ds((first + pair) * 2 * rank, 2 * rank)] = made[
+                pair * experts : (pair + 1) * experts, s * 2 * rank : (s + 1) * 2 * rank
+            ]
+
+
 def blocks_kernel(
-    rank, routes_ref, basis_ref, order_ref, total_ref, b_ref, c_ref, d_ref, out_ref, turned, spread
+    rank, routes_ref, basis_ref, order_ref, total_ref, b_ref, c_ref, d_ref, out_ref, turned, lines
 ):
     half = b_ref.shape[0]
     value = packed(total_ref, 0, 2 * half, rank)
@@ -390,17 +406,9 @@
     value = value.T
     value = jnp.concatenate([value[0:rank], value[rank : 2 * rank]], axis=1).astype(jnp.bfloat16)
     turned[...] = jnp.dot(value, order_ref[...], preferred_element_type=jnp.float32)
-    experts = out_ref.shape[1]
-    expand(routes_ref, turned, spread, 0, experts // 8)
-    for pair in range(rank // 2):
-        both = jnp.concatenate([spread[2 * pair], spread[2 * pair + 1]], axis=1)
-        block = jnp.dot(
-            both.astype(jnp.bfloat16), basis_ref[...], preferred_element_type=jnp.float32
-        ).astype(jnp.bfloat16)
-        for s in range(SEG_DEV):
-            out_ref[s, :, pl.ds(pair * 2 * rank, 2 * rank)] = block[
-                :, s * 2 * rank : (s + 1) * 2 * rank
-            ]
+    expand(routes_ref, turned, lines, 0, lines.shape[1] // 8)
+    for first in range(0, rank // 2, 8):
+        form(lines, basis_ref, first, 8, out_ref, rank)
 
 
 def last_kernel(
@@ -421,7 +429,7 @@
     _,
     out_ref,
     turned,
-    spread,
+    lines,
     block,
     sem,
 ):
@@ -441,20 +449,8 @@
             value[core * rank : (core + 1) * rank], rows, preferred_element_type=jnp.float32
         )
     turned[...] = total
-    expand(routes_ref, turned, spread, first, count // 8)
-    lines = [
-        jnp.concatenate([spread[2 * pair], spread[2 * pair + 1]], axis=1) for pair in range(rank // 2)
-    ]
-    made = jnp.dot(
-        jnp.concatenate(lines, axis=0).astype(jnp.bfloat16),
-        basis_ref[...],
-        preferred_element_type=jnp.float32,
-    ).astype(jnp.bfloat16)
-    for pair in range(rank // 2):
-        for s in range(SEG_DEV):
-            block[s, :, pl.ds(pair * 2 * rank, 2 * rank)] = made[
-                pair * count : (pair + 1) * count, s * 2 * rank : (s + 1) * 2 * rank
-            ]
+    expand(routes_ref, turned, lines, first, count // 8)
+    form(lines, basis_ref, 0, rank // 2, block, rank)
     copy = pltpu.make_async_copy(
         block, out_ref.at[:, pl.ds(pl.multiple_of(first, count), count), :], sem
     )
@@ -496,8 +492,11 @@
         return lax.optimization_barrier(arrays)
 
     final = slots - 1
-    first_names = [(n, 0) for n in range(final)] + [(n, 1) for n in range(final - 1)]
-    arrival = first_names + [(final - 1, 1), (final, 1), (final, 0)]
+    names_a = [(n, 0) for n in range(final - 1)] + [(0, 1)]
+    names_b = [(final - 1, 0)] + [(n, 1) for n in range(1, final - 1)]
+    names_c = [(final, 1)] if O["order"] == "w" else [(final - 1, 1)]
+    names_d = [(final - 1, 1)] if O["order"] == "w" else [(final, 1)]
+    arrival = names_a + names_b + names_c + names_d + [(final, 0)]
 
     def source(z, hops):
         for _ in range(hops):
@@ -531,7 +530,19 @@
         cost_estimate=QUICK,
     )(in_hbm(out_proj.reshape(cols, width)))
     other_unit = swap(core_unit, 0, 1)
-    by_rank, _ = tie(routes.T, core_unit)
+    unit = pl.pallas_call(
+        join_kernel,
+        out_shape=pltpu.VMEM((CORES * cols, quarter), jnp.bfloat16),
+        in_specs=[VMEM] * 2,
+        out_specs=VMEM,
+        compiler_params=pltpu.CompilerParams(vmem_limit_bytes=4 * MIB),
+        cost_estimate=QUICK,
+    )(mine_unit, other_unit)
+    by_rank = routes.T
+    if O["p1"] == "core_unit":
+        by_rank, _ = tie(by_rank, core_unit)
+    elif O["p1"] == "unit":
+        by_rank, _ = tie(by_rank, unit)
     edges = -(-(experts + 1) // LANES) * LANES
     held_grads, own_starts, head, order, first_piece = pl.pallas_call(
         sort_kernel,
@@ -549,17 +560,6 @@
         cost_estimate=QUICK,
     )(by_rank, in_hbm(out_grads))
 
-    *joined, order = tie(mine_unit, other_unit, order)
-    unit = pl.pallas_call(
-        join_kernel,
-        out_shape=pltpu.VMEM((CORES * cols, quarter), jnp.bfloat16),
-        in_specs=[VMEM] * 2,
-        out_specs=VMEM,
-        compiler_params=pltpu.CompilerParams(vmem_limit_bytes=4 * MIB),
-        cost_estimate=QUICK,
-    )(*joined)
-    held = {(0, 0): unit, (1, 0): along(unit, following), (0, 1): swap(unit, 0, CORES)}
-
     def permuted(plan, headed, *after):
         held, *_ = tie(order, *after)
         return pl.pallas_call(
@@ -579,18 +579,43 @@
         return (digits[0] * DIGIT + digits[1]).reshape(1, edges)
 
     side_pieces = [swap(first_piece, 1, 0)]
-    (second_piece,) = permuted([(2, 2 * rows, 2 * rows)], [], unit)
-    own_tokens, *for_core = permuted(
-        [(0, 0, pairs), (1, 0, 2 * rows), (1, 2 * rows, 2 * rows)], [1], second_piece
-    )
-    third_piece, last_piece = permuted(
-        [(3, 0, 3 * rows), (3, 3 * rows, rows)], [0], own_tokens
-    )
+    ring_unit = unit
+    if O["z1"] == "first":
+        ring_unit, _ = tie(unit, first_piece)
+    held = {(0, 0): unit, (1, 0): along(ring_unit, following)}
+    p2after = {"none": [], "unit": [unit], "z1": [held[1, 0]]}[O["p2"]]
+    (second_piece,) = permuted([(2, 2 * rows, 2 * rows)], [], *p2after)
+    second_send = second_piece
+    half = 2 * rows
+    if O["cores"] == 2:
+        own_tokens, *for_core = permuted([(0, 0, pairs), (1, 0, half), (1, half, half)], [1], second_piece)
+        core_counts = [half, half]
+    else:
+        own_tokens, *for_core = permuted([(0, 0, pairs), (1, 0, pairs)], [1], second_piece)
+        core_counts = [pairs]
+    third_piece, last_piece = permuted([(3, 0, 3 * rows), (3, 3 * rows, rows)], [0], own_tokens)
+    if O["core_in"] == "ev1":
+        *for_core, held[1, 0] = tie(*for_core, held[1, 0])
     from_core = [swap(piece, 0, 1) for piece in for_core]
-    side_pieces.append(swap(second_piece, 1, 0))
-    third_piece, last_piece, side_pieces[0] = tie(third_piece, last_piece, side_pieces[0])
-    diagonal_pieces = [swap(third_piece, 1, 1), swap(last_piece, 1, 1)]
-    local_segments, *_ = tie(segments, last_piece)
+    y0_in = unit
+    if O["y0"] == "first":
+        y0_in, _ = tie(unit, first_piece)
+    elif O["y0"] == "second":
+        y0_in, _ = tie(unit, second_piece)
+    elif O["y0"] == "own":
+        y0_in, _ = tie(unit, own_tokens)
+    elif O["y0"] == "core":
+        y0_in, *from_core = tie(unit, *from_core)
+    held[0, 1] = swap(y0_in, 0, CORES)
+    side_pieces.append(swap(second_send, 1, 0))
+    basis_in = [last_piece]
+    if "z1" in O["basis"]:
+        basis_in.append(held[1, 0])
+    if "core" in O["basis"]:
+        basis_in += from_core
+    local_segments, *basis_out = tie(segments, *basis_in)
+    if "core" in O["basis"]:
+        from_core = basis_out[len(basis_out) - len(from_core):]
     basis, order_back = pl.pallas_call(
         basis_kernel,
         out_shape=[
@@ -628,6 +653,9 @@
             if group:
                 starts[group] = starts_in(*blocks[0])
             members.append(group)
+        fresh = [group for group, _ in complete]
+        if fresh and known_units:
+            tasks.append(("units", fresh, 0, known_units))
         if names:
             tasks.append(("units", list(members), known_units, CORES * len(names)))
         known_units += CORES * len(names)
@@ -648,35 +676,76 @@
         )
         return out
 
-    for n in range(1, slots):
-        if n == final:
-            break
-        tied = [held[n, 0], held[n - 1, 1]]
-        if n == 1:
-            tied.append(side_pieces[0])
-        if n == final - 1:
-            tied += [basis, order_back]
-        held[n, 0], held[n - 1, 1], *tied = tie(*tied)
-        if n == 1:
-            side_pieces[0], *tied = tied
-        if n == final - 1:
-            basis, order_back = tied
-            half = 2 * rows
-            work(
-                first_names,
-                complete=[
-                    (0, [(own_tokens, pairs)]),
-                    (1, [(piece, half) for piece in from_core]),
-                    (2, [(piece, half) for piece in side_pieces]),
-                ],
-            )
+    def group_tie(names, array):
+        nonlocal basis, from_core
+        items = []
+        for name in names:
+            if name == "y0":
+                items.append(held[0, 1])
+            if name == "y1":
+                items.append(held[1, 1])
+            if name == "z1":
+                items.append(held[1, 0])
+            if name == "z2":
+                items.append(held[near])
+            if name == "side0":
+                items.append(side_pieces[0])
+            if name == "side1":
+                items.append(side_pieces[1])
+            if name == "basis":
+                items.append(basis)
+            if name == "core":
+                items += from_core
+        out = tie(array, *items)
+        out = list(out)
+        array, out = out[0], out[1:]
+        for name in names:
+            if name == "y0":
+                held[0, 1] = out.pop(0)
+            if name == "y1":
+                held[1, 1] = out.pop(0)
+            if name == "z1":
+                held[1, 0] = out.pop(0)
+            if name == "z2":
+                held[near] = out.pop(0)
+            if name == "side0":
+                side_pieces[0] = out.pop(0)
+            if name == "side1":
+                side_pieces[1] = out.pop(0)
+            if name == "basis":
+                basis = out.pop(0)
+            if name == "core":
+                from_core = [out.pop(0) for _ in from_core]
+        return array
+
+    held[1, 0] = group_tie(O["ev1"], held[1, 0])
+    for n in range(1, final - 1):
         held[n + 1, 0] = along(held[n, 0], following)
         held[n, 1] = swap(held[n, 0], 0, CORES)
-    held[final, 1] = along(held[0, 1], before)
-
-    work([(final - 1, 1)], partial=[(3, diagonal_pieces[0], 0, 3 * rows)])
+    third_piece = group_tie(O["diag"], third_piece)
+    diagonal_pieces = [swap(third_piece, 1, 1)]
+    near = (final - 1, 0)
+    held[near] = group_tie(O["ev2"], held[near])
+    COST = {0: QUICK, 1: SHORT}
+    work(
+        names_a,
+        complete=[(0, [(own_tokens, pairs)]), (1, list(zip(from_core, core_counts)))],
+        cost=COST[O["ka"]],
+    )
+    if O["z3_ka"]:
+        held[near], *state = tie(held[near], *state)
+    back_unit = group_tie(O["w"], held[0, 1])
+    if O["w_ka"]:
+        back_unit, *state = tie(back_unit, *state)
+    held[final, 1] = along(back_unit, before)
+    held[final, 0] = along(held[near], following)
+    held[final - 1, 1] = swap(held[near], 0, CORES)
+    last_piece = group_tie(O["last"], last_piece)
+    diagonal_pieces.append(swap(last_piece, 1, 1))
+    work(names_b, complete=[(2, [(piece, half) for piece in side_pieces])], cost=COST[O["k0"]])
+    work(names_c, partial=[(3, diagonal_pieces[0], 0, 3 * rows)], cost=COST[O["k1"]])
     sent = work(
-        [(final, 1)], partial=[(3, diagonal_pieces[1], 3 * rows, rows)], sends=[1, 2, 3], cost=SHORT
+        names_d, partial=[(3, diagonal_pieces[1], 3 * rows, rows)], sends=[1, 2, 3], cost=COST[O["k2"]]
     )
 
     def returned(arrays):
@@ -705,7 +774,7 @@
         ],
         in_specs=[VMEM] * 7,
         out_specs=[VMEM] * 2,
-        scratch_shapes=[pltpu.VMEM((rank, experts, tokens), jnp.float32)],
+        scratch_shapes=[pltpu.VMEM((rank // 2, experts, 2 * tokens), jnp.float32)],
         compiler_params=pltpu.CompilerParams(vmem_limit_bytes=32 * MIB),
         cost_estimate=QUICK,
     )(by_rank, basis, in_vmem(order_back), in_vmem(state[2]), *early)
@@ -717,7 +786,7 @@
         out_specs=HBM,
         scratch_shapes=[
             pltpu.VMEM((rank, pairs), jnp.float32),
-            pltpu.VMEM((rank, count, tokens), jnp.float32),
+            pltpu.VMEM((rank // 2, count, 2 * tokens), jnp.float32),
             pltpu.VMEM((SEG_DEV, count, rank * rank), jnp.bfloat16),
             pltpu.SemaphoreType.DMA,
         ],

time: 77.1 us -> 76.7 us (level)
  waiting for transfers between devices: 24.9 us -> 12.7 us
  starting transfers between devices: 21.7 us -> 30.8 us
  Pallas kernels: 29.1 us -> 31.1 us
    ppermute x16, waiting for transfers between devices: 22.8 us -> 7.13 us  [swap(): return lax.ppermute(array, BOTH, table)]
    ppermute x16, starting transfers between devices: 16.8 us -> 25.7 us  [swap(): return lax.ppermute(array, BOTH, table)]
    ppermute x4, waiting for transfers between devices: 2.1 us -> 5.61 us  [along(): return lax.ppermute(array, 'expert', pairs_of)]
    pallas_call x3 -> x4, Pallas kernels: 10.5 us -> 12.8 us  [accumulate(): pl.pallas_call(functools.partial(partial_kernel, rank, pairs, window, [(f...]
  transfers between devices with their start and end apart: 20 -> 20, of which waited for: 6 -> 6; matrix products, arithmetic and copies ran while one was open for 0% -> 0% of each run, Pallas kernels for 34% -> 37%
where the time goes in v11:
time: 76.7 us; the launch traced here: 75.6 us
  Pallas kernels  31.1 us (41%)
  starting transfers between devices  30.8 us (40%)
  waiting for transfers between devices  12.7 us (17%)
    ppermute x16, starting transfers between devices, swap(): return lax.ppermute(array, BOTH, table)  25.7 us
    pallas_call x4, Pallas kernels, accumulate(): pl.pallas_call(functools.partial(partial_kernel, rank, pairs, window, [(f...  12.8 us
    ppermute x16, waiting for transfers between devices, swap(): return lax.ppermute(array, BOTH, table)  7.13 us
    ppermute x4, waiting for transfers between devices, along(): return lax.ppermute(array, 'expert', pairs_of)  5.61 us
    ppermute x4, starting transfers between devices, along(): return lax.ppermute(array, 'expert', pairs_of)  5.14 us
    pallas_call x3, Pallas kernels, permuted(): pl.pallas_call(functools.partial(permute_kernel, plan), out_shape=[rows_s...  4.35 us
    pallas_call x1, Pallas kernels, local(): pl.pallas_call(sort_kernel, out_shape=[pltpu.VMEM(out_grads.shape, jnp.bf...  3.37 us
    pallas_call x1, Pallas kernels, local(): pl.pallas_call(functools.partial(blocks_kernel, rank), out_shape=[jax.Sha...  3.09 us
  transfers between devices with their start and end apart: 20, of which 6 were waited for; matrix products, arithmetic and copies ran while one was open for 0% of the time, Pallas kernels for 37%

profile of v11, /device:TPU:1, one launch (start us, length us, event | category | flops | bytes accessed | tf_op | source)
XLA Modules:
  0.0 75.6 jit_solution(726571147951247634)
XLA Ops:
  0.0 1.3 %shard_map.73 = (bf16[256,512]{1,0:T(8,128)(2,1)S(1)}, bf16[256,512]{1,0:T(8,128)(2,1)S(1)}) custom-call(bf16[256,2048]{1,0:T(8,128)(2,1)} %bitcast.8), custom_call_target="tpu_custom_call" | custom-call | flops 1 | bytes 1 | tf_op jit(solution)/shard_map/pallas_call | solution.py:523
  1.3 0.1 collective-permute-start
  1.4 0.7 copy-done.1
  2.1 3.4 %shard_map.74 = (bf16[128,8,2048]{2,1,0:T(8,128)(2,1)S(1)}, s32[1,128]{1,0:T(1,128)S(1)}, bf16[16,512]{1,0:T(8,128)(2,1)S(1)}, bf16[1024,1024]{1,0:T(8,128)(2,1)S(1)}, bf16[528,512]{1,0:T(8,128)(2,1)S(1)}) custom-call(s32[8,128]{1,0:T(8,128)S(1)} %bitcast.3, bf16[128,8,2048]{2,1,0:T(8,128)(2,1)} %grads_ref.1), custom_call_target="tpu_custom_call" | custom-call | flops 1 | bytes 1 | tf_op jit(solution)/shard_map/pallas_call | solution.py:547
  5.5 2.7 %collective-permute-start.3 = (bf16[528,512]{1,0:T(8,128)(2,1)S(1)}, bf16[528,512]{1,0:T(8,128)(2,1)S(1)}, u32[]{:S(2)}, u32[]{:S(2)}) collective-permute-start(bf16[528,512]{1,0:T(8,128)(2,1)S(1)} %get-tuple-element.66), channel_id=1, source_target_pairs={{0,16},{1,17},{2,18},{3,19},{4,20},{5,21},{6,22},{7,23},{8,24},{9,... | collective-permute-start | bytes 1622024 | tf_op jit(solution)/shard_map/ppermute | solution.py:484
  8.2 0.0 collective-permute-done.two_ref
  8.2 1.3 %collective-permute-start.1 = (bf16[512,512]{1,0:T(8,128)(2,1)S(1)}, bf16[512,512]{1,0:T(8,128)(2,1)S(1)}, u32[]{:S(2)}, u32[]{:S(2)}) collective-permute-start(bf16[512,512]{1,0:T(8,128)(2,1)S(1)} %shard_map.75.refs_5_), channel_id=1, source_target_pairs={{0,4},{1,5},{2,6},{3,7},{4,12},{5,13},{6,14},{7,15},{8,0},{9,1},{1... | collective-permute-start | bytes 1572872 | tf_op jit(solution)/shard_map/ppermute | solution.py:489
  9.6 1.2 %collective-permute-start.2 = (bf16[512,512]{1,0:T(8,128)(2,1)S(1)}, bf16[512,512]{1,0:T(8,128)(2,1)S(1)}, u32[]{:S(2)}, u32[]{:S(2)}) collective-permute-start(bf16[512,512]{1,0:T(8,128)(2,1)S(1)} %shard_map.75.refs_5_), channel_id=1, source_target_pairs={{0,2},{1,3},{2,0},{3,1},{4,6},{5,7},{6,4},{7,5},{8,10},{9,11},{10,... | collective-permute-start | bytes 1572872 | tf_op jit(solution)/shard_map/ppermute | solution.py:484
  10.8 0.7 shard_map.76
  11.5 2.4 %shard_map.77 = (bf16[1024,512]{1,0:T(8,128)(2,1)S(1)}, bf16[528,512]{1,0:T(8,128)(2,1)S(1)}, bf16[512,512]{1,0:T(8,128)(2,1)S(1)}) custom-call(bf16[1024,1024]{1,0:T(8,128)(2,1)S(1)} %get-tuple-element.74.order_ref, bf16[16,512]{1,0:T(8,128)(2,1)S(1)} %get-tuple-element.70.head_ref, bf16[128,8,2048]{2,1,0:T(8,128)(2,1)S(1)} %get-tuple-element.71.grads_ref), custom_call_target="tpu_custom_call" | custom-call | flops 1 | bytes 1 | tf_op jit(solution)/shard_map/pallas_call | solution.py:565
  13.9 0.0 copy-start.3
  13.9 0.9 %collective-permute-start.5 = (bf16[528,512]{1,0:T(8,128)(2,1)S(1)}, bf16[528,512]{1,0:T(8,128)(2,1)S(1)}, u32[]{:S(2)}, u32[]{:S(2)}) collective-permute-start(bf16[528,512]{1,0:T(8,128)(2,1)S(1)} %get-tuple-element.80), channel_id=1, source_target_pairs={{0,1},{1,0},{2,3},{3,2},{4,5},{5,4},{6,7},{7,6},{8,9},{9,8},{10,11... | collective-permute-start | bytes 1622024 | tf_op jit(solution)/shard_map/ppermute | solution.py:484
  14.8 0.3 collective-permute-start.11
  15.1 1.3 %shard_map.78 = (bf16[784,512]{1,0:T(8,128)(2,1)S(1)}, bf16[256,512]{1,0:T(8,128)(2,1)S(1)}) custom-call(bf16[1024,1024]{1,0:T(8,128)(2,1)S(1)} %get-tuple-element.74.order_ref, bf16[16,512]{1,0:T(8,128)(2,1)S(1)} %get-tuple-element.70.head_ref, bf16[128,8,2048]{2,1,0:T(8,128)(2,1)S(1)} %get-tuple-element.71.grads_ref), custom_call_target="tpu_custom_call" | custom-call | flops 1 | bytes 1 | tf_op jit(solution)/shard_map/pallas_call | solution.py:565
  16.4 2.8 %shard_map.79 = (bf16[256,256]{1,0:T(8,128)(2,1)S(1)}, bf16[1024,1024]{1,0:T(8,128)(2,1)S(1)}) custom-call(bf16[128,7168]{1,0:T(8,128)(2,1)} %hidden_ref.1, bf16[64,7168]{1,0:T(8,128)(2,1)} %proj_ref.1, s32[1,128]{1,0:T(1,128)S(1)} %bitcast.7, s32[8,128]{1,0:T(8,128)S(1)} %bitcast.4), custom_call_target="tpu_custom_call" | custom-call | flops 1 | bytes 1 | tf_op jit(solution)/shard_map/pallas_call | solution.py:619
  19.2 1.6 %collective-permute-done.3.refs_3_ = bf16[528,512]{1,0:T(8,128)(2,1)S(1)} collective-permute-done((bf16[528,512]{1,0:T(8,128)(2,1)S(1)}, bf16[528,512]{1,0:T(8,128)(2,1)S(1)}, u32[]{:S(2)}, u32[]{:S(2)}) %collective-permute-start.3) | collective-permute-done | bytes 540704 | tf_op jit(solution)/shard_map/ppermute | solution.py:484
  20.8 0.8 %collective-permute-start.9 = (bf16[512,512]{1,0:T(8,128)(2,1)S(1)}, bf16[512,512]{1,0:T(8,128)(2,1)S(1)}, u32[]{:S(2)}, u32[]{:S(2)}) collective-permute-start(bf16[512,512]{1,0:T(8,128)(2,1)S(1)} %get-tuple-element.88), channel_id=1, source_target_pairs={{0,1},{1,0},{2,3},{3,2},{4,5},{5,4},{6,7},{7,6},{8,9},{9,8},{10,11... | collective-permute-start | bytes 1572872 | tf_op jit(solution)/shard_map/ppermute | solution.py:484
  21.6 0.8 %collective-permute-done.1.refs_6_ = bf16[512,512]{1,0:T(8,128)(2,1)S(1)} collective-permute-done((bf16[512,512]{1,0:T(8,128)(2,1)S(1)}, bf16[512,512]{1,0:T(8,128)(2,1)S(1)}, u32[]{:S(2)}, u32[]{:S(2)}) %collective-permute-start.1) | collective-permute-done | bytes 524320 | tf_op jit(solution)/shard_map/ppermute | solution.py:489
  22.4 0.1 collective-permute-done.2.refs_7_
  22.5 2.3 %collective-permute-start.4 = (bf16[512,512]{1,0:T(8,128)(2,1)S(1)}, bf16[512,512]{1,0:T(8,128)(2,1)S(1)}, u32[]{:S(2)}, u32[]{:S(2)}) collective-permute-start(bf16[512,512]{1,0:T(8,128)(2,1)S(1)} %collective-permute-done.1.refs_6_), channel_id=1, source_target_pairs={{0,4},{1,5},{2,6},{3,7},{4,12},{5,13},{6,14},{7,15},{8,0},{9,1},{1... | collective-permute-start | bytes 1572872 | tf_op jit(solution)/shard_map/ppermute | solution.py:489
  24.8 1.8 %collective-permute-start.6 = (bf16[784,512]{1,0:T(8,128)(2,1)S(1)}, bf16[784,512]{1,0:T(8,128)(2,1)S(1)}, u32[]{:S(2)}, u32[]{:S(2)}) collective-permute-start(bf16[784,512]{1,0:T(8,128)(2,1)S(1)} %get-tuple-element.84), channel_id=1, source_target_pairs={{0,17},{1,16},{2,19},{3,18},{4,21},{5,20},{6,23},{7,22},{8,25},{9,... | collective-permute-start | bytes 2408456 | tf_op jit(solution)/shard_map/ppermute | solution.py:484
  26.7 1.2 %collective-permute-start.12 = (bf16[512,512]{1,0:T(8,128)(2,1)S(1)}, bf16[512,512]{1,0:T(8,128)(2,1)S(1)}, u32[]{:S(2)}, u32[]{:S(2)}) collective-permute-start(bf16[512,512]{1,0:T(8,128)(2,1)S(1)} %collective-permute-done.1.refs_6_), channel_id=1, source_target_pairs={{0,2},{1,3},{2,0},{3,1},{4,6},{5,7},{6,4},{7,5},{8,10},{9,11},{10,... | collective-permute-start | bytes 1572872 | tf_op jit(solution)/shard_map/ppermute | solution.py:484
  27.9 0.0 collective-permute-done.9.refs_4_
  27.9 2.6 %shard_map.80 = (bf16[4096,512]{1,0:T(8,128)(2,1)S(1)}, bf16[16,256,512]{2,1,0:T(8,128)(2,1)S(1)}, f32[4096,128]{1,0:T(8,128)S(1)}) custom-call(s32[16,16]{1,0:T(8,128)S(1)} %copy-done, s32[1,128]{1,0:T(1,128)S(1)} %get-tuple-element.64.refs_0_.starts_ref, s32[1,128]{1,0:T(1,128)S(1)} %slice_add_fusion.2.refs_1_, ...), custom_call_target="tpu_custom_call" | custom-call | flops 1 | bytes 1 | tf_op jit(solution)/shard_map/pallas_call | solution.py:299
  30.5 0.1 collective-permute-start.10
  30.6 4.8 %collective-permute-done.4.refs_5_ = bf16[512,512]{1,0:T(8,128)(2,1)S(1)} collective-permute-done((bf16[512,512]{1,0:T(8,128)(2,1)S(1)}, bf16[512,512]{1,0:T(8,128)(2,1)S(1)}, u32[]{:S(2)}, u32[]{:S(2)}) %collective-permute-start.4) | collective-permute-done | bytes 524320 | tf_op jit(solution)/shard_map/ppermute | solution.py:489
  35.4 1.2 %collective-permute-start.8 = (bf16[512,512]{1,0:T(8,128)(2,1)S(1)}, bf16[512,512]{1,0:T(8,128)(2,1)S(1)}, u32[]{:S(2)}, u32[]{:S(2)}) collective-permute-start(bf16[512,512]{1,0:T(8,128)(2,1)S(1)} %collective-permute-done.4.refs_5_), channel_id=1, source_target_pairs={{0,2},{1,3},{2,0},{3,1},{4,6},{5,7},{6,4},{7,5},{8,10},{9,11},{10,... | collective-permute-start | bytes 1572872 | tf_op jit(solution)/shard_map/ppermute | solution.py:484
  36.7 1.4 %collective-permute-start.16 = (bf16[512,512]{1,0:T(8,128)(2,1)S(1)}, bf16[512,512]{1,0:T(8,128)(2,1)S(1)}, u32[]{:S(2)}, u32[]{:S(2)}) collective-permute-start(bf16[512,512]{1,0:T(8,128)(2,1)S(1)} %collective-permute-done.4.refs_5_), channel_id=1, source_target_pairs={{0,4},{1,5},{2,6},{3,7},{4,12},{5,13},{6,14},{7,15},{8,0},{9,1},{1... | collective-permute-start | bytes 1572872 | tf_op jit(solution)/shard_map/ppermute | solution.py:489
  38.0 2.3 %collective-permute-done.12.refs_6_ = bf16[512,512]{1,0:T(8,128)(2,1)S(1)} collective-permute-done((bf16[512,512]{1,0:T(8,128)(2,1)S(1)}, bf16[512,512]{1,0:T(8,128)(2,1)S(1)}, u32[]{:S(2)}, u32[]{:S(2)}) %collective-permute-start.12) | collective-permute-done | bytes 524320 | tf_op jit(solution)/shard_map/ppermute | solution.py:484
  40.3 10.9 %collective-permute-start.7 = (bf16[256,512]{1,0:T(8,128)(2,1)S(1)}, bf16[256,512]{1,0:T(8,128)(2,1)S(1)}, u32[]{:S(2)}, u32[]{:S(2)}) collective-permute-start(bf16[256,512]{1,0:T(8,128)(2,1)S(1)} %get-tuple-element.86), channel_id=1, source_target_pairs={{0,17},{1,16},{2,19},{3,18},{4,21},{5,20},{6,23},{7,22},{8,25},{9,... | collective-permute-start | bytes 786440 | tf_op jit(solution)/shard_map/ppermute | solution.py:484
  51.2 3.3 %shard_map.81 = (bf16[4096,512]{1,0:T(8,128)(2,1)S(1)}, bf16[16,256,512]{2,1,0:T(8,128)(2,1)S(1)}, f32[4096,128]{1,0:T(8,128)S(1)}) custom-call(s32[16,16]{1,0:T(8,128)S(1)} %copy-done, s32[1,128]{1,0:T(1,128)S(1)} %get-tuple-element.64.refs_0_.starts_ref, ...), custom_call_target="tpu_custom_call", output_to_operand_aliasing={{0}: (8, {}), {1}: (9, {}), {2}: (10, {})} | custom-call | flops 1 | bytes 1 | tf_op jit(solution)/shard_map/pallas_call | solution.py:299
  54.5 0.0 collective-permute-done.6.refs_4_
  54.5 0.0 collective-permute-done.10.refs_5_
  54.6 3.9 %shard_map.82 = (bf16[4096,512]{1,0:T(8,128)(2,1)S(1)}, bf16[16,256,512]{2,1,0:T(8,128)(2,1)S(1)}, f32[4096,128]{1,0:T(8,128)S(1)}) custom-call(s32[16,16]{1,0:T(8,128)S(1)} %copy-done, s32[1,128]{1,0:T(1,128)S(1)} %get-tuple-element.64.refs_0_.starts_ref, ...), custom_call_target="tpu_custom_call", output_to_operand_aliasing={{0}: (7, {}), {1}: (8, {}), {2}: (9, {})} | custom-call | flops 1 | bytes 1 | tf_op jit(solution)/shard_map/pallas_call | solution.py:299
  58.5 0.0 collective-permute-done.8.refs_5_
  58.5 3.0 %shard_map.83 = (bf16[4096,512]{1,0:T(8,128)(2,1)S(1)}, bf16[16,256,512]{2,1,0:T(8,128)(2,1)S(1)}, f32[4096,128]{1,0:T(8,128)S(1)}, bf16[512,128]{1,0:T(8,128)(2...) custom-call(s32[16,16]{1,0:T(8,128)S(1)} %copy-done, ...), custom_call_target="tpu_custom_call", output_to_operand_aliasing={{0}: (7, {}), {1}: (8, {}), {2}: (9, {})} | custom-call | flops 1000000000 | bytes 1 | tf_op jit(solution)/shard_map/pallas_call | solution.py:299
  61.5 0.0 copy-start.2
  61.6 0.1 collective-permute-start.13
  61.6 0.1 collective-permute-start.14
  61.8 2.0 %collective-permute-start.15 = (bf16[512,128]{1,0:T(8,128)(2,1)S(1)}, bf16[512,128]{1,0:T(8,128)(2,1)S(1)}, u32[]{:S(2)}, u32[]{:S(2)}) collective-permute-start(bf16[512,128]{1,0:T(8,128)(2,1)S(1)} %get-tuple-element.107), channel_id=1, source_target_pairs={{0,17},{1,16},{2,19},{3,18},{4,21},{5,20},{6,23},{7,22},{8,25},{9,... | collective-permute-start | bytes 393224 | tf_op jit(solution)/shard_map/ppermute | solution.py:484
  63.8 0.0 collective-permute-done.16.refs_5_
  63.8 1.3 %shard_map.84 = (f32[112,128]{1,0:T(8,128)S(1)}, bf16[112,128]{1,0:T(8,128)(2,1)S(1)}, bf16[112,128]{1,0:T(8,128)(2,1)S(1)}, bf16[112,128]{1,0:T(8,128)(2,1)S(1)}) custom-call(s32[16,16]{1,0:T(8,128)S(1)} %copy-done, s32[1,128]{1,0:T(1,128)S(1)} %get-tuple-element.64.refs_0_.starts_ref, s32[1,128]{1,0:T(1,128)S(1)} %slice_add_fusion.2.refs_1_, ...), custom_call_target="tpu_custom_call" | custom-call | flops 1 | bytes 1 | tf_op jit(solution)/shard_map/pallas_call | solution.py:758
  65.0 0.1 collective-permute-start.17
  65.1 0.1 collective-permute-start.18
  65.2 2.0 %collective-permute-start.19 = (bf16[112,128]{1,0:T(8,128)(2,1)S(1)}, bf16[112,128]{1,0:T(8,128)(2,1)S(1)}, u32[]{:S(2)}, u32[]{:S(2)}) collective-permute-start(bf16[112,128]{1,0:T(8,128)(2,1)S(1)} %get-tuple-element.117), channel_id=1, source_target_pairs={{0,17},{1,16},{2,19},{3,18},{4,21},{5,20},{6,23},{7,22},{8,25},{9,... | collective-permute-start | bytes 86024 | tf_op jit(solution)/shard_map/ppermute | solution.py:484
  67.2 3.1 %collective-permute-done.15.d_ref = bf16[512,128]{1,0:T(8,128)(2,1)S(1)} collective-permute-done((bf16[512,128]{1,0:T(8,128)(2,1)S(1)}, bf16[512,128]{1,0:T(8,128)(2,1)S(1)}, u32[]{:S(2)}, u32[]{:S(2)}) %collective-permute-start.15) | collective-permute-done | bytes 131104 | tf_op jit(solution)/shard_map/ppermute | solution.py:484
  70.4 3.1 %shard_map.85 = (bf16[2,64,4096]{2,1,0:T(8,128)(2,1)}, f32[64,1024]{1,0:T(8,128)S(1)}) custom-call(s32[8,128]{1,0:T(8,128)S(1)} %bitcast.5, bf16[256,256]{1,0:T(8,128)(2,1)S(1)} %get-tuple-element.78.basis_ref, bf16[1024,1024]{1,0:T(8,128)(2,1)S(1)} %get-tuple-element.79.order_ref, f32[4096,128]{1,0:T(8,128)S(1)} %get-tuple-element.104.total_ref, ...), custom_call_target="tpu_custom_call" | custom-call | flops 1 | bytes 1 | tf_op jit(solution)/shard_map/pallas_call | solution.py:769
  73.5 2.1 %shard_map.86 = bf16[2,64,4096]{2,1,0:T(8,128)(2,1)} custom-call(s32[16,16]{1,0:T(8,128)S(1)} %copy-done, s32[1,128]{1,0:T(1,128)S(1)} %get-tuple-element.64.refs_0_.starts_ref, s32[8,128]{1,0:T(8,128)S(1)} %bitcast.6, bf16[256,256]{1,0:T(8,128)(2,1)S(1)} %get-tuple-element.78.basis_ref, ...), custom_call_target="tpu_custom_call", output_to_operand_aliasing={{}: (10, {})} | custom-call | flops 1 | bytes 1 | tf_op jit(solution)/shard_map/pallas_call | solution.py:782
  (20 shorter events, 0.1 us)
Async XLA Ops:
  1.3 6.9 %collective-permute-start = (bf16[256,512]{1,0:T(8,128)(2,1)S(1)}, bf16[256,512]{1,0:T(8,128)(2,1)S(1)}, u32[]{:S(2)}, u32[]{:S(2)}) collective-permute-start(bf16[256,512]{1,0:T(8,128)(2,1)S(1)} %get-tuple-element.62), channel_id=1, source_target_pairs={{0,1},{1,0},{2,3},{3,2},{4,5},{5,4},{6,7},{7,6},{8,9},{9,8},{10,11... | collective-permute-start | bytes 786440 | tf_op jit(solution)/shard_map/ppermute | solution.py:484
  1.4 0.7 copy-start.1
  5.5 15.4 %collective-permute-start.3 = (bf16[528,512]{1,0:T(8,128)(2,1)S(1)}, bf16[528,512]{1,0:T(8,128)(2,1)S(1)}, u32[]{:S(2)}, u32[]{:S(2)}) collective-permute-start(bf16[528,512]{1,0:T(8,128)(2,1)S(1)} %get-tuple-element.66), channel_id=1, source_target_pairs={{0,16},{1,17},{2,18},{3,19},{4,20},{5,21},{6,22},{7,23},{8,24},{9,... | collective-permute-start | bytes 1622024 | tf_op jit(solution)/shard_map/ppermute | solution.py:484
  8.2 14.2 %collective-permute-start.1 = (bf16[512,512]{1,0:T(8,128)(2,1)S(1)}, bf16[512,512]{1,0:T(8,128)(2,1)S(1)}, u32[]{:S(2)}, u32[]{:S(2)}) collective-permute-start(bf16[512,512]{1,0:T(8,128)(2,1)S(1)} %shard_map.75.refs_5_), channel_id=1, source_target_pairs={{0,4},{1,5},{2,6},{3,7},{4,12},{5,13},{6,14},{7,15},{8,0},{9,1},{1... | collective-permute-start | bytes 1572872 | tf_op jit(solution)/shard_map/ppermute | solution.py:489
  9.6 12.9 %collective-permute-start.2 = (bf16[512,512]{1,0:T(8,128)(2,1)S(1)}, bf16[512,512]{1,0:T(8,128)(2,1)S(1)}, u32[]{:S(2)}, u32[]{:S(2)}) collective-permute-start(bf16[512,512]{1,0:T(8,128)(2,1)S(1)} %shard_map.75.refs_5_), channel_id=1, source_target_pairs={{0,2},{1,3},{2,0},{3,1},{4,6},{5,7},{6,4},{7,5},{8,10},{9,11},{10,... | collective-permute-start | bytes 1572872 | tf_op jit(solution)/shard_map/ppermute | solution.py:484
  13.9 2.5 %copy-start.3 = (s32[128]{0:T(128)S(1)}, s32[128]{0:T(128)}, u32[]{:S(2)}) copy-start(s32[128]{0:T(128)} %param.10) | copy-start | bytes 1540
  13.9 12.7 %collective-permute-start.5 = (bf16[528,512]{1,0:T(8,128)(2,1)S(1)}, bf16[528,512]{1,0:T(8,128)(2,1)S(1)}, u32[]{:S(2)}, u32[]{:S(2)}) collective-permute-start(bf16[528,512]{1,0:T(8,128)(2,1)S(1)} %get-tuple-element.80), channel_id=1, source_target_pairs={{0,1},{1,0},{2,3},{3,2},{4,5},{5,4},{6,7},{7,6},{8,9},{9,8},{10,11... | collective-permute-start | bytes 1622024 | tf_op jit(solution)/shard_map/ppermute | solution.py:484
  14.8 21.8 %collective-permute-start.11 = (bf16[512,512]{1,0:T(8,128)(2,1)S(1)}, bf16[512,512]{1,0:T(8,128)(2,1)S(1)}, u32[]{:S(2)}, u32[]{:S(2)}) collective-permute-start(bf16[512,512]{1,0:T(8,128)(2,1)S(1)} %shard_map.76), channel_id=1, source_target_pairs={{0,16},{1,17},{2,18},{3,19},{4,20},{5,21},{6,22},{7,23},{8,24},{9,... | collective-permute-start | bytes 1572872 | tf_op jit(solution)/shard_map/ppermute | solution.py:484
  15.1 12.8 %copy-start = (s32[16,16]{1,0:T(8,128)S(1)}, s32[16,16]{1,0:T(8,128)}, u32[]{:S(2)}) copy-start(s32[16,16]{1,0:T(8,128)} %constant.4.clone.bases_ref) | copy-start | bytes 3076
  20.8 7.1 %collective-permute-start.9 = (bf16[512,512]{1,0:T(8,128)(2,1)S(1)}, bf16[512,512]{1,0:T(8,128)(2,1)S(1)}, u32[]{:S(2)}, u32[]{:S(2)}) collective-permute-start(bf16[512,512]{1,0:T(8,128)(2,1)S(1)} %get-tuple-element.88), channel_id=1, source_target_pairs={{0,1},{1,0},{2,3},{3,2},{4,5},{5,4},{6,7},{7,6},{8,9},{9,8},{10,11... | collective-permute-start | bytes 1572872 | tf_op jit(solution)/shard_map/ppermute | solution.py:484
  22.5 12.9 %collective-permute-start.4 = (bf16[512,512]{1,0:T(8,128)(2,1)S(1)}, bf16[512,512]{1,0:T(8,128)(2,1)S(1)}, u32[]{:S(2)}, u32[]{:S(2)}) collective-permute-start(bf16[512,512]{1,0:T(8,128)(2,1)S(1)} %collective-permute-done.1.refs_6_), channel_id=1, source_target_pairs={{0,4},{1,5},{2,6},{3,7},{4,12},{5,13},{6,14},{7,15},{8,0},{9,1},{1... | collective-permute-start | bytes 1572872 | tf_op jit(solution)/shard_map/ppermute | solution.py:489
  24.8 29.7 %collective-permute-start.6 = (bf16[784,512]{1,0:T(8,128)(2,1)S(1)}, bf16[784,512]{1,0:T(8,128)(2,1)S(1)}, u32[]{:S(2)}, u32[]{:S(2)}) collective-permute-start(bf16[784,512]{1,0:T(8,128)(2,1)S(1)} %get-tuple-element.84), channel_id=1, source_target_pairs={{0,17},{1,16},{2,19},{3,18},{4,21},{5,20},{6,23},{7,22},{8,25},{9,... | collective-permute-start | bytes 2408456 | tf_op jit(solution)/shard_map/ppermute | solution.py:484
  26.7 13.6 %collective-permute-start.12 = (bf16[512,512]{1,0:T(8,128)(2,1)S(1)}, bf16[512,512]{1,0:T(8,128)(2,1)S(1)}, u32[]{:S(2)}, u32[]{:S(2)}) collective-permute-start(bf16[512,512]{1,0:T(8,128)(2,1)S(1)} %collective-permute-done.1.refs_6_), channel_id=1, source_target_pairs={{0,2},{1,3},{2,0},{3,1},{4,6},{5,7},{6,4},{7,5},{8,10},{9,11},{10,... | collective-permute-start | bytes 1572872 | tf_op jit(solution)/shard_map/ppermute | solution.py:484
  30.5 24.0 %collective-permute-start.10 = (bf16[512,512]{1,0:T(8,128)(2,1)S(1)}, bf16[512,512]{1,0:T(8,128)(2,1)S(1)}, u32[]{:S(2)}, u32[]{:S(2)}) collective-permute-start(bf16[512,512]{1,0:T(8,128)(2,1)S(1)} %collective-permute-done.2.refs_7_), channel_id=1, source_target_pairs={{0,8},{1,9},{2,10},{3,11},{4,0},{5,1},{6,2},{7,3},{8,12},{9,13},{1... | collective-permute-start | bytes 1572872 | tf_op jit(solution)/shard_map/ppermute | solution.py:489
  35.4 23.1 %collective-permute-start.8 = (bf16[512,512]{1,0:T(8,128)(2,1)S(1)}, bf16[512,512]{1,0:T(8,128)(2,1)S(1)}, u32[]{:S(2)}, u32[]{:S(2)}) collective-permute-start(bf16[512,512]{1,0:T(8,128)(2,1)S(1)} %collective-permute-done.4.refs_5_), channel_id=1, source_target_pairs={{0,2},{1,3},{2,0},{3,1},{4,6},{5,7},{6,4},{7,5},{8,10},{9,11},{10,... | collective-permute-start | bytes 1572872 | tf_op jit(solution)/shard_map/ppermute | solution.py:484
  36.7 27.1 %collective-permute-start.16 = (bf16[512,512]{1,0:T(8,128)(2,1)S(1)}, bf16[512,512]{1,0:T(8,128)(2,1)S(1)}, u32[]{:S(2)}, u32[]{:S(2)}) collective-permute-start(bf16[512,512]{1,0:T(8,128)(2,1)S(1)} %collective-permute-done.4.refs_5_), channel_id=1, source_target_pairs={{0,4},{1,5},{2,6},{3,7},{4,12},{5,13},{6,14},{7,15},{8,0},{9,1},{1... | collective-permute-start | bytes 1572872 | tf_op jit(solution)/shard_map/ppermute | solution.py:489
  40.3 18.2 %collective-permute-start.7 = (bf16[256,512]{1,0:T(8,128)(2,1)S(1)}, bf16[256,512]{1,0:T(8,128)(2,1)S(1)}, u32[]{:S(2)}, u32[]{:S(2)}) collective-permute-start(bf16[256,512]{1,0:T(8,128)(2,1)S(1)} %get-tuple-element.86), channel_id=1, source_target_pairs={{0,17},{1,16},{2,19},{3,18},{4,21},{5,20},{6,23},{7,22},{8,25},{9,... | collective-permute-start | bytes 786440 | tf_op jit(solution)/shard_map/ppermute | solution.py:484
  61.5 8.8 %copy-start.2 = (s32[128,8]{0,1:T(8,128)S(1)}, s32[128,8]{0,1:T(8,128)}, u32[]{:S(2)}) copy-start(s32[128,8]{0,1:T(8,128)} %param.9) | copy-start | bytes 12292
  61.6 3.7 %collective-permute-start.13 = (bf16[512,128]{1,0:T(8,128)(2,1)S(1)}, bf16[512,128]{1,0:T(8,128)(2,1)S(1)}, u32[]{:S(2)}, u32[]{:S(2)}) collective-permute-start(bf16[512,128]{1,0:T(8,128)(2,1)S(1)} %get-tuple-element.105), channel_id=1, source_target_pairs={{0,1},{1,0},{2,3},{3,2},{4,5},{5,4},{6,7},{7,6},{8,9},{9,8},{10,11... | collective-permute-start | bytes 393224 | tf_op jit(solution)/shard_map/ppermute | solution.py:484
  61.6 5.6 %collective-permute-start.14 = (bf16[512,128]{1,0:T(8,128)(2,1)S(1)}, bf16[512,128]{1,0:T(8,128)(2,1)S(1)}, u32[]{:S(2)}, u32[]{:S(2)}) collective-permute-start(bf16[512,128]{1,0:T(8,128)(2,1)S(1)} %get-tuple-element.106), channel_id=1, source_target_pairs={{0,16},{1,17},{2,18},{3,19},{4,20},{5,21},{6,22},{7,23},{8,24},{9,... | collective-permute-start | bytes 393224 | tf_op jit(solution)/shard_map/ppermute | solution.py:484
  61.8 8.6 %collective-permute-start.15 = (bf16[512,128]{1,0:T(8,128)(2,1)S(1)}, bf16[512,128]{1,0:T(8,128)(2,1)S(1)}, u32[]{:S(2)}, u32[]{:S(2)}) collective-permute-start(bf16[512,128]{1,0:T(8,128)(2,1)S(1)} %get-tuple-element.107), channel_id=1, source_target_pairs={{0,17},{1,16},{2,19},{3,18},{4,21},{5,20},{6,23},{7,22},{8,25},{9,... | collective-permute-start | bytes 393224 | tf_op jit(solution)/shard_map/ppermute | solution.py:484
  65.0 8.4 %collective-permute-start.17 = (bf16[112,128]{1,0:T(8,128)(2,1)S(1)}, bf16[112,128]{1,0:T(8,128)(2,1)S(1)}, u32[]{:S(2)}, u32[]{:S(2)}) collective-permute-start(bf16[112,128]{1,0:T(8,128)(2,1)S(1)} %get-tuple-element.115), channel_id=1, source_target_pairs={{0,1},{1,0},{2,3},{3,2},{4,5},{5,4},{6,7},{7,6},{8,9},{9,8},{10,11... | collective-permute-start | bytes 86024 | tf_op jit(solution)/shard_map/ppermute | solution.py:484
  65.1 8.4 %collective-permute-start.18 = (bf16[112,128]{1,0:T(8,128)(2,1)S(1)}, bf16[112,128]{1,0:T(8,128)(2,1)S(1)}, u32[]{:S(2)}, u32[]{:S(2)}) collective-permute-start(bf16[112,128]{1,0:T(8,128)(2,1)S(1)} %get-tuple-element.116), channel_id=1, source_target_pairs={{0,16},{1,17},{2,18},{3,19},{4,20},{5,21},{6,22},{7,23},{8,24},{9,... | collective-permute-start | bytes 86024 | tf_op jit(solution)/shard_map/ppermute | solution.py:484
  65.2 8.3 %collective-permute-start.19 = (bf16[112,128]{1,0:T(8,128)(2,1)S(1)}, bf16[112,128]{1,0:T(8,128)(2,1)S(1)}, u32[]{:S(2)}, u32[]{:S(2)}) collective-permute-start(bf16[112,128]{1,0:T(8,128)(2,1)S(1)} %get-tuple-element.117), channel_id=1, source_target_pairs={{0,17},{1,16},{2,19},{3,18},{4,21},{5,20},{6,23},{7,22},{8,25},{9,... | collective-permute-start | bytes 86024 | tf_op jit(solution)/shard_map/ppermute | solution.py:484

commit v12 on v11

--- a/solution.py
+++ b/solution.py
@@ -9,7 +9,7 @@
 from jax.sharding import PartitionSpec as P
 
 SEG_DEV = 2
-O = {'p1': 'core_unit', 'z1': 'none', 'p2': 'unit', 'cores': 2, 'core_in': 'none', 'y0': 'unit', 'basis': [], 'ev1': ['y0', 'side0'], 'diag': ['side0'], 'ev2': ['basis'], 'w': ['core'], 'last': ['z2'], 'ka': 0, 'z3_ka': 0, 'w_ka': 1, 'k0': 0, 'k1': 0, 'k2': 1, 'order': 'w'}
+O = {'p1': 'core_unit', 'z1': 'none', 'p2': 'unit', 'cores': 2, 'core_in': 'none', 'y0': 'unit', 'basis': [], 'ev1': ['y0', 'side0'], 'diag': ['side0'], 'ev2': ['basis'], 'w': ['z2'], 'last': ['z2'], 'ka': 0, 'z3_ka': 0, 'w_ka': 1, 'k0': 0, 'k1': 0, 'k2': 1, 'y2': 'c'}
 CORES = 2
 SIDES = 2
 QUAD = 4
@@ -319,47 +319,47 @@
     return list(out[:3]), list(out[3:])
 
 
-def late_kernel(
-    rank, pairs, window, place, groups, bases_ref, *refs
-):
-    start_refs, (tokens, unit_ref), outs = refs[:groups], refs[groups : groups + 2], refs[groups + 2 :]
-    cols = unit_ref.shape[0] // CORES
+def late_kernel(rank, pairs, window, place, groups, bases_ref, *refs):
+    start_refs, tokens, refs = refs[:groups], refs[groups], refs[groups + 1 :]
+    unit_refs, outs = refs[:2], refs[2:]
     per_tile = LANES // rank
     low = lax.broadcasted_iota(jnp.int32, (1, LANES), 1) < rank
     device = lax.axis_index("expert")
     first_core = device % CORES == 0
-    folded = []
-    for half in range(CORES):
-        base = bases_ref[device, place + half]
-        offsets, rows = [], []
-        for g in range(groups):
-            at = jnp.minimum(start_refs[g][0, base] & -ALIGN, pairs - window)
-            offsets.append(at)
-            rows.append(tokens[pl.ds(pl.multiple_of(g * pairs + at, ALIGN), window), :])
-        dense = lax.dot_general(
-            jnp.concatenate(rows, axis=0),
-            unit_ref[half * cols : (half + 1) * cols, :],
-            NT,
-            preferred_element_type=jnp.float32,
-        )
-        found = []
-        for g in range(groups):
-            value = jnp.zeros((window, LANES), jnp.float32)
-            number = offsets[g] + lax.broadcasted_iota(jnp.int32, (window, LANES), 0)
-            for j in range(cols // LANES):
-                edge = [start_refs[g][0, base + j * per_tile + i] for i in range(per_tile + 1)]
-                inside = (number >= jnp.where(low, edge[0], edge[1])) & (
-                    number < jnp.where(low, edge[1], edge[2])
-                )
-                part = dense[g * window : (g + 1) * window, j * LANES : (j + 1) * LANES]
-                value = jnp.where(inside, part, value)
-            found.append(value + pltpu.roll(value, rank, 1))
-        folded.append(found)
-    for g, out in enumerate(outs):
-        one, two = folded[0][g], folded[1][g]
-        zero = jnp.where(first_core, one, two)
-        other = jnp.where(first_core, two, one)
-        out[...] = jnp.where(low, zero, other).astype(out.dtype)
+    for u, unit_ref in enumerate(unit_refs):
+        cols = unit_ref.shape[0] // CORES
+        folded = []
+        for half in range(CORES):
+            base = bases_ref[device, place + u * CORES + half]
+            offsets, rows = [], []
+            for g in range(groups):
+                at = jnp.minimum(start_refs[g][0, base] & -ALIGN, pairs - window)
+                offsets.append(at)
+                rows.append(tokens[pl.ds(pl.multiple_of(g * pairs + at, ALIGN), window), :])
+            dense = lax.dot_general(
+                jnp.concatenate(rows, axis=0),
+                unit_ref[half * cols : (half + 1) * cols, :],
+                NT,
+                preferred_element_type=jnp.float32,
+            )
+            found = []
+            for g in range(groups):
+                value = jnp.zeros((window, LANES), jnp.float32)
+                number = offsets[g] + lax.broadcasted_iota(jnp.int32, (window, LANES), 0)
+                for j in range(cols // LANES):
+                    edge = [start_refs[g][0, base + j * per_tile + i] for i in range(per_tile + 1)]
+                    inside = (number >= jnp.where(low, edge[0], edge[1])) & (
+                        number < jnp.where(low, edge[1], edge[2])
+                    )
+                    part = dense[g * window : (g + 1) * window, j * LANES : (j + 1) * LANES]
+                    value = jnp.where(inside, part, value)
+                found.append(value + pltpu.roll(value, rank, 1))
+            folded.append(found)
+        for g, out in enumerate(outs):
+            one, two = folded[0][g], folded[1][g]
+            zero = jnp.where(first_core, one, two)
+            other = jnp.where(first_core, two, one)
+            out[u * window : (u + 1) * window, :] = jnp.where(low, zero, other).astype(out.dtype)
 
 
 def expand(routes_ref, turned, lines, first, tiles):
@@ -433,21 +433,24 @@
     block,
     sem,
 ):
-    window = own_ref.shape[0]
+    window = own_ref.shape[0] // 2
     pairs = order_ref.shape[0]
     value = own_ref[...]
     for ref in (b_ref, c_ref, d_ref):
         value = value + ref[...].astype(jnp.float32)
     value = value.T.astype(jnp.bfloat16)
-    first = bases_ref[lax.axis_index("expert"), place] // count * count
-    unit = bases_ref[lax.axis_index("expert"), place] // (CORES * held) * (CORES * held)
+    device = lax.axis_index("expert")
+    first = bases_ref[device, place] // count * count
     total = turned_ref[...]
-    for core in range(CORES):
-        at = jnp.minimum(starts_ref[0, unit + core * held] & -ALIGN, pairs - window)
-        rows = order_ref[pl.ds(pl.multiple_of(at, ALIGN), window), :]
-        total = total + jnp.dot(
-            value[core * rank : (core + 1) * rank], rows, preferred_element_type=jnp.float32
-        )
+    for u in range(2):
+        unit = bases_ref[device, place + u * CORES] // (CORES * held) * (CORES * held)
+        for core in range(CORES):
+            at = jnp.minimum(starts_ref[0, unit + core * held] & -ALIGN, pairs - window)
+            total = total + jnp.dot(
+                value[core * rank : (core + 1) * rank, u * window : (u + 1) * window],
+                order_ref[pl.ds(pl.multiple_of(at, ALIGN), window), :],
+                preferred_element_type=jnp.float32,
+            )
     turned[...] = total
     expand(routes_ref, turned, lines, first, count // 8)
     form(lines, basis_ref, 0, rank // 2, block, rank)
@@ -494,9 +497,8 @@
     final = slots - 1
     names_a = [(n, 0) for n in range(final - 1)] + [(0, 1)]
     names_b = [(final - 1, 0)] + [(n, 1) for n in range(1, final - 1)]
-    names_c = [(final, 1)] if O["order"] == "w" else [(final - 1, 1)]
-    names_d = [(final - 1, 1)] if O["order"] == "w" else [(final, 1)]
-    arrival = names_a + names_b + names_c + names_d + [(final, 0)]
+    names_c = [(final - 1, 1)]
+    arrival = names_a + names_b + names_c + [(final, 0), (final, 1)]
 
     def source(z, hops):
         for _ in range(hops):
@@ -743,9 +745,11 @@
     last_piece = group_tie(O["last"], last_piece)
     diagonal_pieces.append(swap(last_piece, 1, 1))
     work(names_b, complete=[(2, [(piece, half) for piece in side_pieces])], cost=COST[O["k0"]])
-    work(names_c, partial=[(3, diagonal_pieces[0], 0, 3 * rows)], cost=COST[O["k1"]])
     sent = work(
-        names_d, partial=[(3, diagonal_pieces[1], 3 * rows, rows)], sends=[1, 2, 3], cost=COST[O["k2"]]
+        names_c if O["y2"] == "c" else [], partial=[(3, diagonal_pieces[0], 0, 3 * rows)], sends=[1, 2] if O["y2"] == "c" else [], cost=COST[O["k1"]]
+    )
+    sent = sent + work(
+        [] if O["y2"] == "c" else names_c, partial=[(3, diagonal_pieces[1], 3 * rows, rows)], sends=[3] if O["y2"] == "c" else [1, 2, 3], cost=COST[O["k2"]]
     )
 
     def returned(arrays):
@@ -754,16 +758,16 @@
         ]
 
     early = returned(sent)
-    place = places - CORES
+    place = places - 2 * CORES
     own_late, *sent = pl.pallas_call(
         functools.partial(late_kernel, rank, pairs, window, place, QUAD),
-        out_shape=[pltpu.VMEM((window, LANES), jnp.float32)]
-        + [pltpu.VMEM((window, LANES), jnp.bfloat16)] * (QUAD - 1),
-        in_specs=[SMEM] * (1 + QUAD) + [VMEM] * 2,
+        out_shape=[pltpu.VMEM((2 * window, LANES), jnp.float32)]
+        + [pltpu.VMEM((2 * window, LANES), jnp.bfloat16)] * (QUAD - 1),
+        in_specs=[SMEM] * (1 + QUAD) + [VMEM] * 3,
         out_specs=[VMEM] * QUAD,
         compiler_params=pltpu.CompilerParams(vmem_limit_bytes=8 * MIB),
         cost_estimate=QUICK,
-    )(bases, *[starts[g] for g in range(QUAD)], in_vmem(state[0]), held[final, 0])
+    )(bases, *[starts[g] for g in range(QUAD)], in_vmem(state[0]), held[final, 0], held[final, 1])
     late = returned(sent)
     *early, own_late = tie(*early, own_late)
     out, turned = pl.pallas_call(

time: 76.7 us -> 75.6 us (0.986)
  waiting for transfers between devices: 12.7 us -> 19.2 us
  starting transfers between devices: 30.8 us -> 24.4 us
    ppermute x4, waiting for transfers between devices: 5.61 us -> 14.1 us  [along(): return lax.ppermute(array, 'expert', pairs_of)]
    ppermute x16, starting transfers between devices: 25.7 us -> 17.8 us  [swap(): return lax.ppermute(array, BOTH, table)]
    ppermute x16, waiting for transfers between devices: 7.13 us -> 5.14 us  [swap(): return lax.ppermute(array, BOTH, table)]
    ppermute x4, starting transfers between devices: 5.14 us -> 6.61 us  [along(): return lax.ppermute(array, 'expert', pairs_of)]
    pallas_call x4, Pallas kernels: 12.8 us -> 11.7 us  [accumulate(): pl.pallas_call(functools.partial(partial_kernel, rank, pairs, window, [(f...]
  transfers between devices with their start and end apart: 20 -> 20, of which waited for: 6 -> 8; matrix products, arithmetic and copies ran while one was open for 0% -> 0% of each run, Pallas kernels for 37% -> 36%
where the time goes in v12:
time: 75.6 us; the launch traced here: 75 us
  Pallas kernels  30.4 us (40%)
  starting transfers between devices  24.4 us (32%)
  waiting for transfers between devices  19.2 us (25%)
    ppermute x16, starting transfers between devices, swap(): return lax.ppermute(array, BOTH, table)  17.8 us
    ppermute x4, waiting for transfers between devices, along(): return lax.ppermute(array, 'expert', pairs_of)  14.1 us
    pallas_call x4, Pallas kernels, accumulate(): pl.pallas_call(functools.partial(partial_kernel, rank, pairs, window, [(f...  11.7 us
    ppermute x4, starting transfers between devices, along(): return lax.ppermute(array, 'expert', pairs_of)  6.61 us
    ppermute x16, waiting for transfers between devices, swap(): return lax.ppermute(array, BOTH, table)  5.14 us
    pallas_call x3, Pallas kernels, permuted(): pl.pallas_call(functools.partial(permute_kernel, plan), out_shape=[rows_s...  4.34 us
    pallas_call x1, Pallas kernels, local(): pl.pallas_call(sort_kernel, out_shape=[pltpu.VMEM(out_grads.shape, jnp.bf...  3.37 us
    pallas_call x1, Pallas kernels, local(): pl.pallas_call(functools.partial(blocks_kernel, rank), out_shape=[jax.Sha...  3.09 us
  transfers between devices with their start and end apart: 20, of which 8 were waited for; matrix products, arithmetic and copies ran while one was open for 0% of the time, Pallas kernels for 36%

profile of v12, /device:TPU:1, one launch (start us, length us, event | category | flops | bytes accessed | tf_op | source)
XLA Modules:
  0.0 75.0 jit_solution(14138284079722655964)
XLA Ops:
  0.0 1.3 %shard_map.73 = (bf16[256,512]{1,0:T(8,128)(2,1)S(1)}, bf16[256,512]{1,0:T(8,128)(2,1)S(1)}) custom-call(bf16[256,2048]{1,0:T(8,128)(2,1)} %bitcast.8), custom_call_target="tpu_custom_call" | custom-call | flops 1 | bytes 1 | tf_op jit(solution)/shard_map/pallas_call | solution.py:525
  1.3 0.1 collective-permute-start
  1.4 0.7 copy-done.1
  2.1 3.4 %shard_map.74 = (bf16[128,8,2048]{2,1,0:T(8,128)(2,1)S(1)}, s32[1,128]{1,0:T(1,128)S(1)}, bf16[16,512]{1,0:T(8,128)(2,1)S(1)}, bf16[1024,1024]{1,0:T(8,128)(2,1)S(1)}, bf16[528,512]{1,0:T(8,128)(2,1)S(1)}) custom-call(s32[8,128]{1,0:T(8,128)S(1)} %bitcast.3, bf16[128,8,2048]{2,1,0:T(8,128)(2,1)} %grads_ref.1), custom_call_target="tpu_custom_call" | custom-call | flops 1 | bytes 1 | tf_op jit(solution)/shard_map/pallas_call | solution.py:549
  5.5 2.7 %collective-permute-start.3 = (bf16[528,512]{1,0:T(8,128)(2,1)S(1)}, bf16[528,512]{1,0:T(8,128)(2,1)S(1)}, u32[]{:S(2)}, u32[]{:S(2)}) collective-permute-start(bf16[528,512]{1,0:T(8,128)(2,1)S(1)} %get-tuple-element.67), channel_id=1, source_target_pairs={{0,16},{1,17},{2,18},{3,19},{4,20},{5,21},{6,22},{7,23},{8,24},{9,... | collective-permute-start | bytes 1622024 | tf_op jit(solution)/shard_map/ppermute | solution.py:487
  8.2 1.3 %collective-permute-start.1 = (bf16[512,512]{1,0:T(8,128)(2,1)S(1)}, bf16[512,512]{1,0:T(8,128)(2,1)S(1)}, u32[]{:S(2)}, u32[]{:S(2)}) collective-permute-start(bf16[512,512]{1,0:T(8,128)(2,1)S(1)} %shard_map.75.refs_5_), channel_id=1, source_target_pairs={{0,4},{1,5},{2,6},{3,7},{4,12},{5,13},{6,14},{7,15},{8,0},{9,1},{1... | collective-permute-start | bytes 1572872 | tf_op jit(solution)/shard_map/ppermute | solution.py:492
  9.6 1.2 %collective-permute-start.2 = (bf16[512,512]{1,0:T(8,128)(2,1)S(1)}, bf16[512,512]{1,0:T(8,128)(2,1)S(1)}, u32[]{:S(2)}, u32[]{:S(2)}) collective-permute-start(bf16[512,512]{1,0:T(8,128)(2,1)S(1)} %shard_map.75.refs_5_), channel_id=1, source_target_pairs={{0,2},{1,3},{2,0},{3,1},{4,6},{5,7},{6,4},{7,5},{8,10},{9,11},{10,... | collective-permute-start | bytes 1572872 | tf_op jit(solution)/shard_map/ppermute | solution.py:487
  10.8 0.7 shard_map.76
  11.5 2.4 %shard_map.77 = (bf16[1024,512]{1,0:T(8,128)(2,1)S(1)}, bf16[528,512]{1,0:T(8,128)(2,1)S(1)}, bf16[512,512]{1,0:T(8,128)(2,1)S(1)}) custom-call(bf16[1024,1024]{1,0:T(8,128)(2,1)S(1)} %get-tuple-element.75.order_ref, bf16[16,512]{1,0:T(8,128)(2,1)S(1)} %get-tuple-element.71.head_ref, bf16[128,8,2048]{2,1,0:T(8,128)(2,1)S(1)} %get-tuple-element.72.grads_ref), custom_call_target="tpu_custom_call" | custom-call | flops 1 | bytes 1 | tf_op jit(solution)/shard_map/pallas_call | solution.py:567
  13.9 0.0 copy-start.3
  13.9 0.9 %collective-permute-start.5 = (bf16[528,512]{1,0:T(8,128)(2,1)S(1)}, bf16[528,512]{1,0:T(8,128)(2,1)S(1)}, u32[]{:S(2)}, u32[]{:S(2)}) collective-permute-start(bf16[528,512]{1,0:T(8,128)(2,1)S(1)} %get-tuple-element.81), channel_id=1, source_target_pairs={{0,1},{1,0},{2,3},{3,2},{4,5},{5,4},{6,7},{7,6},{8,9},{9,8},{10,11... | collective-permute-start | bytes 1622024 | tf_op jit(solution)/shard_map/ppermute | solution.py:487
  14.8 0.3 collective-permute-start.9
  15.1 1.3 %shard_map.78 = (bf16[784,512]{1,0:T(8,128)(2,1)S(1)}, bf16[256,512]{1,0:T(8,128)(2,1)S(1)}) custom-call(bf16[1024,1024]{1,0:T(8,128)(2,1)S(1)} %get-tuple-element.75.order_ref, bf16[16,512]{1,0:T(8,128)(2,1)S(1)} %get-tuple-element.71.head_ref, bf16[128,8,2048]{2,1,0:T(8,128)(2,1)S(1)} %get-tuple-element.72.grads_ref), custom_call_target="tpu_custom_call" | custom-call | flops 1 | bytes 1 | tf_op jit(solution)/shard_map/pallas_call | solution.py:567
  16.4 2.8 %shard_map.79 = (bf16[256,256]{1,0:T(8,128)(2,1)S(1)}, bf16[1024,1024]{1,0:T(8,128)(2,1)S(1)}) custom-call(bf16[128,7168]{1,0:T(8,128)(2,1)} %hidden_ref.1, bf16[64,7168]{1,0:T(8,128)(2,1)} %proj_ref.1, s32[1,128]{1,0:T(1,128)S(1)} %bitcast.7, s32[8,128]{1,0:T(8,128)S(1)} %bitcast.4), custom_call_target="tpu_custom_call" | custom-call | flops 1 | bytes 1 | tf_op jit(solution)/shard_map/pallas_call | solution.py:621
  19.2 1.6 %collective-permute-done.3.refs_3_ = bf16[528,512]{1,0:T(8,128)(2,1)S(1)} collective-permute-done((bf16[528,512]{1,0:T(8,128)(2,1)S(1)}, bf16[528,512]{1,0:T(8,128)(2,1)S(1)}, u32[]{:S(2)}, u32[]{:S(2)}) %collective-permute-start.3) | collective-permute-done | bytes 540704 | tf_op jit(solution)/shard_map/ppermute | solution.py:487
  20.8 0.8 %collective-permute-start.11 = (bf16[512,512]{1,0:T(8,128)(2,1)S(1)}, bf16[512,512]{1,0:T(8,128)(2,1)S(1)}, u32[]{:S(2)}, u32[]{:S(2)}) collective-permute-start(bf16[512,512]{1,0:T(8,128)(2,1)S(1)} %get-tuple-element.92), channel_id=1, source_target_pairs={{0,1},{1,0},{2,3},{3,2},{4,5},{5,4},{6,7},{7,6},{8,9},{9,8},{10,11... | collective-permute-start | bytes 1572872 | tf_op jit(solution)/shard_map/ppermute | solution.py:487
  21.6 0.8 %collective-permute-done.1.refs_6_ = bf16[512,512]{1,0:T(8,128)(2,1)S(1)} collective-permute-done((bf16[512,512]{1,0:T(8,128)(2,1)S(1)}, bf16[512,512]{1,0:T(8,128)(2,1)S(1)}, u32[]{:S(2)}, u32[]{:S(2)}) %collective-permute-start.1) | collective-permute-done | bytes 524320 | tf_op jit(solution)/shard_map/ppermute | solution.py:492
  22.4 0.1 collective-permute-done.2.refs_7_
  22.5 2.3 %collective-permute-start.4 = (bf16[512,512]{1,0:T(8,128)(2,1)S(1)}, bf16[512,512]{1,0:T(8,128)(2,1)S(1)}, u32[]{:S(2)}, u32[]{:S(2)}) collective-permute-start(bf16[512,512]{1,0:T(8,128)(2,1)S(1)} %collective-permute-done.1.refs_6_), channel_id=1, source_target_pairs={{0,4},{1,5},{2,6},{3,7},{4,12},{5,13},{6,14},{7,15},{8,0},{9,1},{1... | collective-permute-start | bytes 1572872 | tf_op jit(solution)/shard_map/ppermute | solution.py:492
  24.8 1.8 %collective-permute-start.6 = (bf16[784,512]{1,0:T(8,128)(2,1)S(1)}, bf16[784,512]{1,0:T(8,128)(2,1)S(1)}, u32[]{:S(2)}, u32[]{:S(2)}) collective-permute-start(bf16[784,512]{1,0:T(8,128)(2,1)S(1)} %get-tuple-element.85), channel_id=1, source_target_pairs={{0,17},{1,16},{2,19},{3,18},{4,21},{5,20},{6,23},{7,22},{8,25},{9,... | collective-permute-start | bytes 2408456 | tf_op jit(solution)/shard_map/ppermute | solution.py:487
  26.6 0.0 collective-permute-done.5.refs_3_
  26.7 1.2 %collective-permute-start.10 = (bf16[512,512]{1,0:T(8,128)(2,1)S(1)}, bf16[512,512]{1,0:T(8,128)(2,1)S(1)}, u32[]{:S(2)}, u32[]{:S(2)}) collective-permute-start(bf16[512,512]{1,0:T(8,128)(2,1)S(1)} %collective-permute-done.1.refs_6_), channel_id=1, source_target_pairs={{0,2},{1,3},{2,0},{3,1},{4,6},{5,7},{6,4},{7,5},{8,10},{9,11},{10,... | collective-permute-start | bytes 1572872 | tf_op jit(solution)/shard_map/ppermute | solution.py:487
  27.9 7.5 %collective-permute-done.4.refs_5_ = bf16[512,512]{1,0:T(8,128)(2,1)S(1)} collective-permute-done((bf16[512,512]{1,0:T(8,128)(2,1)S(1)}, bf16[512,512]{1,0:T(8,128)(2,1)S(1)}, u32[]{:S(2)}, u32[]{:S(2)}) %collective-permute-start.4) | collective-permute-done | bytes 524320 | tf_op jit(solution)/shard_map/ppermute | solution.py:492
  35.4 1.2 %collective-permute-start.8 = (bf16[512,512]{1,0:T(8,128)(2,1)S(1)}, bf16[512,512]{1,0:T(8,128)(2,1)S(1)}, u32[]{:S(2)}, u32[]{:S(2)}) collective-permute-start(bf16[512,512]{1,0:T(8,128)(2,1)S(1)} %collective-permute-done.4.refs_5_), channel_id=1, source_target_pairs={{0,2},{1,3},{2,0},{3,1},{4,6},{5,7},{6,4},{7,5},{8,10},{9,11},{10,... | collective-permute-start | bytes 1572872 | tf_op jit(solution)/shard_map/ppermute | solution.py:487
  36.6 0.0 collective-permute-done.11.refs_4_
  36.6 2.6 %shard_map.80 = (bf16[4096,512]{1,0:T(8,128)(2,1)S(1)}, bf16[16,256,512]{2,1,0:T(8,128)(2,1)S(1)}, f32[4096,128]{1,0:T(8,128)S(1)}) custom-call(s32[16,16]{1,0:T(8,128)S(1)} %copy-done, s32[1,128]{1,0:T(1,128)S(1)} %get-tuple-element.65.refs_0_.starts_ref, s32[1,128]{1,0:T(1,128)S(1)} %slice_add_fusion.2.refs_1_, ...), custom_call_target="tpu_custom_call" | custom-call | flops 1 | bytes 1 | tf_op jit(solution)/shard_map/pallas_call | solution.py:299
  39.2 1.5 %collective-permute-start.15 = (bf16[512,512]{1,0:T(8,128)(2,1)S(1)}, bf16[512,512]{1,0:T(8,128)(2,1)S(1)}, u32[]{:S(2)}, u32[]{:S(2)}) collective-permute-start(bf16[512,512]{1,0:T(8,128)(2,1)S(1)} %collective-permute-done.4.refs_5_), channel_id=1, source_target_pairs={{0,4},{1,5},{2,6},{3,7},{4,12},{5,13},{6,14},{7,15},{8,0},{9,1},{1... | collective-permute-start | bytes 1572872 | tf_op jit(solution)/shard_map/ppermute | solution.py:492
  40.7 0.0 collective-permute-done.9.refs_4_
  40.7 3.0 %collective-permute-start.7 = (bf16[256,512]{1,0:T(8,128)(2,1)S(1)}, bf16[256,512]{1,0:T(8,128)(2,1)S(1)}, u32[]{:S(2)}, u32[]{:S(2)}) collective-permute-start(bf16[256,512]{1,0:T(8,128)(2,1)S(1)} %get-tuple-element.89), channel_id=1, source_target_pairs={{0,17},{1,16},{2,19},{3,18},{4,21},{5,20},{6,23},{7,22},{8,25},{9,... | collective-permute-start | bytes 786440 | tf_op jit(solution)/shard_map/ppermute | solution.py:487
  43.7 1.5 %collective-permute-start.16 = (bf16[512,512]{1,0:T(8,128)(2,1)S(1)}, bf16[512,512]{1,0:T(8,128)(2,1)S(1)}, u32[]{:S(2)}, u32[]{:S(2)}) collective-permute-start(bf16[512,512]{1,0:T(8,128)(2,1)S(1)} %collective-permute-done.2.refs_7_), channel_id=1, source_target_pairs={{0,8},{1,9},{2,10},{3,11},{4,0},{5,1},{6,2},{7,3},{8,12},{9,13},{1... | collective-permute-start | bytes 1572872 | tf_op jit(solution)/shard_map/ppermute | solution.py:492
  45.2 3.3 %shard_map.81 = (bf16[4096,512]{1,0:T(8,128)(2,1)S(1)}, bf16[16,256,512]{2,1,0:T(8,128)(2,1)S(1)}, f32[4096,128]{1,0:T(8,128)S(1)}) custom-call(s32[16,16]{1,0:T(8,128)S(1)} %copy-done, s32[1,128]{1,0:T(1,128)S(1)} %get-tuple-element.65.refs_0_.starts_ref, ...), custom_call_target="tpu_custom_call", output_to_operand_aliasing={{0}: (8, {}), {1}: (9, {}), {2}: (10, {})} | custom-call | flops 1 | bytes 1 | tf_op jit(solution)/shard_map/pallas_call | solution.py:299
  48.5 1.1 %collective-permute-done.6.refs_4_ = bf16[784,512]{1,0:T(8,128)(2,1)S(1)} collective-permute-done((bf16[784,512]{1,0:T(8,128)(2,1)S(1)}, bf16[784,512]{1,0:T(8,128)(2,1)S(1)}, u32[]{:S(2)}, u32[]{:S(2)}) %collective-permute-start.6) | collective-permute-done | bytes 802848 | tf_op jit(solution)/shard_map/ppermute | solution.py:487
  49.7 1.8 %collective-permute-done.8.refs_5_ = bf16[512,512]{1,0:T(8,128)(2,1)S(1)} collective-permute-done((bf16[512,512]{1,0:T(8,128)(2,1)S(1)}, bf16[512,512]{1,0:T(8,128)(2,1)S(1)}, u32[]{:S(2)}, u32[]{:S(2)}) %collective-permute-start.8) | collective-permute-done | bytes 524320 | tf_op jit(solution)/shard_map/ppermute | solution.py:487
  51.5 3.9 %shard_map.82 = (bf16[4096,512]{1,0:T(8,128)(2,1)S(1)}, bf16[16,256,512]{2,1,0:T(8,128)(2,1)S(1)}, f32[4096,128]{1,0:T(8,128)S(1)}, bf16[512,128]{1,0:T(8,128)(2,1)S(1)}, bf16[512,128]{1,0:T(8,128)(2,1)S(1)}) custom-call(s32[16,16]{1,0:T(8,128)S(1)} %copy-done, ...), custom_call_target="tpu_custom_call", output_to_operand_aliasing={{0}: (7, {}), {1}: (8, {}), {2}: (9, {})} | custom-call | flops 1 | bytes 1 | tf_op jit(solution)/shard_map/pallas_call | solution.py:299
  55.3 2.0 %shard_map.83 = (bf16[4096,512]{1,0:T(8,128)(2,1)S(1)}, bf16[16,256,512]{2,1,0:T(8,128)(2,1)S(1)}, f32[4096,128]{1,0:T(8,128)S(1)}, bf16[512,128]{1,0:T(8,128)(2,1)S(1)}) custom-call(s32[16,16]{1,0:T(8,128)S(1)} %copy-done, s32[1,128]{1,0:T(1,128)S(1)} %get-tuple-element.65.refs_0_.starts_ref, ...), custom_call_target="tpu_custom_call", output_to_operand_aliasing={{0}: (6, {}), {1}: (7, {}), {2}: (8, {})} | custom-call | flops 1000000000 | bytes 1 | tf_op jit(solution)/shard_map/pallas_call | solution.py:299
  57.4 0.0 copy-start.2
  57.4 1.3 %collective-permute-start.14 = (bf16[512,128]{1,0:T(8,128)(2,1)S(1)}, bf16[512,128]{1,0:T(8,128)(2,1)S(1)}, u32[]{:S(2)}, u32[]{:S(2)}) collective-permute-start(bf16[512,128]{1,0:T(8,128)(2,1)S(1)} %get-tuple-element.108), channel_id=1, source_target_pairs={{0,17},{1,16},{2,19},{3,18},{4,21},{5,20},{6,23},{7,22},{8,25},{9,... | collective-permute-start | bytes 393224 | tf_op jit(solution)/shard_map/ppermute | solution.py:487
  58.7 0.3 collective-permute-start.12
  59.0 0.5 collective-permute-start.13
  59.6 5.8 %collective-permute-done.16.refs_6_ = bf16[512,512]{1,0:T(8,128)(2,1)S(1)} collective-permute-done((bf16[512,512]{1,0:T(8,128)(2,1)S(1)}, bf16[512,512]{1,0:T(8,128)(2,1)S(1)}, u32[]{:S(2)}, u32[]{:S(2)}) %collective-permute-start.16) | collective-permute-done | bytes 524320 | tf_op jit(solution)/shard_map/ppermute | solution.py:492
  65.4 1.5 %shard_map.84 = (f32[224,128]{1,0:T(8,128)S(1)}, bf16[224,128]{1,0:T(8,128)(2,1)S(1)}, bf16[224,128]{1,0:T(8,128)(2,1)S(1)}, bf16[224,128]{1,0:T(8,128)(2,1)S(1)}) custom-call(s32[16,16]{1,0:T(8,128)S(1)} %copy-done, s32[1,128]{1,0:T(1,128)S(1)} %get-tuple-element.65.refs_0_.starts_ref, s32[1,128]{1,0:T(1,128)S(1)} %slice_add_fusion.2.refs_1_, ...), custom_call_target="tpu_custom_call" | custom-call | flops 1 | bytes 1 | tf_op jit(solution)/shard_map/pallas_call | solution.py:762
  66.9 0.4 collective-permute-start.17
  67.3 1.4 %collective-permute-start.18 = (bf16[224,128]{1,0:T(8,128)(2,1)S(1)}, bf16[224,128]{1,0:T(8,128)(2,1)S(1)}, u32[]{:S(2)}, u32[]{:S(2)}) collective-permute-start(bf16[224,128]{1,0:T(8,128)(2,1)S(1)} %get-tuple-element.118), channel_id=1, source_target_pairs={{0,16},{1,17},{2,18},{3,19},{4,20},{5,21},{6,22},{7,23},{8,24},{9,... | collective-permute-start | bytes 172040 | tf_op jit(solution)/shard_map/ppermute | solution.py:487
  68.7 0.4 collective-permute-start.19
  69.1 0.0 collective-permute-done.13.c_ref
  69.1 3.1 %shard_map.85 = (bf16[2,64,4096]{2,1,0:T(8,128)(2,1)}, f32[64,1024]{1,0:T(8,128)S(1)}) custom-call(s32[8,128]{1,0:T(8,128)S(1)} %bitcast.5, bf16[256,256]{1,0:T(8,128)(2,1)S(1)} %get-tuple-element.79.basis_ref, bf16[1024,1024]{1,0:T(8,128)(2,1)S(1)} %get-tuple-element.80.order_ref, f32[4096,128]{1,0:T(8,128)S(1)} %get-tuple-element.105.total_ref, ...), custom_call_target="tpu_custom_call" | custom-call | flops 1 | bytes 1 | tf_op jit(solution)/shard_map/pallas_call | solution.py:773
  72.2 0.5 collective-permute-done.19.d_ref
  72.7 2.2 %shard_map.86 = bf16[2,64,4096]{2,1,0:T(8,128)(2,1)} custom-call(s32[16,16]{1,0:T(8,128)S(1)} %copy-done, s32[1,128]{1,0:T(1,128)S(1)} %get-tuple-element.65.refs_0_.starts_ref, s32[8,128]{1,0:T(8,128)S(1)} %bitcast.6, bf16[256,256]{1,0:T(8,128)(2,1)S(1)} %get-tuple-element.79.basis_ref, ...), custom_call_target="tpu_custom_call", output_to_operand_aliasing={{}: (10, {})} | custom-call | flops 1 | bytes 1 | tf_op jit(solution)/shard_map/pallas_call | solution.py:786
  (20 shorter events, 0.1 us)
Async XLA Ops:
  1.3 6.9 %collective-permute-start = (bf16[256,512]{1,0:T(8,128)(2,1)S(1)}, bf16[256,512]{1,0:T(8,128)(2,1)S(1)}, u32[]{:S(2)}, u32[]{:S(2)}) collective-permute-start(bf16[256,512]{1,0:T(8,128)(2,1)S(1)} %get-tuple-element.63), channel_id=1, source_target_pairs={{0,1},{1,0},{2,3},{3,2},{4,5},{5,4},{6,7},{7,6},{8,9},{9,8},{10,11... | collective-permute-start | bytes 786440 | tf_op jit(solution)/shard_map/ppermute | solution.py:487
  1.4 0.7 copy-start.1
  5.5 15.4 %collective-permute-start.3 = (bf16[528,512]{1,0:T(8,128)(2,1)S(1)}, bf16[528,512]{1,0:T(8,128)(2,1)S(1)}, u32[]{:S(2)}, u32[]{:S(2)}) collective-permute-start(bf16[528,512]{1,0:T(8,128)(2,1)S(1)} %get-tuple-element.67), channel_id=1, source_target_pairs={{0,16},{1,17},{2,18},{3,19},{4,20},{5,21},{6,22},{7,23},{8,24},{9,... | collective-permute-start | bytes 1622024 | tf_op jit(solution)/shard_map/ppermute | solution.py:487
  8.2 14.2 %collective-permute-start.1 = (bf16[512,512]{1,0:T(8,128)(2,1)S(1)}, bf16[512,512]{1,0:T(8,128)(2,1)S(1)}, u32[]{:S(2)}, u32[]{:S(2)}) collective-permute-start(bf16[512,512]{1,0:T(8,128)(2,1)S(1)} %shard_map.75.refs_5_), channel_id=1, source_target_pairs={{0,4},{1,5},{2,6},{3,7},{4,12},{5,13},{6,14},{7,15},{8,0},{9,1},{1... | collective-permute-start | bytes 1572872 | tf_op jit(solution)/shard_map/ppermute | solution.py:492
  9.6 12.9 %collective-permute-start.2 = (bf16[512,512]{1,0:T(8,128)(2,1)S(1)}, bf16[512,512]{1,0:T(8,128)(2,1)S(1)}, u32[]{:S(2)}, u32[]{:S(2)}) collective-permute-start(bf16[512,512]{1,0:T(8,128)(2,1)S(1)} %shard_map.75.refs_5_), channel_id=1, source_target_pairs={{0,2},{1,3},{2,0},{3,1},{4,6},{5,7},{6,4},{7,5},{8,10},{9,11},{10,... | collective-permute-start | bytes 1572872 | tf_op jit(solution)/shard_map/ppermute | solution.py:487
  13.9 2.5 %copy-start.3 = (s32[128]{0:T(128)S(1)}, s32[128]{0:T(128)}, u32[]{:S(2)}) copy-start(s32[128]{0:T(128)} %param.10) | copy-start | bytes 1540
  13.9 12.7 %collective-permute-start.5 = (bf16[528,512]{1,0:T(8,128)(2,1)S(1)}, bf16[528,512]{1,0:T(8,128)(2,1)S(1)}, u32[]{:S(2)}, u32[]{:S(2)}) collective-permute-start(bf16[528,512]{1,0:T(8,128)(2,1)S(1)} %get-tuple-element.81), channel_id=1, source_target_pairs={{0,1},{1,0},{2,3},{3,2},{4,5},{5,4},{6,7},{7,6},{8,9},{9,8},{10,11... | collective-permute-start | bytes 1622024 | tf_op jit(solution)/shard_map/ppermute | solution.py:487
  14.8 25.9 %collective-permute-start.9 = (bf16[512,512]{1,0:T(8,128)(2,1)S(1)}, bf16[512,512]{1,0:T(8,128)(2,1)S(1)}, u32[]{:S(2)}, u32[]{:S(2)}) collective-permute-start(bf16[512,512]{1,0:T(8,128)(2,1)S(1)} %shard_map.76), channel_id=1, source_target_pairs={{0,16},{1,17},{2,18},{3,19},{4,20},{5,21},{6,22},{7,23},{8,24},{9,... | collective-permute-start | bytes 1572872 | tf_op jit(solution)/shard_map/ppermute | solution.py:487
  15.1 21.5 %copy-start = (s32[16,16]{1,0:T(8,128)S(1)}, s32[16,16]{1,0:T(8,128)}, u32[]{:S(2)}) copy-start(s32[16,16]{1,0:T(8,128)} %constant.4.clone.bases_ref) | copy-start | bytes 3076
  20.8 15.8 %collective-permute-start.11 = (bf16[512,512]{1,0:T(8,128)(2,1)S(1)}, bf16[512,512]{1,0:T(8,128)(2,1)S(1)}, u32[]{:S(2)}, u32[]{:S(2)}) collective-permute-start(bf16[512,512]{1,0:T(8,128)(2,1)S(1)} %get-tuple-element.92), channel_id=1, source_target_pairs={{0,1},{1,0},{2,3},{3,2},{4,5},{5,4},{6,7},{7,6},{8,9},{9,8},{10,11... | collective-permute-start | bytes 1572872 | tf_op jit(solution)/shard_map/ppermute | solution.py:487
  22.5 12.9 %collective-permute-start.4 = (bf16[512,512]{1,0:T(8,128)(2,1)S(1)}, bf16[512,512]{1,0:T(8,128)(2,1)S(1)}, u32[]{:S(2)}, u32[]{:S(2)}) collective-permute-start(bf16[512,512]{1,0:T(8,128)(2,1)S(1)} %collective-permute-done.1.refs_6_), channel_id=1, source_target_pairs={{0,4},{1,5},{2,6},{3,7},{4,12},{5,13},{6,14},{7,15},{8,0},{9,1},{1... | collective-permute-start | bytes 1572872 | tf_op jit(solution)/shard_map/ppermute | solution.py:492
  24.8 24.8 %collective-permute-start.6 = (bf16[784,512]{1,0:T(8,128)(2,1)S(1)}, bf16[784,512]{1,0:T(8,128)(2,1)S(1)}, u32[]{:S(2)}, u32[]{:S(2)}) collective-permute-start(bf16[784,512]{1,0:T(8,128)(2,1)S(1)} %get-tuple-element.85), channel_id=1, source_target_pairs={{0,17},{1,16},{2,19},{3,18},{4,21},{5,20},{6,23},{7,22},{8,25},{9,... | collective-permute-start | bytes 2408456 | tf_op jit(solution)/shard_map/ppermute | solution.py:487
  26.7 17.1 %collective-permute-start.10 = (bf16[512,512]{1,0:T(8,128)(2,1)S(1)}, bf16[512,512]{1,0:T(8,128)(2,1)S(1)}, u32[]{:S(2)}, u32[]{:S(2)}) collective-permute-start(bf16[512,512]{1,0:T(8,128)(2,1)S(1)} %collective-permute-done.1.refs_6_), channel_id=1, source_target_pairs={{0,2},{1,3},{2,0},{3,1},{4,6},{5,7},{6,4},{7,5},{8,10},{9,11},{10,... | collective-permute-start | bytes 1572872 | tf_op jit(solution)/shard_map/ppermute | solution.py:487
  35.4 16.1 %collective-permute-start.8 = (bf16[512,512]{1,0:T(8,128)(2,1)S(1)}, bf16[512,512]{1,0:T(8,128)(2,1)S(1)}, u32[]{:S(2)}, u32[]{:S(2)}) collective-permute-start(bf16[512,512]{1,0:T(8,128)(2,1)S(1)} %collective-permute-done.4.refs_5_), channel_id=1, source_target_pairs={{0,2},{1,3},{2,0},{3,1},{4,6},{5,7},{6,4},{7,5},{8,10},{9,11},{10,... | collective-permute-start | bytes 1572872 | tf_op jit(solution)/shard_map/ppermute | solution.py:487
  39.2 26.1 %collective-permute-start.15 = (bf16[512,512]{1,0:T(8,128)(2,1)S(1)}, bf16[512,512]{1,0:T(8,128)(2,1)S(1)}, u32[]{:S(2)}, u32[]{:S(2)}) collective-permute-start(bf16[512,512]{1,0:T(8,128)(2,1)S(1)} %collective-permute-done.4.refs_5_), channel_id=1, source_target_pairs={{0,4},{1,5},{2,6},{3,7},{4,12},{5,13},{6,14},{7,15},{8,0},{9,1},{1... | collective-permute-start | bytes 1572872 | tf_op jit(solution)/shard_map/ppermute | solution.py:492
  40.7 14.7 %collective-permute-start.7 = (bf16[256,512]{1,0:T(8,128)(2,1)S(1)}, bf16[256,512]{1,0:T(8,128)(2,1)S(1)}, u32[]{:S(2)}, u32[]{:S(2)}) collective-permute-start(bf16[256,512]{1,0:T(8,128)(2,1)S(1)} %get-tuple-element.89), channel_id=1, source_target_pairs={{0,17},{1,16},{2,19},{3,18},{4,21},{5,20},{6,23},{7,22},{8,25},{9,... | collective-permute-start | bytes 786440 | tf_op jit(solution)/shard_map/ppermute | solution.py:487
  43.7 21.6 %collective-permute-start.16 = (bf16[512,512]{1,0:T(8,128)(2,1)S(1)}, bf16[512,512]{1,0:T(8,128)(2,1)S(1)}, u32[]{:S(2)}, u32[]{:S(2)}) collective-permute-start(bf16[512,512]{1,0:T(8,128)(2,1)S(1)} %collective-permute-done.2.refs_7_), channel_id=1, source_target_pairs={{0,8},{1,9},{2,10},{3,11},{4,0},{5,1},{6,2},{7,3},{8,12},{9,13},{1... | collective-permute-start | bytes 1572872 | tf_op jit(solution)/shard_map/ppermute | solution.py:492
  57.4 11.8 %copy-start.2 = (s32[128,8]{0,1:T(8,128)S(1)}, s32[128,8]{0,1:T(8,128)}, u32[]{:S(2)}) copy-start(s32[128,8]{0,1:T(8,128)} %param.9) | copy-start | bytes 12292
  57.4 11.3 %collective-permute-start.14 = (bf16[512,128]{1,0:T(8,128)(2,1)S(1)}, bf16[512,128]{1,0:T(8,128)(2,1)S(1)}, u32[]{:S(2)}, u32[]{:S(2)}) collective-permute-start(bf16[512,128]{1,0:T(8,128)(2,1)S(1)} %get-tuple-element.108), channel_id=1, source_target_pairs={{0,17},{1,16},{2,19},{3,18},{4,21},{5,20},{6,23},{7,22},{8,25},{9,... | collective-permute-start | bytes 393224 | tf_op jit(solution)/shard_map/ppermute | solution.py:487
  58.7 10.4 %collective-permute-start.12 = (bf16[512,128]{1,0:T(8,128)(2,1)S(1)}, bf16[512,128]{1,0:T(8,128)(2,1)S(1)}, u32[]{:S(2)}, u32[]{:S(2)}) collective-permute-start(bf16[512,128]{1,0:T(8,128)(2,1)S(1)} %get-tuple-element.106), channel_id=1, source_target_pairs={{0,1},{1,0},{2,3},{3,2},{4,5},{5,4},{6,7},{7,6},{8,9},{9,8},{10,11... | collective-permute-start | bytes 393224 | tf_op jit(solution)/shard_map/ppermute | solution.py:487
  59.0 10.1 %collective-permute-start.13 = (bf16[512,128]{1,0:T(8,128)(2,1)S(1)}, bf16[512,128]{1,0:T(8,128)(2,1)S(1)}, u32[]{:S(2)}, u32[]{:S(2)}) collective-permute-start(bf16[512,128]{1,0:T(8,128)(2,1)S(1)} %get-tuple-element.107), channel_id=1, source_target_pairs={{0,16},{1,17},{2,18},{3,19},{4,20},{5,21},{6,22},{7,23},{8,24},{9,... | collective-permute-start | bytes 393224 | tf_op jit(solution)/shard_map/ppermute | solution.py:487
  66.9 5.3 %collective-permute-start.17 = (bf16[224,128]{1,0:T(8,128)(2,1)S(1)}, bf16[224,128]{1,0:T(8,128)(2,1)S(1)}, u32[]{:S(2)}, u32[]{:S(2)}) collective-permute-start(bf16[224,128]{1,0:T(8,128)(2,1)S(1)} %get-tuple-element.117), channel_id=1, source_target_pairs={{0,1},{1,0},{2,3},{3,2},{4,5},{5,4},{6,7},{7,6},{8,9},{9,8},{10,11... | collective-permute-start | bytes 172040 | tf_op jit(solution)/shard_map/ppermute | solution.py:487
  67.3 4.9 %collective-permute-start.18 = (bf16[224,128]{1,0:T(8,128)(2,1)S(1)}, bf16[224,128]{1,0:T(8,128)(2,1)S(1)}, u32[]{:S(2)}, u32[]{:S(2)}) collective-permute-start(bf16[224,128]{1,0:T(8,128)(2,1)S(1)} %get-tuple-element.118), channel_id=1, source_target_pairs={{0,16},{1,17},{2,18},{3,19},{4,20},{5,21},{6,22},{7,23},{8,24},{9,... | collective-permute-start | bytes 172040 | tf_op jit(solution)/shard_map/ppermute | solution.py:487
  68.7 4.0 %collective-permute-start.19 = (bf16[224,128]{1,0:T(8,128)(2,1)S(1)}, bf16[224,128]{1,0:T(8,128)(2,1)S(1)}, u32[]{:S(2)}, u32[]{:S(2)}) collective-permute-start(bf16[224,128]{1,0:T(8,128)(2,1)S(1)} %get-tuple-element.119), channel_id=1, source_target_pairs={{0,17},{1,16},{2,19},{3,18},{4,21},{5,20},{6,23},{7,22},{8,25},{9,... | collective-permute-start | bytes 172040 | tf_op jit(solution)/shard_map/ppermute | solution.py:487

commit v13 on v12

--- a/solution.py
+++ b/solution.py
@@ -9,7 +9,7 @@
 from jax.sharding import PartitionSpec as P
 
 SEG_DEV = 2
-O = {'p1': 'core_unit', 'z1': 'none', 'p2': 'unit', 'cores': 2, 'core_in': 'none', 'y0': 'unit', 'basis': [], 'ev1': ['y0', 'side0'], 'diag': ['side0'], 'ev2': ['basis'], 'w': ['z2'], 'last': ['z2'], 'ka': 0, 'z3_ka': 0, 'w_ka': 1, 'k0': 0, 'k1': 0, 'k2': 1, 'y2': 'c'}
+O = {'p1': 'core_unit', 'z1': 'none', 'p2': 'unit', 'cores': 2, 'core_in': 'none', 'y0': 'unit', 'basis': [], 'ev1': ['side0'], 'diag': ['side0'], 'ev2': ['basis', 'side0'], 'w': ['basis', 'core'], 'last': ['z2'], 'ka': 0, 'z3_ka': 0, 'w_ka': 0, 'k0': 1, 'k1': 0, 'k2': 1, 'y2': 'c'}
 CORES = 2
 SIDES = 2
 QUAD = 4
@@ -73,18 +73,22 @@
 
 def sort_kernel(
     routes_ref,
+    weight_ref,
     grads_ref,
     held_ref,
+    mine_ref,
+    core_ref,
     starts_ref,
     head_ref,
     order_ref,
     piece_ref,
+    stage,
     sems,
 ):
     width = piece_ref.shape[1]
-    count = sems.shape[0]
+    count = sems.shape[0] - 1
     part = grads_ref.shape[0] // count
-    copies = []
+    copies = [pltpu.make_async_copy(weight_ref, stage, sems.at[count])]
     for n in range(count):
         here = pl.ds(n * part, part)
         copies.append(pltpu.make_async_copy(grads_ref.at[here], held_ref.at[here], sems.at[n]))
@@ -108,7 +112,10 @@
     for first in range(0, pairs, rows):
         ids = first + lax.broadcasted_iota(jnp.int32, (rows, pairs), 0)
         order_ref[first : first + rows, :] = jnp.where(place == ids, 1.0, 0.0).astype(jnp.bfloat16)
-    for copy in copies:
+    copies[0].wait()
+    core_ref[...] = stage[:, columns_of(1, width)]
+    mine_ref[...] = stage[:, columns_of(0, width)]
+    for copy in copies[1:]:
         copy.wait()
     piece_ref[0:rows, :] = jnp.dot(
         order_ref[0:rows, :],
@@ -116,24 +123,6 @@
         preferred_element_type=jnp.float32,
     ).astype(jnp.bfloat16)
     piece_ref[rows:, :] = head_ref[...]
-
-
-def weights_kernel(weight_ref, mine_ref, core_ref, stage, sems):
-    rows, width = mine_ref.shape
-    count = sems.shape[0]
-    part = rows // count
-    copies = [
-        pltpu.make_async_copy(
-            weight_ref.at[pl.ds(n * part, part)], stage.at[pl.ds(n * part, part)], sems.at[n]
-        )
-        for n in range(count)
-    ]
-    for copy in copies:
-        copy.start()
-    for copy in copies:
-        copy.wait()
-    core_ref[...] = stage[:, columns_of(1, width)]
-    mine_ref[...] = stage[:, columns_of(0, width)]
 
 
 def join_kernel(one_ref, two_ref, out_ref):
@@ -522,15 +511,25 @@
     def rows_shape(count):
         return pltpu.VMEM((count, quarter), jnp.bfloat16)
 
-    mine_unit, core_unit = pl.pallas_call(
-        weights_kernel,
-        out_shape=[unit_shape, unit_shape],
-        in_specs=[HBM],
-        out_specs=[VMEM] * 2,
-        scratch_shapes=[pltpu.VMEM((cols, width), jnp.bfloat16), pltpu.SemaphoreType.DMA((4,))],
-        compiler_params=pltpu.CompilerParams(vmem_limit_bytes=8 * MIB),
+    by_rank = routes.T
+    edges = -(-(experts + 1) // LANES) * LANES
+    held_grads, mine_unit, core_unit, own_starts, head, order, first_piece = pl.pallas_call(
+        sort_kernel,
+        out_shape=[
+            pltpu.VMEM(out_grads.shape, jnp.bfloat16),
+            unit_shape,
+            unit_shape,
+            jax.ShapeDtypeStruct((1, edges), jnp.int32),
+            rows_shape(ALIGN),
+            order_shape,
+            rows_shape(2 * rows + ALIGN),
+        ],
+        in_specs=[VMEM, HBM, HBM],
+        out_specs=[VMEM] * 7,
+        scratch_shapes=[pltpu.VMEM((cols, width), jnp.bfloat16), pltpu.SemaphoreType.DMA((9,))],
+        compiler_params=pltpu.CompilerParams(vmem_limit_bytes=12 * MIB),
         cost_estimate=QUICK,
-    )(in_hbm(out_proj.reshape(cols, width)))
+    )(by_rank, in_hbm(out_proj.reshape(cols, width)), in_hbm(out_grads))
     other_unit = swap(core_unit, 0, 1)
     unit = pl.pallas_call(
         join_kernel,
@@ -540,27 +539,6 @@
         compiler_params=pltpu.CompilerParams(vmem_limit_bytes=4 * MIB),
         cost_estimate=QUICK,
     )(mine_unit, other_unit)
-    by_rank = routes.T
-    if O["p1"] == "core_unit":
-        by_rank, _ = tie(by_rank, core_unit)
-    elif O["p1"] == "unit":
-        by_rank, _ = tie(by_rank, unit)
-    edges = -(-(experts + 1) // LANES) * LANES
-    held_grads, own_starts, head, order, first_piece = pl.pallas_call(
-        sort_kernel,
-        out_shape=[
-            pltpu.VMEM(out_grads.shape, jnp.bfloat16),
-            jax.ShapeDtypeStruct((1, edges), jnp.int32),
-            rows_shape(ALIGN),
-            order_shape,
-            rows_shape(2 * rows + ALIGN),
-        ],
-        in_specs=[VMEM, HBM],
-        out_specs=[VMEM] * 5,
-        scratch_shapes=[pltpu.SemaphoreType.DMA((8,))],
-        compiler_params=pltpu.CompilerParams(vmem_limit_bytes=12 * MIB),
-        cost_estimate=QUICK,
-    )(by_rank, in_hbm(out_grads))
 
     def permuted(plan, headed, *after):
         held, *_ = tie(order, *after)

time: 75.6 us -> 74.5 us (0.985)
  Pallas kernels: 30.4 us -> 29 us
  starting transfers between devices: 24.4 us -> 23.1 us
  waiting for transfers between devices: 19.2 us -> 20.2 us
    ppermute x16, waiting for transfers between devices: 5.14 us -> 17 us  [swap(): return lax.ppermute(array, BOTH, table)]
    ppermute x4, waiting for transfers between devices: 14.1 us -> 3.16 us  [along(): return lax.ppermute(array, 'expert', pairs_of)]
    ppermute x4, starting transfers between devices: 6.61 us -> 4.33 us  [along(): return lax.ppermute(array, 'expert', pairs_of)]
    pallas_call x1 -> x0, Pallas kernels: 1.26 us -> none  [local(): pl.pallas_call(weights_kernel, out_shape=[unit_shape, unit_shape], in_spe...]
    ppermute x16, starting transfers between devices: 17.8 us -> 18.8 us  [swap(): return lax.ppermute(array, BOTH, table)]
  transfers between devices with their start and end apart: 20 -> 20, of which waited for: 8 -> 6; matrix products, arithmetic and copies ran while one was open for 0% -> 0% of each run, Pallas kernels for 36% -> 32%
where the time goes in v13:
time: 74.5 us; the launch traced here: 73.3 us
  Pallas kernels  29 us (39%)
  starting transfers between devices  23.1 us (31%)
  waiting for transfers between devices  20.2 us (27%)
    ppermute x16, starting transfers between devices, swap(): return lax.ppermute(array, BOTH, table)  18.8 us
    ppermute x16, waiting for transfers between devices, swap(): return lax.ppermute(array, BOTH, table)  17 us
    pallas_call x4, Pallas kernels, accumulate(): pl.pallas_call(functools.partial(partial_kernel, rank, pairs, window, [(f...  11.7 us
    pallas_call x3, Pallas kernels, permuted(): pl.pallas_call(functools.partial(permute_kernel, plan), out_shape=[rows_s...  4.34 us
    ppermute x4, starting transfers between devices, along(): return lax.ppermute(array, 'expert', pairs_of)  4.33 us
    pallas_call x1, Pallas kernels, local(): pl.pallas_call(sort_kernel, out_shape=[pltpu.VMEM(out_grads.shape, jnp.bf...  3.26 us
    ppermute x4, waiting for transfers between devices, along(): return lax.ppermute(array, 'expert', pairs_of)  3.16 us
    pallas_call x1, Pallas kernels, local(): pl.pallas_call(functools.partial(blocks_kernel, rank), out_shape=[jax.Sha...  3.09 us
  transfers between devices with their start and end apart: 20, of which 6 were waited for; matrix products, arithmetic and copies ran while one was open for 0% of the time, Pallas kernels for 32%

profile of v13, /device:TPU:1, one launch (start us, length us, event | category | flops | bytes accessed | tf_op | source)
XLA Modules:
  0.0 73.3 jit_solution(1168260074546714325)
XLA Ops:
  0.0 0.7 copy-done.1
  0.7 3.3 %shard_map.73 = (bf16[128,8,2048]{2,1,0:T(8,128)(2,1)S(1)}, bf16[256,512]{1,0:T(8,128)(2,1)S(1)}, bf16[256,512]{1,0:T(8,128)(2,1)S(1)}, s32[1,128]{1,0:T(1,128)S...) custom-call(s32[8,128]{1,0:T(8,128)S(1)} %bitcast.3, ...), custom_call_target="tpu_custom_call" | custom-call | flops 1 | bytes 1 | tf_op jit(solution)/shard_map/pallas_call | solution.py:516
  4.0 0.1 collective-permute-start
  4.1 2.7 %collective-permute-start.3 = (bf16[528,512]{1,0:T(8,128)(2,1)S(1)}, bf16[528,512]{1,0:T(8,128)(2,1)S(1)}, u32[]{:S(2)}, u32[]{:S(2)}) collective-permute-start(bf16[528,512]{1,0:T(8,128)(2,1)S(1)} %get-tuple-element.61), channel_id=1, source_target_pairs={{0,16},{1,17},{2,18},{3,19},{4,20},{5,21},{6,22},{7,23},{8,24},{9,... | collective-permute-start | bytes 1622024 | tf_op jit(solution)/shard_map/ppermute | solution.py:476
  6.7 0.0 collective-permute-done.two_ref
  6.8 1.4 %collective-permute-start.2 = (bf16[512,512]{1,0:T(8,128)(2,1)S(1)}, bf16[512,512]{1,0:T(8,128)(2,1)S(1)}, u32[]{:S(2)}, u32[]{:S(2)}) collective-permute-start(bf16[512,512]{1,0:T(8,128)(2,1)S(1)} %shard_map.74.refs_5_), channel_id=1, source_target_pairs={{0,4},{1,5},{2,6},{3,7},{4,12},{5,13},{6,14},{7,15},{8,0},{9,1},{1... | collective-permute-start | bytes 1572872 | tf_op jit(solution)/shard_map/ppermute | solution.py:481
  8.1 0.7 shard_map.75
  8.9 2.4 %shard_map.76 = (bf16[1024,512]{1,0:T(8,128)(2,1)S(1)}, bf16[528,512]{1,0:T(8,128)(2,1)S(1)}, bf16[512,512]{1,0:T(8,128)(2,1)S(1)}) custom-call(bf16[1024,1024]{1,0:T(8,128)(2,1)S(1)} %get-tuple-element.69.order_ref, bf16[16,512]{1,0:T(8,128)(2,1)S(1)} %get-tuple-element.65.head_ref, bf16[128,8,2048]{2,1,0:T(8,128)(2,1)S(1)} %get-tuple-element.66.grads_ref), custom_call_target="tpu_custom_call" | custom-call | flops 1 | bytes 1 | tf_op jit(solution)/shard_map/pallas_call | solution.py:545
  11.2 0.0 copy-start.3
  11.2 0.7 collective-permute-start.5
  11.9 1.3 %collective-permute-start.1 = (bf16[512,512]{1,0:T(8,128)(2,1)S(1)}, bf16[512,512]{1,0:T(8,128)(2,1)S(1)}, u32[]{:S(2)}, u32[]{:S(2)}) collective-permute-start(bf16[512,512]{1,0:T(8,128)(2,1)S(1)} %shard_map.74.refs_5_), channel_id=1, source_target_pairs={{0,2},{1,3},{2,0},{3,1},{4,6},{5,7},{6,4},{7,5},{8,10},{9,11},{10,... | collective-permute-start | bytes 1572872 | tf_op jit(solution)/shard_map/ppermute | solution.py:476
  13.2 0.3 collective-permute-start.6
  13.5 5.8 %collective-permute-done.3.refs_3_ = bf16[528,512]{1,0:T(8,128)(2,1)S(1)} collective-permute-done((bf16[528,512]{1,0:T(8,128)(2,1)S(1)}, bf16[528,512]{1,0:T(8,128)(2,1)S(1)}, u32[]{:S(2)}, u32[]{:S(2)}) %collective-permute-start.3) | collective-permute-done | bytes 540704 | tf_op jit(solution)/shard_map/ppermute | solution.py:476
  19.3 1.6 %collective-permute-done.2.refs_6_ = bf16[512,512]{1,0:T(8,128)(2,1)S(1)} collective-permute-done((bf16[512,512]{1,0:T(8,128)(2,1)S(1)}, bf16[512,512]{1,0:T(8,128)(2,1)S(1)}, u32[]{:S(2)}, u32[]{:S(2)}) %collective-permute-start.2) | collective-permute-done | bytes 524320 | tf_op jit(solution)/shard_map/ppermute | solution.py:481
  20.9 0.5 collective-permute-start.4
  21.4 1.1 %collective-permute-start.10 = (bf16[512,512]{1,0:T(8,128)(2,1)S(1)}, bf16[512,512]{1,0:T(8,128)(2,1)S(1)}, u32[]{:S(2)}, u32[]{:S(2)}) collective-permute-start(bf16[512,512]{1,0:T(8,128)(2,1)S(1)} %shard_map.75), channel_id=1, source_target_pairs={{0,16},{1,17},{2,18},{3,19},{4,20},{5,21},{6,22},{7,23},{8,24},{9,... | collective-permute-start | bytes 1572872 | tf_op jit(solution)/shard_map/ppermute | solution.py:476
  22.5 1.3 %shard_map.77 = (bf16[784,512]{1,0:T(8,128)(2,1)S(1)}, bf16[256,512]{1,0:T(8,128)(2,1)S(1)}) custom-call(bf16[1024,1024]{1,0:T(8,128)(2,1)S(1)} %get-tuple-element.69.order_ref, bf16[16,512]{1,0:T(8,128)(2,1)S(1)} %get-tuple-element.65.head_ref, bf16[128,8,2048]{2,1,0:T(8,128)(2,1)S(1)} %get-tuple-element.66.grads_ref), custom_call_target="tpu_custom_call" | custom-call | flops 1 | bytes 1 | tf_op jit(solution)/shard_map/pallas_call | solution.py:545
  23.8 2.8 %shard_map.78 = (bf16[256,256]{1,0:T(8,128)(2,1)S(1)}, bf16[1024,1024]{1,0:T(8,128)(2,1)S(1)}) custom-call(bf16[128,7168]{1,0:T(8,128)(2,1)} %hidden_ref.1, bf16[64,7168]{1,0:T(8,128)(2,1)} %proj_ref.1, s32[1,128]{1,0:T(1,128)S(1)} %bitcast.7, s32[8,128]{1,0:T(8,128)S(1)} %bitcast.4), custom_call_target="tpu_custom_call" | custom-call | flops 1 | bytes 1 | tf_op jit(solution)/shard_map/pallas_call | solution.py:599
  26.6 2.0 %collective-permute-start.7 = (bf16[784,512]{1,0:T(8,128)(2,1)S(1)}, bf16[784,512]{1,0:T(8,128)(2,1)S(1)}, u32[]{:S(2)}, u32[]{:S(2)}) collective-permute-start(bf16[784,512]{1,0:T(8,128)(2,1)S(1)} %get-tuple-element.82), channel_id=1, source_target_pairs={{0,17},{1,16},{2,19},{3,18},{4,21},{5,20},{6,23},{7,22},{8,25},{9,... | collective-permute-start | bytes 2408456 | tf_op jit(solution)/shard_map/ppermute | solution.py:476
  28.7 1.2 %collective-permute-start.11 = (bf16[512,512]{1,0:T(8,128)(2,1)S(1)}, bf16[512,512]{1,0:T(8,128)(2,1)S(1)}, u32[]{:S(2)}, u32[]{:S(2)}) collective-permute-start(bf16[512,512]{1,0:T(8,128)(2,1)S(1)} %collective-permute-done.2.refs_6_), channel_id=1, source_target_pairs={{0,2},{1,3},{2,0},{3,1},{4,6},{5,7},{6,4},{7,5},{8,10},{9,11},{10,... | collective-permute-start | bytes 1572872 | tf_op jit(solution)/shard_map/ppermute | solution.py:476
  29.9 0.0 collective-permute-done.6.refs_4_
  29.9 2.6 %shard_map.79 = (bf16[4096,512]{1,0:T(8,128)(2,1)S(1)}, bf16[16,256,512]{2,1,0:T(8,128)(2,1)S(1)}, f32[4096,128]{1,0:T(8,128)S(1)}) custom-call(s32[16,16]{1,0:T(8,128)S(1)} %copy-done, s32[1,128]{1,0:T(1,128)S(1)} %get-tuple-element.58.refs_0_.starts_ref, s32[1,128]{1,0:T(1,128)S(1)} %slice_add_fusion.2.refs_1_, ...), custom_call_target="tpu_custom_call" | custom-call | flops 1 | bytes 1 | tf_op jit(solution)/shard_map/pallas_call | solution.py:288
  32.5 1.6 %collective-permute-done.4.refs_5_ = bf16[512,512]{1,0:T(8,128)(2,1)S(1)} collective-permute-done((bf16[512,512]{1,0:T(8,128)(2,1)S(1)}, bf16[512,512]{1,0:T(8,128)(2,1)S(1)}, u32[]{:S(2)}, u32[]{:S(2)}) %collective-permute-start.4) | collective-permute-done | bytes 524320 | tf_op jit(solution)/shard_map/ppermute | solution.py:481
  34.1 1.2 %collective-permute-start.9 = (bf16[512,512]{1,0:T(8,128)(2,1)S(1)}, bf16[512,512]{1,0:T(8,128)(2,1)S(1)}, u32[]{:S(2)}, u32[]{:S(2)}) collective-permute-start(bf16[512,512]{1,0:T(8,128)(2,1)S(1)} %collective-permute-done.4.refs_5_), channel_id=1, source_target_pairs={{0,2},{1,3},{2,0},{3,1},{4,6},{5,7},{6,4},{7,5},{8,10},{9,11},{10,... | collective-permute-start | bytes 1572872 | tf_op jit(solution)/shard_map/ppermute | solution.py:476
  35.3 0.6 collective-permute-start.15
  35.9 0.0 collective-permute-done.10.refs_4_
  35.9 3.6 %collective-permute-start.8 = (bf16[256,512]{1,0:T(8,128)(2,1)S(1)}, bf16[256,512]{1,0:T(8,128)(2,1)S(1)}, u32[]{:S(2)}, u32[]{:S(2)}) collective-permute-start(bf16[256,512]{1,0:T(8,128)(2,1)S(1)} %get-tuple-element.84), channel_id=1, source_target_pairs={{0,17},{1,16},{2,19},{3,18},{4,21},{5,20},{6,23},{7,22},{8,25},{9,... | collective-permute-start | bytes 786440 | tf_op jit(solution)/shard_map/ppermute | solution.py:476
  39.5 2.7 %collective-permute-done.11.refs_6_ = bf16[512,512]{1,0:T(8,128)(2,1)S(1)} collective-permute-done((bf16[512,512]{1,0:T(8,128)(2,1)S(1)}, bf16[512,512]{1,0:T(8,128)(2,1)S(1)}, u32[]{:S(2)}, u32[]{:S(2)}) %collective-permute-start.11) | collective-permute-done | bytes 524320 | tf_op jit(solution)/shard_map/ppermute | solution.py:476
  42.3 1.9 %collective-permute-start.16 = (bf16[512,512]{1,0:T(8,128)(2,1)S(1)}, bf16[512,512]{1,0:T(8,128)(2,1)S(1)}, u32[]{:S(2)}, u32[]{:S(2)}) collective-permute-start(bf16[512,512]{1,0:T(8,128)(2,1)S(1)} %collective-permute-done.1.refs_7_), channel_id=1, source_target_pairs={{0,8},{1,9},{2,10},{3,11},{4,0},{5,1},{6,2},{7,3},{8,12},{9,13},{1... | collective-permute-start | bytes 1572872 | tf_op jit(solution)/shard_map/ppermute | solution.py:481
  44.1 3.3 %shard_map.80 = (bf16[4096,512]{1,0:T(8,128)(2,1)S(1)}, bf16[16,256,512]{2,1,0:T(8,128)(2,1)S(1)}, f32[4096,128]{1,0:T(8,128)S(1)}) custom-call(s32[16,16]{1,0:T(8,128)S(1)} %copy-done, s32[1,128]{1,0:T(1,128)S(1)} %get-tuple-element.58.refs_0_.starts_ref, ...), custom_call_target="tpu_custom_call", output_to_operand_aliasing={{0}: (8, {}), {1}: (9, {}), {2}: (10, {})} | custom-call | flops 1000000000 | bytes 1 | tf_op jit(solution)/shard_map/pallas_call | solution.py:288
  47.4 7.1 %collective-permute-done.7.refs_4_ = bf16[784,512]{1,0:T(8,128)(2,1)S(1)} collective-permute-done((bf16[784,512]{1,0:T(8,128)(2,1)S(1)}, bf16[784,512]{1,0:T(8,128)(2,1)S(1)}, u32[]{:S(2)}, u32[]{:S(2)}) %collective-permute-start.7) | collective-permute-done | bytes 802848 | tf_op jit(solution)/shard_map/ppermute | solution.py:476
  54.6 3.6 %shard_map.81 = (bf16[4096,512]{1,0:T(8,128)(2,1)S(1)}, bf16[16,256,512]{2,1,0:T(8,128)(2,1)S(1)}, f32[4096,128]{1,0:T(8,128)S(1)}, bf16[512,128]{1,0:T(8,128)(2,1)S(1)}, bf16[512,128]{1,0:T(8,128)(2,1)S(1)}) custom-call(s32[16,16]{1,0:T(8,128)S(1)} %copy-done, ...), custom_call_target="tpu_custom_call", output_to_operand_aliasing={{0}: (7, {}), {1}: (8, {}), {2}: (9, {})} | custom-call | flops 1 | bytes 1 | tf_op jit(solution)/shard_map/pallas_call | solution.py:288
  58.2 0.1 collective-permute-start.12
  58.3 1.2 %collective-permute-start.13 = (bf16[512,128]{1,0:T(8,128)(2,1)S(1)}, bf16[512,128]{1,0:T(8,128)(2,1)S(1)}, u32[]{:S(2)}, u32[]{:S(2)}) collective-permute-start(bf16[512,128]{1,0:T(8,128)(2,1)S(1)} %get-tuple-element.97), channel_id=1, source_target_pairs={{0,16},{1,17},{2,18},{3,19},{4,20},{5,21},{6,22},{7,23},{8,24},{9,... | collective-permute-start | bytes 393224 | tf_op jit(solution)/shard_map/ppermute | solution.py:476
  59.5 2.2 %shard_map.82 = (bf16[4096,512]{1,0:T(8,128)(2,1)S(1)}, bf16[16,256,512]{2,1,0:T(8,128)(2,1)S(1)}, f32[4096,128]{1,0:T(8,128)S(1)}, bf16[512,128]{1,0:T(8,128)(2,1)S(1)}) custom-call(s32[16,16]{1,0:T(8,128)S(1)} %copy-done, s32[1,128]{1,0:T(1,128)S(1)} %get-tuple-element.58.refs_0_.starts_ref, ...), custom_call_target="tpu_custom_call", output_to_operand_aliasing={{0}: (6, {}), {1}: (7, {}), {2}: (8, {})} | custom-call | flops 1000000000 | bytes 1 | tf_op jit(solution)/shard_map/pallas_call | solution.py:288
  61.7 0.0 copy-start.2
  61.7 1.0 %collective-permute-start.14 = (bf16[512,128]{1,0:T(8,128)(2,1)S(1)}, bf16[512,128]{1,0:T(8,128)(2,1)S(1)}, u32[]{:S(2)}, u32[]{:S(2)}) collective-permute-start(bf16[512,128]{1,0:T(8,128)(2,1)S(1)} %get-tuple-element.98), channel_id=1, source_target_pairs={{0,17},{1,16},{2,19},{3,18},{4,21},{5,20},{6,23},{7,22},{8,25},{9,... | collective-permute-start | bytes 393224 | tf_op jit(solution)/shard_map/ppermute | solution.py:476
  62.7 0.0 collective-permute-done.15.refs_5_
  62.7 1.5 %shard_map.83 = (f32[224,128]{1,0:T(8,128)S(1)}, bf16[224,128]{1,0:T(8,128)(2,1)S(1)}, bf16[224,128]{1,0:T(8,128)(2,1)S(1)}, bf16[224,128]{1,0:T(8,128)(2,1)S(1)}) custom-call(s32[16,16]{1,0:T(8,128)S(1)} %copy-done, s32[1,128]{1,0:T(1,128)S(1)} %get-tuple-element.58.refs_0_.starts_ref, s32[1,128]{1,0:T(1,128)S(1)} %slice_add_fusion.2.refs_1_, ...), custom_call_target="tpu_custom_call" | custom-call | flops 1 | bytes 1 | tf_op jit(solution)/shard_map/pallas_call | solution.py:740
  64.3 0.1 collective-permute-start.17
  64.4 1.2 %collective-permute-start.18 = (bf16[224,128]{1,0:T(8,128)(2,1)S(1)}, bf16[224,128]{1,0:T(8,128)(2,1)S(1)}, u32[]{:S(2)}, u32[]{:S(2)}) collective-permute-start(bf16[224,128]{1,0:T(8,128)(2,1)S(1)} %get-tuple-element.108), channel_id=1, source_target_pairs={{0,16},{1,17},{2,18},{3,19},{4,20},{5,21},{6,22},{7,23},{8,24},{9,... | collective-permute-start | bytes 172040 | tf_op jit(solution)/shard_map/ppermute | solution.py:476
  65.6 0.9 %collective-permute-start.19 = (bf16[224,128]{1,0:T(8,128)(2,1)S(1)}, bf16[224,128]{1,0:T(8,128)(2,1)S(1)}, u32[]{:S(2)}, u32[]{:S(2)}) collective-permute-start(bf16[224,128]{1,0:T(8,128)(2,1)S(1)} %get-tuple-element.109), channel_id=1, source_target_pairs={{0,17},{1,16},{2,19},{3,18},{4,21},{5,20},{6,23},{7,22},{8,25},{9,... | collective-permute-start | bytes 172040 | tf_op jit(solution)/shard_map/ppermute | solution.py:476
  66.5 0.0 collective-permute-done.13.c_ref
  66.5 1.4 %collective-permute-done.14.d_ref = bf16[512,128]{1,0:T(8,128)(2,1)S(1)} collective-permute-done((bf16[512,128]{1,0:T(8,128)(2,1)S(1)}, bf16[512,128]{1,0:T(8,128)(2,1)S(1)}, u32[]{:S(2)}, u32[]{:S(2)}) %collective-permute-start.14) | collective-permute-done | bytes 131104 | tf_op jit(solution)/shard_map/ppermute | solution.py:476
  67.9 3.1 %shard_map.84 = (bf16[2,64,4096]{2,1,0:T(8,128)(2,1)}, f32[64,1024]{1,0:T(8,128)S(1)}) custom-call(s32[8,128]{1,0:T(8,128)S(1)} %bitcast.5, bf16[256,256]{1,0:T(8,128)(2,1)S(1)} %get-tuple-element.79.basis_ref, bf16[1024,1024]{1,0:T(8,128)(2,1)S(1)} %get-tuple-element.80.order_ref, f32[4096,128]{1,0:T(8,128)S(1)} %get-tuple-element.95.total_ref, ...), custom_call_target="tpu_custom_call" | custom-call | flops 1 | bytes 1 | tf_op jit(solution)/shard_map/pallas_call | solution.py:751
  71.0 0.0 collective-permute-done.18.c_ref
  71.0 0.0 collective-permute-done.19.d_ref
  71.0 2.2 %shard_map.85 = bf16[2,64,4096]{2,1,0:T(8,128)(2,1)} custom-call(s32[16,16]{1,0:T(8,128)S(1)} %copy-done, s32[1,128]{1,0:T(1,128)S(1)} %get-tuple-element.58.refs_0_.starts_ref, s32[8,128]{1,0:T(8,128)S(1)} %bitcast.6, bf16[256,256]{1,0:T(8,128)(2,1)S(1)} %get-tuple-element.79.basis_ref, ...), custom_call_target="tpu_custom_call", output_to_operand_aliasing={{}: (10, {})} | custom-call | flops 1 | bytes 1 | tf_op jit(solution)/shard_map/pallas_call | solution.py:764
  (19 shorter events, 0.1 us)
Async XLA Ops:
  0.0 0.7 copy-start.1
  4.0 2.8 %collective-permute-start = (bf16[256,512]{1,0:T(8,128)(2,1)S(1)}, bf16[256,512]{1,0:T(8,128)(2,1)S(1)}, u32[]{:S(2)}, u32[]{:S(2)}) collective-permute-start(bf16[256,512]{1,0:T(8,128)(2,1)S(1)} %get-tuple-element.60), channel_id=1, source_target_pairs={{0,1},{1,0},{2,3},{3,2},{4,5},{5,4},{6,7},{7,6},{8,9},{9,8},{10,11... | collective-permute-start | bytes 786440 | tf_op jit(solution)/shard_map/ppermute | solution.py:476
  4.1 15.2 %collective-permute-start.3 = (bf16[528,512]{1,0:T(8,128)(2,1)S(1)}, bf16[528,512]{1,0:T(8,128)(2,1)S(1)}, u32[]{:S(2)}, u32[]{:S(2)}) collective-permute-start(bf16[528,512]{1,0:T(8,128)(2,1)S(1)} %get-tuple-element.61), channel_id=1, source_target_pairs={{0,16},{1,17},{2,18},{3,19},{4,20},{5,21},{6,22},{7,23},{8,24},{9,... | collective-permute-start | bytes 1622024 | tf_op jit(solution)/shard_map/ppermute | solution.py:476
  6.8 14.1 %collective-permute-start.2 = (bf16[512,512]{1,0:T(8,128)(2,1)S(1)}, bf16[512,512]{1,0:T(8,128)(2,1)S(1)}, u32[]{:S(2)}, u32[]{:S(2)}) collective-permute-start(bf16[512,512]{1,0:T(8,128)(2,1)S(1)} %shard_map.74.refs_5_), channel_id=1, source_target_pairs={{0,4},{1,5},{2,6},{3,7},{4,12},{5,13},{6,14},{7,15},{8,0},{9,1},{1... | collective-permute-start | bytes 1572872 | tf_op jit(solution)/shard_map/ppermute | solution.py:481
  11.2 12.6 %copy-start.3 = (s32[128]{0:T(128)S(1)}, s32[128]{0:T(128)}, u32[]{:S(2)}) copy-start(s32[128]{0:T(128)} %param.10) | copy-start | bytes 1540
  11.2 15.4 %collective-permute-start.5 = (bf16[528,512]{1,0:T(8,128)(2,1)S(1)}, bf16[528,512]{1,0:T(8,128)(2,1)S(1)}, u32[]{:S(2)}, u32[]{:S(2)}) collective-permute-start(bf16[528,512]{1,0:T(8,128)(2,1)S(1)} %get-tuple-element.77), channel_id=1, source_target_pairs={{0,1},{1,0},{2,3},{3,2},{4,5},{5,4},{6,7},{7,6},{8,9},{9,8},{10,11... | collective-permute-start | bytes 1622024 | tf_op jit(solution)/shard_map/ppermute | solution.py:476
  11.9 16.7 %collective-permute-start.1 = (bf16[512,512]{1,0:T(8,128)(2,1)S(1)}, bf16[512,512]{1,0:T(8,128)(2,1)S(1)}, u32[]{:S(2)}, u32[]{:S(2)}) collective-permute-start(bf16[512,512]{1,0:T(8,128)(2,1)S(1)} %shard_map.74.refs_5_), channel_id=1, source_target_pairs={{0,2},{1,3},{2,0},{3,1},{4,6},{5,7},{6,4},{7,5},{8,10},{9,11},{10,... | collective-permute-start | bytes 1572872 | tf_op jit(solution)/shard_map/ppermute | solution.py:476
  13.2 16.7 %collective-permute-start.6 = (bf16[512,512]{1,0:T(8,128)(2,1)S(1)}, bf16[512,512]{1,0:T(8,128)(2,1)S(1)}, u32[]{:S(2)}, u32[]{:S(2)}) collective-permute-start(bf16[512,512]{1,0:T(8,128)(2,1)S(1)} %get-tuple-element.78), channel_id=1, source_target_pairs={{0,1},{1,0},{2,3},{3,2},{4,5},{5,4},{6,7},{7,6},{8,9},{9,8},{10,11... | collective-permute-start | bytes 1572872 | tf_op jit(solution)/shard_map/ppermute | solution.py:476
  20.9 13.1 %collective-permute-start.4 = (bf16[512,512]{1,0:T(8,128)(2,1)S(1)}, bf16[512,512]{1,0:T(8,128)(2,1)S(1)}, u32[]{:S(2)}, u32[]{:S(2)}) collective-permute-start(bf16[512,512]{1,0:T(8,128)(2,1)S(1)} %collective-permute-done.2.refs_6_), channel_id=1, source_target_pairs={{0,4},{1,5},{2,6},{3,7},{4,12},{5,13},{6,14},{7,15},{8,0},{9,1},{1... | collective-permute-start | bytes 1572872 | tf_op jit(solution)/shard_map/ppermute | solution.py:481
  21.4 14.5 %collective-permute-start.10 = (bf16[512,512]{1,0:T(8,128)(2,1)S(1)}, bf16[512,512]{1,0:T(8,128)(2,1)S(1)}, u32[]{:S(2)}, u32[]{:S(2)}) collective-permute-start(bf16[512,512]{1,0:T(8,128)(2,1)S(1)} %shard_map.75), channel_id=1, source_target_pairs={{0,16},{1,17},{2,18},{3,19},{4,20},{5,21},{6,22},{7,23},{8,24},{9,... | collective-permute-start | bytes 1572872 | tf_op jit(solution)/shard_map/ppermute | solution.py:476
  22.5 7.4 %copy-start = (s32[16,16]{1,0:T(8,128)S(1)}, s32[16,16]{1,0:T(8,128)}, u32[]{:S(2)}) copy-start(s32[16,16]{1,0:T(8,128)} %constant.4.clone.bases_ref) | copy-start | bytes 3076
  26.6 27.9 %collective-permute-start.7 = (bf16[784,512]{1,0:T(8,128)(2,1)S(1)}, bf16[784,512]{1,0:T(8,128)(2,1)S(1)}, u32[]{:S(2)}, u32[]{:S(2)}) collective-permute-start(bf16[784,512]{1,0:T(8,128)(2,1)S(1)} %get-tuple-element.82), channel_id=1, source_target_pairs={{0,17},{1,16},{2,19},{3,18},{4,21},{5,20},{6,23},{7,22},{8,25},{9,... | collective-permute-start | bytes 2408456 | tf_op jit(solution)/shard_map/ppermute | solution.py:476
  28.7 13.6 %collective-permute-start.11 = (bf16[512,512]{1,0:T(8,128)(2,1)S(1)}, bf16[512,512]{1,0:T(8,128)(2,1)S(1)}, u32[]{:S(2)}, u32[]{:S(2)}) collective-permute-start(bf16[512,512]{1,0:T(8,128)(2,1)S(1)} %collective-permute-done.2.refs_6_), channel_id=1, source_target_pairs={{0,2},{1,3},{2,0},{3,1},{4,6},{5,7},{6,4},{7,5},{8,10},{9,11},{10,... | collective-permute-start | bytes 1572872 | tf_op jit(solution)/shard_map/ppermute | solution.py:476
  34.1 20.5 %collective-permute-start.9 = (bf16[512,512]{1,0:T(8,128)(2,1)S(1)}, bf16[512,512]{1,0:T(8,128)(2,1)S(1)}, u32[]{:S(2)}, u32[]{:S(2)}) collective-permute-start(bf16[512,512]{1,0:T(8,128)(2,1)S(1)} %collective-permute-done.4.refs_5_), channel_id=1, source_target_pairs={{0,2},{1,3},{2,0},{3,1},{4,6},{5,7},{6,4},{7,5},{8,10},{9,11},{10,... | collective-permute-start | bytes 1572872 | tf_op jit(solution)/shard_map/ppermute | solution.py:476
  35.3 27.4 %collective-permute-start.15 = (bf16[512,512]{1,0:T(8,128)(2,1)S(1)}, bf16[512,512]{1,0:T(8,128)(2,1)S(1)}, u32[]{:S(2)}, u32[]{:S(2)}) collective-permute-start(bf16[512,512]{1,0:T(8,128)(2,1)S(1)} %collective-permute-done.4.refs_5_), channel_id=1, source_target_pairs={{0,4},{1,5},{2,6},{3,7},{4,12},{5,13},{6,14},{7,15},{8,0},{9,1},{1... | collective-permute-start | bytes 1572872 | tf_op jit(solution)/shard_map/ppermute | solution.py:481
  35.9 23.6 %collective-permute-start.8 = (bf16[256,512]{1,0:T(8,128)(2,1)S(1)}, bf16[256,512]{1,0:T(8,128)(2,1)S(1)}, u32[]{:S(2)}, u32[]{:S(2)}) collective-permute-start(bf16[256,512]{1,0:T(8,128)(2,1)S(1)} %get-tuple-element.84), channel_id=1, source_target_pairs={{0,17},{1,16},{2,19},{3,18},{4,21},{5,20},{6,23},{7,22},{8,25},{9,... | collective-permute-start | bytes 786440 | tf_op jit(solution)/shard_map/ppermute | solution.py:476
  42.3 20.5 %collective-permute-start.16 = (bf16[512,512]{1,0:T(8,128)(2,1)S(1)}, bf16[512,512]{1,0:T(8,128)(2,1)S(1)}, u32[]{:S(2)}, u32[]{:S(2)}) collective-permute-start(bf16[512,512]{1,0:T(8,128)(2,1)S(1)} %collective-permute-done.1.refs_7_), channel_id=1, source_target_pairs={{0,8},{1,9},{2,10},{3,11},{4,0},{5,1},{6,2},{7,3},{8,12},{9,13},{1... | collective-permute-start | bytes 1572872 | tf_op jit(solution)/shard_map/ppermute | solution.py:481
  58.2 7.4 %collective-permute-start.12 = (bf16[512,128]{1,0:T(8,128)(2,1)S(1)}, bf16[512,128]{1,0:T(8,128)(2,1)S(1)}, u32[]{:S(2)}, u32[]{:S(2)}) collective-permute-start(bf16[512,128]{1,0:T(8,128)(2,1)S(1)} %get-tuple-element.96), channel_id=1, source_target_pairs={{0,1},{1,0},{2,3},{3,2},{4,5},{5,4},{6,7},{7,6},{8,9},{9,8},{10,11... | collective-permute-start | bytes 393224 | tf_op jit(solution)/shard_map/ppermute | solution.py:476
  58.3 8.2 %collective-permute-start.13 = (bf16[512,128]{1,0:T(8,128)(2,1)S(1)}, bf16[512,128]{1,0:T(8,128)(2,1)S(1)}, u32[]{:S(2)}, u32[]{:S(2)}) collective-permute-start(bf16[512,128]{1,0:T(8,128)(2,1)S(1)} %get-tuple-element.97), channel_id=1, source_target_pairs={{0,16},{1,17},{2,18},{3,19},{4,20},{5,21},{6,22},{7,23},{8,24},{9,... | collective-permute-start | bytes 393224 | tf_op jit(solution)/shard_map/ppermute | solution.py:476
  61.7 6.1 %copy-start.2 = (s32[128,8]{0,1:T(8,128)S(1)}, s32[128,8]{0,1:T(8,128)}, u32[]{:S(2)}) copy-start(s32[128,8]{0,1:T(8,128)} %param.9) | copy-start | bytes 12292
  61.7 6.1 %collective-permute-start.14 = (bf16[512,128]{1,0:T(8,128)(2,1)S(1)}, bf16[512,128]{1,0:T(8,128)(2,1)S(1)}, u32[]{:S(2)}, u32[]{:S(2)}) collective-permute-start(bf16[512,128]{1,0:T(8,128)(2,1)S(1)} %get-tuple-element.98), channel_id=1, source_target_pairs={{0,17},{1,16},{2,19},{3,18},{4,21},{5,20},{6,23},{7,22},{8,25},{9,... | collective-permute-start | bytes 393224 | tf_op jit(solution)/shard_map/ppermute | solution.py:476
  64.3 6.7 %collective-permute-start.17 = (bf16[224,128]{1,0:T(8,128)(2,1)S(1)}, bf16[224,128]{1,0:T(8,128)(2,1)S(1)}, u32[]{:S(2)}, u32[]{:S(2)}) collective-permute-start(bf16[224,128]{1,0:T(8,128)(2,1)S(1)} %get-tuple-element.107), channel_id=1, source_target_pairs={{0,1},{1,0},{2,3},{3,2},{4,5},{5,4},{6,7},{7,6},{8,9},{9,8},{10,11... | collective-permute-start | bytes 172040 | tf_op jit(solution)/shard_map/ppermute | solution.py:476
  64.4 6.6 %collective-permute-start.18 = (bf16[224,128]{1,0:T(8,128)(2,1)S(1)}, bf16[224,128]{1,0:T(8,128)(2,1)S(1)}, u32[]{:S(2)}, u32[]{:S(2)}) collective-permute-start(bf16[224,128]{1,0:T(8,128)(2,1)S(1)} %get-tuple-element.108), channel_id=1, source_target_pairs={{0,16},{1,17},{2,18},{3,19},{4,20},{5,21},{6,22},{7,23},{8,24},{9,... | collective-permute-start | bytes 172040 | tf_op jit(solution)/shard_map/ppermute | solution.py:476
  65.6 5.4 %collective-permute-start.19 = (bf16[224,128]{1,0:T(8,128)(2,1)S(1)}, bf16[224,128]{1,0:T(8,128)(2,1)S(1)}, u32[]{:S(2)}, u32[]{:S(2)}) collective-permute-start(bf16[224,128]{1,0:T(8,128)(2,1)S(1)} %get-tuple-element.109), channel_id=1, source_target_pairs={{0,17},{1,16},{2,19},{3,18},{4,21},{5,20},{6,23},{7,22},{8,25},{9,... | collective-permute-start | bytes 172040 | tf_op jit(solution)/shard_map/ppermute | solution.py:476

commit v14 on v13

--- a/solution.py
+++ b/solution.py
@@ -9,7 +9,7 @@
 from jax.sharding import PartitionSpec as P
 
 SEG_DEV = 2
-O = {'p1': 'core_unit', 'z1': 'none', 'p2': 'unit', 'cores': 2, 'core_in': 'none', 'y0': 'unit', 'basis': [], 'ev1': ['side0'], 'diag': ['side0'], 'ev2': ['basis', 'side0'], 'w': ['basis', 'core'], 'last': ['z2'], 'ka': 0, 'z3_ka': 0, 'w_ka': 0, 'k0': 1, 'k1': 0, 'k2': 1, 'y2': 'c'}
+O = {'p1': 'core_unit', 'z1': 'none', 'p2': 'unit', 'cores': 1, 'core_in': 'none', 'y0': 'unit', 'basis': [], 'ev1': ['side0'], 'diag': ['side1'], 'ev2': ['basis', 'side0'], 'w': ['basis', 'core'], 'last': ['z2'], 'ka': 1, 'z3_ka': 0, 'w_ka': 0, 'k0': 1, 'k1': 0, 'k2': 1, 'y2': 'd', 'core_k': 'b', 'side_k': 'b'}
 CORES = 2
 SIDES = 2
 QUAD = 4
@@ -709,7 +709,9 @@
     COST = {0: QUICK, 1: SHORT}
     work(
         names_a,
-        complete=[(0, [(own_tokens, pairs)]), (1, list(zip(from_core, core_counts)))],
+        complete=[(0, [(own_tokens, pairs)])]
+        + ([(1, list(zip(from_core, core_counts)))] if O["core_k"] == "a" else [])
+        + ([(2, [(piece, half) for piece in side_pieces])] if O["side_k"] == "a" else []),
         cost=COST[O["ka"]],
     )
     if O["z3_ka"]:
@@ -722,7 +724,12 @@
     held[final - 1, 1] = swap(held[near], 0, CORES)
     last_piece = group_tie(O["last"], last_piece)
     diagonal_pieces.append(swap(last_piece, 1, 1))
-    work(names_b, complete=[(2, [(piece, half) for piece in side_pieces])], cost=COST[O["k0"]])
+    work(
+        names_b,
+        complete=([(1, list(zip(from_core, core_counts)))] if O["core_k"] == "b" else [])
+        + ([(2, [(piece, half) for piece in side_pieces])] if O["side_k"] == "b" else []),
+        cost=COST[O["k0"]],
+    )
     sent = work(
         names_c if O["y2"] == "c" else [], partial=[(3, diagonal_pieces[0], 0, 3 * rows)], sends=[1, 2] if O["y2"] == "c" else [], cost=COST[O["k1"]]
     )

time: 74.5 us -> 74.6 us (level); the launches traced: 73.3 us -> 74.4 us
  waiting for transfers between devices: 20.2 us -> 21.9 us
    ppermute x16 -> x15, waiting for transfers between devices: 17 us -> 20.2 us  [swap(): return lax.ppermute(array, BOTH, table)]
    ppermute x4, waiting for transfers between devices: 3.16 us -> 1.74 us  [along(): return lax.ppermute(array, 'expert', pairs_of)]
    ppermute x16 -> x15, starting transfers between devices: 18.8 us -> 17.6 us  [swap(): return lax.ppermute(array, BOTH, table)]
  transfers between devices with their start and end apart: 20 -> 19, of which waited for: 6 -> 7; matrix products, arithmetic and copies ran while one was open for 0% -> 0% of each run, Pallas kernels for 32% -> 32%
where the time goes in v14:
time: 74.6 us; the launch traced here: 74.4 us
  Pallas kernels  29 us (39%)
  starting transfers between devices  22.7 us (30%)
  waiting for transfers between devices  21.9 us (29%)
    ppermute x15, waiting for transfers between devices, swap(): return lax.ppermute(array, BOTH, table)  20.2 us
    ppermute x15, starting transfers between devices, swap(): return lax.ppermute(array, BOTH, table)  17.6 us
    pallas_call x4, Pallas kernels, accumulate(): pl.pallas_call(functools.partial(partial_kernel, rank, pairs, window, [(f...  11.7 us
    ppermute x4, starting transfers between devices, along(): return lax.ppermute(array, 'expert', pairs_of)  5.07 us
    pallas_call x3, Pallas kernels, permuted(): pl.pallas_call(functools.partial(permute_kernel, plan), out_shape=[rows_s...  4.33 us
    pallas_call x1, Pallas kernels, local(): pl.pallas_call(sort_kernel, out_shape=[pltpu.VMEM(out_grads.shape, jnp.bf...  3.26 us
    pallas_call x1, Pallas kernels, local(): pl.pallas_call(functools.partial(blocks_kernel, rank), out_shape=[jax.Sha...  3.08 us
    pallas_call x1, Pallas kernels, local(): pl.pallas_call(basis_kernel, out_shape=[pltpu.VMEM((2 * tokens, SEG_DEV *...  2.79 us
  transfers between devices with their start and end apart: 19, of which 7 were waited for; matrix products, arithmetic and copies ran while one was open for 0% of the time, Pallas kernels for 32%

profile of v14, /device:TPU:1, one launch (start us, length us, event | category | flops | bytes accessed | tf_op | source)
XLA Modules:
  0.0 74.4 jit_solution(13108315097835979430)
XLA Ops:
  0.0 0.7 copy-done.1
  0.7 3.3 %shard_map.73 = (bf16[128,8,2048]{2,1,0:T(8,128)(2,1)S(1)}, bf16[256,512]{1,0:T(8,128)(2,1)S(1)}, bf16[256,512]{1,0:T(8,128)(2,1)S(1)}, s32[1,128]{1,0:T(1,128)S...) custom-call(s32[8,128]{1,0:T(8,128)S(1)} %bitcast.3, ...), custom_call_target="tpu_custom_call" | custom-call | flops 1 | bytes 1 | tf_op jit(solution)/shard_map/pallas_call | solution.py:516
  4.0 0.1 collective-permute-start
  4.1 2.7 %collective-permute-start.3 = (bf16[528,512]{1,0:T(8,128)(2,1)S(1)}, bf16[528,512]{1,0:T(8,128)(2,1)S(1)}, u32[]{:S(2)}, u32[]{:S(2)}) collective-permute-start(bf16[528,512]{1,0:T(8,128)(2,1)S(1)} %get-tuple-element.61), channel_id=1, source_target_pairs={{0,16},{1,17},{2,18},{3,19},{4,20},{5,21},{6,22},{7,23},{8,24},{9,... | collective-permute-start | bytes 1622024 | tf_op jit(solution)/shard_map/ppermute | solution.py:476
  6.8 1.3 %collective-permute-start.2 = (bf16[512,512]{1,0:T(8,128)(2,1)S(1)}, bf16[512,512]{1,0:T(8,128)(2,1)S(1)}, u32[]{:S(2)}, u32[]{:S(2)}) collective-permute-start(bf16[512,512]{1,0:T(8,128)(2,1)S(1)} %shard_map.74.refs_2_), channel_id=1, source_target_pairs={{0,4},{1,5},{2,6},{3,7},{4,12},{5,13},{6,14},{7,15},{8,0},{9,1},{1... | collective-permute-start | bytes 1572872 | tf_op jit(solution)/shard_map/ppermute | solution.py:481
  8.1 0.7 shard_map.75
  8.9 1.2 %collective-permute-start.6 = (bf16[512,512]{1,0:T(8,128)(2,1)S(1)}, bf16[512,512]{1,0:T(8,128)(2,1)S(1)}, u32[]{:S(2)}, u32[]{:S(2)}) collective-permute-start(bf16[512,512]{1,0:T(8,128)(2,1)S(1)} %shard_map.75), channel_id=1, source_target_pairs={{0,16},{1,17},{2,18},{3,19},{4,20},{5,21},{6,22},{7,23},{8,24},{9,... | collective-permute-start | bytes 1572872 | tf_op jit(solution)/shard_map/ppermute | solution.py:476
  10.1 1.2 %collective-permute-start.1 = (bf16[512,512]{1,0:T(8,128)(2,1)S(1)}, bf16[512,512]{1,0:T(8,128)(2,1)S(1)}, u32[]{:S(2)}, u32[]{:S(2)}) collective-permute-start(bf16[512,512]{1,0:T(8,128)(2,1)S(1)} %shard_map.74.refs_2_), channel_id=1, source_target_pairs={{0,2},{1,3},{2,0},{3,1},{4,6},{5,7},{6,4},{7,5},{8,10},{9,11},{10,... | collective-permute-start | bytes 1572872 | tf_op jit(solution)/shard_map/ppermute | solution.py:476
  11.3 2.3 %shard_map.76 = (bf16[1024,512]{1,0:T(8,128)(2,1)S(1)}, bf16[1040,512]{1,0:T(8,128)(2,1)S(1)}) custom-call(bf16[1024,1024]{1,0:T(8,128)(2,1)S(1)} %get-tuple-element.69.order_ref, bf16[16,512]{1,0:T(8,128)(2,1)S(1)} %get-tuple-element.65.head_ref, bf16[128,8,2048]{2,1,0:T(8,128)(2,1)S(1)} %get-tuple-element.66.grads_ref), custom_call_target="tpu_custom_call" | custom-call | flops 1 | bytes 1 | tf_op jit(solution)/shard_map/pallas_call | solution.py:545
  13.7 0.0 copy-start.3
  13.7 1.3 %collective-permute-start.5 = (bf16[1040,512]{1,0:T(8,128)(2,1)S(1)}, bf16[1040,512]{1,0:T(8,128)(2,1)S(1)}, u32[]{:S(2)}, u32[]{:S(2)}) collective-permute-start(bf16[1040,512]{1,0:T(8,128)(2,1)S(1)} %get-tuple-element.75), channel_id=1, source_target_pairs={{0,1},{1,0},{2,3},{3,2},{4,5},{5,4},{6,7},{7,6},{8,9},{9,8},{10,11... | collective-permute-start | bytes 3194888 | tf_op jit(solution)/shard_map/ppermute | solution.py:476
  15.0 4.3 %collective-permute-done.3.refs_4_ = bf16[528,512]{1,0:T(8,128)(2,1)S(1)} collective-permute-done((bf16[528,512]{1,0:T(8,128)(2,1)S(1)}, bf16[528,512]{1,0:T(8,128)(2,1)S(1)}, u32[]{:S(2)}, u32[]{:S(2)}) %collective-permute-start.3) | collective-permute-done | bytes 540704 | tf_op jit(solution)/shard_map/ppermute | solution.py:476
  19.3 1.6 %collective-permute-done.2.refs_3_ = bf16[512,512]{1,0:T(8,128)(2,1)S(1)} collective-permute-done((bf16[512,512]{1,0:T(8,128)(2,1)S(1)}, bf16[512,512]{1,0:T(8,128)(2,1)S(1)}, u32[]{:S(2)}, u32[]{:S(2)}) %collective-permute-start.2) | collective-permute-done | bytes 524320 | tf_op jit(solution)/shard_map/ppermute | solution.py:481
  20.9 0.5 collective-permute-start.4
  21.4 1.3 %shard_map.77 = (bf16[784,512]{1,0:T(8,128)(2,1)S(1)}, bf16[256,512]{1,0:T(8,128)(2,1)S(1)}) custom-call(bf16[1024,1024]{1,0:T(8,128)(2,1)S(1)} %get-tuple-element.69.order_ref, bf16[16,512]{1,0:T(8,128)(2,1)S(1)} %get-tuple-element.65.head_ref, bf16[128,8,2048]{2,1,0:T(8,128)(2,1)S(1)} %get-tuple-element.66.grads_ref), custom_call_target="tpu_custom_call" | custom-call | flops 1 | bytes 1 | tf_op jit(solution)/shard_map/pallas_call | solution.py:545
  22.7 2.8 %shard_map.78 = (bf16[256,256]{1,0:T(8,128)(2,1)S(1)}, bf16[1024,1024]{1,0:T(8,128)(2,1)S(1)}) custom-call(bf16[128,7168]{1,0:T(8,128)(2,1)} %hidden_ref.1, bf16[64,7168]{1,0:T(8,128)(2,1)} %proj_ref.1, s32[1,128]{1,0:T(1,128)S(1)} %bitcast.7, s32[8,128]{1,0:T(8,128)S(1)} %bitcast.4), custom_call_target="tpu_custom_call" | custom-call | flops 1 | bytes 1 | tf_op jit(solution)/shard_map/pallas_call | solution.py:599
  25.5 1.3 %collective-permute-start.10 = (bf16[512,512]{1,0:T(8,128)(2,1)S(1)}, bf16[512,512]{1,0:T(8,128)(2,1)S(1)}, u32[]{:S(2)}, u32[]{:S(2)}) collective-permute-start(bf16[512,512]{1,0:T(8,128)(2,1)S(1)} %collective-permute-done.2.refs_3_), channel_id=1, source_target_pairs={{0,2},{1,3},{2,0},{3,1},{4,6},{5,7},{6,4},{7,5},{8,10},{9,11},{10,... | collective-permute-start | bytes 1572872 | tf_op jit(solution)/shard_map/ppermute | solution.py:476
  26.8 3.7 %collective-permute-done.6.refs_5_ = bf16[512,512]{1,0:T(8,128)(2,1)S(1)} collective-permute-done((bf16[512,512]{1,0:T(8,128)(2,1)S(1)}, bf16[512,512]{1,0:T(8,128)(2,1)S(1)}, u32[]{:S(2)}, u32[]{:S(2)}) %collective-permute-start.6) | collective-permute-done | bytes 524320 | tf_op jit(solution)/shard_map/ppermute | solution.py:476
  30.5 2.0 %collective-permute-start.7 = (bf16[784,512]{1,0:T(8,128)(2,1)S(1)}, bf16[784,512]{1,0:T(8,128)(2,1)S(1)}, u32[]{:S(2)}, u32[]{:S(2)}) collective-permute-start(bf16[784,512]{1,0:T(8,128)(2,1)S(1)} %get-tuple-element.81), channel_id=1, source_target_pairs={{0,17},{1,16},{2,19},{3,18},{4,21},{5,20},{6,23},{7,22},{8,25},{9,... | collective-permute-start | bytes 2408456 | tf_op jit(solution)/shard_map/ppermute | solution.py:476
  32.6 0.0 collective-permute-done.1.refs_4_
  32.6 2.3 %shard_map.79 = (bf16[4096,512]{1,0:T(8,128)(2,1)S(1)}, bf16[16,256,512]{2,1,0:T(8,128)(2,1)S(1)}, f32[4096,128]{1,0:T(8,128)S(1)}) custom-call(s32[16,16]{1,0:T(8,128)S(1)} %copy-done, s32[1,128]{1,0:T(1,128)S(1)} %get-tuple-element.58.refs_0_.starts_ref, bf16[1024,512]{1,0:T(8,128)(2,1)S(1)} %get-tuple-element.68.refs_1_, ...), custom_call_target="tpu_custom_call" | custom-call | flops 1000000000 | bytes 1 | tf_op jit(solution)/shard_map/pallas_call | solution.py:288
  34.9 0.0 collective-permute-done.4.refs_6_
  34.9 1.3 %collective-permute-start.9 = (bf16[512,512]{1,0:T(8,128)(2,1)S(1)}, bf16[512,512]{1,0:T(8,128)(2,1)S(1)}, u32[]{:S(2)}, u32[]{:S(2)}) collective-permute-start(bf16[512,512]{1,0:T(8,128)(2,1)S(1)} %collective-permute-done.4.refs_6_), channel_id=1, source_target_pairs={{0,2},{1,3},{2,0},{3,1},{4,6},{5,7},{6,4},{7,5},{8,10},{9,11},{10,... | collective-permute-start | bytes 1572872 | tf_op jit(solution)/shard_map/ppermute | solution.py:476
  36.2 1.3 %collective-permute-start.14 = (bf16[512,512]{1,0:T(8,128)(2,1)S(1)}, bf16[512,512]{1,0:T(8,128)(2,1)S(1)}, u32[]{:S(2)}, u32[]{:S(2)}) collective-permute-start(bf16[512,512]{1,0:T(8,128)(2,1)S(1)} %collective-permute-done.4.refs_6_), channel_id=1, source_target_pairs={{0,4},{1,5},{2,6},{3,7},{4,12},{5,13},{6,14},{7,15},{8,0},{9,1},{1... | collective-permute-start | bytes 1572872 | tf_op jit(solution)/shard_map/ppermute | solution.py:481
  37.5 0.0 collective-permute-done.5.refs_3_
  37.5 2.0 %collective-permute-start.8 = (bf16[256,512]{1,0:T(8,128)(2,1)S(1)}, bf16[256,512]{1,0:T(8,128)(2,1)S(1)}, u32[]{:S(2)}, u32[]{:S(2)}) collective-permute-start(bf16[256,512]{1,0:T(8,128)(2,1)S(1)} %get-tuple-element.83), channel_id=1, source_target_pairs={{0,17},{1,16},{2,19},{3,18},{4,21},{5,20},{6,23},{7,22},{8,25},{9,... | collective-permute-start | bytes 786440 | tf_op jit(solution)/shard_map/ppermute | solution.py:476
  39.6 1.9 %collective-permute-start.15 = (bf16[512,512]{1,0:T(8,128)(2,1)S(1)}, bf16[512,512]{1,0:T(8,128)(2,1)S(1)}, u32[]{:S(2)}, u32[]{:S(2)}) collective-permute-start(bf16[512,512]{1,0:T(8,128)(2,1)S(1)} %collective-permute-done.1.refs_4_), channel_id=1, source_target_pairs={{0,8},{1,9},{2,10},{3,11},{4,0},{5,1},{6,2},{7,3},{8,12},{9,13},{1... | collective-permute-start | bytes 1572872 | tf_op jit(solution)/shard_map/ppermute | solution.py:481
  41.5 3.6 %shard_map.80 = (bf16[4096,512]{1,0:T(8,128)(2,1)S(1)}, bf16[16,256,512]{2,1,0:T(8,128)(2,1)S(1)}, f32[4096,128]{1,0:T(8,128)S(1)}) custom-call(s32[16,16]{1,0:T(8,128)S(1)} %copy-done, s32[1,128]{1,0:T(1,128)S(1)} %get-tuple-element.58.refs_0_.starts_ref, ...), custom_call_target="tpu_custom_call", output_to_operand_aliasing={{0}: (9, {}), {1}: (10, {}), {2}: (11, {})} | custom-call | flops 1000000000 | bytes 1 | tf_op jit(solution)/shard_map/pallas_call | solution.py:288
  45.0 6.3 %collective-permute-done.7.refs_4_ = bf16[784,512]{1,0:T(8,128)(2,1)S(1)} collective-permute-done((bf16[784,512]{1,0:T(8,128)(2,1)S(1)}, bf16[784,512]{1,0:T(8,128)(2,1)S(1)}, u32[]{:S(2)}, u32[]{:S(2)}) %collective-permute-start.7) | collective-permute-done | bytes 802848 | tf_op jit(solution)/shard_map/ppermute | solution.py:476
  51.3 2.7 %shard_map.81 = (bf16[4096,512]{1,0:T(8,128)(2,1)S(1)}, bf16[16,256,512]{2,1,0:T(8,128)(2,1)S(1)}, f32[4096,128]{1,0:T(8,128)S(1)}) custom-call(s32[16,16]{1,0:T(8,128)S(1)} %copy-done, s32[1,128]{1,0:T(1,128)S(1)} %get-tuple-element.58.refs_0_.starts_ref, ...), custom_call_target="tpu_custom_call", output_to_operand_aliasing={{0}: (6, {}), {1}: (7, {}), {2}: (8, {})} | custom-call | flops 1 | bytes 1 | tf_op jit(solution)/shard_map/pallas_call | solution.py:288
  54.0 2.6 %collective-permute-done.8.refs_4_ = bf16[256,512]{1,0:T(8,128)(2,1)S(1)} collective-permute-done((bf16[256,512]{1,0:T(8,128)(2,1)S(1)}, bf16[256,512]{1,0:T(8,128)(2,1)S(1)}, u32[]{:S(2)}, u32[]{:S(2)}) %collective-permute-start.8) | collective-permute-done | bytes 262176 | tf_op jit(solution)/shard_map/ppermute | solution.py:476
  56.6 0.0 collective-permute-done.9.refs_5_
  56.6 3.2 %shard_map.82 = (bf16[4096,512]{1,0:T(8,128)(2,1)S(1)}, bf16[16,256,512]{2,1,0:T(8,128)(2,1)S(1)}, f32[4096,128]{1,0:T(8,128)S(1)}, bf16[512,128]{1,0:T(8,128)(2...) custom-call(s32[16,16]{1,0:T(8,128)S(1)} %copy-done, ...), custom_call_target="tpu_custom_call", output_to_operand_aliasing={{0}: (7, {}), {1}: (8, {}), {2}: (9, {})} | custom-call | flops 1000000000 | bytes 1 | tf_op jit(solution)/shard_map/pallas_call | solution.py:288
  59.8 0.0 copy-start.2
  59.8 0.1 collective-permute-start.11
  60.0 1.6 %collective-permute-start.12 = (bf16[512,128]{1,0:T(8,128)(2,1)S(1)}, bf16[512,128]{1,0:T(8,128)(2,1)S(1)}, u32[]{:S(2)}, u32[]{:S(2)}) collective-permute-start(bf16[512,128]{1,0:T(8,128)(2,1)S(1)} %get-tuple-element.97), channel_id=1, source_target_pairs={{0,16},{1,17},{2,18},{3,19},{4,20},{5,21},{6,22},{7,23},{8,24},{9,... | collective-permute-start | bytes 393224 | tf_op jit(solution)/shard_map/ppermute | solution.py:476
  61.6 0.4 collective-permute-start.13
  62.0 0.1 collective-permute-done.15.refs_6_
  62.2 1.5 %shard_map.83 = (f32[224,128]{1,0:T(8,128)S(1)}, bf16[224,128]{1,0:T(8,128)(2,1)S(1)}, bf16[224,128]{1,0:T(8,128)(2,1)S(1)}, bf16[224,128]{1,0:T(8,128)(2,1)S(1)}) custom-call(s32[16,16]{1,0:T(8,128)S(1)} %copy-done, s32[1,128]{1,0:T(1,128)S(1)} %get-tuple-element.58.refs_0_.starts_ref, s32[1,128]{1,0:T(1,128)S(1)} %slice_add_fusion.2.refs_1_, ...), custom_call_target="tpu_custom_call" | custom-call | flops 1 | bytes 1 | tf_op jit(solution)/shard_map/pallas_call | solution.py:747
  63.7 0.6 collective-permute-start.16
  64.3 0.8 %collective-permute-start.17 = (bf16[224,128]{1,0:T(8,128)(2,1)S(1)}, bf16[224,128]{1,0:T(8,128)(2,1)S(1)}, u32[]{:S(2)}, u32[]{:S(2)}) collective-permute-start(bf16[224,128]{1,0:T(8,128)(2,1)S(1)} %get-tuple-element.108), channel_id=1, source_target_pairs={{0,16},{1,17},{2,18},{3,19},{4,20},{5,21},{6,22},{7,23},{8,24},{9,... | collective-permute-start | bytes 172040 | tf_op jit(solution)/shard_map/ppermute | solution.py:476
  65.1 0.9 %collective-permute-start.18 = (bf16[224,128]{1,0:T(8,128)(2,1)S(1)}, bf16[224,128]{1,0:T(8,128)(2,1)S(1)}, u32[]{:S(2)}, u32[]{:S(2)}) collective-permute-start(bf16[224,128]{1,0:T(8,128)(2,1)S(1)} %get-tuple-element.109), channel_id=1, source_target_pairs={{0,17},{1,16},{2,19},{3,18},{4,21},{5,20},{6,23},{7,22},{8,25},{9,... | collective-permute-start | bytes 172040 | tf_op jit(solution)/shard_map/ppermute | solution.py:476
  66.0 0.0 collective-permute-done.12.c_ref
  66.0 3.1 %collective-permute-done.13.d_ref = bf16[512,128]{1,0:T(8,128)(2,1)S(1)} collective-permute-done((bf16[512,128]{1,0:T(8,128)(2,1)S(1)}, bf16[512,128]{1,0:T(8,128)(2,1)S(1)}, u32[]{:S(2)}, u32[]{:S(2)}) %collective-permute-start.13) | collective-permute-done | bytes 131104 | tf_op jit(solution)/shard_map/ppermute | solution.py:476
  69.1 3.1 %shard_map.84 = (bf16[2,64,4096]{2,1,0:T(8,128)(2,1)}, f32[64,1024]{1,0:T(8,128)S(1)}) custom-call(s32[8,128]{1,0:T(8,128)S(1)} %bitcast.5, bf16[256,256]{1,0:T(8,128)(2,1)S(1)} %get-tuple-element.76.basis_ref, bf16[1024,1024]{1,0:T(8,128)(2,1)S(1)} %get-tuple-element.77.order_ref, f32[4096,128]{1,0:T(8,128)S(1)} %get-tuple-element.95.total_ref, ...), custom_call_target="tpu_custom_call" | custom-call | flops 1 | bytes 1 | tf_op jit(solution)/shard_map/pallas_call | solution.py:758
  72.2 0.0 collective-permute-done.16.b_ref
  72.2 0.0 collective-permute-done.17.c_ref
  72.2 2.2 %shard_map.85 = bf16[2,64,4096]{2,1,0:T(8,128)(2,1)} custom-call(s32[16,16]{1,0:T(8,128)S(1)} %copy-done, s32[1,128]{1,0:T(1,128)S(1)} %get-tuple-element.58.refs_0_.starts_ref, s32[8,128]{1,0:T(8,128)S(1)} %bitcast.6, bf16[256,256]{1,0:T(8,128)(2,1)S(1)} %get-tuple-element.76.basis_ref, ...), custom_call_target="tpu_custom_call", output_to_operand_aliasing={{}: (10, {})} | custom-call | flops 1 | bytes 1 | tf_op jit(solution)/shard_map/pallas_call | solution.py:771
  (17 shorter events, 0.1 us)
Async XLA Ops:
  0.0 0.7 copy-start.1
  4.0 2.8 %collective-permute-start = (bf16[256,512]{1,0:T(8,128)(2,1)S(1)}, bf16[256,512]{1,0:T(8,128)(2,1)S(1)}, u32[]{:S(2)}, u32[]{:S(2)}) collective-permute-start(bf16[256,512]{1,0:T(8,128)(2,1)S(1)} %get-tuple-element.60), channel_id=1, source_target_pairs={{0,1},{1,0},{2,3},{3,2},{4,5},{5,4},{6,7},{7,6},{8,9},{9,8},{10,11... | collective-permute-start | bytes 786440 | tf_op jit(solution)/shard_map/ppermute | solution.py:476
  4.1 15.2 %collective-permute-start.3 = (bf16[528,512]{1,0:T(8,128)(2,1)S(1)}, bf16[528,512]{1,0:T(8,128)(2,1)S(1)}, u32[]{:S(2)}, u32[]{:S(2)}) collective-permute-start(bf16[528,512]{1,0:T(8,128)(2,1)S(1)} %get-tuple-element.61), channel_id=1, source_target_pairs={{0,16},{1,17},{2,18},{3,19},{4,20},{5,21},{6,22},{7,23},{8,24},{9,... | collective-permute-start | bytes 1622024 | tf_op jit(solution)/shard_map/ppermute | solution.py:476
  6.8 14.1 %collective-permute-start.2 = (bf16[512,512]{1,0:T(8,128)(2,1)S(1)}, bf16[512,512]{1,0:T(8,128)(2,1)S(1)}, u32[]{:S(2)}, u32[]{:S(2)}) collective-permute-start(bf16[512,512]{1,0:T(8,128)(2,1)S(1)} %shard_map.74.refs_2_), channel_id=1, source_target_pairs={{0,4},{1,5},{2,6},{3,7},{4,12},{5,13},{6,14},{7,15},{8,0},{9,1},{1... | collective-permute-start | bytes 1572872 | tf_op jit(solution)/shard_map/ppermute | solution.py:481
  8.9 21.7 %collective-permute-start.6 = (bf16[512,512]{1,0:T(8,128)(2,1)S(1)}, bf16[512,512]{1,0:T(8,128)(2,1)S(1)}, u32[]{:S(2)}, u32[]{:S(2)}) collective-permute-start(bf16[512,512]{1,0:T(8,128)(2,1)S(1)} %shard_map.75), channel_id=1, source_target_pairs={{0,16},{1,17},{2,18},{3,19},{4,20},{5,21},{6,22},{7,23},{8,24},{9,... | collective-permute-start | bytes 1572872 | tf_op jit(solution)/shard_map/ppermute | solution.py:476
  10.1 22.5 %collective-permute-start.1 = (bf16[512,512]{1,0:T(8,128)(2,1)S(1)}, bf16[512,512]{1,0:T(8,128)(2,1)S(1)}, u32[]{:S(2)}, u32[]{:S(2)}) collective-permute-start(bf16[512,512]{1,0:T(8,128)(2,1)S(1)} %shard_map.74.refs_2_), channel_id=1, source_target_pairs={{0,2},{1,3},{2,0},{3,1},{4,6},{5,7},{6,4},{7,5},{8,10},{9,11},{10,... | collective-permute-start | bytes 1572872 | tf_op jit(solution)/shard_map/ppermute | solution.py:476
  13.7 9.0 %copy-start.3 = (s32[128]{0:T(128)S(1)}, s32[128]{0:T(128)}, u32[]{:S(2)}) copy-start(s32[128]{0:T(128)} %param.10) | copy-start | bytes 1540
  13.7 23.8 %collective-permute-start.5 = (bf16[1040,512]{1,0:T(8,128)(2,1)S(1)}, bf16[1040,512]{1,0:T(8,128)(2,1)S(1)}, u32[]{:S(2)}, u32[]{:S(2)}) collective-permute-start(bf16[1040,512]{1,0:T(8,128)(2,1)S(1)} %get-tuple-element.75), channel_id=1, source_target_pairs={{0,1},{1,0},{2,3},{3,2},{4,5},{5,4},{6,7},{7,6},{8,9},{9,8},{10,11... | collective-permute-start | bytes 3194888 | tf_op jit(solution)/shard_map/ppermute | solution.py:476
  20.9 14.0 %collective-permute-start.4 = (bf16[512,512]{1,0:T(8,128)(2,1)S(1)}, bf16[512,512]{1,0:T(8,128)(2,1)S(1)}, u32[]{:S(2)}, u32[]{:S(2)}) collective-permute-start(bf16[512,512]{1,0:T(8,128)(2,1)S(1)} %collective-permute-done.2.refs_3_), channel_id=1, source_target_pairs={{0,4},{1,5},{2,6},{3,7},{4,12},{5,13},{6,14},{7,15},{8,0},{9,1},{1... | collective-permute-start | bytes 1572872 | tf_op jit(solution)/shard_map/ppermute | solution.py:481
  21.4 11.1 %copy-start = (s32[16,16]{1,0:T(8,128)S(1)}, s32[16,16]{1,0:T(8,128)}, u32[]{:S(2)}) copy-start(s32[16,16]{1,0:T(8,128)} %constant.4.clone.bases_ref) | copy-start | bytes 3076
  25.5 14.1 %collective-permute-start.10 = (bf16[512,512]{1,0:T(8,128)(2,1)S(1)}, bf16[512,512]{1,0:T(8,128)(2,1)S(1)}, u32[]{:S(2)}, u32[]{:S(2)}) collective-permute-start(bf16[512,512]{1,0:T(8,128)(2,1)S(1)} %collective-permute-done.2.refs_3_), channel_id=1, source_target_pairs={{0,2},{1,3},{2,0},{3,1},{4,6},{5,7},{6,4},{7,5},{8,10},{9,11},{10,... | collective-permute-start | bytes 1572872 | tf_op jit(solution)/shard_map/ppermute | solution.py:476
  30.5 20.8 %collective-permute-start.7 = (bf16[784,512]{1,0:T(8,128)(2,1)S(1)}, bf16[784,512]{1,0:T(8,128)(2,1)S(1)}, u32[]{:S(2)}, u32[]{:S(2)}) collective-permute-start(bf16[784,512]{1,0:T(8,128)(2,1)S(1)} %get-tuple-element.81), channel_id=1, source_target_pairs={{0,17},{1,16},{2,19},{3,18},{4,21},{5,20},{6,23},{7,22},{8,25},{9,... | collective-permute-start | bytes 2408456 | tf_op jit(solution)/shard_map/ppermute | solution.py:476
  34.9 21.7 %collective-permute-start.9 = (bf16[512,512]{1,0:T(8,128)(2,1)S(1)}, bf16[512,512]{1,0:T(8,128)(2,1)S(1)}, u32[]{:S(2)}, u32[]{:S(2)}) collective-permute-start(bf16[512,512]{1,0:T(8,128)(2,1)S(1)} %collective-permute-done.4.refs_6_), channel_id=1, source_target_pairs={{0,2},{1,3},{2,0},{3,1},{4,6},{5,7},{6,4},{7,5},{8,10},{9,11},{10,... | collective-permute-start | bytes 1572872 | tf_op jit(solution)/shard_map/ppermute | solution.py:476
  36.2 25.8 %collective-permute-start.14 = (bf16[512,512]{1,0:T(8,128)(2,1)S(1)}, bf16[512,512]{1,0:T(8,128)(2,1)S(1)}, u32[]{:S(2)}, u32[]{:S(2)}) collective-permute-start(bf16[512,512]{1,0:T(8,128)(2,1)S(1)} %collective-permute-done.4.refs_6_), channel_id=1, source_target_pairs={{0,4},{1,5},{2,6},{3,7},{4,12},{5,13},{6,14},{7,15},{8,0},{9,1},{1... | collective-permute-start | bytes 1572872 | tf_op jit(solution)/shard_map/ppermute | solution.py:481
  37.5 19.1 %collective-permute-start.8 = (bf16[256,512]{1,0:T(8,128)(2,1)S(1)}, bf16[256,512]{1,0:T(8,128)(2,1)S(1)}, u32[]{:S(2)}, u32[]{:S(2)}) collective-permute-start(bf16[256,512]{1,0:T(8,128)(2,1)S(1)} %get-tuple-element.83), channel_id=1, source_target_pairs={{0,17},{1,16},{2,19},{3,18},{4,21},{5,20},{6,23},{7,22},{8,25},{9,... | collective-permute-start | bytes 786440 | tf_op jit(solution)/shard_map/ppermute | solution.py:476
  39.6 22.6 %collective-permute-start.15 = (bf16[512,512]{1,0:T(8,128)(2,1)S(1)}, bf16[512,512]{1,0:T(8,128)(2,1)S(1)}, u32[]{:S(2)}, u32[]{:S(2)}) collective-permute-start(bf16[512,512]{1,0:T(8,128)(2,1)S(1)} %collective-permute-done.1.refs_4_), channel_id=1, source_target_pairs={{0,8},{1,9},{2,10},{3,11},{4,0},{5,1},{6,2},{7,3},{8,12},{9,13},{1... | collective-permute-start | bytes 1572872 | tf_op jit(solution)/shard_map/ppermute | solution.py:481
  59.8 9.3 %copy-start.2 = (s32[128,8]{0,1:T(8,128)S(1)}, s32[128,8]{0,1:T(8,128)}, u32[]{:S(2)}) copy-start(s32[128,8]{0,1:T(8,128)} %param.9) | copy-start | bytes 12292
  59.8 5.3 %collective-permute-start.11 = (bf16[512,128]{1,0:T(8,128)(2,1)S(1)}, bf16[512,128]{1,0:T(8,128)(2,1)S(1)}, u32[]{:S(2)}, u32[]{:S(2)}) collective-permute-start(bf16[512,128]{1,0:T(8,128)(2,1)S(1)} %get-tuple-element.96), channel_id=1, source_target_pairs={{0,1},{1,0},{2,3},{3,2},{4,5},{5,4},{6,7},{7,6},{8,9},{9,8},{10,11... | collective-permute-start | bytes 393224 | tf_op jit(solution)/shard_map/ppermute | solution.py:476
  60.0 6.0 %collective-permute-start.12 = (bf16[512,128]{1,0:T(8,128)(2,1)S(1)}, bf16[512,128]{1,0:T(8,128)(2,1)S(1)}, u32[]{:S(2)}, u32[]{:S(2)}) collective-permute-start(bf16[512,128]{1,0:T(8,128)(2,1)S(1)} %get-tuple-element.97), channel_id=1, source_target_pairs={{0,16},{1,17},{2,18},{3,19},{4,20},{5,21},{6,22},{7,23},{8,24},{9,... | collective-permute-start | bytes 393224 | tf_op jit(solution)/shard_map/ppermute | solution.py:476
  61.6 7.5 %collective-permute-start.13 = (bf16[512,128]{1,0:T(8,128)(2,1)S(1)}, bf16[512,128]{1,0:T(8,128)(2,1)S(1)}, u32[]{:S(2)}, u32[]{:S(2)}) collective-permute-start(bf16[512,128]{1,0:T(8,128)(2,1)S(1)} %get-tuple-element.98), channel_id=1, source_target_pairs={{0,17},{1,16},{2,19},{3,18},{4,21},{5,20},{6,23},{7,22},{8,25},{9,... | collective-permute-start | bytes 393224 | tf_op jit(solution)/shard_map/ppermute | solution.py:476
  63.7 8.5 %collective-permute-start.16 = (bf16[224,128]{1,0:T(8,128)(2,1)S(1)}, bf16[224,128]{1,0:T(8,128)(2,1)S(1)}, u32[]{:S(2)}, u32[]{:S(2)}) collective-permute-start(bf16[224,128]{1,0:T(8,128)(2,1)S(1)} %get-tuple-element.107), channel_id=1, source_target_pairs={{0,1},{1,0},{2,3},{3,2},{4,5},{5,4},{6,7},{7,6},{8,9},{9,8},{10,11... | collective-permute-start | bytes 172040 | tf_op jit(solution)/shard_map/ppermute | solution.py:476
  64.3 7.9 %collective-permute-start.17 = (bf16[224,128]{1,0:T(8,128)(2,1)S(1)}, bf16[224,128]{1,0:T(8,128)(2,1)S(1)}, u32[]{:S(2)}, u32[]{:S(2)}) collective-permute-start(bf16[224,128]{1,0:T(8,128)(2,1)S(1)} %get-tuple-element.108), channel_id=1, source_target_pairs={{0,16},{1,17},{2,18},{3,19},{4,20},{5,21},{6,22},{7,23},{8,24},{9,... | collective-permute-start | bytes 172040 | tf_op jit(solution)/shard_map/ppermute | solution.py:476
  65.1 7.1 %collective-permute-start.18 = (bf16[224,128]{1,0:T(8,128)(2,1)S(1)}, bf16[224,128]{1,0:T(8,128)(2,1)S(1)}, u32[]{:S(2)}, u32[]{:S(2)}) collective-permute-start(bf16[224,128]{1,0:T(8,128)(2,1)S(1)} %get-tuple-element.109), channel_id=1, source_target_pairs={{0,17},{1,16},{2,19},{3,18},{4,21},{5,20},{6,23},{7,22},{8,25},{9,... | collective-permute-start | bytes 172040 | tf_op jit(solution)/shard_map/ppermute | solution.py:476

commit v15 on v14

--- a/solution.py
+++ b/solution.py
@@ -9,7 +9,7 @@
 from jax.sharding import PartitionSpec as P
 
 SEG_DEV = 2
-O = {'p1': 'core_unit', 'z1': 'none', 'p2': 'unit', 'cores': 1, 'core_in': 'none', 'y0': 'unit', 'basis': [], 'ev1': ['side0'], 'diag': ['side1'], 'ev2': ['basis', 'side0'], 'w': ['basis', 'core'], 'last': ['z2'], 'ka': 1, 'z3_ka': 0, 'w_ka': 0, 'k0': 1, 'k1': 0, 'k2': 1, 'y2': 'd', 'core_k': 'b', 'side_k': 'b'}
+O = {'p1': 'core_unit', 'z1': 'none', 'p2': 'unit', 'cores': 1, 'core_in': 'none', 'y0': 'unit', 'basis': [], 'ev1': ['side0'], 'diag': ['side0'], 'ev2': ['basis', 'side0'], 'w': ['basis', 'core'], 'last': ['side1'], 'ka': 1, 'z3_ka': 0, 'w_ka': 0, 'k0': 1, 'k1': 0, 'k2': 1, 'y2': 'd', 'core_k': 'b', 'side_k': 'b'}
 CORES = 2
 SIDES = 2
 QUAD = 4

time: 74.6 us -> 74.5 us (level)
  waiting for transfers between devices: 21.9 us -> 24 us
  starting transfers between devices: 22.7 us -> 20.6 us
    ppermute x15, waiting for transfers between devices: 20.2 us -> 22.2 us  [swap(): return lax.ppermute(array, BOTH, table)]
    ppermute x15, starting transfers between devices: 17.6 us -> 15.6 us  [swap(): return lax.ppermute(array, BOTH, table)]
where the time goes in v15:
time: 74.5 us; the launch traced here: 74.4 us
  Pallas kernels  29 us (39%)
  waiting for transfers between devices  24 us (32%)
  starting transfers between devices  20.6 us (28%)
    ppermute x15, waiting for transfers between devices, swap(): return lax.ppermute(array, BOTH, table)  22.2 us
    ppermute x15, starting transfers between devices, swap(): return lax.ppermute(array, BOTH, table)  15.6 us
    pallas_call x4, Pallas kernels, accumulate(): pl.pallas_call(functools.partial(partial_kernel, rank, pairs, window, [(f...  11.7 us
    ppermute x4, starting transfers between devices, along(): return lax.ppermute(array, 'expert', pairs_of)  4.96 us
    pallas_call x3, Pallas kernels, permuted(): pl.pallas_call(functools.partial(permute_kernel, plan), out_shape=[rows_s...  4.33 us
    pallas_call x1, Pallas kernels, local(): pl.pallas_call(sort_kernel, out_shape=[pltpu.VMEM(out_grads.shape, jnp.bf...  3.26 us
    pallas_call x1, Pallas kernels, local(): pl.pallas_call(functools.partial(blocks_kernel, rank), out_shape=[jax.Sha...  3.08 us
    pallas_call x1, Pallas kernels, local(): pl.pallas_call(basis_kernel, out_shape=[pltpu.VMEM((2 * tokens, SEG_DEV *...  2.79 us
  transfers between devices with their start and end apart: 19, of which 7 were waited for; matrix products, arithmetic and copies ran while one was open for 0% of the time, Pallas kernels for 32%

profile of v15, /device:TPU:1, one launch (start us, length us, event | category | flops | bytes accessed | tf_op | source)
XLA Modules:
  0.0 74.4 jit_solution(7594737492888195992)
XLA Ops:
  0.0 0.7 copy-done.1
  0.7 3.3 %shard_map.73 = (bf16[128,8,2048]{2,1,0:T(8,128)(2,1)S(1)}, bf16[256,512]{1,0:T(8,128)(2,1)S(1)}, bf16[256,512]{1,0:T(8,128)(2,1)S(1)}, s32[1,128]{1,0:T(1,128)S...) custom-call(s32[8,128]{1,0:T(8,128)S(1)} %bitcast.3, ...), custom_call_target="tpu_custom_call" | custom-call | flops 1 | bytes 1 | tf_op jit(solution)/shard_map/pallas_call | solution.py:516
  4.0 0.1 collective-permute-start
  4.1 2.7 %collective-permute-start.3 = (bf16[528,512]{1,0:T(8,128)(2,1)S(1)}, bf16[528,512]{1,0:T(8,128)(2,1)S(1)}, u32[]{:S(2)}, u32[]{:S(2)}) collective-permute-start(bf16[528,512]{1,0:T(8,128)(2,1)S(1)} %get-tuple-element.61), channel_id=1, source_target_pairs={{0,16},{1,17},{2,18},{3,19},{4,20},{5,21},{6,22},{7,23},{8,24},{9,... | collective-permute-start | bytes 1622024 | tf_op jit(solution)/shard_map/ppermute | solution.py:476
  6.7 0.0 collective-permute-done.two_ref
  6.8 1.3 %collective-permute-start.2 = (bf16[512,512]{1,0:T(8,128)(2,1)S(1)}, bf16[512,512]{1,0:T(8,128)(2,1)S(1)}, u32[]{:S(2)}, u32[]{:S(2)}) collective-permute-start(bf16[512,512]{1,0:T(8,128)(2,1)S(1)} %shard_map.74.refs_2_), channel_id=1, source_target_pairs={{0,4},{1,5},{2,6},{3,7},{4,12},{5,13},{6,14},{7,15},{8,0},{9,1},{1... | collective-permute-start | bytes 1572872 | tf_op jit(solution)/shard_map/ppermute | solution.py:481
  8.1 0.7 shard_map.75
  8.9 1.2 %collective-permute-start.7 = (bf16[512,512]{1,0:T(8,128)(2,1)S(1)}, bf16[512,512]{1,0:T(8,128)(2,1)S(1)}, u32[]{:S(2)}, u32[]{:S(2)}) collective-permute-start(bf16[512,512]{1,0:T(8,128)(2,1)S(1)} %shard_map.75), channel_id=1, source_target_pairs={{0,16},{1,17},{2,18},{3,19},{4,20},{5,21},{6,22},{7,23},{8,24},{9,... | collective-permute-start | bytes 1572872 | tf_op jit(solution)/shard_map/ppermute | solution.py:476
  10.1 1.2 %collective-permute-start.1 = (bf16[512,512]{1,0:T(8,128)(2,1)S(1)}, bf16[512,512]{1,0:T(8,128)(2,1)S(1)}, u32[]{:S(2)}, u32[]{:S(2)}) collective-permute-start(bf16[512,512]{1,0:T(8,128)(2,1)S(1)} %shard_map.74.refs_2_), channel_id=1, source_target_pairs={{0,2},{1,3},{2,0},{3,1},{4,6},{5,7},{6,4},{7,5},{8,10},{9,11},{10,... | collective-permute-start | bytes 1572872 | tf_op jit(solution)/shard_map/ppermute | solution.py:476
  11.3 2.3 %shard_map.76 = (bf16[1024,512]{1,0:T(8,128)(2,1)S(1)}, bf16[1040,512]{1,0:T(8,128)(2,1)S(1)}) custom-call(bf16[1024,1024]{1,0:T(8,128)(2,1)S(1)} %get-tuple-element.69.order_ref, bf16[16,512]{1,0:T(8,128)(2,1)S(1)} %get-tuple-element.65.head_ref, bf16[128,8,2048]{2,1,0:T(8,128)(2,1)S(1)} %get-tuple-element.66.grads_ref), custom_call_target="tpu_custom_call" | custom-call | flops 1 | bytes 1 | tf_op jit(solution)/shard_map/pallas_call | solution.py:545
  13.7 0.0 copy-start.3
  13.7 1.3 %collective-permute-start.5 = (bf16[1040,512]{1,0:T(8,128)(2,1)S(1)}, bf16[1040,512]{1,0:T(8,128)(2,1)S(1)}, u32[]{:S(2)}, u32[]{:S(2)}) collective-permute-start(bf16[1040,512]{1,0:T(8,128)(2,1)S(1)} %get-tuple-element.77), channel_id=1, source_target_pairs={{0,1},{1,0},{2,3},{3,2},{4,5},{5,4},{6,7},{7,6},{8,9},{9,8},{10,11... | collective-permute-start | bytes 3194888 | tf_op jit(solution)/shard_map/ppermute | solution.py:476
  15.0 4.3 %collective-permute-done.3.refs_4_ = bf16[528,512]{1,0:T(8,128)(2,1)S(1)} collective-permute-done((bf16[528,512]{1,0:T(8,128)(2,1)S(1)}, bf16[528,512]{1,0:T(8,128)(2,1)S(1)}, u32[]{:S(2)}, u32[]{:S(2)}) %collective-permute-start.3) | collective-permute-done | bytes 540704 | tf_op jit(solution)/shard_map/ppermute | solution.py:476
  19.3 1.6 %collective-permute-done.2.refs_3_ = bf16[512,512]{1,0:T(8,128)(2,1)S(1)} collective-permute-done((bf16[512,512]{1,0:T(8,128)(2,1)S(1)}, bf16[512,512]{1,0:T(8,128)(2,1)S(1)}, u32[]{:S(2)}, u32[]{:S(2)}) %collective-permute-start.2) | collective-permute-done | bytes 524320 | tf_op jit(solution)/shard_map/ppermute | solution.py:481
  20.9 0.5 collective-permute-start.4
  21.4 1.3 %shard_map.77 = (bf16[784,512]{1,0:T(8,128)(2,1)S(1)}, bf16[256,512]{1,0:T(8,128)(2,1)S(1)}) custom-call(bf16[1024,1024]{1,0:T(8,128)(2,1)S(1)} %get-tuple-element.69.order_ref, bf16[16,512]{1,0:T(8,128)(2,1)S(1)} %get-tuple-element.65.head_ref, bf16[128,8,2048]{2,1,0:T(8,128)(2,1)S(1)} %get-tuple-element.66.grads_ref), custom_call_target="tpu_custom_call" | custom-call | flops 1 | bytes 1 | tf_op jit(solution)/shard_map/pallas_call | solution.py:545
  22.7 2.8 %shard_map.78 = (bf16[256,256]{1,0:T(8,128)(2,1)S(1)}, bf16[1024,1024]{1,0:T(8,128)(2,1)S(1)}) custom-call(bf16[128,7168]{1,0:T(8,128)(2,1)} %hidden_ref.1, bf16[64,7168]{1,0:T(8,128)(2,1)} %proj_ref.1, s32[1,128]{1,0:T(1,128)S(1)} %bitcast.7, s32[8,128]{1,0:T(8,128)S(1)} %bitcast.4), custom_call_target="tpu_custom_call" | custom-call | flops 1 | bytes 1 | tf_op jit(solution)/shard_map/pallas_call | solution.py:599
  25.5 1.3 %collective-permute-start.10 = (bf16[512,512]{1,0:T(8,128)(2,1)S(1)}, bf16[512,512]{1,0:T(8,128)(2,1)S(1)}, u32[]{:S(2)}, u32[]{:S(2)}) collective-permute-start(bf16[512,512]{1,0:T(8,128)(2,1)S(1)} %collective-permute-done.2.refs_3_), channel_id=1, source_target_pairs={{0,2},{1,3},{2,0},{3,1},{4,6},{5,7},{6,4},{7,5},{8,10},{9,11},{10,... | collective-permute-start | bytes 1572872 | tf_op jit(solution)/shard_map/ppermute | solution.py:476
  26.8 3.7 %collective-permute-done.7.refs_5_ = bf16[512,512]{1,0:T(8,128)(2,1)S(1)} collective-permute-done((bf16[512,512]{1,0:T(8,128)(2,1)S(1)}, bf16[512,512]{1,0:T(8,128)(2,1)S(1)}, u32[]{:S(2)}, u32[]{:S(2)}) %collective-permute-start.7) | collective-permute-done | bytes 524320 | tf_op jit(solution)/shard_map/ppermute | solution.py:476
  30.5 2.0 %collective-permute-start.6 = (bf16[784,512]{1,0:T(8,128)(2,1)S(1)}, bf16[784,512]{1,0:T(8,128)(2,1)S(1)}, u32[]{:S(2)}, u32[]{:S(2)}) collective-permute-start(bf16[784,512]{1,0:T(8,128)(2,1)S(1)} %get-tuple-element.82), channel_id=1, source_target_pairs={{0,17},{1,16},{2,19},{3,18},{4,21},{5,20},{6,23},{7,22},{8,25},{9,... | collective-permute-start | bytes 2408456 | tf_op jit(solution)/shard_map/ppermute | solution.py:476
  32.6 0.0 collective-permute-done.1.refs_4_
  32.6 0.0 collective-permute-start.8
  32.6 2.3 %shard_map.79 = (bf16[4096,512]{1,0:T(8,128)(2,1)S(1)}, bf16[16,256,512]{2,1,0:T(8,128)(2,1)S(1)}, f32[4096,128]{1,0:T(8,128)S(1)}) custom-call(s32[16,16]{1,0:T(8,128)S(1)} %copy-done, s32[1,128]{1,0:T(1,128)S(1)} %get-tuple-element.58.refs_0_.starts_ref, bf16[1024,512]{1,0:T(8,128)(2,1)S(1)} %get-tuple-element.68.refs_1_, ...), custom_call_target="tpu_custom_call" | custom-call | flops 1000000000 | bytes 1 | tf_op jit(solution)/shard_map/pallas_call | solution.py:288
  34.9 0.0 collective-permute-done.4.refs_6_
  34.9 1.3 %collective-permute-start.9 = (bf16[512,512]{1,0:T(8,128)(2,1)S(1)}, bf16[512,512]{1,0:T(8,128)(2,1)S(1)}, u32[]{:S(2)}, u32[]{:S(2)}) collective-permute-start(bf16[512,512]{1,0:T(8,128)(2,1)S(1)} %collective-permute-done.4.refs_6_), channel_id=1, source_target_pairs={{0,2},{1,3},{2,0},{3,1},{4,6},{5,7},{6,4},{7,5},{8,10},{9,11},{10,... | collective-permute-start | bytes 1572872 | tf_op jit(solution)/shard_map/ppermute | solution.py:476
  36.3 1.3 %collective-permute-start.14 = (bf16[512,512]{1,0:T(8,128)(2,1)S(1)}, bf16[512,512]{1,0:T(8,128)(2,1)S(1)}, u32[]{:S(2)}, u32[]{:S(2)}) collective-permute-start(bf16[512,512]{1,0:T(8,128)(2,1)S(1)} %collective-permute-done.4.refs_6_), channel_id=1, source_target_pairs={{0,4},{1,5},{2,6},{3,7},{4,12},{5,13},{6,14},{7,15},{8,0},{9,1},{1... | collective-permute-start | bytes 1572872 | tf_op jit(solution)/shard_map/ppermute | solution.py:481
  37.6 0.0 collective-permute-done.10.refs_7_
  37.6 1.8 %collective-permute-start.15 = (bf16[512,512]{1,0:T(8,128)(2,1)S(1)}, bf16[512,512]{1,0:T(8,128)(2,1)S(1)}, u32[]{:S(2)}, u32[]{:S(2)}) collective-permute-start(bf16[512,512]{1,0:T(8,128)(2,1)S(1)} %collective-permute-done.1.refs_4_), channel_id=1, source_target_pairs={{0,8},{1,9},{2,10},{3,11},{4,0},{5,1},{6,2},{7,3},{8,12},{9,13},{1... | collective-permute-start | bytes 1572872 | tf_op jit(solution)/shard_map/ppermute | solution.py:481
  39.4 3.6 %shard_map.80 = (bf16[4096,512]{1,0:T(8,128)(2,1)S(1)}, bf16[16,256,512]{2,1,0:T(8,128)(2,1)S(1)}, f32[4096,128]{1,0:T(8,128)S(1)}) custom-call(s32[16,16]{1,0:T(8,128)S(1)} %copy-done, s32[1,128]{1,0:T(1,128)S(1)} %get-tuple-element.58.refs_0_.starts_ref, ...), custom_call_target="tpu_custom_call", output_to_operand_aliasing={{0}: (9, {}), {1}: (10, {}), {2}: (11, {})} | custom-call | flops 1000000000 | bytes 1 | tf_op jit(solution)/shard_map/pallas_call | solution.py:288
  42.9 8.4 %collective-permute-done.6.refs_4_ = bf16[784,512]{1,0:T(8,128)(2,1)S(1)} collective-permute-done((bf16[784,512]{1,0:T(8,128)(2,1)S(1)}, bf16[784,512]{1,0:T(8,128)(2,1)S(1)}, u32[]{:S(2)}, u32[]{:S(2)}) %collective-permute-start.6) | collective-permute-done | bytes 802848 | tf_op jit(solution)/shard_map/ppermute | solution.py:476
  51.3 2.7 %shard_map.81 = (bf16[4096,512]{1,0:T(8,128)(2,1)S(1)}, bf16[16,256,512]{2,1,0:T(8,128)(2,1)S(1)}, f32[4096,128]{1,0:T(8,128)S(1)}) custom-call(s32[16,16]{1,0:T(8,128)S(1)} %copy-done, s32[1,128]{1,0:T(1,128)S(1)} %get-tuple-element.58.refs_0_.starts_ref, ...), custom_call_target="tpu_custom_call", output_to_operand_aliasing={{0}: (6, {}), {1}: (7, {}), {2}: (8, {})} | custom-call | flops 1 | bytes 1 | tf_op jit(solution)/shard_map/pallas_call | solution.py:288
  54.0 2.6 %collective-permute-done.8.refs_4_ = bf16[256,512]{1,0:T(8,128)(2,1)S(1)} collective-permute-done((bf16[256,512]{1,0:T(8,128)(2,1)S(1)}, bf16[256,512]{1,0:T(8,128)(2,1)S(1)}, u32[]{:S(2)}, u32[]{:S(2)}) %collective-permute-start.8) | collective-permute-done | bytes 262176 | tf_op jit(solution)/shard_map/ppermute | solution.py:476
  56.6 3.2 %shard_map.82 = (bf16[4096,512]{1,0:T(8,128)(2,1)S(1)}, bf16[16,256,512]{2,1,0:T(8,128)(2,1)S(1)}, f32[4096,128]{1,0:T(8,128)S(1)}, bf16[512,128]{1,0:T(8,128)(2...) custom-call(s32[16,16]{1,0:T(8,128)S(1)} %copy-done, ...), custom_call_target="tpu_custom_call", output_to_operand_aliasing={{0}: (7, {}), {1}: (8, {}), {2}: (9, {})} | custom-call | flops 1000000000 | bytes 1 | tf_op jit(solution)/shard_map/pallas_call | solution.py:288
  59.8 0.0 copy-start.2
  59.8 0.1 collective-permute-start.11
  60.0 1.6 %collective-permute-start.12 = (bf16[512,128]{1,0:T(8,128)(2,1)S(1)}, bf16[512,128]{1,0:T(8,128)(2,1)S(1)}, u32[]{:S(2)}, u32[]{:S(2)}) collective-permute-start(bf16[512,128]{1,0:T(8,128)(2,1)S(1)} %get-tuple-element.97), channel_id=1, source_target_pairs={{0,16},{1,17},{2,18},{3,19},{4,20},{5,21},{6,22},{7,23},{8,24},{9,... | collective-permute-start | bytes 393224 | tf_op jit(solution)/shard_map/ppermute | solution.py:476
  61.6 0.4 collective-permute-start.13
  62.0 0.0 collective-permute-done.14.refs_5_
  62.0 0.2 collective-permute-done.15.refs_6_
  62.2 1.6 %shard_map.83 = (f32[224,128]{1,0:T(8,128)S(1)}, bf16[224,128]{1,0:T(8,128)(2,1)S(1)}, bf16[224,128]{1,0:T(8,128)(2,1)S(1)}, bf16[224,128]{1,0:T(8,128)(2,1)S(1)}) custom-call(s32[16,16]{1,0:T(8,128)S(1)} %copy-done, s32[1,128]{1,0:T(1,128)S(1)} %get-tuple-element.58.refs_0_.starts_ref, s32[1,128]{1,0:T(1,128)S(1)} %slice_add_fusion.2.refs_1_, ...), custom_call_target="tpu_custom_call" | custom-call | flops 1 | bytes 1 | tf_op jit(solution)/shard_map/pallas_call | solution.py:747
  63.8 0.6 collective-permute-start.16
  64.4 1.0 %collective-permute-start.17 = (bf16[224,128]{1,0:T(8,128)(2,1)S(1)}, bf16[224,128]{1,0:T(8,128)(2,1)S(1)}, u32[]{:S(2)}, u32[]{:S(2)}) collective-permute-start(bf16[224,128]{1,0:T(8,128)(2,1)S(1)} %get-tuple-element.108), channel_id=1, source_target_pairs={{0,16},{1,17},{2,18},{3,19},{4,20},{5,21},{6,22},{7,23},{8,24},{9,... | collective-permute-start | bytes 172040 | tf_op jit(solution)/shard_map/ppermute | solution.py:476
  65.3 0.0 collective-permute-done.11.b_ref
  65.3 0.7 collective-permute-start.18
  66.1 0.0 collective-permute-done.12.c_ref
  66.1 3.1 %collective-permute-done.13.d_ref = bf16[512,128]{1,0:T(8,128)(2,1)S(1)} collective-permute-done((bf16[512,128]{1,0:T(8,128)(2,1)S(1)}, bf16[512,128]{1,0:T(8,128)(2,1)S(1)}, u32[]{:S(2)}, u32[]{:S(2)}) %collective-permute-start.13) | collective-permute-done | bytes 131104 | tf_op jit(solution)/shard_map/ppermute | solution.py:476
  69.1 3.1 %shard_map.84 = (bf16[2,64,4096]{2,1,0:T(8,128)(2,1)}, f32[64,1024]{1,0:T(8,128)S(1)}) custom-call(s32[8,128]{1,0:T(8,128)S(1)} %bitcast.5, bf16[256,256]{1,0:T(8,128)(2,1)S(1)} %get-tuple-element.78.basis_ref, bf16[1024,1024]{1,0:T(8,128)(2,1)S(1)} %get-tuple-element.79.order_ref, f32[4096,128]{1,0:T(8,128)S(1)} %get-tuple-element.95.total_ref, ...), custom_call_target="tpu_custom_call" | custom-call | flops 1 | bytes 1 | tf_op jit(solution)/shard_map/pallas_call | solution.py:758
  72.2 2.2 %shard_map.85 = bf16[2,64,4096]{2,1,0:T(8,128)(2,1)} custom-call(s32[16,16]{1,0:T(8,128)S(1)} %copy-done, s32[1,128]{1,0:T(1,128)S(1)} %get-tuple-element.58.refs_0_.starts_ref, s32[8,128]{1,0:T(8,128)S(1)} %bitcast.6, bf16[256,256]{1,0:T(8,128)(2,1)S(1)} %get-tuple-element.78.basis_ref, ...), custom_call_target="tpu_custom_call", output_to_operand_aliasing={{}: (10, {})} | custom-call | flops 1 | bytes 1 | tf_op jit(solution)/shard_map/pallas_call | solution.py:771
  (17 shorter events, 0.1 us)
Async XLA Ops:
  0.0 0.7 copy-start.1
  4.0 2.8 %collective-permute-start = (bf16[256,512]{1,0:T(8,128)(2,1)S(1)}, bf16[256,512]{1,0:T(8,128)(2,1)S(1)}, u32[]{:S(2)}, u32[]{:S(2)}) collective-permute-start(bf16[256,512]{1,0:T(8,128)(2,1)S(1)} %get-tuple-element.60), channel_id=1, source_target_pairs={{0,1},{1,0},{2,3},{3,2},{4,5},{5,4},{6,7},{7,6},{8,9},{9,8},{10,11... | collective-permute-start | bytes 786440 | tf_op jit(solution)/shard_map/ppermute | solution.py:476
  4.1 15.2 %collective-permute-start.3 = (bf16[528,512]{1,0:T(8,128)(2,1)S(1)}, bf16[528,512]{1,0:T(8,128)(2,1)S(1)}, u32[]{:S(2)}, u32[]{:S(2)}) collective-permute-start(bf16[528,512]{1,0:T(8,128)(2,1)S(1)} %get-tuple-element.61), channel_id=1, source_target_pairs={{0,16},{1,17},{2,18},{3,19},{4,20},{5,21},{6,22},{7,23},{8,24},{9,... | collective-permute-start | bytes 1622024 | tf_op jit(solution)/shard_map/ppermute | solution.py:476
  6.8 14.1 %collective-permute-start.2 = (bf16[512,512]{1,0:T(8,128)(2,1)S(1)}, bf16[512,512]{1,0:T(8,128)(2,1)S(1)}, u32[]{:S(2)}, u32[]{:S(2)}) collective-permute-start(bf16[512,512]{1,0:T(8,128)(2,1)S(1)} %shard_map.74.refs_2_), channel_id=1, source_target_pairs={{0,4},{1,5},{2,6},{3,7},{4,12},{5,13},{6,14},{7,15},{8,0},{9,1},{1... | collective-permute-start | bytes 1572872 | tf_op jit(solution)/shard_map/ppermute | solution.py:481
  8.9 21.7 %collective-permute-start.7 = (bf16[512,512]{1,0:T(8,128)(2,1)S(1)}, bf16[512,512]{1,0:T(8,128)(2,1)S(1)}, u32[]{:S(2)}, u32[]{:S(2)}) collective-permute-start(bf16[512,512]{1,0:T(8,128)(2,1)S(1)} %shard_map.75), channel_id=1, source_target_pairs={{0,16},{1,17},{2,18},{3,19},{4,20},{5,21},{6,22},{7,23},{8,24},{9,... | collective-permute-start | bytes 1572872 | tf_op jit(solution)/shard_map/ppermute | solution.py:476
  10.1 22.5 %collective-permute-start.1 = (bf16[512,512]{1,0:T(8,128)(2,1)S(1)}, bf16[512,512]{1,0:T(8,128)(2,1)S(1)}, u32[]{:S(2)}, u32[]{:S(2)}) collective-permute-start(bf16[512,512]{1,0:T(8,128)(2,1)S(1)} %shard_map.74.refs_2_), channel_id=1, source_target_pairs={{0,2},{1,3},{2,0},{3,1},{4,6},{5,7},{6,4},{7,5},{8,10},{9,11},{10,... | collective-permute-start | bytes 1572872 | tf_op jit(solution)/shard_map/ppermute | solution.py:476
  13.7 9.0 %copy-start.3 = (s32[128]{0:T(128)S(1)}, s32[128]{0:T(128)}, u32[]{:S(2)}) copy-start(s32[128]{0:T(128)} %param.10) | copy-start | bytes 1540
  13.7 22.6 %collective-permute-start.5 = (bf16[1040,512]{1,0:T(8,128)(2,1)S(1)}, bf16[1040,512]{1,0:T(8,128)(2,1)S(1)}, u32[]{:S(2)}, u32[]{:S(2)}) collective-permute-start(bf16[1040,512]{1,0:T(8,128)(2,1)S(1)} %get-tuple-element.77), channel_id=1, source_target_pairs={{0,1},{1,0},{2,3},{3,2},{4,5},{5,4},{6,7},{7,6},{8,9},{9,8},{10,11... | collective-permute-start | bytes 3194888 | tf_op jit(solution)/shard_map/ppermute | solution.py:476
  20.9 14.0 %collective-permute-start.4 = (bf16[512,512]{1,0:T(8,128)(2,1)S(1)}, bf16[512,512]{1,0:T(8,128)(2,1)S(1)}, u32[]{:S(2)}, u32[]{:S(2)}) collective-permute-start(bf16[512,512]{1,0:T(8,128)(2,1)S(1)} %collective-permute-done.2.refs_3_), channel_id=1, source_target_pairs={{0,4},{1,5},{2,6},{3,7},{4,12},{5,13},{6,14},{7,15},{8,0},{9,1},{1... | collective-permute-start | bytes 1572872 | tf_op jit(solution)/shard_map/ppermute | solution.py:481
  21.4 11.2 %copy-start = (s32[16,16]{1,0:T(8,128)S(1)}, s32[16,16]{1,0:T(8,128)}, u32[]{:S(2)}) copy-start(s32[16,16]{1,0:T(8,128)} %constant.4.clone.bases_ref) | copy-start | bytes 3076
  25.5 12.1 %collective-permute-start.10 = (bf16[512,512]{1,0:T(8,128)(2,1)S(1)}, bf16[512,512]{1,0:T(8,128)(2,1)S(1)}, u32[]{:S(2)}, u32[]{:S(2)}) collective-permute-start(bf16[512,512]{1,0:T(8,128)(2,1)S(1)} %collective-permute-done.2.refs_3_), channel_id=1, source_target_pairs={{0,2},{1,3},{2,0},{3,1},{4,6},{5,7},{6,4},{7,5},{8,10},{9,11},{10,... | collective-permute-start | bytes 1572872 | tf_op jit(solution)/shard_map/ppermute | solution.py:476
  30.5 20.8 %collective-permute-start.6 = (bf16[784,512]{1,0:T(8,128)(2,1)S(1)}, bf16[784,512]{1,0:T(8,128)(2,1)S(1)}, u32[]{:S(2)}, u32[]{:S(2)}) collective-permute-start(bf16[784,512]{1,0:T(8,128)(2,1)S(1)} %get-tuple-element.82), channel_id=1, source_target_pairs={{0,17},{1,16},{2,19},{3,18},{4,21},{5,20},{6,23},{7,22},{8,25},{9,... | collective-permute-start | bytes 2408456 | tf_op jit(solution)/shard_map/ppermute | solution.py:476
  32.6 24.0 %collective-permute-start.8 = (bf16[256,512]{1,0:T(8,128)(2,1)S(1)}, bf16[256,512]{1,0:T(8,128)(2,1)S(1)}, u32[]{:S(2)}, u32[]{:S(2)}) collective-permute-start(bf16[256,512]{1,0:T(8,128)(2,1)S(1)} %get-tuple-element.83), channel_id=1, source_target_pairs={{0,17},{1,16},{2,19},{3,18},{4,21},{5,20},{6,23},{7,22},{8,25},{9,... | collective-permute-start | bytes 786440 | tf_op jit(solution)/shard_map/ppermute | solution.py:476
  34.9 21.7 %collective-permute-start.9 = (bf16[512,512]{1,0:T(8,128)(2,1)S(1)}, bf16[512,512]{1,0:T(8,128)(2,1)S(1)}, u32[]{:S(2)}, u32[]{:S(2)}) collective-permute-start(bf16[512,512]{1,0:T(8,128)(2,1)S(1)} %collective-permute-done.4.refs_6_), channel_id=1, source_target_pairs={{0,2},{1,3},{2,0},{3,1},{4,6},{5,7},{6,4},{7,5},{8,10},{9,11},{10,... | collective-permute-start | bytes 1572872 | tf_op jit(solution)/shard_map/ppermute | solution.py:476
  36.3 25.8 %collective-permute-start.14 = (bf16[512,512]{1,0:T(8,128)(2,1)S(1)}, bf16[512,512]{1,0:T(8,128)(2,1)S(1)}, u32[]{:S(2)}, u32[]{:S(2)}) collective-permute-start(bf16[512,512]{1,0:T(8,128)(2,1)S(1)} %collective-permute-done.4.refs_6_), channel_id=1, source_target_pairs={{0,4},{1,5},{2,6},{3,7},{4,12},{5,13},{6,14},{7,15},{8,0},{9,1},{1... | collective-permute-start | bytes 1572872 | tf_op jit(solution)/shard_map/ppermute | solution.py:481
  37.6 24.7 %collective-permute-start.15 = (bf16[512,512]{1,0:T(8,128)(2,1)S(1)}, bf16[512,512]{1,0:T(8,128)(2,1)S(1)}, u32[]{:S(2)}, u32[]{:S(2)}) collective-permute-start(bf16[512,512]{1,0:T(8,128)(2,1)S(1)} %collective-permute-done.1.refs_4_), channel_id=1, source_target_pairs={{0,8},{1,9},{2,10},{3,11},{4,0},{5,1},{6,2},{7,3},{8,12},{9,13},{1... | collective-permute-start | bytes 1572872 | tf_op jit(solution)/shard_map/ppermute | solution.py:481
  59.8 9.3 %copy-start.2 = (s32[128,8]{0,1:T(8,128)S(1)}, s32[128,8]{0,1:T(8,128)}, u32[]{:S(2)}) copy-start(s32[128,8]{0,1:T(8,128)} %param.9) | copy-start | bytes 12292
  59.8 5.5 %collective-permute-start.11 = (bf16[512,128]{1,0:T(8,128)(2,1)S(1)}, bf16[512,128]{1,0:T(8,128)(2,1)S(1)}, u32[]{:S(2)}, u32[]{:S(2)}) collective-permute-start(bf16[512,128]{1,0:T(8,128)(2,1)S(1)} %get-tuple-element.96), channel_id=1, source_target_pairs={{0,1},{1,0},{2,3},{3,2},{4,5},{5,4},{6,7},{7,6},{8,9},{9,8},{10,11... | collective-permute-start | bytes 393224 | tf_op jit(solution)/shard_map/ppermute | solution.py:476
  60.0 6.1 %collective-permute-start.12 = (bf16[512,128]{1,0:T(8,128)(2,1)S(1)}, bf16[512,128]{1,0:T(8,128)(2,1)S(1)}, u32[]{:S(2)}, u32[]{:S(2)}) collective-permute-start(bf16[512,128]{1,0:T(8,128)(2,1)S(1)} %get-tuple-element.97), channel_id=1, source_target_pairs={{0,16},{1,17},{2,18},{3,19},{4,20},{5,21},{6,22},{7,23},{8,24},{9,... | collective-permute-start | bytes 393224 | tf_op jit(solution)/shard_map/ppermute | solution.py:476
  61.6 7.5 %collective-permute-start.13 = (bf16[512,128]{1,0:T(8,128)(2,1)S(1)}, bf16[512,128]{1,0:T(8,128)(2,1)S(1)}, u32[]{:S(2)}, u32[]{:S(2)}) collective-permute-start(bf16[512,128]{1,0:T(8,128)(2,1)S(1)} %get-tuple-element.98), channel_id=1, source_target_pairs={{0,17},{1,16},{2,19},{3,18},{4,21},{5,20},{6,23},{7,22},{8,25},{9,... | collective-permute-start | bytes 393224 | tf_op jit(solution)/shard_map/ppermute | solution.py:476
  63.8 8.4 %collective-permute-start.16 = (bf16[224,128]{1,0:T(8,128)(2,1)S(1)}, bf16[224,128]{1,0:T(8,128)(2,1)S(1)}, u32[]{:S(2)}, u32[]{:S(2)}) collective-permute-start(bf16[224,128]{1,0:T(8,128)(2,1)S(1)} %get-tuple-element.107), channel_id=1, source_target_pairs={{0,1},{1,0},{2,3},{3,2},{4,5},{5,4},{6,7},{7,6},{8,9},{9,8},{10,11... | collective-permute-start | bytes 172040 | tf_op jit(solution)/shard_map/ppermute | solution.py:476
  64.4 7.9 %collective-permute-start.17 = (bf16[224,128]{1,0:T(8,128)(2,1)S(1)}, bf16[224,128]{1,0:T(8,128)(2,1)S(1)}, u32[]{:S(2)}, u32[]{:S(2)}) collective-permute-start(bf16[224,128]{1,0:T(8,128)(2,1)S(1)} %get-tuple-element.108), channel_id=1, source_target_pairs={{0,16},{1,17},{2,18},{3,19},{4,20},{5,21},{6,22},{7,23},{8,24},{9,... | collective-permute-start | bytes 172040 | tf_op jit(solution)/shard_map/ppermute | solution.py:476
  65.3 6.9 %collective-permute-start.18 = (bf16[224,128]{1,0:T(8,128)(2,1)S(1)}, bf16[224,128]{1,0:T(8,128)(2,1)S(1)}, u32[]{:S(2)}, u32[]{:S(2)}) collective-permute-start(bf16[224,128]{1,0:T(8,128)(2,1)S(1)} %get-tuple-element.109), channel_id=1, source_target_pairs={{0,17},{1,16},{2,19},{3,18},{4,21},{5,20},{6,23},{7,22},{8,25},{9,... | collective-permute-start | bytes 172040 | tf_op jit(solution)/shard_map/ppermute | solution.py:476

commit v16 on v13

--- a/solution.py
+++ b/solution.py
@@ -9,7 +9,6 @@
 from jax.sharding import PartitionSpec as P
 
 SEG_DEV = 2
-O = {'p1': 'core_unit', 'z1': 'none', 'p2': 'unit', 'cores': 2, 'core_in': 'none', 'y0': 'unit', 'basis': [], 'ev1': ['side0'], 'diag': ['side0'], 'ev2': ['basis', 'side0'], 'w': ['basis', 'core'], 'last': ['z2'], 'ka': 0, 'z3_ka': 0, 'w_ka': 0, 'k0': 1, 'k1': 0, 'k2': 1, 'y2': 'c'}
 CORES = 2
 SIDES = 2
 QUAD = 4
@@ -558,44 +557,16 @@
         digits = block[count : count + 2, :edges].astype(jnp.int32)
         return (digits[0] * DIGIT + digits[1]).reshape(1, edges)
 
+    half = 2 * rows
     side_pieces = [swap(first_piece, 1, 0)]
-    ring_unit = unit
-    if O["z1"] == "first":
-        ring_unit, _ = tie(unit, first_piece)
-    held = {(0, 0): unit, (1, 0): along(ring_unit, following)}
-    p2after = {"none": [], "unit": [unit], "z1": [held[1, 0]]}[O["p2"]]
-    (second_piece,) = permuted([(2, 2 * rows, 2 * rows)], [], *p2after)
-    second_send = second_piece
-    half = 2 * rows
-    if O["cores"] == 2:
-        own_tokens, *for_core = permuted([(0, 0, pairs), (1, 0, half), (1, half, half)], [1], second_piece)
-        core_counts = [half, half]
-    else:
-        own_tokens, *for_core = permuted([(0, 0, pairs), (1, 0, pairs)], [1], second_piece)
-        core_counts = [pairs]
+    held = {(0, 0): unit, (1, 0): along(unit, following)}
+    (second_piece,) = permuted([(2, half, half)], [], unit)
+    own_tokens, for_core = permuted([(0, 0, pairs), (1, 0, pairs)], [1], second_piece)
     third_piece, last_piece = permuted([(3, 0, 3 * rows), (3, 3 * rows, rows)], [0], own_tokens)
-    if O["core_in"] == "ev1":
-        *for_core, held[1, 0] = tie(*for_core, held[1, 0])
-    from_core = [swap(piece, 0, 1) for piece in for_core]
-    y0_in = unit
-    if O["y0"] == "first":
-        y0_in, _ = tie(unit, first_piece)
-    elif O["y0"] == "second":
-        y0_in, _ = tie(unit, second_piece)
-    elif O["y0"] == "own":
-        y0_in, _ = tie(unit, own_tokens)
-    elif O["y0"] == "core":
-        y0_in, *from_core = tie(unit, *from_core)
-    held[0, 1] = swap(y0_in, 0, CORES)
-    side_pieces.append(swap(second_send, 1, 0))
-    basis_in = [last_piece]
-    if "z1" in O["basis"]:
-        basis_in.append(held[1, 0])
-    if "core" in O["basis"]:
-        basis_in += from_core
-    local_segments, *basis_out = tie(segments, *basis_in)
-    if "core" in O["basis"]:
-        from_core = basis_out[len(basis_out) - len(from_core):]
+    from_core = swap(for_core, 0, 1)
+    held[0, 1] = swap(unit, 0, CORES)
+    side_pieces.append(swap(second_piece, 1, 0))
+    local_segments, _ = tie(segments, last_piece)
     basis, order_back = pl.pallas_call(
         basis_kernel,
         out_shape=[
@@ -656,79 +627,29 @@
         )
         return out
 
-    def group_tie(names, array):
-        nonlocal basis, from_core
-        items = []
-        for name in names:
-            if name == "y0":
-                items.append(held[0, 1])
-            if name == "y1":
-                items.append(held[1, 1])
-            if name == "z1":
-                items.append(held[1, 0])
-            if name == "z2":
-                items.append(held[near])
-            if name == "side0":
-                items.append(side_pieces[0])
-            if name == "side1":
-                items.append(side_pieces[1])
-            if name == "basis":
-                items.append(basis)
-            if name == "core":
-                items += from_core
-        out = tie(array, *items)
-        out = list(out)
-        array, out = out[0], out[1:]
-        for name in names:
-            if name == "y0":
-                held[0, 1] = out.pop(0)
-            if name == "y1":
-                held[1, 1] = out.pop(0)
-            if name == "z1":
-                held[1, 0] = out.pop(0)
-            if name == "z2":
-                held[near] = out.pop(0)
-            if name == "side0":
-                side_pieces[0] = out.pop(0)
-            if name == "side1":
-                side_pieces[1] = out.pop(0)
-            if name == "basis":
-                basis = out.pop(0)
-            if name == "core":
-                from_core = [out.pop(0) for _ in from_core]
-        return array
-
-    held[1, 0] = group_tie(O["ev1"], held[1, 0])
+    held[1, 0], side_pieces[0] = tie(held[1, 0], side_pieces[0])
     for n in range(1, final - 1):
         held[n + 1, 0] = along(held[n, 0], following)
         held[n, 1] = swap(held[n, 0], 0, CORES)
-    third_piece = group_tie(O["diag"], third_piece)
+    third_piece, side_pieces[0] = tie(third_piece, side_pieces[0])
     diagonal_pieces = [swap(third_piece, 1, 1)]
     near = (final - 1, 0)
-    held[near] = group_tie(O["ev2"], held[near])
-    COST = {0: QUICK, 1: SHORT}
-    work(
-        names_a,
-        complete=[(0, [(own_tokens, pairs)]), (1, list(zip(from_core, core_counts)))],
-        cost=COST[O["ka"]],
-    )
-    if O["z3_ka"]:
-        held[near], *state = tie(held[near], *state)
-    back_unit = group_tie(O["w"], held[0, 1])
-    if O["w_ka"]:
-        back_unit, *state = tie(back_unit, *state)
+    held[near], basis, side_pieces[0] = tie(held[near], basis, side_pieces[0])
+    work(names_a, complete=[(0, [(own_tokens, pairs)])], cost=SHORT)
+    back_unit, basis, from_core = tie(held[0, 1], basis, from_core)
     held[final, 1] = along(back_unit, before)
     held[final, 0] = along(held[near], following)
     held[final - 1, 1] = swap(held[near], 0, CORES)
-    last_piece = group_tie(O["last"], last_piece)
+    last_piece, side_pieces[1] = tie(last_piece, side_pieces[1])
     diagonal_pieces.append(swap(last_piece, 1, 1))
-    work(names_b, complete=[(2, [(piece, half) for piece in side_pieces])], cost=COST[O["k0"]])
-    sent = work(
-        names_c if O["y2"] == "c" else [], partial=[(3, diagonal_pieces[0], 0, 3 * rows)], sends=[1, 2] if O["y2"] == "c" else [], cost=COST[O["k1"]]
+    work(
+        names_b,
+        complete=[(1, [(from_core, pairs)]), (2, [(piece, half) for piece in side_pieces])],
+        cost=SHORT,
     )
-    sent = sent + work(
-        [] if O["y2"] == "c" else names_c, partial=[(3, diagonal_pieces[1], 3 * rows, rows)], sends=[3] if O["y2"] == "c" else [1, 2, 3], cost=COST[O["k2"]]
-    )
+    work([], partial=[(3, diagonal_pieces[0], 0, 3 * rows)])
+    sent = work(names_c, sends=[1, 2])
+    sent = sent + work([], partial=[(3, diagonal_pieces[1], 3 * rows, rows)], sends=[3], cost=SHORT)
 
     def returned(arrays):
         return [

time: 74.5 us -> 73.3 us (0.984)
  starting transfers between devices: 23.1 us -> 20.4 us
  waiting for transfers between devices: 20.2 us -> 21 us
    ppermute x16 -> x15, starting transfers between devices: 18.8 us -> 15.4 us  [swap(): return lax.ppermute(array, BOTH, table)]
    ppermute x16 -> x15, waiting for transfers between devices: 17 us -> 18 us  [swap(): return lax.ppermute(array, BOTH, table)]
    pallas_call x4 -> x5, Pallas kernels: 11.7 us -> 12.5 us  [accumulate(): pl.pallas_call(functools.partial(partial_kernel, rank, pairs, window, [(f...]
  transfers between devices with their start and end apart: 20 -> 19, of which waited for: 6 -> 7; matrix products, arithmetic and copies ran while one was open for 0% -> 0% of each run, Pallas kernels for 32% -> 34%
where the time goes in v16:
time: 73.3 us; the launch traced here: 72.1 us
  Pallas kernels  29.7 us (41%)
  waiting for transfers between devices  21 us (29%)
  starting transfers between devices  20.4 us (28%)
    ppermute x15, waiting for transfers between devices, swap(): return lax.ppermute(array, BOTH, table)  18 us
    ppermute x15, starting transfers between devices, swap(): return lax.ppermute(array, BOTH, table)  15.4 us
    pallas_call x5, Pallas kernels, accumulate(): pl.pallas_call(functools.partial(partial_kernel, rank, pairs, window, [(f...  12.5 us
    ppermute x4, starting transfers between devices, along(): return lax.ppermute(array, 'expert', pairs_of)  4.97 us
    pallas_call x3, Pallas kernels, permuted(): pl.pallas_call(functools.partial(permute_kernel, plan), out_shape=[rows_s...  4.32 us
    pallas_call x1, Pallas kernels, local(): pl.pallas_call(sort_kernel, out_shape=[pltpu.VMEM(out_grads.shape, jnp.bf...  3.26 us
    pallas_call x1, Pallas kernels, local(): pl.pallas_call(functools.partial(blocks_kernel, rank), out_shape=[jax.Sha...  3.08 us
    ppermute x4, waiting for transfers between devices, along(): return lax.ppermute(array, 'expert', pairs_of)  3.03 us
  transfers between devices with their start and end apart: 19, of which 7 were waited for; matrix products, arithmetic and copies ran while one was open for 0% of the time, Pallas kernels for 34%

profile of v16, /device:TPU:1, one launch (start us, length us, event | category | flops | bytes accessed | tf_op | source)
XLA Modules:
  0.0 72.1 jit_solution(15831488303806089278)
XLA Ops:
  0.0 0.7 copy-done.1
  0.7 3.3 %shard_map.73 = (bf16[128,8,2048]{2,1,0:T(8,128)(2,1)S(1)}, bf16[256,512]{1,0:T(8,128)(2,1)S(1)}, bf16[256,512]{1,0:T(8,128)(2,1)S(1)}, s32[1,128]{1,0:T(1,128)S...) custom-call(s32[8,128]{1,0:T(8,128)S(1)} %bitcast.3, ...), custom_call_target="tpu_custom_call" | custom-call | flops 1 | bytes 1 | tf_op jit(solution)/shard_map/pallas_call | solution.py:515
  4.0 0.1 collective-permute-start
  4.1 2.7 %collective-permute-start.3 = (bf16[528,512]{1,0:T(8,128)(2,1)S(1)}, bf16[528,512]{1,0:T(8,128)(2,1)S(1)}, u32[]{:S(2)}, u32[]{:S(2)}) collective-permute-start(bf16[528,512]{1,0:T(8,128)(2,1)S(1)} %get-tuple-element.64), channel_id=1, source_target_pairs={{0,16},{1,17},{2,18},{3,19},{4,20},{5,21},{6,22},{7,23},{8,24},{9,... | collective-permute-start | bytes 1622024 | tf_op jit(solution)/shard_map/ppermute | solution.py:475
  6.7 0.0 collective-permute-done.two_ref
  6.8 1.4 %collective-permute-start.2 = (bf16[512,512]{1,0:T(8,128)(2,1)S(1)}, bf16[512,512]{1,0:T(8,128)(2,1)S(1)}, u32[]{:S(2)}, u32[]{:S(2)}) collective-permute-start(bf16[512,512]{1,0:T(8,128)(2,1)S(1)} %shard_map.74.refs_2_), channel_id=1, source_target_pairs={{0,4},{1,5},{2,6},{3,7},{4,12},{5,13},{6,14},{7,15},{8,0},{9,1},{1... | collective-permute-start | bytes 1572872 | tf_op jit(solution)/shard_map/ppermute | solution.py:480
  8.1 0.7 shard_map.75
  8.9 1.2 %collective-permute-start.7 = (bf16[512,512]{1,0:T(8,128)(2,1)S(1)}, bf16[512,512]{1,0:T(8,128)(2,1)S(1)}, u32[]{:S(2)}, u32[]{:S(2)}) collective-permute-start(bf16[512,512]{1,0:T(8,128)(2,1)S(1)} %shard_map.75), channel_id=1, source_target_pairs={{0,16},{1,17},{2,18},{3,19},{4,20},{5,21},{6,22},{7,23},{8,24},{9,... | collective-permute-start | bytes 1572872 | tf_op jit(solution)/shard_map/ppermute | solution.py:475
  10.1 1.2 %collective-permute-start.1 = (bf16[512,512]{1,0:T(8,128)(2,1)S(1)}, bf16[512,512]{1,0:T(8,128)(2,1)S(1)}, u32[]{:S(2)}, u32[]{:S(2)}) collective-permute-start(bf16[512,512]{1,0:T(8,128)(2,1)S(1)} %shard_map.74.refs_2_), channel_id=1, source_target_pairs={{0,2},{1,3},{2,0},{3,1},{4,6},{5,7},{6,4},{7,5},{8,10},{9,11},{10,... | collective-permute-start | bytes 1572872 | tf_op jit(solution)/shard_map/ppermute | solution.py:475
  11.3 2.3 %shard_map.76 = (bf16[1024,512]{1,0:T(8,128)(2,1)S(1)}, bf16[1040,512]{1,0:T(8,128)(2,1)S(1)}) custom-call(bf16[1024,1024]{1,0:T(8,128)(2,1)S(1)} %get-tuple-element.72.order_ref, bf16[16,512]{1,0:T(8,128)(2,1)S(1)} %get-tuple-element.68.head_ref, bf16[128,8,2048]{2,1,0:T(8,128)(2,1)S(1)} %get-tuple-element.69.grads_ref), custom_call_target="tpu_custom_call" | custom-call | flops 1 | bytes 1 | tf_op jit(solution)/shard_map/pallas_call | solution.py:544
  13.7 0.0 copy-start.3
  13.7 1.3 %collective-permute-start.5 = (bf16[1040,512]{1,0:T(8,128)(2,1)S(1)}, bf16[1040,512]{1,0:T(8,128)(2,1)S(1)}, u32[]{:S(2)}, u32[]{:S(2)}) collective-permute-start(bf16[1040,512]{1,0:T(8,128)(2,1)S(1)} %get-tuple-element.80), channel_id=1, source_target_pairs={{0,1},{1,0},{2,3},{3,2},{4,5},{5,4},{6,7},{7,6},{8,9},{9,8},{10,11... | collective-permute-start | bytes 3194888 | tf_op jit(solution)/shard_map/ppermute | solution.py:475
  15.0 4.3 %collective-permute-done.3.refs_4_ = bf16[528,512]{1,0:T(8,128)(2,1)S(1)} collective-permute-done((bf16[528,512]{1,0:T(8,128)(2,1)S(1)}, bf16[528,512]{1,0:T(8,128)(2,1)S(1)}, u32[]{:S(2)}, u32[]{:S(2)}) %collective-permute-start.3) | collective-permute-done | bytes 540704 | tf_op jit(solution)/shard_map/ppermute | solution.py:475
  19.3 1.6 %collective-permute-done.2.refs_3_ = bf16[512,512]{1,0:T(8,128)(2,1)S(1)} collective-permute-done((bf16[512,512]{1,0:T(8,128)(2,1)S(1)}, bf16[512,512]{1,0:T(8,128)(2,1)S(1)}, u32[]{:S(2)}, u32[]{:S(2)}) %collective-permute-start.2) | collective-permute-done | bytes 524320 | tf_op jit(solution)/shard_map/ppermute | solution.py:480
  20.9 0.5 collective-permute-start.4
  21.4 1.3 %shard_map.77 = (bf16[784,512]{1,0:T(8,128)(2,1)S(1)}, bf16[256,512]{1,0:T(8,128)(2,1)S(1)}) custom-call(bf16[1024,1024]{1,0:T(8,128)(2,1)S(1)} %get-tuple-element.72.order_ref, bf16[16,512]{1,0:T(8,128)(2,1)S(1)} %get-tuple-element.68.head_ref, bf16[128,8,2048]{2,1,0:T(8,128)(2,1)S(1)} %get-tuple-element.69.grads_ref), custom_call_target="tpu_custom_call" | custom-call | flops 1 | bytes 1 | tf_op jit(solution)/shard_map/pallas_call | solution.py:544
  22.7 2.8 %shard_map.78 = (bf16[256,256]{1,0:T(8,128)(2,1)S(1)}, bf16[1024,1024]{1,0:T(8,128)(2,1)S(1)}) custom-call(bf16[128,7168]{1,0:T(8,128)(2,1)} %hidden_ref.1, bf16[64,7168]{1,0:T(8,128)(2,1)} %proj_ref.1, s32[1,128]{1,0:T(1,128)S(1)} %bitcast.7, s32[8,128]{1,0:T(8,128)S(1)} %bitcast.4), custom_call_target="tpu_custom_call" | custom-call | flops 1 | bytes 1 | tf_op jit(solution)/shard_map/pallas_call | solution.py:570
  25.5 1.3 %collective-permute-start.10 = (bf16[512,512]{1,0:T(8,128)(2,1)S(1)}, bf16[512,512]{1,0:T(8,128)(2,1)S(1)}, u32[]{:S(2)}, u32[]{:S(2)}) collective-permute-start(bf16[512,512]{1,0:T(8,128)(2,1)S(1)} %collective-permute-done.2.refs_3_), channel_id=1, source_target_pairs={{0,2},{1,3},{2,0},{3,1},{4,6},{5,7},{6,4},{7,5},{8,10},{9,11},{10,... | collective-permute-start | bytes 1572872 | tf_op jit(solution)/shard_map/ppermute | solution.py:475
  26.8 3.7 %collective-permute-done.7.refs_5_ = bf16[512,512]{1,0:T(8,128)(2,1)S(1)} collective-permute-done((bf16[512,512]{1,0:T(8,128)(2,1)S(1)}, bf16[512,512]{1,0:T(8,128)(2,1)S(1)}, u32[]{:S(2)}, u32[]{:S(2)}) %collective-permute-start.7) | collective-permute-done | bytes 524320 | tf_op jit(solution)/shard_map/ppermute | solution.py:475
  30.5 2.0 %collective-permute-start.6 = (bf16[784,512]{1,0:T(8,128)(2,1)S(1)}, bf16[784,512]{1,0:T(8,128)(2,1)S(1)}, u32[]{:S(2)}, u32[]{:S(2)}) collective-permute-start(bf16[784,512]{1,0:T(8,128)(2,1)S(1)} %get-tuple-element.85), channel_id=1, source_target_pairs={{0,17},{1,16},{2,19},{3,18},{4,21},{5,20},{6,23},{7,22},{8,25},{9,... | collective-permute-start | bytes 2408456 | tf_op jit(solution)/shard_map/ppermute | solution.py:475
  32.6 0.0 collective-permute-start.8
  32.6 2.3 %shard_map.79 = (bf16[4096,512]{1,0:T(8,128)(2,1)S(1)}, bf16[16,256,512]{2,1,0:T(8,128)(2,1)S(1)}, f32[4096,128]{1,0:T(8,128)S(1)}) custom-call(s32[16,16]{1,0:T(8,128)S(1)} %copy-done, s32[1,128]{1,0:T(1,128)S(1)} %get-tuple-element.61.refs_0_.starts_ref, bf16[1024,512]{1,0:T(8,128)(2,1)S(1)} %get-tuple-element.71.refs_1_, ...), custom_call_target="tpu_custom_call" | custom-call | flops 1000000000 | bytes 1 | tf_op jit(solution)/shard_map/pallas_call | solution.py:287
  34.9 0.0 collective-permute-done.4.refs_6_
  34.9 1.3 %collective-permute-start.9 = (bf16[512,512]{1,0:T(8,128)(2,1)S(1)}, bf16[512,512]{1,0:T(8,128)(2,1)S(1)}, u32[]{:S(2)}, u32[]{:S(2)}) collective-permute-start(bf16[512,512]{1,0:T(8,128)(2,1)S(1)} %collective-permute-done.4.refs_6_), channel_id=1, source_target_pairs={{0,2},{1,3},{2,0},{3,1},{4,6},{5,7},{6,4},{7,5},{8,10},{9,11},{10,... | collective-permute-start | bytes 1572872 | tf_op jit(solution)/shard_map/ppermute | solution.py:475
  36.2 1.3 %collective-permute-start.14 = (bf16[512,512]{1,0:T(8,128)(2,1)S(1)}, bf16[512,512]{1,0:T(8,128)(2,1)S(1)}, u32[]{:S(2)}, u32[]{:S(2)}) collective-permute-start(bf16[512,512]{1,0:T(8,128)(2,1)S(1)} %collective-permute-done.4.refs_6_), channel_id=1, source_target_pairs={{0,4},{1,5},{2,6},{3,7},{4,12},{5,13},{6,14},{7,15},{8,0},{9,1},{1... | collective-permute-start | bytes 1572872 | tf_op jit(solution)/shard_map/ppermute | solution.py:480
  37.6 0.0 collective-permute-done.10.refs_7_
  37.6 1.8 %collective-permute-start.15 = (bf16[512,512]{1,0:T(8,128)(2,1)S(1)}, bf16[512,512]{1,0:T(8,128)(2,1)S(1)}, u32[]{:S(2)}, u32[]{:S(2)}) collective-permute-start(bf16[512,512]{1,0:T(8,128)(2,1)S(1)} %collective-permute-done.1.refs_4_), channel_id=1, source_target_pairs={{0,8},{1,9},{2,10},{3,11},{4,0},{5,1},{6,2},{7,3},{8,12},{9,13},{1... | collective-permute-start | bytes 1572872 | tf_op jit(solution)/shard_map/ppermute | solution.py:480
  39.4 3.5 %shard_map.80 = (bf16[4096,512]{1,0:T(8,128)(2,1)S(1)}, bf16[16,256,512]{2,1,0:T(8,128)(2,1)S(1)}, f32[4096,128]{1,0:T(8,128)S(1)}) custom-call(s32[16,16]{1,0:T(8,128)S(1)} %copy-done, s32[1,128]{1,0:T(1,128)S(1)} %get-tuple-element.61.refs_0_.starts_ref, ...), custom_call_target="tpu_custom_call", output_to_operand_aliasing={{0}: (9, {}), {1}: (10, {}), {2}: (11, {})} | custom-call | flops 1000000000 | bytes 1 | tf_op jit(solution)/shard_map/pallas_call | solution.py:287
  42.9 8.4 %collective-permute-done.6.refs_4_ = bf16[784,512]{1,0:T(8,128)(2,1)S(1)} collective-permute-done((bf16[784,512]{1,0:T(8,128)(2,1)S(1)}, bf16[784,512]{1,0:T(8,128)(2,1)S(1)}, u32[]{:S(2)}, u32[]{:S(2)}) %collective-permute-start.6) | collective-permute-done | bytes 802848 | tf_op jit(solution)/shard_map/ppermute | solution.py:475
  51.3 2.7 %shard_map.81 = (bf16[4096,512]{1,0:T(8,128)(2,1)S(1)}, bf16[16,256,512]{2,1,0:T(8,128)(2,1)S(1)}, f32[4096,128]{1,0:T(8,128)S(1)}) custom-call(s32[16,16]{1,0:T(8,128)S(1)} %copy-done, s32[1,128]{1,0:T(1,128)S(1)} %get-tuple-element.61.refs_0_.starts_ref, ...), custom_call_target="tpu_custom_call", output_to_operand_aliasing={{0}: (6, {}), {1}: (7, {}), {2}: (8, {})} | custom-call | flops 1 | bytes 1 | tf_op jit(solution)/shard_map/pallas_call | solution.py:287
  54.0 0.0 collective-permute-done.9.refs_4_
  54.0 1.7 %shard_map.82 = (bf16[4096,512]{1,0:T(8,128)(2,1)S(1)}, bf16[16,256,512]{2,1,0:T(8,128)(2,1)S(1)}, f32[4096,128]{1,0:T(8,128)S(1)}, bf16[512,128]{1,0:T(8,128)(2,1)S(1)}, bf16[512,128]{1,0:T(8,128)(2,1)S(1)}) custom-call(s32[16,16]{1,0:T(8,128)S(1)} %copy-done, ...), custom_call_target="tpu_custom_call", output_to_operand_aliasing={{0}: (6, {}), {1}: (7, {}), {2}: (8, {})} | custom-call | flops 1 | bytes 1 | tf_op jit(solution)/shard_map/pallas_call | solution.py:287
  55.7 0.9 %collective-permute-done.8.refs_4_ = bf16[256,512]{1,0:T(8,128)(2,1)S(1)} collective-permute-done((bf16[256,512]{1,0:T(8,128)(2,1)S(1)}, bf16[256,512]{1,0:T(8,128)(2,1)S(1)}, u32[]{:S(2)}, u32[]{:S(2)}) %collective-permute-start.8) | collective-permute-done | bytes 262176 | tf_op jit(solution)/shard_map/ppermute | solution.py:475
  56.6 2.2 %shard_map.83 = (bf16[4096,512]{1,0:T(8,128)(2,1)S(1)}, bf16[16,256,512]{2,1,0:T(8,128)(2,1)S(1)}, f32[4096,128]{1,0:T(8,128)S(1)}, bf16[512,128]{1,0:T(8,128)(2,1)S(1)}) custom-call(s32[16,16]{1,0:T(8,128)S(1)} %copy-done, s32[1,128]{1,0:T(1,128)S(1)} %get-tuple-element.61.refs_0_.starts_ref, ...), custom_call_target="tpu_custom_call", output_to_operand_aliasing={{0}: (6, {}), {1}: (7, {}), {2}: (8, {})} | custom-call | flops 1000000000 | bytes 1 | tf_op jit(solution)/shard_map/pallas_call | solution.py:287
  58.9 0.0 copy-start.2
  58.9 1.4 %collective-permute-start.13 = (bf16[512,128]{1,0:T(8,128)(2,1)S(1)}, bf16[512,128]{1,0:T(8,128)(2,1)S(1)}, u32[]{:S(2)}, u32[]{:S(2)}) collective-permute-start(bf16[512,128]{1,0:T(8,128)(2,1)S(1)} %get-tuple-element.104), channel_id=1, source_target_pairs={{0,17},{1,16},{2,19},{3,18},{4,21},{5,20},{6,23},{7,22},{8,25},{9,... | collective-permute-start | bytes 393224 | tf_op jit(solution)/shard_map/ppermute | solution.py:475
  60.3 0.5 collective-permute-start.12
  60.8 0.0 collective-permute-done.14.refs_5_
  60.8 1.4 %collective-permute-done.15.refs_6_ = bf16[512,512]{1,0:T(8,128)(2,1)S(1)} collective-permute-done((bf16[512,512]{1,0:T(8,128)(2,1)S(1)}, bf16[512,512]{1,0:T(8,128)(2,1)S(1)}, u32[]{:S(2)}, u32[]{:S(2)}) %collective-permute-start.15) | collective-permute-done | bytes 524320 | tf_op jit(solution)/shard_map/ppermute | solution.py:480
  62.2 1.6 %shard_map.84 = (f32[224,128]{1,0:T(8,128)S(1)}, bf16[224,128]{1,0:T(8,128)(2,1)S(1)}, bf16[224,128]{1,0:T(8,128)(2,1)S(1)}, bf16[224,128]{1,0:T(8,128)(2,1)S(1)}) custom-call(s32[16,16]{1,0:T(8,128)S(1)} %copy-done, s32[1,128]{1,0:T(1,128)S(1)} %get-tuple-element.61.refs_0_.starts_ref, s32[1,128]{1,0:T(1,128)S(1)} %slice_add_fusion.2.refs_1_, ...), custom_call_target="tpu_custom_call" | custom-call | flops 1 | bytes 1 | tf_op jit(solution)/shard_map/pallas_call | solution.py:661
  63.8 0.6 collective-permute-start.16
  64.3 1.0 %collective-permute-start.17 = (bf16[224,128]{1,0:T(8,128)(2,1)S(1)}, bf16[224,128]{1,0:T(8,128)(2,1)S(1)}, u32[]{:S(2)}, u32[]{:S(2)}) collective-permute-start(bf16[224,128]{1,0:T(8,128)(2,1)S(1)} %get-tuple-element.114), channel_id=1, source_target_pairs={{0,16},{1,17},{2,18},{3,19},{4,20},{5,21},{6,22},{7,23},{8,24},{9,... | collective-permute-start | bytes 172040 | tf_op jit(solution)/shard_map/ppermute | solution.py:475
  65.3 0.7 collective-permute-start.18
  66.1 0.0 collective-permute-done.11.b_ref
  66.1 0.6 collective-permute-done.12.c_ref
  66.7 3.1 %shard_map.85 = (bf16[2,64,4096]{2,1,0:T(8,128)(2,1)}, f32[64,1024]{1,0:T(8,128)S(1)}) custom-call(s32[8,128]{1,0:T(8,128)S(1)} %bitcast.5, bf16[256,256]{1,0:T(8,128)(2,1)S(1)} %get-tuple-element.81.basis_ref, bf16[1024,1024]{1,0:T(8,128)(2,1)S(1)} %get-tuple-element.82.order_ref, f32[4096,128]{1,0:T(8,128)S(1)} %get-tuple-element.101.total_ref, ...), custom_call_target="tpu_custom_call" | custom-call | flops 1 | bytes 1 | tf_op jit(solution)/shard_map/pallas_call | solution.py:672
  69.7 0.0 collective-permute-done.16.b_ref
  69.8 2.2 %shard_map.86 = bf16[2,64,4096]{2,1,0:T(8,128)(2,1)} custom-call(s32[16,16]{1,0:T(8,128)S(1)} %copy-done, s32[1,128]{1,0:T(1,128)S(1)} %get-tuple-element.61.refs_0_.starts_ref, s32[8,128]{1,0:T(8,128)S(1)} %bitcast.6, bf16[256,256]{1,0:T(8,128)(2,1)S(1)} %get-tuple-element.81.basis_ref, ...), custom_call_target="tpu_custom_call", output_to_operand_aliasing={{}: (10, {})} | custom-call | flops 1 | bytes 1 | tf_op jit(solution)/shard_map/pallas_call | solution.py:685
  (18 shorter events, 0.1 us)
Async XLA Ops:
  0.0 0.7 copy-start.1
  4.0 2.8 %collective-permute-start = (bf16[256,512]{1,0:T(8,128)(2,1)S(1)}, bf16[256,512]{1,0:T(8,128)(2,1)S(1)}, u32[]{:S(2)}, u32[]{:S(2)}) collective-permute-start(bf16[256,512]{1,0:T(8,128)(2,1)S(1)} %get-tuple-element.63), channel_id=1, source_target_pairs={{0,1},{1,0},{2,3},{3,2},{4,5},{5,4},{6,7},{7,6},{8,9},{9,8},{10,11... | collective-permute-start | bytes 786440 | tf_op jit(solution)/shard_map/ppermute | solution.py:475
  4.1 15.2 %collective-permute-start.3 = (bf16[528,512]{1,0:T(8,128)(2,1)S(1)}, bf16[528,512]{1,0:T(8,128)(2,1)S(1)}, u32[]{:S(2)}, u32[]{:S(2)}) collective-permute-start(bf16[528,512]{1,0:T(8,128)(2,1)S(1)} %get-tuple-element.64), channel_id=1, source_target_pairs={{0,16},{1,17},{2,18},{3,19},{4,20},{5,21},{6,22},{7,23},{8,24},{9,... | collective-permute-start | bytes 1622024 | tf_op jit(solution)/shard_map/ppermute | solution.py:475
  6.8 14.1 %collective-permute-start.2 = (bf16[512,512]{1,0:T(8,128)(2,1)S(1)}, bf16[512,512]{1,0:T(8,128)(2,1)S(1)}, u32[]{:S(2)}, u32[]{:S(2)}) collective-permute-start(bf16[512,512]{1,0:T(8,128)(2,1)S(1)} %shard_map.74.refs_2_), channel_id=1, source_target_pairs={{0,4},{1,5},{2,6},{3,7},{4,12},{5,13},{6,14},{7,15},{8,0},{9,1},{1... | collective-permute-start | bytes 1572872 | tf_op jit(solution)/shard_map/ppermute | solution.py:480
  8.9 21.7 %collective-permute-start.7 = (bf16[512,512]{1,0:T(8,128)(2,1)S(1)}, bf16[512,512]{1,0:T(8,128)(2,1)S(1)}, u32[]{:S(2)}, u32[]{:S(2)}) collective-permute-start(bf16[512,512]{1,0:T(8,128)(2,1)S(1)} %shard_map.75), channel_id=1, source_target_pairs={{0,16},{1,17},{2,18},{3,19},{4,20},{5,21},{6,22},{7,23},{8,24},{9,... | collective-permute-start | bytes 1572872 | tf_op jit(solution)/shard_map/ppermute | solution.py:475
  10.1 22.5 %collective-permute-start.1 = (bf16[512,512]{1,0:T(8,128)(2,1)S(1)}, bf16[512,512]{1,0:T(8,128)(2,1)S(1)}, u32[]{:S(2)}, u32[]{:S(2)}) collective-permute-start(bf16[512,512]{1,0:T(8,128)(2,1)S(1)} %shard_map.74.refs_2_), channel_id=1, source_target_pairs={{0,2},{1,3},{2,0},{3,1},{4,6},{5,7},{6,4},{7,5},{8,10},{9,11},{10,... | collective-permute-start | bytes 1572872 | tf_op jit(solution)/shard_map/ppermute | solution.py:475
  13.7 9.0 %copy-start.3 = (s32[128]{0:T(128)S(1)}, s32[128]{0:T(128)}, u32[]{:S(2)}) copy-start(s32[128]{0:T(128)} %param.10) | copy-start | bytes 1540
  13.7 22.6 %collective-permute-start.5 = (bf16[1040,512]{1,0:T(8,128)(2,1)S(1)}, bf16[1040,512]{1,0:T(8,128)(2,1)S(1)}, u32[]{:S(2)}, u32[]{:S(2)}) collective-permute-start(bf16[1040,512]{1,0:T(8,128)(2,1)S(1)} %get-tuple-element.80), channel_id=1, source_target_pairs={{0,1},{1,0},{2,3},{3,2},{4,5},{5,4},{6,7},{7,6},{8,9},{9,8},{10,11... | collective-permute-start | bytes 3194888 | tf_op jit(solution)/shard_map/ppermute | solution.py:475
  20.9 14.0 %collective-permute-start.4 = (bf16[512,512]{1,0:T(8,128)(2,1)S(1)}, bf16[512,512]{1,0:T(8,128)(2,1)S(1)}, u32[]{:S(2)}, u32[]{:S(2)}) collective-permute-start(bf16[512,512]{1,0:T(8,128)(2,1)S(1)} %collective-permute-done.2.refs_3_), channel_id=1, source_target_pairs={{0,4},{1,5},{2,6},{3,7},{4,12},{5,13},{6,14},{7,15},{8,0},{9,1},{1... | collective-permute-start | bytes 1572872 | tf_op jit(solution)/shard_map/ppermute | solution.py:480
  21.4 11.2 %copy-start = (s32[16,16]{1,0:T(8,128)S(1)}, s32[16,16]{1,0:T(8,128)}, u32[]{:S(2)}) copy-start(s32[16,16]{1,0:T(8,128)} %constant.4.clone.bases_ref) | copy-start | bytes 3076
  25.5 12.1 %collective-permute-start.10 = (bf16[512,512]{1,0:T(8,128)(2,1)S(1)}, bf16[512,512]{1,0:T(8,128)(2,1)S(1)}, u32[]{:S(2)}, u32[]{:S(2)}) collective-permute-start(bf16[512,512]{1,0:T(8,128)(2,1)S(1)} %collective-permute-done.2.refs_3_), channel_id=1, source_target_pairs={{0,2},{1,3},{2,0},{3,1},{4,6},{5,7},{6,4},{7,5},{8,10},{9,11},{10,... | collective-permute-start | bytes 1572872 | tf_op jit(solution)/shard_map/ppermute | solution.py:475
  30.5 20.8 %collective-permute-start.6 = (bf16[784,512]{1,0:T(8,128)(2,1)S(1)}, bf16[784,512]{1,0:T(8,128)(2,1)S(1)}, u32[]{:S(2)}, u32[]{:S(2)}) collective-permute-start(bf16[784,512]{1,0:T(8,128)(2,1)S(1)} %get-tuple-element.85), channel_id=1, source_target_pairs={{0,17},{1,16},{2,19},{3,18},{4,21},{5,20},{6,23},{7,22},{8,25},{9,... | collective-permute-start | bytes 2408456 | tf_op jit(solution)/shard_map/ppermute | solution.py:475
  32.6 24.0 %collective-permute-start.8 = (bf16[256,512]{1,0:T(8,128)(2,1)S(1)}, bf16[256,512]{1,0:T(8,128)(2,1)S(1)}, u32[]{:S(2)}, u32[]{:S(2)}) collective-permute-start(bf16[256,512]{1,0:T(8,128)(2,1)S(1)} %get-tuple-element.86), channel_id=1, source_target_pairs={{0,17},{1,16},{2,19},{3,18},{4,21},{5,20},{6,23},{7,22},{8,25},{9,... | collective-permute-start | bytes 786440 | tf_op jit(solution)/shard_map/ppermute | solution.py:475
  34.9 19.0 %collective-permute-start.9 = (bf16[512,512]{1,0:T(8,128)(2,1)S(1)}, bf16[512,512]{1,0:T(8,128)(2,1)S(1)}, u32[]{:S(2)}, u32[]{:S(2)}) collective-permute-start(bf16[512,512]{1,0:T(8,128)(2,1)S(1)} %collective-permute-done.4.refs_6_), channel_id=1, source_target_pairs={{0,2},{1,3},{2,0},{3,1},{4,6},{5,7},{6,4},{7,5},{8,10},{9,11},{10,... | collective-permute-start | bytes 1572872 | tf_op jit(solution)/shard_map/ppermute | solution.py:475
  36.2 24.6 %collective-permute-start.14 = (bf16[512,512]{1,0:T(8,128)(2,1)S(1)}, bf16[512,512]{1,0:T(8,128)(2,1)S(1)}, u32[]{:S(2)}, u32[]{:S(2)}) collective-permute-start(bf16[512,512]{1,0:T(8,128)(2,1)S(1)} %collective-permute-done.4.refs_6_), channel_id=1, source_target_pairs={{0,4},{1,5},{2,6},{3,7},{4,12},{5,13},{6,14},{7,15},{8,0},{9,1},{1... | collective-permute-start | bytes 1572872 | tf_op jit(solution)/shard_map/ppermute | solution.py:480
  37.6 24.7 %collective-permute-start.15 = (bf16[512,512]{1,0:T(8,128)(2,1)S(1)}, bf16[512,512]{1,0:T(8,128)(2,1)S(1)}, u32[]{:S(2)}, u32[]{:S(2)}) collective-permute-start(bf16[512,512]{1,0:T(8,128)(2,1)S(1)} %collective-permute-done.1.refs_4_), channel_id=1, source_target_pairs={{0,8},{1,9},{2,10},{3,11},{4,0},{5,1},{6,2},{7,3},{8,12},{9,13},{1... | collective-permute-start | bytes 1572872 | tf_op jit(solution)/shard_map/ppermute | solution.py:480
  58.9 7.8 %copy-start.2 = (s32[128,8]{0,1:T(8,128)S(1)}, s32[128,8]{0,1:T(8,128)}, u32[]{:S(2)}) copy-start(s32[128,8]{0,1:T(8,128)} %param.9) | copy-start | bytes 12292
  58.9 6.5 %collective-permute-start.13 = (bf16[512,128]{1,0:T(8,128)(2,1)S(1)}, bf16[512,128]{1,0:T(8,128)(2,1)S(1)}, u32[]{:S(2)}, u32[]{:S(2)}) collective-permute-start(bf16[512,128]{1,0:T(8,128)(2,1)S(1)} %get-tuple-element.104), channel_id=1, source_target_pairs={{0,17},{1,16},{2,19},{3,18},{4,21},{5,20},{6,23},{7,22},{8,25},{9,... | collective-permute-start | bytes 393224 | tf_op jit(solution)/shard_map/ppermute | solution.py:475
  60.3 5.7 %collective-permute-start.11 = (bf16[512,128]{1,0:T(8,128)(2,1)S(1)}, bf16[512,128]{1,0:T(8,128)(2,1)S(1)}, u32[]{:S(2)}, u32[]{:S(2)}) collective-permute-start(bf16[512,128]{1,0:T(8,128)(2,1)S(1)} %get-tuple-element.102), channel_id=1, source_target_pairs={{0,1},{1,0},{2,3},{3,2},{4,5},{5,4},{6,7},{7,6},{8,9},{9,8},{10,11... | collective-permute-start | bytes 393224 | tf_op jit(solution)/shard_map/ppermute | solution.py:475
  60.3 6.3 %collective-permute-start.12 = (bf16[512,128]{1,0:T(8,128)(2,1)S(1)}, bf16[512,128]{1,0:T(8,128)(2,1)S(1)}, u32[]{:S(2)}, u32[]{:S(2)}) collective-permute-start(bf16[512,128]{1,0:T(8,128)(2,1)S(1)} %get-tuple-element.103), channel_id=1, source_target_pairs={{0,16},{1,17},{2,18},{3,19},{4,20},{5,21},{6,22},{7,23},{8,24},{9,... | collective-permute-start | bytes 393224 | tf_op jit(solution)/shard_map/ppermute | solution.py:475
  63.8 6.0 %collective-permute-start.16 = (bf16[224,128]{1,0:T(8,128)(2,1)S(1)}, bf16[224,128]{1,0:T(8,128)(2,1)S(1)}, u32[]{:S(2)}, u32[]{:S(2)}) collective-permute-start(bf16[224,128]{1,0:T(8,128)(2,1)S(1)} %get-tuple-element.113), channel_id=1, source_target_pairs={{0,1},{1,0},{2,3},{3,2},{4,5},{5,4},{6,7},{7,6},{8,9},{9,8},{10,11... | collective-permute-start | bytes 172040 | tf_op jit(solution)/shard_map/ppermute | solution.py:475
  64.3 5.4 %collective-permute-start.17 = (bf16[224,128]{1,0:T(8,128)(2,1)S(1)}, bf16[224,128]{1,0:T(8,128)(2,1)S(1)}, u32[]{:S(2)}, u32[]{:S(2)}) collective-permute-start(bf16[224,128]{1,0:T(8,128)(2,1)S(1)} %get-tuple-element.114), channel_id=1, source_target_pairs={{0,16},{1,17},{2,18},{3,19},{4,20},{5,21},{6,22},{7,23},{8,24},{9,... | collective-permute-start | bytes 172040 | tf_op jit(solution)/shard_map/ppermute | solution.py:475
  65.3 4.4 %collective-permute-start.18 = (bf16[224,128]{1,0:T(8,128)(2,1)S(1)}, bf16[224,128]{1,0:T(8,128)(2,1)S(1)}, u32[]{:S(2)}, u32[]{:S(2)}) collective-permute-start(bf16[224,128]{1,0:T(8,128)(2,1)S(1)} %get-tuple-element.115), channel_id=1, source_target_pairs={{0,17},{1,16},{2,19},{3,18},{4,21},{5,20},{6,23},{7,22},{8,25},{9,... | collective-permute-start | bytes 172040 | tf_op jit(solution)/shard_map/ppermute | solution.py:475

commit v17 on v16

--- a/solution.py
+++ b/solution.py
@@ -657,6 +657,7 @@
         ]
 
     early = returned(sent)
+    held_tokens, *early[:2] = tie(state[0], *early[:2])
     place = places - 2 * CORES
     own_late, *sent = pl.pallas_call(
         functools.partial(late_kernel, rank, pairs, window, place, QUAD),
@@ -666,7 +667,7 @@
         out_specs=[VMEM] * QUAD,
         compiler_params=pltpu.CompilerParams(vmem_limit_bytes=8 * MIB),
         cost_estimate=QUICK,
-    )(bases, *[starts[g] for g in range(QUAD)], in_vmem(state[0]), held[final, 0], held[final, 1])
+    )(bases, *[starts[g] for g in range(QUAD)], in_vmem(held_tokens), held[final, 0], held[final, 1])
     late = returned(sent)
     *early, own_late = tie(*early, own_late)
     out, turned = pl.pallas_call(

time: 73.3 us -> 72.1 us (0.984)
  waiting for transfers between devices: 21 us -> 20.1 us
    ppermute x15, waiting for transfers between devices: 18 us -> 17 us  [swap(): return lax.ppermute(array, BOTH, table)]
where the time goes in v17:
time: 72.1 us; the launch traced here: 71.6 us
  Pallas kernels  29.7 us (41%)
  starting transfers between devices  20.7 us (29%)
  waiting for transfers between devices  20.1 us (28%)
    ppermute x15, waiting for transfers between devices, swap(): return lax.ppermute(array, BOTH, table)  17 us
    ppermute x15, starting transfers between devices, swap(): return lax.ppermute(array, BOTH, table)  15.8 us
    pallas_call x5, Pallas kernels, accumulate(): pl.pallas_call(functools.partial(partial_kernel, rank, pairs, window, [(f...  12.5 us
    ppermute x4, starting transfers between devices, along(): return lax.ppermute(array, 'expert', pairs_of)  4.97 us
    pallas_call x3, Pallas kernels, permuted(): pl.pallas_call(functools.partial(permute_kernel, plan), out_shape=[rows_s...  4.32 us
    pallas_call x1, Pallas kernels, local(): pl.pallas_call(sort_kernel, out_shape=[pltpu.VMEM(out_grads.shape, jnp.bf...  3.26 us
    pallas_call x1, Pallas kernels, local(): pl.pallas_call(functools.partial(blocks_kernel, rank), out_shape=[jax.Sha...  3.09 us
    ppermute x4, waiting for transfers between devices, along(): return lax.ppermute(array, 'expert', pairs_of)  3.02 us
  transfers between devices with their start and end apart: 19, of which 7 were waited for; matrix products, arithmetic and copies ran while one was open for 0% of the time, Pallas kernels for 34%

profile of v17, /device:TPU:1, one launch (start us, length us, event | category | flops | bytes accessed | tf_op | source)
XLA Modules:
  0.0 71.6 jit_solution(1859060720098035561)
XLA Ops:
  0.0 0.7 copy-done.1
  0.7 3.3 %shard_map.73 = (bf16[128,8,2048]{2,1,0:T(8,128)(2,1)S(1)}, bf16[256,512]{1,0:T(8,128)(2,1)S(1)}, bf16[256,512]{1,0:T(8,128)(2,1)S(1)}, s32[1,128]{1,0:T(1,128)S...) custom-call(s32[8,128]{1,0:T(8,128)S(1)} %bitcast.3, ...), custom_call_target="tpu_custom_call" | custom-call | flops 1 | bytes 1 | tf_op jit(solution)/shard_map/pallas_call | solution.py:515
  4.0 0.1 collective-permute-start
  4.1 2.7 %collective-permute-start.3 = (bf16[528,512]{1,0:T(8,128)(2,1)S(1)}, bf16[528,512]{1,0:T(8,128)(2,1)S(1)}, u32[]{:S(2)}, u32[]{:S(2)}) collective-permute-start(bf16[528,512]{1,0:T(8,128)(2,1)S(1)} %get-tuple-element.67), channel_id=1, source_target_pairs={{0,16},{1,17},{2,18},{3,19},{4,20},{5,21},{6,22},{7,23},{8,24},{9,... | collective-permute-start | bytes 1622024 | tf_op jit(solution)/shard_map/ppermute | solution.py:475
  6.7 0.0 collective-permute-done.two_ref
  6.8 1.4 %collective-permute-start.2 = (bf16[512,512]{1,0:T(8,128)(2,1)S(1)}, bf16[512,512]{1,0:T(8,128)(2,1)S(1)}, u32[]{:S(2)}, u32[]{:S(2)}) collective-permute-start(bf16[512,512]{1,0:T(8,128)(2,1)S(1)} %shard_map.74.refs_2_), channel_id=1, source_target_pairs={{0,4},{1,5},{2,6},{3,7},{4,12},{5,13},{6,14},{7,15},{8,0},{9,1},{1... | collective-permute-start | bytes 1572872 | tf_op jit(solution)/shard_map/ppermute | solution.py:480
  8.1 0.7 %shard_map.75 = bf16[512,512]{1,0:T(8,128)(2,1)S(1)} custom-call(bf16[1024,1024]{1,0:T(8,128)(2,1)S(1)} %get-tuple-element.75.order_ref, bf16[16,512]{1,0:T(8,128)(2,1)S(1)} %get-tuple-element.71.head_ref, bf16[128,8,2048]{2,1,0:T(8,128)(2,1)S(1)} %get-tuple-element.72.grads_ref), custom_call_target="tpu_custom_call" | custom-call | flops 1 | bytes 1 | tf_op jit(solution)/shard_map/pallas_call | solution.py:544
  8.9 1.2 %collective-permute-start.7 = (bf16[512,512]{1,0:T(8,128)(2,1)S(1)}, bf16[512,512]{1,0:T(8,128)(2,1)S(1)}, u32[]{:S(2)}, u32[]{:S(2)}) collective-permute-start(bf16[512,512]{1,0:T(8,128)(2,1)S(1)} %shard_map.75), channel_id=1, source_target_pairs={{0,16},{1,17},{2,18},{3,19},{4,20},{5,21},{6,22},{7,23},{8,24},{9,... | collective-permute-start | bytes 1572872 | tf_op jit(solution)/shard_map/ppermute | solution.py:475
  10.1 1.2 %collective-permute-start.1 = (bf16[512,512]{1,0:T(8,128)(2,1)S(1)}, bf16[512,512]{1,0:T(8,128)(2,1)S(1)}, u32[]{:S(2)}, u32[]{:S(2)}) collective-permute-start(bf16[512,512]{1,0:T(8,128)(2,1)S(1)} %shard_map.74.refs_2_), channel_id=1, source_target_pairs={{0,2},{1,3},{2,0},{3,1},{4,6},{5,7},{6,4},{7,5},{8,10},{9,11},{10,... | collective-permute-start | bytes 1572872 | tf_op jit(solution)/shard_map/ppermute | solution.py:475
  11.3 2.3 %shard_map.76 = (bf16[1024,512]{1,0:T(8,128)(2,1)S(1)}, bf16[1040,512]{1,0:T(8,128)(2,1)S(1)}) custom-call(bf16[1024,1024]{1,0:T(8,128)(2,1)S(1)} %get-tuple-element.75.order_ref, bf16[16,512]{1,0:T(8,128)(2,1)S(1)} %get-tuple-element.71.head_ref, bf16[128,8,2048]{2,1,0:T(8,128)(2,1)S(1)} %get-tuple-element.72.grads_ref), custom_call_target="tpu_custom_call" | custom-call | flops 1 | bytes 1 | tf_op jit(solution)/shard_map/pallas_call | solution.py:544
  13.7 0.0 copy-start.3
  13.7 1.3 %collective-permute-start.5 = (bf16[1040,512]{1,0:T(8,128)(2,1)S(1)}, bf16[1040,512]{1,0:T(8,128)(2,1)S(1)}, u32[]{:S(2)}, u32[]{:S(2)}) collective-permute-start(bf16[1040,512]{1,0:T(8,128)(2,1)S(1)} %get-tuple-element.83), channel_id=1, source_target_pairs={{0,1},{1,0},{2,3},{3,2},{4,5},{5,4},{6,7},{7,6},{8,9},{9,8},{10,11... | collective-permute-start | bytes 3194888 | tf_op jit(solution)/shard_map/ppermute | solution.py:475
  15.0 4.3 %collective-permute-done.3.refs_4_ = bf16[528,512]{1,0:T(8,128)(2,1)S(1)} collective-permute-done((bf16[528,512]{1,0:T(8,128)(2,1)S(1)}, bf16[528,512]{1,0:T(8,128)(2,1)S(1)}, u32[]{:S(2)}, u32[]{:S(2)}) %collective-permute-start.3) | collective-permute-done | bytes 540704 | tf_op jit(solution)/shard_map/ppermute | solution.py:475
  19.3 1.6 %collective-permute-done.2.refs_3_ = bf16[512,512]{1,0:T(8,128)(2,1)S(1)} collective-permute-done((bf16[512,512]{1,0:T(8,128)(2,1)S(1)}, bf16[512,512]{1,0:T(8,128)(2,1)S(1)}, u32[]{:S(2)}, u32[]{:S(2)}) %collective-permute-start.2) | collective-permute-done | bytes 524320 | tf_op jit(solution)/shard_map/ppermute | solution.py:480
  20.9 0.5 collective-permute-start.4
  21.4 1.3 %shard_map.77 = (bf16[784,512]{1,0:T(8,128)(2,1)S(1)}, bf16[256,512]{1,0:T(8,128)(2,1)S(1)}) custom-call(bf16[1024,1024]{1,0:T(8,128)(2,1)S(1)} %get-tuple-element.75.order_ref, bf16[16,512]{1,0:T(8,128)(2,1)S(1)} %get-tuple-element.71.head_ref, bf16[128,8,2048]{2,1,0:T(8,128)(2,1)S(1)} %get-tuple-element.72.grads_ref), custom_call_target="tpu_custom_call" | custom-call | flops 1 | bytes 1 | tf_op jit(solution)/shard_map/pallas_call | solution.py:544
  22.7 2.8 %shard_map.78 = (bf16[256,256]{1,0:T(8,128)(2,1)S(1)}, bf16[1024,1024]{1,0:T(8,128)(2,1)S(1)}) custom-call(bf16[128,7168]{1,0:T(8,128)(2,1)} %hidden_ref.1, bf16[64,7168]{1,0:T(8,128)(2,1)} %proj_ref.1, s32[1,128]{1,0:T(1,128)S(1)} %bitcast.7, s32[8,128]{1,0:T(8,128)S(1)} %bitcast.4), custom_call_target="tpu_custom_call" | custom-call | flops 1 | bytes 1 | tf_op jit(solution)/shard_map/pallas_call | solution.py:570
  25.5 1.3 %collective-permute-start.10 = (bf16[512,512]{1,0:T(8,128)(2,1)S(1)}, bf16[512,512]{1,0:T(8,128)(2,1)S(1)}, u32[]{:S(2)}, u32[]{:S(2)}) collective-permute-start(bf16[512,512]{1,0:T(8,128)(2,1)S(1)} %collective-permute-done.2.refs_3_), channel_id=1, source_target_pairs={{0,2},{1,3},{2,0},{3,1},{4,6},{5,7},{6,4},{7,5},{8,10},{9,11},{10,... | collective-permute-start | bytes 1572872 | tf_op jit(solution)/shard_map/ppermute | solution.py:475
  26.8 3.7 %collective-permute-done.7.refs_5_ = bf16[512,512]{1,0:T(8,128)(2,1)S(1)} collective-permute-done((bf16[512,512]{1,0:T(8,128)(2,1)S(1)}, bf16[512,512]{1,0:T(8,128)(2,1)S(1)}, u32[]{:S(2)}, u32[]{:S(2)}) %collective-permute-start.7) | collective-permute-done | bytes 524320 | tf_op jit(solution)/shard_map/ppermute | solution.py:475
  30.5 2.0 %collective-permute-start.6 = (bf16[784,512]{1,0:T(8,128)(2,1)S(1)}, bf16[784,512]{1,0:T(8,128)(2,1)S(1)}, u32[]{:S(2)}, u32[]{:S(2)}) collective-permute-start(bf16[784,512]{1,0:T(8,128)(2,1)S(1)} %get-tuple-element.88), channel_id=1, source_target_pairs={{0,17},{1,16},{2,19},{3,18},{4,21},{5,20},{6,23},{7,22},{8,25},{9,... | collective-permute-start | bytes 2408456 | tf_op jit(solution)/shard_map/ppermute | solution.py:475
  32.6 0.0 collective-permute-start.8
  32.6 2.3 %shard_map.79 = (bf16[4096,512]{1,0:T(8,128)(2,1)S(1)}, bf16[16,256,512]{2,1,0:T(8,128)(2,1)S(1)}, f32[4096,128]{1,0:T(8,128)S(1)}) custom-call(s32[16,16]{1,0:T(8,128)S(1)} %copy-done, s32[1,128]{1,0:T(1,128)S(1)} %get-tuple-element.64.refs_0_.starts_ref, bf16[1024,512]{1,0:T(8,128)(2,1)S(1)} %get-tuple-element.74.refs_1_, ...), custom_call_target="tpu_custom_call" | custom-call | flops 1000000000 | bytes 1 | tf_op jit(solution)/shard_map/pallas_call | solution.py:287
  34.9 0.0 collective-permute-done.4.refs_6_
  34.9 1.3 %collective-permute-start.9 = (bf16[512,512]{1,0:T(8,128)(2,1)S(1)}, bf16[512,512]{1,0:T(8,128)(2,1)S(1)}, u32[]{:S(2)}, u32[]{:S(2)}) collective-permute-start(bf16[512,512]{1,0:T(8,128)(2,1)S(1)} %collective-permute-done.4.refs_6_), channel_id=1, source_target_pairs={{0,2},{1,3},{2,0},{3,1},{4,6},{5,7},{6,4},{7,5},{8,10},{9,11},{10,... | collective-permute-start | bytes 1572872 | tf_op jit(solution)/shard_map/ppermute | solution.py:475
  36.2 1.3 %collective-permute-start.14 = (bf16[512,512]{1,0:T(8,128)(2,1)S(1)}, bf16[512,512]{1,0:T(8,128)(2,1)S(1)}, u32[]{:S(2)}, u32[]{:S(2)}) collective-permute-start(bf16[512,512]{1,0:T(8,128)(2,1)S(1)} %collective-permute-done.4.refs_6_), channel_id=1, source_target_pairs={{0,4},{1,5},{2,6},{3,7},{4,12},{5,13},{6,14},{7,15},{8,0},{9,1},{1... | collective-permute-start | bytes 1572872 | tf_op jit(solution)/shard_map/ppermute | solution.py:480
  37.6 0.0 collective-permute-done.10.refs_7_
  37.6 1.8 %collective-permute-start.15 = (bf16[512,512]{1,0:T(8,128)(2,1)S(1)}, bf16[512,512]{1,0:T(8,128)(2,1)S(1)}, u32[]{:S(2)}, u32[]{:S(2)}) collective-permute-start(bf16[512,512]{1,0:T(8,128)(2,1)S(1)} %collective-permute-done.1.refs_4_), channel_id=1, source_target_pairs={{0,8},{1,9},{2,10},{3,11},{4,0},{5,1},{6,2},{7,3},{8,12},{9,13},{1... | collective-permute-start | bytes 1572872 | tf_op jit(solution)/shard_map/ppermute | solution.py:480
  39.4 3.5 %shard_map.80 = (bf16[4096,512]{1,0:T(8,128)(2,1)S(1)}, bf16[16,256,512]{2,1,0:T(8,128)(2,1)S(1)}, f32[4096,128]{1,0:T(8,128)S(1)}) custom-call(s32[16,16]{1,0:T(8,128)S(1)} %copy-done, s32[1,128]{1,0:T(1,128)S(1)} %get-tuple-element.64.refs_0_.starts_ref, ...), custom_call_target="tpu_custom_call", output_to_operand_aliasing={{0}: (9, {}), {1}: (10, {}), {2}: (11, {})} | custom-call | flops 1000000000 | bytes 1 | tf_op jit(solution)/shard_map/pallas_call | solution.py:287
  42.9 8.4 %collective-permute-done.6.refs_4_ = bf16[784,512]{1,0:T(8,128)(2,1)S(1)} collective-permute-done((bf16[784,512]{1,0:T(8,128)(2,1)S(1)}, bf16[784,512]{1,0:T(8,128)(2,1)S(1)}, u32[]{:S(2)}, u32[]{:S(2)}) %collective-permute-start.6) | collective-permute-done | bytes 802848 | tf_op jit(solution)/shard_map/ppermute | solution.py:475
  51.3 2.9 %shard_map.81 = (bf16[4096,512]{1,0:T(8,128)(2,1)S(1)}, bf16[16,256,512]{2,1,0:T(8,128)(2,1)S(1)}, f32[4096,128]{1,0:T(8,128)S(1)}) custom-call(s32[16,16]{1,0:T(8,128)S(1)} %copy-done, s32[1,128]{1,0:T(1,128)S(1)} %get-tuple-element.64.refs_0_.starts_ref, ...), custom_call_target="tpu_custom_call", output_to_operand_aliasing={{0}: (6, {}), {1}: (7, {}), {2}: (8, {})} | custom-call | flops 1 | bytes 1 | tf_op jit(solution)/shard_map/pallas_call | solution.py:287
  54.2 0.0 collective-permute-done.9.refs_4_
  54.2 1.7 %shard_map.82 = (bf16[4096,512]{1,0:T(8,128)(2,1)S(1)}, bf16[16,256,512]{2,1,0:T(8,128)(2,1)S(1)}, f32[4096,128]{1,0:T(8,128)S(1)}, bf16[512,128]{1,0:T(8,128)(2,1)S(1)}, bf16[512,128]{1,0:T(8,128)(2,1)S(1)}) custom-call(s32[16,16]{1,0:T(8,128)S(1)} %copy-done, ...), custom_call_target="tpu_custom_call", output_to_operand_aliasing={{0}: (6, {}), {1}: (7, {}), {2}: (8, {})} | custom-call | flops 1 | bytes 1 | tf_op jit(solution)/shard_map/pallas_call | solution.py:287
  55.9 0.1 collective-permute-start.11
  56.0 1.6 %collective-permute-start.12 = (bf16[512,128]{1,0:T(8,128)(2,1)S(1)}, bf16[512,128]{1,0:T(8,128)(2,1)S(1)}, u32[]{:S(2)}, u32[]{:S(2)}) collective-permute-start(bf16[512,128]{1,0:T(8,128)(2,1)S(1)} %get-tuple-element.107), channel_id=1, source_target_pairs={{0,16},{1,17},{2,18},{3,19},{4,20},{5,21},{6,22},{7,23},{8,24},{9,... | collective-permute-start | bytes 393224 | tf_op jit(solution)/shard_map/ppermute | solution.py:475
  57.6 0.0 collective-permute-done.8.refs_4_
  57.6 2.0 %shard_map.83 = (bf16[4096,512]{1,0:T(8,128)(2,1)S(1)}, bf16[16,256,512]{2,1,0:T(8,128)(2,1)S(1)}, f32[4096,128]{1,0:T(8,128)S(1)}, bf16[512,128]{1,0:T(8,128)(2,1)S(1)}) custom-call(s32[16,16]{1,0:T(8,128)S(1)} %copy-done, s32[1,128]{1,0:T(1,128)S(1)} %get-tuple-element.64.refs_0_.starts_ref, ...), custom_call_target="tpu_custom_call", output_to_operand_aliasing={{0}: (6, {}), {1}: (7, {}), {2}: (8, {})} | custom-call | flops 1000000000 | bytes 1 | tf_op jit(solution)/shard_map/pallas_call | solution.py:287
  59.6 0.0 copy-start.2
  59.6 0.7 collective-permute-start.13
  60.3 0.0 collective-permute-done.11.b_ref
  60.3 0.5 collective-permute-done.12.c_ref
  60.8 1.4 %collective-permute-done.15.refs_6_ = bf16[512,512]{1,0:T(8,128)(2,1)S(1)} collective-permute-done((bf16[512,512]{1,0:T(8,128)(2,1)S(1)}, bf16[512,512]{1,0:T(8,128)(2,1)S(1)}, u32[]{:S(2)}, u32[]{:S(2)}) %collective-permute-start.15) | collective-permute-done | bytes 524320 | tf_op jit(solution)/shard_map/ppermute | solution.py:480
  62.2 1.6 %shard_map.84 = (f32[224,128]{1,0:T(8,128)S(1)}, bf16[224,128]{1,0:T(8,128)(2,1)S(1)}, bf16[224,128]{1,0:T(8,128)(2,1)S(1)}, bf16[224,128]{1,0:T(8,128)(2,1)S(1)}) custom-call(s32[16,16]{1,0:T(8,128)S(1)} %copy-done, s32[1,128]{1,0:T(1,128)S(1)} %get-tuple-element.64.refs_0_.starts_ref, s32[1,128]{1,0:T(1,128)S(1)} %slice_add_fusion.2.refs_1_, ...), custom_call_target="tpu_custom_call" | custom-call | flops 1 | bytes 1 | tf_op jit(solution)/shard_map/pallas_call | solution.py:662
  63.8 0.6 collective-permute-start.16
  64.3 1.0 %collective-permute-start.17 = (bf16[224,128]{1,0:T(8,128)(2,1)S(1)}, bf16[224,128]{1,0:T(8,128)(2,1)S(1)}, u32[]{:S(2)}, u32[]{:S(2)}) collective-permute-start(bf16[224,128]{1,0:T(8,128)(2,1)S(1)} %get-tuple-element.120), channel_id=1, source_target_pairs={{0,16},{1,17},{2,18},{3,19},{4,20},{5,21},{6,22},{7,23},{8,24},{9,... | collective-permute-start | bytes 172040 | tf_op jit(solution)/shard_map/ppermute | solution.py:475
  65.3 0.7 collective-permute-start.18
  66.1 3.1 %shard_map.85 = (bf16[2,64,4096]{2,1,0:T(8,128)(2,1)}, f32[64,1024]{1,0:T(8,128)S(1)}) custom-call(s32[8,128]{1,0:T(8,128)S(1)} %bitcast.5, bf16[256,256]{1,0:T(8,128)(2,1)S(1)} %get-tuple-element.84.basis_ref, bf16[1024,1024]{1,0:T(8,128)(2,1)S(1)} %get-tuple-element.85.order_ref, f32[4096,128]{1,0:T(8,128)S(1)} %get-tuple-element.104.total_ref, ...), custom_call_target="tpu_custom_call" | custom-call | flops 1 | bytes 1 | tf_op jit(solution)/shard_map/pallas_call | solution.py:673
  69.2 0.1 collective-permute-done.18.d_ref
  69.2 2.2 %shard_map.86 = bf16[2,64,4096]{2,1,0:T(8,128)(2,1)} custom-call(s32[16,16]{1,0:T(8,128)S(1)} %copy-done, s32[1,128]{1,0:T(1,128)S(1)} %get-tuple-element.64.refs_0_.starts_ref, s32[8,128]{1,0:T(8,128)S(1)} %bitcast.6, bf16[256,256]{1,0:T(8,128)(2,1)S(1)} %get-tuple-element.84.basis_ref, ...), custom_call_target="tpu_custom_call", output_to_operand_aliasing={{}: (10, {})} | custom-call | flops 1 | bytes 1 | tf_op jit(solution)/shard_map/pallas_call | solution.py:686
  (18 shorter events, 0.1 us)
Async XLA Ops:
  0.0 0.7 copy-start.1
  4.0 2.8 %collective-permute-start = (bf16[256,512]{1,0:T(8,128)(2,1)S(1)}, bf16[256,512]{1,0:T(8,128)(2,1)S(1)}, u32[]{:S(2)}, u32[]{:S(2)}) collective-permute-start(bf16[256,512]{1,0:T(8,128)(2,1)S(1)} %get-tuple-element.66), channel_id=1, source_target_pairs={{0,1},{1,0},{2,3},{3,2},{4,5},{5,4},{6,7},{7,6},{8,9},{9,8},{10,11... | collective-permute-start | bytes 786440 | tf_op jit(solution)/shard_map/ppermute | solution.py:475
  4.1 15.2 %collective-permute-start.3 = (bf16[528,512]{1,0:T(8,128)(2,1)S(1)}, bf16[528,512]{1,0:T(8,128)(2,1)S(1)}, u32[]{:S(2)}, u32[]{:S(2)}) collective-permute-start(bf16[528,512]{1,0:T(8,128)(2,1)S(1)} %get-tuple-element.67), channel_id=1, source_target_pairs={{0,16},{1,17},{2,18},{3,19},{4,20},{5,21},{6,22},{7,23},{8,24},{9,... | collective-permute-start | bytes 1622024 | tf_op jit(solution)/shard_map/ppermute | solution.py:475
  6.8 14.1 %collective-permute-start.2 = (bf16[512,512]{1,0:T(8,128)(2,1)S(1)}, bf16[512,512]{1,0:T(8,128)(2,1)S(1)}, u32[]{:S(2)}, u32[]{:S(2)}) collective-permute-start(bf16[512,512]{1,0:T(8,128)(2,1)S(1)} %shard_map.74.refs_2_), channel_id=1, source_target_pairs={{0,4},{1,5},{2,6},{3,7},{4,12},{5,13},{6,14},{7,15},{8,0},{9,1},{1... | collective-permute-start | bytes 1572872 | tf_op jit(solution)/shard_map/ppermute | solution.py:480
  8.9 21.7 %collective-permute-start.7 = (bf16[512,512]{1,0:T(8,128)(2,1)S(1)}, bf16[512,512]{1,0:T(8,128)(2,1)S(1)}, u32[]{:S(2)}, u32[]{:S(2)}) collective-permute-start(bf16[512,512]{1,0:T(8,128)(2,1)S(1)} %shard_map.75), channel_id=1, source_target_pairs={{0,16},{1,17},{2,18},{3,19},{4,20},{5,21},{6,22},{7,23},{8,24},{9,... | collective-permute-start | bytes 1572872 | tf_op jit(solution)/shard_map/ppermute | solution.py:475
  10.1 22.5 %collective-permute-start.1 = (bf16[512,512]{1,0:T(8,128)(2,1)S(1)}, bf16[512,512]{1,0:T(8,128)(2,1)S(1)}, u32[]{:S(2)}, u32[]{:S(2)}) collective-permute-start(bf16[512,512]{1,0:T(8,128)(2,1)S(1)} %shard_map.74.refs_2_), channel_id=1, source_target_pairs={{0,2},{1,3},{2,0},{3,1},{4,6},{5,7},{6,4},{7,5},{8,10},{9,11},{10,... | collective-permute-start | bytes 1572872 | tf_op jit(solution)/shard_map/ppermute | solution.py:475
  13.7 9.0 %copy-start.3 = (s32[128]{0:T(128)S(1)}, s32[128]{0:T(128)}, u32[]{:S(2)}) copy-start(s32[128]{0:T(128)} %param.10) | copy-start | bytes 1540
  13.7 22.6 %collective-permute-start.5 = (bf16[1040,512]{1,0:T(8,128)(2,1)S(1)}, bf16[1040,512]{1,0:T(8,128)(2,1)S(1)}, u32[]{:S(2)}, u32[]{:S(2)}) collective-permute-start(bf16[1040,512]{1,0:T(8,128)(2,1)S(1)} %get-tuple-element.83), channel_id=1, source_target_pairs={{0,1},{1,0},{2,3},{3,2},{4,5},{5,4},{6,7},{7,6},{8,9},{9,8},{10,11... | collective-permute-start | bytes 3194888 | tf_op jit(solution)/shard_map/ppermute | solution.py:475
  20.9 14.0 %collective-permute-start.4 = (bf16[512,512]{1,0:T(8,128)(2,1)S(1)}, bf16[512,512]{1,0:T(8,128)(2,1)S(1)}, u32[]{:S(2)}, u32[]{:S(2)}) collective-permute-start(bf16[512,512]{1,0:T(8,128)(2,1)S(1)} %collective-permute-done.2.refs_3_), channel_id=1, source_target_pairs={{0,4},{1,5},{2,6},{3,7},{4,12},{5,13},{6,14},{7,15},{8,0},{9,1},{1... | collective-permute-start | bytes 1572872 | tf_op jit(solution)/shard_map/ppermute | solution.py:480
  21.4 11.2 %copy-start = (s32[16,16]{1,0:T(8,128)S(1)}, s32[16,16]{1,0:T(8,128)}, u32[]{:S(2)}) copy-start(s32[16,16]{1,0:T(8,128)} %constant.4.clone.bases_ref) | copy-start | bytes 3076
  25.5 12.1 %collective-permute-start.10 = (bf16[512,512]{1,0:T(8,128)(2,1)S(1)}, bf16[512,512]{1,0:T(8,128)(2,1)S(1)}, u32[]{:S(2)}, u32[]{:S(2)}) collective-permute-start(bf16[512,512]{1,0:T(8,128)(2,1)S(1)} %collective-permute-done.2.refs_3_), channel_id=1, source_target_pairs={{0,2},{1,3},{2,0},{3,1},{4,6},{5,7},{6,4},{7,5},{8,10},{9,11},{10,... | collective-permute-start | bytes 1572872 | tf_op jit(solution)/shard_map/ppermute | solution.py:475
  30.5 20.8 %collective-permute-start.6 = (bf16[784,512]{1,0:T(8,128)(2,1)S(1)}, bf16[784,512]{1,0:T(8,128)(2,1)S(1)}, u32[]{:S(2)}, u32[]{:S(2)}) collective-permute-start(bf16[784,512]{1,0:T(8,128)(2,1)S(1)} %get-tuple-element.88), channel_id=1, source_target_pairs={{0,17},{1,16},{2,19},{3,18},{4,21},{5,20},{6,23},{7,22},{8,25},{9,... | collective-permute-start | bytes 2408456 | tf_op jit(solution)/shard_map/ppermute | solution.py:475
  32.6 25.0 %collective-permute-start.8 = (bf16[256,512]{1,0:T(8,128)(2,1)S(1)}, bf16[256,512]{1,0:T(8,128)(2,1)S(1)}, u32[]{:S(2)}, u32[]{:S(2)}) collective-permute-start(bf16[256,512]{1,0:T(8,128)(2,1)S(1)} %get-tuple-element.89), channel_id=1, source_target_pairs={{0,17},{1,16},{2,19},{3,18},{4,21},{5,20},{6,23},{7,22},{8,25},{9,... | collective-permute-start | bytes 786440 | tf_op jit(solution)/shard_map/ppermute | solution.py:475
  34.9 19.3 %collective-permute-start.9 = (bf16[512,512]{1,0:T(8,128)(2,1)S(1)}, bf16[512,512]{1,0:T(8,128)(2,1)S(1)}, u32[]{:S(2)}, u32[]{:S(2)}) collective-permute-start(bf16[512,512]{1,0:T(8,128)(2,1)S(1)} %collective-permute-done.4.refs_6_), channel_id=1, source_target_pairs={{0,2},{1,3},{2,0},{3,1},{4,6},{5,7},{6,4},{7,5},{8,10},{9,11},{10,... | collective-permute-start | bytes 1572872 | tf_op jit(solution)/shard_map/ppermute | solution.py:475
  36.2 24.6 %collective-permute-start.14 = (bf16[512,512]{1,0:T(8,128)(2,1)S(1)}, bf16[512,512]{1,0:T(8,128)(2,1)S(1)}, u32[]{:S(2)}, u32[]{:S(2)}) collective-permute-start(bf16[512,512]{1,0:T(8,128)(2,1)S(1)} %collective-permute-done.4.refs_6_), channel_id=1, source_target_pairs={{0,4},{1,5},{2,6},{3,7},{4,12},{5,13},{6,14},{7,15},{8,0},{9,1},{1... | collective-permute-start | bytes 1572872 | tf_op jit(solution)/shard_map/ppermute | solution.py:480
  37.6 24.7 %collective-permute-start.15 = (bf16[512,512]{1,0:T(8,128)(2,1)S(1)}, bf16[512,512]{1,0:T(8,128)(2,1)S(1)}, u32[]{:S(2)}, u32[]{:S(2)}) collective-permute-start(bf16[512,512]{1,0:T(8,128)(2,1)S(1)} %collective-permute-done.1.refs_4_), channel_id=1, source_target_pairs={{0,8},{1,9},{2,10},{3,11},{4,0},{5,1},{6,2},{7,3},{8,12},{9,13},{1... | collective-permute-start | bytes 1572872 | tf_op jit(solution)/shard_map/ppermute | solution.py:480
  55.9 4.4 %collective-permute-start.11 = (bf16[512,128]{1,0:T(8,128)(2,1)S(1)}, bf16[512,128]{1,0:T(8,128)(2,1)S(1)}, u32[]{:S(2)}, u32[]{:S(2)}) collective-permute-start(bf16[512,128]{1,0:T(8,128)(2,1)S(1)} %get-tuple-element.106), channel_id=1, source_target_pairs={{0,1},{1,0},{2,3},{3,2},{4,5},{5,4},{6,7},{7,6},{8,9},{9,8},{10,11... | collective-permute-start | bytes 393224 | tf_op jit(solution)/shard_map/ppermute | solution.py:475
  56.0 4.8 %collective-permute-start.12 = (bf16[512,128]{1,0:T(8,128)(2,1)S(1)}, bf16[512,128]{1,0:T(8,128)(2,1)S(1)}, u32[]{:S(2)}, u32[]{:S(2)}) collective-permute-start(bf16[512,128]{1,0:T(8,128)(2,1)S(1)} %get-tuple-element.107), channel_id=1, source_target_pairs={{0,16},{1,17},{2,18},{3,19},{4,20},{5,21},{6,22},{7,23},{8,24},{9,... | collective-permute-start | bytes 393224 | tf_op jit(solution)/shard_map/ppermute | solution.py:475
  59.6 6.4 %copy-start.2 = (s32[128,8]{0,1:T(8,128)S(1)}, s32[128,8]{0,1:T(8,128)}, u32[]{:S(2)}) copy-start(s32[128,8]{0,1:T(8,128)} %param.9) | copy-start | bytes 12292
  59.6 6.4 %collective-permute-start.13 = (bf16[512,128]{1,0:T(8,128)(2,1)S(1)}, bf16[512,128]{1,0:T(8,128)(2,1)S(1)}, u32[]{:S(2)}, u32[]{:S(2)}) collective-permute-start(bf16[512,128]{1,0:T(8,128)(2,1)S(1)} %get-tuple-element.110), channel_id=1, source_target_pairs={{0,17},{1,16},{2,19},{3,18},{4,21},{5,20},{6,23},{7,22},{8,25},{9,... | collective-permute-start | bytes 393224 | tf_op jit(solution)/shard_map/ppermute | solution.py:475
  63.8 5.4 %collective-permute-start.16 = (bf16[224,128]{1,0:T(8,128)(2,1)S(1)}, bf16[224,128]{1,0:T(8,128)(2,1)S(1)}, u32[]{:S(2)}, u32[]{:S(2)}) collective-permute-start(bf16[224,128]{1,0:T(8,128)(2,1)S(1)} %get-tuple-element.119), channel_id=1, source_target_pairs={{0,1},{1,0},{2,3},{3,2},{4,5},{5,4},{6,7},{7,6},{8,9},{9,8},{10,11... | collective-permute-start | bytes 172040 | tf_op jit(solution)/shard_map/ppermute | solution.py:475
  64.3 4.8 %collective-permute-start.17 = (bf16[224,128]{1,0:T(8,128)(2,1)S(1)}, bf16[224,128]{1,0:T(8,128)(2,1)S(1)}, u32[]{:S(2)}, u32[]{:S(2)}) collective-permute-start(bf16[224,128]{1,0:T(8,128)(2,1)S(1)} %get-tuple-element.120), channel_id=1, source_target_pairs={{0,16},{1,17},{2,18},{3,19},{4,20},{5,21},{6,22},{7,23},{8,24},{9,... | collective-permute-start | bytes 172040 | tf_op jit(solution)/shard_map/ppermute | solution.py:475
  65.3 3.9 %collective-permute-start.18 = (bf16[224,128]{1,0:T(8,128)(2,1)S(1)}, bf16[224,128]{1,0:T(8,128)(2,1)S(1)}, u32[]{:S(2)}, u32[]{:S(2)}) collective-permute-start(bf16[224,128]{1,0:T(8,128)(2,1)S(1)} %get-tuple-element.121), channel_id=1, source_target_pairs={{0,17},{1,16},{2,19},{3,18},{4,21},{5,20},{6,23},{7,22},{8,25},{9,... | collective-permute-start | bytes 172040 | tf_op jit(solution)/shard_map/ppermute | solution.py:475

commit v18 on v17

--- a/solution.py
+++ b/solution.py
@@ -639,7 +639,8 @@
     back_unit, basis, from_core = tie(held[0, 1], basis, from_core)
     held[final, 1] = along(back_unit, before)
     held[final, 0] = along(held[near], following)
-    held[final - 1, 1] = swap(held[near], 0, CORES)
+    crossing, from_core = tie(held[near], from_core)
+    held[final - 1, 1] = swap(crossing, 0, CORES)
     last_piece, side_pieces[1] = tie(last_piece, side_pieces[1])
     diagonal_pieces.append(swap(last_piece, 1, 1))
     work(

time: 72.1 us -> 71.8 us (level)
  waiting for transfers between devices: 20.1 us -> 19.1 us
    ppermute x4, waiting for transfers between devices: 3.02 us -> 1.95 us  [along(): return lax.ppermute(array, 'expert', pairs_of)]
where the time goes in v18:
time: 71.8 us; the launch traced here: 71.2 us
  Pallas kernels  29.7 us (41%)
  starting transfers between devices  21.3 us (30%)
  waiting for transfers between devices  19.1 us (27%)
    ppermute x15, waiting for transfers between devices, swap(): return lax.ppermute(array, BOTH, table)  17.1 us
    ppermute x15, starting transfers between devices, swap(): return lax.ppermute(array, BOTH, table)  16.3 us
    pallas_call x5, Pallas kernels, accumulate(): pl.pallas_call(functools.partial(partial_kernel, rank, pairs, window, [(f...  12.5 us
    ppermute x4, starting transfers between devices, along(): return lax.ppermute(array, 'expert', pairs_of)  5.02 us
    pallas_call x3, Pallas kernels, permuted(): pl.pallas_call(functools.partial(permute_kernel, plan), out_shape=[rows_s...  4.32 us
    pallas_call x1, Pallas kernels, local(): pl.pallas_call(sort_kernel, out_shape=[pltpu.VMEM(out_grads.shape, jnp.bf...  3.26 us
    pallas_call x1, Pallas kernels, local(): pl.pallas_call(functools.partial(blocks_kernel, rank), out_shape=[jax.Sha...  3.09 us
    pallas_call x1, Pallas kernels, local(): pl.pallas_call(basis_kernel, out_shape=[pltpu.VMEM((2 * tokens, SEG_DEV *...  2.79 us
  transfers between devices with their start and end apart: 19, of which 7 were waited for; matrix products, arithmetic and copies ran while one was open for 0% of the time, Pallas kernels for 34%

profile of v18, /device:TPU:1, one launch (start us, length us, event | category | flops | bytes accessed | tf_op | source)
XLA Modules:
  0.0 71.2 jit_solution(2642470446470859261)
XLA Ops:
  0.0 0.7 copy-done.1
  0.7 3.3 %shard_map.73 = (bf16[128,8,2048]{2,1,0:T(8,128)(2,1)S(1)}, bf16[256,512]{1,0:T(8,128)(2,1)S(1)}, bf16[256,512]{1,0:T(8,128)(2,1)S(1)}, s32[1,128]{1,0:T(1,128)S...) custom-call(s32[8,128]{1,0:T(8,128)S(1)} %bitcast.3, ...), custom_call_target="tpu_custom_call" | custom-call | flops 1 | bytes 1 | tf_op jit(solution)/shard_map/pallas_call | solution.py:515
  4.0 0.1 collective-permute-start
  4.1 2.7 %collective-permute-start.3 = (bf16[528,512]{1,0:T(8,128)(2,1)S(1)}, bf16[528,512]{1,0:T(8,128)(2,1)S(1)}, u32[]{:S(2)}, u32[]{:S(2)}) collective-permute-start(bf16[528,512]{1,0:T(8,128)(2,1)S(1)} %get-tuple-element.69), channel_id=1, source_target_pairs={{0,16},{1,17},{2,18},{3,19},{4,20},{5,21},{6,22},{7,23},{8,24},{9,... | collective-permute-start | bytes 1622024 | tf_op jit(solution)/shard_map/ppermute | solution.py:475
  6.8 1.4 %collective-permute-start.2 = (bf16[512,512]{1,0:T(8,128)(2,1)S(1)}, bf16[512,512]{1,0:T(8,128)(2,1)S(1)}, u32[]{:S(2)}, u32[]{:S(2)}) collective-permute-start(bf16[512,512]{1,0:T(8,128)(2,1)S(1)} %shard_map.74.refs_2_), channel_id=1, source_target_pairs={{0,4},{1,5},{2,6},{3,7},{4,12},{5,13},{6,14},{7,15},{8,0},{9,1},{1... | collective-permute-start | bytes 1572872 | tf_op jit(solution)/shard_map/ppermute | solution.py:480
  8.1 0.7 %shard_map.75 = bf16[512,512]{1,0:T(8,128)(2,1)S(1)} custom-call(bf16[1024,1024]{1,0:T(8,128)(2,1)S(1)} %get-tuple-element.77.order_ref, bf16[16,512]{1,0:T(8,128)(2,1)S(1)} %get-tuple-element.73.head_ref, bf16[128,8,2048]{2,1,0:T(8,128)(2,1)S(1)} %get-tuple-element.74.grads_ref), custom_call_target="tpu_custom_call" | custom-call | flops 1 | bytes 1 | tf_op jit(solution)/shard_map/pallas_call | solution.py:544
  8.9 1.2 %collective-permute-start.7 = (bf16[512,512]{1,0:T(8,128)(2,1)S(1)}, bf16[512,512]{1,0:T(8,128)(2,1)S(1)}, u32[]{:S(2)}, u32[]{:S(2)}) collective-permute-start(bf16[512,512]{1,0:T(8,128)(2,1)S(1)} %shard_map.75), channel_id=1, source_target_pairs={{0,16},{1,17},{2,18},{3,19},{4,20},{5,21},{6,22},{7,23},{8,24},{9,... | collective-permute-start | bytes 1572872 | tf_op jit(solution)/shard_map/ppermute | solution.py:475
  10.1 1.2 %collective-permute-start.1 = (bf16[512,512]{1,0:T(8,128)(2,1)S(1)}, bf16[512,512]{1,0:T(8,128)(2,1)S(1)}, u32[]{:S(2)}, u32[]{:S(2)}) collective-permute-start(bf16[512,512]{1,0:T(8,128)(2,1)S(1)} %shard_map.74.refs_2_), channel_id=1, source_target_pairs={{0,2},{1,3},{2,0},{3,1},{4,6},{5,7},{6,4},{7,5},{8,10},{9,11},{10,... | collective-permute-start | bytes 1572872 | tf_op jit(solution)/shard_map/ppermute | solution.py:475
  11.3 2.3 %shard_map.76 = (bf16[1024,512]{1,0:T(8,128)(2,1)S(1)}, bf16[1040,512]{1,0:T(8,128)(2,1)S(1)}) custom-call(bf16[1024,1024]{1,0:T(8,128)(2,1)S(1)} %get-tuple-element.77.order_ref, bf16[16,512]{1,0:T(8,128)(2,1)S(1)} %get-tuple-element.73.head_ref, bf16[128,8,2048]{2,1,0:T(8,128)(2,1)S(1)} %get-tuple-element.74.grads_ref), custom_call_target="tpu_custom_call" | custom-call | flops 1 | bytes 1 | tf_op jit(solution)/shard_map/pallas_call | solution.py:544
  13.7 0.0 copy-start.3
  13.7 1.3 %collective-permute-start.5 = (bf16[1040,512]{1,0:T(8,128)(2,1)S(1)}, bf16[1040,512]{1,0:T(8,128)(2,1)S(1)}, u32[]{:S(2)}, u32[]{:S(2)}) collective-permute-start(bf16[1040,512]{1,0:T(8,128)(2,1)S(1)} %get-tuple-element.85), channel_id=1, source_target_pairs={{0,1},{1,0},{2,3},{3,2},{4,5},{5,4},{6,7},{7,6},{8,9},{9,8},{10,11... | collective-permute-start | bytes 3194888 | tf_op jit(solution)/shard_map/ppermute | solution.py:475
  15.0 4.3 %collective-permute-done.3.refs_4_ = bf16[528,512]{1,0:T(8,128)(2,1)S(1)} collective-permute-done((bf16[528,512]{1,0:T(8,128)(2,1)S(1)}, bf16[528,512]{1,0:T(8,128)(2,1)S(1)}, u32[]{:S(2)}, u32[]{:S(2)}) %collective-permute-start.3) | collective-permute-done | bytes 540704 | tf_op jit(solution)/shard_map/ppermute | solution.py:475
  19.3 1.6 %collective-permute-done.2.refs_3_ = bf16[512,512]{1,0:T(8,128)(2,1)S(1)} collective-permute-done((bf16[512,512]{1,0:T(8,128)(2,1)S(1)}, bf16[512,512]{1,0:T(8,128)(2,1)S(1)}, u32[]{:S(2)}, u32[]{:S(2)}) %collective-permute-start.2) | collective-permute-done | bytes 524320 | tf_op jit(solution)/shard_map/ppermute | solution.py:480
  20.9 0.5 collective-permute-start.4
  21.4 1.3 %shard_map.77 = (bf16[784,512]{1,0:T(8,128)(2,1)S(1)}, bf16[256,512]{1,0:T(8,128)(2,1)S(1)}) custom-call(bf16[1024,1024]{1,0:T(8,128)(2,1)S(1)} %get-tuple-element.77.order_ref, bf16[16,512]{1,0:T(8,128)(2,1)S(1)} %get-tuple-element.73.head_ref, bf16[128,8,2048]{2,1,0:T(8,128)(2,1)S(1)} %get-tuple-element.74.grads_ref), custom_call_target="tpu_custom_call" | custom-call | flops 1 | bytes 1 | tf_op jit(solution)/shard_map/pallas_call | solution.py:544
  22.7 2.8 %shard_map.78 = (bf16[256,256]{1,0:T(8,128)(2,1)S(1)}, bf16[1024,1024]{1,0:T(8,128)(2,1)S(1)}) custom-call(bf16[128,7168]{1,0:T(8,128)(2,1)} %hidden_ref.1, bf16[64,7168]{1,0:T(8,128)(2,1)} %proj_ref.1, s32[1,128]{1,0:T(1,128)S(1)} %bitcast.7, s32[8,128]{1,0:T(8,128)S(1)} %bitcast.4), custom_call_target="tpu_custom_call" | custom-call | flops 1 | bytes 1 | tf_op jit(solution)/shard_map/pallas_call | solution.py:570
  25.5 1.3 %collective-permute-start.10 = (bf16[512,512]{1,0:T(8,128)(2,1)S(1)}, bf16[512,512]{1,0:T(8,128)(2,1)S(1)}, u32[]{:S(2)}, u32[]{:S(2)}) collective-permute-start(bf16[512,512]{1,0:T(8,128)(2,1)S(1)} %collective-permute-done.2.refs_3_), channel_id=1, source_target_pairs={{0,2},{1,3},{2,0},{3,1},{4,6},{5,7},{6,4},{7,5},{8,10},{9,11},{10,... | collective-permute-start | bytes 1572872 | tf_op jit(solution)/shard_map/ppermute | solution.py:475
  26.8 3.7 %collective-permute-done.7.refs_5_ = bf16[512,512]{1,0:T(8,128)(2,1)S(1)} collective-permute-done((bf16[512,512]{1,0:T(8,128)(2,1)S(1)}, bf16[512,512]{1,0:T(8,128)(2,1)S(1)}, u32[]{:S(2)}, u32[]{:S(2)}) %collective-permute-start.7) | collective-permute-done | bytes 524320 | tf_op jit(solution)/shard_map/ppermute | solution.py:475
  30.5 2.0 %collective-permute-start.6 = (bf16[784,512]{1,0:T(8,128)(2,1)S(1)}, bf16[784,512]{1,0:T(8,128)(2,1)S(1)}, u32[]{:S(2)}, u32[]{:S(2)}) collective-permute-start(bf16[784,512]{1,0:T(8,128)(2,1)S(1)} %get-tuple-element.92), channel_id=1, source_target_pairs={{0,17},{1,16},{2,19},{3,18},{4,21},{5,20},{6,23},{7,22},{8,25},{9,... | collective-permute-start | bytes 2408456 | tf_op jit(solution)/shard_map/ppermute | solution.py:475
  32.6 0.0 collective-permute-done.1.refs_4_
  32.6 0.0 collective-permute-start.8
  32.6 2.3 %shard_map.79 = (bf16[4096,512]{1,0:T(8,128)(2,1)S(1)}, bf16[16,256,512]{2,1,0:T(8,128)(2,1)S(1)}, f32[4096,128]{1,0:T(8,128)S(1)}) custom-call(s32[16,16]{1,0:T(8,128)S(1)} %copy-done, s32[1,128]{1,0:T(1,128)S(1)} %get-tuple-element.66.refs_0_.starts_ref, bf16[1024,512]{1,0:T(8,128)(2,1)S(1)} %get-tuple-element.76.refs_1_, ...), custom_call_target="tpu_custom_call" | custom-call | flops 1000000000 | bytes 1 | tf_op jit(solution)/shard_map/pallas_call | solution.py:287
  34.9 1.3 %collective-permute-start.14 = (bf16[512,512]{1,0:T(8,128)(2,1)S(1)}, bf16[512,512]{1,0:T(8,128)(2,1)S(1)}, u32[]{:S(2)}, u32[]{:S(2)}) collective-permute-start(bf16[512,512]{1,0:T(8,128)(2,1)S(1)} %collective-permute-done.4.refs_6_), channel_id=1, source_target_pairs={{0,4},{1,5},{2,6},{3,7},{4,12},{5,13},{6,14},{7,15},{8,0},{9,1},{1... | collective-permute-start | bytes 1572872 | tf_op jit(solution)/shard_map/ppermute | solution.py:480
  36.3 0.0 collective-permute-done.5.refs_3_
  36.3 1.2 %collective-permute-start.9 = (bf16[512,512]{1,0:T(8,128)(2,1)S(1)}, bf16[512,512]{1,0:T(8,128)(2,1)S(1)}, u32[]{:S(2)}, u32[]{:S(2)}) collective-permute-start(bf16[512,512]{1,0:T(8,128)(2,1)S(1)} %collective-permute-done.4.refs_6_), channel_id=1, source_target_pairs={{0,2},{1,3},{2,0},{3,1},{4,6},{5,7},{6,4},{7,5},{8,10},{9,11},{10,... | collective-permute-start | bytes 1572872 | tf_op jit(solution)/shard_map/ppermute | solution.py:475
  37.5 0.0 collective-permute-done.10.refs_7_
  37.6 1.8 %collective-permute-start.15 = (bf16[512,512]{1,0:T(8,128)(2,1)S(1)}, bf16[512,512]{1,0:T(8,128)(2,1)S(1)}, u32[]{:S(2)}, u32[]{:S(2)}) collective-permute-start(bf16[512,512]{1,0:T(8,128)(2,1)S(1)} %collective-permute-done.1.refs_4_), channel_id=1, source_target_pairs={{0,8},{1,9},{2,10},{3,11},{4,0},{5,1},{6,2},{7,3},{8,12},{9,13},{1... | collective-permute-start | bytes 1572872 | tf_op jit(solution)/shard_map/ppermute | solution.py:480
  39.4 3.5 %shard_map.80 = (bf16[4096,512]{1,0:T(8,128)(2,1)S(1)}, bf16[16,256,512]{2,1,0:T(8,128)(2,1)S(1)}, f32[4096,128]{1,0:T(8,128)S(1)}) custom-call(s32[16,16]{1,0:T(8,128)S(1)} %copy-done, s32[1,128]{1,0:T(1,128)S(1)} %get-tuple-element.66.refs_0_.starts_ref, ...), custom_call_target="tpu_custom_call", output_to_operand_aliasing={{0}: (9, {}), {1}: (10, {}), {2}: (11, {})} | custom-call | flops 1000000000 | bytes 1 | tf_op jit(solution)/shard_map/pallas_call | solution.py:287
  42.9 8.4 %collective-permute-done.6.refs_4_ = bf16[784,512]{1,0:T(8,128)(2,1)S(1)} collective-permute-done((bf16[784,512]{1,0:T(8,128)(2,1)S(1)}, bf16[784,512]{1,0:T(8,128)(2,1)S(1)}, u32[]{:S(2)}, u32[]{:S(2)}) %collective-permute-start.6) | collective-permute-done | bytes 802848 | tf_op jit(solution)/shard_map/ppermute | solution.py:475
  51.3 2.7 %shard_map.81 = (bf16[4096,512]{1,0:T(8,128)(2,1)S(1)}, bf16[16,256,512]{2,1,0:T(8,128)(2,1)S(1)}, f32[4096,128]{1,0:T(8,128)S(1)}) custom-call(s32[16,16]{1,0:T(8,128)S(1)} %copy-done, s32[1,128]{1,0:T(1,128)S(1)} %get-tuple-element.66.refs_0_.starts_ref, ...), custom_call_target="tpu_custom_call", output_to_operand_aliasing={{0}: (6, {}), {1}: (7, {}), {2}: (8, {})} | custom-call | flops 1 | bytes 1 | tf_op jit(solution)/shard_map/pallas_call | solution.py:287
  54.0 0.0 collective-permute-done.9.refs_4_
  54.0 1.7 %shard_map.82 = (bf16[4096,512]{1,0:T(8,128)(2,1)S(1)}, bf16[16,256,512]{2,1,0:T(8,128)(2,1)S(1)}, f32[4096,128]{1,0:T(8,128)S(1)}, bf16[512,128]{1,0:T(8,128)(2,1)S(1)}, bf16[512,128]{1,0:T(8,128)(2,1)S(1)}) custom-call(s32[16,16]{1,0:T(8,128)S(1)} %copy-done, ...), custom_call_target="tpu_custom_call", output_to_operand_aliasing={{0}: (6, {}), {1}: (7, {}), {2}: (8, {})} | custom-call | flops 1 | bytes 1 | tf_op jit(solution)/shard_map/pallas_call | solution.py:287
  55.7 0.1 collective-permute-start.11
  55.8 1.6 %collective-permute-start.12 = (bf16[512,128]{1,0:T(8,128)(2,1)S(1)}, bf16[512,128]{1,0:T(8,128)(2,1)S(1)}, u32[]{:S(2)}, u32[]{:S(2)}) collective-permute-start(bf16[512,128]{1,0:T(8,128)(2,1)S(1)} %get-tuple-element.111), channel_id=1, source_target_pairs={{0,16},{1,17},{2,18},{3,19},{4,20},{5,21},{6,22},{7,23},{8,24},{9,... | collective-permute-start | bytes 393224 | tf_op jit(solution)/shard_map/ppermute | solution.py:475
  57.4 0.0 collective-permute-done.8.refs_4_
  57.4 2.2 %shard_map.83 = (bf16[4096,512]{1,0:T(8,128)(2,1)S(1)}, bf16[16,256,512]{2,1,0:T(8,128)(2,1)S(1)}, f32[4096,128]{1,0:T(8,128)S(1)}, bf16[512,128]{1,0:T(8,128)(2,1)S(1)}) custom-call(s32[16,16]{1,0:T(8,128)S(1)} %copy-done, s32[1,128]{1,0:T(1,128)S(1)} %get-tuple-element.66.refs_0_.starts_ref, ...), custom_call_target="tpu_custom_call", output_to_operand_aliasing={{0}: (6, {}), {1}: (7, {}), {2}: (8, {})} | custom-call | flops 1000000000 | bytes 1 | tf_op jit(solution)/shard_map/pallas_call | solution.py:287
  59.6 0.0 copy-start.2
  59.7 0.9 %collective-permute-start.13 = (bf16[512,128]{1,0:T(8,128)(2,1)S(1)}, bf16[512,128]{1,0:T(8,128)(2,1)S(1)}, u32[]{:S(2)}, u32[]{:S(2)}) collective-permute-start(bf16[512,128]{1,0:T(8,128)(2,1)S(1)} %get-tuple-element.114), channel_id=1, source_target_pairs={{0,17},{1,16},{2,19},{3,18},{4,21},{5,20},{6,23},{7,22},{8,25},{9,... | collective-permute-start | bytes 393224 | tf_op jit(solution)/shard_map/ppermute | solution.py:475
  60.5 0.0 collective-permute-done.11.b_ref
  60.5 0.1 collective-permute-done.12.c_ref
  60.6 0.3 collective-permute-done.15.refs_6_
  61.0 1.5 %shard_map.84 = (f32[224,128]{1,0:T(8,128)S(1)}, bf16[224,128]{1,0:T(8,128)(2,1)S(1)}, bf16[224,128]{1,0:T(8,128)(2,1)S(1)}, bf16[224,128]{1,0:T(8,128)(2,1)S(1)}) custom-call(s32[16,16]{1,0:T(8,128)S(1)} %copy-done, s32[1,128]{1,0:T(1,128)S(1)} %get-tuple-element.66.refs_0_.starts_ref, s32[1,128]{1,0:T(1,128)S(1)} %slice_add_fusion.2.refs_1_, ...), custom_call_target="tpu_custom_call" | custom-call | flops 1 | bytes 1 | tf_op jit(solution)/shard_map/pallas_call | solution.py:663
  62.5 0.9 %collective-permute-start.16 = (bf16[224,128]{1,0:T(8,128)(2,1)S(1)}, bf16[224,128]{1,0:T(8,128)(2,1)S(1)}, u32[]{:S(2)}, u32[]{:S(2)}) collective-permute-start(bf16[224,128]{1,0:T(8,128)(2,1)S(1)} %get-tuple-element.123), channel_id=1, source_target_pairs={{0,1},{1,0},{2,3},{3,2},{4,5},{5,4},{6,7},{7,6},{8,9},{9,8},{10,11... | collective-permute-start | bytes 172040 | tf_op jit(solution)/shard_map/ppermute | solution.py:475
  63.5 1.5 %collective-permute-start.17 = (bf16[224,128]{1,0:T(8,128)(2,1)S(1)}, bf16[224,128]{1,0:T(8,128)(2,1)S(1)}, u32[]{:S(2)}, u32[]{:S(2)}) collective-permute-start(bf16[224,128]{1,0:T(8,128)(2,1)S(1)} %get-tuple-element.124), channel_id=1, source_target_pairs={{0,16},{1,17},{2,18},{3,19},{4,20},{5,21},{6,22},{7,23},{8,24},{9,... | collective-permute-start | bytes 172040 | tf_op jit(solution)/shard_map/ppermute | solution.py:475
  65.0 0.2 collective-permute-start.18
  65.2 3.1 %shard_map.85 = (bf16[2,64,4096]{2,1,0:T(8,128)(2,1)}, f32[64,1024]{1,0:T(8,128)S(1)}) custom-call(s32[8,128]{1,0:T(8,128)S(1)} %bitcast.5, bf16[256,256]{1,0:T(8,128)(2,1)S(1)} %get-tuple-element.86.basis_ref, bf16[1024,1024]{1,0:T(8,128)(2,1)S(1)} %get-tuple-element.87.order_ref, f32[4096,128]{1,0:T(8,128)S(1)} %get-tuple-element.108.total_ref, ...), custom_call_target="tpu_custom_call" | custom-call | flops 1 | bytes 1 | tf_op jit(solution)/shard_map/pallas_call | solution.py:674
  68.3 0.6 collective-permute-done.18.d_ref
  68.8 2.2 %shard_map.86 = bf16[2,64,4096]{2,1,0:T(8,128)(2,1)} custom-call(s32[16,16]{1,0:T(8,128)S(1)} %copy-done, s32[1,128]{1,0:T(1,128)S(1)} %get-tuple-element.66.refs_0_.starts_ref, s32[8,128]{1,0:T(8,128)S(1)} %bitcast.6, bf16[256,256]{1,0:T(8,128)(2,1)S(1)} %get-tuple-element.86.basis_ref, ...), custom_call_target="tpu_custom_call", output_to_operand_aliasing={{}: (10, {})} | custom-call | flops 1 | bytes 1 | tf_op jit(solution)/shard_map/pallas_call | solution.py:687
  (18 shorter events, 0.1 us)
Async XLA Ops:
  0.0 0.7 copy-start.1
  4.0 2.8 %collective-permute-start = (bf16[256,512]{1,0:T(8,128)(2,1)S(1)}, bf16[256,512]{1,0:T(8,128)(2,1)S(1)}, u32[]{:S(2)}, u32[]{:S(2)}) collective-permute-start(bf16[256,512]{1,0:T(8,128)(2,1)S(1)} %get-tuple-element.68), channel_id=1, source_target_pairs={{0,1},{1,0},{2,3},{3,2},{4,5},{5,4},{6,7},{7,6},{8,9},{9,8},{10,11... | collective-permute-start | bytes 786440 | tf_op jit(solution)/shard_map/ppermute | solution.py:475
  4.1 15.2 %collective-permute-start.3 = (bf16[528,512]{1,0:T(8,128)(2,1)S(1)}, bf16[528,512]{1,0:T(8,128)(2,1)S(1)}, u32[]{:S(2)}, u32[]{:S(2)}) collective-permute-start(bf16[528,512]{1,0:T(8,128)(2,1)S(1)} %get-tuple-element.69), channel_id=1, source_target_pairs={{0,16},{1,17},{2,18},{3,19},{4,20},{5,21},{6,22},{7,23},{8,24},{9,... | collective-permute-start | bytes 1622024 | tf_op jit(solution)/shard_map/ppermute | solution.py:475
  6.8 14.1 %collective-permute-start.2 = (bf16[512,512]{1,0:T(8,128)(2,1)S(1)}, bf16[512,512]{1,0:T(8,128)(2,1)S(1)}, u32[]{:S(2)}, u32[]{:S(2)}) collective-permute-start(bf16[512,512]{1,0:T(8,128)(2,1)S(1)} %shard_map.74.refs_2_), channel_id=1, source_target_pairs={{0,4},{1,5},{2,6},{3,7},{4,12},{5,13},{6,14},{7,15},{8,0},{9,1},{1... | collective-permute-start | bytes 1572872 | tf_op jit(solution)/shard_map/ppermute | solution.py:480
  8.9 21.7 %collective-permute-start.7 = (bf16[512,512]{1,0:T(8,128)(2,1)S(1)}, bf16[512,512]{1,0:T(8,128)(2,1)S(1)}, u32[]{:S(2)}, u32[]{:S(2)}) collective-permute-start(bf16[512,512]{1,0:T(8,128)(2,1)S(1)} %shard_map.75), channel_id=1, source_target_pairs={{0,16},{1,17},{2,18},{3,19},{4,20},{5,21},{6,22},{7,23},{8,24},{9,... | collective-permute-start | bytes 1572872 | tf_op jit(solution)/shard_map/ppermute | solution.py:475
  10.1 22.5 %collective-permute-start.1 = (bf16[512,512]{1,0:T(8,128)(2,1)S(1)}, bf16[512,512]{1,0:T(8,128)(2,1)S(1)}, u32[]{:S(2)}, u32[]{:S(2)}) collective-permute-start(bf16[512,512]{1,0:T(8,128)(2,1)S(1)} %shard_map.74.refs_2_), channel_id=1, source_target_pairs={{0,2},{1,3},{2,0},{3,1},{4,6},{5,7},{6,4},{7,5},{8,10},{9,11},{10,... | collective-permute-start | bytes 1572872 | tf_op jit(solution)/shard_map/ppermute | solution.py:475
  13.7 9.0 %copy-start.3 = (s32[128]{0:T(128)S(1)}, s32[128]{0:T(128)}, u32[]{:S(2)}) copy-start(s32[128]{0:T(128)} %param.10) | copy-start | bytes 1540
  13.7 22.6 %collective-permute-start.5 = (bf16[1040,512]{1,0:T(8,128)(2,1)S(1)}, bf16[1040,512]{1,0:T(8,128)(2,1)S(1)}, u32[]{:S(2)}, u32[]{:S(2)}) collective-permute-start(bf16[1040,512]{1,0:T(8,128)(2,1)S(1)} %get-tuple-element.85), channel_id=1, source_target_pairs={{0,1},{1,0},{2,3},{3,2},{4,5},{5,4},{6,7},{7,6},{8,9},{9,8},{10,11... | collective-permute-start | bytes 3194888 | tf_op jit(solution)/shard_map/ppermute | solution.py:475
  20.9 14.0 %collective-permute-start.4 = (bf16[512,512]{1,0:T(8,128)(2,1)S(1)}, bf16[512,512]{1,0:T(8,128)(2,1)S(1)}, u32[]{:S(2)}, u32[]{:S(2)}) collective-permute-start(bf16[512,512]{1,0:T(8,128)(2,1)S(1)} %collective-permute-done.2.refs_3_), channel_id=1, source_target_pairs={{0,4},{1,5},{2,6},{3,7},{4,12},{5,13},{6,14},{7,15},{8,0},{9,1},{1... | collective-permute-start | bytes 1572872 | tf_op jit(solution)/shard_map/ppermute | solution.py:480
  21.4 11.2 %copy-start = (s32[16,16]{1,0:T(8,128)S(1)}, s32[16,16]{1,0:T(8,128)}, u32[]{:S(2)}) copy-start(s32[16,16]{1,0:T(8,128)} %constant.4.clone.bases_ref) | copy-start | bytes 3076
  25.5 12.1 %collective-permute-start.10 = (bf16[512,512]{1,0:T(8,128)(2,1)S(1)}, bf16[512,512]{1,0:T(8,128)(2,1)S(1)}, u32[]{:S(2)}, u32[]{:S(2)}) collective-permute-start(bf16[512,512]{1,0:T(8,128)(2,1)S(1)} %collective-permute-done.2.refs_3_), channel_id=1, source_target_pairs={{0,2},{1,3},{2,0},{3,1},{4,6},{5,7},{6,4},{7,5},{8,10},{9,11},{10,... | collective-permute-start | bytes 1572872 | tf_op jit(solution)/shard_map/ppermute | solution.py:475
  30.5 20.8 %collective-permute-start.6 = (bf16[784,512]{1,0:T(8,128)(2,1)S(1)}, bf16[784,512]{1,0:T(8,128)(2,1)S(1)}, u32[]{:S(2)}, u32[]{:S(2)}) collective-permute-start(bf16[784,512]{1,0:T(8,128)(2,1)S(1)} %get-tuple-element.92), channel_id=1, source_target_pairs={{0,17},{1,16},{2,19},{3,18},{4,21},{5,20},{6,23},{7,22},{8,25},{9,... | collective-permute-start | bytes 2408456 | tf_op jit(solution)/shard_map/ppermute | solution.py:475
  32.6 24.8 %collective-permute-start.8 = (bf16[256,512]{1,0:T(8,128)(2,1)S(1)}, bf16[256,512]{1,0:T(8,128)(2,1)S(1)}, u32[]{:S(2)}, u32[]{:S(2)}) collective-permute-start(bf16[256,512]{1,0:T(8,128)(2,1)S(1)} %get-tuple-element.93), channel_id=1, source_target_pairs={{0,17},{1,16},{2,19},{3,18},{4,21},{5,20},{6,23},{7,22},{8,25},{9,... | collective-permute-start | bytes 786440 | tf_op jit(solution)/shard_map/ppermute | solution.py:475
  34.9 25.7 %collective-permute-start.14 = (bf16[512,512]{1,0:T(8,128)(2,1)S(1)}, bf16[512,512]{1,0:T(8,128)(2,1)S(1)}, u32[]{:S(2)}, u32[]{:S(2)}) collective-permute-start(bf16[512,512]{1,0:T(8,128)(2,1)S(1)} %collective-permute-done.4.refs_6_), channel_id=1, source_target_pairs={{0,4},{1,5},{2,6},{3,7},{4,12},{5,13},{6,14},{7,15},{8,0},{9,1},{1... | collective-permute-start | bytes 1572872 | tf_op jit(solution)/shard_map/ppermute | solution.py:480
  36.3 17.7 %collective-permute-start.9 = (bf16[512,512]{1,0:T(8,128)(2,1)S(1)}, bf16[512,512]{1,0:T(8,128)(2,1)S(1)}, u32[]{:S(2)}, u32[]{:S(2)}) collective-permute-start(bf16[512,512]{1,0:T(8,128)(2,1)S(1)} %collective-permute-done.4.refs_6_), channel_id=1, source_target_pairs={{0,2},{1,3},{2,0},{3,1},{4,6},{5,7},{6,4},{7,5},{8,10},{9,11},{10,... | collective-permute-start | bytes 1572872 | tf_op jit(solution)/shard_map/ppermute | solution.py:475
  37.6 23.4 %collective-permute-start.15 = (bf16[512,512]{1,0:T(8,128)(2,1)S(1)}, bf16[512,512]{1,0:T(8,128)(2,1)S(1)}, u32[]{:S(2)}, u32[]{:S(2)}) collective-permute-start(bf16[512,512]{1,0:T(8,128)(2,1)S(1)} %collective-permute-done.1.refs_4_), channel_id=1, source_target_pairs={{0,8},{1,9},{2,10},{3,11},{4,0},{5,1},{6,2},{7,3},{8,12},{9,13},{1... | collective-permute-start | bytes 1572872 | tf_op jit(solution)/shard_map/ppermute | solution.py:480
  55.7 4.8 %collective-permute-start.11 = (bf16[512,128]{1,0:T(8,128)(2,1)S(1)}, bf16[512,128]{1,0:T(8,128)(2,1)S(1)}, u32[]{:S(2)}, u32[]{:S(2)}) collective-permute-start(bf16[512,128]{1,0:T(8,128)(2,1)S(1)} %get-tuple-element.110), channel_id=1, source_target_pairs={{0,1},{1,0},{2,3},{3,2},{4,5},{5,4},{6,7},{7,6},{8,9},{9,8},{10,11... | collective-permute-start | bytes 393224 | tf_op jit(solution)/shard_map/ppermute | solution.py:475
  55.8 4.8 %collective-permute-start.12 = (bf16[512,128]{1,0:T(8,128)(2,1)S(1)}, bf16[512,128]{1,0:T(8,128)(2,1)S(1)}, u32[]{:S(2)}, u32[]{:S(2)}) collective-permute-start(bf16[512,128]{1,0:T(8,128)(2,1)S(1)} %get-tuple-element.111), channel_id=1, source_target_pairs={{0,16},{1,17},{2,18},{3,19},{4,20},{5,21},{6,22},{7,23},{8,24},{9,... | collective-permute-start | bytes 393224 | tf_op jit(solution)/shard_map/ppermute | solution.py:475
  59.6 5.5 %copy-start.2 = (s32[128,8]{0,1:T(8,128)S(1)}, s32[128,8]{0,1:T(8,128)}, u32[]{:S(2)}) copy-start(s32[128,8]{0,1:T(8,128)} %param.9) | copy-start | bytes 12292
  59.7 5.5 %collective-permute-start.13 = (bf16[512,128]{1,0:T(8,128)(2,1)S(1)}, bf16[512,128]{1,0:T(8,128)(2,1)S(1)}, u32[]{:S(2)}, u32[]{:S(2)}) collective-permute-start(bf16[512,128]{1,0:T(8,128)(2,1)S(1)} %get-tuple-element.114), channel_id=1, source_target_pairs={{0,17},{1,16},{2,19},{3,18},{4,21},{5,20},{6,23},{7,22},{8,25},{9,... | collective-permute-start | bytes 393224 | tf_op jit(solution)/shard_map/ppermute | solution.py:475
  62.5 5.7 %collective-permute-start.16 = (bf16[224,128]{1,0:T(8,128)(2,1)S(1)}, bf16[224,128]{1,0:T(8,128)(2,1)S(1)}, u32[]{:S(2)}, u32[]{:S(2)}) collective-permute-start(bf16[224,128]{1,0:T(8,128)(2,1)S(1)} %get-tuple-element.123), channel_id=1, source_target_pairs={{0,1},{1,0},{2,3},{3,2},{4,5},{5,4},{6,7},{7,6},{8,9},{9,8},{10,11... | collective-permute-start | bytes 172040 | tf_op jit(solution)/shard_map/ppermute | solution.py:475
  63.5 4.8 %collective-permute-start.17 = (bf16[224,128]{1,0:T(8,128)(2,1)S(1)}, bf16[224,128]{1,0:T(8,128)(2,1)S(1)}, u32[]{:S(2)}, u32[]{:S(2)}) collective-permute-start(bf16[224,128]{1,0:T(8,128)(2,1)S(1)} %get-tuple-element.124), channel_id=1, source_target_pairs={{0,16},{1,17},{2,18},{3,19},{4,20},{5,21},{6,22},{7,23},{8,24},{9,... | collective-permute-start | bytes 172040 | tf_op jit(solution)/shard_map/ppermute | solution.py:475
  65.0 3.9 %collective-permute-start.18 = (bf16[224,128]{1,0:T(8,128)(2,1)S(1)}, bf16[224,128]{1,0:T(8,128)(2,1)S(1)}, u32[]{:S(2)}, u32[]{:S(2)}) collective-permute-start(bf16[224,128]{1,0:T(8,128)(2,1)S(1)} %get-tuple-element.125), channel_id=1, source_target_pairs={{0,17},{1,16},{2,19},{3,18},{4,21},{5,20},{6,23},{7,22},{8,25},{9,... | collective-permute-start | bytes 172040 | tf_op jit(solution)/shard_map/ppermute | solution.py:475
